TPU v7x, 32 devices: a whole 2x2x4 slice. The times are simulated.
32 devices in a mesh: seq: 8 (over y, x, core), head: 4 (over z).
Axes of the slice: x: 2, y: 2, z: 4, core: 2. Of those that a mesh axis runs over, the one named last changes fastest.
Arguments:
- queries: bfloat16 [3072, 4096], P('seq', 'head'), may hold values from -108 to 108
- keys_in: bfloat16 [3072, 4096], P('seq', 'head'), may hold values from -4 to 4
- values: bfloat16 [3072, 4096], P('seq', 'head'), may hold values from -6 to 6
- out_grad: bfloat16 [3072, 4096], P('seq', 'head'), may hold values from -6 to 6
- out_weight: bfloat16 [4096, 4096], P('head'), may hold values from -0.09375 to 0.09375
- doc_ids: int32 [3072], P('seq'), may hold values from 0 to 7, never falling along the last dimension, each value on 1 to 1920 neighbouring positions
Outputs:
- query_grad: bfloat16 [3072, 4096], P('seq', 'head')
- key_grad: bfloat16 [3072, 4096], P('seq', 'head')
- value_grad: bfloat16 [3072, 4096], P('seq', 'head')
Inputs may be any that keep to these rules, and one draw needn't show every extreme that they name: `doc_ids`: document ids never fall along the rows.
All inputs are finite; a program needn't handle non-finite values.
Results may differ from a plain program's by a relative error of at most 0.0085.
Values may be sent and summed in bfloat16 or wider, within the bound.
No kernel may reach another device: no remote copies, remote signals or barrier semaphores. Data moves between devices by JAX's collectives and lax.ppermute only.
A program may use at most 192 MiB of HBM per device.

v0:
```python
import functools
import math

import jax
import jax.numpy as jnp
from jax import lax
from jax.experimental import pallas as pl
from jax.experimental.pallas import tpu as pltpu
from jax.sharding import PartitionSpec as P

HD = 128
DOC_VALUES = 8
DOC_ROWS = 16
NEG_LARGE = -1e30
VMEM_LIMIT = 56 * 1024 * 1024
PARAMS = pltpu.CompilerParams(vmem_limit_bytes=VMEM_LIMIT)

NN = (((1,), (0,)), ((), ()))
NT = (((1,), (1,)), ((), ()))
SMEM_SPEC = pl.BlockSpec(memory_space=pltpu.SMEM)
VMEM_SPEC = pl.BlockSpec(memory_space=pltpu.VMEM)


def dot32(a, b, dims=NN):
    return lax.dot_general(a, b, dims, preferred_element_type=jnp.float32)


def block_size(total, wanted):
    size = min(wanted, total)
    while total % size or size % 128:
        size -= 128
    return size


def aligned(index, size):
    return pl.ds(pl.multiple_of(index * size, size), size)


def pack_kernel(heads, rows, me_s, q_ref, k_ref, v_ref, doc_ref, *outs):
    own = lax.rem(me_s[0], heads)
    docs = doc_ref[...].astype(jnp.float32)
    docs = jnp.concatenate([docs, jnp.zeros((DOC_ROWS - docs.shape[0], HD), jnp.float32)], axis=0)
    docs = docs.astype(jnp.bfloat16)
    for d, out in enumerate(outs):
        columns = aligned(own ^ d, HD)
        for part, ref in enumerate((q_ref, k_ref, v_ref)):
            out[part * rows:(part + 1) * rows, :] = ref[:, columns]
        out[3 * rows:, :] = docs


def pack_heads(me, q, k, v, doc_ids):
    rows, width = q.shape
    heads = width // HD
    return pl.pallas_call(
        functools.partial(pack_kernel, heads, rows),
        in_specs=[SMEM_SPEC] + [VMEM_SPEC] * 4,
        out_specs=[VMEM_SPEC] * heads,
        out_shape=[jax.ShapeDtypeStruct((3 * rows + DOC_ROWS, HD), q.dtype)] * heads,
        compiler_params=PARAMS,
    )(me, q, k, v, doc_ids.reshape(rows // HD, HD))


def unpack_kernel(heads, rows, me_s, *refs):
    own = lax.rem(me_s[0], heads)
    for d in range(heads):
        columns = aligned(own ^ d, HD)
        for part in range(3):
            refs[heads + part][:, columns] = refs[d][part * rows:(part + 1) * rows, :]


def unpack_heads(me, blocks, rows):
    heads = len(blocks)
    return pl.pallas_call(
        functools.partial(unpack_kernel, heads, rows),
        in_specs=[SMEM_SPEC] + [VMEM_SPEC] * heads,
        out_specs=[VMEM_SPEC] * 3,
        out_shape=[jax.ShapeDtypeStruct((rows, heads * HD), blocks[0].dtype)] * 3,
        compiler_params=PARAMS,
    )(me, *blocks)


def project_kernel(first, where_s, *refs):
    if first:
        o_ref, w_ref, out_ref = refs
        out_ref[...] = dot32(o_ref[...], w_ref[...], NT)
    else:
        o_ref, w_ref, acc_ref, out_ref = refs
        out_ref[...] = acc_ref[...] + dot32(o_ref[...], w_ref[...], NT)


def project_last_kernel(where_s, o_ref, w_ref, acc_ref, *outs):
    step = pl.program_id(0)
    both = (acc_ref[...] + dot32(o_ref[...], w_ref[...], NT)).astype(jnp.bfloat16)
    odd = where_s[1] == 1
    near = jnp.where(odd, both[:, HD:], both[:, :HD])
    far = jnp.where(odd, both[:, :HD], both[:, HD:])
    for j in range(len(outs) // 2):

        @pl.when(step == j)
        def _():
            outs[2 * j][...] = near
            outs[2 * j + 1][...] = far


def project(me, block, weight, features, acc, last):
    rows, width = features.shape
    pairs = weight.shape[0] // (2 * HD)
    where = jnp.stack([block, lax.rem(me, 2), lax.rem(me // 2, pairs)])
    feature_spec = pl.BlockSpec((rows, width), lambda j, w: (0, 0))
    weight_spec = pl.BlockSpec((2 * HD, width), lambda j, w: (w[2] ^ j, w[0]))
    acc_spec = pl.BlockSpec((rows, 2 * HD), lambda j, w: (0, w[2] ^ j))
    cost = pl.CostEstimate(
        flops=2 * rows * width * weight.shape[0],
        bytes_accessed=2 * width * weight.shape[0] + 8 * rows * weight.shape[0],
        transcendentals=0,
    )
    if last:
        kernel = project_last_kernel
        out_specs = [pl.BlockSpec((rows, HD), lambda j, w: (0, 0))] * (2 * pairs)
        out_shape = [jax.ShapeDtypeStruct((rows, HD), jnp.bfloat16)] * (2 * pairs)
    else:
        kernel = functools.partial(project_kernel, acc is None)
        out_specs = acc_spec
        out_shape = jax.ShapeDtypeStruct((rows, weight.shape[0]), jnp.float32)
    return pl.pallas_call(
        kernel,
        grid_spec=pltpu.PrefetchScalarGridSpec(
            num_scalar_prefetch=1,
            grid=(pairs,),
            in_specs=[feature_spec, weight_spec] + ([] if acc is None else [acc_spec]),
            out_specs=out_specs,
        ),
        out_shape=out_shape,
        compiler_params=PARAMS,
        cost_estimate=cost,
    )(where, features, weight, *([] if acc is None else [acc]))


def visible(first_row, q0, k0, shape):
    key = lax.broadcasted_iota(jnp.int32, shape, 0)
    last_row = q0 - k0 + lax.broadcasted_iota(jnp.int32, (1, shape[1]), 1)
    return (key >= first_row - k0) & (key <= last_row)


def plan_size(total, bq, bk):
    return sum(((q + 1) * bq + bk - 1) // bk for q in range(total // bq)) + 2


def fill_plan(lows, total, bq, bk, own, plan_q, plan_k, count_ref):
    def put(qi):
        def at(ki, count):
            plan_q[count] = qi
            plan_k[count] = ki
            return count + 1

        return at

    count = 0
    for qi, low in enumerate(lows):
        high = ((qi + 1) * bq + bk - 1) // bk
        if own is not None:
            wanted = ((qi + 1) * bq > own[0]) & (qi * bq < own[1])
            low = jnp.where(wanted, low, jnp.maximum(low, own[0] // bk))
            high = jnp.where(wanted, high, jnp.minimum(high, (own[1] + bk - 1) // bk))
        count = lax.fori_loop(low, high, put(qi), count)
    count_ref[0] = (count + 1) // 2
    for spare in range(2):
        plan_q[count + spare] = 0
        plan_k[count + spare] = total // bk - 1


def pipelined(plan_q, plan_k, count_ref, early, late, buffers):
    early(plan_q[0], plan_k[0], buffers[0])

    @pl.loop(0, count_ref[0])
    def _(i):
        for turn in range(2):
            now = 2 * i + turn
            late(plan_q[now], plan_k[now], buffers[turn])
            early(plan_q[now + 1], plan_k[now + 1], buffers[1 - turn])


def forward_kernel(peers, heads, rows, bq, bk, me_s, *refs):
    blocks = refs[:peers]
    q_ref, k_ref, v_ref, first_ref, out_ref, log_ref, plan_q, plan_k, count_ref = refs[peers:peers + 9]
    own_q, own_k, own_count, qt_ref, vt_ref, doc_ref, sum_ref, s0, top0, s1, top1 = refs[peers + 9:]
    total = q_ref.shape[0]
    factor = HD ** (-0.5) * math.log2(math.e)
    me = me_s[0]
    for d, block in enumerate(blocks):
        place = me ^ d
        for part, ref in enumerate((q_ref, k_ref, v_ref)):
            ref[aligned(place, rows), :] = block[part * rows:(part + 1) * rows, :]
        docs = block[3 * rows:, :].astype(jnp.float32)
        for t in range(rows // HD):
            doc_ref[:, aligned(place * (rows // HD) + t, HD)] = docs[t:t + 1, :]
    docs = doc_ref[...]
    first = jnp.zeros(docs.shape, jnp.float32)
    for value in range(1, DOC_VALUES):
        before = jnp.sum((docs < value).astype(jnp.float32))
        first = jnp.where(docs >= value, before, first)
    first = first.astype(jnp.int32)
    first_ref[...] = first
    lows = [jnp.min(first[:, qi * bq:(qi + 1) * bq]) // bk for qi in range(total // bq)]
    fill_plan(lows, total, bq, bk, None, own_q, own_k, own_count)
    group = (me // heads) * heads * rows
    own = None if heads == peers else (group, group + heads * rows)
    fill_plan(lows, total, bq, bk, own, plan_q, plan_k, count_ref)
    qt_ref[...] = q_ref[...].T
    vt_ref[...] = v_ref[...].T
    out_ref[...] = jnp.zeros_like(out_ref)
    log_ref[...] = jnp.full_like(log_ref, NEG_LARGE)
    sum_ref[...] = jnp.zeros_like(sum_ref)

    def early(qi, ki, buffer):
        s_ref, top_ref = buffer
        keys, queries = aligned(ki, bk), aligned(qi, bq)
        s = dot32(k_ref[keys, :], qt_ref[:, queries]) * factor
        s = jnp.where(visible(first_ref[:, queries], qi * bq, ki * bk, (bk, bq)), s, NEG_LARGE)
        s_ref[...] = s
        top_ref[...] = jnp.max(s, axis=0, keepdims=True)

    def late(qi, ki, buffer):
        s_ref, top_ref = buffer
        keys, queries = aligned(ki, bk), aligned(qi, bq)
        top = log_ref[:, queries]
        new_top = jnp.maximum(top, top_ref[...])
        p = jnp.exp2(s_ref[...] - new_top)
        fix = jnp.exp2(top - new_top)
        high = p.astype(jnp.bfloat16)
        rest = (p - high.astype(jnp.float32)).astype(jnp.bfloat16)
        vt = vt_ref[:, keys]
        out_ref[:, queries] = out_ref[:, queries] * fix + (dot32(vt, high) + dot32(vt, rest))
        sum_ref[:, queries] = sum_ref[:, queries] * fix + jnp.sum(p, axis=0, keepdims=True)
        log_ref[:, queries] = new_top

    pipelined(own_q, own_k, own_count, early, late, ((s0, top0), (s1, top1)))
    total_p = sum_ref[...]
    out_ref[...] = out_ref[...] / total_p
    log_ref[...] = log_ref[...] + jnp.log2(total_p)


def backward_kernel(peers, heads, rows, bq, bk, me_s, plan_q, plan_k, count_ref, q_ref, k_ref, v_ref,
                    first_ref, out_ref, log_ref, *refs):
    blocks = refs[:peers]
    results = refs[peers:peers + heads]
    g_ref, qt_ref, gt_ref, kt_ref, dot_ref, dk_acc, dv_acc, dq_acc, p0, ds0, p1, ds1 = refs[peers + heads:]
    scale = HD ** (-0.5)
    factor = scale * math.log2(math.e)
    me = me_s[0]
    for d, block in enumerate(blocks):
        g_ref[aligned(me ^ d, rows), :] = block[...]
    qt_ref[...] = q_ref[...].T
    gt_ref[...] = g_ref[...].T
    kt_ref[...] = k_ref[...].T
    dot_ref[...] = jnp.sum(gt_ref[...].astype(jnp.float32) * out_ref[...], axis=0, keepdims=True)
    dk_acc[...] = jnp.zeros_like(dk_acc)
    dv_acc[...] = jnp.zeros_like(dv_acc)
    dq_acc[...] = jnp.zeros_like(dq_acc)

    def early(qi, ki, buffer):
        p_ref, ds_ref = buffer
        keys, queries = aligned(ki, bk), aligned(qi, bq)
        p = jnp.exp2(dot32(k_ref[keys, :], qt_ref[:, queries]) * factor - log_ref[:, queries])
        p = jnp.where(visible(first_ref[:, queries], qi * bq, ki * bk, (bk, bq)), p, 0.0)
        p_ref[...] = p.astype(jnp.bfloat16)
        dp = dot32(v_ref[keys, :], gt_ref[:, queries])
        ds_ref[...] = (p * (dp - dot_ref[:, queries])).astype(jnp.bfloat16)

    def late(qi, ki, buffer):
        p_ref, ds_ref = buffer
        keys, queries = aligned(ki, bk), aligned(qi, bq)
        dv_acc[keys, :] += dot32(p_ref[...], g_ref[queries, :])
        dk_acc[keys, :] += dot32(ds_ref[...], q_ref[queries, :])
        dq_acc[:, queries] += dot32(kt_ref[:, keys], ds_ref[...])

    pipelined(plan_q, plan_k, count_ref, early, late, ((p0, ds0), (p1, ds1)))
    for d, result in enumerate(results):
        own = aligned(me ^ d, rows)
        result[:rows, :] = (scale * dq_acc[:, own]).T.astype(result.dtype)
        result[rows:2 * rows, :] = (scale * dk_acc[own, :]).astype(result.dtype)
        result[2 * rows:, :] = dv_acc[own, :].astype(result.dtype)


def attention_cost(total, products):
    return pl.CostEstimate(
        flops=products * total * total * HD // 2,
        bytes_accessed=16 * total * HD,
        transcendentals=total * total // 4,
    )


def attention_forward(me, blocks, rows, heads):
    peers = len(blocks)
    total = peers * rows
    bq, bk = block_size(total, 512), block_size(total, 256)
    size = plan_size(total, bq, bk)
    return pl.pallas_call(
        functools.partial(forward_kernel, peers, heads, rows, bq, bk),
        in_specs=[SMEM_SPEC] + [VMEM_SPEC] * peers,
        out_specs=[VMEM_SPEC] * 6 + [SMEM_SPEC] * 3,
        out_shape=[jax.ShapeDtypeStruct((total, HD), jnp.bfloat16)] * 3
        + [
            jax.ShapeDtypeStruct((1, total), jnp.int32),
            jax.ShapeDtypeStruct((HD, total), jnp.float32),
            jax.ShapeDtypeStruct((1, total), jnp.float32),
            jax.ShapeDtypeStruct((size,), jnp.int32),
            jax.ShapeDtypeStruct((size,), jnp.int32),
            jax.ShapeDtypeStruct((1,), jnp.int32),
        ],
        scratch_shapes=[
            pltpu.SMEM((size,), jnp.int32),
            pltpu.SMEM((size,), jnp.int32),
            pltpu.SMEM((1,), jnp.int32),
            pltpu.VMEM((HD, total), jnp.bfloat16),
            pltpu.VMEM((HD, total), jnp.bfloat16),
            pltpu.VMEM((1, total), jnp.float32),
            pltpu.VMEM((1, total), jnp.float32),
        ]
        + [pltpu.VMEM((bk, bq), jnp.float32), pltpu.VMEM((1, bq), jnp.float32)] * 2,
        compiler_params=PARAMS,
        cost_estimate=attention_cost(total, 3),
    )(me, *blocks)


def attention_backward(me, heads, state, blocks):
    peers, rows = len(blocks), blocks[0].shape[0]
    total = peers * rows
    bq, bk = block_size(total, 512), block_size(total, 256)
    return pl.pallas_call(
        functools.partial(backward_kernel, peers, heads, rows, bq, bk),
        in_specs=[SMEM_SPEC] * 4 + [VMEM_SPEC] * (6 + peers),
        out_specs=[VMEM_SPEC] * heads,
        out_shape=[jax.ShapeDtypeStruct((3 * rows, HD), jnp.bfloat16)] * heads,
        scratch_shapes=[
            pltpu.VMEM((total, HD), jnp.bfloat16),
            pltpu.VMEM((HD, total), jnp.bfloat16),
            pltpu.VMEM((HD, total), jnp.bfloat16),
            pltpu.VMEM((HD, total), jnp.bfloat16),
            pltpu.VMEM((1, total), jnp.float32),
            pltpu.VMEM((total, HD), jnp.float32),
            pltpu.VMEM((total, HD), jnp.float32),
            pltpu.VMEM((HD, total), jnp.float32),
        ]
        + [pltpu.VMEM((bk, bq), jnp.bfloat16)] * 4,
        compiler_params=PARAMS,
        cost_estimate=attention_cost(total, 5),
    )(me, *state[6:], *state[:6], *blocks)


def per_device(peers, groups, queries, keys_in, values, out_grad, out_weight, doc_ids):
    rows, width = queries.shape
    heads = width // HD
    me = lax.axis_index("seq")
    me_vector = me.reshape(1)

    def exchange(x, d):
        return x if d == 0 else lax.ppermute(x, "seq", [(i, i ^ d) for i in range(peers)])

    def pass_on(x):
        return lax.ppermute(x, "head", [(i, (i + 1) % groups) for i in range(groups)])

    order = [*range(peers - 2, 0, -2), *range(peers - 1, 0, -2)]

    def exchange_all(blocks, wanted):
        moved = {d: exchange(blocks[d % heads], d) for d in order if d < wanted}
        return [blocks[0]] + [moved[d] for d in range(1, wanted)]

    packed = list(pack_heads(me_vector, queries, keys_in, values, doc_ids))
    received = exchange_all(packed, peers)

    after = lax.optimization_barrier
    features, acc = out_grad, None
    for step in range(groups):
        block = lax.rem(lax.axis_index("head") + groups - step, groups)
        last = step == groups - 1
        if step == 0:
            features, packed[0] = after((features, packed[0]))
        if not last:
            passed = pass_on(features)
        if step == groups - 2:
            received[0], features = after((received[0], features))
            state = list(attention_forward(me_vector, received, rows, heads))
            features, state[1] = after((features, state[1]))
        acc = project(me, block, out_weight, features, acc, last)
        if not last:
            features = passed
            if step < groups - 2:
                batch = order[step * len(order) // (groups - 2):(step + 1) * len(order) // (groups - 2)]
                features, acc, here = after((features, acc, [received[d] for d in batch]))
                for d, block in zip(batch, here):
                    received[d] = block
    grads = exchange_all(acc, peers)

    results = attention_backward(me_vector, heads, state, grads)
    returned = exchange_all(results, heads)
    return tuple(unpack_heads(me_vector, returned, rows))


def solution(mesh):
    in_specs = (
        P("seq", "head"),
        P("seq", "head"),
        P("seq", "head"),
        P("seq", "head"),
        P("head", None),
        P("seq"),
    )
    out_specs = (P("seq", "head"), P("seq", "head"), P("seq", "head"))
    return jax.shard_map(
        functools.partial(per_device, mesh.shape["seq"], mesh.shape["head"]),
        mesh=mesh, in_specs=in_specs, out_specs=out_specs, check_vma=False,
    )
```

profile of v0, /device:TPU:0, one launch (start us, length us, event | category | flops | bytes accessed | tf_op | source)
XLA Modules:
  0.0 154.2 jit_solution(301272252295068601)
XLA Ops:
  0.6 3.7 %shard_map.85 = (bf16[1168,128]{1,0:T(8,128)(2,1)}, bf16[1168,128]{1,0:T(8,128)(2,1)}, bf16[1168,128]{1,0:T(8,128)(2,1)}, bf16[1168,128]{1,0:T(8,128)(2,1)}, bf1...) custom-call(s32[1]{0:T(128)} %bitcast.me_s, ...), custom_call_target="tpu_custom_call" | custom-call | tf_op jit(solution)/shard_map/pallas_call | solution.py:54
  4.4 3.0 %collective-permute-start = (bf16[384,1024]{1,0:T(8,128)(2,1)S(1)}, bf16[384,1024]{1,0:T(8,128)(2,1)S(1)}, u32[]{:S(2)}, u32[]{:S(2)}) collective-permute-start(bf16[384,1024]{1,0:T(8,128)(2,1)S(1)} %copy-done.2), channel_id=1, source_target_pairs={{0,1},{1,2},{2,3},{3,0},{4,5},{5,6},{6,7},{7,4},{8,9},{9,10},{10,1... | collective-permute-start | bytes 2359304 | tf_op jit(solution)/shard_map/ppermute | solution.py:361
  7.4 2.4 %collective-permute-start.1 = (bf16[1168,128]{1,0:T(8,128)(2,1)}, bf16[1168,128]{1,0:T(8,128)(2,1)S(1)}, u32[]{:S(2)}, u32[]{:S(2)}) collective-permute-start(bf16[1168,128]{1,0:T(8,128)(2,1)} %get-tuple-element.54), channel_id=1, source_target_pairs={{0,24},{4,28},{8,16},{12,20},{16,8},{20,12},{24,0},{28,4},{1,25},{... | collective-permute-start | bytes 897032 | tf_op jit(solution)/shard_map/ppermute | solution.py:358
  9.8 0.5 collective-permute-start.2
  10.3 0.5 collective-permute-start.3
  10.9 0.6 add_add_fusion.where_s
  11.5 5.6 %shard_map.86.refs_2_ = f32[384,1024]{1,0:T(8,128)} custom-call(s32[3]{0:T(128)} %add_add_fusion.where_s, bf16[384,1024]{1,0:T(8,128)(2,1)} %refs_0_, bf16[1024,4096]{1,0:T(8,128)(2,1)} %w_ref.1), custom_call_target="tpu_custom_call" | custom-call | flops 805306368 | bytes 5242880 | tf_op jit(solution)/shard_map/pallas_call | solution.py:125
  17.1 1.5 collective-permute-done.1.refs_6_
  18.6 4.9 %collective-permute-done.2.refs_4_ = bf16[1168,128]{1,0:T(8,128)(2,1)S(1)} collective-permute-done((bf16[1168,128]{1,0:T(8,128)(2,1)}, bf16[1168,128]{1,0:T(8,128)(2,1)S(1)}, u32[]{:S(2)}, u32[]{:S(2)}) %collective-permute-start.2) | collective-permute-done | bytes 299040 | tf_op jit(solution)/shard_map/ppermute | solution.py:358
  23.6 3.4 %collective-permute-done.refs_0_ = bf16[384,1024]{1,0:T(8,128)(2,1)S(1)} collective-permute-done((bf16[384,1024]{1,0:T(8,128)(2,1)S(1)}, bf16[384,1024]{1,0:T(8,128)(2,1)S(1)}, u32[]{:S(2)}, u32[]{:S(2)}) %collective-permute-start) | collective-permute-done | bytes 786464 | tf_op jit(solution)/shard_map/ppermute | solution.py:361
  27.0 1.1 collective-permute-start.5
  28.0 1.6 %collective-permute-start.6 = (bf16[1168,128]{1,0:T(8,128)(2,1)S(1)}, bf16[1168,128]{1,0:T(8,128)(2,1)}, u32[]{:S(2)}, u32[]{:S(2)}) collective-permute-start(bf16[1168,128]{1,0:T(8,128)(2,1)S(1)} %copy-done.16), channel_id=1, source_target_pairs={{0,20},{4,16},{8,28},{12,24},{16,4},{20,0},{24,12},{28,8},{1,21},{... | collective-permute-start | bytes 897032 | tf_op jit(solution)/shard_map/ppermute | solution.py:358
  29.6 0.1 collective-permute-start.7
  29.8 0.5 collective-permute-start.8
  30.3 0.6 add_add_fusion.1.where_s
  30.9 5.7 %shard_map.87.refs_2_ = f32[384,1024]{1,0:T(8,128)} custom-call(s32[3]{0:T(128)} %add_add_fusion.1.where_s, bf16[384,1024]{1,0:T(8,128)(2,1)} %copy-done, bf16[1024,4096]{1,0:T(8,128)(2,1)} %w_ref.1, f32[384,1024]{1,0:T(8,128)} %shard_map.86.refs_2_), custom_call_target="tpu_custom_call" | custom-call | flops 805306368 | bytes 5242880 | tf_op jit(solution)/shard_map/pallas_call | solution.py:125
  36.6 0.9 collective-permute-done.5.refs_7_
  37.6 6.3 %collective-permute-done.6.refs_5_ = bf16[1168,128]{1,0:T(8,128)(2,1)} collective-permute-done((bf16[1168,128]{1,0:T(8,128)(2,1)S(1)}, bf16[1168,128]{1,0:T(8,128)(2,1)}, u32[]{:S(2)}, u32[]{:S(2)}) %collective-permute-start.6) | collective-permute-done | bytes 299040 | tf_op jit(solution)/shard_map/ppermute | solution.py:358
  43.8 3.6 %collective-permute-done.4.refs_0_ = bf16[384,1024]{1,0:T(8,128)(2,1)S(1)} collective-permute-done((bf16[384,1024]{1,0:T(8,128)(2,1)S(1)}, bf16[384,1024]{1,0:T(8,128)(2,1)S(1)}, u32[]{:S(2)}, u32[]{:S(2)}) %collective-permute-start.4) | collective-permute-done | bytes 786464 | tf_op jit(solution)/shard_map/ppermute | solution.py:361
  47.5 0.7 add_add_fusion.2
  48.2 22.1 %shard_map.88 = (bf16[3072,128]{1,0:T(8,128)(2,1)}, bf16[3072,128]{1,0:T(8,128)(2,1)}, bf16[3072,128]{1,0:T(8,128)(2,1)}, s32[1,3072]{1,0:T(1,128)}, f32[128,307...) custom-call(s32[1]{0:T(128)} %bitcast.me_s, ...), custom_call_target="tpu_custom_call" | custom-call | flops 1811939328 | bytes 6291456 | tf_op jit(solution)/shard_map/pallas_call | solution.py:298
  70.3 5.7 %shard_map.89.acc_ref = f32[384,1024]{1,0:T(8,128)} custom-call(s32[3]{0:T(128)} %get-tuple-element.102.where_s, bf16[384,1024]{1,0:T(8,128)(2,1)} %copy-done.1, bf16[1024,4096]{1,0:T(8,128)(2,1)} %w_ref.1, f32[384,1024]{1,0:T(8,128)} %shard_map.87.refs_2_), custom_call_target="tpu_custom_call" | custom-call | flops 805306368 | bytes 5242880 | tf_op jit(solution)/shard_map/pallas_call | solution.py:125
  76.0 0.9 copy-done.3
  76.9 5.7 %shard_map.90 = (bf16[384,128]{1,0:T(8,128)(2,1)}, bf16[384,128]{1,0:T(8,128)(2,1)}, bf16[384,128]{1,0:T(8,128)(2,1)}, bf16[384,128]{1,0:T(8,128)(2,1)}, bf16[38...) custom-call(s32[3]{0:T(128)} %get-tuple-element.101.where_s, ...), custom_call_target="tpu_custom_call" | custom-call | flops 805306368 | bytes 5242880 | tf_op jit(solution)/shard_map/pallas_call | solution.py:125
  82.6 1.3 collective-permute-start.11
  83.9 0.5 collective-permute-start.12
  84.5 1.3 collective-permute-start.13
  85.8 0.4 collective-permute-start.14
  86.2 2.2 %collective-permute-start.15 = (bf16[384,128]{1,0:T(8,128)(2,1)}, bf16[384,128]{1,0:T(8,128)(2,1)S(1)}, u32[]{:S(2)}, u32[]{:S(2)}) collective-permute-start(bf16[384,128]{1,0:T(8,128)(2,1)} %get-tuple-element.91), channel_id=1, source_target_pairs={{0,24},{4,28},{8,16},{12,20},{16,8},{20,12},{24,0},{28,4},{1,25},{... | collective-permute-start | bytes 294920 | tf_op jit(solution)/shard_map/ppermute | solution.py:358
  88.4 0.1 collective-permute-done.11.refs_2_
  88.5 1.0 collective-permute-start.16
  89.5 0.2 collective-permute-done.12.refs_3_
  89.7 0.6 collective-permute-done.13.refs_4_
  90.3 5.2 %collective-permute-done.14.refs_5_ = bf16[384,128]{1,0:T(8,128)(2,1)S(1)} collective-permute-done((bf16[384,128]{1,0:T(8,128)(2,1)}, bf16[384,128]{1,0:T(8,128)(2,1)S(1)}, u32[]{:S(2)}, u32[]{:S(2)}) %collective-permute-start.14) | collective-permute-done | bytes 98336 | tf_op jit(solution)/shard_map/ppermute | solution.py:358
  95.5 0.6 copy-done.21
  96.2 23.0 %shard_map.91 = (bf16[1152,128]{1,0:T(8,128)(2,1)}, bf16[1152,128]{1,0:T(8,128)(2,1)}, bf16[1152,128]{1,0:T(8,128)(2,1)}, bf16[1152,128]{1,0:T(8,128)(2,1)}, bf1...) custom-call(s32[1]{0:T(128)} %bitcast.me_s, ...), custom_call_target="tpu_custom_call" | custom-call | flops 3019898880 | bytes 6291456 | tf_op jit(solution)/shard_map/pallas_call | solution.py:330
  119.2 0.5 collective-permute-start.17
  119.6 1.3 collective-permute-start.18
  120.9 0.2 collective-permute-start.19
  121.1 1.3 collective-permute-start.20
  122.4 0.7 collective-permute-start.21
  123.2 2.2 %collective-permute-start.22 = (bf16[1152,128]{1,0:T(8,128)(2,1)}, bf16[1152,128]{1,0:T(8,128)(2,1)S(1)}, u32[]{:S(2)}, u32[]{:S(2)}) collective-permute-start(bf16[1152,128]{1,0:T(8,128)(2,1)} %get-tuple-element.99), channel_id=1, source_target_pairs={{0,24},{4,28},{8,16},{12,20},{16,8},{20,12},{24,0},{28,4},{1,25},{... | collective-permute-start | bytes 884744 | tf_op jit(solution)/shard_map/ppermute | solution.py:358
  125.4 4.3 %collective-permute-done.18.refs_2_ = bf16[1152,128]{1,0:T(8,128)(2,1)S(1)} collective-permute-done((bf16[1152,128]{1,0:T(8,128)(2,1)}, bf16[1152,128]{1,0:T(8,128)(2,1)S(1)}, u32[]{:S(2)}, u32[]{:S(2)}) %collective-permute-start.18) | collective-permute-done | bytes 294944 | tf_op jit(solution)/shard_map/ppermute | solution.py:358
  129.7 0.2 collective-permute-start.23
  129.9 5.0 %collective-permute-done.19.refs_3_ = bf16[1152,128]{1,0:T(8,128)(2,1)S(1)} collective-permute-done((bf16[1152,128]{1,0:T(8,128)(2,1)}, bf16[1152,128]{1,0:T(8,128)(2,1)S(1)}, u32[]{:S(2)}, u32[]{:S(2)}) %collective-permute-start.19) | collective-permute-done | bytes 294944 | tf_op jit(solution)/shard_map/ppermute | solution.py:358
  134.9 14.7 %collective-permute-done.21.refs_5_ = bf16[1152,128]{1,0:T(8,128)(2,1)S(1)} collective-permute-done((bf16[1152,128]{1,0:T(8,128)(2,1)}, bf16[1152,128]{1,0:T(8,128)(2,1)S(1)}, u32[]{:S(2)}, u32[]{:S(2)}) %collective-permute-start.21) | collective-permute-done | bytes 294944 | tf_op jit(solution)/shard_map/ppermute | solution.py:358
  149.6 0.7 copy-done.8
  150.5 3.7 %shard_map.92 = (bf16[384,1024]{1,0:T(8,128)(2,1)}, bf16[384,1024]{1,0:T(8,128)(2,1)}, bf16[384,1024]{1,0:T(8,128)(2,1)}) custom-call(s32[1]{0:T(128)} %bitcast.me_s, bf16[1152,128]{1,0:T(8,128)(2,1)} %get-tuple-element.93.refs_0_, bf16[1152,128]{1,0:T(8,128)(2,1)} %copy-done.4, bf16[1152,128]{1,0:T(8,128)(2,1)} %copy-done.5, bf16[1152,128]{1,0:T(8,128)(2,1)} %copy-done.6, ...), custom_call_target="tpu_custom_call" | custom-call | tf_op jit(solution)/shard_map/pallas_call | solution.py:73
  (59 shorter events, 0.5 us)
Async XLA Ops:
  0.6 3.7 %copy-start.2 = (bf16[384,1024]{1,0:T(8,128)(2,1)S(1)}, bf16[384,1024]{1,0:T(8,128)(2,1)}, u32[]{:S(2)}) copy-start(bf16[384,1024]{1,0:T(8,128)(2,1)} %refs_0_) | copy-start | bytes 2359300
  4.4 22.6 %collective-permute-start = (bf16[384,1024]{1,0:T(8,128)(2,1)S(1)}, bf16[384,1024]{1,0:T(8,128)(2,1)S(1)}, u32[]{:S(2)}, u32[]{:S(2)}) collective-permute-start(bf16[384,1024]{1,0:T(8,128)(2,1)S(1)} %copy-done.2), channel_id=1, source_target_pairs={{0,1},{1,2},{2,3},{3,0},{4,5},{5,6},{6,7},{7,4},{8,9},{9,10},{10,1... | collective-permute-start | bytes 2359304 | tf_op jit(solution)/shard_map/ppermute | solution.py:361
  7.4 11.2 %collective-permute-start.1 = (bf16[1168,128]{1,0:T(8,128)(2,1)}, bf16[1168,128]{1,0:T(8,128)(2,1)S(1)}, u32[]{:S(2)}, u32[]{:S(2)}) collective-permute-start(bf16[1168,128]{1,0:T(8,128)(2,1)} %get-tuple-element.54), channel_id=1, source_target_pairs={{0,24},{4,28},{8,16},{12,20},{16,8},{20,12},{24,0},{28,4},{1,25},{... | collective-permute-start | bytes 897032 | tf_op jit(solution)/shard_map/ppermute | solution.py:358
  9.8 13.6 %collective-permute-start.2 = (bf16[1168,128]{1,0:T(8,128)(2,1)}, bf16[1168,128]{1,0:T(8,128)(2,1)S(1)}, u32[]{:S(2)}, u32[]{:S(2)}) collective-permute-start(bf16[1168,128]{1,0:T(8,128)(2,1)} %get-tuple-element.55), channel_id=1, source_target_pairs={{0,16},{4,20},{8,24},{12,28},{16,0},{20,4},{24,8},{28,12},{1,17},{... | collective-permute-start | bytes 897032 | tf_op jit(solution)/shard_map/ppermute | solution.py:358
  10.3 13.2 %collective-permute-start.3 = (bf16[1168,128]{1,0:T(8,128)(2,1)}, bf16[1168,128]{1,0:T(8,128)(2,1)S(1)}, u32[]{:S(2)}, u32[]{:S(2)}) collective-permute-start(bf16[1168,128]{1,0:T(8,128)(2,1)} %get-tuple-element.56), channel_id=1, source_target_pairs={{0,8},{4,12},{8,0},{12,4},{16,24},{20,28},{24,16},{28,20},{1,9},{5... | collective-permute-start | bytes 897032 | tf_op jit(solution)/shard_map/ppermute | solution.py:358
  11.5 16.6 %copy-start.16 = (bf16[1168,128]{1,0:T(8,128)(2,1)S(1)}, bf16[1168,128]{1,0:T(8,128)(2,1)}, u32[]{:S(2)}) copy-start(bf16[1168,128]{1,0:T(8,128)(2,1)} %get-tuple-element.60) | copy-start | bytes 897028
  11.5 18.1 %copy-start.15 = (bf16[1168,128]{1,0:T(8,128)(2,1)S(1)}, bf16[1168,128]{1,0:T(8,128)(2,1)}, u32[]{:S(2)}) copy-start(bf16[1168,128]{1,0:T(8,128)(2,1)} %get-tuple-element.61) | copy-start | bytes 897028
  11.5 18.3 %copy-start.14 = (bf16[1168,128]{1,0:T(8,128)(2,1)S(1)}, bf16[1168,128]{1,0:T(8,128)(2,1)}, u32[]{:S(2)}) copy-start(bf16[1168,128]{1,0:T(8,128)(2,1)} %get-tuple-element.62) | copy-start | bytes 897028
  18.6 18.1 %copy-start.11 = (bf16[1168,128]{1,0:T(8,128)(2,1)}, bf16[1168,128]{1,0:T(8,128)(2,1)S(1)}, u32[]{:S(2)}) copy-start(bf16[1168,128]{1,0:T(8,128)(2,1)S(1)} %collective-permute-done.1.refs_6_) | copy-start | bytes 897028
  23.5 13.2 %copy-start.12 = (bf16[1168,128]{1,0:T(8,128)(2,1)}, bf16[1168,128]{1,0:T(8,128)(2,1)S(1)}, u32[]{:S(2)}) copy-start(bf16[1168,128]{1,0:T(8,128)(2,1)S(1)} %collective-permute-done.2.refs_4_) | copy-start | bytes 897028
  23.6 13.1 %copy-start.13 = (bf16[1168,128]{1,0:T(8,128)(2,1)}, bf16[1168,128]{1,0:T(8,128)(2,1)S(1)}, u32[]{:S(2)}) copy-start(bf16[1168,128]{1,0:T(8,128)(2,1)S(1)} %collective-permute-done.3.refs_2_) | copy-start | bytes 897028
  26.9 3.9 %copy-start = (bf16[384,1024]{1,0:T(8,128)(2,1)}, bf16[384,1024]{1,0:T(8,128)(2,1)S(1)}, u32[]{:S(2)}) copy-start(bf16[384,1024]{1,0:T(8,128)(2,1)S(1)} %collective-permute-done.refs_0_) | copy-start | bytes 2359300
  27.0 20.5 %collective-permute-start.4 = (bf16[384,1024]{1,0:T(8,128)(2,1)S(1)}, bf16[384,1024]{1,0:T(8,128)(2,1)S(1)}, u32[]{:S(2)}, u32[]{:S(2)}) collective-permute-start(bf16[384,1024]{1,0:T(8,128)(2,1)S(1)} %collective-permute-done.refs_0_), channel_id=1, source_target_pairs={{0,1},{1,2},{2,3},{3,0},{4,5},{5,6},{6,7},{7,4},{8,9},{9,10},{10,1... | collective-permute-start | bytes 2359304 | tf_op jit(solution)/shard_map/ppermute | solution.py:361
  27.0 10.6 %collective-permute-start.5 = (bf16[1168,128]{1,0:T(8,128)(2,1)}, bf16[1168,128]{1,0:T(8,128)(2,1)}, u32[]{:S(2)}, u32[]{:S(2)}) collective-permute-start(bf16[1168,128]{1,0:T(8,128)(2,1)} %get-tuple-element.59), channel_id=1, source_target_pairs={{0,28},{4,24},{8,20},{12,16},{16,12},{20,8},{24,4},{28,0},{1,29},{... | collective-permute-start | bytes 897032 | tf_op jit(solution)/shard_map/ppermute | solution.py:358
  28.0 15.8 %collective-permute-start.6 = (bf16[1168,128]{1,0:T(8,128)(2,1)S(1)}, bf16[1168,128]{1,0:T(8,128)(2,1)}, u32[]{:S(2)}, u32[]{:S(2)}) collective-permute-start(bf16[1168,128]{1,0:T(8,128)(2,1)S(1)} %copy-done.16), channel_id=1, source_target_pairs={{0,20},{4,16},{8,28},{12,24},{16,4},{20,0},{24,12},{28,8},{1,21},{... | collective-permute-start | bytes 897032 | tf_op jit(solution)/shard_map/ppermute | solution.py:358
  29.6 14.2 %collective-permute-start.7 = (bf16[1168,128]{1,0:T(8,128)(2,1)S(1)}, bf16[1168,128]{1,0:T(8,128)(2,1)}, u32[]{:S(2)}, u32[]{:S(2)}) collective-permute-start(bf16[1168,128]{1,0:T(8,128)(2,1)S(1)} %copy-done.15), channel_id=1, source_target_pairs={{0,12},{4,8},{8,4},{12,0},{16,28},{20,24},{24,20},{28,16},{1,13},{... | collective-permute-start | bytes 897032 | tf_op jit(solution)/shard_map/ppermute | solution.py:358
  29.8 14.1 %collective-permute-start.8 = (bf16[1168,128]{1,0:T(8,128)(2,1)S(1)}, bf16[1168,128]{1,0:T(8,128)(2,1)}, u32[]{:S(2)}, u32[]{:S(2)}) collective-permute-start(bf16[1168,128]{1,0:T(8,128)(2,1)S(1)} %copy-done.14), channel_id=1, source_target_pairs={{0,4},{4,0},{8,12},{12,8},{16,20},{20,16},{24,28},{28,24},{1,5},{5... | collective-permute-start | bytes 897032 | tf_op jit(solution)/shard_map/ppermute | solution.py:358
  47.5 22.8 %copy-start.1 = (bf16[384,1024]{1,0:T(8,128)(2,1)}, bf16[384,1024]{1,0:T(8,128)(2,1)S(1)}, u32[]{:S(2)}) copy-start(bf16[384,1024]{1,0:T(8,128)(2,1)S(1)} %collective-permute-done.4.refs_0_) | copy-start | bytes 2359300
  47.5 28.5 %collective-permute-start.9 = (bf16[384,1024]{1,0:T(8,128)(2,1)S(1)}, bf16[384,1024]{1,0:T(8,128)(2,1)S(1)}, u32[]{:S(2)}, u32[]{:S(2)}) collective-permute-start(bf16[384,1024]{1,0:T(8,128)(2,1)S(1)} %collective-permute-done.4.refs_0_), channel_id=1, source_target_pairs={{0,1},{1,2},{2,3},{3,0},{4,5},{5,6},{6,7},{7,4},{8,9},{9,10},{10,1... | collective-permute-start | bytes 2359304 | tf_op jit(solution)/shard_map/ppermute | solution.py:361
  76.0 0.9 copy-start.3
  82.6 3.6 %collective-permute-start.10 = (bf16[384,128]{1,0:T(8,128)(2,1)}, bf16[384,128]{1,0:T(8,128)(2,1)S(1)}, u32[]{:S(2)}, u32[]{:S(2)}) collective-permute-start(bf16[384,128]{1,0:T(8,128)(2,1)} %get-tuple-element.86), channel_id=1, source_target_pairs={{0,4},{4,0},{8,12},{12,8},{16,20},{20,16},{24,28},{28,24},{1,5},{5... | collective-permute-start | bytes 294920 | tf_op jit(solution)/shard_map/ppermute | solution.py:358
  82.6 5.9 %collective-permute-start.11 = (bf16[384,128]{1,0:T(8,128)(2,1)}, bf16[384,128]{1,0:T(8,128)(2,1)S(1)}, u32[]{:S(2)}, u32[]{:S(2)}) collective-permute-start(bf16[384,128]{1,0:T(8,128)(2,1)} %get-tuple-element.87), channel_id=1, source_target_pairs={{0,8},{4,12},{8,0},{12,4},{16,24},{20,28},{24,16},{28,20},{1,9},{5... | collective-permute-start | bytes 294920 | tf_op jit(solution)/shard_map/ppermute | solution.py:358
  83.9 5.8 %collective-permute-start.12 = (bf16[384,128]{1,0:T(8,128)(2,1)}, bf16[384,128]{1,0:T(8,128)(2,1)S(1)}, u32[]{:S(2)}, u32[]{:S(2)}) collective-permute-start(bf16[384,128]{1,0:T(8,128)(2,1)} %get-tuple-element.88), channel_id=1, source_target_pairs={{0,12},{4,8},{8,4},{12,0},{16,28},{20,24},{24,20},{28,16},{1,13},{... | collective-permute-start | bytes 294920 | tf_op jit(solution)/shard_map/ppermute | solution.py:358
  84.5 5.8 %collective-permute-start.13 = (bf16[384,128]{1,0:T(8,128)(2,1)}, bf16[384,128]{1,0:T(8,128)(2,1)S(1)}, u32[]{:S(2)}, u32[]{:S(2)}) collective-permute-start(bf16[384,128]{1,0:T(8,128)(2,1)} %get-tuple-element.89), channel_id=1, source_target_pairs={{0,16},{4,20},{8,24},{12,28},{16,0},{20,4},{24,8},{28,12},{1,17},{... | collective-permute-start | bytes 294920 | tf_op jit(solution)/shard_map/ppermute | solution.py:358
  85.8 9.7 %collective-permute-start.14 = (bf16[384,128]{1,0:T(8,128)(2,1)}, bf16[384,128]{1,0:T(8,128)(2,1)S(1)}, u32[]{:S(2)}, u32[]{:S(2)}) collective-permute-start(bf16[384,128]{1,0:T(8,128)(2,1)} %get-tuple-element.90), channel_id=1, source_target_pairs={{0,20},{4,16},{8,28},{12,24},{16,4},{20,0},{24,12},{28,8},{1,21},{... | collective-permute-start | bytes 294920 | tf_op jit(solution)/shard_map/ppermute | solution.py:358
  86.2 9.3 %copy-start.17 = (bf16[384,128]{1,0:T(8,128)(2,1)}, bf16[384,128]{1,0:T(8,128)(2,1)S(1)}, u32[]{:S(2)}) copy-start(bf16[384,128]{1,0:T(8,128)(2,1)S(1)} %collective-permute-done.10.refs_1_) | copy-start | bytes 294916
  86.2 9.3 %collective-permute-start.15 = (bf16[384,128]{1,0:T(8,128)(2,1)}, bf16[384,128]{1,0:T(8,128)(2,1)S(1)}, u32[]{:S(2)}, u32[]{:S(2)}) collective-permute-start(bf16[384,128]{1,0:T(8,128)(2,1)} %get-tuple-element.91), channel_id=1, source_target_pairs={{0,24},{4,28},{8,16},{12,20},{16,8},{20,12},{24,0},{28,4},{1,25},{... | collective-permute-start | bytes 294920 | tf_op jit(solution)/shard_map/ppermute | solution.py:358
  88.5 7.0 %copy-start.18 = (bf16[384,128]{1,0:T(8,128)(2,1)}, bf16[384,128]{1,0:T(8,128)(2,1)S(1)}, u32[]{:S(2)}) copy-start(bf16[384,128]{1,0:T(8,128)(2,1)S(1)} %collective-permute-done.11.refs_2_) | copy-start | bytes 294916
  88.5 7.0 %collective-permute-start.16 = (bf16[384,128]{1,0:T(8,128)(2,1)}, bf16[384,128]{1,0:T(8,128)(2,1)S(1)}, u32[]{:S(2)}, u32[]{:S(2)}) collective-permute-start(bf16[384,128]{1,0:T(8,128)(2,1)} %get-tuple-element.92), channel_id=1, source_target_pairs={{0,28},{4,24},{8,20},{12,16},{16,12},{20,8},{24,4},{28,0},{1,29},{... | collective-permute-start | bytes 294920 | tf_op jit(solution)/shard_map/ppermute | solution.py:358
  89.7 5.8 %copy-start.19 = (bf16[384,128]{1,0:T(8,128)(2,1)}, bf16[384,128]{1,0:T(8,128)(2,1)S(1)}, u32[]{:S(2)}) copy-start(bf16[384,128]{1,0:T(8,128)(2,1)S(1)} %collective-permute-done.12.refs_3_) | copy-start | bytes 294916
  90.3 5.2 %copy-start.20 = (bf16[384,128]{1,0:T(8,128)(2,1)}, bf16[384,128]{1,0:T(8,128)(2,1)S(1)}, u32[]{:S(2)}) copy-start(bf16[384,128]{1,0:T(8,128)(2,1)S(1)} %collective-permute-done.13.refs_4_) | copy-start | bytes 294916
  95.5 0.6 copy-start.21
  95.5 0.7 copy-start.22
  95.5 0.7 copy-start.23
  119.2 4.0 %collective-permute-start.17 = (bf16[1152,128]{1,0:T(8,128)(2,1)}, bf16[1152,128]{1,0:T(8,128)(2,1)S(1)}, u32[]{:S(2)}, u32[]{:S(2)}) collective-permute-start(bf16[1152,128]{1,0:T(8,128)(2,1)} %get-tuple-element.94), channel_id=1, source_target_pairs={{0,4},{4,0},{8,12},{12,8},{16,20},{20,16},{24,28},{28,24},{1,5},{5... | collective-permute-start | bytes 884744 | tf_op jit(solution)/shard_map/ppermute | solution.py:358
  119.6 10.1 %collective-permute-start.18 = (bf16[1152,128]{1,0:T(8,128)(2,1)}, bf16[1152,128]{1,0:T(8,128)(2,1)S(1)}, u32[]{:S(2)}, u32[]{:S(2)}) collective-permute-start(bf16[1152,128]{1,0:T(8,128)(2,1)} %get-tuple-element.95), channel_id=1, source_target_pairs={{0,8},{4,12},{8,0},{12,4},{16,24},{20,28},{24,16},{28,20},{1,9},{5... | collective-permute-start | bytes 884744 | tf_op jit(solution)/shard_map/ppermute | solution.py:358
  120.9 14.0 %collective-permute-start.19 = (bf16[1152,128]{1,0:T(8,128)(2,1)}, bf16[1152,128]{1,0:T(8,128)(2,1)S(1)}, u32[]{:S(2)}, u32[]{:S(2)}) collective-permute-start(bf16[1152,128]{1,0:T(8,128)(2,1)} %get-tuple-element.96), channel_id=1, source_target_pairs={{0,12},{4,8},{8,4},{12,0},{16,28},{20,24},{24,20},{28,16},{1,13},{... | collective-permute-start | bytes 884744 | tf_op jit(solution)/shard_map/ppermute | solution.py:358
  121.1 13.8 %collective-permute-start.20 = (bf16[1152,128]{1,0:T(8,128)(2,1)}, bf16[1152,128]{1,0:T(8,128)(2,1)S(1)}, u32[]{:S(2)}, u32[]{:S(2)}) collective-permute-start(bf16[1152,128]{1,0:T(8,128)(2,1)} %get-tuple-element.97), channel_id=1, source_target_pairs={{0,16},{4,20},{8,24},{12,28},{16,0},{20,4},{24,8},{28,12},{1,17},{... | collective-permute-start | bytes 884744 | tf_op jit(solution)/shard_map/ppermute | solution.py:358
  122.4 27.2 %collective-permute-start.21 = (bf16[1152,128]{1,0:T(8,128)(2,1)}, bf16[1152,128]{1,0:T(8,128)(2,1)S(1)}, u32[]{:S(2)}, u32[]{:S(2)}) collective-permute-start(bf16[1152,128]{1,0:T(8,128)(2,1)} %get-tuple-element.98), channel_id=1, source_target_pairs={{0,20},{4,16},{8,28},{12,24},{16,4},{20,0},{24,12},{28,8},{1,21},{... | collective-permute-start | bytes 884744 | tf_op jit(solution)/shard_map/ppermute | solution.py:358
  123.2 26.4 %copy-start.4 = (bf16[1152,128]{1,0:T(8,128)(2,1)}, bf16[1152,128]{1,0:T(8,128)(2,1)S(1)}, u32[]{:S(2)}) copy-start(bf16[1152,128]{1,0:T(8,128)(2,1)S(1)} %collective-permute-done.17.refs_1_) | copy-start | bytes 884740
  123.2 26.4 %collective-permute-start.22 = (bf16[1152,128]{1,0:T(8,128)(2,1)}, bf16[1152,128]{1,0:T(8,128)(2,1)S(1)}, u32[]{:S(2)}, u32[]{:S(2)}) collective-permute-start(bf16[1152,128]{1,0:T(8,128)(2,1)} %get-tuple-element.99), channel_id=1, source_target_pairs={{0,24},{4,28},{8,16},{12,20},{16,8},{20,12},{24,0},{28,4},{1,25},{... | collective-permute-start | bytes 884744 | tf_op jit(solution)/shard_map/ppermute | solution.py:358
  129.7 19.9 %copy-start.5 = (bf16[1152,128]{1,0:T(8,128)(2,1)}, bf16[1152,128]{1,0:T(8,128)(2,1)S(1)}, u32[]{:S(2)}) copy-start(bf16[1152,128]{1,0:T(8,128)(2,1)S(1)} %collective-permute-done.18.refs_2_) | copy-start | bytes 884740
  129.7 19.9 %collective-permute-start.23 = (bf16[1152,128]{1,0:T(8,128)(2,1)}, bf16[1152,128]{1,0:T(8,128)(2,1)S(1)}, u32[]{:S(2)}, u32[]{:S(2)}) collective-permute-start(bf16[1152,128]{1,0:T(8,128)(2,1)} %get-tuple-element.100), channel_id=1, source_target_pairs={{0,28},{4,24},{8,20},{12,16},{16,12},{20,8},{24,4},{28,0},{1,29},{... | collective-permute-start | bytes 884744 | tf_op jit(solution)/shard_map/ppermute | solution.py:358
  134.9 14.7 %copy-start.6 = (bf16[1152,128]{1,0:T(8,128)(2,1)}, bf16[1152,128]{1,0:T(8,128)(2,1)S(1)}, u32[]{:S(2)}) copy-start(bf16[1152,128]{1,0:T(8,128)(2,1)S(1)} %collective-permute-done.19.refs_3_) | copy-start | bytes 884740
  134.9 14.7 %copy-start.7 = (bf16[1152,128]{1,0:T(8,128)(2,1)}, bf16[1152,128]{1,0:T(8,128)(2,1)S(1)}, u32[]{:S(2)}) copy-start(bf16[1152,128]{1,0:T(8,128)(2,1)S(1)} %collective-permute-done.20.refs_4_) | copy-start | bytes 884740
  149.6 0.7 copy-start.8
  149.6 0.8 copy-start.9
  149.6 0.9 copy-start.10
where the time goes:
time: 152 us; the launch traced here: 154 us
  Pallas kernels  75.1 us (49%)
  waiting for transfers between devices  50.8 us (33%)
  starting transfers between devices  23 us (15%)
  local copies, waits for them, and re-layouts  2.48 us (2%)
  other arithmetic  1.94 us (1%)
    ppermute x21, waiting for transfers between devices, exchange(): lax.ppermute(x, 'seq', [(i, i ^ d) for i in range(peers)])  43.8 us
    pallas_call x1, Pallas kernels, attention_backward(): pl.pallas_call(functools.partial(backward_kernel, peers, heads, rows, bq,...  23 us
    pallas_call x4, Pallas kernels, project(): pl.pallas_call(kernel, grid_spec=pltpu.PrefetchScalarGridSpec(num_scalar_...  22.7 us
    pallas_call x1, Pallas kernels, attention_forward(): pl.pallas_call(functools.partial(forward_kernel, peers, heads, rows, bq,...  22.1 us
    ppermute x21, starting transfers between devices, exchange(): lax.ppermute(x, 'seq', [(i, i ^ d) for i in range(peers)])  20 us
    ppermute x3, waiting for transfers between devices, pass_on(): lax.ppermute(x, 'head', [(i, (i + 1) % groups) for i in range(groups)])  7.03 us
    pallas_call x1, Pallas kernels, pack_heads(): pl.pallas_call(functools.partial(pack_kernel, heads, rows), in_specs=[SME...  3.71 us
    pallas_call x1, Pallas kernels, unpack_heads(): pl.pallas_call(functools.partial(unpack_kernel, heads, rows), in_specs=[S...  3.66 us
  transfers between devices with their start and end apart: 24, of which 14 were waited for; matrix products, arithmetic and copies ran while one was open for 1% of the time, Pallas kernels for 25%

commit v1 on v0

--- a/solution.py
+++ b/solution.py
@@ -79,61 +79,50 @@
     )(me, *blocks)
 
 
-def project_kernel(first, where_s, *refs):
-    if first:
-        o_ref, w_ref, out_ref = refs
-        out_ref[...] = dot32(o_ref[...], w_ref[...], NT)
-    else:
-        o_ref, w_ref, acc_ref, out_ref = refs
-        out_ref[...] = acc_ref[...] + dot32(o_ref[...], w_ref[...], NT)
-
-
-def project_last_kernel(where_s, o_ref, w_ref, acc_ref, *outs):
-    step = pl.program_id(0)
-    both = (acc_ref[...] + dot32(o_ref[...], w_ref[...], NT)).astype(jnp.bfloat16)
-    odd = where_s[1] == 1
-    near = jnp.where(odd, both[:, HD:], both[:, :HD])
-    far = jnp.where(odd, both[:, :HD], both[:, HD:])
-    for j in range(len(outs) // 2):
-
-        @pl.when(step == j)
-        def _():
-            outs[2 * j][...] = near
-            outs[2 * j + 1][...] = far
-
-
-def project(me, block, weight, features, acc, last):
+def project_kernel(first, o_ref, w_ref, *refs):
+    out_ref = refs[-1]
+    for pair in range(w_ref.shape[1] // (2 * HD)):
+        columns = slice(pair * 2 * HD, (pair + 1) * 2 * HD)
+        both = dot32(o_ref[...], w_ref[:, columns])
+        out_ref[:, columns] = both if first else refs[0][:, columns] + both
+
+
+def project_last_kernel(me_s, o_ref, w_ref, acc_ref, *outs):
+    pairs = len(outs) // 2
+    odd = lax.rem(me_s[0], 2) == 1
+    for j in range(pairs):
+        columns = aligned(lax.rem(me_s[0] // 2, pairs) ^ j, 2 * HD)
+        both = (acc_ref[:, columns] + dot32(o_ref[...], w_ref[:, columns])).astype(jnp.bfloat16)
+        outs[2 * j][...] = jnp.where(odd, both[:, HD:], both[:, :HD])
+        outs[2 * j + 1][...] = jnp.where(odd, both[:, :HD], both[:, HD:])
+
+
+def project(me, weight, features, acc, last):
     rows, width = features.shape
-    pairs = weight.shape[0] // (2 * HD)
-    where = jnp.stack([block, lax.rem(me, 2), lax.rem(me // 2, pairs)])
-    feature_spec = pl.BlockSpec((rows, width), lambda j, w: (0, 0))
-    weight_spec = pl.BlockSpec((2 * HD, width), lambda j, w: (w[2] ^ j, w[0]))
-    acc_spec = pl.BlockSpec((rows, 2 * HD), lambda j, w: (0, w[2] ^ j))
+    columns = weight.shape[1]
     cost = pl.CostEstimate(
-        flops=2 * rows * width * weight.shape[0],
-        bytes_accessed=2 * width * weight.shape[0] + 8 * rows * weight.shape[0],
+        flops=2 * rows * width * columns,
+        bytes_accessed=2 * width * columns + 8 * rows * columns,
         transcendentals=0,
     )
     if last:
-        kernel = project_last_kernel
-        out_specs = [pl.BlockSpec((rows, HD), lambda j, w: (0, 0))] * (2 * pairs)
-        out_shape = [jax.ShapeDtypeStruct((rows, HD), jnp.bfloat16)] * (2 * pairs)
-    else:
-        kernel = functools.partial(project_kernel, acc is None)
-        out_specs = acc_spec
-        out_shape = jax.ShapeDtypeStruct((rows, weight.shape[0]), jnp.float32)
+        return pl.pallas_call(
+            project_last_kernel,
+            in_specs=[SMEM_SPEC] + [VMEM_SPEC] * 3,
+            out_specs=[VMEM_SPEC] * (columns // HD),
+            out_shape=[jax.ShapeDtypeStruct((rows, HD), jnp.bfloat16)] * (columns // HD),
+            compiler_params=PARAMS,
+            cost_estimate=cost,
+        )(me, features, weight, acc)
+    operands = (features, weight) + (() if acc is None else (acc,))
     return pl.pallas_call(
-        kernel,
-        grid_spec=pltpu.PrefetchScalarGridSpec(
-            num_scalar_prefetch=1,
-            grid=(pairs,),
-            in_specs=[feature_spec, weight_spec] + ([] if acc is None else [acc_spec]),
-            out_specs=out_specs,
-        ),
-        out_shape=out_shape,
+        functools.partial(project_kernel, acc is None),
+        in_specs=[VMEM_SPEC] * len(operands),
+        out_specs=VMEM_SPEC,
+        out_shape=jax.ShapeDtypeStruct((rows, columns), jnp.float32),
         compiler_params=PARAMS,
         cost_estimate=cost,
-    )(where, features, weight, *([] if acc is None else [acc]))
+    )(*operands)
 
 
 def visible(first_row, q0, k0, shape):
@@ -182,8 +171,9 @@
 
 def forward_kernel(peers, heads, rows, bq, bk, me_s, *refs):
     blocks = refs[:peers]
-    q_ref, k_ref, v_ref, first_ref, out_ref, log_ref, plan_q, plan_k, count_ref = refs[peers:peers + 9]
-    own_q, own_k, own_count, qt_ref, vt_ref, doc_ref, sum_ref, s0, top0, s1, top1 = refs[peers + 9:]
+    q_ref, k_ref, v_ref, qt_ref, kt_ref, first_ref, out_ref, log_ref = refs[peers:peers + 8]
+    plan_q, plan_k, count_ref, own_q, own_k, own_count = refs[peers + 8:peers + 14]
+    vt_ref, doc_ref, sum_ref, s0, top0, s1, top1 = refs[peers + 14:]
     total = q_ref.shape[0]
     factor = HD ** (-0.5) * math.log2(math.e)
     me = me_s[0]
@@ -207,6 +197,7 @@
     own = None if heads == peers else (group, group + heads * rows)
     fill_plan(lows, total, bq, bk, own, plan_q, plan_k, count_ref)
     qt_ref[...] = q_ref[...].T
+    kt_ref[...] = k_ref[...].T
     vt_ref[...] = v_ref[...].T
     out_ref[...] = jnp.zeros_like(out_ref)
     log_ref[...] = jnp.full_like(log_ref, NEG_LARGE)
@@ -241,18 +232,16 @@
 
 
 def backward_kernel(peers, heads, rows, bq, bk, me_s, plan_q, plan_k, count_ref, q_ref, k_ref, v_ref,
-                    first_ref, out_ref, log_ref, *refs):
+                    qt_ref, kt_ref, first_ref, out_ref, log_ref, *refs):
     blocks = refs[:peers]
     results = refs[peers:peers + heads]
-    g_ref, qt_ref, gt_ref, kt_ref, dot_ref, dk_acc, dv_acc, dq_acc, p0, ds0, p1, ds1 = refs[peers + heads:]
+    g_ref, gt_ref, dot_ref, dk_acc, dv_acc, dq_acc, p0, ds0, p1, ds1 = refs[peers + heads:]
     scale = HD ** (-0.5)
     factor = scale * math.log2(math.e)
     me = me_s[0]
     for d, block in enumerate(blocks):
         g_ref[aligned(me ^ d, rows), :] = block[...]
-    qt_ref[...] = q_ref[...].T
     gt_ref[...] = g_ref[...].T
-    kt_ref[...] = k_ref[...].T
     dot_ref[...] = jnp.sum(gt_ref[...].astype(jnp.float32) * out_ref[...], axis=0, keepdims=True)
     dk_acc[...] = jnp.zeros_like(dk_acc)
     dv_acc[...] = jnp.zeros_like(dv_acc)
@@ -277,7 +266,7 @@
     pipelined(plan_q, plan_k, count_ref, early, late, ((p0, ds0), (p1, ds1)))
     for d, result in enumerate(results):
         own = aligned(me ^ d, rows)
-        result[:rows, :] = (scale * dq_acc[:, own]).T.astype(result.dtype)
+        result[:rows, :] = (scale * dq_acc[:, own]).astype(result.dtype).T
         result[rows:2 * rows, :] = (scale * dk_acc[own, :]).astype(result.dtype)
         result[2 * rows:, :] = dv_acc[own, :].astype(result.dtype)
 
@@ -298,8 +287,9 @@
     return pl.pallas_call(
         functools.partial(forward_kernel, peers, heads, rows, bq, bk),
         in_specs=[SMEM_SPEC] + [VMEM_SPEC] * peers,
-        out_specs=[VMEM_SPEC] * 6 + [SMEM_SPEC] * 3,
+        out_specs=[VMEM_SPEC] * 8 + [SMEM_SPEC] * 3,
         out_shape=[jax.ShapeDtypeStruct((total, HD), jnp.bfloat16)] * 3
+        + [jax.ShapeDtypeStruct((HD, total), jnp.bfloat16)] * 2
         + [
             jax.ShapeDtypeStruct((1, total), jnp.int32),
             jax.ShapeDtypeStruct((HD, total), jnp.float32),
@@ -313,7 +303,6 @@
             pltpu.SMEM((size,), jnp.int32),
             pltpu.SMEM((1,), jnp.int32),
             pltpu.VMEM((HD, total), jnp.bfloat16),
-            pltpu.VMEM((HD, total), jnp.bfloat16),
             pltpu.VMEM((1, total), jnp.float32),
             pltpu.VMEM((1, total), jnp.float32),
         ]
@@ -329,13 +318,11 @@
     bq, bk = block_size(total, 512), block_size(total, 256)
     return pl.pallas_call(
         functools.partial(backward_kernel, peers, heads, rows, bq, bk),
-        in_specs=[SMEM_SPEC] * 4 + [VMEM_SPEC] * (6 + peers),
+        in_specs=[SMEM_SPEC] * 4 + [VMEM_SPEC] * (8 + peers),
         out_specs=[VMEM_SPEC] * heads,
         out_shape=[jax.ShapeDtypeStruct((3 * rows, HD), jnp.bfloat16)] * heads,
         scratch_shapes=[
             pltpu.VMEM((total, HD), jnp.bfloat16),
-            pltpu.VMEM((HD, total), jnp.bfloat16),
-            pltpu.VMEM((HD, total), jnp.bfloat16),
             pltpu.VMEM((HD, total), jnp.bfloat16),
             pltpu.VMEM((1, total), jnp.float32),
             pltpu.VMEM((total, HD), jnp.float32),
@@ -345,7 +332,7 @@
         + [pltpu.VMEM((bk, bq), jnp.bfloat16)] * 4,
         compiler_params=PARAMS,
         cost_estimate=attention_cost(total, 5),
-    )(me, *state[6:], *state[:6], *blocks)
+    )(me, *state[8:], *state[:8], *blocks)
 
 
 def per_device(peers, groups, queries, keys_in, values, out_grad, out_weight, doc_ids):
@@ -371,23 +358,25 @@
 
     after = lax.optimization_barrier
     features, acc = out_grad, None
+    weights = []
     for step in range(groups):
         block = lax.rem(lax.axis_index("head") + groups - step, groups)
+        weights.append(lax.dynamic_slice_in_dim(out_weight, block * width, width, 1).T)
+    for step in range(groups):
         last = step == groups - 1
-        if step == 0:
-            features, packed[0] = after((features, packed[0]))
         if not last:
             passed = pass_on(features)
         if step == groups - 2:
             received[0], features = after((received[0], features))
             state = list(attention_forward(me_vector, received, rows, heads))
             features, state[1] = after((features, state[1]))
-        acc = project(me, block, out_weight, features, acc, last)
+        acc = project(me_vector, weights[step], features, acc, last)
         if not last:
             features = passed
             if step < groups - 2:
                 batch = order[step * len(order) // (groups - 2):(step + 1) * len(order) // (groups - 2)]
-                features, acc, here = after((features, acc, [received[d] for d in batch]))
+                here = [received[d] for d in batch]
+                features, acc, here, weights[2:] = after((features, acc, here, weights[2:]))
                 for d, block in zip(batch, here):
                     received[d] = block
     grads = exchange_all(acc, peers)

time: 152 us -> 153 us (level); the launches traced: 154 us -> 153 us
  local copies, waits for them, and re-layouts: 2.48 us -> 23.3 us
  waiting for transfers between devices: 50.8 us -> 37.6 us
  Pallas kernels: 75.1 us -> 66.4 us
  starting transfers between devices: 23 us -> 25.4 us
  other arithmetic: 1.94 us -> 0 us
    unnamed x48 -> x40, local copies, waits for them, and re-layouts: 2.48 us -> 16.8 us
    ppermute x21, waiting for transfers between devices: 43.8 us -> 36 us  [exchange(): lax.ppermute(x, 'seq', [(i, i ^ d) for i in range(peers)])]
    dynamic_slice x0 -> x1, local copies, waits for them, and re-layouts: none -> 6.44 us  [per_device(): lax.dynamic_slice_in_dim(out_weight, block * width, width, 1)]
    pallas_call x4, Pallas kernels: 22.7 us -> 17 us  [the longest x3 12.9 us: project(): pl.pallas_call(functools.partial(project_kernel, acc is None), in_specs=[...]
    ppermute x3, waiting for transfers between devices: 7.03 us -> 1.57 us  [pass_on(): lax.ppermute(x, 'head', [(i, (i + 1) % groups) for i in range(groups)])]
    another operation x3 -> x0, other arithmetic: 1.94 us -> none  [project(): where = jnp.stack([block, lax.rem(me, 2), lax.rem(me // 2, pairs)])]
    ppermute x3, starting transfers between devices: 3.03 us -> 4.78 us  [pass_on(): lax.ppermute(x, 'head', [(i, (i + 1) % groups) for i in range(groups)])]
    pallas_call x1, Pallas kernels: 23 us -> 21.3 us  [attention_backward(): pl.pallas_call(functools.partial(backward_kernel, peers, heads, rows, bq,...]
  transfers between devices with their start and end apart: 24 -> 24, of which waited for: 14 -> 8; matrix products, arithmetic and copies ran while one was open for 1% -> 14% of each run, Pallas kernels for 25% -> 24%
where the time goes in v1:
time: 153 us
  Pallas kernels  66.4 us (43%)
  waiting for transfers between devices  37.6 us (25%)
  starting transfers between devices  25.4 us (17%)
  local copies, waits for them, and re-layouts  23.3 us (15%)
    ppermute x21, waiting for transfers between devices, exchange(): lax.ppermute(x, 'seq', [(i, i ^ d) for i in range(peers)])  36 us
    pallas_call x1, Pallas kernels, attention_backward(): pl.pallas_call(functools.partial(backward_kernel, peers, heads, rows, bq,...  21.3 us
    pallas_call x1, Pallas kernels, attention_forward(): pl.pallas_call(functools.partial(forward_kernel, peers, heads, rows, bq,...  20.7 us
    ppermute x21, starting transfers between devices, exchange(): lax.ppermute(x, 'seq', [(i, i ^ d) for i in range(peers)])  20.6 us
    unnamed x40, local copies, waits for them, and re-layouts  16.8 us
    pallas_call x3, Pallas kernels, project(): pl.pallas_call(functools.partial(project_kernel, acc is None), in_specs=[...  12.9 us
    dynamic_slice x1, local copies, waits for them, and re-layouts, per_device(): lax.dynamic_slice_in_dim(out_weight, block * width, width, 1)  6.44 us
    ppermute x3, starting transfers between devices, pass_on(): lax.ppermute(x, 'head', [(i, (i + 1) % groups) for i in range(groups)])  4.78 us
  transfers between devices with their start and end apart: 24, of which 8 were waited for; matrix products, arithmetic and copies ran while one was open for 14% of the time, Pallas kernels for 24%

profile of v1, /device:TPU:0, one launch (start us, length us, event | category | flops | bytes accessed | tf_op | source)
XLA Modules:
  0.0 153.4 jit_solution(12827025801538973847)
XLA Ops:
  0.6 3.1 %collective-permute-start = (bf16[384,1024]{1,0:T(8,128)(2,1)}, bf16[384,1024]{1,0:T(8,128)(2,1)S(1)}, u32[]{:S(2)}, u32[]{:S(2)}) collective-permute-start(bf16[384,1024]{1,0:T(8,128)(2,1)} %o_ref.1), channel_id=1, source_target_pairs={{0,1},{1,2},{2,3},{3,0},{4,5},{5,6},{6,7},{7,4},{8,9},{9,10},{10,1... | collective-permute-start | bytes 2359304 | tf_op jit(solution)/shard_map/ppermute | solution.py:348
  3.7 3.6 %shard_map.85 = (bf16[1168,128]{1,0:T(8,128)(2,1)}, bf16[1168,128]{1,0:T(8,128)(2,1)}, bf16[1168,128]{1,0:T(8,128)(2,1)}, bf16[1168,128]{1,0:T(8,128)(2,1)}, bf1...) custom-call(s32[1]{0:T(128)} %bitcast.me_s, ...), custom_call_target="tpu_custom_call" | custom-call | tf_op jit(solution)/shard_map/pallas_call | solution.py:54
  7.3 2.4 %collective-permute-start.1 = (bf16[1168,128]{1,0:T(8,128)(2,1)}, bf16[1168,128]{1,0:T(8,128)(2,1)S(1)}, u32[]{:S(2)}, u32[]{:S(2)}) collective-permute-start(bf16[1168,128]{1,0:T(8,128)(2,1)} %get-tuple-element.58), channel_id=1, source_target_pairs={{0,24},{4,28},{8,16},{12,20},{16,8},{20,12},{24,0},{28,4},{1,25},{... | collective-permute-start | bytes 897032 | tf_op jit(solution)/shard_map/ppermute | solution.py:345
  9.8 0.5 collective-permute-start.2
  10.3 0.5 collective-permute-start.3
  10.8 6.4 %constant_dynamic-slice_fusion = (bf16[1024,1024]{1,0:T(8,128)(2,1)S(1)}, bf16[1024,1024]{1,0:T(8,128)(2,1)}, bf16[1024,1024]{1,0:T(8,128)(2,1)}, bf16[1024,1024]{1,0:T(8,128)(2,1)}) fusion(bf16[1024,4096]{1,0:T(8,128)(2,1)} %param.10, s32[]{:T(128)S(6)} %select_n.15, s32[]{:T(128)S(6)} %select_n.14, s32[]{:T(128)S(6)} %select_n.13, s32[]{:T(128)S(6)} %select_n.12), kind=kLoop, calls=%fused_computation | loop fusion | bytes 16777232 | tf_op jit(solution)/shard_map/dynamic_slice | solution.py:364
  17.3 3.9 %copy.13 = bf16[1024,1024]{0,1:T(8,128)(2,1)} copy(bf16[1024,1024]{1,0:T(8,128)(2,1)} %get-tuple-element.114) | data formatting | bytes 4194304
  21.2 3.9 %copy.14 = bf16[1024,1024]{0,1:T(8,128)(2,1)} copy(bf16[1024,1024]{1,0:T(8,128)(2,1)} %get-tuple-element.113) | data formatting | bytes 4194304
  25.1 3.9 %copy.15 = bf16[1024,1024]{0,1:T(8,128)(2,1)} copy(bf16[1024,1024]{1,0:T(8,128)(2,1)} %get-tuple-element.112) | data formatting | bytes 4194304
  29.1 4.0 %shard_map.86.refs_0_ = f32[384,1024]{1,0:T(8,128)} custom-call(bf16[384,1024]{1,0:T(8,128)(2,1)} %o_ref.1, bf16[1024,1024]{1,0:T(8,128)(2,1)} %bitcast.9), custom_call_target="tpu_custom_call" | custom-call | flops 805306368 | bytes 5242880 | tf_op jit(solution)/shard_map/pallas_call | solution.py:118
  33.2 1.6 %collective-permute-start.4 = (bf16[384,1024]{1,0:T(8,128)(2,1)S(1)}, bf16[384,1024]{1,0:T(8,128)(2,1)}, u32[]{:S(2)}, u32[]{:S(2)}) collective-permute-start(bf16[384,1024]{1,0:T(8,128)(2,1)S(1)} %collective-permute-done.o_ref), channel_id=1, source_target_pairs={{0,1},{1,2},{2,3},{3,0},{4,5},{5,6},{6,7},{7,4},{8,9},{9,10},{10,1... | collective-permute-start | bytes 2359304 | tf_op jit(solution)/shard_map/ppermute | solution.py:348
  34.8 0.5 collective-permute-start.5
  35.3 2.2 %collective-permute-start.6 = (bf16[1168,128]{1,0:T(8,128)(2,1)}, bf16[1168,128]{1,0:T(8,128)(2,1)}, u32[]{:S(2)}, u32[]{:S(2)}) collective-permute-start(bf16[1168,128]{1,0:T(8,128)(2,1)} %get-tuple-element.64), channel_id=1, source_target_pairs={{0,20},{4,16},{8,28},{12,24},{16,4},{20,0},{24,12},{28,8},{1,21},{... | collective-permute-start | bytes 897032 | tf_op jit(solution)/shard_map/ppermute | solution.py:345
  37.5 0.1 collective-permute-start.7
  37.5 0.6 collective-permute-start.8
  38.1 2.6 %copy.16 = bf16[1024,1024]{0,1:T(8,128)(2,1)} copy(bf16[1024,1024]{1,0:T(8,128)(2,1)S(1)} %get-tuple-element.111) | data formatting | bytes 4194304
  40.7 4.4 %shard_map.87.refs_0_ = f32[384,1024]{1,0:T(8,128)} custom-call(bf16[384,1024]{1,0:T(8,128)(2,1)} %copy-done.1, bf16[1024,1024]{1,0:T(8,128)(2,1)} %bitcast.7, f32[384,1024]{1,0:T(8,128)} %shard_map.86.refs_0_), custom_call_target="tpu_custom_call" | custom-call | flops 805306368 | bytes 5242880 | tf_op jit(solution)/shard_map/pallas_call | solution.py:118
  45.2 0.3 collective-permute-done.5.refs_7_
  45.4 6.3 %collective-permute-done.6.refs_5_ = bf16[1168,128]{1,0:T(8,128)(2,1)} collective-permute-done((bf16[1168,128]{1,0:T(8,128)(2,1)}, bf16[1168,128]{1,0:T(8,128)(2,1)}, u32[]{:S(2)}, u32[]{:S(2)}) %collective-permute-start.6) | collective-permute-done | bytes 299040 | tf_op jit(solution)/shard_map/ppermute | solution.py:345
  51.7 1.6 %collective-permute-done.4.o_ref = bf16[384,1024]{1,0:T(8,128)(2,1)} collective-permute-done((bf16[384,1024]{1,0:T(8,128)(2,1)S(1)}, bf16[384,1024]{1,0:T(8,128)(2,1)}, u32[]{:S(2)}, u32[]{:S(2)}) %collective-permute-start.4) | collective-permute-done | bytes 786464 | tf_op jit(solution)/shard_map/ppermute | solution.py:348
  53.3 0.1 collective-permute-start.9
  53.4 20.7 %shard_map.88 = (bf16[3072,128]{1,0:T(8,128)(2,1)}, bf16[3072,128]{1,0:T(8,128)(2,1)}, bf16[3072,128]{1,0:T(8,128)(2,1)}, bf16[128,3072]{1,0:T(8,128)(2,1)}, bf1...) custom-call(s32[1]{0:T(128)} %bitcast.me_s, ...), custom_call_target="tpu_custom_call" | custom-call | flops 1811939328 | bytes 6291456 | tf_op jit(solution)/shard_map/pallas_call | solution.py:287
  74.1 4.5 %shard_map.89.acc_ref = f32[384,1024]{1,0:T(8,128)} custom-call(bf16[384,1024]{1,0:T(8,128)(2,1)} %collective-permute-done.4.o_ref, bf16[1024,1024]{1,0:T(8,128)(2,1)} %bitcast.6, f32[384,1024]{1,0:T(8,128)} %shard_map.87.refs_0_), custom_call_target="tpu_custom_call" | custom-call | flops 805306368 | bytes 5242880 | tf_op jit(solution)/shard_map/pallas_call | solution.py:118
  78.6 0.9 copy-done
  79.5 4.0 %shard_map.90 = (bf16[384,128]{1,0:T(8,128)(2,1)}, bf16[384,128]{1,0:T(8,128)(2,1)}, bf16[384,128]{1,0:T(8,128)(2,1)}, bf16[384,128]{1,0:T(8,128)(2,1)}, bf16[38...) custom-call(s32[1]{0:T(128)} %bitcast.me_s, ...), custom_call_target="tpu_custom_call" | custom-call | flops 805306368 | bytes 5242880 | tf_op jit(solution)/shard_map/pallas_call | solution.py:109
  83.5 1.4 collective-permute-start.11
  85.0 0.4 collective-permute-start.12
  85.4 1.4 collective-permute-start.13
  86.8 0.2 collective-permute-start.14
  87.0 2.4 %collective-permute-start.15 = (bf16[384,128]{1,0:T(8,128)(2,1)}, bf16[384,128]{1,0:T(8,128)(2,1)S(1)}, u32[]{:S(2)}, u32[]{:S(2)}) collective-permute-start(bf16[384,128]{1,0:T(8,128)(2,1)} %get-tuple-element.101), channel_id=1, source_target_pairs={{0,24},{4,28},{8,16},{12,20},{16,8},{20,12},{24,0},{28,4},{1,25},{... | collective-permute-start | bytes 294920 | tf_op jit(solution)/shard_map/ppermute | solution.py:345
  89.4 1.2 collective-permute-start.16
  90.6 0.5 collective-permute-done.13.refs_4_
  91.2 5.1 %collective-permute-done.14.refs_5_ = bf16[384,128]{1,0:T(8,128)(2,1)S(1)} collective-permute-done((bf16[384,128]{1,0:T(8,128)(2,1)}, bf16[384,128]{1,0:T(8,128)(2,1)S(1)}, u32[]{:S(2)}, u32[]{:S(2)}) %collective-permute-start.14) | collective-permute-done | bytes 98336 | tf_op jit(solution)/shard_map/ppermute | solution.py:345
  96.4 0.6 copy-done.15
  97.0 21.3 %shard_map.91 = (bf16[1152,128]{1,0:T(8,128)(2,1)}, bf16[1152,128]{1,0:T(8,128)(2,1)}, bf16[1152,128]{1,0:T(8,128)(2,1)}, bf16[1152,128]{1,0:T(8,128)(2,1)}, bf1...) custom-call(s32[1]{0:T(128)} %bitcast.me_s, ...), custom_call_target="tpu_custom_call" | custom-call | flops 3019898880 | bytes 6291456 | tf_op jit(solution)/shard_map/pallas_call | solution.py:319
  118.3 0.5 collective-permute-start.17
  118.8 1.4 collective-permute-start.18
  120.3 1.5 collective-permute-start.20
  121.8 0.6 collective-permute-start.21
  122.4 2.4 %collective-permute-start.22 = (bf16[1152,128]{1,0:T(8,128)(2,1)}, bf16[1152,128]{1,0:T(8,128)(2,1)S(1)}, u32[]{:S(2)}, u32[]{:S(2)}) collective-permute-start(bf16[1152,128]{1,0:T(8,128)(2,1)} %get-tuple-element.109), channel_id=1, source_target_pairs={{0,24},{4,28},{8,16},{12,20},{16,8},{20,12},{24,0},{28,4},{1,25},{... | collective-permute-start | bytes 884744 | tf_op jit(solution)/shard_map/ppermute | solution.py:345
  124.7 4.2 %collective-permute-done.18.refs_2_ = bf16[1152,128]{1,0:T(8,128)(2,1)S(1)} collective-permute-done((bf16[1152,128]{1,0:T(8,128)(2,1)}, bf16[1152,128]{1,0:T(8,128)(2,1)S(1)}, u32[]{:S(2)}, u32[]{:S(2)}) %collective-permute-start.18) | collective-permute-done | bytes 294944 | tf_op jit(solution)/shard_map/ppermute | solution.py:345
  128.9 0.3 collective-permute-start.23
  129.2 5.0 %collective-permute-done.19.refs_3_ = bf16[1152,128]{1,0:T(8,128)(2,1)S(1)} collective-permute-done((bf16[1152,128]{1,0:T(8,128)(2,1)}, bf16[1152,128]{1,0:T(8,128)(2,1)S(1)}, u32[]{:S(2)}, u32[]{:S(2)}) %collective-permute-start.19) | collective-permute-done | bytes 294944 | tf_op jit(solution)/shard_map/ppermute | solution.py:345
  134.3 14.5 %collective-permute-done.21.refs_5_ = bf16[1152,128]{1,0:T(8,128)(2,1)S(1)} collective-permute-done((bf16[1152,128]{1,0:T(8,128)(2,1)}, bf16[1152,128]{1,0:T(8,128)(2,1)S(1)}, u32[]{:S(2)}, u32[]{:S(2)}) %collective-permute-start.21) | collective-permute-done | bytes 294944 | tf_op jit(solution)/shard_map/ppermute | solution.py:345
  148.8 0.7 copy-done.6
  149.5 0.1 copy-done.7
  149.6 0.1 copy-done.8
  149.7 3.7 %shard_map.92 = (bf16[384,1024]{1,0:T(8,128)(2,1)}, bf16[384,1024]{1,0:T(8,128)(2,1)}, bf16[384,1024]{1,0:T(8,128)(2,1)}) custom-call(s32[1]{0:T(128)} %bitcast.me_s, bf16[1152,128]{1,0:T(8,128)(2,1)} %get-tuple-element.103.refs_0_, bf16[1152,128]{1,0:T(8,128)(2,1)} %copy-done.2, bf16[1152,128]{1,0:T(8,128)(2,1)} %copy-done.3, bf16[1152,128]{1,0:T(8,128)(2,1)} %copy-done.4, ...), custom_call_target="tpu_custom_call" | custom-call | tf_op jit(solution)/shard_map/pallas_call | solution.py:73
  (49 shorter events, 0.2 us)
Async XLA Ops:
  0.6 32.5 %collective-permute-start = (bf16[384,1024]{1,0:T(8,128)(2,1)}, bf16[384,1024]{1,0:T(8,128)(2,1)S(1)}, u32[]{:S(2)}, u32[]{:S(2)}) collective-permute-start(bf16[384,1024]{1,0:T(8,128)(2,1)} %o_ref.1), channel_id=1, source_target_pairs={{0,1},{1,2},{2,3},{3,0},{4,5},{5,6},{6,7},{7,4},{8,9},{9,10},{10,1... | collective-permute-start | bytes 2359304 | tf_op jit(solution)/shard_map/ppermute | solution.py:348
  7.3 25.8 %collective-permute-start.1 = (bf16[1168,128]{1,0:T(8,128)(2,1)}, bf16[1168,128]{1,0:T(8,128)(2,1)S(1)}, u32[]{:S(2)}, u32[]{:S(2)}) collective-permute-start(bf16[1168,128]{1,0:T(8,128)(2,1)} %get-tuple-element.58), channel_id=1, source_target_pairs={{0,24},{4,28},{8,16},{12,20},{16,8},{20,12},{24,0},{28,4},{1,25},{... | collective-permute-start | bytes 897032 | tf_op jit(solution)/shard_map/ppermute | solution.py:345
  9.8 23.3 %collective-permute-start.2 = (bf16[1168,128]{1,0:T(8,128)(2,1)}, bf16[1168,128]{1,0:T(8,128)(2,1)S(1)}, u32[]{:S(2)}, u32[]{:S(2)}) collective-permute-start(bf16[1168,128]{1,0:T(8,128)(2,1)} %get-tuple-element.59), channel_id=1, source_target_pairs={{0,16},{4,20},{8,24},{12,28},{16,0},{20,4},{24,8},{28,12},{1,17},{... | collective-permute-start | bytes 897032 | tf_op jit(solution)/shard_map/ppermute | solution.py:345
  10.3 22.8 %collective-permute-start.3 = (bf16[1168,128]{1,0:T(8,128)(2,1)}, bf16[1168,128]{1,0:T(8,128)(2,1)}, u32[]{:S(2)}, u32[]{:S(2)}) collective-permute-start(bf16[1168,128]{1,0:T(8,128)(2,1)} %get-tuple-element.60), channel_id=1, source_target_pairs={{0,8},{4,12},{8,0},{12,4},{16,24},{20,28},{24,16},{28,20},{1,9},{5... | collective-permute-start | bytes 897032 | tf_op jit(solution)/shard_map/ppermute | solution.py:345
  33.1 7.6 %copy-start.9 = (bf16[1168,128]{1,0:T(8,128)(2,1)}, bf16[1168,128]{1,0:T(8,128)(2,1)S(1)}, u32[]{:S(2)}) copy-start(bf16[1168,128]{1,0:T(8,128)(2,1)S(1)} %collective-permute-done.1.refs_6_) | copy-start | bytes 897028
  33.1 7.6 %copy-start.10 = (bf16[1168,128]{1,0:T(8,128)(2,1)}, bf16[1168,128]{1,0:T(8,128)(2,1)S(1)}, u32[]{:S(2)}) copy-start(bf16[1168,128]{1,0:T(8,128)(2,1)S(1)} %collective-permute-done.2.refs_4_) | copy-start | bytes 897028
  33.2 7.5 %copy-start.1 = (bf16[384,1024]{1,0:T(8,128)(2,1)}, bf16[384,1024]{1,0:T(8,128)(2,1)S(1)}, u32[]{:S(2)}) copy-start(bf16[384,1024]{1,0:T(8,128)(2,1)S(1)} %collective-permute-done.o_ref) | copy-start | bytes 2359300
  33.2 20.1 %collective-permute-start.4 = (bf16[384,1024]{1,0:T(8,128)(2,1)S(1)}, bf16[384,1024]{1,0:T(8,128)(2,1)}, u32[]{:S(2)}, u32[]{:S(2)}) collective-permute-start(bf16[384,1024]{1,0:T(8,128)(2,1)S(1)} %collective-permute-done.o_ref), channel_id=1, source_target_pairs={{0,1},{1,2},{2,3},{3,0},{4,5},{5,6},{6,7},{7,4},{8,9},{9,10},{10,1... | collective-permute-start | bytes 2359304 | tf_op jit(solution)/shard_map/ppermute | solution.py:348
  34.8 10.6 %collective-permute-start.5 = (bf16[1168,128]{1,0:T(8,128)(2,1)}, bf16[1168,128]{1,0:T(8,128)(2,1)}, u32[]{:S(2)}, u32[]{:S(2)}) collective-permute-start(bf16[1168,128]{1,0:T(8,128)(2,1)} %get-tuple-element.63), channel_id=1, source_target_pairs={{0,28},{4,24},{8,20},{12,16},{16,12},{20,8},{24,4},{28,0},{1,29},{... | collective-permute-start | bytes 897032 | tf_op jit(solution)/shard_map/ppermute | solution.py:345
  35.3 16.4 %collective-permute-start.6 = (bf16[1168,128]{1,0:T(8,128)(2,1)}, bf16[1168,128]{1,0:T(8,128)(2,1)}, u32[]{:S(2)}, u32[]{:S(2)}) collective-permute-start(bf16[1168,128]{1,0:T(8,128)(2,1)} %get-tuple-element.64), channel_id=1, source_target_pairs={{0,20},{4,16},{8,28},{12,24},{16,4},{20,0},{24,12},{28,8},{1,21},{... | collective-permute-start | bytes 897032 | tf_op jit(solution)/shard_map/ppermute | solution.py:345
  37.5 14.2 %collective-permute-start.7 = (bf16[1168,128]{1,0:T(8,128)(2,1)}, bf16[1168,128]{1,0:T(8,128)(2,1)}, u32[]{:S(2)}, u32[]{:S(2)}) collective-permute-start(bf16[1168,128]{1,0:T(8,128)(2,1)} %get-tuple-element.65), channel_id=1, source_target_pairs={{0,12},{4,8},{8,4},{12,0},{16,28},{20,24},{24,20},{28,16},{1,13},{... | collective-permute-start | bytes 897032 | tf_op jit(solution)/shard_map/ppermute | solution.py:345
  37.5 14.2 %collective-permute-start.8 = (bf16[1168,128]{1,0:T(8,128)(2,1)}, bf16[1168,128]{1,0:T(8,128)(2,1)}, u32[]{:S(2)}, u32[]{:S(2)}) collective-permute-start(bf16[1168,128]{1,0:T(8,128)(2,1)} %get-tuple-element.66), channel_id=1, source_target_pairs={{0,4},{4,0},{8,12},{12,8},{16,20},{20,16},{24,28},{28,24},{1,5},{5... | collective-permute-start | bytes 897032 | tf_op jit(solution)/shard_map/ppermute | solution.py:345
  53.3 25.3 %collective-permute-start.9 = (bf16[384,1024]{1,0:T(8,128)(2,1)}, bf16[384,1024]{1,0:T(8,128)(2,1)S(1)}, u32[]{:S(2)}, u32[]{:S(2)}) collective-permute-start(bf16[384,1024]{1,0:T(8,128)(2,1)} %collective-permute-done.4.o_ref), channel_id=1, source_target_pairs={{0,1},{1,2},{2,3},{3,0},{4,5},{5,6},{6,7},{7,4},{8,9},{9,10},{10,1... | collective-permute-start | bytes 2359304 | tf_op jit(solution)/shard_map/ppermute | solution.py:348
  78.6 0.9 copy-start
  83.5 3.5 %collective-permute-start.10 = (bf16[384,128]{1,0:T(8,128)(2,1)}, bf16[384,128]{1,0:T(8,128)(2,1)S(1)}, u32[]{:S(2)}, u32[]{:S(2)}) collective-permute-start(bf16[384,128]{1,0:T(8,128)(2,1)} %get-tuple-element.96), channel_id=1, source_target_pairs={{0,4},{4,0},{8,12},{12,8},{16,20},{20,16},{24,28},{28,24},{1,5},{5... | collective-permute-start | bytes 294920 | tf_op jit(solution)/shard_map/ppermute | solution.py:345
  83.5 5.9 %collective-permute-start.11 = (bf16[384,128]{1,0:T(8,128)(2,1)}, bf16[384,128]{1,0:T(8,128)(2,1)S(1)}, u32[]{:S(2)}, u32[]{:S(2)}) collective-permute-start(bf16[384,128]{1,0:T(8,128)(2,1)} %get-tuple-element.97), channel_id=1, source_target_pairs={{0,8},{4,12},{8,0},{12,4},{16,24},{20,28},{24,16},{28,20},{1,9},{5... | collective-permute-start | bytes 294920 | tf_op jit(solution)/shard_map/ppermute | solution.py:345
  85.0 5.7 %collective-permute-start.12 = (bf16[384,128]{1,0:T(8,128)(2,1)}, bf16[384,128]{1,0:T(8,128)(2,1)S(1)}, u32[]{:S(2)}, u32[]{:S(2)}) collective-permute-start(bf16[384,128]{1,0:T(8,128)(2,1)} %get-tuple-element.98), channel_id=1, source_target_pairs={{0,12},{4,8},{8,4},{12,0},{16,28},{20,24},{24,20},{28,16},{1,13},{... | collective-permute-start | bytes 294920 | tf_op jit(solution)/shard_map/ppermute | solution.py:345
  85.4 5.8 %collective-permute-start.13 = (bf16[384,128]{1,0:T(8,128)(2,1)}, bf16[384,128]{1,0:T(8,128)(2,1)S(1)}, u32[]{:S(2)}, u32[]{:S(2)}) collective-permute-start(bf16[384,128]{1,0:T(8,128)(2,1)} %get-tuple-element.99), channel_id=1, source_target_pairs={{0,16},{4,20},{8,24},{12,28},{16,0},{20,4},{24,8},{28,12},{1,17},{... | collective-permute-start | bytes 294920 | tf_op jit(solution)/shard_map/ppermute | solution.py:345
  86.8 9.5 %collective-permute-start.14 = (bf16[384,128]{1,0:T(8,128)(2,1)}, bf16[384,128]{1,0:T(8,128)(2,1)S(1)}, u32[]{:S(2)}, u32[]{:S(2)}) collective-permute-start(bf16[384,128]{1,0:T(8,128)(2,1)} %get-tuple-element.100), channel_id=1, source_target_pairs={{0,20},{4,16},{8,28},{12,24},{16,4},{20,0},{24,12},{28,8},{1,21},{... | collective-permute-start | bytes 294920 | tf_op jit(solution)/shard_map/ppermute | solution.py:345
  87.0 9.3 %copy-start.11 = (bf16[384,128]{1,0:T(8,128)(2,1)}, bf16[384,128]{1,0:T(8,128)(2,1)S(1)}, u32[]{:S(2)}) copy-start(bf16[384,128]{1,0:T(8,128)(2,1)S(1)} %collective-permute-done.10.refs_1_) | copy-start | bytes 294916
  87.0 9.3 %collective-permute-start.15 = (bf16[384,128]{1,0:T(8,128)(2,1)}, bf16[384,128]{1,0:T(8,128)(2,1)S(1)}, u32[]{:S(2)}, u32[]{:S(2)}) collective-permute-start(bf16[384,128]{1,0:T(8,128)(2,1)} %get-tuple-element.101), channel_id=1, source_target_pairs={{0,24},{4,28},{8,16},{12,20},{16,8},{20,12},{24,0},{28,4},{1,25},{... | collective-permute-start | bytes 294920 | tf_op jit(solution)/shard_map/ppermute | solution.py:345
  89.4 6.9 %copy-start.12 = (bf16[384,128]{1,0:T(8,128)(2,1)}, bf16[384,128]{1,0:T(8,128)(2,1)S(1)}, u32[]{:S(2)}) copy-start(bf16[384,128]{1,0:T(8,128)(2,1)S(1)} %collective-permute-done.11.refs_2_) | copy-start | bytes 294916
  89.4 6.9 %collective-permute-start.16 = (bf16[384,128]{1,0:T(8,128)(2,1)}, bf16[384,128]{1,0:T(8,128)(2,1)S(1)}, u32[]{:S(2)}, u32[]{:S(2)}) collective-permute-start(bf16[384,128]{1,0:T(8,128)(2,1)} %get-tuple-element.102), channel_id=1, source_target_pairs={{0,28},{4,24},{8,20},{12,16},{16,12},{20,8},{24,4},{28,0},{1,29},{... | collective-permute-start | bytes 294920 | tf_op jit(solution)/shard_map/ppermute | solution.py:345
  90.6 5.7 %copy-start.13 = (bf16[384,128]{1,0:T(8,128)(2,1)}, bf16[384,128]{1,0:T(8,128)(2,1)S(1)}, u32[]{:S(2)}) copy-start(bf16[384,128]{1,0:T(8,128)(2,1)S(1)} %collective-permute-done.12.refs_3_) | copy-start | bytes 294916
  91.2 5.2 %copy-start.14 = (bf16[384,128]{1,0:T(8,128)(2,1)}, bf16[384,128]{1,0:T(8,128)(2,1)S(1)}, u32[]{:S(2)}) copy-start(bf16[384,128]{1,0:T(8,128)(2,1)S(1)} %collective-permute-done.13.refs_4_) | copy-start | bytes 294916
  96.3 0.6 copy-start.15
  96.3 0.7 copy-start.16
  96.3 0.7 copy-start.17
  118.3 4.0 %collective-permute-start.17 = (bf16[1152,128]{1,0:T(8,128)(2,1)}, bf16[1152,128]{1,0:T(8,128)(2,1)S(1)}, u32[]{:S(2)}, u32[]{:S(2)}) collective-permute-start(bf16[1152,128]{1,0:T(8,128)(2,1)} %get-tuple-element.104), channel_id=1, source_target_pairs={{0,4},{4,0},{8,12},{12,8},{16,20},{20,16},{24,28},{28,24},{1,5},{5... | collective-permute-start | bytes 884744 | tf_op jit(solution)/shard_map/ppermute | solution.py:345
  118.8 10.1 %collective-permute-start.18 = (bf16[1152,128]{1,0:T(8,128)(2,1)}, bf16[1152,128]{1,0:T(8,128)(2,1)S(1)}, u32[]{:S(2)}, u32[]{:S(2)}) collective-permute-start(bf16[1152,128]{1,0:T(8,128)(2,1)} %get-tuple-element.105), channel_id=1, source_target_pairs={{0,8},{4,12},{8,0},{12,4},{16,24},{20,28},{24,16},{28,20},{1,9},{5... | collective-permute-start | bytes 884744 | tf_op jit(solution)/shard_map/ppermute | solution.py:345
  120.3 14.0 %collective-permute-start.19 = (bf16[1152,128]{1,0:T(8,128)(2,1)}, bf16[1152,128]{1,0:T(8,128)(2,1)S(1)}, u32[]{:S(2)}, u32[]{:S(2)}) collective-permute-start(bf16[1152,128]{1,0:T(8,128)(2,1)} %get-tuple-element.106), channel_id=1, source_target_pairs={{0,12},{4,8},{8,4},{12,0},{16,28},{20,24},{24,20},{28,16},{1,13},{... | collective-permute-start | bytes 884744 | tf_op jit(solution)/shard_map/ppermute | solution.py:345
  120.3 14.0 %collective-permute-start.20 = (bf16[1152,128]{1,0:T(8,128)(2,1)}, bf16[1152,128]{1,0:T(8,128)(2,1)S(1)}, u32[]{:S(2)}, u32[]{:S(2)}) collective-permute-start(bf16[1152,128]{1,0:T(8,128)(2,1)} %get-tuple-element.107), channel_id=1, source_target_pairs={{0,16},{4,20},{8,24},{12,28},{16,0},{20,4},{24,8},{28,12},{1,17},{... | collective-permute-start | bytes 884744 | tf_op jit(solution)/shard_map/ppermute | solution.py:345
  121.8 27.0 %collective-permute-start.21 = (bf16[1152,128]{1,0:T(8,128)(2,1)}, bf16[1152,128]{1,0:T(8,128)(2,1)S(1)}, u32[]{:S(2)}, u32[]{:S(2)}) collective-permute-start(bf16[1152,128]{1,0:T(8,128)(2,1)} %get-tuple-element.108), channel_id=1, source_target_pairs={{0,20},{4,16},{8,28},{12,24},{16,4},{20,0},{24,12},{28,8},{1,21},{... | collective-permute-start | bytes 884744 | tf_op jit(solution)/shard_map/ppermute | solution.py:345
  122.4 26.4 %copy-start.2 = (bf16[1152,128]{1,0:T(8,128)(2,1)}, bf16[1152,128]{1,0:T(8,128)(2,1)S(1)}, u32[]{:S(2)}) copy-start(bf16[1152,128]{1,0:T(8,128)(2,1)S(1)} %collective-permute-done.17.refs_1_) | copy-start | bytes 884740
  122.4 26.4 %collective-permute-start.22 = (bf16[1152,128]{1,0:T(8,128)(2,1)}, bf16[1152,128]{1,0:T(8,128)(2,1)S(1)}, u32[]{:S(2)}, u32[]{:S(2)}) collective-permute-start(bf16[1152,128]{1,0:T(8,128)(2,1)} %get-tuple-element.109), channel_id=1, source_target_pairs={{0,24},{4,28},{8,16},{12,20},{16,8},{20,12},{24,0},{28,4},{1,25},{... | collective-permute-start | bytes 884744 | tf_op jit(solution)/shard_map/ppermute | solution.py:345
  128.9 19.9 %copy-start.3 = (bf16[1152,128]{1,0:T(8,128)(2,1)}, bf16[1152,128]{1,0:T(8,128)(2,1)S(1)}, u32[]{:S(2)}) copy-start(bf16[1152,128]{1,0:T(8,128)(2,1)S(1)} %collective-permute-done.18.refs_2_) | copy-start | bytes 884740
  128.9 19.9 %collective-permute-start.23 = (bf16[1152,128]{1,0:T(8,128)(2,1)}, bf16[1152,128]{1,0:T(8,128)(2,1)S(1)}, u32[]{:S(2)}, u32[]{:S(2)}) collective-permute-start(bf16[1152,128]{1,0:T(8,128)(2,1)} %get-tuple-element.110), channel_id=1, source_target_pairs={{0,28},{4,24},{8,20},{12,16},{16,12},{20,8},{24,4},{28,0},{1,29},{... | collective-permute-start | bytes 884744 | tf_op jit(solution)/shard_map/ppermute | solution.py:345
  134.3 14.5 %copy-start.4 = (bf16[1152,128]{1,0:T(8,128)(2,1)}, bf16[1152,128]{1,0:T(8,128)(2,1)S(1)}, u32[]{:S(2)}) copy-start(bf16[1152,128]{1,0:T(8,128)(2,1)S(1)} %collective-permute-done.19.refs_3_) | copy-start | bytes 884740
  134.3 14.5 %copy-start.5 = (bf16[1152,128]{1,0:T(8,128)(2,1)}, bf16[1152,128]{1,0:T(8,128)(2,1)S(1)}, u32[]{:S(2)}) copy-start(bf16[1152,128]{1,0:T(8,128)(2,1)S(1)} %collective-permute-done.20.refs_4_) | copy-start | bytes 884740
  148.8 0.7 copy-start.6
  148.8 0.8 copy-start.7
  148.8 0.9 copy-start.8

commit v2 on v1

--- a/solution.py
+++ b/solution.py
@@ -12,8 +12,7 @@
 DOC_VALUES = 8
 DOC_ROWS = 16
 NEG_LARGE = -1e30
-VMEM_LIMIT = 56 * 1024 * 1024
-PARAMS = pltpu.CompilerParams(vmem_limit_bytes=VMEM_LIMIT)
+VMEM_SPARE = 6 * 1024 * 1024
 
 NN = (((1,), (0,)), ((), ()))
 NT = (((1,), (1,)), ((), ()))
@@ -34,6 +33,11 @@
 
 def aligned(index, size):
     return pl.ds(pl.multiple_of(index * size, size), size)
+
+
+def params(arrays, scratch=()):
+    total = sum(math.prod(a.shape) * jnp.dtype(a.dtype).itemsize for a in (*arrays, *scratch))
+    return pltpu.CompilerParams(vmem_limit_bytes=total + VMEM_SPARE)
 
 
 def pack_kernel(heads, rows, me_s, q_ref, k_ref, v_ref, doc_ref, *outs):
@@ -51,12 +55,13 @@
 def pack_heads(me, q, k, v, doc_ids):
     rows, width = q.shape
     heads = width // HD
+    out_shape = [jax.ShapeDtypeStruct((3 * rows + DOC_ROWS, HD), q.dtype)] * heads
     return pl.pallas_call(
         functools.partial(pack_kernel, heads, rows),
         in_specs=[SMEM_SPEC] + [VMEM_SPEC] * 4,
         out_specs=[VMEM_SPEC] * heads,
-        out_shape=[jax.ShapeDtypeStruct((3 * rows + DOC_ROWS, HD), q.dtype)] * heads,
-        compiler_params=PARAMS,
+        out_shape=out_shape,
+        compiler_params=params([q, k, v, *out_shape]),
     )(me, q, k, v, doc_ids.reshape(rows // HD, HD))
 
 
@@ -75,31 +80,33 @@
         in_specs=[SMEM_SPEC] + [VMEM_SPEC] * heads,
         out_specs=[VMEM_SPEC] * 3,
         out_shape=[jax.ShapeDtypeStruct((rows, heads * HD), blocks[0].dtype)] * 3,
-        compiler_params=PARAMS,
+        compiler_params=params([*blocks, *blocks]),
     )(me, *blocks)
 
 
 def project_kernel(first, o_ref, w_ref, *refs):
     out_ref = refs[-1]
-    for pair in range(w_ref.shape[1] // (2 * HD)):
-        columns = slice(pair * 2 * HD, (pair + 1) * 2 * HD)
-        both = dot32(o_ref[...], w_ref[:, columns])
-        out_ref[:, columns] = both if first else refs[0][:, columns] + both
+    for pair in range(w_ref.shape[0] // (2 * HD)):
+        part = slice(pair * 2 * HD, (pair + 1) * 2 * HD)
+        both = dot32(o_ref[...], w_ref[part, :], NT)
+        out_ref[:, part] = both if first else refs[0][:, part] + both
 
 
 def project_last_kernel(me_s, o_ref, w_ref, acc_ref, *outs):
     pairs = len(outs) // 2
     odd = lax.rem(me_s[0], 2) == 1
     for j in range(pairs):
-        columns = aligned(lax.rem(me_s[0] // 2, pairs) ^ j, 2 * HD)
-        both = (acc_ref[:, columns] + dot32(o_ref[...], w_ref[:, columns])).astype(jnp.bfloat16)
+        part = aligned(lax.rem(me_s[0] // 2, pairs) ^ j, 2 * HD)
+        both = (acc_ref[:, part] + dot32(o_ref[...], w_ref[part, :], NT)).astype(jnp.bfloat16)
         outs[2 * j][...] = jnp.where(odd, both[:, HD:], both[:, :HD])
         outs[2 * j + 1][...] = jnp.where(odd, both[:, :HD], both[:, HD:])
 
 
 def project(me, weight, features, acc, last):
     rows, width = features.shape
-    columns = weight.shape[1]
+    columns = weight.shape[0]
+    heads = columns // HD
+    total = jax.ShapeDtypeStruct((rows, columns), jnp.float32)
     cost = pl.CostEstimate(
         flops=2 * rows * width * columns,
         bytes_accessed=2 * width * columns + 8 * rows * columns,
@@ -109,9 +116,9 @@
         return pl.pallas_call(
             project_last_kernel,
             in_specs=[SMEM_SPEC] + [VMEM_SPEC] * 3,
-            out_specs=[VMEM_SPEC] * (columns // HD),
-            out_shape=[jax.ShapeDtypeStruct((rows, HD), jnp.bfloat16)] * (columns // HD),
-            compiler_params=PARAMS,
+            out_specs=[VMEM_SPEC] * heads,
+            out_shape=[jax.ShapeDtypeStruct((rows, HD), jnp.bfloat16)] * heads,
+            compiler_params=params([features, weight, total, total]),
             cost_estimate=cost,
         )(me, features, weight, acc)
     operands = (features, weight) + (() if acc is None else (acc,))
@@ -119,8 +126,8 @@
         functools.partial(project_kernel, acc is None),
         in_specs=[VMEM_SPEC] * len(operands),
         out_specs=VMEM_SPEC,
-        out_shape=jax.ShapeDtypeStruct((rows, columns), jnp.float32),
-        compiler_params=PARAMS,
+        out_shape=total,
+        compiler_params=params([features, weight, total, total]),
         cost_estimate=cost,
     )(*operands)
 
@@ -284,30 +291,27 @@
     total = peers * rows
     bq, bk = block_size(total, 512), block_size(total, 256)
     size = plan_size(total, bq, bk)
+    vectors = [
+        *[jax.ShapeDtypeStruct((total, HD), jnp.bfloat16)] * 3,
+        *[jax.ShapeDtypeStruct((HD, total), jnp.bfloat16)] * 2,
+        jax.ShapeDtypeStruct((1, total), jnp.int32),
+        jax.ShapeDtypeStruct((HD, total), jnp.float32),
+        jax.ShapeDtypeStruct((1, total), jnp.float32),
+    ]
+    plan = [(size,), (size,), (1,)]
+    scratch = [
+        pltpu.VMEM((HD, total), jnp.bfloat16),
+        pltpu.VMEM((1, total), jnp.float32),
+        pltpu.VMEM((1, total), jnp.float32),
+        *[pltpu.VMEM((bk, bq), jnp.float32), pltpu.VMEM((1, bq), jnp.float32)] * 2,
+    ]
     return pl.pallas_call(
         functools.partial(forward_kernel, peers, heads, rows, bq, bk),
         in_specs=[SMEM_SPEC] + [VMEM_SPEC] * peers,
-        out_specs=[VMEM_SPEC] * 8 + [SMEM_SPEC] * 3,
-        out_shape=[jax.ShapeDtypeStruct((total, HD), jnp.bfloat16)] * 3
-        + [jax.ShapeDtypeStruct((HD, total), jnp.bfloat16)] * 2
-        + [
-            jax.ShapeDtypeStruct((1, total), jnp.int32),
-            jax.ShapeDtypeStruct((HD, total), jnp.float32),
-            jax.ShapeDtypeStruct((1, total), jnp.float32),
-            jax.ShapeDtypeStruct((size,), jnp.int32),
-            jax.ShapeDtypeStruct((size,), jnp.int32),
-            jax.ShapeDtypeStruct((1,), jnp.int32),
-        ],
-        scratch_shapes=[
-            pltpu.SMEM((size,), jnp.int32),
-            pltpu.SMEM((size,), jnp.int32),
-            pltpu.SMEM((1,), jnp.int32),
-            pltpu.VMEM((HD, total), jnp.bfloat16),
-            pltpu.VMEM((1, total), jnp.float32),
-            pltpu.VMEM((1, total), jnp.float32),
-        ]
-        + [pltpu.VMEM((bk, bq), jnp.float32), pltpu.VMEM((1, bq), jnp.float32)] * 2,
-        compiler_params=PARAMS,
+        out_specs=[VMEM_SPEC] * len(vectors) + [SMEM_SPEC] * 3,
+        out_shape=vectors + [jax.ShapeDtypeStruct(shape, jnp.int32) for shape in plan],
+        scratch_shapes=[pltpu.SMEM(shape, jnp.int32) for shape in plan] + scratch,
+        compiler_params=params([*blocks, *vectors], scratch),
         cost_estimate=attention_cost(total, 3),
     )(me, *blocks)
 
@@ -316,23 +320,26 @@
     peers, rows = len(blocks), blocks[0].shape[0]
     total = peers * rows
     bq, bk = block_size(total, 512), block_size(total, 256)
+    vectors, plan = state[:8], state[8:]
+    out_shape = [jax.ShapeDtypeStruct((3 * rows, HD), jnp.bfloat16)] * heads
+    scratch = [
+        pltpu.VMEM((total, HD), jnp.bfloat16),
+        pltpu.VMEM((HD, total), jnp.bfloat16),
+        pltpu.VMEM((1, total), jnp.float32),
+        pltpu.VMEM((total, HD), jnp.float32),
+        pltpu.VMEM((total, HD), jnp.float32),
+        pltpu.VMEM((HD, total), jnp.float32),
+        *[pltpu.VMEM((bk, bq), jnp.bfloat16)] * 4,
+    ]
     return pl.pallas_call(
         functools.partial(backward_kernel, peers, heads, rows, bq, bk),
         in_specs=[SMEM_SPEC] * 4 + [VMEM_SPEC] * (8 + peers),
         out_specs=[VMEM_SPEC] * heads,
-        out_shape=[jax.ShapeDtypeStruct((3 * rows, HD), jnp.bfloat16)] * heads,
-        scratch_shapes=[
-            pltpu.VMEM((total, HD), jnp.bfloat16),
-            pltpu.VMEM((HD, total), jnp.bfloat16),
-            pltpu.VMEM((1, total), jnp.float32),
-            pltpu.VMEM((total, HD), jnp.float32),
-            pltpu.VMEM((total, HD), jnp.float32),
-            pltpu.VMEM((HD, total), jnp.float32),
-        ]
-        + [pltpu.VMEM((bk, bq), jnp.bfloat16)] * 4,
-        compiler_params=PARAMS,
+        out_shape=out_shape,
+        scratch_shapes=scratch,
+        compiler_params=params([*vectors, *blocks, *out_shape], scratch),
         cost_estimate=attention_cost(total, 5),
-    )(me, *state[8:], *state[:8], *blocks)
+    )(me, *plan, *vectors, *blocks)
 
 
 def per_device(peers, groups, queries, keys_in, values, out_grad, out_weight, doc_ids):
@@ -361,7 +368,7 @@
     weights = []
     for step in range(groups):
         block = lax.rem(lax.axis_index("head") + groups - step, groups)
-        weights.append(lax.dynamic_slice_in_dim(out_weight, block * width, width, 1).T)
+        weights.append(lax.dynamic_slice_in_dim(out_weight, block * width, width, 1))
     for step in range(groups):
         last = step == groups - 1
         if not last:

time: 153 us -> 131 us (0.86)
  Pallas kernels: 66.4 us -> 46.6 us
  waiting for transfers between devices: 37.6 us -> 54.7 us
  local copies, waits for them, and re-layouts: 23.3 us -> 8.62 us
  starting transfers between devices: 25.4 us -> 22 us
    ppermute x21, waiting for transfers between devices: 36 us -> 51.7 us  [exchange(): lax.ppermute(x, 'seq', [(i, i ^ d) for i in range(peers)])]
    unnamed x40 -> x10, local copies, waits for them, and re-layouts: 16.8 us -> 4.08 us
    pallas_call x3, Pallas kernels: 12.9 us -> 3.05 us  [project(): pl.pallas_call(functools.partial(project_kernel, acc is None), in_specs=[...]
    ppermute x21, starting transfers between devices: 20.6 us -> 17.4 us  [exchange(): lax.ppermute(x, 'seq', [(i, i ^ d) for i in range(peers)])]
    pallas_call x1, Pallas kernels: 4.04 us -> 1.03 us  [project(): pl.pallas_call(project_last_kernel, in_specs=[SMEM_SPEC] + [VMEM_SPEC] *...]
    pallas_call x1, Pallas kernels: 3.63 us -> 1.43 us  [pack_heads(): pl.pallas_call(functools.partial(pack_kernel, heads, rows), in_specs=[SME...]
    dynamic_slice x1, local copies, waits for them, and re-layouts: 6.44 us -> 4.54 us  [per_device(): lax.dynamic_slice_in_dim(out_weight, block * width, width, 1)]
    pallas_call x1, Pallas kernels: 3.66 us -> 2.08 us  [unpack_heads(): pl.pallas_call(functools.partial(unpack_kernel, heads, rows), in_specs=[S...]
  transfers between devices with their start and end apart: 24 -> 24, of which waited for: 8 -> 14; matrix products, arithmetic and copies ran while one was open for 14% -> 3% of each run, Pallas kernels for 24% -> 18%
where the time goes in v2:
time: 131 us; the launch traced here: 133 us
  waiting for transfers between devices  54.7 us (42%)
  Pallas kernels  46.6 us (36%)
  starting transfers between devices  22 us (17%)
  local copies, waits for them, and re-layouts  8.62 us (7%)
    ppermute x21, waiting for transfers between devices, exchange(): lax.ppermute(x, 'seq', [(i, i ^ d) for i in range(peers)])  51.7 us
    pallas_call x1, Pallas kernels, attention_backward(): pl.pallas_call(functools.partial(backward_kernel, peers, heads, rows, bq,...  19.8 us
    pallas_call x1, Pallas kernels, attention_forward(): pl.pallas_call(functools.partial(forward_kernel, peers, heads, rows, bq,...  19.2 us
    ppermute x21, starting transfers between devices, exchange(): lax.ppermute(x, 'seq', [(i, i ^ d) for i in range(peers)])  17.4 us
    ppermute x3, starting transfers between devices, pass_on(): lax.ppermute(x, 'head', [(i, (i + 1) % groups) for i in range(groups)])  4.66 us
    dynamic_slice x1, local copies, waits for them, and re-layouts, per_device(): lax.dynamic_slice_in_dim(out_weight, block * width, width, 1)  4.54 us
    unnamed x10, local copies, waits for them, and re-layouts  4.08 us
    pallas_call x3, Pallas kernels, project(): pl.pallas_call(functools.partial(project_kernel, acc is None), in_specs=[...  3.05 us
  transfers between devices with their start and end apart: 24, of which 14 were waited for; matrix products, arithmetic and copies ran while one was open for 3% of the time, Pallas kernels for 18%

profile of v2, /device:TPU:0, one launch (start us, length us, event | category | flops | bytes accessed | tf_op | source)
XLA Modules:
  0.0 132.6 jit_solution(14255562078550417716)
XLA Ops:
  0.6 3.1 %collective-permute-start = (bf16[384,1024]{1,0:T(8,128)(2,1)}, bf16[384,1024]{1,0:T(8,128)(2,1)S(1)}, u32[]{:S(2)}, u32[]{:S(2)}) collective-permute-start(bf16[384,1024]{1,0:T(8,128)(2,1)} %o_ref.1), channel_id=1, source_target_pairs={{0,1},{1,2},{2,3},{3,0},{4,5},{5,6},{6,7},{7,4},{8,9},{9,10},{10,1... | collective-permute-start | bytes 2359304 | tf_op jit(solution)/shard_map/ppermute | solution.py:355
  3.7 1.1 copy-done
  4.8 1.1 copy-done.1
  6.0 1.1 copy-done.2
  7.1 0.7 copy-done.4
  7.8 1.4 %shard_map.85 = (bf16[1168,128]{1,0:T(8,128)(2,1)S(1)}, bf16[1168,128]{1,0:T(8,128)(2,1)S(1)}, bf16[1168,128]{1,0:T(8,128)(2,1)S(1)}, bf16[1168,128]{1,0:T(8,128...) custom-call(s32[1]{0:T(128)} %bitcast.me_s, ...), custom_call_target="tpu_custom_call" | custom-call | tf_op jit(solution)/shard_map/pallas_call | solution.py:59
  9.2 2.4 %collective-permute-start.1 = (bf16[1168,128]{1,0:T(8,128)(2,1)}, bf16[1168,128]{1,0:T(8,128)(2,1)S(1)}, u32[]{:S(2)}, u32[]{:S(2)}) collective-permute-start(bf16[1168,128]{1,0:T(8,128)(2,1)} %get-tuple-element.58), channel_id=1, source_target_pairs={{0,24},{4,28},{8,16},{12,20},{16,8},{20,12},{24,0},{28,4},{1,25},{... | collective-permute-start | bytes 897032 | tf_op jit(solution)/shard_map/ppermute | solution.py:352
  11.7 0.5 collective-permute-start.2
  12.2 0.5 collective-permute-start.3
  12.7 4.5 %constant_dynamic-slice_fusion = (bf16[1024,1024]{1,0:T(8,128)(2,1)S(1)}, bf16[1024,1024]{1,0:T(8,128)(2,1)S(1)}, bf16[1024,1024]{1,0:T(8,128)(2,1)S(1)}, bf16[1024,1024]{1,0:T(8,128)(2,1)S(1)}) fusion(bf16[1024,4096]{1,0:T(8,128)(2,1)} %param.10, s32[]{:T(128)S(6)} %select_n.15, s32[]{:T(128)S(6)} %select_n.13, s32[]{:T(128)S(6)} %select_n.12, s32[]{:T(128)S(6)} %select_n.14), kind=kLoop, calls=%fused_computation | loop fusion | bytes 16777232 | tf_op jit(solution)/shard_map/dynamic_slice | solution.py:371
  17.3 1.0 shard_map.86.refs_0_
  18.3 2.1 %collective-permute-done.1.refs_6_ = bf16[1168,128]{1,0:T(8,128)(2,1)S(1)} collective-permute-done((bf16[1168,128]{1,0:T(8,128)(2,1)}, bf16[1168,128]{1,0:T(8,128)(2,1)S(1)}, u32[]{:S(2)}, u32[]{:S(2)}) %collective-permute-start.1) | collective-permute-done | bytes 299040 | tf_op jit(solution)/shard_map/ppermute | solution.py:352
  20.4 4.9 %collective-permute-done.2.refs_4_ = bf16[1168,128]{1,0:T(8,128)(2,1)S(1)} collective-permute-done((bf16[1168,128]{1,0:T(8,128)(2,1)}, bf16[1168,128]{1,0:T(8,128)(2,1)S(1)}, u32[]{:S(2)}, u32[]{:S(2)}) %collective-permute-start.2) | collective-permute-done | bytes 299040 | tf_op jit(solution)/shard_map/ppermute | solution.py:352
  25.3 0.1 collective-permute-done.3.refs_2_
  25.4 1.6 %collective-permute-start.4 = (bf16[384,1024]{1,0:T(8,128)(2,1)S(1)}, bf16[384,1024]{1,0:T(8,128)(2,1)S(1)}, u32[]{:S(2)}, u32[]{:S(2)}) collective-permute-start(bf16[384,1024]{1,0:T(8,128)(2,1)S(1)} %collective-permute-done.o_ref), channel_id=1, source_target_pairs={{0,1},{1,2},{2,3},{3,0},{4,5},{5,6},{6,7},{7,4},{8,9},{9,10},{10,1... | collective-permute-start | bytes 2359304 | tf_op jit(solution)/shard_map/ppermute | solution.py:355
  27.0 0.2 collective-permute-start.5
  27.2 2.5 %collective-permute-start.6 = (bf16[1168,128]{1,0:T(8,128)(2,1)S(1)}, bf16[1168,128]{1,0:T(8,128)(2,1)S(1)}, u32[]{:S(2)}, u32[]{:S(2)}) collective-permute-start(bf16[1168,128]{1,0:T(8,128)(2,1)S(1)} %get-tuple-element.64), channel_id=1, source_target_pairs={{0,20},{4,16},{8,28},{12,24},{16,4},{20,0},{24,12},{28,8},{1,21},{... | collective-permute-start | bytes 897032 | tf_op jit(solution)/shard_map/ppermute | solution.py:352
  29.7 0.6 collective-permute-start.8
  30.3 1.0 shard_map.87.refs_0_
  31.3 6.0 %collective-permute-done.5.refs_7_ = bf16[1168,128]{1,0:T(8,128)(2,1)S(1)} collective-permute-done((bf16[1168,128]{1,0:T(8,128)(2,1)S(1)}, bf16[1168,128]{1,0:T(8,128)(2,1)S(1)}, u32[]{:S(2)}, u32[]{:S(2)}) %collective-permute-start.5) | collective-permute-done | bytes 299040 | tf_op jit(solution)/shard_map/ppermute | solution.py:352
  37.3 6.1 %collective-permute-done.6.refs_5_ = bf16[1168,128]{1,0:T(8,128)(2,1)S(1)} collective-permute-done((bf16[1168,128]{1,0:T(8,128)(2,1)S(1)}, bf16[1168,128]{1,0:T(8,128)(2,1)S(1)}, u32[]{:S(2)}, u32[]{:S(2)}) %collective-permute-start.6) | collective-permute-done | bytes 299040 | tf_op jit(solution)/shard_map/ppermute | solution.py:352
  43.4 0.2 collective-permute-done.7.refs_3_
  43.6 3.0 %collective-permute-done.4.o_ref = bf16[384,1024]{1,0:T(8,128)(2,1)S(1)} collective-permute-done((bf16[384,1024]{1,0:T(8,128)(2,1)S(1)}, bf16[384,1024]{1,0:T(8,128)(2,1)S(1)}, u32[]{:S(2)}, u32[]{:S(2)}) %collective-permute-start.4) | collective-permute-done | bytes 786464 | tf_op jit(solution)/shard_map/ppermute | solution.py:355
  46.6 19.2 %shard_map.88 = (bf16[3072,128]{1,0:T(8,128)(2,1)S(1)}, bf16[3072,128]{1,0:T(8,128)(2,1)S(1)}, bf16[3072,128]{1,0:T(8,128)(2,1)S(1)}, bf16[128,3072]{1,0:T(8,128...) custom-call(s32[1]{0:T(128)} %bitcast.me_s, ...), custom_call_target="tpu_custom_call" | custom-call | flops 1811939328 | bytes 6291456 | tf_op jit(solution)/shard_map/pallas_call | solution.py:308
  65.8 1.0 shard_map.89.acc_ref
  66.9 1.0 shard_map.90
  67.9 0.1 collective-permute-start.10
  68.0 1.6 %collective-permute-start.11 = (bf16[384,128]{1,0:T(8,128)(2,1)S(1)}, bf16[384,128]{1,0:T(8,128)(2,1)S(1)}, u32[]{:S(2)}, u32[]{:S(2)}) collective-permute-start(bf16[384,128]{1,0:T(8,128)(2,1)S(1)} %get-tuple-element.97), channel_id=1, source_target_pairs={{0,8},{4,12},{8,0},{12,4},{16,24},{20,28},{24,16},{28,20},{1,9},{5... | collective-permute-start | bytes 294920 | tf_op jit(solution)/shard_map/ppermute | solution.py:352
  69.5 0.3 collective-permute-start.12
  69.8 1.6 %collective-permute-start.13 = (bf16[384,128]{1,0:T(8,128)(2,1)S(1)}, bf16[384,128]{1,0:T(8,128)(2,1)S(1)}, u32[]{:S(2)}, u32[]{:S(2)}) collective-permute-start(bf16[384,128]{1,0:T(8,128)(2,1)S(1)} %get-tuple-element.99), channel_id=1, source_target_pairs={{0,16},{4,20},{8,24},{12,28},{16,0},{20,4},{24,8},{28,12},{1,17},{... | collective-permute-start | bytes 294920 | tf_op jit(solution)/shard_map/ppermute | solution.py:352
  71.5 0.1 collective-permute-start.14
  71.5 1.3 collective-permute-start.15
  72.8 0.8 collective-permute-done.11.refs_2_
  73.6 0.6 collective-permute-start.16
  74.2 0.6 collective-permute-done.12.refs_3_
  74.8 0.5 collective-permute-done.13.refs_4_
  75.3 5.5 %collective-permute-done.14.refs_5_ = bf16[384,128]{1,0:T(8,128)(2,1)S(1)} collective-permute-done((bf16[384,128]{1,0:T(8,128)(2,1)S(1)}, bf16[384,128]{1,0:T(8,128)(2,1)S(1)}, u32[]{:S(2)}, u32[]{:S(2)}) %collective-permute-start.14) | collective-permute-done | bytes 98336 | tf_op jit(solution)/shard_map/ppermute | solution.py:352
  80.8 19.8 %shard_map.91 = (bf16[1152,128]{1,0:T(8,128)(2,1)S(1)}, bf16[1152,128]{1,0:T(8,128)(2,1)S(1)}, bf16[1152,128]{1,0:T(8,128)(2,1)S(1)}, bf16[1152,128]{1,0:T(8,128...) custom-call(s32[1]{0:T(128)} %bitcast.me_s, ...), custom_call_target="tpu_custom_call" | custom-call | flops 3019898880 | bytes 6291456 | tf_op jit(solution)/shard_map/pallas_call | solution.py:334
  100.6 0.3 collective-permute-start.17
  100.9 1.5 %collective-permute-start.18 = (bf16[1152,128]{1,0:T(8,128)(2,1)S(1)}, bf16[1152,128]{1,0:T(8,128)(2,1)S(1)}, u32[]{:S(2)}, u32[]{:S(2)}) collective-permute-start(bf16[1152,128]{1,0:T(8,128)(2,1)S(1)} %get-tuple-element.105), channel_id=1, source_target_pairs={{0,8},{4,12},{8,0},{12,4},{16,24},{20,28},{24,16},{28,20},{1,9},{5... | collective-permute-start | bytes 884744 | tf_op jit(solution)/shard_map/ppermute | solution.py:352
  102.4 0.1 collective-permute-start.19
  102.5 1.5 %collective-permute-start.20 = (bf16[1152,128]{1,0:T(8,128)(2,1)S(1)}, bf16[1152,128]{1,0:T(8,128)(2,1)S(1)}, u32[]{:S(2)}, u32[]{:S(2)}) collective-permute-start(bf16[1152,128]{1,0:T(8,128)(2,1)S(1)} %get-tuple-element.107), channel_id=1, source_target_pairs={{0,16},{4,20},{8,24},{12,28},{16,0},{20,4},{24,8},{28,12},{1,17},{... | collective-permute-start | bytes 884744 | tf_op jit(solution)/shard_map/ppermute | solution.py:352
  104.0 0.4 collective-permute-start.21
  104.4 1.2 collective-permute-start.22
  105.6 5.1 %collective-permute-done.18.refs_2_ = bf16[1152,128]{1,0:T(8,128)(2,1)S(1)} collective-permute-done((bf16[1152,128]{1,0:T(8,128)(2,1)S(1)}, bf16[1152,128]{1,0:T(8,128)(2,1)S(1)}, u32[]{:S(2)}, u32[]{:S(2)}) %collective-permute-start.18) | collective-permute-done | bytes 294944 | tf_op jit(solution)/shard_map/ppermute | solution.py:352
  110.7 5.3 %collective-permute-done.19.refs_3_ = bf16[1152,128]{1,0:T(8,128)(2,1)S(1)} collective-permute-done((bf16[1152,128]{1,0:T(8,128)(2,1)S(1)}, bf16[1152,128]{1,0:T(8,128)(2,1)S(1)}, u32[]{:S(2)}, u32[]{:S(2)}) %collective-permute-start.19) | collective-permute-done | bytes 294944 | tf_op jit(solution)/shard_map/ppermute | solution.py:352
  116.1 14.5 %collective-permute-done.21.refs_5_ = bf16[1152,128]{1,0:T(8,128)(2,1)S(1)} collective-permute-done((bf16[1152,128]{1,0:T(8,128)(2,1)S(1)}, bf16[1152,128]{1,0:T(8,128)(2,1)S(1)}, u32[]{:S(2)}, u32[]{:S(2)}) %collective-permute-start.21) | collective-permute-done | bytes 294944 | tf_op jit(solution)/shard_map/ppermute | solution.py:352
  130.6 2.1 %shard_map.92 = (bf16[384,1024]{1,0:T(8,128)(2,1)}, bf16[384,1024]{1,0:T(8,128)(2,1)}, bf16[384,1024]{1,0:T(8,128)(2,1)}) custom-call(s32[1]{0:T(128)} %bitcast.me_s, bf16[1152,128]{1,0:T(8,128)(2,1)S(1)} %get-tuple-element.103.refs_0_, bf16[1152,128]{1,0:T(8,128)(2,1)S(1)} %collective-permute-done.17.refs_1_, ...), custom_call_target="tpu_custom_call" | custom-call | tf_op jit(solution)/shard_map/pallas_call | solution.py:78
  (19 shorter events, 0.1 us)
Async XLA Ops:
  0.6 24.8 %collective-permute-start = (bf16[384,1024]{1,0:T(8,128)(2,1)}, bf16[384,1024]{1,0:T(8,128)(2,1)S(1)}, u32[]{:S(2)}, u32[]{:S(2)}) collective-permute-start(bf16[384,1024]{1,0:T(8,128)(2,1)} %o_ref.1), channel_id=1, source_target_pairs={{0,1},{1,2},{2,3},{3,0},{4,5},{5,6},{6,7},{7,4},{8,9},{9,10},{10,1... | collective-permute-start | bytes 2359304 | tf_op jit(solution)/shard_map/ppermute | solution.py:355
  3.7 1.1 copy-start
  4.8 1.1 copy-start.1
  6.0 1.1 copy-start.2
  7.1 0.7 copy-start.4
  9.2 11.2 %collective-permute-start.1 = (bf16[1168,128]{1,0:T(8,128)(2,1)}, bf16[1168,128]{1,0:T(8,128)(2,1)S(1)}, u32[]{:S(2)}, u32[]{:S(2)}) collective-permute-start(bf16[1168,128]{1,0:T(8,128)(2,1)} %get-tuple-element.58), channel_id=1, source_target_pairs={{0,24},{4,28},{8,16},{12,20},{16,8},{20,12},{24,0},{28,4},{1,25},{... | collective-permute-start | bytes 897032 | tf_op jit(solution)/shard_map/ppermute | solution.py:352
  11.7 13.6 %collective-permute-start.2 = (bf16[1168,128]{1,0:T(8,128)(2,1)}, bf16[1168,128]{1,0:T(8,128)(2,1)S(1)}, u32[]{:S(2)}, u32[]{:S(2)}) collective-permute-start(bf16[1168,128]{1,0:T(8,128)(2,1)} %get-tuple-element.59), channel_id=1, source_target_pairs={{0,16},{4,20},{8,24},{12,28},{16,0},{20,4},{24,8},{28,12},{1,17},{... | collective-permute-start | bytes 897032 | tf_op jit(solution)/shard_map/ppermute | solution.py:352
  12.2 13.2 %collective-permute-start.3 = (bf16[1168,128]{1,0:T(8,128)(2,1)S(1)}, bf16[1168,128]{1,0:T(8,128)(2,1)S(1)}, u32[]{:S(2)}, u32[]{:S(2)}) collective-permute-start(bf16[1168,128]{1,0:T(8,128)(2,1)S(1)} %get-tuple-element.60), channel_id=1, source_target_pairs={{0,8},{4,12},{8,0},{12,4},{16,24},{20,28},{24,16},{28,20},{1,9},{5... | collective-permute-start | bytes 897032 | tf_op jit(solution)/shard_map/ppermute | solution.py:352
  12.7 4.5 %copy-start.3 = (bf16[384,1024]{1,0:T(8,128)(2,1)S(1)}, bf16[384,1024]{1,0:T(8,128)(2,1)}, u32[]{:S(2)}) copy-start(bf16[384,1024]{1,0:T(8,128)(2,1)} %o_ref.1) | copy-start | bytes 2359300
  25.4 21.2 %collective-permute-start.4 = (bf16[384,1024]{1,0:T(8,128)(2,1)S(1)}, bf16[384,1024]{1,0:T(8,128)(2,1)S(1)}, u32[]{:S(2)}, u32[]{:S(2)}) collective-permute-start(bf16[384,1024]{1,0:T(8,128)(2,1)S(1)} %collective-permute-done.o_ref), channel_id=1, source_target_pairs={{0,1},{1,2},{2,3},{3,0},{4,5},{5,6},{6,7},{7,4},{8,9},{9,10},{10,1... | collective-permute-start | bytes 2359304 | tf_op jit(solution)/shard_map/ppermute | solution.py:355
  27.0 10.3 %collective-permute-start.5 = (bf16[1168,128]{1,0:T(8,128)(2,1)S(1)}, bf16[1168,128]{1,0:T(8,128)(2,1)S(1)}, u32[]{:S(2)}, u32[]{:S(2)}) collective-permute-start(bf16[1168,128]{1,0:T(8,128)(2,1)S(1)} %get-tuple-element.63), channel_id=1, source_target_pairs={{0,28},{4,24},{8,20},{12,16},{16,12},{20,8},{24,4},{28,0},{1,29},{... | collective-permute-start | bytes 897032 | tf_op jit(solution)/shard_map/ppermute | solution.py:352
  27.2 16.2 %collective-permute-start.6 = (bf16[1168,128]{1,0:T(8,128)(2,1)S(1)}, bf16[1168,128]{1,0:T(8,128)(2,1)S(1)}, u32[]{:S(2)}, u32[]{:S(2)}) collective-permute-start(bf16[1168,128]{1,0:T(8,128)(2,1)S(1)} %get-tuple-element.64), channel_id=1, source_target_pairs={{0,20},{4,16},{8,28},{12,24},{16,4},{20,0},{24,12},{28,8},{1,21},{... | collective-permute-start | bytes 897032 | tf_op jit(solution)/shard_map/ppermute | solution.py:352
  29.6 14.0 %collective-permute-start.7 = (bf16[1168,128]{1,0:T(8,128)(2,1)S(1)}, bf16[1168,128]{1,0:T(8,128)(2,1)S(1)}, u32[]{:S(2)}, u32[]{:S(2)}) collective-permute-start(bf16[1168,128]{1,0:T(8,128)(2,1)S(1)} %get-tuple-element.65), channel_id=1, source_target_pairs={{0,12},{4,8},{8,4},{12,0},{16,28},{20,24},{24,20},{28,16},{1,13},{... | collective-permute-start | bytes 897032 | tf_op jit(solution)/shard_map/ppermute | solution.py:352
  29.7 14.0 %collective-permute-start.8 = (bf16[1168,128]{1,0:T(8,128)(2,1)S(1)}, bf16[1168,128]{1,0:T(8,128)(2,1)S(1)}, u32[]{:S(2)}, u32[]{:S(2)}) collective-permute-start(bf16[1168,128]{1,0:T(8,128)(2,1)S(1)} %get-tuple-element.66), channel_id=1, source_target_pairs={{0,4},{4,0},{8,12},{12,8},{16,20},{20,16},{24,28},{28,24},{1,5},{5... | collective-permute-start | bytes 897032 | tf_op jit(solution)/shard_map/ppermute | solution.py:352
  46.6 20.3 %collective-permute-start.9 = (bf16[384,1024]{1,0:T(8,128)(2,1)S(1)}, bf16[384,1024]{1,0:T(8,128)(2,1)S(1)}, u32[]{:S(2)}, u32[]{:S(2)}) collective-permute-start(bf16[384,1024]{1,0:T(8,128)(2,1)S(1)} %collective-permute-done.4.o_ref), channel_id=1, source_target_pairs={{0,1},{1,2},{2,3},{3,0},{4,5},{5,6},{6,7},{7,4},{8,9},{9,10},{10,1... | collective-permute-start | bytes 2359304 | tf_op jit(solution)/shard_map/ppermute | solution.py:355
  67.9 3.6 %collective-permute-start.10 = (bf16[384,128]{1,0:T(8,128)(2,1)S(1)}, bf16[384,128]{1,0:T(8,128)(2,1)S(1)}, u32[]{:S(2)}, u32[]{:S(2)}) collective-permute-start(bf16[384,128]{1,0:T(8,128)(2,1)S(1)} %get-tuple-element.96), channel_id=1, source_target_pairs={{0,4},{4,0},{8,12},{12,8},{16,20},{20,16},{24,28},{28,24},{1,5},{5... | collective-permute-start | bytes 294920 | tf_op jit(solution)/shard_map/ppermute | solution.py:352
  68.0 5.7 %collective-permute-start.11 = (bf16[384,128]{1,0:T(8,128)(2,1)S(1)}, bf16[384,128]{1,0:T(8,128)(2,1)S(1)}, u32[]{:S(2)}, u32[]{:S(2)}) collective-permute-start(bf16[384,128]{1,0:T(8,128)(2,1)S(1)} %get-tuple-element.97), channel_id=1, source_target_pairs={{0,8},{4,12},{8,0},{12,4},{16,24},{20,28},{24,16},{28,20},{1,9},{5... | collective-permute-start | bytes 294920 | tf_op jit(solution)/shard_map/ppermute | solution.py:352
  69.5 5.3 %collective-permute-start.12 = (bf16[384,128]{1,0:T(8,128)(2,1)S(1)}, bf16[384,128]{1,0:T(8,128)(2,1)S(1)}, u32[]{:S(2)}, u32[]{:S(2)}) collective-permute-start(bf16[384,128]{1,0:T(8,128)(2,1)S(1)} %get-tuple-element.98), channel_id=1, source_target_pairs={{0,12},{4,8},{8,4},{12,0},{16,28},{20,24},{24,20},{28,16},{1,13},{... | collective-permute-start | bytes 294920 | tf_op jit(solution)/shard_map/ppermute | solution.py:352
  69.8 5.5 %collective-permute-start.13 = (bf16[384,128]{1,0:T(8,128)(2,1)S(1)}, bf16[384,128]{1,0:T(8,128)(2,1)S(1)}, u32[]{:S(2)}, u32[]{:S(2)}) collective-permute-start(bf16[384,128]{1,0:T(8,128)(2,1)S(1)} %get-tuple-element.99), channel_id=1, source_target_pairs={{0,16},{4,20},{8,24},{12,28},{16,0},{20,4},{24,8},{28,12},{1,17},{... | collective-permute-start | bytes 294920 | tf_op jit(solution)/shard_map/ppermute | solution.py:352
  71.5 9.3 %collective-permute-start.14 = (bf16[384,128]{1,0:T(8,128)(2,1)S(1)}, bf16[384,128]{1,0:T(8,128)(2,1)S(1)}, u32[]{:S(2)}, u32[]{:S(2)}) collective-permute-start(bf16[384,128]{1,0:T(8,128)(2,1)S(1)} %get-tuple-element.100), channel_id=1, source_target_pairs={{0,20},{4,16},{8,28},{12,24},{16,4},{20,0},{24,12},{28,8},{1,21},{... | collective-permute-start | bytes 294920 | tf_op jit(solution)/shard_map/ppermute | solution.py:352
  71.5 9.2 %collective-permute-start.15 = (bf16[384,128]{1,0:T(8,128)(2,1)S(1)}, bf16[384,128]{1,0:T(8,128)(2,1)S(1)}, u32[]{:S(2)}, u32[]{:S(2)}) collective-permute-start(bf16[384,128]{1,0:T(8,128)(2,1)S(1)} %get-tuple-element.101), channel_id=1, source_target_pairs={{0,24},{4,28},{8,16},{12,20},{16,8},{20,12},{24,0},{28,4},{1,25},{... | collective-permute-start | bytes 294920 | tf_op jit(solution)/shard_map/ppermute | solution.py:352
  73.6 7.1 %collective-permute-start.16 = (bf16[384,128]{1,0:T(8,128)(2,1)S(1)}, bf16[384,128]{1,0:T(8,128)(2,1)S(1)}, u32[]{:S(2)}, u32[]{:S(2)}) collective-permute-start(bf16[384,128]{1,0:T(8,128)(2,1)S(1)} %get-tuple-element.102), channel_id=1, source_target_pairs={{0,28},{4,24},{8,20},{12,16},{16,12},{20,8},{24,4},{28,0},{1,29},{... | collective-permute-start | bytes 294920 | tf_op jit(solution)/shard_map/ppermute | solution.py:352
  100.6 3.8 %collective-permute-start.17 = (bf16[1152,128]{1,0:T(8,128)(2,1)S(1)}, bf16[1152,128]{1,0:T(8,128)(2,1)S(1)}, u32[]{:S(2)}, u32[]{:S(2)}) collective-permute-start(bf16[1152,128]{1,0:T(8,128)(2,1)S(1)} %get-tuple-element.104), channel_id=1, source_target_pairs={{0,4},{4,0},{8,12},{12,8},{16,20},{20,16},{24,28},{28,24},{1,5},{5... | collective-permute-start | bytes 884744 | tf_op jit(solution)/shard_map/ppermute | solution.py:352
  100.9 9.8 %collective-permute-start.18 = (bf16[1152,128]{1,0:T(8,128)(2,1)S(1)}, bf16[1152,128]{1,0:T(8,128)(2,1)S(1)}, u32[]{:S(2)}, u32[]{:S(2)}) collective-permute-start(bf16[1152,128]{1,0:T(8,128)(2,1)S(1)} %get-tuple-element.105), channel_id=1, source_target_pairs={{0,8},{4,12},{8,0},{12,4},{16,24},{20,28},{24,16},{28,20},{1,9},{5... | collective-permute-start | bytes 884744 | tf_op jit(solution)/shard_map/ppermute | solution.py:352
  102.4 13.7 %collective-permute-start.19 = (bf16[1152,128]{1,0:T(8,128)(2,1)S(1)}, bf16[1152,128]{1,0:T(8,128)(2,1)S(1)}, u32[]{:S(2)}, u32[]{:S(2)}) collective-permute-start(bf16[1152,128]{1,0:T(8,128)(2,1)S(1)} %get-tuple-element.106), channel_id=1, source_target_pairs={{0,12},{4,8},{8,4},{12,0},{16,28},{20,24},{24,20},{28,16},{1,13},{... | collective-permute-start | bytes 884744 | tf_op jit(solution)/shard_map/ppermute | solution.py:352
  102.5 13.6 %collective-permute-start.20 = (bf16[1152,128]{1,0:T(8,128)(2,1)S(1)}, bf16[1152,128]{1,0:T(8,128)(2,1)S(1)}, u32[]{:S(2)}, u32[]{:S(2)}) collective-permute-start(bf16[1152,128]{1,0:T(8,128)(2,1)S(1)} %get-tuple-element.107), channel_id=1, source_target_pairs={{0,16},{4,20},{8,24},{12,28},{16,0},{20,4},{24,8},{28,12},{1,17},{... | collective-permute-start | bytes 884744 | tf_op jit(solution)/shard_map/ppermute | solution.py:352
  104.0 26.6 %collective-permute-start.21 = (bf16[1152,128]{1,0:T(8,128)(2,1)S(1)}, bf16[1152,128]{1,0:T(8,128)(2,1)S(1)}, u32[]{:S(2)}, u32[]{:S(2)}) collective-permute-start(bf16[1152,128]{1,0:T(8,128)(2,1)S(1)} %get-tuple-element.108), channel_id=1, source_target_pairs={{0,20},{4,16},{8,28},{12,24},{16,4},{20,0},{24,12},{28,8},{1,21},{... | collective-permute-start | bytes 884744 | tf_op jit(solution)/shard_map/ppermute | solution.py:352
  104.4 26.2 %collective-permute-start.22 = (bf16[1152,128]{1,0:T(8,128)(2,1)S(1)}, bf16[1152,128]{1,0:T(8,128)(2,1)S(1)}, u32[]{:S(2)}, u32[]{:S(2)}) collective-permute-start(bf16[1152,128]{1,0:T(8,128)(2,1)S(1)} %get-tuple-element.109), channel_id=1, source_target_pairs={{0,24},{4,28},{8,16},{12,20},{16,8},{20,12},{24,0},{28,4},{1,25},{... | collective-permute-start | bytes 884744 | tf_op jit(solution)/shard_map/ppermute | solution.py:352
  110.7 19.8 %collective-permute-start.23 = (bf16[1152,128]{1,0:T(8,128)(2,1)S(1)}, bf16[1152,128]{1,0:T(8,128)(2,1)S(1)}, u32[]{:S(2)}, u32[]{:S(2)}) collective-permute-start(bf16[1152,128]{1,0:T(8,128)(2,1)S(1)} %get-tuple-element.110), channel_id=1, source_target_pairs={{0,28},{4,24},{8,20},{12,16},{16,12},{20,8},{24,4},{28,0},{1,29},{... | collective-permute-start | bytes 884744 | tf_op jit(solution)/shard_map/ppermute | solution.py:352

commit v3 on v2

--- a/solution.py
+++ b/solution.py
@@ -11,6 +11,7 @@
 HD = 128
 DOC_VALUES = 8
 DOC_ROWS = 16
+ONES_ROWS = 16
 NEG_LARGE = -1e30
 VMEM_SPARE = 6 * 1024 * 1024
 
@@ -138,6 +139,13 @@
     return (key >= first_row - k0) & (key <= last_row)
 
 
+def block_sizes(total):
+    return (
+        (block_size(total, 256), block_size(total, 256)),
+        (block_size(total, 256), block_size(total, 512)),
+    )
+
+
 def plan_size(total, bq, bk):
     return sum(((q + 1) * bq + bk - 1) // bk for q in range(total // bq)) + 2
 
@@ -153,7 +161,7 @@
 
     count = 0
     for qi, low in enumerate(lows):
-        high = ((qi + 1) * bq + bk - 1) // bk
+        low, high = low // bk, ((qi + 1) * bq + bk - 1) // bk
         if own is not None:
             wanted = ((qi + 1) * bq > own[0]) & (qi * bq < own[1])
             low = jnp.where(wanted, low, jnp.maximum(low, own[0] // bk))
@@ -198,14 +206,17 @@
         first = jnp.where(docs >= value, before, first)
     first = first.astype(jnp.int32)
     first_ref[...] = first
-    lows = [jnp.min(first[:, qi * bq:(qi + 1) * bq]) // bk for qi in range(total // bq)]
+    lows = [jnp.min(first[:, qi * bq:(qi + 1) * bq]) for qi in range(total // bq)]
     fill_plan(lows, total, bq, bk, None, own_q, own_k, own_count)
     group = (me // heads) * heads * rows
     own = None if heads == peers else (group, group + heads * rows)
-    fill_plan(lows, total, bq, bk, own, plan_q, plan_k, count_ref)
+    back_q, back_k = block_sizes(total)[1]
+    lows = [jnp.min(first[:, qi * back_q:(qi + 1) * back_q]) for qi in range(total // back_q)]
+    fill_plan(lows, total, back_q, back_k, own, plan_q, plan_k, count_ref)
     qt_ref[...] = q_ref[...].T
     kt_ref[...] = k_ref[...].T
-    vt_ref[...] = v_ref[...].T
+    vt_ref[:HD, :] = v_ref[...].T
+    vt_ref[HD:, :] = jnp.ones((ONES_ROWS, total), jnp.bfloat16)
     out_ref[...] = jnp.zeros_like(out_ref)
     log_ref[...] = jnp.full_like(log_ref, NEG_LARGE)
     sum_ref[...] = jnp.zeros_like(sum_ref)
@@ -228,8 +239,9 @@
         high = p.astype(jnp.bfloat16)
         rest = (p - high.astype(jnp.float32)).astype(jnp.bfloat16)
         vt = vt_ref[:, keys]
-        out_ref[:, queries] = out_ref[:, queries] * fix + (dot32(vt, high) + dot32(vt, rest))
-        sum_ref[:, queries] = sum_ref[:, queries] * fix + jnp.sum(p, axis=0, keepdims=True)
+        sums = dot32(vt, high) + dot32(vt, rest)
+        out_ref[:, queries] = out_ref[:, queries] * fix + sums[:HD, :]
+        sum_ref[:, queries] = sum_ref[:, queries] * fix + sums[HD:HD + 1, :]
         log_ref[:, queries] = new_top
 
     pipelined(own_q, own_k, own_count, early, late, ((s0, top0), (s1, top1)))
@@ -289,8 +301,9 @@
 def attention_forward(me, blocks, rows, heads):
     peers = len(blocks)
     total = peers * rows
-    bq, bk = block_size(total, 512), block_size(total, 256)
-    size = plan_size(total, bq, bk)
+    (bq, bk), back = block_sizes(total)
+    plan = [(plan_size(total, *back),)] * 2 + [(1,)]
+    own_plan = [(plan_size(total, bq, bk),)] * 2 + [(1,)]
     vectors = [
         *[jax.ShapeDtypeStruct((total, HD), jnp.bfloat16)] * 3,
         *[jax.ShapeDtypeStruct((HD, total), jnp.bfloat16)] * 2,
@@ -298,9 +311,8 @@
         jax.ShapeDtypeStruct((HD, total), jnp.float32),
         jax.ShapeDtypeStruct((1, total), jnp.float32),
     ]
-    plan = [(size,), (size,), (1,)]
     scratch = [
-        pltpu.VMEM((HD, total), jnp.bfloat16),
+        pltpu.VMEM((HD + ONES_ROWS, total), jnp.bfloat16),
         pltpu.VMEM((1, total), jnp.float32),
         pltpu.VMEM((1, total), jnp.float32),
         *[pltpu.VMEM((bk, bq), jnp.float32), pltpu.VMEM((1, bq), jnp.float32)] * 2,
@@ -310,7 +322,7 @@
         in_specs=[SMEM_SPEC] + [VMEM_SPEC] * peers,
         out_specs=[VMEM_SPEC] * len(vectors) + [SMEM_SPEC] * 3,
         out_shape=vectors + [jax.ShapeDtypeStruct(shape, jnp.int32) for shape in plan],
-        scratch_shapes=[pltpu.SMEM(shape, jnp.int32) for shape in plan] + scratch,
+        scratch_shapes=[pltpu.SMEM(shape, jnp.int32) for shape in own_plan] + scratch,
         compiler_params=params([*blocks, *vectors], scratch),
         cost_estimate=attention_cost(total, 3),
     )(me, *blocks)
@@ -319,7 +331,7 @@
 def attention_backward(me, heads, state, blocks):
     peers, rows = len(blocks), blocks[0].shape[0]
     total = peers * rows
-    bq, bk = block_size(total, 512), block_size(total, 256)
+    bq, bk = block_sizes(total)[1]
     vectors, plan = state[:8], state[8:]
     out_shape = [jax.ShapeDtypeStruct((3 * rows, HD), jnp.bfloat16)] * heads
     scratch = [

time: 131 us -> 130 us (level); the launches traced: 133 us -> 130 us
  Pallas kernels: 46.6 us -> 41.1 us
  waiting for transfers between devices: 54.7 us -> 57.7 us
    pallas_call x1, Pallas kernels: 19.2 us -> 16.2 us  [attention_forward(): pl.pallas_call(functools.partial(forward_kernel, peers, heads, rows, bq,...]
    ppermute x3, waiting for transfers between devices: 3.01 us -> 6.01 us  [pass_on(): lax.ppermute(x, 'head', [(i, (i + 1) % groups) for i in range(groups)])]
    pallas_call x1, Pallas kernels: 19.8 us -> 17.3 us  [attention_backward(): pl.pallas_call(functools.partial(backward_kernel, peers, heads, rows, bq,...]
  transfers between devices with their start and end apart: 24 -> 24, of which waited for: 14 -> 15; matrix products, arithmetic and copies ran while one was open for 3% -> 3% of each run, Pallas kernels for 18% -> 16%
where the time goes in v3:
time: 130 us
  waiting for transfers between devices  57.7 us (44%)
  Pallas kernels  41.1 us (32%)
  starting transfers between devices  22 us (17%)
  local copies, waits for them, and re-layouts  8.62 us (7%)
    ppermute x21, waiting for transfers between devices, exchange(): lax.ppermute(x, 'seq', [(i, i ^ d) for i in range(peers)])  51.7 us
    ppermute x21, starting transfers between devices, exchange(): lax.ppermute(x, 'seq', [(i, i ^ d) for i in range(peers)])  17.4 us
    pallas_call x1, Pallas kernels, attention_backward(): pl.pallas_call(functools.partial(backward_kernel, peers, heads, rows, bq,...  17.3 us
    pallas_call x1, Pallas kernels, attention_forward(): pl.pallas_call(functools.partial(forward_kernel, peers, heads, rows, bq,...  16.2 us
    ppermute x3, waiting for transfers between devices, pass_on(): lax.ppermute(x, 'head', [(i, (i + 1) % groups) for i in range(groups)])  6.01 us
    ppermute x3, starting transfers between devices, pass_on(): lax.ppermute(x, 'head', [(i, (i + 1) % groups) for i in range(groups)])  4.66 us
    dynamic_slice x1, local copies, waits for them, and re-layouts, per_device(): lax.dynamic_slice_in_dim(out_weight, block * width, width, 1)  4.54 us
    unnamed x10, local copies, waits for them, and re-layouts  4.08 us
  transfers between devices with their start and end apart: 24, of which 15 were waited for; matrix products, arithmetic and copies ran while one was open for 3% of the time, Pallas kernels for 16%

profile of v3, /device:TPU:0, one launch (start us, length us, event | category | flops | bytes accessed | tf_op | source)
XLA Modules:
  0.0 130.1 jit_solution(8942242845474468937)
XLA Ops:
  0.6 3.1 %collective-permute-start = (bf16[384,1024]{1,0:T(8,128)(2,1)}, bf16[384,1024]{1,0:T(8,128)(2,1)S(1)}, u32[]{:S(2)}, u32[]{:S(2)}) collective-permute-start(bf16[384,1024]{1,0:T(8,128)(2,1)} %o_ref.1), channel_id=1, source_target_pairs={{0,1},{1,2},{2,3},{3,0},{4,5},{5,6},{6,7},{7,4},{8,9},{9,10},{10,1... | collective-permute-start | bytes 2359304 | tf_op jit(solution)/shard_map/ppermute | solution.py:367
  3.7 1.1 copy-done
  4.8 1.1 copy-done.1
  6.0 1.1 copy-done.2
  7.1 0.7 copy-done.4
  7.8 1.4 %shard_map.85 = (bf16[1168,128]{1,0:T(8,128)(2,1)S(1)}, bf16[1168,128]{1,0:T(8,128)(2,1)S(1)}, bf16[1168,128]{1,0:T(8,128)(2,1)S(1)}, bf16[1168,128]{1,0:T(8,128...) custom-call(s32[1]{0:T(128)} %bitcast.me_s, ...), custom_call_target="tpu_custom_call" | custom-call | tf_op jit(solution)/shard_map/pallas_call | solution.py:60
  9.2 2.4 %collective-permute-start.1 = (bf16[1168,128]{1,0:T(8,128)(2,1)}, bf16[1168,128]{1,0:T(8,128)(2,1)S(1)}, u32[]{:S(2)}, u32[]{:S(2)}) collective-permute-start(bf16[1168,128]{1,0:T(8,128)(2,1)} %get-tuple-element.58), channel_id=1, source_target_pairs={{0,24},{4,28},{8,16},{12,20},{16,8},{20,12},{24,0},{28,4},{1,25},{... | collective-permute-start | bytes 897032 | tf_op jit(solution)/shard_map/ppermute | solution.py:364
  11.7 0.5 collective-permute-start.2
  12.2 0.5 collective-permute-start.3
  12.7 4.5 %constant_dynamic-slice_fusion = (bf16[1024,1024]{1,0:T(8,128)(2,1)S(1)}, bf16[1024,1024]{1,0:T(8,128)(2,1)S(1)}, bf16[1024,1024]{1,0:T(8,128)(2,1)S(1)}, bf16[1024,1024]{1,0:T(8,128)(2,1)S(1)}) fusion(bf16[1024,4096]{1,0:T(8,128)(2,1)} %param.10, s32[]{:T(128)S(6)} %select_n.15, s32[]{:T(128)S(6)} %select_n.13, s32[]{:T(128)S(6)} %select_n.12, s32[]{:T(128)S(6)} %select_n.14), kind=kLoop, calls=%fused_computation | loop fusion | bytes 16777232 | tf_op jit(solution)/shard_map/dynamic_slice | solution.py:383
  17.3 1.0 shard_map.86.refs_0_
  18.3 2.1 %collective-permute-done.1.refs_6_ = bf16[1168,128]{1,0:T(8,128)(2,1)S(1)} collective-permute-done((bf16[1168,128]{1,0:T(8,128)(2,1)}, bf16[1168,128]{1,0:T(8,128)(2,1)S(1)}, u32[]{:S(2)}, u32[]{:S(2)}) %collective-permute-start.1) | collective-permute-done | bytes 299040 | tf_op jit(solution)/shard_map/ppermute | solution.py:364
  20.4 4.9 %collective-permute-done.2.refs_4_ = bf16[1168,128]{1,0:T(8,128)(2,1)S(1)} collective-permute-done((bf16[1168,128]{1,0:T(8,128)(2,1)}, bf16[1168,128]{1,0:T(8,128)(2,1)S(1)}, u32[]{:S(2)}, u32[]{:S(2)}) %collective-permute-start.2) | collective-permute-done | bytes 299040 | tf_op jit(solution)/shard_map/ppermute | solution.py:364
  25.3 0.1 collective-permute-done.3.refs_2_
  25.4 1.6 %collective-permute-start.4 = (bf16[384,1024]{1,0:T(8,128)(2,1)S(1)}, bf16[384,1024]{1,0:T(8,128)(2,1)S(1)}, u32[]{:S(2)}, u32[]{:S(2)}) collective-permute-start(bf16[384,1024]{1,0:T(8,128)(2,1)S(1)} %collective-permute-done.o_ref), channel_id=1, source_target_pairs={{0,1},{1,2},{2,3},{3,0},{4,5},{5,6},{6,7},{7,4},{8,9},{9,10},{10,1... | collective-permute-start | bytes 2359304 | tf_op jit(solution)/shard_map/ppermute | solution.py:367
  27.0 0.2 collective-permute-start.5
  27.2 2.5 %collective-permute-start.6 = (bf16[1168,128]{1,0:T(8,128)(2,1)S(1)}, bf16[1168,128]{1,0:T(8,128)(2,1)S(1)}, u32[]{:S(2)}, u32[]{:S(2)}) collective-permute-start(bf16[1168,128]{1,0:T(8,128)(2,1)S(1)} %get-tuple-element.64), channel_id=1, source_target_pairs={{0,20},{4,16},{8,28},{12,24},{16,4},{20,0},{24,12},{28,8},{1,21},{... | collective-permute-start | bytes 897032 | tf_op jit(solution)/shard_map/ppermute | solution.py:364
  29.7 0.6 collective-permute-start.8
  30.3 1.0 shard_map.87.refs_0_
  31.3 6.0 %collective-permute-done.5.refs_7_ = bf16[1168,128]{1,0:T(8,128)(2,1)S(1)} collective-permute-done((bf16[1168,128]{1,0:T(8,128)(2,1)S(1)}, bf16[1168,128]{1,0:T(8,128)(2,1)S(1)}, u32[]{:S(2)}, u32[]{:S(2)}) %collective-permute-start.5) | collective-permute-done | bytes 299040 | tf_op jit(solution)/shard_map/ppermute | solution.py:364
  37.3 6.1 %collective-permute-done.6.refs_5_ = bf16[1168,128]{1,0:T(8,128)(2,1)S(1)} collective-permute-done((bf16[1168,128]{1,0:T(8,128)(2,1)S(1)}, bf16[1168,128]{1,0:T(8,128)(2,1)S(1)}, u32[]{:S(2)}, u32[]{:S(2)}) %collective-permute-start.6) | collective-permute-done | bytes 299040 | tf_op jit(solution)/shard_map/ppermute | solution.py:364
  43.4 0.2 collective-permute-done.7.refs_3_
  43.6 3.0 %collective-permute-done.4.o_ref = bf16[384,1024]{1,0:T(8,128)(2,1)S(1)} collective-permute-done((bf16[384,1024]{1,0:T(8,128)(2,1)S(1)}, bf16[384,1024]{1,0:T(8,128)(2,1)S(1)}, u32[]{:S(2)}, u32[]{:S(2)}) %collective-permute-start.4) | collective-permute-done | bytes 786464 | tf_op jit(solution)/shard_map/ppermute | solution.py:367
  46.6 16.2 %shard_map.88 = (bf16[3072,128]{1,0:T(8,128)(2,1)S(1)}, bf16[3072,128]{1,0:T(8,128)(2,1)S(1)}, bf16[3072,128]{1,0:T(8,128)(2,1)S(1)}, bf16[128,3072]{1,0:T(8,128...) custom-call(s32[1]{0:T(128)} %bitcast.me_s, ...), custom_call_target="tpu_custom_call" | custom-call | flops 1811939328 | bytes 6291456 | tf_op jit(solution)/shard_map/pallas_call | solution.py:320
  62.8 1.0 shard_map.89.acc_ref
  63.8 3.1 %collective-permute-done.9.o_ref = bf16[384,1024]{1,0:T(8,128)(2,1)S(1)} collective-permute-done((bf16[384,1024]{1,0:T(8,128)(2,1)S(1)}, bf16[384,1024]{1,0:T(8,128)(2,1)S(1)}, u32[]{:S(2)}, u32[]{:S(2)}) %collective-permute-start.9) | collective-permute-done | bytes 786464 | tf_op jit(solution)/shard_map/ppermute | solution.py:367
  66.9 1.0 shard_map.90
  67.9 0.1 collective-permute-start.10
  68.0 1.6 %collective-permute-start.11 = (bf16[384,128]{1,0:T(8,128)(2,1)S(1)}, bf16[384,128]{1,0:T(8,128)(2,1)S(1)}, u32[]{:S(2)}, u32[]{:S(2)}) collective-permute-start(bf16[384,128]{1,0:T(8,128)(2,1)S(1)} %get-tuple-element.97), channel_id=1, source_target_pairs={{0,8},{4,12},{8,0},{12,4},{16,24},{20,28},{24,16},{28,20},{1,9},{5... | collective-permute-start | bytes 294920 | tf_op jit(solution)/shard_map/ppermute | solution.py:364
  69.5 0.3 collective-permute-start.12
  69.8 1.6 %collective-permute-start.13 = (bf16[384,128]{1,0:T(8,128)(2,1)S(1)}, bf16[384,128]{1,0:T(8,128)(2,1)S(1)}, u32[]{:S(2)}, u32[]{:S(2)}) collective-permute-start(bf16[384,128]{1,0:T(8,128)(2,1)S(1)} %get-tuple-element.99), channel_id=1, source_target_pairs={{0,16},{4,20},{8,24},{12,28},{16,0},{20,4},{24,8},{28,12},{1,17},{... | collective-permute-start | bytes 294920 | tf_op jit(solution)/shard_map/ppermute | solution.py:364
  71.5 1.3 collective-permute-start.15
  72.8 0.8 collective-permute-done.11.refs_2_
  73.6 0.6 collective-permute-start.16
  74.2 0.6 collective-permute-done.12.refs_3_
  74.8 0.5 collective-permute-done.13.refs_4_
  75.3 5.5 %collective-permute-done.14.refs_5_ = bf16[384,128]{1,0:T(8,128)(2,1)S(1)} collective-permute-done((bf16[384,128]{1,0:T(8,128)(2,1)S(1)}, bf16[384,128]{1,0:T(8,128)(2,1)S(1)}, u32[]{:S(2)}, u32[]{:S(2)}) %collective-permute-start.14) | collective-permute-done | bytes 98336 | tf_op jit(solution)/shard_map/ppermute | solution.py:364
  80.8 17.3 %shard_map.91 = (bf16[1152,128]{1,0:T(8,128)(2,1)S(1)}, bf16[1152,128]{1,0:T(8,128)(2,1)S(1)}, bf16[1152,128]{1,0:T(8,128)(2,1)S(1)}, bf16[1152,128]{1,0:T(8,128...) custom-call(s32[1]{0:T(128)} %bitcast.me_s, ...), custom_call_target="tpu_custom_call" | custom-call | flops 3019898880 | bytes 6291456 | tf_op jit(solution)/shard_map/pallas_call | solution.py:346
  98.1 0.3 collective-permute-start.17
  98.4 1.5 %collective-permute-start.18 = (bf16[1152,128]{1,0:T(8,128)(2,1)S(1)}, bf16[1152,128]{1,0:T(8,128)(2,1)S(1)}, u32[]{:S(2)}, u32[]{:S(2)}) collective-permute-start(bf16[1152,128]{1,0:T(8,128)(2,1)S(1)} %get-tuple-element.105), channel_id=1, source_target_pairs={{0,8},{4,12},{8,0},{12,4},{16,24},{20,28},{24,16},{28,20},{1,9},{5... | collective-permute-start | bytes 884744 | tf_op jit(solution)/shard_map/ppermute | solution.py:364
  99.9 0.1 collective-permute-start.19
  100.0 1.5 %collective-permute-start.20 = (bf16[1152,128]{1,0:T(8,128)(2,1)S(1)}, bf16[1152,128]{1,0:T(8,128)(2,1)S(1)}, u32[]{:S(2)}, u32[]{:S(2)}) collective-permute-start(bf16[1152,128]{1,0:T(8,128)(2,1)S(1)} %get-tuple-element.107), channel_id=1, source_target_pairs={{0,16},{4,20},{8,24},{12,28},{16,0},{20,4},{24,8},{28,12},{1,17},{... | collective-permute-start | bytes 884744 | tf_op jit(solution)/shard_map/ppermute | solution.py:364
  101.5 0.4 collective-permute-start.21
  101.9 1.2 collective-permute-start.22
  103.1 5.1 %collective-permute-done.18.refs_2_ = bf16[1152,128]{1,0:T(8,128)(2,1)S(1)} collective-permute-done((bf16[1152,128]{1,0:T(8,128)(2,1)S(1)}, bf16[1152,128]{1,0:T(8,128)(2,1)S(1)}, u32[]{:S(2)}, u32[]{:S(2)}) %collective-permute-start.18) | collective-permute-done | bytes 294944 | tf_op jit(solution)/shard_map/ppermute | solution.py:364
  108.2 5.4 %collective-permute-done.19.refs_3_ = bf16[1152,128]{1,0:T(8,128)(2,1)S(1)} collective-permute-done((bf16[1152,128]{1,0:T(8,128)(2,1)S(1)}, bf16[1152,128]{1,0:T(8,128)(2,1)S(1)}, u32[]{:S(2)}, u32[]{:S(2)}) %collective-permute-start.19) | collective-permute-done | bytes 294944 | tf_op jit(solution)/shard_map/ppermute | solution.py:364
  113.6 14.5 %collective-permute-done.21.refs_5_ = bf16[1152,128]{1,0:T(8,128)(2,1)S(1)} collective-permute-done((bf16[1152,128]{1,0:T(8,128)(2,1)S(1)}, bf16[1152,128]{1,0:T(8,128)(2,1)S(1)}, u32[]{:S(2)}, u32[]{:S(2)}) %collective-permute-start.21) | collective-permute-done | bytes 294944 | tf_op jit(solution)/shard_map/ppermute | solution.py:364
  128.1 2.1 %shard_map.92 = (bf16[384,1024]{1,0:T(8,128)(2,1)}, bf16[384,1024]{1,0:T(8,128)(2,1)}, bf16[384,1024]{1,0:T(8,128)(2,1)}) custom-call(s32[1]{0:T(128)} %bitcast.me_s, bf16[1152,128]{1,0:T(8,128)(2,1)S(1)} %get-tuple-element.103.refs_0_, bf16[1152,128]{1,0:T(8,128)(2,1)S(1)} %collective-permute-done.17.refs_1_, ...), custom_call_target="tpu_custom_call" | custom-call | tf_op jit(solution)/shard_map/pallas_call | solution.py:79
  (19 shorter events, 0.1 us)
Async XLA Ops:
  0.6 24.8 %collective-permute-start = (bf16[384,1024]{1,0:T(8,128)(2,1)}, bf16[384,1024]{1,0:T(8,128)(2,1)S(1)}, u32[]{:S(2)}, u32[]{:S(2)}) collective-permute-start(bf16[384,1024]{1,0:T(8,128)(2,1)} %o_ref.1), channel_id=1, source_target_pairs={{0,1},{1,2},{2,3},{3,0},{4,5},{5,6},{6,7},{7,4},{8,9},{9,10},{10,1... | collective-permute-start | bytes 2359304 | tf_op jit(solution)/shard_map/ppermute | solution.py:367
  3.7 1.1 copy-start
  4.8 1.1 copy-start.1
  6.0 1.1 copy-start.2
  7.1 0.7 copy-start.4
  9.2 11.2 %collective-permute-start.1 = (bf16[1168,128]{1,0:T(8,128)(2,1)}, bf16[1168,128]{1,0:T(8,128)(2,1)S(1)}, u32[]{:S(2)}, u32[]{:S(2)}) collective-permute-start(bf16[1168,128]{1,0:T(8,128)(2,1)} %get-tuple-element.58), channel_id=1, source_target_pairs={{0,24},{4,28},{8,16},{12,20},{16,8},{20,12},{24,0},{28,4},{1,25},{... | collective-permute-start | bytes 897032 | tf_op jit(solution)/shard_map/ppermute | solution.py:364
  11.7 13.6 %collective-permute-start.2 = (bf16[1168,128]{1,0:T(8,128)(2,1)}, bf16[1168,128]{1,0:T(8,128)(2,1)S(1)}, u32[]{:S(2)}, u32[]{:S(2)}) collective-permute-start(bf16[1168,128]{1,0:T(8,128)(2,1)} %get-tuple-element.59), channel_id=1, source_target_pairs={{0,16},{4,20},{8,24},{12,28},{16,0},{20,4},{24,8},{28,12},{1,17},{... | collective-permute-start | bytes 897032 | tf_op jit(solution)/shard_map/ppermute | solution.py:364
  12.2 13.2 %collective-permute-start.3 = (bf16[1168,128]{1,0:T(8,128)(2,1)S(1)}, bf16[1168,128]{1,0:T(8,128)(2,1)S(1)}, u32[]{:S(2)}, u32[]{:S(2)}) collective-permute-start(bf16[1168,128]{1,0:T(8,128)(2,1)S(1)} %get-tuple-element.60), channel_id=1, source_target_pairs={{0,8},{4,12},{8,0},{12,4},{16,24},{20,28},{24,16},{28,20},{1,9},{5... | collective-permute-start | bytes 897032 | tf_op jit(solution)/shard_map/ppermute | solution.py:364
  12.7 4.5 %copy-start.3 = (bf16[384,1024]{1,0:T(8,128)(2,1)S(1)}, bf16[384,1024]{1,0:T(8,128)(2,1)}, u32[]{:S(2)}) copy-start(bf16[384,1024]{1,0:T(8,128)(2,1)} %o_ref.1) | copy-start | bytes 2359300
  25.4 21.2 %collective-permute-start.4 = (bf16[384,1024]{1,0:T(8,128)(2,1)S(1)}, bf16[384,1024]{1,0:T(8,128)(2,1)S(1)}, u32[]{:S(2)}, u32[]{:S(2)}) collective-permute-start(bf16[384,1024]{1,0:T(8,128)(2,1)S(1)} %collective-permute-done.o_ref), channel_id=1, source_target_pairs={{0,1},{1,2},{2,3},{3,0},{4,5},{5,6},{6,7},{7,4},{8,9},{9,10},{10,1... | collective-permute-start | bytes 2359304 | tf_op jit(solution)/shard_map/ppermute | solution.py:367
  27.0 10.3 %collective-permute-start.5 = (bf16[1168,128]{1,0:T(8,128)(2,1)S(1)}, bf16[1168,128]{1,0:T(8,128)(2,1)S(1)}, u32[]{:S(2)}, u32[]{:S(2)}) collective-permute-start(bf16[1168,128]{1,0:T(8,128)(2,1)S(1)} %get-tuple-element.63), channel_id=1, source_target_pairs={{0,28},{4,24},{8,20},{12,16},{16,12},{20,8},{24,4},{28,0},{1,29},{... | collective-permute-start | bytes 897032 | tf_op jit(solution)/shard_map/ppermute | solution.py:364
  27.2 16.2 %collective-permute-start.6 = (bf16[1168,128]{1,0:T(8,128)(2,1)S(1)}, bf16[1168,128]{1,0:T(8,128)(2,1)S(1)}, u32[]{:S(2)}, u32[]{:S(2)}) collective-permute-start(bf16[1168,128]{1,0:T(8,128)(2,1)S(1)} %get-tuple-element.64), channel_id=1, source_target_pairs={{0,20},{4,16},{8,28},{12,24},{16,4},{20,0},{24,12},{28,8},{1,21},{... | collective-permute-start | bytes 897032 | tf_op jit(solution)/shard_map/ppermute | solution.py:364
  29.6 14.0 %collective-permute-start.7 = (bf16[1168,128]{1,0:T(8,128)(2,1)S(1)}, bf16[1168,128]{1,0:T(8,128)(2,1)S(1)}, u32[]{:S(2)}, u32[]{:S(2)}) collective-permute-start(bf16[1168,128]{1,0:T(8,128)(2,1)S(1)} %get-tuple-element.65), channel_id=1, source_target_pairs={{0,12},{4,8},{8,4},{12,0},{16,28},{20,24},{24,20},{28,16},{1,13},{... | collective-permute-start | bytes 897032 | tf_op jit(solution)/shard_map/ppermute | solution.py:364
  29.7 14.0 %collective-permute-start.8 = (bf16[1168,128]{1,0:T(8,128)(2,1)S(1)}, bf16[1168,128]{1,0:T(8,128)(2,1)S(1)}, u32[]{:S(2)}, u32[]{:S(2)}) collective-permute-start(bf16[1168,128]{1,0:T(8,128)(2,1)S(1)} %get-tuple-element.66), channel_id=1, source_target_pairs={{0,4},{4,0},{8,12},{12,8},{16,20},{20,16},{24,28},{28,24},{1,5},{5... | collective-permute-start | bytes 897032 | tf_op jit(solution)/shard_map/ppermute | solution.py:364
  46.6 20.3 %collective-permute-start.9 = (bf16[384,1024]{1,0:T(8,128)(2,1)S(1)}, bf16[384,1024]{1,0:T(8,128)(2,1)S(1)}, u32[]{:S(2)}, u32[]{:S(2)}) collective-permute-start(bf16[384,1024]{1,0:T(8,128)(2,1)S(1)} %collective-permute-done.4.o_ref), channel_id=1, source_target_pairs={{0,1},{1,2},{2,3},{3,0},{4,5},{5,6},{6,7},{7,4},{8,9},{9,10},{10,1... | collective-permute-start | bytes 2359304 | tf_op jit(solution)/shard_map/ppermute | solution.py:367
  67.9 3.6 %collective-permute-start.10 = (bf16[384,128]{1,0:T(8,128)(2,1)S(1)}, bf16[384,128]{1,0:T(8,128)(2,1)S(1)}, u32[]{:S(2)}, u32[]{:S(2)}) collective-permute-start(bf16[384,128]{1,0:T(8,128)(2,1)S(1)} %get-tuple-element.96), channel_id=1, source_target_pairs={{0,4},{4,0},{8,12},{12,8},{16,20},{20,16},{24,28},{28,24},{1,5},{5... | collective-permute-start | bytes 294920 | tf_op jit(solution)/shard_map/ppermute | solution.py:364
  68.0 5.7 %collective-permute-start.11 = (bf16[384,128]{1,0:T(8,128)(2,1)S(1)}, bf16[384,128]{1,0:T(8,128)(2,1)S(1)}, u32[]{:S(2)}, u32[]{:S(2)}) collective-permute-start(bf16[384,128]{1,0:T(8,128)(2,1)S(1)} %get-tuple-element.97), channel_id=1, source_target_pairs={{0,8},{4,12},{8,0},{12,4},{16,24},{20,28},{24,16},{28,20},{1,9},{5... | collective-permute-start | bytes 294920 | tf_op jit(solution)/shard_map/ppermute | solution.py:364
  69.5 5.3 %collective-permute-start.12 = (bf16[384,128]{1,0:T(8,128)(2,1)S(1)}, bf16[384,128]{1,0:T(8,128)(2,1)S(1)}, u32[]{:S(2)}, u32[]{:S(2)}) collective-permute-start(bf16[384,128]{1,0:T(8,128)(2,1)S(1)} %get-tuple-element.98), channel_id=1, source_target_pairs={{0,12},{4,8},{8,4},{12,0},{16,28},{20,24},{24,20},{28,16},{1,13},{... | collective-permute-start | bytes 294920 | tf_op jit(solution)/shard_map/ppermute | solution.py:364
  69.8 5.5 %collective-permute-start.13 = (bf16[384,128]{1,0:T(8,128)(2,1)S(1)}, bf16[384,128]{1,0:T(8,128)(2,1)S(1)}, u32[]{:S(2)}, u32[]{:S(2)}) collective-permute-start(bf16[384,128]{1,0:T(8,128)(2,1)S(1)} %get-tuple-element.99), channel_id=1, source_target_pairs={{0,16},{4,20},{8,24},{12,28},{16,0},{20,4},{24,8},{28,12},{1,17},{... | collective-permute-start | bytes 294920 | tf_op jit(solution)/shard_map/ppermute | solution.py:364
  71.5 9.3 %collective-permute-start.14 = (bf16[384,128]{1,0:T(8,128)(2,1)S(1)}, bf16[384,128]{1,0:T(8,128)(2,1)S(1)}, u32[]{:S(2)}, u32[]{:S(2)}) collective-permute-start(bf16[384,128]{1,0:T(8,128)(2,1)S(1)} %get-tuple-element.100), channel_id=1, source_target_pairs={{0,20},{4,16},{8,28},{12,24},{16,4},{20,0},{24,12},{28,8},{1,21},{... | collective-permute-start | bytes 294920 | tf_op jit(solution)/shard_map/ppermute | solution.py:364
  71.5 9.2 %collective-permute-start.15 = (bf16[384,128]{1,0:T(8,128)(2,1)S(1)}, bf16[384,128]{1,0:T(8,128)(2,1)S(1)}, u32[]{:S(2)}, u32[]{:S(2)}) collective-permute-start(bf16[384,128]{1,0:T(8,128)(2,1)S(1)} %get-tuple-element.101), channel_id=1, source_target_pairs={{0,24},{4,28},{8,16},{12,20},{16,8},{20,12},{24,0},{28,4},{1,25},{... | collective-permute-start | bytes 294920 | tf_op jit(solution)/shard_map/ppermute | solution.py:364
  73.6 7.1 %collective-permute-start.16 = (bf16[384,128]{1,0:T(8,128)(2,1)S(1)}, bf16[384,128]{1,0:T(8,128)(2,1)S(1)}, u32[]{:S(2)}, u32[]{:S(2)}) collective-permute-start(bf16[384,128]{1,0:T(8,128)(2,1)S(1)} %get-tuple-element.102), channel_id=1, source_target_pairs={{0,28},{4,24},{8,20},{12,16},{16,12},{20,8},{24,4},{28,0},{1,29},{... | collective-permute-start | bytes 294920 | tf_op jit(solution)/shard_map/ppermute | solution.py:364
  98.1 3.8 %collective-permute-start.17 = (bf16[1152,128]{1,0:T(8,128)(2,1)S(1)}, bf16[1152,128]{1,0:T(8,128)(2,1)S(1)}, u32[]{:S(2)}, u32[]{:S(2)}) collective-permute-start(bf16[1152,128]{1,0:T(8,128)(2,1)S(1)} %get-tuple-element.104), channel_id=1, source_target_pairs={{0,4},{4,0},{8,12},{12,8},{16,20},{20,16},{24,28},{28,24},{1,5},{5... | collective-permute-start | bytes 884744 | tf_op jit(solution)/shard_map/ppermute | solution.py:364
  98.4 9.8 %collective-permute-start.18 = (bf16[1152,128]{1,0:T(8,128)(2,1)S(1)}, bf16[1152,128]{1,0:T(8,128)(2,1)S(1)}, u32[]{:S(2)}, u32[]{:S(2)}) collective-permute-start(bf16[1152,128]{1,0:T(8,128)(2,1)S(1)} %get-tuple-element.105), channel_id=1, source_target_pairs={{0,8},{4,12},{8,0},{12,4},{16,24},{20,28},{24,16},{28,20},{1,9},{5... | collective-permute-start | bytes 884744 | tf_op jit(solution)/shard_map/ppermute | solution.py:364
  99.9 13.7 %collective-permute-start.19 = (bf16[1152,128]{1,0:T(8,128)(2,1)S(1)}, bf16[1152,128]{1,0:T(8,128)(2,1)S(1)}, u32[]{:S(2)}, u32[]{:S(2)}) collective-permute-start(bf16[1152,128]{1,0:T(8,128)(2,1)S(1)} %get-tuple-element.106), channel_id=1, source_target_pairs={{0,12},{4,8},{8,4},{12,0},{16,28},{20,24},{24,20},{28,16},{1,13},{... | collective-permute-start | bytes 884744 | tf_op jit(solution)/shard_map/ppermute | solution.py:364
  100.0 13.6 %collective-permute-start.20 = (bf16[1152,128]{1,0:T(8,128)(2,1)S(1)}, bf16[1152,128]{1,0:T(8,128)(2,1)S(1)}, u32[]{:S(2)}, u32[]{:S(2)}) collective-permute-start(bf16[1152,128]{1,0:T(8,128)(2,1)S(1)} %get-tuple-element.107), channel_id=1, source_target_pairs={{0,16},{4,20},{8,24},{12,28},{16,0},{20,4},{24,8},{28,12},{1,17},{... | collective-permute-start | bytes 884744 | tf_op jit(solution)/shard_map/ppermute | solution.py:364
  101.5 26.6 %collective-permute-start.21 = (bf16[1152,128]{1,0:T(8,128)(2,1)S(1)}, bf16[1152,128]{1,0:T(8,128)(2,1)S(1)}, u32[]{:S(2)}, u32[]{:S(2)}) collective-permute-start(bf16[1152,128]{1,0:T(8,128)(2,1)S(1)} %get-tuple-element.108), channel_id=1, source_target_pairs={{0,20},{4,16},{8,28},{12,24},{16,4},{20,0},{24,12},{28,8},{1,21},{... | collective-permute-start | bytes 884744 | tf_op jit(solution)/shard_map/ppermute | solution.py:364
  101.9 26.2 %collective-permute-start.22 = (bf16[1152,128]{1,0:T(8,128)(2,1)S(1)}, bf16[1152,128]{1,0:T(8,128)(2,1)S(1)}, u32[]{:S(2)}, u32[]{:S(2)}) collective-permute-start(bf16[1152,128]{1,0:T(8,128)(2,1)S(1)} %get-tuple-element.109), channel_id=1, source_target_pairs={{0,24},{4,28},{8,16},{12,20},{16,8},{20,12},{24,0},{28,4},{1,25},{... | collective-permute-start | bytes 884744 | tf_op jit(solution)/shard_map/ppermute | solution.py:364
  108.2 19.8 %collective-permute-start.23 = (bf16[1152,128]{1,0:T(8,128)(2,1)S(1)}, bf16[1152,128]{1,0:T(8,128)(2,1)S(1)}, u32[]{:S(2)}, u32[]{:S(2)}) collective-permute-start(bf16[1152,128]{1,0:T(8,128)(2,1)S(1)} %get-tuple-element.110), channel_id=1, source_target_pairs={{0,28},{4,24},{8,20},{12,16},{16,12},{20,8},{24,4},{28,0},{1,29},{... | collective-permute-start | bytes 884744 | tf_op jit(solution)/shard_map/ppermute | solution.py:364

commit v4 on v3

--- a/solution.py
+++ b/solution.py
@@ -41,16 +41,23 @@
     return pltpu.CompilerParams(vmem_limit_bytes=total + VMEM_SPARE)
 
 
-def pack_kernel(heads, rows, me_s, q_ref, k_ref, v_ref, doc_ref, *outs):
+def pack_kernel(heads, rows, me_s, q_ref, k_ref, v_ref, doc_ref, *refs):
+    outs, done = refs[:heads], refs[heads]
     own = lax.rem(me_s[0], heads)
+    copies = []
+    for d, out in enumerate(outs):
+        columns = aligned(own ^ d, HD)
+        for part, ref in enumerate((q_ref, k_ref, v_ref)):
+            place = out.at[pl.ds(part * rows, rows), :]
+            copies.append(pltpu.make_async_copy(ref.at[:, columns], place, done.at[d, part]))
+            copies[-1].start()
     docs = doc_ref[...].astype(jnp.float32)
     docs = jnp.concatenate([docs, jnp.zeros((DOC_ROWS - docs.shape[0], HD), jnp.float32)], axis=0)
     docs = docs.astype(jnp.bfloat16)
-    for d, out in enumerate(outs):
-        columns = aligned(own ^ d, HD)
-        for part, ref in enumerate((q_ref, k_ref, v_ref)):
-            out[part * rows:(part + 1) * rows, :] = ref[:, columns]
+    for out in outs:
         out[3 * rows:, :] = docs
+    for copy in copies:
+        copy.wait()
 
 
 def pack_heads(me, q, k, v, doc_ids):
@@ -59,10 +66,11 @@
     out_shape = [jax.ShapeDtypeStruct((3 * rows + DOC_ROWS, HD), q.dtype)] * heads
     return pl.pallas_call(
         functools.partial(pack_kernel, heads, rows),
-        in_specs=[SMEM_SPEC] + [VMEM_SPEC] * 4,
+        in_specs=[SMEM_SPEC] + [pl.BlockSpec(memory_space=pltpu.HBM)] * 3 + [VMEM_SPEC],
         out_specs=[VMEM_SPEC] * heads,
         out_shape=out_shape,
-        compiler_params=params([q, k, v, *out_shape]),
+        scratch_shapes=[pltpu.SemaphoreType.DMA((heads, 3))],
+        compiler_params=params(out_shape),
     )(me, q, k, v, doc_ids.reshape(rows // HD, HD))
 
 
@@ -142,7 +150,7 @@
 def block_sizes(total):
     return (
         (block_size(total, 256), block_size(total, 256)),
-        (block_size(total, 256), block_size(total, 512)),
+        (block_size(total, 256), block_size(total, 256)),
     )
 
 
@@ -247,7 +255,7 @@
     pipelined(own_q, own_k, own_count, early, late, ((s0, top0), (s1, top1)))
     total_p = sum_ref[...]
     out_ref[...] = out_ref[...] / total_p
-    log_ref[...] = log_ref[...] + jnp.log2(total_p)
+    log_ref[...] = math.log(2.0) * (log_ref[...] + jnp.log2(total_p))
 
 
 def backward_kernel(peers, heads, rows, bq, bk, me_s, plan_q, plan_k, count_ref, q_ref, k_ref, v_ref,
@@ -256,7 +264,6 @@
     results = refs[peers:peers + heads]
     g_ref, gt_ref, dot_ref, dk_acc, dv_acc, dq_acc, p0, ds0, p1, ds1 = refs[peers + heads:]
     scale = HD ** (-0.5)
-    factor = scale * math.log2(math.e)
     me = me_s[0]
     for d, block in enumerate(blocks):
         g_ref[aligned(me ^ d, rows), :] = block[...]
@@ -269,7 +276,7 @@
     def early(qi, ki, buffer):
         p_ref, ds_ref = buffer
         keys, queries = aligned(ki, bk), aligned(qi, bq)
-        p = jnp.exp2(dot32(k_ref[keys, :], qt_ref[:, queries]) * factor - log_ref[:, queries])
+        p = jnp.exp(dot32(k_ref[keys, :], qt_ref[:, queries]) * scale - log_ref[:, queries])
         p = jnp.where(visible(first_ref[:, queries], qi * bq, ki * bk, (bk, bq)), p, 0.0)
         p_ref[...] = p.astype(jnp.bfloat16)
         dp = dot32(v_ref[keys, :], gt_ref[:, queries])
@@ -375,6 +382,9 @@
     packed = list(pack_heads(me_vector, queries, keys_in, values, doc_ids))
     received = exchange_all(packed, peers)
 
+    def share(step):
+        return len(order) * step * (step + 1) // ((groups - 2) * (groups - 1))
+
     after = lax.optimization_barrier
     features, acc = out_grad, None
     weights = []
@@ -393,7 +403,7 @@
         if not last:
             features = passed
             if step < groups - 2:
-                batch = order[step * len(order) // (groups - 2):(step + 1) * len(order) // (groups - 2)]
+                batch = order[share(step):share(step + 1)]
                 here = [received[d] for d in batch]
                 features, acc, here, weights[2:] = after((features, acc, here, weights[2:]))
                 for d, block in zip(batch, here):

time: 130 us -> 132 us (1.015)
  waiting for transfers between devices: 57.7 us -> 61 us
  Pallas kernels: 41.1 us -> 38 us
  starting transfers between devices: 22 us -> 23.7 us
    ppermute x21, waiting for transfers between devices: 51.7 us -> 55.6 us  [exchange(): lax.ppermute(x, 'seq', [(i, i ^ d) for i in range(peers)])]
    pallas_call x1, Pallas kernels: 16.2 us -> 14.1 us  [attention_forward(): pl.pallas_call(functools.partial(forward_kernel, peers, heads, rows, bq,...]
    ppermute x3, starting transfers between devices: 4.66 us -> 6.23 us  [pass_on(): lax.ppermute(x, 'head', [(i, (i + 1) % groups) for i in range(groups)])]
  transfers between devices with their start and end apart: 24 -> 24, of which waited for: 15 -> 14; matrix products, arithmetic and copies ran while one was open for 3% -> 3% of each run, Pallas kernels for 16% -> 14%
where the time goes in v4:
time: 132 us
  waiting for transfers between devices  61 us (46%)
  Pallas kernels  38 us (29%)
  starting transfers between devices  23.7 us (18%)
  local copies, waits for them, and re-layouts  8.62 us (7%)
    ppermute x21, waiting for transfers between devices, exchange(): lax.ppermute(x, 'seq', [(i, i ^ d) for i in range(peers)])  55.6 us
    ppermute x21, starting transfers between devices, exchange(): lax.ppermute(x, 'seq', [(i, i ^ d) for i in range(peers)])  17.4 us
    pallas_call x1, Pallas kernels, attention_backward(): pl.pallas_call(functools.partial(backward_kernel, peers, heads, rows, bq,...  16.2 us
    pallas_call x1, Pallas kernels, attention_forward(): pl.pallas_call(functools.partial(forward_kernel, peers, heads, rows, bq,...  14.1 us
    ppermute x3, starting transfers between devices, pass_on(): lax.ppermute(x, 'head', [(i, (i + 1) % groups) for i in range(groups)])  6.23 us
    ppermute x3, waiting for transfers between devices, pass_on(): lax.ppermute(x, 'head', [(i, (i + 1) % groups) for i in range(groups)])  5.36 us
    dynamic_slice x1, local copies, waits for them, and re-layouts, per_device(): lax.dynamic_slice_in_dim(out_weight, block * width, width, 1)  4.54 us
    unnamed x10, local copies, waits for them, and re-layouts  4.08 us
  transfers between devices with their start and end apart: 24, of which 14 were waited for; matrix products, arithmetic and copies ran while one was open for 3% of the time, Pallas kernels for 14%

profile of v4, /device:TPU:0, one launch (start us, length us, event | category | flops | bytes accessed | tf_op | source)
XLA Modules:
  0.0 132.0 jit_solution(6128959499075475920)
XLA Ops:
  0.6 3.1 %collective-permute-start = (bf16[384,1024]{1,0:T(8,128)(2,1)}, bf16[384,1024]{1,0:T(8,128)(2,1)S(1)}, u32[]{:S(2)}, u32[]{:S(2)}) collective-permute-start(bf16[384,1024]{1,0:T(8,128)(2,1)} %o_ref.1), channel_id=1, source_target_pairs={{0,1},{1,2},{2,3},{3,0},{4,5},{5,6},{6,7},{7,4},{8,9},{9,10},{10,1... | collective-permute-start | bytes 2359304 | tf_op jit(solution)/shard_map/ppermute | solution.py:374
  3.7 1.1 copy-done
  4.8 1.1 copy-done.1
  6.0 1.1 copy-done.2
  7.1 0.7 copy-done.4
  7.8 1.6 %shard_map.85 = (bf16[1168,128]{1,0:T(8,128)(2,1)S(1)}, bf16[1168,128]{1,0:T(8,128)(2,1)S(1)}, bf16[1168,128]{1,0:T(8,128)(2,1)S(1)}, bf16[1168,128]{1,0:T(8,128...) custom-call(s32[1]{0:T(128)} %bitcast.me_s, ...), custom_call_target="tpu_custom_call" | custom-call | tf_op jit(solution)/shard_map/pallas_call | solution.py:67
  9.4 2.5 %collective-permute-start.1 = (bf16[1168,128]{1,0:T(8,128)(2,1)}, bf16[1168,128]{1,0:T(8,128)(2,1)S(1)}, u32[]{:S(2)}, u32[]{:S(2)}) collective-permute-start(bf16[1168,128]{1,0:T(8,128)(2,1)} %get-tuple-element.58), channel_id=1, source_target_pairs={{0,24},{4,28},{8,16},{12,20},{16,8},{20,12},{24,0},{28,4},{1,25},{... | collective-permute-start | bytes 897032 | tf_op jit(solution)/shard_map/ppermute | solution.py:371
  11.9 0.5 collective-permute-start.2
  12.4 4.5 %constant_dynamic-slice_fusion = (bf16[1024,1024]{1,0:T(8,128)(2,1)S(1)}, bf16[1024,1024]{1,0:T(8,128)(2,1)S(1)}, bf16[1024,1024]{1,0:T(8,128)(2,1)S(1)}, bf16[1024,1024]{1,0:T(8,128)(2,1)S(1)}) fusion(bf16[1024,4096]{1,0:T(8,128)(2,1)} %param.10, s32[]{:T(128)S(6)} %select_n.15, s32[]{:T(128)S(6)} %select_n.13, s32[]{:T(128)S(6)} %select_n.12, s32[]{:T(128)S(6)} %select_n.14), kind=kLoop, calls=%fused_computation | loop fusion | bytes 16777232 | tf_op jit(solution)/shard_map/dynamic_slice | solution.py:393
  17.0 1.0 shard_map.86.refs_0_
  18.0 1.2 collective-permute-done.1.refs_6_
  19.2 6.3 %collective-permute-done.2.refs_4_ = bf16[1168,128]{1,0:T(8,128)(2,1)S(1)} collective-permute-done((bf16[1168,128]{1,0:T(8,128)(2,1)S(1)}, bf16[1168,128]{1,0:T(8,128)(2,1)S(1)}, u32[]{:S(2)}, u32[]{:S(2)}) %collective-permute-start.2) | collective-permute-done | bytes 299040 | tf_op jit(solution)/shard_map/ppermute | solution.py:371
  25.6 1.6 %collective-permute-start.3 = (bf16[384,1024]{1,0:T(8,128)(2,1)S(1)}, bf16[384,1024]{1,0:T(8,128)(2,1)S(1)}, u32[]{:S(2)}, u32[]{:S(2)}) collective-permute-start(bf16[384,1024]{1,0:T(8,128)(2,1)S(1)} %collective-permute-done.o_ref), channel_id=1, source_target_pairs={{0,1},{1,2},{2,3},{3,0},{4,5},{5,6},{6,7},{7,4},{8,9},{9,10},{10,1... | collective-permute-start | bytes 2359304 | tf_op jit(solution)/shard_map/ppermute | solution.py:374
  27.1 1.5 %collective-permute-start.4 = (bf16[1168,128]{1,0:T(8,128)(2,1)S(1)}, bf16[1168,128]{1,0:T(8,128)(2,1)S(1)}, u32[]{:S(2)}, u32[]{:S(2)}) collective-permute-start(bf16[1168,128]{1,0:T(8,128)(2,1)S(1)} %get-tuple-element.62), channel_id=1, source_target_pairs={{0,8},{4,12},{8,0},{12,4},{16,24},{20,28},{24,16},{28,20},{1,9},{5... | collective-permute-start | bytes 897032 | tf_op jit(solution)/shard_map/ppermute | solution.py:371
  28.6 0.6 collective-permute-start.5
  29.2 1.2 collective-permute-start.6
  30.3 0.6 collective-permute-start.7
  30.9 6.2 %collective-permute-done.4.refs_2_ = bf16[1168,128]{1,0:T(8,128)(2,1)S(1)} collective-permute-done((bf16[1168,128]{1,0:T(8,128)(2,1)S(1)}, bf16[1168,128]{1,0:T(8,128)(2,1)S(1)}, u32[]{:S(2)}, u32[]{:S(2)}) %collective-permute-start.4) | collective-permute-done | bytes 299040 | tf_op jit(solution)/shard_map/ppermute | solution.py:371
  37.1 1.0 shard_map.87.refs_0_
  38.2 4.4 %collective-permute-done.5.refs_7_ = bf16[1168,128]{1,0:T(8,128)(2,1)S(1)} collective-permute-done((bf16[1168,128]{1,0:T(8,128)(2,1)S(1)}, bf16[1168,128]{1,0:T(8,128)(2,1)S(1)}, u32[]{:S(2)}, u32[]{:S(2)}) %collective-permute-start.5) | collective-permute-done | bytes 299040 | tf_op jit(solution)/shard_map/ppermute | solution.py:371
  42.6 0.8 collective-permute-done.6.refs_5_
  43.4 4.3 %collective-permute-done.7.refs_3_ = bf16[1168,128]{1,0:T(8,128)(2,1)S(1)} collective-permute-done((bf16[1168,128]{1,0:T(8,128)(2,1)S(1)}, bf16[1168,128]{1,0:T(8,128)(2,1)S(1)}, u32[]{:S(2)}, u32[]{:S(2)}) %collective-permute-start.7) | collective-permute-done | bytes 299040 | tf_op jit(solution)/shard_map/ppermute | solution.py:371
  47.7 1.6 %collective-permute-start.9 = (bf16[384,1024]{1,0:T(8,128)(2,1)S(1)}, bf16[384,1024]{1,0:T(8,128)(2,1)S(1)}, u32[]{:S(2)}, u32[]{:S(2)}) collective-permute-start(bf16[384,1024]{1,0:T(8,128)(2,1)S(1)} %collective-permute-done.3.o_ref), channel_id=1, source_target_pairs={{0,1},{1,2},{2,3},{3,0},{4,5},{5,6},{6,7},{7,4},{8,9},{9,10},{10,1... | collective-permute-start | bytes 2359304 | tf_op jit(solution)/shard_map/ppermute | solution.py:374
  49.3 14.1 %shard_map.88 = (bf16[3072,128]{1,0:T(8,128)(2,1)S(1)}, bf16[3072,128]{1,0:T(8,128)(2,1)S(1)}, bf16[3072,128]{1,0:T(8,128)(2,1)S(1)}, bf16[128,3072]{1,0:T(8,128...) custom-call(s32[1]{0:T(128)} %bitcast.me_s, ...), custom_call_target="tpu_custom_call" | custom-call | flops 1811939328 | bytes 6291456 | tf_op jit(solution)/shard_map/pallas_call | solution.py:327
  63.4 1.0 shard_map.89.acc_ref
  64.4 5.4 %collective-permute-done.9.o_ref = bf16[384,1024]{1,0:T(8,128)(2,1)S(1)} collective-permute-done((bf16[384,1024]{1,0:T(8,128)(2,1)S(1)}, bf16[384,1024]{1,0:T(8,128)(2,1)S(1)}, u32[]{:S(2)}, u32[]{:S(2)}) %collective-permute-start.9) | collective-permute-done | bytes 786464 | tf_op jit(solution)/shard_map/ppermute | solution.py:374
  69.8 1.0 shard_map.90
  70.9 1.4 %collective-permute-start.11 = (bf16[384,128]{1,0:T(8,128)(2,1)S(1)}, bf16[384,128]{1,0:T(8,128)(2,1)S(1)}, u32[]{:S(2)}, u32[]{:S(2)}) collective-permute-start(bf16[384,128]{1,0:T(8,128)(2,1)S(1)} %get-tuple-element.97), channel_id=1, source_target_pairs={{0,8},{4,12},{8,0},{12,4},{16,24},{20,28},{24,16},{28,20},{1,9},{5... | collective-permute-start | bytes 294920 | tf_op jit(solution)/shard_map/ppermute | solution.py:371
  72.3 0.5 collective-permute-start.12
  72.8 1.3 collective-permute-start.13
  74.1 0.4 collective-permute-start.14
  74.5 1.2 collective-permute-start.15
  75.7 0.9 collective-permute-done.11.refs_2_
  76.6 0.6 collective-permute-start.16
  77.2 0.6 collective-permute-done.12.refs_3_
  77.8 0.6 collective-permute-done.13.refs_4_
  78.4 5.2 %collective-permute-done.14.refs_5_ = bf16[384,128]{1,0:T(8,128)(2,1)S(1)} collective-permute-done((bf16[384,128]{1,0:T(8,128)(2,1)S(1)}, bf16[384,128]{1,0:T(8,128)(2,1)S(1)}, u32[]{:S(2)}, u32[]{:S(2)}) %collective-permute-start.14) | collective-permute-done | bytes 98336 | tf_op jit(solution)/shard_map/ppermute | solution.py:371
  83.6 16.2 %shard_map.91 = (bf16[1152,128]{1,0:T(8,128)(2,1)S(1)}, bf16[1152,128]{1,0:T(8,128)(2,1)S(1)}, bf16[1152,128]{1,0:T(8,128)(2,1)S(1)}, bf16[1152,128]{1,0:T(8,128...) custom-call(s32[1]{0:T(128)} %bitcast.me_s, ...), custom_call_target="tpu_custom_call" | custom-call | flops 3019898880 | bytes 6291456 | tf_op jit(solution)/shard_map/pallas_call | solution.py:353
  99.8 0.5 collective-permute-start.17
  100.2 1.3 collective-permute-start.18
  101.5 0.2 collective-permute-start.19
  101.7 1.3 collective-permute-start.20
  103.0 0.7 collective-permute-start.21
  103.7 1.2 collective-permute-start.22
  105.0 5.1 %collective-permute-done.18.refs_2_ = bf16[1152,128]{1,0:T(8,128)(2,1)S(1)} collective-permute-done((bf16[1152,128]{1,0:T(8,128)(2,1)S(1)}, bf16[1152,128]{1,0:T(8,128)(2,1)S(1)}, u32[]{:S(2)}, u32[]{:S(2)}) %collective-permute-start.18) | collective-permute-done | bytes 294944 | tf_op jit(solution)/shard_map/ppermute | solution.py:371
  110.1 5.1 %collective-permute-done.19.refs_3_ = bf16[1152,128]{1,0:T(8,128)(2,1)S(1)} collective-permute-done((bf16[1152,128]{1,0:T(8,128)(2,1)S(1)}, bf16[1152,128]{1,0:T(8,128)(2,1)S(1)}, u32[]{:S(2)}, u32[]{:S(2)}) %collective-permute-start.19) | collective-permute-done | bytes 294944 | tf_op jit(solution)/shard_map/ppermute | solution.py:371
  115.2 14.7 %collective-permute-done.21.refs_5_ = bf16[1152,128]{1,0:T(8,128)(2,1)S(1)} collective-permute-done((bf16[1152,128]{1,0:T(8,128)(2,1)S(1)}, bf16[1152,128]{1,0:T(8,128)(2,1)S(1)}, u32[]{:S(2)}, u32[]{:S(2)}) %collective-permute-start.21) | collective-permute-done | bytes 294944 | tf_op jit(solution)/shard_map/ppermute | solution.py:371
  129.9 2.1 %shard_map.92 = (bf16[384,1024]{1,0:T(8,128)(2,1)}, bf16[384,1024]{1,0:T(8,128)(2,1)}, bf16[384,1024]{1,0:T(8,128)(2,1)}) custom-call(s32[1]{0:T(128)} %bitcast.me_s, bf16[1152,128]{1,0:T(8,128)(2,1)S(1)} %get-tuple-element.103.refs_0_, bf16[1152,128]{1,0:T(8,128)(2,1)S(1)} %collective-permute-done.17.refs_1_, ...), custom_call_target="tpu_custom_call" | custom-call | tf_op jit(solution)/shard_map/pallas_call | solution.py:87
  (19 shorter events, 0.1 us)
Async XLA Ops:
  0.6 24.9 %collective-permute-start = (bf16[384,1024]{1,0:T(8,128)(2,1)}, bf16[384,1024]{1,0:T(8,128)(2,1)S(1)}, u32[]{:S(2)}, u32[]{:S(2)}) collective-permute-start(bf16[384,1024]{1,0:T(8,128)(2,1)} %o_ref.1), channel_id=1, source_target_pairs={{0,1},{1,2},{2,3},{3,0},{4,5},{5,6},{6,7},{7,4},{8,9},{9,10},{10,1... | collective-permute-start | bytes 2359304 | tf_op jit(solution)/shard_map/ppermute | solution.py:374
  3.7 1.1 copy-start
  4.8 1.1 copy-start.1
  6.0 1.1 copy-start.2
  7.1 0.7 copy-start.4
  9.4 9.8 %collective-permute-start.1 = (bf16[1168,128]{1,0:T(8,128)(2,1)}, bf16[1168,128]{1,0:T(8,128)(2,1)S(1)}, u32[]{:S(2)}, u32[]{:S(2)}) collective-permute-start(bf16[1168,128]{1,0:T(8,128)(2,1)} %get-tuple-element.58), channel_id=1, source_target_pairs={{0,24},{4,28},{8,16},{12,20},{16,8},{20,12},{24,0},{28,4},{1,25},{... | collective-permute-start | bytes 897032 | tf_op jit(solution)/shard_map/ppermute | solution.py:371
  11.9 13.6 %collective-permute-start.2 = (bf16[1168,128]{1,0:T(8,128)(2,1)S(1)}, bf16[1168,128]{1,0:T(8,128)(2,1)S(1)}, u32[]{:S(2)}, u32[]{:S(2)}) collective-permute-start(bf16[1168,128]{1,0:T(8,128)(2,1)S(1)} %get-tuple-element.59), channel_id=1, source_target_pairs={{0,16},{4,20},{8,24},{12,28},{16,0},{20,4},{24,8},{28,12},{1,17},{... | collective-permute-start | bytes 897032 | tf_op jit(solution)/shard_map/ppermute | solution.py:371
  12.4 4.5 %copy-start.3 = (bf16[384,1024]{1,0:T(8,128)(2,1)S(1)}, bf16[384,1024]{1,0:T(8,128)(2,1)}, u32[]{:S(2)}) copy-start(bf16[384,1024]{1,0:T(8,128)(2,1)} %o_ref.1) | copy-start | bytes 2359300
  25.6 22.2 %collective-permute-start.3 = (bf16[384,1024]{1,0:T(8,128)(2,1)S(1)}, bf16[384,1024]{1,0:T(8,128)(2,1)S(1)}, u32[]{:S(2)}, u32[]{:S(2)}) collective-permute-start(bf16[384,1024]{1,0:T(8,128)(2,1)S(1)} %collective-permute-done.o_ref), channel_id=1, source_target_pairs={{0,1},{1,2},{2,3},{3,0},{4,5},{5,6},{6,7},{7,4},{8,9},{9,10},{10,1... | collective-permute-start | bytes 2359304 | tf_op jit(solution)/shard_map/ppermute | solution.py:374
  27.1 10.0 %collective-permute-start.4 = (bf16[1168,128]{1,0:T(8,128)(2,1)S(1)}, bf16[1168,128]{1,0:T(8,128)(2,1)S(1)}, u32[]{:S(2)}, u32[]{:S(2)}) collective-permute-start(bf16[1168,128]{1,0:T(8,128)(2,1)S(1)} %get-tuple-element.62), channel_id=1, source_target_pairs={{0,8},{4,12},{8,0},{12,4},{16,24},{20,28},{24,16},{28,20},{1,9},{5... | collective-permute-start | bytes 897032 | tf_op jit(solution)/shard_map/ppermute | solution.py:371
  28.6 14.0 %collective-permute-start.5 = (bf16[1168,128]{1,0:T(8,128)(2,1)S(1)}, bf16[1168,128]{1,0:T(8,128)(2,1)S(1)}, u32[]{:S(2)}, u32[]{:S(2)}) collective-permute-start(bf16[1168,128]{1,0:T(8,128)(2,1)S(1)} %get-tuple-element.63), channel_id=1, source_target_pairs={{0,28},{4,24},{8,20},{12,16},{16,12},{20,8},{24,4},{28,0},{1,29},{... | collective-permute-start | bytes 897032 | tf_op jit(solution)/shard_map/ppermute | solution.py:371
  29.2 14.3 %collective-permute-start.6 = (bf16[1168,128]{1,0:T(8,128)(2,1)S(1)}, bf16[1168,128]{1,0:T(8,128)(2,1)S(1)}, u32[]{:S(2)}, u32[]{:S(2)}) collective-permute-start(bf16[1168,128]{1,0:T(8,128)(2,1)S(1)} %get-tuple-element.64), channel_id=1, source_target_pairs={{0,20},{4,16},{8,28},{12,24},{16,4},{20,0},{24,12},{28,8},{1,21},{... | collective-permute-start | bytes 897032 | tf_op jit(solution)/shard_map/ppermute | solution.py:371
  30.3 17.4 %collective-permute-start.7 = (bf16[1168,128]{1,0:T(8,128)(2,1)S(1)}, bf16[1168,128]{1,0:T(8,128)(2,1)S(1)}, u32[]{:S(2)}, u32[]{:S(2)}) collective-permute-start(bf16[1168,128]{1,0:T(8,128)(2,1)S(1)} %get-tuple-element.65), channel_id=1, source_target_pairs={{0,12},{4,8},{8,4},{12,0},{16,28},{20,24},{24,20},{28,16},{1,13},{... | collective-permute-start | bytes 897032 | tf_op jit(solution)/shard_map/ppermute | solution.py:371
  37.1 10.6 %collective-permute-start.8 = (bf16[1168,128]{1,0:T(8,128)(2,1)S(1)}, bf16[1168,128]{1,0:T(8,128)(2,1)S(1)}, u32[]{:S(2)}, u32[]{:S(2)}) collective-permute-start(bf16[1168,128]{1,0:T(8,128)(2,1)S(1)} %get-tuple-element.66), channel_id=1, source_target_pairs={{0,4},{4,0},{8,12},{12,8},{16,20},{20,16},{24,28},{28,24},{1,5},{5... | collective-permute-start | bytes 897032 | tf_op jit(solution)/shard_map/ppermute | solution.py:371
  47.7 22.1 %collective-permute-start.9 = (bf16[384,1024]{1,0:T(8,128)(2,1)S(1)}, bf16[384,1024]{1,0:T(8,128)(2,1)S(1)}, u32[]{:S(2)}, u32[]{:S(2)}) collective-permute-start(bf16[384,1024]{1,0:T(8,128)(2,1)S(1)} %collective-permute-done.3.o_ref), channel_id=1, source_target_pairs={{0,1},{1,2},{2,3},{3,0},{4,5},{5,6},{6,7},{7,4},{8,9},{9,10},{10,1... | collective-permute-start | bytes 2359304 | tf_op jit(solution)/shard_map/ppermute | solution.py:374
  70.8 3.6 %collective-permute-start.10 = (bf16[384,128]{1,0:T(8,128)(2,1)S(1)}, bf16[384,128]{1,0:T(8,128)(2,1)S(1)}, u32[]{:S(2)}, u32[]{:S(2)}) collective-permute-start(bf16[384,128]{1,0:T(8,128)(2,1)S(1)} %get-tuple-element.96), channel_id=1, source_target_pairs={{0,4},{4,0},{8,12},{12,8},{16,20},{20,16},{24,28},{28,24},{1,5},{5... | collective-permute-start | bytes 294920 | tf_op jit(solution)/shard_map/ppermute | solution.py:371
  70.9 5.7 %collective-permute-start.11 = (bf16[384,128]{1,0:T(8,128)(2,1)S(1)}, bf16[384,128]{1,0:T(8,128)(2,1)S(1)}, u32[]{:S(2)}, u32[]{:S(2)}) collective-permute-start(bf16[384,128]{1,0:T(8,128)(2,1)S(1)} %get-tuple-element.97), channel_id=1, source_target_pairs={{0,8},{4,12},{8,0},{12,4},{16,24},{20,28},{24,16},{28,20},{1,9},{5... | collective-permute-start | bytes 294920 | tf_op jit(solution)/shard_map/ppermute | solution.py:371
  72.3 5.5 %collective-permute-start.12 = (bf16[384,128]{1,0:T(8,128)(2,1)S(1)}, bf16[384,128]{1,0:T(8,128)(2,1)S(1)}, u32[]{:S(2)}, u32[]{:S(2)}) collective-permute-start(bf16[384,128]{1,0:T(8,128)(2,1)S(1)} %get-tuple-element.98), channel_id=1, source_target_pairs={{0,12},{4,8},{8,4},{12,0},{16,28},{20,24},{24,20},{28,16},{1,13},{... | collective-permute-start | bytes 294920 | tf_op jit(solution)/shard_map/ppermute | solution.py:371
  72.8 5.6 %collective-permute-start.13 = (bf16[384,128]{1,0:T(8,128)(2,1)S(1)}, bf16[384,128]{1,0:T(8,128)(2,1)S(1)}, u32[]{:S(2)}, u32[]{:S(2)}) collective-permute-start(bf16[384,128]{1,0:T(8,128)(2,1)S(1)} %get-tuple-element.99), channel_id=1, source_target_pairs={{0,16},{4,20},{8,24},{12,28},{16,0},{20,4},{24,8},{28,12},{1,17},{... | collective-permute-start | bytes 294920 | tf_op jit(solution)/shard_map/ppermute | solution.py:371
  74.1 9.5 %collective-permute-start.14 = (bf16[384,128]{1,0:T(8,128)(2,1)S(1)}, bf16[384,128]{1,0:T(8,128)(2,1)S(1)}, u32[]{:S(2)}, u32[]{:S(2)}) collective-permute-start(bf16[384,128]{1,0:T(8,128)(2,1)S(1)} %get-tuple-element.100), channel_id=1, source_target_pairs={{0,20},{4,16},{8,28},{12,24},{16,4},{20,0},{24,12},{28,8},{1,21},{... | collective-permute-start | bytes 294920 | tf_op jit(solution)/shard_map/ppermute | solution.py:371
  74.5 9.1 %collective-permute-start.15 = (bf16[384,128]{1,0:T(8,128)(2,1)S(1)}, bf16[384,128]{1,0:T(8,128)(2,1)S(1)}, u32[]{:S(2)}, u32[]{:S(2)}) collective-permute-start(bf16[384,128]{1,0:T(8,128)(2,1)S(1)} %get-tuple-element.101), channel_id=1, source_target_pairs={{0,24},{4,28},{8,16},{12,20},{16,8},{20,12},{24,0},{28,4},{1,25},{... | collective-permute-start | bytes 294920 | tf_op jit(solution)/shard_map/ppermute | solution.py:371
  76.6 7.0 %collective-permute-start.16 = (bf16[384,128]{1,0:T(8,128)(2,1)S(1)}, bf16[384,128]{1,0:T(8,128)(2,1)S(1)}, u32[]{:S(2)}, u32[]{:S(2)}) collective-permute-start(bf16[384,128]{1,0:T(8,128)(2,1)S(1)} %get-tuple-element.102), channel_id=1, source_target_pairs={{0,28},{4,24},{8,20},{12,16},{16,12},{20,8},{24,4},{28,0},{1,29},{... | collective-permute-start | bytes 294920 | tf_op jit(solution)/shard_map/ppermute | solution.py:371
  99.8 4.0 %collective-permute-start.17 = (bf16[1152,128]{1,0:T(8,128)(2,1)S(1)}, bf16[1152,128]{1,0:T(8,128)(2,1)S(1)}, u32[]{:S(2)}, u32[]{:S(2)}) collective-permute-start(bf16[1152,128]{1,0:T(8,128)(2,1)S(1)} %get-tuple-element.104), channel_id=1, source_target_pairs={{0,4},{4,0},{8,12},{12,8},{16,20},{20,16},{24,28},{28,24},{1,5},{5... | collective-permute-start | bytes 884744 | tf_op jit(solution)/shard_map/ppermute | solution.py:371
  100.2 9.9 %collective-permute-start.18 = (bf16[1152,128]{1,0:T(8,128)(2,1)S(1)}, bf16[1152,128]{1,0:T(8,128)(2,1)S(1)}, u32[]{:S(2)}, u32[]{:S(2)}) collective-permute-start(bf16[1152,128]{1,0:T(8,128)(2,1)S(1)} %get-tuple-element.105), channel_id=1, source_target_pairs={{0,8},{4,12},{8,0},{12,4},{16,24},{20,28},{24,16},{28,20},{1,9},{5... | collective-permute-start | bytes 884744 | tf_op jit(solution)/shard_map/ppermute | solution.py:371
  101.5 13.7 %collective-permute-start.19 = (bf16[1152,128]{1,0:T(8,128)(2,1)S(1)}, bf16[1152,128]{1,0:T(8,128)(2,1)S(1)}, u32[]{:S(2)}, u32[]{:S(2)}) collective-permute-start(bf16[1152,128]{1,0:T(8,128)(2,1)S(1)} %get-tuple-element.106), channel_id=1, source_target_pairs={{0,12},{4,8},{8,4},{12,0},{16,28},{20,24},{24,20},{28,16},{1,13},{... | collective-permute-start | bytes 884744 | tf_op jit(solution)/shard_map/ppermute | solution.py:371
  101.7 13.5 %collective-permute-start.20 = (bf16[1152,128]{1,0:T(8,128)(2,1)S(1)}, bf16[1152,128]{1,0:T(8,128)(2,1)S(1)}, u32[]{:S(2)}, u32[]{:S(2)}) collective-permute-start(bf16[1152,128]{1,0:T(8,128)(2,1)S(1)} %get-tuple-element.107), channel_id=1, source_target_pairs={{0,16},{4,20},{8,24},{12,28},{16,0},{20,4},{24,8},{28,12},{1,17},{... | collective-permute-start | bytes 884744 | tf_op jit(solution)/shard_map/ppermute | solution.py:371
  103.0 26.9 %collective-permute-start.21 = (bf16[1152,128]{1,0:T(8,128)(2,1)S(1)}, bf16[1152,128]{1,0:T(8,128)(2,1)S(1)}, u32[]{:S(2)}, u32[]{:S(2)}) collective-permute-start(bf16[1152,128]{1,0:T(8,128)(2,1)S(1)} %get-tuple-element.108), channel_id=1, source_target_pairs={{0,20},{4,16},{8,28},{12,24},{16,4},{20,0},{24,12},{28,8},{1,21},{... | collective-permute-start | bytes 884744 | tf_op jit(solution)/shard_map/ppermute | solution.py:371
  103.7 26.2 %collective-permute-start.22 = (bf16[1152,128]{1,0:T(8,128)(2,1)S(1)}, bf16[1152,128]{1,0:T(8,128)(2,1)S(1)}, u32[]{:S(2)}, u32[]{:S(2)}) collective-permute-start(bf16[1152,128]{1,0:T(8,128)(2,1)S(1)} %get-tuple-element.109), channel_id=1, source_target_pairs={{0,24},{4,28},{8,16},{12,20},{16,8},{20,12},{24,0},{28,4},{1,25},{... | collective-permute-start | bytes 884744 | tf_op jit(solution)/shard_map/ppermute | solution.py:371
  110.1 19.9 %collective-permute-start.23 = (bf16[1152,128]{1,0:T(8,128)(2,1)S(1)}, bf16[1152,128]{1,0:T(8,128)(2,1)S(1)}, u32[]{:S(2)}, u32[]{:S(2)}) collective-permute-start(bf16[1152,128]{1,0:T(8,128)(2,1)S(1)} %get-tuple-element.110), channel_id=1, source_target_pairs={{0,28},{4,24},{8,20},{12,16},{16,12},{20,8},{24,4},{28,0},{1,29},{... | collective-permute-start | bytes 884744 | tf_op jit(solution)/shard_map/ppermute | solution.py:371

commit v5 on v4

--- a/solution.py
+++ b/solution.py
@@ -141,10 +141,9 @@
     )(*operands)
 
 
-def visible(first_row, q0, k0, shape):
+def at_or_before(q0, k0, shape):
     key = lax.broadcasted_iota(jnp.int32, shape, 0)
-    last_row = q0 - k0 + lax.broadcasted_iota(jnp.int32, (1, shape[1]), 1)
-    return (key >= first_row - k0) & (key <= last_row)
+    return key <= q0 - k0 + lax.broadcasted_iota(jnp.int32, (1, shape[1]), 1)
 
 
 def block_sizes(total):
@@ -167,42 +166,55 @@
 
         return at
 
-    count = 0
+    spans = []
     for qi, low in enumerate(lows):
         low, high = low // bk, ((qi + 1) * bq + bk - 1) // bk
         if own is not None:
             wanted = ((qi + 1) * bq > own[0]) & (qi * bq < own[1])
             low = jnp.where(wanted, low, jnp.maximum(low, own[0] // bk))
             high = jnp.where(wanted, high, jnp.minimum(high, (own[1] + bk - 1) // bk))
-        count = lax.fori_loop(low, high, put(qi), count)
-    count_ref[0] = (count + 1) // 2
+        whole = jnp.maximum(low, jnp.minimum(high, qi * bq // bk))
+        spans.append((low, whole, high))
+    count = 0
+    for qi, (low, whole, high) in enumerate(spans):
+        count = lax.fori_loop(low, whole, put(qi), count)
+    count_ref[0] = jnp.maximum(count - 1, 0) // 2
+    for qi, (low, whole, high) in enumerate(spans):
+        count = lax.fori_loop(whole, high, put(qi), count)
+    count_ref[1] = (count + 1) // 2
     for spare in range(2):
         plan_q[count + spare] = 0
         plan_k[count + spare] = total // bk - 1
 
 
 def pipelined(plan_q, plan_k, count_ref, early, late, buffers):
-    early(plan_q[0], plan_k[0], buffers[0])
-
-    @pl.loop(0, count_ref[0])
-    def _(i):
-        for turn in range(2):
-            now = 2 * i + turn
-            late(plan_q[now], plan_k[now], buffers[turn])
-            early(plan_q[now + 1], plan_k[now + 1], buffers[1 - turn])
+    early(plan_q[0], plan_k[0], buffers[0], True)
+
+    def turns(diagonal):
+        def body(i, carry):
+            for turn in range(2):
+                now = 2 * i + turn
+                late(plan_q[now], plan_k[now], buffers[turn])
+                early(plan_q[now + 1], plan_k[now + 1], buffers[1 - turn], diagonal)
+            return carry
+
+        return body
+
+    lax.fori_loop(0, count_ref[0], turns(False), 0)
+    lax.fori_loop(count_ref[0], count_ref[1], turns(True), 0)
 
 
 def forward_kernel(peers, heads, rows, bq, bk, me_s, *refs):
     blocks = refs[:peers]
-    q_ref, k_ref, v_ref, qt_ref, kt_ref, first_ref, out_ref, log_ref = refs[peers:peers + 8]
-    plan_q, plan_k, count_ref, own_q, own_k, own_count = refs[peers + 8:peers + 14]
-    vt_ref, doc_ref, sum_ref, s0, top0, s1, top1 = refs[peers + 14:]
+    q_ref, v_ref, kx_ref, qtx_ref, kt_ref, out_ref, log_ref = refs[peers:peers + 7]
+    plan_q, plan_k, count_ref, own_q, own_k, own_count = refs[peers + 7:peers + 13]
+    vt_ref, doc_ref, sum_ref, s0, top0, s1, top1 = refs[peers + 13:]
     total = q_ref.shape[0]
     factor = HD ** (-0.5) * math.log2(math.e)
     me = me_s[0]
     for d, block in enumerate(blocks):
         place = me ^ d
-        for part, ref in enumerate((q_ref, k_ref, v_ref)):
+        for part, ref in enumerate((q_ref, kx_ref.at[:, :HD], v_ref)):
             ref[aligned(place, rows), :] = block[part * rows:(part + 1) * rows, :]
         docs = block[3 * rows:, :].astype(jnp.float32)
         for t in range(rows // HD):
@@ -213,7 +225,6 @@
         before = jnp.sum((docs < value).astype(jnp.float32))
         first = jnp.where(docs >= value, before, first)
     first = first.astype(jnp.int32)
-    first_ref[...] = first
     lows = [jnp.min(first[:, qi * bq:(qi + 1) * bq]) for qi in range(total // bq)]
     fill_plan(lows, total, bq, bk, None, own_q, own_k, own_count)
     group = (me // heads) * heads * rows
@@ -221,19 +232,23 @@
     back_q, back_k = block_sizes(total)[1]
     lows = [jnp.min(first[:, qi * back_q:(qi + 1) * back_q]) for qi in range(total // back_q)]
     fill_plan(lows, total, back_q, back_k, own, plan_q, plan_k, count_ref)
-    qt_ref[...] = q_ref[...].T
-    kt_ref[...] = k_ref[...].T
+    same = lax.broadcasted_iota(jnp.int32, (HD, total), 0).astype(jnp.float32) == docs
+    qtx_ref[:HD, :] = q_ref[...].T
+    qtx_ref[HD:, :] = jnp.where(same, 0.0, NEG_LARGE).astype(jnp.bfloat16)
+    kx_ref[:, HD:] = jnp.where(same, 1.0, 0.0).astype(jnp.bfloat16).T
+    kt_ref[...] = kx_ref[:, :HD].T
     vt_ref[:HD, :] = v_ref[...].T
     vt_ref[HD:, :] = jnp.ones((ONES_ROWS, total), jnp.bfloat16)
     out_ref[...] = jnp.zeros_like(out_ref)
     log_ref[...] = jnp.full_like(log_ref, NEG_LARGE)
     sum_ref[...] = jnp.zeros_like(sum_ref)
 
-    def early(qi, ki, buffer):
+    def early(qi, ki, buffer, diagonal):
         s_ref, top_ref = buffer
         keys, queries = aligned(ki, bk), aligned(qi, bq)
-        s = dot32(k_ref[keys, :], qt_ref[:, queries]) * factor
-        s = jnp.where(visible(first_ref[:, queries], qi * bq, ki * bk, (bk, bq)), s, NEG_LARGE)
+        s = dot32(kx_ref[keys, :], qtx_ref[:, queries]) * factor
+        if diagonal:
+            s = jnp.where(at_or_before(qi * bq, ki * bk, (bk, bq)), s, NEG_LARGE)
         s_ref[...] = s
         top_ref[...] = jnp.max(s, axis=0, keepdims=True)
 
@@ -258,8 +273,8 @@
     log_ref[...] = math.log(2.0) * (log_ref[...] + jnp.log2(total_p))
 
 
-def backward_kernel(peers, heads, rows, bq, bk, me_s, plan_q, plan_k, count_ref, q_ref, k_ref, v_ref,
-                    qt_ref, kt_ref, first_ref, out_ref, log_ref, *refs):
+def backward_kernel(peers, heads, rows, bq, bk, me_s, plan_q, plan_k, count_ref, q_ref, v_ref,
+                    kx_ref, qtx_ref, kt_ref, out_ref, log_ref, *refs):
     blocks = refs[:peers]
     results = refs[peers:peers + heads]
     g_ref, gt_ref, dot_ref, dk_acc, dv_acc, dq_acc, p0, ds0, p1, ds1 = refs[peers + heads:]
@@ -273,11 +288,12 @@
     dv_acc[...] = jnp.zeros_like(dv_acc)
     dq_acc[...] = jnp.zeros_like(dq_acc)
 
-    def early(qi, ki, buffer):
+    def early(qi, ki, buffer, diagonal):
         p_ref, ds_ref = buffer
         keys, queries = aligned(ki, bk), aligned(qi, bq)
-        p = jnp.exp(dot32(k_ref[keys, :], qt_ref[:, queries]) * scale - log_ref[:, queries])
-        p = jnp.where(visible(first_ref[:, queries], qi * bq, ki * bk, (bk, bq)), p, 0.0)
+        p = jnp.exp(dot32(kx_ref[keys, :], qtx_ref[:, queries]) * scale - log_ref[:, queries])
+        if diagonal:
+            p = jnp.where(at_or_before(qi * bq, ki * bk, (bk, bq)), p, 0.0)
         p_ref[...] = p.astype(jnp.bfloat16)
         dp = dot32(v_ref[keys, :], gt_ref[:, queries])
         ds_ref[...] = (p * (dp - dot_ref[:, queries])).astype(jnp.bfloat16)
@@ -309,12 +325,13 @@
     peers = len(blocks)
     total = peers * rows
     (bq, bk), back = block_sizes(total)
-    plan = [(plan_size(total, *back),)] * 2 + [(1,)]
-    own_plan = [(plan_size(total, bq, bk),)] * 2 + [(1,)]
+    plan = [(plan_size(total, *back),)] * 2 + [(2,)]
+    own_plan = [(plan_size(total, bq, bk),)] * 2 + [(2,)]
     vectors = [
-        *[jax.ShapeDtypeStruct((total, HD), jnp.bfloat16)] * 3,
-        *[jax.ShapeDtypeStruct((HD, total), jnp.bfloat16)] * 2,
-        jax.ShapeDtypeStruct((1, total), jnp.int32),
+        *[jax.ShapeDtypeStruct((total, HD), jnp.bfloat16)] * 2,
+        jax.ShapeDtypeStruct((total, 2 * HD), jnp.bfloat16),
+        jax.ShapeDtypeStruct((2 * HD, total), jnp.bfloat16),
+        jax.ShapeDtypeStruct((HD, total), jnp.bfloat16),
         jax.ShapeDtypeStruct((HD, total), jnp.float32),
         jax.ShapeDtypeStruct((1, total), jnp.float32),
     ]
@@ -339,7 +356,7 @@
     peers, rows = len(blocks), blocks[0].shape[0]
     total = peers * rows
     bq, bk = block_sizes(total)[1]
-    vectors, plan = state[:8], state[8:]
+    vectors, plan = state[:7], state[7:]
     out_shape = [jax.ShapeDtypeStruct((3 * rows, HD), jnp.bfloat16)] * heads
     scratch = [
         pltpu.VMEM((total, HD), jnp.bfloat16),
@@ -352,7 +369,7 @@
     ]
     return pl.pallas_call(
         functools.partial(backward_kernel, peers, heads, rows, bq, bk),
-        in_specs=[SMEM_SPEC] * 4 + [VMEM_SPEC] * (8 + peers),
+        in_specs=[SMEM_SPEC] * 4 + [VMEM_SPEC] * (7 + peers),
         out_specs=[VMEM_SPEC] * heads,
         out_shape=out_shape,
         scratch_shapes=scratch,
@@ -373,7 +390,7 @@
     def pass_on(x):
         return lax.ppermute(x, "head", [(i, (i + 1) % groups) for i in range(groups)])
 
-    order = [*range(peers - 2, 0, -2), *range(peers - 1, 0, -2)]
+    order = [*range(2, peers, 2), *range(peers - 1, 0, -2)]
 
     def exchange_all(blocks, wanted):
         moved = {d: exchange(blocks[d % heads], d) for d in order if d < wanted}

time: 132 us -> 129 us (0.977)
  waiting for transfers between devices: 61 us -> 55 us
  Pallas kernels: 38 us -> 41.1 us
    ppermute x21, waiting for transfers between devices: 55.6 us -> 47.7 us  [exchange(): lax.ppermute(x, 'seq', [(i, i ^ d) for i in range(peers)])]
    ppermute x21, starting transfers between devices: 17.4 us -> 20.4 us  [exchange(): lax.ppermute(x, 'seq', [(i, i ^ d) for i in range(peers)])]
    pallas_call x1, Pallas kernels: 14.1 us -> 16.6 us  [attention_forward(): pl.pallas_call(functools.partial(forward_kernel, peers, heads, rows, bq,...]
    ppermute x3, starting transfers between devices: 6.23 us -> 3.82 us  [pass_on(): lax.ppermute(x, 'head', [(i, (i + 1) % groups) for i in range(groups)])]
    ppermute x3, waiting for transfers between devices: 5.36 us -> 7.25 us  [pass_on(): lax.ppermute(x, 'head', [(i, (i + 1) % groups) for i in range(groups)])]
  transfers between devices with their start and end apart: 24 -> 24, of which waited for: 14 -> 13; matrix products, arithmetic and copies ran while one was open for 3% -> 4% of each run, Pallas kernels for 14% -> 16%
where the time goes in v5:
time: 129 us; the launch traced here: 130 us
  waiting for transfers between devices  55 us (43%)
  Pallas kernels  41.1 us (32%)
  starting transfers between devices  24.2 us (19%)
  local copies, waits for them, and re-layouts  8.62 us (7%)
    ppermute x21, waiting for transfers between devices, exchange(): lax.ppermute(x, 'seq', [(i, i ^ d) for i in range(peers)])  47.7 us
    ppermute x21, starting transfers between devices, exchange(): lax.ppermute(x, 'seq', [(i, i ^ d) for i in range(peers)])  20.4 us
    pallas_call x1, Pallas kernels, attention_backward(): pl.pallas_call(functools.partial(backward_kernel, peers, heads, rows, bq,...  16.7 us
    pallas_call x1, Pallas kernels, attention_forward(): pl.pallas_call(functools.partial(forward_kernel, peers, heads, rows, bq,...  16.6 us
    ppermute x3, waiting for transfers between devices, pass_on(): lax.ppermute(x, 'head', [(i, (i + 1) % groups) for i in range(groups)])  7.25 us
    dynamic_slice x1, local copies, waits for them, and re-layouts, per_device(): lax.dynamic_slice_in_dim(out_weight, block * width, width, 1)  4.54 us
    unnamed x10, local copies, waits for them, and re-layouts  4.08 us
    ppermute x3, starting transfers between devices, pass_on(): lax.ppermute(x, 'head', [(i, (i + 1) % groups) for i in range(groups)])  3.82 us
  transfers between devices with their start and end apart: 24, of which 13 were waited for; matrix products, arithmetic and copies ran while one was open for 4% of the time, Pallas kernels for 16%

profile of v5, /device:TPU:0, one launch (start us, length us, event | category | flops | bytes accessed | tf_op | source)
XLA Modules:
  0.0 129.6 jit_solution(9573939122788643525)
XLA Ops:
  0.6 3.1 %collective-permute-start = (bf16[384,1024]{1,0:T(8,128)(2,1)}, bf16[384,1024]{1,0:T(8,128)(2,1)S(1)}, u32[]{:S(2)}, u32[]{:S(2)}) collective-permute-start(bf16[384,1024]{1,0:T(8,128)(2,1)} %o_ref.1), channel_id=1, source_target_pairs={{0,1},{1,2},{2,3},{3,0},{4,5},{5,6},{6,7},{7,4},{8,9},{9,10},{10,1... | collective-permute-start | bytes 2359304 | tf_op jit(solution)/shard_map/ppermute | solution.py:391
  3.7 1.1 copy-done
  4.8 1.1 copy-done.1
  6.0 1.1 copy-done.2
  7.1 0.7 copy-done.4
  7.8 1.6 %shard_map.85 = (bf16[1168,128]{1,0:T(8,128)(2,1)S(1)}, bf16[1168,128]{1,0:T(8,128)(2,1)S(1)}, bf16[1168,128]{1,0:T(8,128)(2,1)}, bf16[1168,128]{1,0:T(8,128)(2,...) custom-call(s32[1]{0:T(128)} %bitcast.me_s, ...), custom_call_target="tpu_custom_call" | custom-call | tf_op jit(solution)/shard_map/pallas_call | solution.py:67
  9.4 1.6 %collective-permute-start.1 = (bf16[1168,128]{1,0:T(8,128)(2,1)}, bf16[1168,128]{1,0:T(8,128)(2,1)S(1)}, u32[]{:S(2)}, u32[]{:S(2)}) collective-permute-start(bf16[1168,128]{1,0:T(8,128)(2,1)} %get-tuple-element.57), channel_id=1, source_target_pairs={{0,8},{4,12},{8,0},{12,4},{16,24},{20,28},{24,16},{28,20},{1,9},{5... | collective-permute-start | bytes 897032 | tf_op jit(solution)/shard_map/ppermute | solution.py:388
  11.0 1.5 %collective-permute-start.2 = (bf16[1168,128]{1,0:T(8,128)(2,1)S(1)}, bf16[1168,128]{1,0:T(8,128)(2,1)S(1)}, u32[]{:S(2)}, u32[]{:S(2)}) collective-permute-start(bf16[1168,128]{1,0:T(8,128)(2,1)S(1)} %get-tuple-element.58), channel_id=1, source_target_pairs={{0,16},{4,20},{8,24},{12,28},{16,0},{20,4},{24,8},{28,12},{1,17},{... | collective-permute-start | bytes 897032 | tf_op jit(solution)/shard_map/ppermute | solution.py:388
  12.5 4.5 %constant_dynamic-slice_fusion = (bf16[1024,1024]{1,0:T(8,128)(2,1)S(1)}, bf16[1024,1024]{1,0:T(8,128)(2,1)S(1)}, bf16[1024,1024]{1,0:T(8,128)(2,1)S(1)}, bf16[1024,1024]{1,0:T(8,128)(2,1)S(1)}) fusion(bf16[1024,4096]{1,0:T(8,128)(2,1)} %param.10, s32[]{:T(128)S(6)} %select_n.15, s32[]{:T(128)S(6)} %select_n.13, s32[]{:T(128)S(6)} %select_n.12, s32[]{:T(128)S(6)} %select_n.14), kind=kLoop, calls=%fused_computation | loop fusion | bytes 16777232 | tf_op jit(solution)/shard_map/dynamic_slice | solution.py:410
  17.0 1.0 shard_map.86.refs_0_
  18.1 0.2 collective-permute-done.1.refs_2_
  18.2 1.0 collective-permute-done.2.refs_4_
  19.2 4.2 %collective-permute-done.o_ref = bf16[384,1024]{1,0:T(8,128)(2,1)S(1)} collective-permute-done((bf16[384,1024]{1,0:T(8,128)(2,1)}, bf16[384,1024]{1,0:T(8,128)(2,1)S(1)}, u32[]{:S(2)}, u32[]{:S(2)}) %collective-permute-start) | collective-permute-done | bytes 786464 | tf_op jit(solution)/shard_map/ppermute | solution.py:391
  23.5 0.0 collective-permute-start.3
  23.5 2.4 %collective-permute-start.4 = (bf16[1168,128]{1,0:T(8,128)(2,1)S(1)}, bf16[1168,128]{1,0:T(8,128)(2,1)S(1)}, u32[]{:S(2)}, u32[]{:S(2)}) collective-permute-start(bf16[1168,128]{1,0:T(8,128)(2,1)S(1)} %get-tuple-element.61), channel_id=1, source_target_pairs={{0,24},{4,28},{8,16},{12,20},{16,8},{20,12},{24,0},{28,4},{1,25},{... | collective-permute-start | bytes 897032 | tf_op jit(solution)/shard_map/ppermute | solution.py:388
  25.9 0.0 collective-permute-start.5
  25.9 1.7 %collective-permute-start.6 = (bf16[1168,128]{1,0:T(8,128)(2,1)S(1)}, bf16[1168,128]{1,0:T(8,128)(2,1)S(1)}, u32[]{:S(2)}, u32[]{:S(2)}) collective-permute-start(bf16[1168,128]{1,0:T(8,128)(2,1)S(1)} %get-tuple-element.63), channel_id=1, source_target_pairs={{0,20},{4,16},{8,28},{12,24},{16,4},{20,0},{24,12},{28,8},{1,21},{... | collective-permute-start | bytes 897032 | tf_op jit(solution)/shard_map/ppermute | solution.py:388
  27.7 6.9 %collective-permute-done.4.refs_6_ = bf16[1168,128]{1,0:T(8,128)(2,1)S(1)} collective-permute-done((bf16[1168,128]{1,0:T(8,128)(2,1)S(1)}, bf16[1168,128]{1,0:T(8,128)(2,1)S(1)}, u32[]{:S(2)}, u32[]{:S(2)}) %collective-permute-start.4) | collective-permute-done | bytes 299040 | tf_op jit(solution)/shard_map/ppermute | solution.py:388
  34.5 1.0 shard_map.87.refs_0_
  35.6 4.4 %collective-permute-done.5.refs_7_ = bf16[1168,128]{1,0:T(8,128)(2,1)S(1)} collective-permute-done((bf16[1168,128]{1,0:T(8,128)(2,1)S(1)}, bf16[1168,128]{1,0:T(8,128)(2,1)S(1)}, u32[]{:S(2)}, u32[]{:S(2)}) %collective-permute-start.5) | collective-permute-done | bytes 299040 | tf_op jit(solution)/shard_map/ppermute | solution.py:388
  39.9 5.5 %collective-permute-done.6.refs_5_ = bf16[1168,128]{1,0:T(8,128)(2,1)S(1)} collective-permute-done((bf16[1168,128]{1,0:T(8,128)(2,1)S(1)}, bf16[1168,128]{1,0:T(8,128)(2,1)S(1)}, u32[]{:S(2)}, u32[]{:S(2)}) %collective-permute-start.6) | collective-permute-done | bytes 299040 | tf_op jit(solution)/shard_map/ppermute | solution.py:388
  45.4 0.7 collective-permute-start.9
  46.2 16.6 %shard_map.88 = (bf16[3072,128]{1,0:T(8,128)(2,1)S(1)}, bf16[3072,128]{1,0:T(8,128)(2,1)S(1)}, bf16[3072,256]{1,0:T(8,128)(2,1)S(1)}, bf16[256,3072]{1,0:T(8,128...) custom-call(s32[1]{0:T(128)} %bitcast.me_s, ...), custom_call_target="tpu_custom_call" | custom-call | flops 1811939328 | bytes 6291456 | tf_op jit(solution)/shard_map/pallas_call | solution.py:344
  62.8 1.0 shard_map.89.acc_ref
  63.8 3.0 %collective-permute-done.9.o_ref = bf16[384,1024]{1,0:T(8,128)(2,1)S(1)} collective-permute-done((bf16[384,1024]{1,0:T(8,128)(2,1)S(1)}, bf16[384,1024]{1,0:T(8,128)(2,1)S(1)}, u32[]{:S(2)}, u32[]{:S(2)}) %collective-permute-start.9) | collective-permute-done | bytes 786464 | tf_op jit(solution)/shard_map/ppermute | solution.py:391
  66.8 1.1 shard_map.90
  67.9 0.1 collective-permute-start.10
  68.0 1.3 %collective-permute-start.11 = (bf16[384,128]{1,0:T(8,128)(2,1)S(1)}, bf16[384,128]{1,0:T(8,128)(2,1)S(1)}, u32[]{:S(2)}, u32[]{:S(2)}) collective-permute-start(bf16[384,128]{1,0:T(8,128)(2,1)S(1)} %get-tuple-element.95), channel_id=1, source_target_pairs={{0,8},{4,12},{8,0},{12,4},{16,24},{20,28},{24,16},{28,20},{1,9},{5... | collective-permute-start | bytes 294920 | tf_op jit(solution)/shard_map/ppermute | solution.py:388
  69.3 0.5 collective-permute-start.12
  69.8 1.3 collective-permute-start.13
  71.1 0.4 collective-permute-start.14
  71.5 2.2 %collective-permute-start.15 = (bf16[384,128]{1,0:T(8,128)(2,1)S(1)}, bf16[384,128]{1,0:T(8,128)(2,1)S(1)}, u32[]{:S(2)}, u32[]{:S(2)}) collective-permute-start(bf16[384,128]{1,0:T(8,128)(2,1)S(1)} %get-tuple-element.99), channel_id=1, source_target_pairs={{0,24},{4,28},{8,16},{12,20},{16,8},{20,12},{24,0},{28,4},{1,25},{... | collective-permute-start | bytes 294920 | tf_op jit(solution)/shard_map/ppermute | solution.py:388
  73.7 0.9 collective-permute-start.16
  74.6 0.2 collective-permute-done.12.refs_3_
  74.8 0.6 collective-permute-done.13.refs_4_
  75.5 5.2 %collective-permute-done.14.refs_5_ = bf16[384,128]{1,0:T(8,128)(2,1)S(1)} collective-permute-done((bf16[384,128]{1,0:T(8,128)(2,1)S(1)}, bf16[384,128]{1,0:T(8,128)(2,1)S(1)}, u32[]{:S(2)}, u32[]{:S(2)}) %collective-permute-start.14) | collective-permute-done | bytes 98336 | tf_op jit(solution)/shard_map/ppermute | solution.py:388
  80.6 16.7 %shard_map.91 = (bf16[1152,128]{1,0:T(8,128)(2,1)S(1)}, bf16[1152,128]{1,0:T(8,128)(2,1)S(1)}, bf16[1152,128]{1,0:T(8,128)(2,1)S(1)}, bf16[1152,128]{1,0:T(8,128...) custom-call(s32[1]{0:T(128)} %bitcast.me_s, ...), custom_call_target="tpu_custom_call" | custom-call | flops 3019898880 | bytes 6291456 | tf_op jit(solution)/shard_map/pallas_call | solution.py:370
  97.4 0.5 collective-permute-start.17
  97.8 1.3 collective-permute-start.18
  99.1 0.2 collective-permute-start.19
  99.3 1.3 %collective-permute-start.20 = (bf16[1152,128]{1,0:T(8,128)(2,1)S(1)}, bf16[1152,128]{1,0:T(8,128)(2,1)S(1)}, u32[]{:S(2)}, u32[]{:S(2)}) collective-permute-start(bf16[1152,128]{1,0:T(8,128)(2,1)S(1)} %get-tuple-element.105), channel_id=1, source_target_pairs={{0,16},{4,20},{8,24},{12,28},{16,0},{20,4},{24,8},{28,12},{1,17},{... | collective-permute-start | bytes 884744 | tf_op jit(solution)/shard_map/ppermute | solution.py:388
  100.6 0.7 collective-permute-start.21
  101.3 2.2 %collective-permute-start.22 = (bf16[1152,128]{1,0:T(8,128)(2,1)S(1)}, bf16[1152,128]{1,0:T(8,128)(2,1)S(1)}, u32[]{:S(2)}, u32[]{:S(2)}) collective-permute-start(bf16[1152,128]{1,0:T(8,128)(2,1)S(1)} %get-tuple-element.107), channel_id=1, source_target_pairs={{0,24},{4,28},{8,16},{12,20},{16,8},{20,12},{24,0},{28,4},{1,25},{... | collective-permute-start | bytes 884744 | tf_op jit(solution)/shard_map/ppermute | solution.py:388
  103.5 4.1 %collective-permute-done.18.refs_2_ = bf16[1152,128]{1,0:T(8,128)(2,1)S(1)} collective-permute-done((bf16[1152,128]{1,0:T(8,128)(2,1)S(1)}, bf16[1152,128]{1,0:T(8,128)(2,1)S(1)}, u32[]{:S(2)}, u32[]{:S(2)}) %collective-permute-start.18) | collective-permute-done | bytes 294944 | tf_op jit(solution)/shard_map/ppermute | solution.py:388
  107.7 0.2 collective-permute-start.23
  107.9 4.9 %collective-permute-done.19.refs_3_ = bf16[1152,128]{1,0:T(8,128)(2,1)S(1)} collective-permute-done((bf16[1152,128]{1,0:T(8,128)(2,1)S(1)}, bf16[1152,128]{1,0:T(8,128)(2,1)S(1)}, u32[]{:S(2)}, u32[]{:S(2)}) %collective-permute-start.19) | collective-permute-done | bytes 294944 | tf_op jit(solution)/shard_map/ppermute | solution.py:388
  112.8 14.8 %collective-permute-done.21.refs_5_ = bf16[1152,128]{1,0:T(8,128)(2,1)S(1)} collective-permute-done((bf16[1152,128]{1,0:T(8,128)(2,1)S(1)}, bf16[1152,128]{1,0:T(8,128)(2,1)S(1)}, u32[]{:S(2)}, u32[]{:S(2)}) %collective-permute-start.21) | collective-permute-done | bytes 294944 | tf_op jit(solution)/shard_map/ppermute | solution.py:388
  127.6 2.1 %shard_map.92 = (bf16[384,1024]{1,0:T(8,128)(2,1)}, bf16[384,1024]{1,0:T(8,128)(2,1)}, bf16[384,1024]{1,0:T(8,128)(2,1)}) custom-call(s32[1]{0:T(128)} %bitcast.me_s, bf16[1152,128]{1,0:T(8,128)(2,1)S(1)} %get-tuple-element.101.refs_0_, bf16[1152,128]{1,0:T(8,128)(2,1)S(1)} %collective-permute-done.17.refs_1_, ...), custom_call_target="tpu_custom_call" | custom-call | tf_op jit(solution)/shard_map/pallas_call | solution.py:87
  (19 shorter events, 0.0 us)
Async XLA Ops:
  0.6 22.9 %collective-permute-start = (bf16[384,1024]{1,0:T(8,128)(2,1)}, bf16[384,1024]{1,0:T(8,128)(2,1)S(1)}, u32[]{:S(2)}, u32[]{:S(2)}) collective-permute-start(bf16[384,1024]{1,0:T(8,128)(2,1)} %o_ref.1), channel_id=1, source_target_pairs={{0,1},{1,2},{2,3},{3,0},{4,5},{5,6},{6,7},{7,4},{8,9},{9,10},{10,1... | collective-permute-start | bytes 2359304 | tf_op jit(solution)/shard_map/ppermute | solution.py:391
  3.7 1.1 copy-start
  4.8 1.1 copy-start.1
  6.0 1.1 copy-start.2
  7.1 0.7 copy-start.4
  9.4 8.8 %collective-permute-start.1 = (bf16[1168,128]{1,0:T(8,128)(2,1)}, bf16[1168,128]{1,0:T(8,128)(2,1)S(1)}, u32[]{:S(2)}, u32[]{:S(2)}) collective-permute-start(bf16[1168,128]{1,0:T(8,128)(2,1)} %get-tuple-element.57), channel_id=1, source_target_pairs={{0,8},{4,12},{8,0},{12,4},{16,24},{20,28},{24,16},{28,20},{1,9},{5... | collective-permute-start | bytes 897032 | tf_op jit(solution)/shard_map/ppermute | solution.py:388
  11.0 8.3 %collective-permute-start.2 = (bf16[1168,128]{1,0:T(8,128)(2,1)S(1)}, bf16[1168,128]{1,0:T(8,128)(2,1)S(1)}, u32[]{:S(2)}, u32[]{:S(2)}) collective-permute-start(bf16[1168,128]{1,0:T(8,128)(2,1)S(1)} %get-tuple-element.58), channel_id=1, source_target_pairs={{0,16},{4,20},{8,24},{12,28},{16,0},{20,4},{24,8},{28,12},{1,17},{... | collective-permute-start | bytes 897032 | tf_op jit(solution)/shard_map/ppermute | solution.py:388
  12.5 4.5 %copy-start.3 = (bf16[384,1024]{1,0:T(8,128)(2,1)S(1)}, bf16[384,1024]{1,0:T(8,128)(2,1)}, u32[]{:S(2)}) copy-start(bf16[384,1024]{1,0:T(8,128)(2,1)} %o_ref.1) | copy-start | bytes 2359300
  23.5 21.9 %collective-permute-start.3 = (bf16[384,1024]{1,0:T(8,128)(2,1)S(1)}, bf16[384,1024]{1,0:T(8,128)(2,1)S(1)}, u32[]{:S(2)}, u32[]{:S(2)}) collective-permute-start(bf16[384,1024]{1,0:T(8,128)(2,1)S(1)} %collective-permute-done.o_ref), channel_id=1, source_target_pairs={{0,1},{1,2},{2,3},{3,0},{4,5},{5,6},{6,7},{7,4},{8,9},{9,10},{10,1... | collective-permute-start | bytes 2359304 | tf_op jit(solution)/shard_map/ppermute | solution.py:391
  23.5 11.0 %collective-permute-start.4 = (bf16[1168,128]{1,0:T(8,128)(2,1)S(1)}, bf16[1168,128]{1,0:T(8,128)(2,1)S(1)}, u32[]{:S(2)}, u32[]{:S(2)}) collective-permute-start(bf16[1168,128]{1,0:T(8,128)(2,1)S(1)} %get-tuple-element.61), channel_id=1, source_target_pairs={{0,24},{4,28},{8,16},{12,20},{16,8},{20,12},{24,0},{28,4},{1,25},{... | collective-permute-start | bytes 897032 | tf_op jit(solution)/shard_map/ppermute | solution.py:388
  25.9 14.0 %collective-permute-start.5 = (bf16[1168,128]{1,0:T(8,128)(2,1)S(1)}, bf16[1168,128]{1,0:T(8,128)(2,1)S(1)}, u32[]{:S(2)}, u32[]{:S(2)}) collective-permute-start(bf16[1168,128]{1,0:T(8,128)(2,1)S(1)} %get-tuple-element.62), channel_id=1, source_target_pairs={{0,28},{4,24},{8,20},{12,16},{16,12},{20,8},{24,4},{28,0},{1,29},{... | collective-permute-start | bytes 897032 | tf_op jit(solution)/shard_map/ppermute | solution.py:388
  25.9 19.5 %collective-permute-start.6 = (bf16[1168,128]{1,0:T(8,128)(2,1)S(1)}, bf16[1168,128]{1,0:T(8,128)(2,1)S(1)}, u32[]{:S(2)}, u32[]{:S(2)}) collective-permute-start(bf16[1168,128]{1,0:T(8,128)(2,1)S(1)} %get-tuple-element.63), channel_id=1, source_target_pairs={{0,20},{4,16},{8,28},{12,24},{16,4},{20,0},{24,12},{28,8},{1,21},{... | collective-permute-start | bytes 897032 | tf_op jit(solution)/shard_map/ppermute | solution.py:388
  27.7 17.8 %collective-permute-start.7 = (bf16[1168,128]{1,0:T(8,128)(2,1)S(1)}, bf16[1168,128]{1,0:T(8,128)(2,1)S(1)}, u32[]{:S(2)}, u32[]{:S(2)}) collective-permute-start(bf16[1168,128]{1,0:T(8,128)(2,1)S(1)} %get-tuple-element.64), channel_id=1, source_target_pairs={{0,12},{4,8},{8,4},{12,0},{16,28},{20,24},{24,20},{28,16},{1,13},{... | collective-permute-start | bytes 897032 | tf_op jit(solution)/shard_map/ppermute | solution.py:388
  34.5 10.9 %collective-permute-start.8 = (bf16[1168,128]{1,0:T(8,128)(2,1)S(1)}, bf16[1168,128]{1,0:T(8,128)(2,1)S(1)}, u32[]{:S(2)}, u32[]{:S(2)}) collective-permute-start(bf16[1168,128]{1,0:T(8,128)(2,1)S(1)} %get-tuple-element.65), channel_id=1, source_target_pairs={{0,4},{4,0},{8,12},{12,8},{16,20},{20,16},{24,28},{28,24},{1,5},{5... | collective-permute-start | bytes 897032 | tf_op jit(solution)/shard_map/ppermute | solution.py:388
  45.4 21.4 %collective-permute-start.9 = (bf16[384,1024]{1,0:T(8,128)(2,1)S(1)}, bf16[384,1024]{1,0:T(8,128)(2,1)S(1)}, u32[]{:S(2)}, u32[]{:S(2)}) collective-permute-start(bf16[384,1024]{1,0:T(8,128)(2,1)S(1)} %collective-permute-done.3.o_ref), channel_id=1, source_target_pairs={{0,1},{1,2},{2,3},{3,0},{4,5},{5,6},{6,7},{7,4},{8,9},{9,10},{10,1... | collective-permute-start | bytes 2359304 | tf_op jit(solution)/shard_map/ppermute | solution.py:391
  67.9 3.6 %collective-permute-start.10 = (bf16[384,128]{1,0:T(8,128)(2,1)S(1)}, bf16[384,128]{1,0:T(8,128)(2,1)S(1)}, u32[]{:S(2)}, u32[]{:S(2)}) collective-permute-start(bf16[384,128]{1,0:T(8,128)(2,1)S(1)} %get-tuple-element.94), channel_id=1, source_target_pairs={{0,4},{4,0},{8,12},{12,8},{16,20},{20,16},{24,28},{28,24},{1,5},{5... | collective-permute-start | bytes 294920 | tf_op jit(solution)/shard_map/ppermute | solution.py:388
  68.0 5.7 %collective-permute-start.11 = (bf16[384,128]{1,0:T(8,128)(2,1)S(1)}, bf16[384,128]{1,0:T(8,128)(2,1)S(1)}, u32[]{:S(2)}, u32[]{:S(2)}) collective-permute-start(bf16[384,128]{1,0:T(8,128)(2,1)S(1)} %get-tuple-element.95), channel_id=1, source_target_pairs={{0,8},{4,12},{8,0},{12,4},{16,24},{20,28},{24,16},{28,20},{1,9},{5... | collective-permute-start | bytes 294920 | tf_op jit(solution)/shard_map/ppermute | solution.py:388
  69.3 5.5 %collective-permute-start.12 = (bf16[384,128]{1,0:T(8,128)(2,1)S(1)}, bf16[384,128]{1,0:T(8,128)(2,1)S(1)}, u32[]{:S(2)}, u32[]{:S(2)}) collective-permute-start(bf16[384,128]{1,0:T(8,128)(2,1)S(1)} %get-tuple-element.96), channel_id=1, source_target_pairs={{0,12},{4,8},{8,4},{12,0},{16,28},{20,24},{24,20},{28,16},{1,13},{... | collective-permute-start | bytes 294920 | tf_op jit(solution)/shard_map/ppermute | solution.py:388
  69.8 5.6 %collective-permute-start.13 = (bf16[384,128]{1,0:T(8,128)(2,1)S(1)}, bf16[384,128]{1,0:T(8,128)(2,1)S(1)}, u32[]{:S(2)}, u32[]{:S(2)}) collective-permute-start(bf16[384,128]{1,0:T(8,128)(2,1)S(1)} %get-tuple-element.97), channel_id=1, source_target_pairs={{0,16},{4,20},{8,24},{12,28},{16,0},{20,4},{24,8},{28,12},{1,17},{... | collective-permute-start | bytes 294920 | tf_op jit(solution)/shard_map/ppermute | solution.py:388
  71.1 9.5 %collective-permute-start.14 = (bf16[384,128]{1,0:T(8,128)(2,1)S(1)}, bf16[384,128]{1,0:T(8,128)(2,1)S(1)}, u32[]{:S(2)}, u32[]{:S(2)}) collective-permute-start(bf16[384,128]{1,0:T(8,128)(2,1)S(1)} %get-tuple-element.98), channel_id=1, source_target_pairs={{0,20},{4,16},{8,28},{12,24},{16,4},{20,0},{24,12},{28,8},{1,21},{... | collective-permute-start | bytes 294920 | tf_op jit(solution)/shard_map/ppermute | solution.py:388
  71.5 9.1 %collective-permute-start.15 = (bf16[384,128]{1,0:T(8,128)(2,1)S(1)}, bf16[384,128]{1,0:T(8,128)(2,1)S(1)}, u32[]{:S(2)}, u32[]{:S(2)}) collective-permute-start(bf16[384,128]{1,0:T(8,128)(2,1)S(1)} %get-tuple-element.99), channel_id=1, source_target_pairs={{0,24},{4,28},{8,16},{12,20},{16,8},{20,12},{24,0},{28,4},{1,25},{... | collective-permute-start | bytes 294920 | tf_op jit(solution)/shard_map/ppermute | solution.py:388
  73.7 6.9 %collective-permute-start.16 = (bf16[384,128]{1,0:T(8,128)(2,1)S(1)}, bf16[384,128]{1,0:T(8,128)(2,1)S(1)}, u32[]{:S(2)}, u32[]{:S(2)}) collective-permute-start(bf16[384,128]{1,0:T(8,128)(2,1)S(1)} %get-tuple-element.100), channel_id=1, source_target_pairs={{0,28},{4,24},{8,20},{12,16},{16,12},{20,8},{24,4},{28,0},{1,29},{... | collective-permute-start | bytes 294920 | tf_op jit(solution)/shard_map/ppermute | solution.py:388
  97.4 4.0 %collective-permute-start.17 = (bf16[1152,128]{1,0:T(8,128)(2,1)S(1)}, bf16[1152,128]{1,0:T(8,128)(2,1)S(1)}, u32[]{:S(2)}, u32[]{:S(2)}) collective-permute-start(bf16[1152,128]{1,0:T(8,128)(2,1)S(1)} %get-tuple-element.102), channel_id=1, source_target_pairs={{0,4},{4,0},{8,12},{12,8},{16,20},{20,16},{24,28},{28,24},{1,5},{5... | collective-permute-start | bytes 884744 | tf_op jit(solution)/shard_map/ppermute | solution.py:388
  97.8 9.9 %collective-permute-start.18 = (bf16[1152,128]{1,0:T(8,128)(2,1)S(1)}, bf16[1152,128]{1,0:T(8,128)(2,1)S(1)}, u32[]{:S(2)}, u32[]{:S(2)}) collective-permute-start(bf16[1152,128]{1,0:T(8,128)(2,1)S(1)} %get-tuple-element.103), channel_id=1, source_target_pairs={{0,8},{4,12},{8,0},{12,4},{16,24},{20,28},{24,16},{28,20},{1,9},{5... | collective-permute-start | bytes 884744 | tf_op jit(solution)/shard_map/ppermute | solution.py:388
  99.1 13.7 %collective-permute-start.19 = (bf16[1152,128]{1,0:T(8,128)(2,1)S(1)}, bf16[1152,128]{1,0:T(8,128)(2,1)S(1)}, u32[]{:S(2)}, u32[]{:S(2)}) collective-permute-start(bf16[1152,128]{1,0:T(8,128)(2,1)S(1)} %get-tuple-element.104), channel_id=1, source_target_pairs={{0,12},{4,8},{8,4},{12,0},{16,28},{20,24},{24,20},{28,16},{1,13},{... | collective-permute-start | bytes 884744 | tf_op jit(solution)/shard_map/ppermute | solution.py:388
  99.3 13.5 %collective-permute-start.20 = (bf16[1152,128]{1,0:T(8,128)(2,1)S(1)}, bf16[1152,128]{1,0:T(8,128)(2,1)S(1)}, u32[]{:S(2)}, u32[]{:S(2)}) collective-permute-start(bf16[1152,128]{1,0:T(8,128)(2,1)S(1)} %get-tuple-element.105), channel_id=1, source_target_pairs={{0,16},{4,20},{8,24},{12,28},{16,0},{20,4},{24,8},{28,12},{1,17},{... | collective-permute-start | bytes 884744 | tf_op jit(solution)/shard_map/ppermute | solution.py:388
  100.6 26.9 %collective-permute-start.21 = (bf16[1152,128]{1,0:T(8,128)(2,1)S(1)}, bf16[1152,128]{1,0:T(8,128)(2,1)S(1)}, u32[]{:S(2)}, u32[]{:S(2)}) collective-permute-start(bf16[1152,128]{1,0:T(8,128)(2,1)S(1)} %get-tuple-element.106), channel_id=1, source_target_pairs={{0,20},{4,16},{8,28},{12,24},{16,4},{20,0},{24,12},{28,8},{1,21},{... | collective-permute-start | bytes 884744 | tf_op jit(solution)/shard_map/ppermute | solution.py:388
  101.3 26.2 %collective-permute-start.22 = (bf16[1152,128]{1,0:T(8,128)(2,1)S(1)}, bf16[1152,128]{1,0:T(8,128)(2,1)S(1)}, u32[]{:S(2)}, u32[]{:S(2)}) collective-permute-start(bf16[1152,128]{1,0:T(8,128)(2,1)S(1)} %get-tuple-element.107), channel_id=1, source_target_pairs={{0,24},{4,28},{8,16},{12,20},{16,8},{20,12},{24,0},{28,4},{1,25},{... | collective-permute-start | bytes 884744 | tf_op jit(solution)/shard_map/ppermute | solution.py:388
  107.7 19.9 %collective-permute-start.23 = (bf16[1152,128]{1,0:T(8,128)(2,1)S(1)}, bf16[1152,128]{1,0:T(8,128)(2,1)S(1)}, u32[]{:S(2)}, u32[]{:S(2)}) collective-permute-start(bf16[1152,128]{1,0:T(8,128)(2,1)S(1)} %get-tuple-element.108), channel_id=1, source_target_pairs={{0,28},{4,24},{8,20},{12,16},{16,12},{20,8},{24,4},{28,0},{1,29},{... | collective-permute-start | bytes 884744 | tf_op jit(solution)/shard_map/ppermute | solution.py:388

commit v6 on v5

--- a/solution.py
+++ b/solution.py
@@ -14,6 +14,7 @@
 ONES_ROWS = 16
 NEG_LARGE = -1e30
 VMEM_SPARE = 6 * 1024 * 1024
+LIST_BYTES = 16 * 1024 * 1024
 
 NN = (((1,), (0,)), ((), ()))
 NT = (((1,), (1,)), ((), ()))
@@ -188,14 +189,14 @@
 
 
 def pipelined(plan_q, plan_k, count_ref, early, late, buffers):
-    early(plan_q[0], plan_k[0], buffers[0], True)
+    early(0, plan_q[0], plan_k[0], buffers[0], True)
 
     def turns(diagonal):
         def body(i, carry):
             for turn in range(2):
                 now = 2 * i + turn
-                late(plan_q[now], plan_k[now], buffers[turn])
-                early(plan_q[now + 1], plan_k[now + 1], buffers[1 - turn], diagonal)
+                late(now, plan_q[now], plan_k[now], buffers[turn])
+                early(now + 1, plan_q[now + 1], plan_k[now + 1], buffers[1 - turn], diagonal)
             return carry
 
         return body
@@ -204,8 +205,11 @@
     lax.fori_loop(count_ref[0], count_ref[1], turns(True), 0)
 
 
-def forward_kernel(peers, heads, rows, bq, bk, me_s, *refs):
+def forward_kernel(peers, heads, rows, bq, bk, kept, me_s, *refs):
     blocks = refs[:peers]
+    if kept:
+        p_list, top_list = refs[peers + 7:peers + 9]
+        refs = refs[:peers + 7] + refs[peers + 9:]
     q_ref, v_ref, kx_ref, qtx_ref, kt_ref, out_ref, log_ref = refs[peers:peers + 7]
     plan_q, plan_k, count_ref, own_q, own_k, own_count = refs[peers + 7:peers + 13]
     vt_ref, doc_ref, sum_ref, s0, top0, s1, top1 = refs[peers + 13:]
@@ -243,7 +247,7 @@
     log_ref[...] = jnp.full_like(log_ref, NEG_LARGE)
     sum_ref[...] = jnp.zeros_like(sum_ref)
 
-    def early(qi, ki, buffer, diagonal):
+    def early(now, qi, ki, buffer, diagonal):
         s_ref, top_ref = buffer
         keys, queries = aligned(ki, bk), aligned(qi, bq)
         s = dot32(kx_ref[keys, :], qtx_ref[:, queries]) * factor
@@ -252,7 +256,7 @@
         s_ref[...] = s
         top_ref[...] = jnp.max(s, axis=0, keepdims=True)
 
-    def late(qi, ki, buffer):
+    def late(now, qi, ki, buffer):
         s_ref, top_ref = buffer
         keys, queries = aligned(ki, bk), aligned(qi, bq)
         top = log_ref[:, queries]
@@ -261,6 +265,9 @@
         fix = jnp.exp2(top - new_top)
         high = p.astype(jnp.bfloat16)
         rest = (p - high.astype(jnp.float32)).astype(jnp.bfloat16)
+        if kept:
+            p_list[now] = high
+            top_list[now] = new_top
         vt = vt_ref[:, keys]
         sums = dot32(vt, high) + dot32(vt, rest)
         out_ref[:, queries] = out_ref[:, queries] * fix + sums[:HD, :]
@@ -270,15 +277,19 @@
     pipelined(own_q, own_k, own_count, early, late, ((s0, top0), (s1, top1)))
     total_p = sum_ref[...]
     out_ref[...] = out_ref[...] / total_p
-    log_ref[...] = math.log(2.0) * (log_ref[...] + jnp.log2(total_p))
-
-
-def backward_kernel(peers, heads, rows, bq, bk, me_s, plan_q, plan_k, count_ref, q_ref, v_ref,
+    log_ref[...] = log_ref[...] + jnp.log2(total_p)
+
+
+def backward_kernel(peers, heads, rows, bq, bk, kept, me_s, plan_q, plan_k, count_ref, q_ref, v_ref,
                     kx_ref, qtx_ref, kt_ref, out_ref, log_ref, *refs):
+    if kept:
+        p_list, top_list = refs[:2]
+        refs = refs[2:]
     blocks = refs[:peers]
     results = refs[peers:peers + heads]
     g_ref, gt_ref, dot_ref, dk_acc, dv_acc, dq_acc, p0, ds0, p1, ds1 = refs[peers + heads:]
     scale = HD ** (-0.5)
+    factor = scale * math.log2(math.e)
     me = me_s[0]
     for d, block in enumerate(blocks):
         g_ref[aligned(me ^ d, rows), :] = block[...]
@@ -288,17 +299,21 @@
     dv_acc[...] = jnp.zeros_like(dv_acc)
     dq_acc[...] = jnp.zeros_like(dq_acc)
 
-    def early(qi, ki, buffer, diagonal):
+    def early(now, qi, ki, buffer, diagonal):
         p_ref, ds_ref = buffer
         keys, queries = aligned(ki, bk), aligned(qi, bq)
-        p = jnp.exp(dot32(kx_ref[keys, :], qtx_ref[:, queries]) * scale - log_ref[:, queries])
-        if diagonal:
-            p = jnp.where(at_or_before(qi * bq, ki * bk, (bk, bq)), p, 0.0)
+        log_row = log_ref[:, queries]
+        if kept:
+            p = p_list[now].astype(jnp.float32) * jnp.exp2(top_list[now] - log_row)
+        else:
+            p = jnp.exp2(dot32(kx_ref[keys, :], qtx_ref[:, queries]) * factor - log_row)
+            if diagonal:
+                p = jnp.where(at_or_before(qi * bq, ki * bk, (bk, bq)), p, 0.0)
         p_ref[...] = p.astype(jnp.bfloat16)
         dp = dot32(v_ref[keys, :], gt_ref[:, queries])
         ds_ref[...] = (p * (dp - dot_ref[:, queries])).astype(jnp.bfloat16)
 
-    def late(qi, ki, buffer):
+    def late(now, qi, ki, buffer):
         p_ref, ds_ref = buffer
         keys, queries = aligned(ki, bk), aligned(qi, bq)
         dv_acc[keys, :] += dot32(p_ref[...], g_ref[queries, :])
@@ -311,6 +326,12 @@
         result[:rows, :] = (scale * dq_acc[:, own]).astype(result.dtype).T
         result[rows:2 * rows, :] = (scale * dk_acc[own, :]).astype(result.dtype)
         result[2 * rows:, :] = dv_acc[own, :].astype(result.dtype)
+
+
+def keeps_list(total, peers, heads):
+    forward, backward = block_sizes(total)
+    size = plan_size(total, *forward) * math.prod(forward) * 2
+    return forward == backward and heads == peers and size <= LIST_BYTES
 
 
 def attention_cost(total, products):
@@ -335,6 +356,10 @@
         jax.ShapeDtypeStruct((HD, total), jnp.float32),
         jax.ShapeDtypeStruct((1, total), jnp.float32),
     ]
+    kept = keeps_list(total, peers, heads)
+    if kept:
+        vectors.append(jax.ShapeDtypeStruct((*own_plan[0], bk, bq), jnp.bfloat16))
+        vectors.append(jax.ShapeDtypeStruct((*own_plan[0], 1, bq), jnp.float32))
     scratch = [
         pltpu.VMEM((HD + ONES_ROWS, total), jnp.bfloat16),
         pltpu.VMEM((1, total), jnp.float32),
@@ -342,7 +367,7 @@
         *[pltpu.VMEM((bk, bq), jnp.float32), pltpu.VMEM((1, bq), jnp.float32)] * 2,
     ]
     return pl.pallas_call(
-        functools.partial(forward_kernel, peers, heads, rows, bq, bk),
+        functools.partial(forward_kernel, peers, heads, rows, bq, bk, kept),
         in_specs=[SMEM_SPEC] + [VMEM_SPEC] * peers,
         out_specs=[VMEM_SPEC] * len(vectors) + [SMEM_SPEC] * 3,
         out_shape=vectors + [jax.ShapeDtypeStruct(shape, jnp.int32) for shape in plan],
@@ -356,7 +381,8 @@
     peers, rows = len(blocks), blocks[0].shape[0]
     total = peers * rows
     bq, bk = block_sizes(total)[1]
-    vectors, plan = state[:7], state[7:]
+    vectors, plan = state[:-3], state[-3:]
+    kept = keeps_list(total, peers, heads)
     out_shape = [jax.ShapeDtypeStruct((3 * rows, HD), jnp.bfloat16)] * heads
     scratch = [
         pltpu.VMEM((total, HD), jnp.bfloat16),
@@ -368,8 +394,8 @@
         *[pltpu.VMEM((bk, bq), jnp.bfloat16)] * 4,
     ]
     return pl.pallas_call(
-        functools.partial(backward_kernel, peers, heads, rows, bq, bk),
-        in_specs=[SMEM_SPEC] * 4 + [VMEM_SPEC] * (7 + peers),
+        functools.partial(backward_kernel, peers, heads, rows, bq, bk, kept),
+        in_specs=[SMEM_SPEC] * 4 + [VMEM_SPEC] * (len(vectors) + peers),
         out_specs=[VMEM_SPEC] * heads,
         out_shape=out_shape,
         scratch_shapes=scratch,

time: 129 us -> 129 us (level); the launches traced: 130 us -> 127 us
  Pallas kernels: 41.1 us -> 37.5 us
  waiting for transfers between devices: 55 us -> 56.5 us
    pallas_call x1, Pallas kernels: 16.7 us -> 14.6 us  [attention_backward(): pl.pallas_call(functools.partial(backward_kernel, peers, heads, rows, bq,...]
    pallas_call x1, Pallas kernels: 16.6 us -> 15.1 us  [attention_forward(): pl.pallas_call(functools.partial(forward_kernel, peers, heads, rows, bq,...]
    ppermute x3, waiting for transfers between devices: 7.25 us -> 8.74 us  [pass_on(): lax.ppermute(x, 'head', [(i, (i + 1) % groups) for i in range(groups)])]
where the time goes in v6:
time: 129 us; the launch traced here: 127 us
  waiting for transfers between devices  56.5 us (44%)
  Pallas kernels  37.5 us (29%)
  starting transfers between devices  24.2 us (19%)
  local copies, waits for them, and re-layouts  8.62 us (7%)
    ppermute x21, waiting for transfers between devices, exchange(): lax.ppermute(x, 'seq', [(i, i ^ d) for i in range(peers)])  47.7 us
    ppermute x21, starting transfers between devices, exchange(): lax.ppermute(x, 'seq', [(i, i ^ d) for i in range(peers)])  20.3 us
    pallas_call x1, Pallas kernels, attention_forward(): pl.pallas_call(functools.partial(forward_kernel, peers, heads, rows, bq,...  15.1 us
    pallas_call x1, Pallas kernels, attention_backward(): pl.pallas_call(functools.partial(backward_kernel, peers, heads, rows, bq,...  14.6 us
    ppermute x3, waiting for transfers between devices, pass_on(): lax.ppermute(x, 'head', [(i, (i + 1) % groups) for i in range(groups)])  8.74 us
    dynamic_slice x1, local copies, waits for them, and re-layouts, per_device(): lax.dynamic_slice_in_dim(out_weight, block * width, width, 1)  4.54 us
    unnamed x10, local copies, waits for them, and re-layouts  4.08 us
    ppermute x3, starting transfers between devices, pass_on(): lax.ppermute(x, 'head', [(i, (i + 1) % groups) for i in range(groups)])  3.82 us
  transfers between devices with their start and end apart: 24, of which 13 were waited for; matrix products, arithmetic and copies ran while one was open for 4% of the time, Pallas kernels for 16%

profile of v6, /device:TPU:0, one launch (start us, length us, event | category | flops | bytes accessed | tf_op | source)
XLA Modules:
  0.0 127.5 jit_solution(7112609383777057860)
XLA Ops:
  0.6 3.1 %collective-permute-start = (bf16[384,1024]{1,0:T(8,128)(2,1)}, bf16[384,1024]{1,0:T(8,128)(2,1)S(1)}, u32[]{:S(2)}, u32[]{:S(2)}) collective-permute-start(bf16[384,1024]{1,0:T(8,128)(2,1)} %o_ref.1), channel_id=1, source_target_pairs={{0,1},{1,2},{2,3},{3,0},{4,5},{5,6},{6,7},{7,4},{8,9},{9,10},{10,1... | collective-permute-start | bytes 2359304 | tf_op jit(solution)/shard_map/ppermute | solution.py:417
  3.7 1.1 copy-done
  4.8 1.1 copy-done.1
  6.0 1.1 copy-done.2
  7.1 0.7 copy-done.4
  7.8 1.6 %shard_map.85 = (bf16[1168,128]{1,0:T(8,128)(2,1)S(1)}, bf16[1168,128]{1,0:T(8,128)(2,1)S(1)}, bf16[1168,128]{1,0:T(8,128)(2,1)}, bf16[1168,128]{1,0:T(8,128)(2,...) custom-call(s32[1]{0:T(128)} %bitcast.me_s, ...), custom_call_target="tpu_custom_call" | custom-call | tf_op jit(solution)/shard_map/pallas_call | solution.py:68
  9.4 1.6 %collective-permute-start.1 = (bf16[1168,128]{1,0:T(8,128)(2,1)}, bf16[1168,128]{1,0:T(8,128)(2,1)S(1)}, u32[]{:S(2)}, u32[]{:S(2)}) collective-permute-start(bf16[1168,128]{1,0:T(8,128)(2,1)} %get-tuple-element.59), channel_id=1, source_target_pairs={{0,8},{4,12},{8,0},{12,4},{16,24},{20,28},{24,16},{28,20},{1,9},{5... | collective-permute-start | bytes 897032 | tf_op jit(solution)/shard_map/ppermute | solution.py:414
  11.0 1.5 %collective-permute-start.2 = (bf16[1168,128]{1,0:T(8,128)(2,1)S(1)}, bf16[1168,128]{1,0:T(8,128)(2,1)S(1)}, u32[]{:S(2)}, u32[]{:S(2)}) collective-permute-start(bf16[1168,128]{1,0:T(8,128)(2,1)S(1)} %get-tuple-element.60), channel_id=1, source_target_pairs={{0,16},{4,20},{8,24},{12,28},{16,0},{20,4},{24,8},{28,12},{1,17},{... | collective-permute-start | bytes 897032 | tf_op jit(solution)/shard_map/ppermute | solution.py:414
  12.5 4.5 %constant_dynamic-slice_fusion = (bf16[1024,1024]{1,0:T(8,128)(2,1)S(1)}, bf16[1024,1024]{1,0:T(8,128)(2,1)S(1)}, bf16[1024,1024]{1,0:T(8,128)(2,1)S(1)}, bf16[1024,1024]{1,0:T(8,128)(2,1)S(1)}) fusion(bf16[1024,4096]{1,0:T(8,128)(2,1)} %param.10, s32[]{:T(128)S(6)} %select_n.15, s32[]{:T(128)S(6)} %select_n.13, s32[]{:T(128)S(6)} %select_n.12, s32[]{:T(128)S(6)} %select_n.14), kind=kLoop, calls=%fused_computation | loop fusion | bytes 16777232 | tf_op jit(solution)/shard_map/dynamic_slice | solution.py:436
  17.0 1.0 shard_map.86.refs_0_
  18.1 0.2 collective-permute-done.1.refs_2_
  18.2 1.0 collective-permute-done.2.refs_4_
  19.2 4.2 %collective-permute-done.o_ref = bf16[384,1024]{1,0:T(8,128)(2,1)S(1)} collective-permute-done((bf16[384,1024]{1,0:T(8,128)(2,1)}, bf16[384,1024]{1,0:T(8,128)(2,1)S(1)}, u32[]{:S(2)}, u32[]{:S(2)}) %collective-permute-start) | collective-permute-done | bytes 786464 | tf_op jit(solution)/shard_map/ppermute | solution.py:417
  23.5 0.0 collective-permute-start.3
  23.5 2.4 %collective-permute-start.4 = (bf16[1168,128]{1,0:T(8,128)(2,1)S(1)}, bf16[1168,128]{1,0:T(8,128)(2,1)S(1)}, u32[]{:S(2)}, u32[]{:S(2)}) collective-permute-start(bf16[1168,128]{1,0:T(8,128)(2,1)S(1)} %get-tuple-element.63), channel_id=1, source_target_pairs={{0,24},{4,28},{8,16},{12,20},{16,8},{20,12},{24,0},{28,4},{1,25},{... | collective-permute-start | bytes 897032 | tf_op jit(solution)/shard_map/ppermute | solution.py:414
  25.9 0.0 collective-permute-start.5
  25.9 1.7 %collective-permute-start.6 = (bf16[1168,128]{1,0:T(8,128)(2,1)S(1)}, bf16[1168,128]{1,0:T(8,128)(2,1)S(1)}, u32[]{:S(2)}, u32[]{:S(2)}) collective-permute-start(bf16[1168,128]{1,0:T(8,128)(2,1)S(1)} %get-tuple-element.65), channel_id=1, source_target_pairs={{0,20},{4,16},{8,28},{12,24},{16,4},{20,0},{24,12},{28,8},{1,21},{... | collective-permute-start | bytes 897032 | tf_op jit(solution)/shard_map/ppermute | solution.py:414
  27.7 6.9 %collective-permute-done.4.refs_6_ = bf16[1168,128]{1,0:T(8,128)(2,1)S(1)} collective-permute-done((bf16[1168,128]{1,0:T(8,128)(2,1)S(1)}, bf16[1168,128]{1,0:T(8,128)(2,1)S(1)}, u32[]{:S(2)}, u32[]{:S(2)}) %collective-permute-start.4) | collective-permute-done | bytes 299040 | tf_op jit(solution)/shard_map/ppermute | solution.py:414
  34.5 1.0 shard_map.87.refs_0_
  35.6 4.4 %collective-permute-done.5.refs_7_ = bf16[1168,128]{1,0:T(8,128)(2,1)S(1)} collective-permute-done((bf16[1168,128]{1,0:T(8,128)(2,1)S(1)}, bf16[1168,128]{1,0:T(8,128)(2,1)S(1)}, u32[]{:S(2)}, u32[]{:S(2)}) %collective-permute-start.5) | collective-permute-done | bytes 299040 | tf_op jit(solution)/shard_map/ppermute | solution.py:414
  39.9 5.5 %collective-permute-done.6.refs_5_ = bf16[1168,128]{1,0:T(8,128)(2,1)S(1)} collective-permute-done((bf16[1168,128]{1,0:T(8,128)(2,1)S(1)}, bf16[1168,128]{1,0:T(8,128)(2,1)S(1)}, u32[]{:S(2)}, u32[]{:S(2)}) %collective-permute-start.6) | collective-permute-done | bytes 299040 | tf_op jit(solution)/shard_map/ppermute | solution.py:414
  45.4 0.7 collective-permute-start.9
  46.2 15.1 %shard_map.88 = (bf16[3072,128]{1,0:T(8,128)(2,1)S(1)}, bf16[3072,128]{1,0:T(8,128)(2,1)S(1)}, bf16[3072,256]{1,0:T(8,128)(2,1)S(1)}, bf16[256,3072]{1,0:T(8,128...) custom-call(s32[1]{0:T(128)} %bitcast.me_s, ...), custom_call_target="tpu_custom_call" | custom-call | flops 1811939328 | bytes 6291456 | tf_op jit(solution)/shard_map/pallas_call | solution.py:369
  61.3 1.0 shard_map.89.acc_ref
  62.3 4.5 %collective-permute-done.9.o_ref = bf16[384,1024]{1,0:T(8,128)(2,1)S(1)} collective-permute-done((bf16[384,1024]{1,0:T(8,128)(2,1)S(1)}, bf16[384,1024]{1,0:T(8,128)(2,1)S(1)}, u32[]{:S(2)}, u32[]{:S(2)}) %collective-permute-start.9) | collective-permute-done | bytes 786464 | tf_op jit(solution)/shard_map/ppermute | solution.py:417
  66.8 1.0 shard_map.90
  67.9 0.1 collective-permute-start.10
  68.0 1.3 %collective-permute-start.11 = (bf16[384,128]{1,0:T(8,128)(2,1)S(1)}, bf16[384,128]{1,0:T(8,128)(2,1)S(1)}, u32[]{:S(2)}, u32[]{:S(2)}) collective-permute-start(bf16[384,128]{1,0:T(8,128)(2,1)S(1)} %get-tuple-element.99), channel_id=1, source_target_pairs={{0,8},{4,12},{8,0},{12,4},{16,24},{20,28},{24,16},{28,20},{1,9},{5... | collective-permute-start | bytes 294920 | tf_op jit(solution)/shard_map/ppermute | solution.py:414
  69.3 0.6 collective-permute-start.12
  69.8 1.3 collective-permute-start.13
  71.1 0.4 collective-permute-start.14
  71.5 2.2 %collective-permute-start.15 = (bf16[384,128]{1,0:T(8,128)(2,1)S(1)}, bf16[384,128]{1,0:T(8,128)(2,1)S(1)}, u32[]{:S(2)}, u32[]{:S(2)}) collective-permute-start(bf16[384,128]{1,0:T(8,128)(2,1)S(1)} %get-tuple-element.103), channel_id=1, source_target_pairs={{0,24},{4,28},{8,16},{12,20},{16,8},{20,12},{24,0},{28,4},{1,25},{... | collective-permute-start | bytes 294920 | tf_op jit(solution)/shard_map/ppermute | solution.py:414
  73.7 0.9 collective-permute-start.16
  74.6 0.2 collective-permute-done.12.refs_5_
  74.8 0.6 collective-permute-done.13.refs_6_
  75.4 5.2 %collective-permute-done.14.refs_7_ = bf16[384,128]{1,0:T(8,128)(2,1)S(1)} collective-permute-done((bf16[384,128]{1,0:T(8,128)(2,1)S(1)}, bf16[384,128]{1,0:T(8,128)(2,1)S(1)}, u32[]{:S(2)}, u32[]{:S(2)}) %collective-permute-start.14) | collective-permute-done | bytes 98336 | tf_op jit(solution)/shard_map/ppermute | solution.py:414
  80.6 14.6 %shard_map.91 = (bf16[1152,128]{1,0:T(8,128)(2,1)S(1)}, bf16[1152,128]{1,0:T(8,128)(2,1)S(1)}, bf16[1152,128]{1,0:T(8,128)(2,1)S(1)}, bf16[1152,128]{1,0:T(8,128...) custom-call(s32[1]{0:T(128)} %bitcast.me_s, ...), custom_call_target="tpu_custom_call" | custom-call | flops 3019898880 | bytes 6291456 | tf_op jit(solution)/shard_map/pallas_call | solution.py:396
  95.2 0.5 collective-permute-start.17
  95.6 1.2 collective-permute-start.18
  96.9 0.2 collective-permute-start.19
  97.1 1.3 %collective-permute-start.20 = (bf16[1152,128]{1,0:T(8,128)(2,1)S(1)}, bf16[1152,128]{1,0:T(8,128)(2,1)S(1)}, u32[]{:S(2)}, u32[]{:S(2)}) collective-permute-start(bf16[1152,128]{1,0:T(8,128)(2,1)S(1)} %get-tuple-element.109), channel_id=1, source_target_pairs={{0,16},{4,20},{8,24},{12,28},{16,0},{20,4},{24,8},{28,12},{1,17},{... | collective-permute-start | bytes 884744 | tf_op jit(solution)/shard_map/ppermute | solution.py:414
  98.4 0.7 collective-permute-start.21
  99.1 2.2 %collective-permute-start.22 = (bf16[1152,128]{1,0:T(8,128)(2,1)S(1)}, bf16[1152,128]{1,0:T(8,128)(2,1)S(1)}, u32[]{:S(2)}, u32[]{:S(2)}) collective-permute-start(bf16[1152,128]{1,0:T(8,128)(2,1)S(1)} %get-tuple-element.111), channel_id=1, source_target_pairs={{0,24},{4,28},{8,16},{12,20},{16,8},{20,12},{24,0},{28,4},{1,25},{... | collective-permute-start | bytes 884744 | tf_op jit(solution)/shard_map/ppermute | solution.py:414
  101.4 4.2 %collective-permute-done.18.refs_2_ = bf16[1152,128]{1,0:T(8,128)(2,1)S(1)} collective-permute-done((bf16[1152,128]{1,0:T(8,128)(2,1)S(1)}, bf16[1152,128]{1,0:T(8,128)(2,1)S(1)}, u32[]{:S(2)}, u32[]{:S(2)}) %collective-permute-start.18) | collective-permute-done | bytes 294944 | tf_op jit(solution)/shard_map/ppermute | solution.py:414
  105.5 0.2 collective-permute-start.23
  105.7 4.9 %collective-permute-done.19.refs_3_ = bf16[1152,128]{1,0:T(8,128)(2,1)S(1)} collective-permute-done((bf16[1152,128]{1,0:T(8,128)(2,1)S(1)}, bf16[1152,128]{1,0:T(8,128)(2,1)S(1)}, u32[]{:S(2)}, u32[]{:S(2)}) %collective-permute-start.19) | collective-permute-done | bytes 294944 | tf_op jit(solution)/shard_map/ppermute | solution.py:414
  110.6 14.8 %collective-permute-done.21.refs_5_ = bf16[1152,128]{1,0:T(8,128)(2,1)S(1)} collective-permute-done((bf16[1152,128]{1,0:T(8,128)(2,1)S(1)}, bf16[1152,128]{1,0:T(8,128)(2,1)S(1)}, u32[]{:S(2)}, u32[]{:S(2)}) %collective-permute-start.21) | collective-permute-done | bytes 294944 | tf_op jit(solution)/shard_map/ppermute | solution.py:414
  125.4 2.1 %shard_map.92 = (bf16[384,1024]{1,0:T(8,128)(2,1)}, bf16[384,1024]{1,0:T(8,128)(2,1)}, bf16[384,1024]{1,0:T(8,128)(2,1)}) custom-call(s32[1]{0:T(128)} %bitcast.me_s, bf16[1152,128]{1,0:T(8,128)(2,1)S(1)} %get-tuple-element.105.refs_0_, bf16[1152,128]{1,0:T(8,128)(2,1)S(1)} %collective-permute-done.17.refs_1_, ...), custom_call_target="tpu_custom_call" | custom-call | tf_op jit(solution)/shard_map/pallas_call | solution.py:88
  (19 shorter events, 0.0 us)
Async XLA Ops:
  0.6 22.9 %collective-permute-start = (bf16[384,1024]{1,0:T(8,128)(2,1)}, bf16[384,1024]{1,0:T(8,128)(2,1)S(1)}, u32[]{:S(2)}, u32[]{:S(2)}) collective-permute-start(bf16[384,1024]{1,0:T(8,128)(2,1)} %o_ref.1), channel_id=1, source_target_pairs={{0,1},{1,2},{2,3},{3,0},{4,5},{5,6},{6,7},{7,4},{8,9},{9,10},{10,1... | collective-permute-start | bytes 2359304 | tf_op jit(solution)/shard_map/ppermute | solution.py:417
  3.7 1.1 copy-start
  4.8 1.1 copy-start.1
  6.0 1.1 copy-start.2
  7.1 0.7 copy-start.4
  9.4 8.8 %collective-permute-start.1 = (bf16[1168,128]{1,0:T(8,128)(2,1)}, bf16[1168,128]{1,0:T(8,128)(2,1)S(1)}, u32[]{:S(2)}, u32[]{:S(2)}) collective-permute-start(bf16[1168,128]{1,0:T(8,128)(2,1)} %get-tuple-element.59), channel_id=1, source_target_pairs={{0,8},{4,12},{8,0},{12,4},{16,24},{20,28},{24,16},{28,20},{1,9},{5... | collective-permute-start | bytes 897032 | tf_op jit(solution)/shard_map/ppermute | solution.py:414
  11.0 8.3 %collective-permute-start.2 = (bf16[1168,128]{1,0:T(8,128)(2,1)S(1)}, bf16[1168,128]{1,0:T(8,128)(2,1)S(1)}, u32[]{:S(2)}, u32[]{:S(2)}) collective-permute-start(bf16[1168,128]{1,0:T(8,128)(2,1)S(1)} %get-tuple-element.60), channel_id=1, source_target_pairs={{0,16},{4,20},{8,24},{12,28},{16,0},{20,4},{24,8},{28,12},{1,17},{... | collective-permute-start | bytes 897032 | tf_op jit(solution)/shard_map/ppermute | solution.py:414
  12.5 4.5 %copy-start.3 = (bf16[384,1024]{1,0:T(8,128)(2,1)S(1)}, bf16[384,1024]{1,0:T(8,128)(2,1)}, u32[]{:S(2)}) copy-start(bf16[384,1024]{1,0:T(8,128)(2,1)} %o_ref.1) | copy-start | bytes 2359300
  23.5 21.9 %collective-permute-start.3 = (bf16[384,1024]{1,0:T(8,128)(2,1)S(1)}, bf16[384,1024]{1,0:T(8,128)(2,1)S(1)}, u32[]{:S(2)}, u32[]{:S(2)}) collective-permute-start(bf16[384,1024]{1,0:T(8,128)(2,1)S(1)} %collective-permute-done.o_ref), channel_id=1, source_target_pairs={{0,1},{1,2},{2,3},{3,0},{4,5},{5,6},{6,7},{7,4},{8,9},{9,10},{10,1... | collective-permute-start | bytes 2359304 | tf_op jit(solution)/shard_map/ppermute | solution.py:417
  23.5 11.0 %collective-permute-start.4 = (bf16[1168,128]{1,0:T(8,128)(2,1)S(1)}, bf16[1168,128]{1,0:T(8,128)(2,1)S(1)}, u32[]{:S(2)}, u32[]{:S(2)}) collective-permute-start(bf16[1168,128]{1,0:T(8,128)(2,1)S(1)} %get-tuple-element.63), channel_id=1, source_target_pairs={{0,24},{4,28},{8,16},{12,20},{16,8},{20,12},{24,0},{28,4},{1,25},{... | collective-permute-start | bytes 897032 | tf_op jit(solution)/shard_map/ppermute | solution.py:414
  25.9 14.0 %collective-permute-start.5 = (bf16[1168,128]{1,0:T(8,128)(2,1)S(1)}, bf16[1168,128]{1,0:T(8,128)(2,1)S(1)}, u32[]{:S(2)}, u32[]{:S(2)}) collective-permute-start(bf16[1168,128]{1,0:T(8,128)(2,1)S(1)} %get-tuple-element.64), channel_id=1, source_target_pairs={{0,28},{4,24},{8,20},{12,16},{16,12},{20,8},{24,4},{28,0},{1,29},{... | collective-permute-start | bytes 897032 | tf_op jit(solution)/shard_map/ppermute | solution.py:414
  25.9 19.5 %collective-permute-start.6 = (bf16[1168,128]{1,0:T(8,128)(2,1)S(1)}, bf16[1168,128]{1,0:T(8,128)(2,1)S(1)}, u32[]{:S(2)}, u32[]{:S(2)}) collective-permute-start(bf16[1168,128]{1,0:T(8,128)(2,1)S(1)} %get-tuple-element.65), channel_id=1, source_target_pairs={{0,20},{4,16},{8,28},{12,24},{16,4},{20,0},{24,12},{28,8},{1,21},{... | collective-permute-start | bytes 897032 | tf_op jit(solution)/shard_map/ppermute | solution.py:414
  27.7 17.8 %collective-permute-start.7 = (bf16[1168,128]{1,0:T(8,128)(2,1)S(1)}, bf16[1168,128]{1,0:T(8,128)(2,1)S(1)}, u32[]{:S(2)}, u32[]{:S(2)}) collective-permute-start(bf16[1168,128]{1,0:T(8,128)(2,1)S(1)} %get-tuple-element.66), channel_id=1, source_target_pairs={{0,12},{4,8},{8,4},{12,0},{16,28},{20,24},{24,20},{28,16},{1,13},{... | collective-permute-start | bytes 897032 | tf_op jit(solution)/shard_map/ppermute | solution.py:414
  34.5 10.9 %collective-permute-start.8 = (bf16[1168,128]{1,0:T(8,128)(2,1)S(1)}, bf16[1168,128]{1,0:T(8,128)(2,1)S(1)}, u32[]{:S(2)}, u32[]{:S(2)}) collective-permute-start(bf16[1168,128]{1,0:T(8,128)(2,1)S(1)} %get-tuple-element.67), channel_id=1, source_target_pairs={{0,4},{4,0},{8,12},{12,8},{16,20},{20,16},{24,28},{28,24},{1,5},{5... | collective-permute-start | bytes 897032 | tf_op jit(solution)/shard_map/ppermute | solution.py:414
  45.4 21.4 %collective-permute-start.9 = (bf16[384,1024]{1,0:T(8,128)(2,1)S(1)}, bf16[384,1024]{1,0:T(8,128)(2,1)S(1)}, u32[]{:S(2)}, u32[]{:S(2)}) collective-permute-start(bf16[384,1024]{1,0:T(8,128)(2,1)S(1)} %collective-permute-done.3.o_ref), channel_id=1, source_target_pairs={{0,1},{1,2},{2,3},{3,0},{4,5},{5,6},{6,7},{7,4},{8,9},{9,10},{10,1... | collective-permute-start | bytes 2359304 | tf_op jit(solution)/shard_map/ppermute | solution.py:417
  67.9 3.6 %collective-permute-start.10 = (bf16[384,128]{1,0:T(8,128)(2,1)S(1)}, bf16[384,128]{1,0:T(8,128)(2,1)S(1)}, u32[]{:S(2)}, u32[]{:S(2)}) collective-permute-start(bf16[384,128]{1,0:T(8,128)(2,1)S(1)} %get-tuple-element.98), channel_id=1, source_target_pairs={{0,4},{4,0},{8,12},{12,8},{16,20},{20,16},{24,28},{28,24},{1,5},{5... | collective-permute-start | bytes 294920 | tf_op jit(solution)/shard_map/ppermute | solution.py:414
  68.0 5.7 %collective-permute-start.11 = (bf16[384,128]{1,0:T(8,128)(2,1)S(1)}, bf16[384,128]{1,0:T(8,128)(2,1)S(1)}, u32[]{:S(2)}, u32[]{:S(2)}) collective-permute-start(bf16[384,128]{1,0:T(8,128)(2,1)S(1)} %get-tuple-element.99), channel_id=1, source_target_pairs={{0,8},{4,12},{8,0},{12,4},{16,24},{20,28},{24,16},{28,20},{1,9},{5... | collective-permute-start | bytes 294920 | tf_op jit(solution)/shard_map/ppermute | solution.py:414
  69.3 5.6 %collective-permute-start.12 = (bf16[384,128]{1,0:T(8,128)(2,1)S(1)}, bf16[384,128]{1,0:T(8,128)(2,1)S(1)}, u32[]{:S(2)}, u32[]{:S(2)}) collective-permute-start(bf16[384,128]{1,0:T(8,128)(2,1)S(1)} %get-tuple-element.100), channel_id=1, source_target_pairs={{0,12},{4,8},{8,4},{12,0},{16,28},{20,24},{24,20},{28,16},{1,13},{... | collective-permute-start | bytes 294920 | tf_op jit(solution)/shard_map/ppermute | solution.py:414
  69.8 5.6 %collective-permute-start.13 = (bf16[384,128]{1,0:T(8,128)(2,1)S(1)}, bf16[384,128]{1,0:T(8,128)(2,1)S(1)}, u32[]{:S(2)}, u32[]{:S(2)}) collective-permute-start(bf16[384,128]{1,0:T(8,128)(2,1)S(1)} %get-tuple-element.101), channel_id=1, source_target_pairs={{0,16},{4,20},{8,24},{12,28},{16,0},{20,4},{24,8},{28,12},{1,17},{... | collective-permute-start | bytes 294920 | tf_op jit(solution)/shard_map/ppermute | solution.py:414
  71.1 9.5 %collective-permute-start.14 = (bf16[384,128]{1,0:T(8,128)(2,1)S(1)}, bf16[384,128]{1,0:T(8,128)(2,1)S(1)}, u32[]{:S(2)}, u32[]{:S(2)}) collective-permute-start(bf16[384,128]{1,0:T(8,128)(2,1)S(1)} %get-tuple-element.102), channel_id=1, source_target_pairs={{0,20},{4,16},{8,28},{12,24},{16,4},{20,0},{24,12},{28,8},{1,21},{... | collective-permute-start | bytes 294920 | tf_op jit(solution)/shard_map/ppermute | solution.py:414
  71.5 9.1 %collective-permute-start.15 = (bf16[384,128]{1,0:T(8,128)(2,1)S(1)}, bf16[384,128]{1,0:T(8,128)(2,1)S(1)}, u32[]{:S(2)}, u32[]{:S(2)}) collective-permute-start(bf16[384,128]{1,0:T(8,128)(2,1)S(1)} %get-tuple-element.103), channel_id=1, source_target_pairs={{0,24},{4,28},{8,16},{12,20},{16,8},{20,12},{24,0},{28,4},{1,25},{... | collective-permute-start | bytes 294920 | tf_op jit(solution)/shard_map/ppermute | solution.py:414
  73.7 6.9 %collective-permute-start.16 = (bf16[384,128]{1,0:T(8,128)(2,1)S(1)}, bf16[384,128]{1,0:T(8,128)(2,1)S(1)}, u32[]{:S(2)}, u32[]{:S(2)}) collective-permute-start(bf16[384,128]{1,0:T(8,128)(2,1)S(1)} %get-tuple-element.104), channel_id=1, source_target_pairs={{0,28},{4,24},{8,20},{12,16},{16,12},{20,8},{24,4},{28,0},{1,29},{... | collective-permute-start | bytes 294920 | tf_op jit(solution)/shard_map/ppermute | solution.py:414
  95.2 4.0 %collective-permute-start.17 = (bf16[1152,128]{1,0:T(8,128)(2,1)S(1)}, bf16[1152,128]{1,0:T(8,128)(2,1)S(1)}, u32[]{:S(2)}, u32[]{:S(2)}) collective-permute-start(bf16[1152,128]{1,0:T(8,128)(2,1)S(1)} %get-tuple-element.106), channel_id=1, source_target_pairs={{0,4},{4,0},{8,12},{12,8},{16,20},{20,16},{24,28},{28,24},{1,5},{5... | collective-permute-start | bytes 884744 | tf_op jit(solution)/shard_map/ppermute | solution.py:414
  95.6 9.9 %collective-permute-start.18 = (bf16[1152,128]{1,0:T(8,128)(2,1)S(1)}, bf16[1152,128]{1,0:T(8,128)(2,1)S(1)}, u32[]{:S(2)}, u32[]{:S(2)}) collective-permute-start(bf16[1152,128]{1,0:T(8,128)(2,1)S(1)} %get-tuple-element.107), channel_id=1, source_target_pairs={{0,8},{4,12},{8,0},{12,4},{16,24},{20,28},{24,16},{28,20},{1,9},{5... | collective-permute-start | bytes 884744 | tf_op jit(solution)/shard_map/ppermute | solution.py:414
  96.9 13.7 %collective-permute-start.19 = (bf16[1152,128]{1,0:T(8,128)(2,1)S(1)}, bf16[1152,128]{1,0:T(8,128)(2,1)S(1)}, u32[]{:S(2)}, u32[]{:S(2)}) collective-permute-start(bf16[1152,128]{1,0:T(8,128)(2,1)S(1)} %get-tuple-element.108), channel_id=1, source_target_pairs={{0,12},{4,8},{8,4},{12,0},{16,28},{20,24},{24,20},{28,16},{1,13},{... | collective-permute-start | bytes 884744 | tf_op jit(solution)/shard_map/ppermute | solution.py:414
  97.1 13.5 %collective-permute-start.20 = (bf16[1152,128]{1,0:T(8,128)(2,1)S(1)}, bf16[1152,128]{1,0:T(8,128)(2,1)S(1)}, u32[]{:S(2)}, u32[]{:S(2)}) collective-permute-start(bf16[1152,128]{1,0:T(8,128)(2,1)S(1)} %get-tuple-element.109), channel_id=1, source_target_pairs={{0,16},{4,20},{8,24},{12,28},{16,0},{20,4},{24,8},{28,12},{1,17},{... | collective-permute-start | bytes 884744 | tf_op jit(solution)/shard_map/ppermute | solution.py:414
  98.4 27.0 %collective-permute-start.21 = (bf16[1152,128]{1,0:T(8,128)(2,1)S(1)}, bf16[1152,128]{1,0:T(8,128)(2,1)S(1)}, u32[]{:S(2)}, u32[]{:S(2)}) collective-permute-start(bf16[1152,128]{1,0:T(8,128)(2,1)S(1)} %get-tuple-element.110), channel_id=1, source_target_pairs={{0,20},{4,16},{8,28},{12,24},{16,4},{20,0},{24,12},{28,8},{1,21},{... | collective-permute-start | bytes 884744 | tf_op jit(solution)/shard_map/ppermute | solution.py:414
  99.1 26.2 %collective-permute-start.22 = (bf16[1152,128]{1,0:T(8,128)(2,1)S(1)}, bf16[1152,128]{1,0:T(8,128)(2,1)S(1)}, u32[]{:S(2)}, u32[]{:S(2)}) collective-permute-start(bf16[1152,128]{1,0:T(8,128)(2,1)S(1)} %get-tuple-element.111), channel_id=1, source_target_pairs={{0,24},{4,28},{8,16},{12,20},{16,8},{20,12},{24,0},{28,4},{1,25},{... | collective-permute-start | bytes 884744 | tf_op jit(solution)/shard_map/ppermute | solution.py:414
  105.5 19.9 %collective-permute-start.23 = (bf16[1152,128]{1,0:T(8,128)(2,1)S(1)}, bf16[1152,128]{1,0:T(8,128)(2,1)S(1)}, u32[]{:S(2)}, u32[]{:S(2)}) collective-permute-start(bf16[1152,128]{1,0:T(8,128)(2,1)S(1)} %get-tuple-element.112), channel_id=1, source_target_pairs={{0,28},{4,24},{8,20},{12,16},{16,12},{20,8},{24,4},{28,0},{1,29},{... | collective-permute-start | bytes 884744 | tf_op jit(solution)/shard_map/ppermute | solution.py:414

commit v7 on v6

--- a/solution.py
+++ b/solution.py
@@ -102,17 +102,20 @@
         out_ref[:, part] = both if first else refs[0][:, part] + both
 
 
-def project_last_kernel(me_s, o_ref, w_ref, acc_ref, *outs):
+def project_last_kernel(me_s, o_ref, w_ref, acc_ref, upper_ref, *outs):
     pairs = len(outs) // 2
     odd = lax.rem(me_s[0], 2) == 1
+    cut = upper_ref.shape[0]
     for j in range(pairs):
         part = aligned(lax.rem(me_s[0] // 2, pairs) ^ j, 2 * HD)
-        both = (acc_ref[:, part] + dot32(o_ref[...], w_ref[part, :], NT)).astype(jnp.bfloat16)
-        outs[2 * j][...] = jnp.where(odd, both[:, HD:], both[:, :HD])
-        outs[2 * j + 1][...] = jnp.where(odd, both[:, :HD], both[:, HD:])
-
-
-def project(me, weight, features, acc, last):
+        lower = acc_ref[:, part] + dot32(o_ref[...], w_ref[part, :], NT)
+        for place, value in ((slice(0, cut), upper_ref[:, part]), (slice(cut, None), lower)):
+            both = value.astype(jnp.bfloat16)
+            outs[2 * j][place, :] = jnp.where(odd, both[:, HD:], both[:, :HD])
+            outs[2 * j + 1][place, :] = jnp.where(odd, both[:, :HD], both[:, HD:])
+
+
+def project(me, weight, features, acc, upper=None):
     rows, width = features.shape
     columns = weight.shape[0]
     heads = columns // HD
@@ -122,15 +125,15 @@
         bytes_accessed=2 * width * columns + 8 * rows * columns,
         transcendentals=0,
     )
-    if last:
+    if upper is not None:
         return pl.pallas_call(
             project_last_kernel,
-            in_specs=[SMEM_SPEC] + [VMEM_SPEC] * 3,
+            in_specs=[SMEM_SPEC] + [VMEM_SPEC] * 4,
             out_specs=[VMEM_SPEC] * heads,
-            out_shape=[jax.ShapeDtypeStruct((rows, HD), jnp.bfloat16)] * heads,
-            compiler_params=params([features, weight, total, total]),
+            out_shape=[jax.ShapeDtypeStruct((upper.shape[0] + rows, HD), jnp.bfloat16)] * heads,
+            compiler_params=params([features, weight, total, upper, upper]),
             cost_estimate=cost,
-        )(me, features, weight, acc)
+        )(me, features, weight, acc, upper)
     operands = (features, weight) + (() if acc is None else (acc,))
     return pl.pallas_call(
         functools.partial(project_kernel, acc is None),
@@ -264,12 +267,13 @@
         p = jnp.exp2(s_ref[...] - new_top)
         fix = jnp.exp2(top - new_top)
         high = p.astype(jnp.bfloat16)
-        rest = (p - high.astype(jnp.float32)).astype(jnp.bfloat16)
+        vt = vt_ref[:, keys]
+        sums = dot32(vt, high)
         if kept:
             p_list[now] = high
             top_list[now] = new_top
-        vt = vt_ref[:, keys]
-        sums = dot32(vt, high) + dot32(vt, rest)
+        else:
+            sums = sums + dot32(vt, (p - high.astype(jnp.float32)).astype(jnp.bfloat16))
         out_ref[:, queries] = out_ref[:, queries] * fix + sums[:HD, :]
         sum_ref[:, queries] = sum_ref[:, queries] * fix + sums[HD:HD + 1, :]
         log_ref[:, queries] = new_top
@@ -425,32 +429,38 @@
     packed = list(pack_heads(me_vector, queries, keys_in, values, doc_ids))
     received = exchange_all(packed, peers)
 
-    def share(step):
-        return len(order) * step * (step + 1) // ((groups - 2) * (groups - 1))
-
     after = lax.optimization_barrier
-    features, acc = out_grad, None
     weights = []
     for step in range(groups):
         block = lax.rem(lax.axis_index("head") + groups - step, groups)
         weights.append(lax.dynamic_slice_in_dim(out_weight, block * width, width, 1))
+
+    cut = 2 * rows // 3 // 16 * 16
+    upper, lower = out_grad[:cut], out_grad[cut:]
+    upper_acc, lower_acc = None, None
+    gates = [0, 1] + [1 + (len(order) - 2) * step // max(groups - 3, 1) for step in range(1, groups - 2)]
     for step in range(groups):
-        last = step == groups - 1
-        if not last:
-            passed = pass_on(features)
+        passed_upper = pass_on(upper) if step < groups - 1 else None
+        passed_lower = pass_on(lower) if step > 0 else None
         if step == groups - 2:
-            received[0], features = after((received[0], features))
+            received[0], upper, lower = after((received[0], upper, lower))
             state = list(attention_forward(me_vector, received, rows, heads))
-            features, state[1] = after((features, state[1]))
-        acc = project(me_vector, weights[step], features, acc, last)
-        if not last:
-            features = passed
-            if step < groups - 2:
-                batch = order[share(step):share(step + 1)]
-                here = [received[d] for d in batch]
-                features, acc, here, weights[2:] = after((features, acc, here, weights[2:]))
-                for d, block in zip(batch, here):
-                    received[d] = block
+            upper, lower, state[1] = after((upper, lower, state[1]))
+        upper_acc = project(me_vector, weights[step], upper, upper_acc)
+        if step > 0:
+            lower_acc = project(me_vector, weights[step - 1], lower, lower_acc)
+            lower = passed_lower
+        if step < groups - 1:
+            upper = passed_upper
+            batch = order[gates[step]:gates[step + 1]] if step < groups - 2 else []
+            here = [received[d] for d in batch]
+            fixed = [upper_acc] + ([lower_acc] if step > 0 else [])
+            upper, lower, fixed, here, weights[2:] = after((upper, lower, fixed, here, weights[2:]))
+            upper_acc = fixed[0]
+            lower_acc = fixed[1] if step > 0 else None
+            for d, block in zip(batch, here):
+                received[d] = block
+    acc = project(me_vector, weights[-1], lower, lower_acc, upper_acc)
     grads = exchange_all(acc, peers)
 
     results = attention_backward(me_vector, heads, state, grads)

time: 129 us -> 135 us (1.047)
  starting transfers between devices: 24.2 us -> 31 us
  waiting for transfers between devices: 56.5 us -> 52.4 us
  local copies, waits for them, and re-layouts: 8.62 us -> 10.6 us
    ppermute x21, waiting for transfers between devices: 47.7 us -> 41.1 us  [exchange(): lax.ppermute(x, 'seq', [(i, i ^ d) for i in range(peers)])]
    ppermute x3 -> x6, starting transfers between devices: 3.82 us -> 7.59 us  [pass_on(): lax.ppermute(x, 'head', [(i, (i + 1) % groups) for i in range(groups)])]
    ppermute x21, starting transfers between devices: 20.3 us -> 23.4 us  [exchange(): lax.ppermute(x, 'seq', [(i, i ^ d) for i in range(peers)])]
    ppermute x3 -> x6, waiting for transfers between devices: 8.74 us -> 11.3 us  [pass_on(): lax.ppermute(x, 'head', [(i, (i + 1) % groups) for i in range(groups)])]
    pallas_call x3 -> x7, Pallas kernels: 3.06 us -> 5.45 us  [project(): pl.pallas_call(functools.partial(project_kernel, acc is None), in_specs=[...]
    slice x0 -> x2, local copies, waits for them, and re-layouts: none -> 2.05 us  [per_device(): upper, lower = (out_grad[:cut], out_grad[cut:])]
    unnamed x10 -> x8, local copies, waits for them, and re-layouts: 4.08 us -> 4.08 us
  transfers between devices with their start and end apart: 24 -> 27, of which waited for: 13 -> 11; matrix products, arithmetic and copies ran while one was open for 4% -> 4% of each run, Pallas kernels for 16% -> 16%
where the time goes in v7:
time: 135 us; the launch traced here: 133 us
  waiting for transfers between devices  52.4 us (39%)
  Pallas kernels  38.6 us (29%)
  starting transfers between devices  31 us (23%)
  local copies, waits for them, and re-layouts  10.6 us (8%)
    ppermute x21, waiting for transfers between devices, exchange(): lax.ppermute(x, 'seq', [(i, i ^ d) for i in range(peers)])  41.1 us
    ppermute x21, starting transfers between devices, exchange(): lax.ppermute(x, 'seq', [(i, i ^ d) for i in range(peers)])  23.4 us
    pallas_call x1, Pallas kernels, attention_forward(): pl.pallas_call(functools.partial(forward_kernel, peers, heads, rows, bq,...  14.4 us
    pallas_call x1, Pallas kernels, attention_backward(): pl.pallas_call(functools.partial(backward_kernel, peers, heads, rows, bq,...  14 us
    ppermute x6, waiting for transfers between devices, pass_on(): lax.ppermute(x, 'head', [(i, (i + 1) % groups) for i in range(groups)])  11.3 us
    ppermute x6, starting transfers between devices, pass_on(): lax.ppermute(x, 'head', [(i, (i + 1) % groups) for i in range(groups)])  7.59 us
    pallas_call x7, Pallas kernels, project(): pl.pallas_call(functools.partial(project_kernel, acc is None), in_specs=[...  5.45 us
    dynamic_slice x1, local copies, waits for them, and re-layouts, per_device(): lax.dynamic_slice_in_dim(out_weight, block * width, width, 1)  4.47 us
  transfers between devices with their start and end apart: 27, of which 11 were waited for; matrix products, arithmetic and copies ran while one was open for 4% of the time, Pallas kernels for 16%

profile of v7, /device:TPU:0, one launch (start us, length us, event | category | flops | bytes accessed | tf_op | source)
XLA Modules:
  0.0 133.4 jit_solution(7224226730612198300)
XLA Ops:
  0.6 1.1 slice.6.o_ref
  1.7 3.1 %collective-permute-start = (bf16[256,1024]{1,0:T(8,128)(2,1)S(1)}, bf16[256,1024]{1,0:T(8,128)(2,1)S(1)}, u32[]{:S(2)}, u32[]{:S(2)}) collective-permute-start(bf16[256,1024]{1,0:T(8,128)(2,1)S(1)} %slice.6.o_ref), channel_id=1, source_target_pairs={{0,1},{1,2},{2,3},{3,0},{4,5},{5,6},{6,7},{7,4},{8,9},{9,10},{10,1... | collective-permute-start | bytes 1572872 | tf_op jit(solution)/shard_map/ppermute | solution.py:421
  4.8 1.1 copy-done
  5.9 1.1 copy-done.1
  7.1 1.1 copy-done.2
  8.2 0.7 copy-done.3
  8.9 1.8 %shard_map.85 = (bf16[1168,128]{1,0:T(8,128)(2,1)S(1)}, bf16[1168,128]{1,0:T(8,128)(2,1)S(1)}, bf16[1168,128]{1,0:T(8,128)(2,1)}, bf16[1168,128]{1,0:T(8,128)(2,...) custom-call(s32[1]{0:T(128)} %bitcast.me_s, ...), custom_call_target="tpu_custom_call" | custom-call | tf_op jit(solution)/shard_map/pallas_call | solution.py:68
  10.7 1.6 %collective-permute-start.1 = (bf16[1168,128]{1,0:T(8,128)(2,1)}, bf16[1168,128]{1,0:T(8,128)(2,1)S(1)}, u32[]{:S(2)}, u32[]{:S(2)}) collective-permute-start(bf16[1168,128]{1,0:T(8,128)(2,1)} %get-tuple-element.69), channel_id=1, source_target_pairs={{0,8},{4,12},{8,0},{12,4},{16,24},{20,28},{24,16},{28,20},{1,9},{5... | collective-permute-start | bytes 897032 | tf_op jit(solution)/shard_map/ppermute | solution.py:418
  12.2 1.5 %collective-permute-start.4 = (bf16[1168,128]{1,0:T(8,128)(2,1)}, bf16[1168,128]{1,0:T(8,128)(2,1)S(1)}, u32[]{:S(2)}, u32[]{:S(2)}) collective-permute-start(bf16[1168,128]{1,0:T(8,128)(2,1)} %get-tuple-element.73), channel_id=1, source_target_pairs={{0,16},{4,20},{8,24},{12,28},{16,0},{20,4},{24,8},{28,12},{1,17},{... | collective-permute-start | bytes 897032 | tf_op jit(solution)/shard_map/ppermute | solution.py:418
  13.8 0.5 collective-permute-start.5
  14.2 4.5 %constant_dynamic-slice_fusion = (bf16[1024,1024]{1,0:T(8,128)(2,1)S(1)}, bf16[1024,1024]{1,0:T(8,128)(2,1)S(1)}, bf16[1024,1024]{1,0:T(8,128)(2,1)S(1)}, bf16[1024,1024]{1,0:T(8,128)(2,1)S(1)}) fusion(bf16[1024,4096]{1,0:T(8,128)(2,1)} %param.10, s32[]{:T(128)S(6)} %select_n.15, s32[]{:T(128)S(6)} %select_n.13, s32[]{:T(128)S(6)} %select_n.12, s32[]{:T(128)S(6)} %select_n.14), kind=kLoop, calls=%fused_computation | loop fusion | bytes 16777232 | tf_op jit(solution)/shard_map/dynamic_slice | solution.py:436
  18.7 1.0 slice.7.o_ref
  19.7 0.7 shard_map.86.refs_0_
  20.4 0.6 collective-permute-done.1.refs_2_
  21.0 1.6 %collective-permute-start.2 = (bf16[256,1024]{1,0:T(8,128)(2,1)S(1)}, bf16[256,1024]{1,0:T(8,128)(2,1)S(1)}, u32[]{:S(2)}, u32[]{:S(2)}) collective-permute-start(bf16[256,1024]{1,0:T(8,128)(2,1)S(1)} %collective-permute-done.o_ref), channel_id=1, source_target_pairs={{0,1},{1,2},{2,3},{3,0},{4,5},{5,6},{6,7},{7,4},{8,9},{9,10},{10,1... | collective-permute-start | bytes 1572872 | tf_op jit(solution)/shard_map/ppermute | solution.py:421
  22.6 2.7 %collective-permute-start.7 = (bf16[1168,128]{1,0:T(8,128)(2,1)S(1)}, bf16[1168,128]{1,0:T(8,128)(2,1)S(1)}, u32[]{:S(2)}, u32[]{:S(2)}) collective-permute-start(bf16[1168,128]{1,0:T(8,128)(2,1)S(1)} %get-tuple-element.76), channel_id=1, source_target_pairs={{0,20},{4,16},{8,28},{12,24},{16,4},{20,0},{24,12},{28,8},{1,21},{... | collective-permute-start | bytes 897032 | tf_op jit(solution)/shard_map/ppermute | solution.py:418
  25.2 8.5 %collective-permute-done.4.refs_4_ = bf16[1168,128]{1,0:T(8,128)(2,1)S(1)} collective-permute-done((bf16[1168,128]{1,0:T(8,128)(2,1)}, bf16[1168,128]{1,0:T(8,128)(2,1)S(1)}, u32[]{:S(2)}, u32[]{:S(2)}) %collective-permute-start.4) | collective-permute-done | bytes 299040 | tf_op jit(solution)/shard_map/ppermute | solution.py:418
  33.8 1.6 %collective-permute-start.3 = (bf16[128,1024]{1,0:T(8,128)(2,1)S(1)}, bf16[128,1024]{1,0:T(8,128)(2,1)S(1)}, u32[]{:S(2)}, u32[]{:S(2)}) collective-permute-start(bf16[128,1024]{1,0:T(8,128)(2,1)S(1)} %slice.7.o_ref), channel_id=1, source_target_pairs={{0,1},{1,2},{2,3},{3,0},{4,5},{5,6},{6,7},{7,4},{8,9},{9,10},{10,1... | collective-permute-start | bytes 786440 | tf_op jit(solution)/shard_map/ppermute | solution.py:421
  35.4 0.7 shard_map.87.refs_0_
  36.2 0.8 shard_map.88.refs_0_
  37.1 2.8 %collective-permute-done.7.refs_5_ = bf16[1168,128]{1,0:T(8,128)(2,1)S(1)} collective-permute-done((bf16[1168,128]{1,0:T(8,128)(2,1)S(1)}, bf16[1168,128]{1,0:T(8,128)(2,1)S(1)}, u32[]{:S(2)}, u32[]{:S(2)}) %collective-permute-start.7) | collective-permute-done | bytes 299040 | tf_op jit(solution)/shard_map/ppermute | solution.py:418
  39.9 1.3 %collective-permute-done.8.refs_3_ = bf16[1168,128]{1,0:T(8,128)(2,1)S(1)} collective-permute-done((bf16[1168,128]{1,0:T(8,128)(2,1)S(1)}, bf16[1168,128]{1,0:T(8,128)(2,1)S(1)}, u32[]{:S(2)}, u32[]{:S(2)}) %collective-permute-start.8) | collective-permute-done | bytes 299040 | tf_op jit(solution)/shard_map/ppermute | solution.py:418
  41.2 2.2 %collective-permute-done.3.o_ref = bf16[128,1024]{1,0:T(8,128)(2,1)S(1)} collective-permute-done((bf16[128,1024]{1,0:T(8,128)(2,1)S(1)}, bf16[128,1024]{1,0:T(8,128)(2,1)S(1)}, u32[]{:S(2)}, u32[]{:S(2)}) %collective-permute-start.3) | collective-permute-done | bytes 262176 | tf_op jit(solution)/shard_map/ppermute | solution.py:421
  43.4 1.4 %collective-permute-start.11 = (bf16[128,1024]{1,0:T(8,128)(2,1)S(1)}, bf16[128,1024]{1,0:T(8,128)(2,1)S(1)}, u32[]{:S(2)}, u32[]{:S(2)}) collective-permute-start(bf16[128,1024]{1,0:T(8,128)(2,1)S(1)} %collective-permute-done.3.o_ref), channel_id=1, source_target_pairs={{0,1},{1,2},{2,3},{3,0},{4,5},{5,6},{6,7},{7,4},{8,9},{9,10},{10,1... | collective-permute-start | bytes 786440 | tf_op jit(solution)/shard_map/ppermute | solution.py:421
  44.8 14.4 %shard_map.89 = (bf16[3072,128]{1,0:T(8,128)(2,1)S(1)}, bf16[3072,128]{1,0:T(8,128)(2,1)S(1)}, bf16[3072,256]{1,0:T(8,128)(2,1)S(1)}, bf16[256,3072]{1,0:T(8,128...) custom-call(s32[1]{0:T(128)} %bitcast.me_s, ...), custom_call_target="tpu_custom_call" | custom-call | flops 1811939328 | bytes 6291456 | tf_op jit(solution)/shard_map/pallas_call | solution.py:373
  59.2 0.8 shard_map.91.refs_0_
  60.0 0.8 shard_map.90.refs_0_
  60.8 2.5 %collective-permute-done.11.o_ref = bf16[128,1024]{1,0:T(8,128)(2,1)S(1)} collective-permute-done((bf16[128,1024]{1,0:T(8,128)(2,1)S(1)}, bf16[128,1024]{1,0:T(8,128)(2,1)S(1)}, u32[]{:S(2)}, u32[]{:S(2)}) %collective-permute-start.11) | collective-permute-done | bytes 262176 | tf_op jit(solution)/shard_map/ppermute | solution.py:421
  63.3 0.8 shard_map.92.acc_ref
  64.1 0.7 shard_map.93.upper_ref
  64.9 6.6 %collective-permute-done.12.o_ref = bf16[128,1024]{1,0:T(8,128)(2,1)S(1)} collective-permute-done((bf16[128,1024]{1,0:T(8,128)(2,1)S(1)}, bf16[128,1024]{1,0:T(8,128)(2,1)S(1)}, u32[]{:S(2)}, u32[]{:S(2)}) %collective-permute-start.12) | collective-permute-done | bytes 262176 | tf_op jit(solution)/shard_map/ppermute | solution.py:421
  71.5 0.8 shard_map.94
  72.4 3.1 %collective-permute-start.14 = (bf16[384,128]{1,0:T(8,128)(2,1)S(1)}, bf16[384,128]{1,0:T(8,128)(2,1)S(1)}, u32[]{:S(2)}, u32[]{:S(2)}) collective-permute-start(bf16[384,128]{1,0:T(8,128)(2,1)S(1)} %get-tuple-element.119), channel_id=1, source_target_pairs={{0,8},{4,12},{8,0},{12,4},{16,24},{20,28},{24,16},{28,20},{1,9},{5... | collective-permute-start | bytes 294920 | tf_op jit(solution)/shard_map/ppermute | solution.py:418
  75.6 2.6 %collective-permute-start.16 = (bf16[384,128]{1,0:T(8,128)(2,1)S(1)}, bf16[384,128]{1,0:T(8,128)(2,1)S(1)}, u32[]{:S(2)}, u32[]{:S(2)}) collective-permute-start(bf16[384,128]{1,0:T(8,128)(2,1)S(1)} %get-tuple-element.121), channel_id=1, source_target_pairs={{0,16},{4,20},{8,24},{12,28},{16,0},{20,4},{24,8},{28,12},{1,17},{... | collective-permute-start | bytes 294920 | tf_op jit(solution)/shard_map/ppermute | solution.py:418
  78.2 2.9 %collective-permute-start.18 = (bf16[384,128]{1,0:T(8,128)(2,1)S(1)}, bf16[384,128]{1,0:T(8,128)(2,1)S(1)}, u32[]{:S(2)}, u32[]{:S(2)}) collective-permute-start(bf16[384,128]{1,0:T(8,128)(2,1)S(1)} %get-tuple-element.123), channel_id=1, source_target_pairs={{0,24},{4,28},{8,16},{12,20},{16,8},{20,12},{24,0},{28,4},{1,25},{... | collective-permute-start | bytes 294920 | tf_op jit(solution)/shard_map/ppermute | solution.py:418
  81.1 0.9 collective-permute-start.19
  82.0 5.6 %collective-permute-done.17.refs_7_ = bf16[384,128]{1,0:T(8,128)(2,1)S(1)} collective-permute-done((bf16[384,128]{1,0:T(8,128)(2,1)S(1)}, bf16[384,128]{1,0:T(8,128)(2,1)S(1)}, u32[]{:S(2)}, u32[]{:S(2)}) %collective-permute-start.17) | collective-permute-done | bytes 98336 | tf_op jit(solution)/shard_map/ppermute | solution.py:418
  87.6 14.0 %shard_map.95 = (bf16[1152,128]{1,0:T(8,128)(2,1)S(1)}, bf16[1152,128]{1,0:T(8,128)(2,1)S(1)}, bf16[1152,128]{1,0:T(8,128)(2,1)S(1)}, bf16[1152,128]{1,0:T(8,128...) custom-call(s32[1]{0:T(128)} %bitcast.me_s, ...), custom_call_target="tpu_custom_call" | custom-call | flops 3019898880 | bytes 6291456 | tf_op jit(solution)/shard_map/pallas_call | solution.py:400
  101.6 0.2 collective-permute-start.20
  101.8 1.8 %collective-permute-start.21 = (bf16[1152,128]{1,0:T(8,128)(2,1)S(1)}, bf16[1152,128]{1,0:T(8,128)(2,1)S(1)}, u32[]{:S(2)}, u32[]{:S(2)}) collective-permute-start(bf16[1152,128]{1,0:T(8,128)(2,1)S(1)} %get-tuple-element.127), channel_id=1, source_target_pairs={{0,8},{4,12},{8,0},{12,4},{16,24},{20,28},{24,16},{28,20},{1,9},{5... | collective-permute-start | bytes 884744 | tf_op jit(solution)/shard_map/ppermute | solution.py:418
  103.6 1.7 %collective-permute-start.23 = (bf16[1152,128]{1,0:T(8,128)(2,1)S(1)}, bf16[1152,128]{1,0:T(8,128)(2,1)S(1)}, u32[]{:S(2)}, u32[]{:S(2)}) collective-permute-start(bf16[1152,128]{1,0:T(8,128)(2,1)S(1)} %get-tuple-element.129), channel_id=1, source_target_pairs={{0,16},{4,20},{8,24},{12,28},{16,0},{20,4},{24,8},{28,12},{1,17},{... | collective-permute-start | bytes 884744 | tf_op jit(solution)/shard_map/ppermute | solution.py:418
  105.2 0.1 collective-permute-start.24
  105.3 2.9 %collective-permute-start.25 = (bf16[1152,128]{1,0:T(8,128)(2,1)S(1)}, bf16[1152,128]{1,0:T(8,128)(2,1)S(1)}, u32[]{:S(2)}, u32[]{:S(2)}) collective-permute-start(bf16[1152,128]{1,0:T(8,128)(2,1)S(1)} %get-tuple-element.131), channel_id=1, source_target_pairs={{0,24},{4,28},{8,16},{12,20},{16,8},{20,12},{24,0},{28,4},{1,25},{... | collective-permute-start | bytes 884744 | tf_op jit(solution)/shard_map/ppermute | solution.py:418
  108.2 3.5 %collective-permute-done.21.refs_2_ = bf16[1152,128]{1,0:T(8,128)(2,1)S(1)} collective-permute-done((bf16[1152,128]{1,0:T(8,128)(2,1)S(1)}, bf16[1152,128]{1,0:T(8,128)(2,1)S(1)}, u32[]{:S(2)}, u32[]{:S(2)}) %collective-permute-start.21) | collective-permute-done | bytes 294944 | tf_op jit(solution)/shard_map/ppermute | solution.py:418
  111.6 0.9 collective-permute-start.26
  112.5 4.7 %collective-permute-done.22.refs_3_ = bf16[1152,128]{1,0:T(8,128)(2,1)S(1)} collective-permute-done((bf16[1152,128]{1,0:T(8,128)(2,1)S(1)}, bf16[1152,128]{1,0:T(8,128)(2,1)S(1)}, u32[]{:S(2)}, u32[]{:S(2)}) %collective-permute-start.22) | collective-permute-done | bytes 294944 | tf_op jit(solution)/shard_map/ppermute | solution.py:418
  117.2 14.0 %collective-permute-done.24.refs_5_ = bf16[1152,128]{1,0:T(8,128)(2,1)S(1)} collective-permute-done((bf16[1152,128]{1,0:T(8,128)(2,1)S(1)}, bf16[1152,128]{1,0:T(8,128)(2,1)S(1)}, u32[]{:S(2)}, u32[]{:S(2)}) %collective-permute-start.24) | collective-permute-done | bytes 294944 | tf_op jit(solution)/shard_map/ppermute | solution.py:418
  131.3 2.1 %shard_map.96 = (bf16[384,1024]{1,0:T(8,128)(2,1)}, bf16[384,1024]{1,0:T(8,128)(2,1)}, bf16[384,1024]{1,0:T(8,128)(2,1)}) custom-call(s32[1]{0:T(128)} %bitcast.me_s, bf16[1152,128]{1,0:T(8,128)(2,1)S(1)} %get-tuple-element.125.refs_0_, bf16[1152,128]{1,0:T(8,128)(2,1)S(1)} %collective-permute-done.20.refs_1_, ...), custom_call_target="tpu_custom_call" | custom-call | tf_op jit(solution)/shard_map/pallas_call | solution.py:88
  (29 shorter events, 0.3 us)
Async XLA Ops:
  1.7 19.3 %collective-permute-start = (bf16[256,1024]{1,0:T(8,128)(2,1)S(1)}, bf16[256,1024]{1,0:T(8,128)(2,1)S(1)}, u32[]{:S(2)}, u32[]{:S(2)}) collective-permute-start(bf16[256,1024]{1,0:T(8,128)(2,1)S(1)} %slice.6.o_ref), channel_id=1, source_target_pairs={{0,1},{1,2},{2,3},{3,0},{4,5},{5,6},{6,7},{7,4},{8,9},{9,10},{10,1... | collective-permute-start | bytes 1572872 | tf_op jit(solution)/shard_map/ppermute | solution.py:421
  4.8 1.1 copy-start
  5.9 1.1 copy-start.1
  7.1 1.1 copy-start.2
  8.2 0.7 copy-start.3
  10.7 10.3 %collective-permute-start.1 = (bf16[1168,128]{1,0:T(8,128)(2,1)}, bf16[1168,128]{1,0:T(8,128)(2,1)S(1)}, u32[]{:S(2)}, u32[]{:S(2)}) collective-permute-start(bf16[1168,128]{1,0:T(8,128)(2,1)} %get-tuple-element.69), channel_id=1, source_target_pairs={{0,8},{4,12},{8,0},{12,4},{16,24},{20,28},{24,16},{28,20},{1,9},{5... | collective-permute-start | bytes 897032 | tf_op jit(solution)/shard_map/ppermute | solution.py:418
  12.2 21.5 %collective-permute-start.4 = (bf16[1168,128]{1,0:T(8,128)(2,1)}, bf16[1168,128]{1,0:T(8,128)(2,1)S(1)}, u32[]{:S(2)}, u32[]{:S(2)}) collective-permute-start(bf16[1168,128]{1,0:T(8,128)(2,1)} %get-tuple-element.73), channel_id=1, source_target_pairs={{0,16},{4,20},{8,24},{12,28},{16,0},{20,4},{24,8},{28,12},{1,17},{... | collective-permute-start | bytes 897032 | tf_op jit(solution)/shard_map/ppermute | solution.py:418
  13.8 20.0 %collective-permute-start.5 = (bf16[1168,128]{1,0:T(8,128)(2,1)}, bf16[1168,128]{1,0:T(8,128)(2,1)S(1)}, u32[]{:S(2)}, u32[]{:S(2)}) collective-permute-start(bf16[1168,128]{1,0:T(8,128)(2,1)} %get-tuple-element.74), channel_id=1, source_target_pairs={{0,24},{4,28},{8,16},{12,20},{16,8},{20,12},{24,0},{28,4},{1,25},{... | collective-permute-start | bytes 897032 | tf_op jit(solution)/shard_map/ppermute | solution.py:418
  21.0 22.4 %collective-permute-start.2 = (bf16[256,1024]{1,0:T(8,128)(2,1)S(1)}, bf16[256,1024]{1,0:T(8,128)(2,1)S(1)}, u32[]{:S(2)}, u32[]{:S(2)}) collective-permute-start(bf16[256,1024]{1,0:T(8,128)(2,1)S(1)} %collective-permute-done.o_ref), channel_id=1, source_target_pairs={{0,1},{1,2},{2,3},{3,0},{4,5},{5,6},{6,7},{7,4},{8,9},{9,10},{10,1... | collective-permute-start | bytes 1572872 | tf_op jit(solution)/shard_map/ppermute | solution.py:421
  22.6 13.6 %collective-permute-start.6 = (bf16[1168,128]{1,0:T(8,128)(2,1)S(1)}, bf16[1168,128]{1,0:T(8,128)(2,1)S(1)}, u32[]{:S(2)}, u32[]{:S(2)}) collective-permute-start(bf16[1168,128]{1,0:T(8,128)(2,1)S(1)} %get-tuple-element.75), channel_id=1, source_target_pairs={{0,28},{4,24},{8,20},{12,16},{16,12},{20,8},{24,4},{28,0},{1,29},{... | collective-permute-start | bytes 897032 | tf_op jit(solution)/shard_map/ppermute | solution.py:418
  22.6 17.3 %collective-permute-start.7 = (bf16[1168,128]{1,0:T(8,128)(2,1)S(1)}, bf16[1168,128]{1,0:T(8,128)(2,1)S(1)}, u32[]{:S(2)}, u32[]{:S(2)}) collective-permute-start(bf16[1168,128]{1,0:T(8,128)(2,1)S(1)} %get-tuple-element.76), channel_id=1, source_target_pairs={{0,20},{4,16},{8,28},{12,24},{16,4},{20,0},{24,12},{28,8},{1,21},{... | collective-permute-start | bytes 897032 | tf_op jit(solution)/shard_map/ppermute | solution.py:418
  33.8 7.4 %collective-permute-start.8 = (bf16[1168,128]{1,0:T(8,128)(2,1)S(1)}, bf16[1168,128]{1,0:T(8,128)(2,1)S(1)}, u32[]{:S(2)}, u32[]{:S(2)}) collective-permute-start(bf16[1168,128]{1,0:T(8,128)(2,1)S(1)} %get-tuple-element.77), channel_id=1, source_target_pairs={{0,12},{4,8},{8,4},{12,0},{16,28},{20,24},{24,20},{28,16},{1,13},{... | collective-permute-start | bytes 897032 | tf_op jit(solution)/shard_map/ppermute | solution.py:418
  33.8 9.6 %collective-permute-start.3 = (bf16[128,1024]{1,0:T(8,128)(2,1)S(1)}, bf16[128,1024]{1,0:T(8,128)(2,1)S(1)}, u32[]{:S(2)}, u32[]{:S(2)}) collective-permute-start(bf16[128,1024]{1,0:T(8,128)(2,1)S(1)} %slice.7.o_ref), channel_id=1, source_target_pairs={{0,1},{1,2},{2,3},{3,0},{4,5},{5,6},{6,7},{7,4},{8,9},{9,10},{10,1... | collective-permute-start | bytes 786440 | tf_op jit(solution)/shard_map/ppermute | solution.py:421
  36.1 8.6 %collective-permute-start.9 = (bf16[1168,128]{1,0:T(8,128)(2,1)S(1)}, bf16[1168,128]{1,0:T(8,128)(2,1)S(1)}, u32[]{:S(2)}, u32[]{:S(2)}) collective-permute-start(bf16[1168,128]{1,0:T(8,128)(2,1)S(1)} %get-tuple-element.83), channel_id=1, source_target_pairs={{0,4},{4,0},{8,12},{12,8},{16,20},{20,16},{24,28},{28,24},{1,5},{5... | collective-permute-start | bytes 897032 | tf_op jit(solution)/shard_map/ppermute | solution.py:418
  43.4 19.9 %collective-permute-start.10 = (bf16[256,1024]{1,0:T(8,128)(2,1)S(1)}, bf16[256,1024]{1,0:T(8,128)(2,1)S(1)}, u32[]{:S(2)}, u32[]{:S(2)}) collective-permute-start(bf16[256,1024]{1,0:T(8,128)(2,1)S(1)} %collective-permute-done.2.o_ref), channel_id=1, source_target_pairs={{0,1},{1,2},{2,3},{3,0},{4,5},{5,6},{6,7},{7,4},{8,9},{9,10},{10,1... | collective-permute-start | bytes 1572872 | tf_op jit(solution)/shard_map/ppermute | solution.py:421
  43.4 19.9 %collective-permute-start.11 = (bf16[128,1024]{1,0:T(8,128)(2,1)S(1)}, bf16[128,1024]{1,0:T(8,128)(2,1)S(1)}, u32[]{:S(2)}, u32[]{:S(2)}) collective-permute-start(bf16[128,1024]{1,0:T(8,128)(2,1)S(1)} %collective-permute-done.3.o_ref), channel_id=1, source_target_pairs={{0,1},{1,2},{2,3},{3,0},{4,5},{5,6},{6,7},{7,4},{8,9},{9,10},{10,1... | collective-permute-start | bytes 786440 | tf_op jit(solution)/shard_map/ppermute | solution.py:421
  63.3 8.2 %collective-permute-start.12 = (bf16[128,1024]{1,0:T(8,128)(2,1)S(1)}, bf16[128,1024]{1,0:T(8,128)(2,1)S(1)}, u32[]{:S(2)}, u32[]{:S(2)}) collective-permute-start(bf16[128,1024]{1,0:T(8,128)(2,1)S(1)} %collective-permute-done.11.o_ref), channel_id=1, source_target_pairs={{0,1},{1,2},{2,3},{3,0},{4,5},{5,6},{6,7},{7,4},{8,9},{9,10},{10,1... | collective-permute-start | bytes 786440 | tf_op jit(solution)/shard_map/ppermute | solution.py:421
  72.3 5.9 %collective-permute-start.13 = (bf16[384,128]{1,0:T(8,128)(2,1)S(1)}, bf16[384,128]{1,0:T(8,128)(2,1)S(1)}, u32[]{:S(2)}, u32[]{:S(2)}) collective-permute-start(bf16[384,128]{1,0:T(8,128)(2,1)S(1)} %get-tuple-element.118), channel_id=1, source_target_pairs={{0,4},{4,0},{8,12},{12,8},{16,20},{20,16},{24,28},{28,24},{1,5},{5... | collective-permute-start | bytes 294920 | tf_op jit(solution)/shard_map/ppermute | solution.py:418
  72.4 8.7 %collective-permute-start.14 = (bf16[384,128]{1,0:T(8,128)(2,1)S(1)}, bf16[384,128]{1,0:T(8,128)(2,1)S(1)}, u32[]{:S(2)}, u32[]{:S(2)}) collective-permute-start(bf16[384,128]{1,0:T(8,128)(2,1)S(1)} %get-tuple-element.119), channel_id=1, source_target_pairs={{0,8},{4,12},{8,0},{12,4},{16,24},{20,28},{24,16},{28,20},{1,9},{5... | collective-permute-start | bytes 294920 | tf_op jit(solution)/shard_map/ppermute | solution.py:418
  75.5 6.5 %collective-permute-start.15 = (bf16[384,128]{1,0:T(8,128)(2,1)S(1)}, bf16[384,128]{1,0:T(8,128)(2,1)S(1)}, u32[]{:S(2)}, u32[]{:S(2)}) collective-permute-start(bf16[384,128]{1,0:T(8,128)(2,1)S(1)} %get-tuple-element.120), channel_id=1, source_target_pairs={{0,12},{4,8},{8,4},{12,0},{16,28},{20,24},{24,20},{28,16},{1,13},{... | collective-permute-start | bytes 294920 | tf_op jit(solution)/shard_map/ppermute | solution.py:418
  75.6 6.4 %collective-permute-start.16 = (bf16[384,128]{1,0:T(8,128)(2,1)S(1)}, bf16[384,128]{1,0:T(8,128)(2,1)S(1)}, u32[]{:S(2)}, u32[]{:S(2)}) collective-permute-start(bf16[384,128]{1,0:T(8,128)(2,1)S(1)} %get-tuple-element.121), channel_id=1, source_target_pairs={{0,16},{4,20},{8,24},{12,28},{16,0},{20,4},{24,8},{28,12},{1,17},{... | collective-permute-start | bytes 294920 | tf_op jit(solution)/shard_map/ppermute | solution.py:418
  78.2 9.4 %collective-permute-start.17 = (bf16[384,128]{1,0:T(8,128)(2,1)S(1)}, bf16[384,128]{1,0:T(8,128)(2,1)S(1)}, u32[]{:S(2)}, u32[]{:S(2)}) collective-permute-start(bf16[384,128]{1,0:T(8,128)(2,1)S(1)} %get-tuple-element.122), channel_id=1, source_target_pairs={{0,20},{4,16},{8,28},{12,24},{16,4},{20,0},{24,12},{28,8},{1,21},{... | collective-permute-start | bytes 294920 | tf_op jit(solution)/shard_map/ppermute | solution.py:418
  78.2 9.4 %collective-permute-start.18 = (bf16[384,128]{1,0:T(8,128)(2,1)S(1)}, bf16[384,128]{1,0:T(8,128)(2,1)S(1)}, u32[]{:S(2)}, u32[]{:S(2)}) collective-permute-start(bf16[384,128]{1,0:T(8,128)(2,1)S(1)} %get-tuple-element.123), channel_id=1, source_target_pairs={{0,24},{4,28},{8,16},{12,20},{16,8},{20,12},{24,0},{28,4},{1,25},{... | collective-permute-start | bytes 294920 | tf_op jit(solution)/shard_map/ppermute | solution.py:418
  81.1 6.5 %collective-permute-start.19 = (bf16[384,128]{1,0:T(8,128)(2,1)S(1)}, bf16[384,128]{1,0:T(8,128)(2,1)S(1)}, u32[]{:S(2)}, u32[]{:S(2)}) collective-permute-start(bf16[384,128]{1,0:T(8,128)(2,1)S(1)} %get-tuple-element.124), channel_id=1, source_target_pairs={{0,28},{4,24},{8,20},{12,16},{16,12},{20,8},{24,4},{28,0},{1,29},{... | collective-permute-start | bytes 294920 | tf_op jit(solution)/shard_map/ppermute | solution.py:418
  101.6 3.7 %collective-permute-start.20 = (bf16[1152,128]{1,0:T(8,128)(2,1)S(1)}, bf16[1152,128]{1,0:T(8,128)(2,1)S(1)}, u32[]{:S(2)}, u32[]{:S(2)}) collective-permute-start(bf16[1152,128]{1,0:T(8,128)(2,1)S(1)} %get-tuple-element.126), channel_id=1, source_target_pairs={{0,4},{4,0},{8,12},{12,8},{16,20},{20,16},{24,28},{28,24},{1,5},{5... | collective-permute-start | bytes 884744 | tf_op jit(solution)/shard_map/ppermute | solution.py:418
  101.8 9.8 %collective-permute-start.21 = (bf16[1152,128]{1,0:T(8,128)(2,1)S(1)}, bf16[1152,128]{1,0:T(8,128)(2,1)S(1)}, u32[]{:S(2)}, u32[]{:S(2)}) collective-permute-start(bf16[1152,128]{1,0:T(8,128)(2,1)S(1)} %get-tuple-element.127), channel_id=1, source_target_pairs={{0,8},{4,12},{8,0},{12,4},{16,24},{20,28},{24,16},{28,20},{1,9},{5... | collective-permute-start | bytes 884744 | tf_op jit(solution)/shard_map/ppermute | solution.py:418
  103.6 13.7 %collective-permute-start.22 = (bf16[1152,128]{1,0:T(8,128)(2,1)S(1)}, bf16[1152,128]{1,0:T(8,128)(2,1)S(1)}, u32[]{:S(2)}, u32[]{:S(2)}) collective-permute-start(bf16[1152,128]{1,0:T(8,128)(2,1)S(1)} %get-tuple-element.128), channel_id=1, source_target_pairs={{0,12},{4,8},{8,4},{12,0},{16,28},{20,24},{24,20},{28,16},{1,13},{... | collective-permute-start | bytes 884744 | tf_op jit(solution)/shard_map/ppermute | solution.py:418
  103.6 13.7 %collective-permute-start.23 = (bf16[1152,128]{1,0:T(8,128)(2,1)S(1)}, bf16[1152,128]{1,0:T(8,128)(2,1)S(1)}, u32[]{:S(2)}, u32[]{:S(2)}) collective-permute-start(bf16[1152,128]{1,0:T(8,128)(2,1)S(1)} %get-tuple-element.129), channel_id=1, source_target_pairs={{0,16},{4,20},{8,24},{12,28},{16,0},{20,4},{24,8},{28,12},{1,17},{... | collective-permute-start | bytes 884744 | tf_op jit(solution)/shard_map/ppermute | solution.py:418
  105.2 26.0 %collective-permute-start.24 = (bf16[1152,128]{1,0:T(8,128)(2,1)S(1)}, bf16[1152,128]{1,0:T(8,128)(2,1)S(1)}, u32[]{:S(2)}, u32[]{:S(2)}) collective-permute-start(bf16[1152,128]{1,0:T(8,128)(2,1)S(1)} %get-tuple-element.130), channel_id=1, source_target_pairs={{0,20},{4,16},{8,28},{12,24},{16,4},{20,0},{24,12},{28,8},{1,21},{... | collective-permute-start | bytes 884744 | tf_op jit(solution)/shard_map/ppermute | solution.py:418
  105.3 26.0 %collective-permute-start.25 = (bf16[1152,128]{1,0:T(8,128)(2,1)S(1)}, bf16[1152,128]{1,0:T(8,128)(2,1)S(1)}, u32[]{:S(2)}, u32[]{:S(2)}) collective-permute-start(bf16[1152,128]{1,0:T(8,128)(2,1)S(1)} %get-tuple-element.131), channel_id=1, source_target_pairs={{0,24},{4,28},{8,16},{12,20},{16,8},{20,12},{24,0},{28,4},{1,25},{... | collective-permute-start | bytes 884744 | tf_op jit(solution)/shard_map/ppermute | solution.py:418
  111.6 19.6 %collective-permute-start.26 = (bf16[1152,128]{1,0:T(8,128)(2,1)S(1)}, bf16[1152,128]{1,0:T(8,128)(2,1)S(1)}, u32[]{:S(2)}, u32[]{:S(2)}) collective-permute-start(bf16[1152,128]{1,0:T(8,128)(2,1)S(1)} %get-tuple-element.132), channel_id=1, source_target_pairs={{0,28},{4,24},{8,20},{12,16},{16,12},{20,8},{24,4},{28,0},{1,29},{... | collective-permute-start | bytes 884744 | tf_op jit(solution)/shard_map/ppermute | solution.py:418

commit v8 on v6

--- a/solution.py
+++ b/solution.py
@@ -208,17 +208,17 @@
 def forward_kernel(peers, heads, rows, bq, bk, kept, me_s, *refs):
     blocks = refs[:peers]
     if kept:
-        p_list, top_list = refs[peers + 7:peers + 9]
-        refs = refs[:peers + 7] + refs[peers + 9:]
-    q_ref, v_ref, kx_ref, qtx_ref, kt_ref, out_ref, log_ref = refs[peers:peers + 7]
-    plan_q, plan_k, count_ref, own_q, own_k, own_count = refs[peers + 7:peers + 13]
-    vt_ref, doc_ref, sum_ref, s0, top0, s1, top1 = refs[peers + 13:]
-    total = q_ref.shape[0]
+        p_list, top_list = refs[peers + 6:peers + 8]
+        refs = refs[:peers + 6] + refs[peers + 8:]
+    v_ref, qx_ref, kx_ref, kt_ref, rows_ref, log_ref = refs[peers:peers + 6]
+    plan_q, plan_k, count_ref, own_q, own_k, own_count = refs[peers + 6:peers + 12]
+    vt_ref, out_ref, doc_ref, sum_ref, s0, top0, s1, top1 = refs[peers + 12:]
+    total = v_ref.shape[0]
     factor = HD ** (-0.5) * math.log2(math.e)
     me = me_s[0]
     for d, block in enumerate(blocks):
         place = me ^ d
-        for part, ref in enumerate((q_ref, kx_ref.at[:, :HD], v_ref)):
+        for part, ref in enumerate((qx_ref.at[:, :HD], kx_ref.at[:, :HD], v_ref)):
             ref[aligned(place, rows), :] = block[part * rows:(part + 1) * rows, :]
         docs = block[3 * rows:, :].astype(jnp.float32)
         for t in range(rows // HD):
@@ -237,9 +237,9 @@
     lows = [jnp.min(first[:, qi * back_q:(qi + 1) * back_q]) for qi in range(total // back_q)]
     fill_plan(lows, total, back_q, back_k, own, plan_q, plan_k, count_ref)
     same = lax.broadcasted_iota(jnp.int32, (HD, total), 0).astype(jnp.float32) == docs
-    qtx_ref[:HD, :] = q_ref[...].T
-    qtx_ref[HD:, :] = jnp.where(same, 0.0, NEG_LARGE).astype(jnp.bfloat16)
-    kx_ref[:, HD:] = jnp.where(same, 1.0, 0.0).astype(jnp.bfloat16).T
+    ones = jnp.where(same, 1.0, 0.0).astype(jnp.bfloat16).T
+    kx_ref[:, HD:] = ones
+    qx_ref[:, HD:] = ((1.0 - ones.astype(jnp.float32)) * NEG_LARGE).astype(jnp.bfloat16)
     kt_ref[...] = kx_ref[:, :HD].T
     vt_ref[:HD, :] = v_ref[...].T
     vt_ref[HD:, :] = jnp.ones((ONES_ROWS, total), jnp.bfloat16)
@@ -250,7 +250,7 @@
     def early(now, qi, ki, buffer, diagonal):
         s_ref, top_ref = buffer
         keys, queries = aligned(ki, bk), aligned(qi, bq)
-        s = dot32(kx_ref[keys, :], qtx_ref[:, queries]) * factor
+        s = dot32(kx_ref[keys, :], qx_ref[queries, :], NT) * factor
         if diagonal:
             s = jnp.where(at_or_before(qi * bq, ki * bk, (bk, bq)), s, NEG_LARGE)
         s_ref[...] = s
@@ -264,37 +264,46 @@
         p = jnp.exp2(s_ref[...] - new_top)
         fix = jnp.exp2(top - new_top)
         high = p.astype(jnp.bfloat16)
-        rest = (p - high.astype(jnp.float32)).astype(jnp.bfloat16)
+        vt = vt_ref[:, keys]
+        sums = dot32(vt, high)
         if kept:
             p_list[now] = high
             top_list[now] = new_top
-        vt = vt_ref[:, keys]
-        sums = dot32(vt, high) + dot32(vt, rest)
+        else:
+            sums = sums + dot32(vt, (p - high.astype(jnp.float32)).astype(jnp.bfloat16))
         out_ref[:, queries] = out_ref[:, queries] * fix + sums[:HD, :]
         sum_ref[:, queries] = sum_ref[:, queries] * fix + sums[HD:HD + 1, :]
         log_ref[:, queries] = new_top
 
     pipelined(own_q, own_k, own_count, early, late, ((s0, top0), (s1, top1)))
     total_p = sum_ref[...]
-    out_ref[...] = out_ref[...] / total_p
+    rows_ref[...] = (out_ref[...] / total_p).T
     log_ref[...] = log_ref[...] + jnp.log2(total_p)
 
 
-def backward_kernel(peers, heads, rows, bq, bk, kept, me_s, plan_q, plan_k, count_ref, q_ref, v_ref,
-                    kx_ref, qtx_ref, kt_ref, out_ref, log_ref, *refs):
+def backward_kernel(peers, heads, rows, bq, bk, kept, me_s, plan_q, plan_k, count_ref, v_ref,
+                    qx_ref, kx_ref, kt_ref, rows_ref, log_ref, *refs):
     if kept:
         p_list, top_list = refs[:2]
         refs = refs[2:]
     blocks = refs[:peers]
     results = refs[peers:peers + heads]
-    g_ref, gt_ref, dot_ref, dk_acc, dv_acc, dq_acc, p0, ds0, p1, ds1 = refs[peers + heads:]
+    g_ref, dot_ref, dk_acc, dv_acc, dq_acc, p0, ds0, p1, ds1 = refs[peers + heads:]
     scale = HD ** (-0.5)
     factor = scale * math.log2(math.e)
     me = me_s[0]
     for d, block in enumerate(blocks):
         g_ref[aligned(me ^ d, rows), :] = block[...]
-    gt_ref[...] = g_ref[...].T
-    dot_ref[...] = jnp.sum(gt_ref[...].astype(jnp.float32) * out_ref[...], axis=0, keepdims=True)
+    ones = jnp.ones((ONES_ROWS, HD), jnp.bfloat16)
+    for start in range(0, g_ref.shape[0], bq):
+        part = slice(start, start + bq)
+        left = g_ref[part, :].astype(jnp.float32) * rows_ref[part, :]
+        dots = 0.0
+        for _ in range(3):
+            term = left.astype(jnp.bfloat16)
+            left = left - term.astype(jnp.float32)
+            dots = dots + dot32(ones, term, NT)
+        dot_ref[:, part] = dots[:1, :]
     dk_acc[...] = jnp.zeros_like(dk_acc)
     dv_acc[...] = jnp.zeros_like(dv_acc)
     dq_acc[...] = jnp.zeros_like(dq_acc)
@@ -306,18 +315,18 @@
         if kept:
             p = p_list[now].astype(jnp.float32) * jnp.exp2(top_list[now] - log_row)
         else:
-            p = jnp.exp2(dot32(kx_ref[keys, :], qtx_ref[:, queries]) * factor - log_row)
+            p = jnp.exp2(dot32(kx_ref[keys, :], qx_ref[queries, :], NT) * factor - log_row)
             if diagonal:
                 p = jnp.where(at_or_before(qi * bq, ki * bk, (bk, bq)), p, 0.0)
         p_ref[...] = p.astype(jnp.bfloat16)
-        dp = dot32(v_ref[keys, :], gt_ref[:, queries])
+        dp = dot32(v_ref[keys, :], g_ref[queries, :], NT)
         ds_ref[...] = (p * (dp - dot_ref[:, queries])).astype(jnp.bfloat16)
 
     def late(now, qi, ki, buffer):
         p_ref, ds_ref = buffer
         keys, queries = aligned(ki, bk), aligned(qi, bq)
         dv_acc[keys, :] += dot32(p_ref[...], g_ref[queries, :])
-        dk_acc[keys, :] += dot32(ds_ref[...], q_ref[queries, :])
+        dk_acc[keys, :] += dot32(ds_ref[...], qx_ref[queries, :HD])
         dq_acc[:, queries] += dot32(kt_ref[:, keys], ds_ref[...])
 
     pipelined(plan_q, plan_k, count_ref, early, late, ((p0, ds0), (p1, ds1)))
@@ -349,11 +358,10 @@
     plan = [(plan_size(total, *back),)] * 2 + [(2,)]
     own_plan = [(plan_size(total, bq, bk),)] * 2 + [(2,)]
     vectors = [
-        *[jax.ShapeDtypeStruct((total, HD), jnp.bfloat16)] * 2,
-        jax.ShapeDtypeStruct((total, 2 * HD), jnp.bfloat16),
-        jax.ShapeDtypeStruct((2 * HD, total), jnp.bfloat16),
+        jax.ShapeDtypeStruct((total, HD), jnp.bfloat16),
+        *[jax.ShapeDtypeStruct((total, 2 * HD), jnp.bfloat16)] * 2,
         jax.ShapeDtypeStruct((HD, total), jnp.bfloat16),
-        jax.ShapeDtypeStruct((HD, total), jnp.float32),
+        jax.ShapeDtypeStruct((total, HD), jnp.float32),
         jax.ShapeDtypeStruct((1, total), jnp.float32),
     ]
     kept = keeps_list(total, peers, heads)
@@ -362,6 +370,7 @@
         vectors.append(jax.ShapeDtypeStruct((*own_plan[0], 1, bq), jnp.float32))
     scratch = [
         pltpu.VMEM((HD + ONES_ROWS, total), jnp.bfloat16),
+        pltpu.VMEM((HD, total), jnp.float32),
         pltpu.VMEM((1, total), jnp.float32),
         pltpu.VMEM((1, total), jnp.float32),
         *[pltpu.VMEM((bk, bq), jnp.float32), pltpu.VMEM((1, bq), jnp.float32)] * 2,
@@ -386,7 +395,6 @@
     out_shape = [jax.ShapeDtypeStruct((3 * rows, HD), jnp.bfloat16)] * heads
     scratch = [
         pltpu.VMEM((total, HD), jnp.bfloat16),
-        pltpu.VMEM((HD, total), jnp.bfloat16),
         pltpu.VMEM((1, total), jnp.float32),
         pltpu.VMEM((total, HD), jnp.float32),
         pltpu.VMEM((total, HD), jnp.float32),

time: 129 us -> 128 us (level)
  waiting for transfers between devices: 56.5 us -> 51.8 us
  local copies, waits for them, and re-layouts: 8.62 us -> 11.8 us
    ppermute x3, waiting for transfers between devices: 8.74 us -> 4.59 us  [pass_on(): lax.ppermute(x, 'head', [(i, (i + 1) % groups) for i in range(groups)])]
    unnamed x10 -> x26, local copies, waits for them, and re-layouts: 4.08 us -> 6.98 us
  transfers between devices with their start and end apart: 24 -> 24, of which waited for: 13 -> 12; matrix products, arithmetic and copies ran while one was open for 4% -> 4% of each run, Pallas kernels for 16% -> 16%
where the time goes in v8:
time: 128 us; the launch traced here: 127 us
  waiting for transfers between devices  51.8 us (40%)
  Pallas kernels  38.4 us (30%)
  starting transfers between devices  24.7 us (19%)
  local copies, waits for them, and re-layouts  11.8 us (9%)
    ppermute x21, waiting for transfers between devices, exchange(): lax.ppermute(x, 'seq', [(i, i ^ d) for i in range(peers)])  47.2 us
    ppermute x21, starting transfers between devices, exchange(): lax.ppermute(x, 'seq', [(i, i ^ d) for i in range(peers)])  20.3 us
    pallas_call x1, Pallas kernels, attention_forward(): pl.pallas_call(functools.partial(forward_kernel, peers, heads, rows, bq,...  16 us
    pallas_call x1, Pallas kernels, attention_backward(): pl.pallas_call(functools.partial(backward_kernel, peers, heads, rows, bq,...  14.5 us
    unnamed x26, local copies, waits for them, and re-layouts  6.98 us
    dynamic_slice x1, local copies, waits for them, and re-layouts, per_device(): lax.dynamic_slice_in_dim(out_weight, block * width, width, 1)  4.79 us
    ppermute x3, waiting for transfers between devices, pass_on(): lax.ppermute(x, 'head', [(i, (i + 1) % groups) for i in range(groups)])  4.59 us
    ppermute x3, starting transfers between devices, pass_on(): lax.ppermute(x, 'head', [(i, (i + 1) % groups) for i in range(groups)])  4.43 us
  transfers between devices with their start and end apart: 24, of which 12 were waited for; matrix products, arithmetic and copies ran while one was open for 4% of the time, Pallas kernels for 16%

profile of v8, /device:TPU:0, one launch (start us, length us, event | category | flops | bytes accessed | tf_op | source)
XLA Modules:
  0.0 127.4 jit_solution(1181400498866017996)
XLA Ops:
  0.6 3.1 %collective-permute-start = (bf16[384,1024]{1,0:T(8,128)(2,1)}, bf16[384,1024]{1,0:T(8,128)(2,1)S(1)}, u32[]{:S(2)}, u32[]{:S(2)}) collective-permute-start(bf16[384,1024]{1,0:T(8,128)(2,1)} %o_ref.1), channel_id=1, source_target_pairs={{0,1},{1,2},{2,3},{3,0},{4,5},{5,6},{6,7},{7,4},{8,9},{9,10},{10,1... | collective-permute-start | bytes 2359304 | tf_op jit(solution)/shard_map/ppermute | solution.py:425
  3.7 1.1 copy-done
  4.8 1.1 copy-done.1
  6.0 1.1 copy-done.2
  7.1 0.7 copy-done.4
  7.8 1.7 %shard_map.85 = (bf16[1168,128]{1,0:T(8,128)(2,1)S(1)}, bf16[1168,128]{1,0:T(8,128)(2,1)S(1)}, bf16[1168,128]{1,0:T(8,128)(2,1)}, bf16[1168,128]{1,0:T(8,128)(2,...) custom-call(s32[1]{0:T(128)} %bitcast.me_s, ...), custom_call_target="tpu_custom_call" | custom-call | tf_op jit(solution)/shard_map/pallas_call | solution.py:68
  9.5 0.7 copy-done.5
  10.2 0.7 copy-done.7
  10.9 0.7 copy-done.9
  11.7 0.7 copy-done.11
  12.4 1.5 %collective-permute-start.1 = (bf16[1168,128]{1,0:T(8,128)(2,1)}, bf16[1168,128]{1,0:T(8,128)(2,1)S(1)}, u32[]{:S(2)}, u32[]{:S(2)}) collective-permute-start(bf16[1168,128]{1,0:T(8,128)(2,1)} %get-tuple-element.58), channel_id=1, source_target_pairs={{0,8},{4,12},{8,0},{12,4},{16,24},{20,28},{24,16},{28,20},{1,9},{5... | collective-permute-start | bytes 897032 | tf_op jit(solution)/shard_map/ppermute | solution.py:422
  13.9 1.5 %collective-permute-start.2 = (bf16[1168,128]{1,0:T(8,128)(2,1)}, bf16[1168,128]{1,0:T(8,128)(2,1)S(1)}, u32[]{:S(2)}, u32[]{:S(2)}) collective-permute-start(bf16[1168,128]{1,0:T(8,128)(2,1)} %get-tuple-element.59), channel_id=1, source_target_pairs={{0,16},{4,20},{8,24},{12,28},{16,0},{20,4},{24,8},{28,12},{1,17},{... | collective-permute-start | bytes 897032 | tf_op jit(solution)/shard_map/ppermute | solution.py:422
  15.4 4.8 %constant_dynamic-slice_fusion = (bf16[1024,1024]{1,0:T(8,128)(2,1)S(1)}, bf16[1024,1024]{1,0:T(8,128)(2,1)S(1)}, bf16[1024,1024]{1,0:T(8,128)(2,1)S(1)}, bf16[1024,1024]{1,0:T(8,128)(2,1)S(1)}) fusion(bf16[1024,4096]{1,0:T(8,128)(2,1)} %param.10, s32[]{:T(128)S(6)} %select_n.15, s32[]{:T(128)S(6)} %select_n.13, s32[]{:T(128)S(6)} %select_n.12, s32[]{:T(128)S(6)} %select_n.14), kind=kLoop, calls=%fused_computation | loop fusion | bytes 16777232 | tf_op jit(solution)/shard_map/dynamic_slice | solution.py:444
  20.3 1.0 shard_map.86.refs_0_
  21.3 1.1 collective-permute-done.2.refs_4_
  22.4 1.1 collective-permute-done.o_ref
  23.5 0.5 collective-permute-start.3
  24.0 2.0 %collective-permute-start.4 = (bf16[1168,128]{1,0:T(8,128)(2,1)S(1)}, bf16[1168,128]{1,0:T(8,128)(2,1)S(1)}, u32[]{:S(2)}, u32[]{:S(2)}) collective-permute-start(bf16[1168,128]{1,0:T(8,128)(2,1)S(1)} %copy-done.12), channel_id=1, source_target_pairs={{0,24},{4,28},{8,16},{12,20},{16,8},{20,12},{24,0},{28,4},{1,25},{... | collective-permute-start | bytes 897032 | tf_op jit(solution)/shard_map/ppermute | solution.py:422
  26.0 2.2 %collective-permute-start.6 = (bf16[1168,128]{1,0:T(8,128)(2,1)S(1)}, bf16[1168,128]{1,0:T(8,128)(2,1)S(1)}, u32[]{:S(2)}, u32[]{:S(2)}) collective-permute-start(bf16[1168,128]{1,0:T(8,128)(2,1)S(1)} %copy-done.8), channel_id=1, source_target_pairs={{0,20},{4,16},{8,28},{12,24},{16,4},{20,0},{24,12},{28,8},{1,21},{... | collective-permute-start | bytes 897032 | tf_op jit(solution)/shard_map/ppermute | solution.py:422
  28.1 6.9 %collective-permute-done.4.refs_6_ = bf16[1168,128]{1,0:T(8,128)(2,1)S(1)} collective-permute-done((bf16[1168,128]{1,0:T(8,128)(2,1)S(1)}, bf16[1168,128]{1,0:T(8,128)(2,1)S(1)}, u32[]{:S(2)}, u32[]{:S(2)}) %collective-permute-start.4) | collective-permute-done | bytes 299040 | tf_op jit(solution)/shard_map/ppermute | solution.py:422
  35.0 1.0 shard_map.87.refs_0_
  36.0 3.9 %collective-permute-done.5.refs_7_ = bf16[1168,128]{1,0:T(8,128)(2,1)S(1)} collective-permute-done((bf16[1168,128]{1,0:T(8,128)(2,1)S(1)}, bf16[1168,128]{1,0:T(8,128)(2,1)S(1)}, u32[]{:S(2)}, u32[]{:S(2)}) %collective-permute-start.5) | collective-permute-done | bytes 299040 | tf_op jit(solution)/shard_map/ppermute | solution.py:422
  39.9 5.5 %collective-permute-done.6.refs_5_ = bf16[1168,128]{1,0:T(8,128)(2,1)S(1)} collective-permute-done((bf16[1168,128]{1,0:T(8,128)(2,1)S(1)}, bf16[1168,128]{1,0:T(8,128)(2,1)S(1)}, u32[]{:S(2)}, u32[]{:S(2)}) %collective-permute-start.6) | collective-permute-done | bytes 299040 | tf_op jit(solution)/shard_map/ppermute | solution.py:422
  45.4 0.9 collective-permute-start.9
  46.3 16.0 %shard_map.88 = (bf16[3072,128]{1,0:T(8,128)(2,1)S(1)}, bf16[3072,256]{1,0:T(8,128)(2,1)S(1)}, bf16[3072,256]{1,0:T(8,128)(2,1)S(1)}, bf16[128,3072]{1,0:T(8,128...) custom-call(s32[1]{0:T(128)} %bitcast.me_s, ...), custom_call_target="tpu_custom_call" | custom-call | flops 1811939328 | bytes 6291456 | tf_op jit(solution)/shard_map/pallas_call | solution.py:378
  62.3 1.0 shard_map.89.acc_ref
  63.4 3.5 %collective-permute-done.9.o_ref = bf16[384,1024]{1,0:T(8,128)(2,1)S(1)} collective-permute-done((bf16[384,1024]{1,0:T(8,128)(2,1)S(1)}, bf16[384,1024]{1,0:T(8,128)(2,1)S(1)}, u32[]{:S(2)}, u32[]{:S(2)}) %collective-permute-start.9) | collective-permute-done | bytes 786464 | tf_op jit(solution)/shard_map/ppermute | solution.py:425
  66.9 1.0 shard_map.90
  68.0 1.3 %collective-permute-start.11 = (bf16[384,128]{1,0:T(8,128)(2,1)S(1)}, bf16[384,128]{1,0:T(8,128)(2,1)S(1)}, u32[]{:S(2)}, u32[]{:S(2)}) collective-permute-start(bf16[384,128]{1,0:T(8,128)(2,1)S(1)} %get-tuple-element.97), channel_id=1, source_target_pairs={{0,8},{4,12},{8,0},{12,4},{16,24},{20,28},{24,16},{28,20},{1,9},{5... | collective-permute-start | bytes 294920 | tf_op jit(solution)/shard_map/ppermute | solution.py:422
  69.3 0.6 collective-permute-start.12
  69.8 1.2 collective-permute-start.13
  71.1 0.4 collective-permute-start.14
  71.5 2.2 %collective-permute-start.15 = (bf16[384,128]{1,0:T(8,128)(2,1)S(1)}, bf16[384,128]{1,0:T(8,128)(2,1)S(1)}, u32[]{:S(2)}, u32[]{:S(2)}) collective-permute-start(bf16[384,128]{1,0:T(8,128)(2,1)S(1)} %get-tuple-element.101), channel_id=1, source_target_pairs={{0,24},{4,28},{8,16},{12,20},{16,8},{20,12},{24,0},{28,4},{1,25},{... | collective-permute-start | bytes 294920 | tf_op jit(solution)/shard_map/ppermute | solution.py:422
  73.7 0.9 collective-permute-start.16
  74.8 0.6 collective-permute-done.13.refs_6_
  75.4 5.2 %collective-permute-done.14.refs_7_ = bf16[384,128]{1,0:T(8,128)(2,1)S(1)} collective-permute-done((bf16[384,128]{1,0:T(8,128)(2,1)S(1)}, bf16[384,128]{1,0:T(8,128)(2,1)S(1)}, u32[]{:S(2)}, u32[]{:S(2)}) %collective-permute-start.14) | collective-permute-done | bytes 98336 | tf_op jit(solution)/shard_map/ppermute | solution.py:422
  80.6 14.5 %shard_map.91 = (bf16[1152,128]{1,0:T(8,128)(2,1)S(1)}, bf16[1152,128]{1,0:T(8,128)(2,1)S(1)}, bf16[1152,128]{1,0:T(8,128)(2,1)S(1)}, bf16[1152,128]{1,0:T(8,128...) custom-call(s32[1]{0:T(128)} %bitcast.me_s, ...), custom_call_target="tpu_custom_call" | custom-call | flops 3019898880 | bytes 6291456 | tf_op jit(solution)/shard_map/pallas_call | solution.py:404
  95.1 0.5 collective-permute-start.17
  95.6 1.2 collective-permute-start.18
  96.9 0.2 collective-permute-start.19
  97.1 1.3 %collective-permute-start.20 = (bf16[1152,128]{1,0:T(8,128)(2,1)S(1)}, bf16[1152,128]{1,0:T(8,128)(2,1)S(1)}, u32[]{:S(2)}, u32[]{:S(2)}) collective-permute-start(bf16[1152,128]{1,0:T(8,128)(2,1)S(1)} %get-tuple-element.107), channel_id=1, source_target_pairs={{0,16},{4,20},{8,24},{12,28},{16,0},{20,4},{24,8},{28,12},{1,17},{... | collective-permute-start | bytes 884744 | tf_op jit(solution)/shard_map/ppermute | solution.py:422
  98.4 0.8 collective-permute-start.21
  99.1 2.2 %collective-permute-start.22 = (bf16[1152,128]{1,0:T(8,128)(2,1)S(1)}, bf16[1152,128]{1,0:T(8,128)(2,1)S(1)}, u32[]{:S(2)}, u32[]{:S(2)}) collective-permute-start(bf16[1152,128]{1,0:T(8,128)(2,1)S(1)} %get-tuple-element.109), channel_id=1, source_target_pairs={{0,24},{4,28},{8,16},{12,20},{16,8},{20,12},{24,0},{28,4},{1,25},{... | collective-permute-start | bytes 884744 | tf_op jit(solution)/shard_map/ppermute | solution.py:422
  101.3 4.2 %collective-permute-done.18.refs_2_ = bf16[1152,128]{1,0:T(8,128)(2,1)S(1)} collective-permute-done((bf16[1152,128]{1,0:T(8,128)(2,1)S(1)}, bf16[1152,128]{1,0:T(8,128)(2,1)S(1)}, u32[]{:S(2)}, u32[]{:S(2)}) %collective-permute-start.18) | collective-permute-done | bytes 294944 | tf_op jit(solution)/shard_map/ppermute | solution.py:422
  105.5 0.2 collective-permute-start.23
  105.7 4.9 %collective-permute-done.19.refs_3_ = bf16[1152,128]{1,0:T(8,128)(2,1)S(1)} collective-permute-done((bf16[1152,128]{1,0:T(8,128)(2,1)S(1)}, bf16[1152,128]{1,0:T(8,128)(2,1)S(1)}, u32[]{:S(2)}, u32[]{:S(2)}) %collective-permute-start.19) | collective-permute-done | bytes 294944 | tf_op jit(solution)/shard_map/ppermute | solution.py:422
  110.6 14.8 %collective-permute-done.21.refs_5_ = bf16[1152,128]{1,0:T(8,128)(2,1)S(1)} collective-permute-done((bf16[1152,128]{1,0:T(8,128)(2,1)S(1)}, bf16[1152,128]{1,0:T(8,128)(2,1)S(1)}, u32[]{:S(2)}, u32[]{:S(2)}) %collective-permute-start.21) | collective-permute-done | bytes 294944 | tf_op jit(solution)/shard_map/ppermute | solution.py:422
  125.4 2.1 %shard_map.92 = (bf16[384,1024]{1,0:T(8,128)(2,1)}, bf16[384,1024]{1,0:T(8,128)(2,1)}, bf16[384,1024]{1,0:T(8,128)(2,1)}) custom-call(s32[1]{0:T(128)} %bitcast.me_s, bf16[1152,128]{1,0:T(8,128)(2,1)S(1)} %get-tuple-element.103.refs_0_, bf16[1152,128]{1,0:T(8,128)(2,1)S(1)} %collective-permute-done.17.refs_1_, ...), custom_call_target="tpu_custom_call" | custom-call | tf_op jit(solution)/shard_map/pallas_call | solution.py:88
  (35 shorter events, 0.4 us)
Async XLA Ops:
  0.6 22.9 %collective-permute-start = (bf16[384,1024]{1,0:T(8,128)(2,1)}, bf16[384,1024]{1,0:T(8,128)(2,1)S(1)}, u32[]{:S(2)}, u32[]{:S(2)}) collective-permute-start(bf16[384,1024]{1,0:T(8,128)(2,1)} %o_ref.1), channel_id=1, source_target_pairs={{0,1},{1,2},{2,3},{3,0},{4,5},{5,6},{6,7},{7,4},{8,9},{9,10},{10,1... | collective-permute-start | bytes 2359304 | tf_op jit(solution)/shard_map/ppermute | solution.py:425
  3.7 1.1 copy-start
  4.8 1.1 copy-start.1
  6.0 1.1 copy-start.2
  7.1 0.7 copy-start.4
  9.5 0.7 copy-start.5
  10.2 0.7 copy-start.7
  10.9 0.7 copy-start.9
  11.7 0.7 copy-start.11
  12.4 8.9 %collective-permute-start.1 = (bf16[1168,128]{1,0:T(8,128)(2,1)}, bf16[1168,128]{1,0:T(8,128)(2,1)S(1)}, u32[]{:S(2)}, u32[]{:S(2)}) collective-permute-start(bf16[1168,128]{1,0:T(8,128)(2,1)} %get-tuple-element.58), channel_id=1, source_target_pairs={{0,8},{4,12},{8,0},{12,4},{16,24},{20,28},{24,16},{28,20},{1,9},{5... | collective-permute-start | bytes 897032 | tf_op jit(solution)/shard_map/ppermute | solution.py:422
  13.9 8.5 %collective-permute-start.2 = (bf16[1168,128]{1,0:T(8,128)(2,1)}, bf16[1168,128]{1,0:T(8,128)(2,1)S(1)}, u32[]{:S(2)}, u32[]{:S(2)}) collective-permute-start(bf16[1168,128]{1,0:T(8,128)(2,1)} %get-tuple-element.59), channel_id=1, source_target_pairs={{0,16},{4,20},{8,24},{12,28},{16,0},{20,4},{24,8},{28,12},{1,17},{... | collective-permute-start | bytes 897032 | tf_op jit(solution)/shard_map/ppermute | solution.py:422
  15.4 4.8 %copy-start.3 = (bf16[384,1024]{1,0:T(8,128)(2,1)S(1)}, bf16[384,1024]{1,0:T(8,128)(2,1)}, u32[]{:S(2)}) copy-start(bf16[384,1024]{1,0:T(8,128)(2,1)} %o_ref.1) | copy-start | bytes 2359300
  20.2 3.7 %copy-start.12 = (bf16[1168,128]{1,0:T(8,128)(2,1)S(1)}, bf16[1168,128]{1,0:T(8,128)(2,1)}, u32[]{:S(2)}) copy-start(bf16[1168,128]{1,0:T(8,128)(2,1)} %copy-done.11) | copy-start | bytes 897028
  20.2 5.7 %copy-start.10 = (bf16[1168,128]{1,0:T(8,128)(2,1)S(1)}, bf16[1168,128]{1,0:T(8,128)(2,1)}, u32[]{:S(2)}) copy-start(bf16[1168,128]{1,0:T(8,128)(2,1)} %copy-done.9) | copy-start | bytes 897028
  20.2 5.7 %copy-start.8 = (bf16[1168,128]{1,0:T(8,128)(2,1)S(1)}, bf16[1168,128]{1,0:T(8,128)(2,1)}, u32[]{:S(2)}) copy-start(bf16[1168,128]{1,0:T(8,128)(2,1)} %copy-done.7) | copy-start | bytes 897028
  20.3 7.9 %copy-start.6 = (bf16[1168,128]{1,0:T(8,128)(2,1)S(1)}, bf16[1168,128]{1,0:T(8,128)(2,1)}, u32[]{:S(2)}) copy-start(bf16[1168,128]{1,0:T(8,128)(2,1)} %copy-done.5) | copy-start | bytes 897028
  23.5 21.9 %collective-permute-start.3 = (bf16[384,1024]{1,0:T(8,128)(2,1)S(1)}, bf16[384,1024]{1,0:T(8,128)(2,1)S(1)}, u32[]{:S(2)}, u32[]{:S(2)}) collective-permute-start(bf16[384,1024]{1,0:T(8,128)(2,1)S(1)} %collective-permute-done.o_ref), channel_id=1, source_target_pairs={{0,1},{1,2},{2,3},{3,0},{4,5},{5,6},{6,7},{7,4},{8,9},{9,10},{10,1... | collective-permute-start | bytes 2359304 | tf_op jit(solution)/shard_map/ppermute | solution.py:425
  24.0 11.0 %collective-permute-start.4 = (bf16[1168,128]{1,0:T(8,128)(2,1)S(1)}, bf16[1168,128]{1,0:T(8,128)(2,1)S(1)}, u32[]{:S(2)}, u32[]{:S(2)}) collective-permute-start(bf16[1168,128]{1,0:T(8,128)(2,1)S(1)} %copy-done.12), channel_id=1, source_target_pairs={{0,24},{4,28},{8,16},{12,20},{16,8},{20,12},{24,0},{28,4},{1,25},{... | collective-permute-start | bytes 897032 | tf_op jit(solution)/shard_map/ppermute | solution.py:422
  25.9 14.0 %collective-permute-start.5 = (bf16[1168,128]{1,0:T(8,128)(2,1)S(1)}, bf16[1168,128]{1,0:T(8,128)(2,1)S(1)}, u32[]{:S(2)}, u32[]{:S(2)}) collective-permute-start(bf16[1168,128]{1,0:T(8,128)(2,1)S(1)} %copy-done.10), channel_id=1, source_target_pairs={{0,28},{4,24},{8,20},{12,16},{16,12},{20,8},{24,4},{28,0},{1,29},{... | collective-permute-start | bytes 897032 | tf_op jit(solution)/shard_map/ppermute | solution.py:422
  26.0 19.5 %collective-permute-start.6 = (bf16[1168,128]{1,0:T(8,128)(2,1)S(1)}, bf16[1168,128]{1,0:T(8,128)(2,1)S(1)}, u32[]{:S(2)}, u32[]{:S(2)}) collective-permute-start(bf16[1168,128]{1,0:T(8,128)(2,1)S(1)} %copy-done.8), channel_id=1, source_target_pairs={{0,20},{4,16},{8,28},{12,24},{16,4},{20,0},{24,12},{28,8},{1,21},{... | collective-permute-start | bytes 897032 | tf_op jit(solution)/shard_map/ppermute | solution.py:422
  28.1 17.3 %collective-permute-start.7 = (bf16[1168,128]{1,0:T(8,128)(2,1)S(1)}, bf16[1168,128]{1,0:T(8,128)(2,1)S(1)}, u32[]{:S(2)}, u32[]{:S(2)}) collective-permute-start(bf16[1168,128]{1,0:T(8,128)(2,1)S(1)} %copy-done.6), channel_id=1, source_target_pairs={{0,12},{4,8},{8,4},{12,0},{16,28},{20,24},{24,20},{28,16},{1,13},{... | collective-permute-start | bytes 897032 | tf_op jit(solution)/shard_map/ppermute | solution.py:422
  35.0 10.4 %collective-permute-start.8 = (bf16[1168,128]{1,0:T(8,128)(2,1)S(1)}, bf16[1168,128]{1,0:T(8,128)(2,1)S(1)}, u32[]{:S(2)}, u32[]{:S(2)}) collective-permute-start(bf16[1168,128]{1,0:T(8,128)(2,1)S(1)} %get-tuple-element.66), channel_id=1, source_target_pairs={{0,4},{4,0},{8,12},{12,8},{16,20},{20,16},{24,28},{28,24},{1,5},{5... | collective-permute-start | bytes 897032 | tf_op jit(solution)/shard_map/ppermute | solution.py:422
  45.4 21.4 %collective-permute-start.9 = (bf16[384,1024]{1,0:T(8,128)(2,1)S(1)}, bf16[384,1024]{1,0:T(8,128)(2,1)S(1)}, u32[]{:S(2)}, u32[]{:S(2)}) collective-permute-start(bf16[384,1024]{1,0:T(8,128)(2,1)S(1)} %collective-permute-done.3.o_ref), channel_id=1, source_target_pairs={{0,1},{1,2},{2,3},{3,0},{4,5},{5,6},{6,7},{7,4},{8,9},{9,10},{10,1... | collective-permute-start | bytes 2359304 | tf_op jit(solution)/shard_map/ppermute | solution.py:425
  67.9 3.6 %collective-permute-start.10 = (bf16[384,128]{1,0:T(8,128)(2,1)S(1)}, bf16[384,128]{1,0:T(8,128)(2,1)S(1)}, u32[]{:S(2)}, u32[]{:S(2)}) collective-permute-start(bf16[384,128]{1,0:T(8,128)(2,1)S(1)} %get-tuple-element.96), channel_id=1, source_target_pairs={{0,4},{4,0},{8,12},{12,8},{16,20},{20,16},{24,28},{28,24},{1,5},{5... | collective-permute-start | bytes 294920 | tf_op jit(solution)/shard_map/ppermute | solution.py:422
  68.0 5.7 %collective-permute-start.11 = (bf16[384,128]{1,0:T(8,128)(2,1)S(1)}, bf16[384,128]{1,0:T(8,128)(2,1)S(1)}, u32[]{:S(2)}, u32[]{:S(2)}) collective-permute-start(bf16[384,128]{1,0:T(8,128)(2,1)S(1)} %get-tuple-element.97), channel_id=1, source_target_pairs={{0,8},{4,12},{8,0},{12,4},{16,24},{20,28},{24,16},{28,20},{1,9},{5... | collective-permute-start | bytes 294920 | tf_op jit(solution)/shard_map/ppermute | solution.py:422
  69.3 5.6 %collective-permute-start.12 = (bf16[384,128]{1,0:T(8,128)(2,1)S(1)}, bf16[384,128]{1,0:T(8,128)(2,1)S(1)}, u32[]{:S(2)}, u32[]{:S(2)}) collective-permute-start(bf16[384,128]{1,0:T(8,128)(2,1)S(1)} %get-tuple-element.98), channel_id=1, source_target_pairs={{0,12},{4,8},{8,4},{12,0},{16,28},{20,24},{24,20},{28,16},{1,13},{... | collective-permute-start | bytes 294920 | tf_op jit(solution)/shard_map/ppermute | solution.py:422
  69.8 5.6 %collective-permute-start.13 = (bf16[384,128]{1,0:T(8,128)(2,1)S(1)}, bf16[384,128]{1,0:T(8,128)(2,1)S(1)}, u32[]{:S(2)}, u32[]{:S(2)}) collective-permute-start(bf16[384,128]{1,0:T(8,128)(2,1)S(1)} %get-tuple-element.99), channel_id=1, source_target_pairs={{0,16},{4,20},{8,24},{12,28},{16,0},{20,4},{24,8},{28,12},{1,17},{... | collective-permute-start | bytes 294920 | tf_op jit(solution)/shard_map/ppermute | solution.py:422
  71.1 9.5 %collective-permute-start.14 = (bf16[384,128]{1,0:T(8,128)(2,1)S(1)}, bf16[384,128]{1,0:T(8,128)(2,1)S(1)}, u32[]{:S(2)}, u32[]{:S(2)}) collective-permute-start(bf16[384,128]{1,0:T(8,128)(2,1)S(1)} %get-tuple-element.100), channel_id=1, source_target_pairs={{0,20},{4,16},{8,28},{12,24},{16,4},{20,0},{24,12},{28,8},{1,21},{... | collective-permute-start | bytes 294920 | tf_op jit(solution)/shard_map/ppermute | solution.py:422
  71.5 9.1 %collective-permute-start.15 = (bf16[384,128]{1,0:T(8,128)(2,1)S(1)}, bf16[384,128]{1,0:T(8,128)(2,1)S(1)}, u32[]{:S(2)}, u32[]{:S(2)}) collective-permute-start(bf16[384,128]{1,0:T(8,128)(2,1)S(1)} %get-tuple-element.101), channel_id=1, source_target_pairs={{0,24},{4,28},{8,16},{12,20},{16,8},{20,12},{24,0},{28,4},{1,25},{... | collective-permute-start | bytes 294920 | tf_op jit(solution)/shard_map/ppermute | solution.py:422
  73.7 6.9 %collective-permute-start.16 = (bf16[384,128]{1,0:T(8,128)(2,1)S(1)}, bf16[384,128]{1,0:T(8,128)(2,1)S(1)}, u32[]{:S(2)}, u32[]{:S(2)}) collective-permute-start(bf16[384,128]{1,0:T(8,128)(2,1)S(1)} %get-tuple-element.102), channel_id=1, source_target_pairs={{0,28},{4,24},{8,20},{12,16},{16,12},{20,8},{24,4},{28,0},{1,29},{... | collective-permute-start | bytes 294920 | tf_op jit(solution)/shard_map/ppermute | solution.py:422
  95.1 4.0 %collective-permute-start.17 = (bf16[1152,128]{1,0:T(8,128)(2,1)S(1)}, bf16[1152,128]{1,0:T(8,128)(2,1)S(1)}, u32[]{:S(2)}, u32[]{:S(2)}) collective-permute-start(bf16[1152,128]{1,0:T(8,128)(2,1)S(1)} %get-tuple-element.104), channel_id=1, source_target_pairs={{0,4},{4,0},{8,12},{12,8},{16,20},{20,16},{24,28},{28,24},{1,5},{5... | collective-permute-start | bytes 884744 | tf_op jit(solution)/shard_map/ppermute | solution.py:422
  95.6 9.9 %collective-permute-start.18 = (bf16[1152,128]{1,0:T(8,128)(2,1)S(1)}, bf16[1152,128]{1,0:T(8,128)(2,1)S(1)}, u32[]{:S(2)}, u32[]{:S(2)}) collective-permute-start(bf16[1152,128]{1,0:T(8,128)(2,1)S(1)} %get-tuple-element.105), channel_id=1, source_target_pairs={{0,8},{4,12},{8,0},{12,4},{16,24},{20,28},{24,16},{28,20},{1,9},{5... | collective-permute-start | bytes 884744 | tf_op jit(solution)/shard_map/ppermute | solution.py:422
  96.9 13.7 %collective-permute-start.19 = (bf16[1152,128]{1,0:T(8,128)(2,1)S(1)}, bf16[1152,128]{1,0:T(8,128)(2,1)S(1)}, u32[]{:S(2)}, u32[]{:S(2)}) collective-permute-start(bf16[1152,128]{1,0:T(8,128)(2,1)S(1)} %get-tuple-element.106), channel_id=1, source_target_pairs={{0,12},{4,8},{8,4},{12,0},{16,28},{20,24},{24,20},{28,16},{1,13},{... | collective-permute-start | bytes 884744 | tf_op jit(solution)/shard_map/ppermute | solution.py:422
  97.1 13.5 %collective-permute-start.20 = (bf16[1152,128]{1,0:T(8,128)(2,1)S(1)}, bf16[1152,128]{1,0:T(8,128)(2,1)S(1)}, u32[]{:S(2)}, u32[]{:S(2)}) collective-permute-start(bf16[1152,128]{1,0:T(8,128)(2,1)S(1)} %get-tuple-element.107), channel_id=1, source_target_pairs={{0,16},{4,20},{8,24},{12,28},{16,0},{20,4},{24,8},{28,12},{1,17},{... | collective-permute-start | bytes 884744 | tf_op jit(solution)/shard_map/ppermute | solution.py:422
  98.4 27.0 %collective-permute-start.21 = (bf16[1152,128]{1,0:T(8,128)(2,1)S(1)}, bf16[1152,128]{1,0:T(8,128)(2,1)S(1)}, u32[]{:S(2)}, u32[]{:S(2)}) collective-permute-start(bf16[1152,128]{1,0:T(8,128)(2,1)S(1)} %get-tuple-element.108), channel_id=1, source_target_pairs={{0,20},{4,16},{8,28},{12,24},{16,4},{20,0},{24,12},{28,8},{1,21},{... | collective-permute-start | bytes 884744 | tf_op jit(solution)/shard_map/ppermute | solution.py:422
  99.1 26.2 %collective-permute-start.22 = (bf16[1152,128]{1,0:T(8,128)(2,1)S(1)}, bf16[1152,128]{1,0:T(8,128)(2,1)S(1)}, u32[]{:S(2)}, u32[]{:S(2)}) collective-permute-start(bf16[1152,128]{1,0:T(8,128)(2,1)S(1)} %get-tuple-element.109), channel_id=1, source_target_pairs={{0,24},{4,28},{8,16},{12,20},{16,8},{20,12},{24,0},{28,4},{1,25},{... | collective-permute-start | bytes 884744 | tf_op jit(solution)/shard_map/ppermute | solution.py:422
  105.5 19.9 %collective-permute-start.23 = (bf16[1152,128]{1,0:T(8,128)(2,1)S(1)}, bf16[1152,128]{1,0:T(8,128)(2,1)S(1)}, u32[]{:S(2)}, u32[]{:S(2)}) collective-permute-start(bf16[1152,128]{1,0:T(8,128)(2,1)S(1)} %get-tuple-element.110), channel_id=1, source_target_pairs={{0,28},{4,24},{8,20},{12,16},{16,12},{20,8},{24,4},{28,0},{1,29},{... | collective-permute-start | bytes 884744 | tf_op jit(solution)/shard_map/ppermute | solution.py:422

commit v9 on v8

--- a/solution.py
+++ b/solution.py
@@ -94,50 +94,55 @@
     )(me, *blocks)
 
 
-def project_kernel(first, o_ref, w_ref, *refs):
-    out_ref = refs[-1]
-    for pair in range(w_ref.shape[0] // (2 * HD)):
+def project_kernel(count, *refs):
+    features, weights, rest = refs[:count], refs[count:2 * count], refs[2 * count:]
+    out_ref = rest[-1]
+    for pair in range(out_ref.shape[1] // (2 * HD)):
         part = slice(pair * 2 * HD, (pair + 1) * 2 * HD)
-        both = dot32(o_ref[...], w_ref[part, :], NT)
-        out_ref[:, part] = both if first else refs[0][:, part] + both
-
-
-def project_last_kernel(me_s, o_ref, w_ref, acc_ref, *outs):
+        both = sum(dot32(o_ref[...], w_ref[part, :], NT) for o_ref, w_ref in zip(features, weights))
+        out_ref[:, part] = both if len(rest) == 1 else rest[0][:, part] + both
+
+
+def project_last_kernel(count, me_s, *refs):
+    features, weights, acc_ref, outs = refs[:count], refs[count:2 * count], refs[2 * count], refs[2 * count + 1:]
     pairs = len(outs) // 2
     odd = lax.rem(me_s[0], 2) == 1
     for j in range(pairs):
         part = aligned(lax.rem(me_s[0] // 2, pairs) ^ j, 2 * HD)
-        both = (acc_ref[:, part] + dot32(o_ref[...], w_ref[part, :], NT)).astype(jnp.bfloat16)
+        both = acc_ref[:, part]
+        for o_ref, w_ref in zip(features, weights):
+            both = both + dot32(o_ref[...], w_ref[part, :], NT)
+        both = both.astype(jnp.bfloat16)
         outs[2 * j][...] = jnp.where(odd, both[:, HD:], both[:, :HD])
         outs[2 * j + 1][...] = jnp.where(odd, both[:, :HD], both[:, HD:])
 
 
-def project(me, weight, features, acc, last):
-    rows, width = features.shape
-    columns = weight.shape[0]
-    heads = columns // HD
+def project(me, weights, features, acc, last):
+    rows, width = features[0].shape
+    columns = weights[0].shape[0]
+    heads, count = columns // HD, len(features)
     total = jax.ShapeDtypeStruct((rows, columns), jnp.float32)
     cost = pl.CostEstimate(
-        flops=2 * rows * width * columns,
-        bytes_accessed=2 * width * columns + 8 * rows * columns,
+        flops=2 * count * rows * width * columns,
+        bytes_accessed=2 * count * width * columns + 8 * rows * columns,
         transcendentals=0,
     )
+    operands = (*features, *weights) + (() if acc is None else (acc,))
     if last:
         return pl.pallas_call(
-            project_last_kernel,
-            in_specs=[SMEM_SPEC] + [VMEM_SPEC] * 3,
+            functools.partial(project_last_kernel, count),
+            in_specs=[SMEM_SPEC] + [VMEM_SPEC] * len(operands),
             out_specs=[VMEM_SPEC] * heads,
             out_shape=[jax.ShapeDtypeStruct((rows, HD), jnp.bfloat16)] * heads,
-            compiler_params=params([features, weight, total, total]),
+            compiler_params=params([*operands, total]),
             cost_estimate=cost,
-        )(me, features, weight, acc)
-    operands = (features, weight) + (() if acc is None else (acc,))
+        )(me, *operands)
     return pl.pallas_call(
-        functools.partial(project_kernel, acc is None),
+        functools.partial(project_kernel, count),
         in_specs=[VMEM_SPEC] * len(operands),
         out_specs=VMEM_SPEC,
         out_shape=total,
-        compiler_params=params([features, weight, total, total]),
+        compiler_params=params([*operands, total]),
         cost_estimate=cost,
     )(*operands)
 
@@ -421,8 +426,8 @@
     def exchange(x, d):
         return x if d == 0 else lax.ppermute(x, "seq", [(i, i ^ d) for i in range(peers)])
 
-    def pass_on(x):
-        return lax.ppermute(x, "head", [(i, (i + 1) % groups) for i in range(groups)])
+    def pass_on(x, way):
+        return lax.ppermute(x, "head", [(i, i + way) for i in range(groups) if 0 <= i + way < groups])
 
     order = [*range(2, peers, 2), *range(peers - 1, 0, -2)]
 
@@ -437,26 +442,29 @@
         return len(order) * step * (step + 1) // ((groups - 2) * (groups - 1))
 
     after = lax.optimization_barrier
-    features, acc = out_grad, None
     weights = []
     for step in range(groups):
         block = lax.rem(lax.axis_index("head") + groups - step, groups)
         weights.append(lax.dynamic_slice_in_dim(out_weight, block * width, width, 1))
+    features, acc = [out_grad, out_grad], None
     for step in range(groups):
         last = step == groups - 1
         if not last:
-            passed = pass_on(features)
+            passed = [pass_on(features[0], 1), pass_on(features[1], -1)]
         if step == groups - 2:
             received[0], features = after((received[0], features))
             state = list(attention_forward(me_vector, received, rows, heads))
             features, state[1] = after((features, state[1]))
-        acc = project(me_vector, weights[step], features, acc, last)
+        if step == 0:
+            acc = project(me_vector, weights[:1], features[:1], acc, last)
+        else:
+            acc = project(me_vector, [weights[step], weights[groups - step]], features, acc, last)
         if not last:
             features = passed
             if step < groups - 2:
                 batch = order[share(step):share(step + 1)]
                 here = [received[d] for d in batch]
-                features, acc, here, weights[2:] = after((features, acc, here, weights[2:]))
+                features, acc, here, weights[1:] = after((features, acc, here, weights[1:]))
                 for d, block in zip(batch, here):
                     received[d] = block
     grads = exchange_all(acc, peers)

time: 128 us -> 143 us (1.12)
  starting transfers between devices: 24.7 us -> 38.3 us
  Pallas kernels: 38.4 us -> 42.1 us
  local copies, waits for them, and re-layouts: 11.8 us -> 10 us
    ppermute x3 -> x6, starting transfers between devices: 4.43 us -> 16.9 us  [pass_on(): lax.ppermute(x, 'head', [(i, i + way) for i in range(groups) if 0 <= i +...]
    pallas_call x4, Pallas kernels: 4.08 us -> 6.51 us  [the longest x3 4.67 us: project(): pl.pallas_call(functools.partial(project_kernel, count), in_specs=[VMEM_S...]
    unnamed x26 -> x18, local copies, waits for them, and re-layouts: 6.98 us -> 5.51 us
    ppermute x3 -> x6, waiting for transfers between devices: 4.59 us -> 3.92 us  [pass_on(): lax.ppermute(x, 'head', [(i, i + way) for i in range(groups) if 0 <= i +...]
  transfers between devices with their start and end apart: 24 -> 27, of which waited for: 12 -> 12; matrix products, arithmetic and copies ran while one was open for 4% -> 3% of each run, Pallas kernels for 16% -> 16%
where the time goes in v9:
time: 143 us
  waiting for transfers between devices  51.2 us (36%)
  Pallas kernels  42.1 us (29%)
  starting transfers between devices  38.3 us (27%)
  local copies, waits for them, and re-layouts  10 us (7%)
    ppermute x21, waiting for transfers between devices, exchange(): lax.ppermute(x, 'seq', [(i, i ^ d) for i in range(peers)])  47.3 us
    ppermute x21, starting transfers between devices, exchange(): lax.ppermute(x, 'seq', [(i, i ^ d) for i in range(peers)])  21.4 us
    ppermute x6, starting transfers between devices, pass_on(): lax.ppermute(x, 'head', [(i, i + way) for i in range(groups) if 0 <= i +...  16.9 us
    pallas_call x1, Pallas kernels, attention_forward(): pl.pallas_call(functools.partial(forward_kernel, peers, heads, rows, bq,...  16.7 us
    pallas_call x1, Pallas kernels, attention_backward(): pl.pallas_call(functools.partial(backward_kernel, peers, heads, rows, bq,...  15.1 us
    unnamed x18, local copies, waits for them, and re-layouts  5.51 us
    pallas_call x3, Pallas kernels, project(): pl.pallas_call(functools.partial(project_kernel, count), in_specs=[VMEM_S...  4.67 us
    dynamic_slice x1, local copies, waits for them, and re-layouts, per_device(): lax.dynamic_slice_in_dim(out_weight, block * width, width, 1)  4.54 us
  transfers between devices with their start and end apart: 27, of which 12 were waited for; matrix products, arithmetic and copies ran while one was open for 3% of the time, Pallas kernels for 16%

profile of v9, /device:TPU:0, one launch (start us, length us, event | category | flops | bytes accessed | tf_op | source)
XLA Modules:
  0.0 142.5 jit_solution(3207676999634588317)
XLA Ops:
  0.6 5.0 %collective-permute-start = (bf16[384,1024]{1,0:T(8,128)(2,1)}, bf16[384,1024]{1,0:T(8,128)(2,1)S(1)}, u32[]{:S(2)}, u32[]{:S(2)}) collective-permute-start(bf16[384,1024]{1,0:T(8,128)(2,1)} %refs_0_.1), channel_id=1, source_target_pairs={{0,1},{1,2},{2,3},{4,5},{5,6},{6,7},{8,9},{9,10},{10,11},{12,13},{... | collective-permute-start | bytes 2359304 | tf_op jit(solution)/shard_map/ppermute | solution.py:430
  5.6 1.3 collective-permute-start.1
  6.9 1.1 copy-done
  8.1 1.1 copy-done.1
  9.2 1.1 copy-done.2
  10.3 0.7 copy-done.4
  11.0 1.7 %shard_map.85 = (bf16[1168,128]{1,0:T(8,128)(2,1)S(1)}, bf16[1168,128]{1,0:T(8,128)(2,1)S(1)}, bf16[1168,128]{1,0:T(8,128)(2,1)}, bf16[1168,128]{1,0:T(8,128)(2,...) custom-call(s32[1]{0:T(128)} %bitcast.me_s, ...), custom_call_target="tpu_custom_call" | custom-call | tf_op jit(solution)/shard_map/pallas_call | solution.py:68
  12.7 0.7 copy-done.5
  13.4 0.7 copy-done.7
  14.2 1.5 %collective-permute-start.2 = (bf16[1168,128]{1,0:T(8,128)(2,1)}, bf16[1168,128]{1,0:T(8,128)(2,1)S(1)}, u32[]{:S(2)}, u32[]{:S(2)}) collective-permute-start(bf16[1168,128]{1,0:T(8,128)(2,1)} %get-tuple-element.64), channel_id=1, source_target_pairs={{0,8},{4,12},{8,0},{12,4},{16,24},{20,28},{24,16},{28,20},{1,9},{5... | collective-permute-start | bytes 897032 | tf_op jit(solution)/shard_map/ppermute | solution.py:427
  15.7 1.5 %collective-permute-start.3 = (bf16[1168,128]{1,0:T(8,128)(2,1)}, bf16[1168,128]{1,0:T(8,128)(2,1)S(1)}, u32[]{:S(2)}, u32[]{:S(2)}) collective-permute-start(bf16[1168,128]{1,0:T(8,128)(2,1)} %get-tuple-element.65), channel_id=1, source_target_pairs={{0,16},{4,20},{8,24},{12,28},{16,0},{20,4},{24,8},{28,12},{1,17},{... | collective-permute-start | bytes 897032 | tf_op jit(solution)/shard_map/ppermute | solution.py:427
  17.2 4.5 %constant_dynamic-slice_fusion = (bf16[1024,1024]{1,0:T(8,128)(2,1)S(1)}, bf16[1024,1024]{1,0:T(8,128)(2,1)S(1)}, bf16[1024,1024]{1,0:T(8,128)(2,1)S(1)}, bf16[1024,1024]{1,0:T(8,128)(2,1)S(1)}) fusion(bf16[1024,4096]{1,0:T(8,128)(2,1)} %param.10, s32[]{:T(128)S(6)} %select_n.15, s32[]{:T(128)S(6)} %select_n.13, s32[]{:T(128)S(6)} %select_n.12, s32[]{:T(128)S(6)} %select_n.14), kind=kLoop, calls=%fused_computation | loop fusion | bytes 16777232 | tf_op jit(solution)/shard_map/dynamic_slice | solution.py:448
  21.7 1.0 shard_map.86.refs_4_
  22.9 1.2 collective-permute-done.3.refs_4_
  24.1 2.6 %collective-permute-done.1.refs_1_ = bf16[384,1024]{1,0:T(8,128)(2,1)S(1)} collective-permute-done((bf16[384,1024]{1,0:T(8,128)(2,1)}, bf16[384,1024]{1,0:T(8,128)(2,1)S(1)}, u32[]{:S(2)}, u32[]{:S(2)}) %collective-permute-start.1) | collective-permute-done | bytes 786464 | tf_op jit(solution)/shard_map/ppermute | solution.py:430
  26.7 3.5 %collective-permute-start.4 = (bf16[384,1024]{1,0:T(8,128)(2,1)S(1)}, bf16[384,1024]{1,0:T(8,128)(2,1)S(1)}, u32[]{:S(2)}, u32[]{:S(2)}) collective-permute-start(bf16[384,1024]{1,0:T(8,128)(2,1)S(1)} %collective-permute-done.refs_0_), channel_id=1, source_target_pairs={{0,1},{1,2},{2,3},{4,5},{5,6},{6,7},{8,9},{9,10},{10,11},{12,13},{... | collective-permute-start | bytes 2359304 | tf_op jit(solution)/shard_map/ppermute | solution.py:430
  30.2 1.3 collective-permute-start.5
  31.6 2.5 %collective-permute-start.6 = (bf16[1168,128]{1,0:T(8,128)(2,1)S(1)}, bf16[1168,128]{1,0:T(8,128)(2,1)S(1)}, u32[]{:S(2)}, u32[]{:S(2)}) collective-permute-start(bf16[1168,128]{1,0:T(8,128)(2,1)S(1)} %copy-done.6), channel_id=1, source_target_pairs={{0,24},{4,28},{8,16},{12,20},{16,8},{20,12},{24,0},{28,4},{1,25},{... | collective-permute-start | bytes 897032 | tf_op jit(solution)/shard_map/ppermute | solution.py:427
  34.1 0.2 collective-permute-start.7
  34.4 1.5 %collective-permute-start.8 = (bf16[1168,128]{1,0:T(8,128)(2,1)S(1)}, bf16[1168,128]{1,0:T(8,128)(2,1)S(1)}, u32[]{:S(2)}, u32[]{:S(2)}) collective-permute-start(bf16[1168,128]{1,0:T(8,128)(2,1)S(1)} %get-tuple-element.73), channel_id=1, source_target_pairs={{0,20},{4,16},{8,28},{12,24},{16,4},{20,0},{24,12},{28,8},{1,21},{... | collective-permute-start | bytes 897032 | tf_op jit(solution)/shard_map/ppermute | solution.py:427
  35.8 6.7 %collective-permute-done.6.refs_6_ = bf16[1168,128]{1,0:T(8,128)(2,1)S(1)} collective-permute-done((bf16[1168,128]{1,0:T(8,128)(2,1)S(1)}, bf16[1168,128]{1,0:T(8,128)(2,1)S(1)}, u32[]{:S(2)}, u32[]{:S(2)}) %collective-permute-start.6) | collective-permute-done | bytes 299040 | tf_op jit(solution)/shard_map/ppermute | solution.py:427
  42.8 1.8 %shard_map.87.refs_4_ = f32[384,1024]{1,0:T(8,128)S(1)} custom-call(bf16[384,1024]{1,0:T(8,128)(2,1)S(1)} %collective-permute-done.refs_0_, bf16[384,1024]{1,0:T(8,128)(2,1)S(1)} %collective-permute-done.1.refs_1_, bf16[1024,1024]{1,0:T(8,128)(2,1)S(1)} %get-tuple-element.102.refs_2_.refs_3_, bf16[1024,1024]{1,0:T(8,128)(2,1)S(1)} %get-tuple-element.101.refs_3_.refs_2_, ...), custom_call_target="tpu_custom_call" | custom-call | flops 1610612736 | bytes 7340032 | tf_op jit(solution)/shard_map/pallas_call | solution.py:140
  44.6 3.4 %collective-permute-done.7.refs_7_ = bf16[1168,128]{1,0:T(8,128)(2,1)S(1)} collective-permute-done((bf16[1168,128]{1,0:T(8,128)(2,1)S(1)}, bf16[1168,128]{1,0:T(8,128)(2,1)S(1)}, u32[]{:S(2)}, u32[]{:S(2)}) %collective-permute-start.7) | collective-permute-done | bytes 299040 | tf_op jit(solution)/shard_map/ppermute | solution.py:427
  48.0 6.7 %collective-permute-done.8.refs_5_ = bf16[1168,128]{1,0:T(8,128)(2,1)S(1)} collective-permute-done((bf16[1168,128]{1,0:T(8,128)(2,1)S(1)}, bf16[1168,128]{1,0:T(8,128)(2,1)S(1)}, u32[]{:S(2)}, u32[]{:S(2)}) %collective-permute-start.8) | collective-permute-done | bytes 299040 | tf_op jit(solution)/shard_map/ppermute | solution.py:427
  54.8 4.6 %collective-permute-start.11 = (bf16[384,1024]{1,0:T(8,128)(2,1)S(1)}, bf16[384,1024]{1,0:T(8,128)(2,1)S(1)}, u32[]{:S(2)}, u32[]{:S(2)}) collective-permute-start(bf16[384,1024]{1,0:T(8,128)(2,1)S(1)} %collective-permute-done.4.refs_0_), channel_id=1, source_target_pairs={{0,1},{1,2},{2,3},{4,5},{5,6},{6,7},{8,9},{9,10},{10,11},{12,13},{... | collective-permute-start | bytes 2359304 | tf_op jit(solution)/shard_map/ppermute | solution.py:430
  59.4 1.3 collective-permute-start.12
  60.7 16.7 %shard_map.88 = (bf16[3072,128]{1,0:T(8,128)(2,1)S(1)}, bf16[3072,256]{1,0:T(8,128)(2,1)S(1)}, bf16[3072,256]{1,0:T(8,128)(2,1)S(1)}, bf16[128,3072]{1,0:T(8,128...) custom-call(s32[1]{0:T(128)} %bitcast.me_s, ...), custom_call_target="tpu_custom_call" | custom-call | flops 1811939328 | bytes 6291456 | tf_op jit(solution)/shard_map/pallas_call | solution.py:383
  77.4 1.8 %shard_map.89.refs_4_ = f32[384,1024]{1,0:T(8,128)S(1)} custom-call(bf16[384,1024]{1,0:T(8,128)(2,1)S(1)} %collective-permute-done.4.refs_0_, bf16[384,1024]{1,0:T(8,128)(2,1)S(1)} %collective-permute-done.5.refs_1_, bf16[1024,1024]{1,0:T(8,128)(2,1)S(1)} %get-tuple-element.105.refs_2_.refs_3_, bf16[1024,1024]{1,0:T(8,128)(2,1)S(1)} %get-tuple-element.105.refs_2_.refs_3_, ...), custom_call_target="tpu_custom_call" | custom-call | flops 1610612736 | bytes 7340032 | tf_op jit(solution)/shard_map/pallas_call | solution.py:140
  79.2 1.3 collective-permute-done.12.refs_1_
  80.6 1.8 %shard_map.90 = (bf16[384,128]{1,0:T(8,128)(2,1)S(1)}, bf16[384,128]{1,0:T(8,128)(2,1)S(1)}, bf16[384,128]{1,0:T(8,128)(2,1)S(1)}, bf16[384,128]{1,0:T(8,128)(2,...) custom-call(s32[1]{0:T(128)} %bitcast.me_s, ...), custom_call_target="tpu_custom_call" | custom-call | flops 1610612736 | bytes 7340032 | tf_op jit(solution)/shard_map/pallas_call | solution.py:132
  82.5 1.6 %collective-permute-start.14 = (bf16[384,128]{1,0:T(8,128)(2,1)S(1)}, bf16[384,128]{1,0:T(8,128)(2,1)S(1)}, u32[]{:S(2)}, u32[]{:S(2)}) collective-permute-start(bf16[384,128]{1,0:T(8,128)(2,1)S(1)} %get-tuple-element.109), channel_id=1, source_target_pairs={{0,8},{4,12},{8,0},{12,4},{16,24},{20,28},{24,16},{28,20},{1,9},{5... | collective-permute-start | bytes 294920 | tf_op jit(solution)/shard_map/ppermute | solution.py:427
  84.0 0.3 collective-permute-start.15
  84.4 1.5 %collective-permute-start.16 = (bf16[384,128]{1,0:T(8,128)(2,1)S(1)}, bf16[384,128]{1,0:T(8,128)(2,1)S(1)}, u32[]{:S(2)}, u32[]{:S(2)}) collective-permute-start(bf16[384,128]{1,0:T(8,128)(2,1)S(1)} %get-tuple-element.111), channel_id=1, source_target_pairs={{0,16},{4,20},{8,24},{12,28},{16,0},{20,4},{24,8},{28,12},{1,17},{... | collective-permute-start | bytes 294920 | tf_op jit(solution)/shard_map/ppermute | solution.py:427
  86.1 2.4 %collective-permute-start.18 = (bf16[384,128]{1,0:T(8,128)(2,1)S(1)}, bf16[384,128]{1,0:T(8,128)(2,1)S(1)}, u32[]{:S(2)}, u32[]{:S(2)}) collective-permute-start(bf16[384,128]{1,0:T(8,128)(2,1)S(1)} %get-tuple-element.113), channel_id=1, source_target_pairs={{0,24},{4,28},{8,16},{12,20},{16,8},{20,12},{24,0},{28,4},{1,25},{... | collective-permute-start | bytes 294920 | tf_op jit(solution)/shard_map/ppermute | solution.py:427
  88.5 0.9 collective-permute-start.19
  89.4 0.5 collective-permute-done.16.refs_6_
  89.9 5.2 %collective-permute-done.17.refs_7_ = bf16[384,128]{1,0:T(8,128)(2,1)S(1)} collective-permute-done((bf16[384,128]{1,0:T(8,128)(2,1)S(1)}, bf16[384,128]{1,0:T(8,128)(2,1)S(1)}, u32[]{:S(2)}, u32[]{:S(2)}) %collective-permute-start.17) | collective-permute-done | bytes 98336 | tf_op jit(solution)/shard_map/ppermute | solution.py:427
  95.2 15.1 %shard_map.91 = (bf16[1152,128]{1,0:T(8,128)(2,1)S(1)}, bf16[1152,128]{1,0:T(8,128)(2,1)S(1)}, bf16[1152,128]{1,0:T(8,128)(2,1)S(1)}, bf16[1152,128]{1,0:T(8,128...) custom-call(s32[1]{0:T(128)} %bitcast.me_s, ...), custom_call_target="tpu_custom_call" | custom-call | flops 3019898880 | bytes 6291456 | tf_op jit(solution)/shard_map/pallas_call | solution.py:409
  110.3 0.4 collective-permute-start.20
  110.7 1.5 %collective-permute-start.21 = (bf16[1152,128]{1,0:T(8,128)(2,1)S(1)}, bf16[1152,128]{1,0:T(8,128)(2,1)S(1)}, u32[]{:S(2)}, u32[]{:S(2)}) collective-permute-start(bf16[1152,128]{1,0:T(8,128)(2,1)S(1)} %get-tuple-element.117), channel_id=1, source_target_pairs={{0,8},{4,12},{8,0},{12,4},{16,24},{20,28},{24,16},{28,20},{1,9},{5... | collective-permute-start | bytes 884744 | tf_op jit(solution)/shard_map/ppermute | solution.py:427
  112.2 1.5 %collective-permute-start.23 = (bf16[1152,128]{1,0:T(8,128)(2,1)S(1)}, bf16[1152,128]{1,0:T(8,128)(2,1)S(1)}, u32[]{:S(2)}, u32[]{:S(2)}) collective-permute-start(bf16[1152,128]{1,0:T(8,128)(2,1)S(1)} %get-tuple-element.119), channel_id=1, source_target_pairs={{0,16},{4,20},{8,24},{12,28},{16,0},{20,4},{24,8},{28,12},{1,17},{... | collective-permute-start | bytes 884744 | tf_op jit(solution)/shard_map/ppermute | solution.py:427
  113.7 0.5 collective-permute-start.24
  114.2 2.4 %collective-permute-start.25 = (bf16[1152,128]{1,0:T(8,128)(2,1)S(1)}, bf16[1152,128]{1,0:T(8,128)(2,1)S(1)}, u32[]{:S(2)}, u32[]{:S(2)}) collective-permute-start(bf16[1152,128]{1,0:T(8,128)(2,1)S(1)} %get-tuple-element.121), channel_id=1, source_target_pairs={{0,24},{4,28},{8,16},{12,20},{16,8},{20,12},{24,0},{28,4},{1,25},{... | collective-permute-start | bytes 884744 | tf_op jit(solution)/shard_map/ppermute | solution.py:427
  116.6 3.9 %collective-permute-done.21.refs_2_ = bf16[1152,128]{1,0:T(8,128)(2,1)S(1)} collective-permute-done((bf16[1152,128]{1,0:T(8,128)(2,1)S(1)}, bf16[1152,128]{1,0:T(8,128)(2,1)S(1)}, u32[]{:S(2)}, u32[]{:S(2)}) %collective-permute-start.21) | collective-permute-done | bytes 294944 | tf_op jit(solution)/shard_map/ppermute | solution.py:427
  120.5 0.5 collective-permute-start.26
  121.1 4.8 %collective-permute-done.22.refs_3_ = bf16[1152,128]{1,0:T(8,128)(2,1)S(1)} collective-permute-done((bf16[1152,128]{1,0:T(8,128)(2,1)S(1)}, bf16[1152,128]{1,0:T(8,128)(2,1)S(1)}, u32[]{:S(2)}, u32[]{:S(2)}) %collective-permute-start.22) | collective-permute-done | bytes 294944 | tf_op jit(solution)/shard_map/ppermute | solution.py:427
  125.9 14.6 %collective-permute-done.24.refs_5_ = bf16[1152,128]{1,0:T(8,128)(2,1)S(1)} collective-permute-done((bf16[1152,128]{1,0:T(8,128)(2,1)S(1)}, bf16[1152,128]{1,0:T(8,128)(2,1)S(1)}, u32[]{:S(2)}, u32[]{:S(2)}) %collective-permute-start.24) | collective-permute-done | bytes 294944 | tf_op jit(solution)/shard_map/ppermute | solution.py:427
  140.4 2.1 %shard_map.92 = (bf16[384,1024]{1,0:T(8,128)(2,1)}, bf16[384,1024]{1,0:T(8,128)(2,1)}, bf16[384,1024]{1,0:T(8,128)(2,1)}) custom-call(s32[1]{0:T(128)} %bitcast.me_s, bf16[1152,128]{1,0:T(8,128)(2,1)S(1)} %get-tuple-element.115.refs_0_, bf16[1152,128]{1,0:T(8,128)(2,1)S(1)} %collective-permute-done.20.refs_1_, ...), custom_call_target="tpu_custom_call" | custom-call | tf_op jit(solution)/shard_map/pallas_call | solution.py:88
  (33 shorter events, 0.8 us)
Async XLA Ops:
  0.6 23.5 %collective-permute-start = (bf16[384,1024]{1,0:T(8,128)(2,1)}, bf16[384,1024]{1,0:T(8,128)(2,1)S(1)}, u32[]{:S(2)}, u32[]{:S(2)}) collective-permute-start(bf16[384,1024]{1,0:T(8,128)(2,1)} %refs_0_.1), channel_id=1, source_target_pairs={{0,1},{1,2},{2,3},{4,5},{5,6},{6,7},{8,9},{9,10},{10,11},{12,13},{... | collective-permute-start | bytes 2359304 | tf_op jit(solution)/shard_map/ppermute | solution.py:430
  5.6 21.1 %collective-permute-start.1 = (bf16[384,1024]{1,0:T(8,128)(2,1)}, bf16[384,1024]{1,0:T(8,128)(2,1)S(1)}, u32[]{:S(2)}, u32[]{:S(2)}) collective-permute-start(bf16[384,1024]{1,0:T(8,128)(2,1)} %refs_0_.1), channel_id=1, source_target_pairs={{1,0},{2,1},{3,2},{5,4},{6,5},{7,6},{9,8},{10,9},{11,10},{13,12},{... | collective-permute-start | bytes 2359304 | tf_op jit(solution)/shard_map/ppermute | solution.py:430
  6.9 1.1 copy-start
  8.1 1.1 copy-start.1
  9.2 1.1 copy-start.2
  10.3 0.7 copy-start.4
  12.7 0.7 copy-start.5
  13.4 0.7 copy-start.7
  14.2 8.8 %collective-permute-start.2 = (bf16[1168,128]{1,0:T(8,128)(2,1)}, bf16[1168,128]{1,0:T(8,128)(2,1)S(1)}, u32[]{:S(2)}, u32[]{:S(2)}) collective-permute-start(bf16[1168,128]{1,0:T(8,128)(2,1)} %get-tuple-element.64), channel_id=1, source_target_pairs={{0,8},{4,12},{8,0},{12,4},{16,24},{20,28},{24,16},{28,20},{1,9},{5... | collective-permute-start | bytes 897032 | tf_op jit(solution)/shard_map/ppermute | solution.py:427
  15.7 8.5 %collective-permute-start.3 = (bf16[1168,128]{1,0:T(8,128)(2,1)}, bf16[1168,128]{1,0:T(8,128)(2,1)S(1)}, u32[]{:S(2)}, u32[]{:S(2)}) collective-permute-start(bf16[1168,128]{1,0:T(8,128)(2,1)} %get-tuple-element.65), channel_id=1, source_target_pairs={{0,16},{4,20},{8,24},{12,28},{16,0},{20,4},{24,8},{28,12},{1,17},{... | collective-permute-start | bytes 897032 | tf_op jit(solution)/shard_map/ppermute | solution.py:427
  17.2 4.5 %copy-start.3 = (bf16[384,1024]{1,0:T(8,128)(2,1)S(1)}, bf16[384,1024]{1,0:T(8,128)(2,1)}, u32[]{:S(2)}) copy-start(bf16[384,1024]{1,0:T(8,128)(2,1)} %refs_0_.1) | copy-start | bytes 2359300
  21.7 9.8 %copy-start.8 = (bf16[1168,128]{1,0:T(8,128)(2,1)S(1)}, bf16[1168,128]{1,0:T(8,128)(2,1)}, u32[]{:S(2)}) copy-start(bf16[1168,128]{1,0:T(8,128)(2,1)} %copy-done.7) | copy-start | bytes 897028
  21.7 9.9 %copy-start.6 = (bf16[1168,128]{1,0:T(8,128)(2,1)S(1)}, bf16[1168,128]{1,0:T(8,128)(2,1)}, u32[]{:S(2)}) copy-start(bf16[1168,128]{1,0:T(8,128)(2,1)} %copy-done.5) | copy-start | bytes 897028
  26.7 28.1 %collective-permute-start.4 = (bf16[384,1024]{1,0:T(8,128)(2,1)S(1)}, bf16[384,1024]{1,0:T(8,128)(2,1)S(1)}, u32[]{:S(2)}, u32[]{:S(2)}) collective-permute-start(bf16[384,1024]{1,0:T(8,128)(2,1)S(1)} %collective-permute-done.refs_0_), channel_id=1, source_target_pairs={{0,1},{1,2},{2,3},{4,5},{5,6},{6,7},{8,9},{9,10},{10,11},{12,13},{... | collective-permute-start | bytes 2359304 | tf_op jit(solution)/shard_map/ppermute | solution.py:430
  30.2 24.6 %collective-permute-start.5 = (bf16[384,1024]{1,0:T(8,128)(2,1)S(1)}, bf16[384,1024]{1,0:T(8,128)(2,1)S(1)}, u32[]{:S(2)}, u32[]{:S(2)}) collective-permute-start(bf16[384,1024]{1,0:T(8,128)(2,1)S(1)} %collective-permute-done.1.refs_1_), channel_id=1, source_target_pairs={{1,0},{2,1},{3,2},{5,4},{6,5},{7,6},{9,8},{10,9},{11,10},{13,12},{... | collective-permute-start | bytes 2359304 | tf_op jit(solution)/shard_map/ppermute | solution.py:430
  31.5 2.8 %collective-permute-start.10 = (bf16[1168,128]{1,0:T(8,128)(2,1)S(1)}, bf16[1168,128]{1,0:T(8,128)(2,1)S(1)}, u32[]{:S(2)}, u32[]{:S(2)}) collective-permute-start(bf16[1168,128]{1,0:T(8,128)(2,1)S(1)} %copy-done.8), channel_id=1, source_target_pairs={{0,4},{4,0},{8,12},{12,8},{16,20},{20,16},{24,28},{28,24},{1,5},{5... | collective-permute-start | bytes 897032 | tf_op jit(solution)/shard_map/ppermute | solution.py:427
  31.6 11.0 %collective-permute-start.6 = (bf16[1168,128]{1,0:T(8,128)(2,1)S(1)}, bf16[1168,128]{1,0:T(8,128)(2,1)S(1)}, u32[]{:S(2)}, u32[]{:S(2)}) collective-permute-start(bf16[1168,128]{1,0:T(8,128)(2,1)S(1)} %copy-done.6), channel_id=1, source_target_pairs={{0,24},{4,28},{8,16},{12,20},{16,8},{20,12},{24,0},{28,4},{1,25},{... | collective-permute-start | bytes 897032 | tf_op jit(solution)/shard_map/ppermute | solution.py:427
  34.1 13.9 %collective-permute-start.7 = (bf16[1168,128]{1,0:T(8,128)(2,1)S(1)}, bf16[1168,128]{1,0:T(8,128)(2,1)S(1)}, u32[]{:S(2)}, u32[]{:S(2)}) collective-permute-start(bf16[1168,128]{1,0:T(8,128)(2,1)S(1)} %get-tuple-element.72), channel_id=1, source_target_pairs={{0,28},{4,24},{8,20},{12,16},{16,12},{20,8},{24,4},{28,0},{1,29},{... | collective-permute-start | bytes 897032 | tf_op jit(solution)/shard_map/ppermute | solution.py:427
  34.4 20.4 %collective-permute-start.8 = (bf16[1168,128]{1,0:T(8,128)(2,1)S(1)}, bf16[1168,128]{1,0:T(8,128)(2,1)S(1)}, u32[]{:S(2)}, u32[]{:S(2)}) collective-permute-start(bf16[1168,128]{1,0:T(8,128)(2,1)S(1)} %get-tuple-element.73), channel_id=1, source_target_pairs={{0,20},{4,16},{8,28},{12,24},{16,4},{20,0},{24,12},{28,8},{1,21},{... | collective-permute-start | bytes 897032 | tf_op jit(solution)/shard_map/ppermute | solution.py:427
  42.6 12.2 %collective-permute-start.9 = (bf16[1168,128]{1,0:T(8,128)(2,1)S(1)}, bf16[1168,128]{1,0:T(8,128)(2,1)S(1)}, u32[]{:S(2)}, u32[]{:S(2)}) collective-permute-start(bf16[1168,128]{1,0:T(8,128)(2,1)S(1)} %get-tuple-element.74), channel_id=1, source_target_pairs={{0,12},{4,8},{8,4},{12,0},{16,28},{20,24},{24,20},{28,16},{1,13},{... | collective-permute-start | bytes 897032 | tf_op jit(solution)/shard_map/ppermute | solution.py:427
  54.8 24.4 %collective-permute-start.11 = (bf16[384,1024]{1,0:T(8,128)(2,1)S(1)}, bf16[384,1024]{1,0:T(8,128)(2,1)S(1)}, u32[]{:S(2)}, u32[]{:S(2)}) collective-permute-start(bf16[384,1024]{1,0:T(8,128)(2,1)S(1)} %collective-permute-done.4.refs_0_), channel_id=1, source_target_pairs={{0,1},{1,2},{2,3},{4,5},{5,6},{6,7},{8,9},{9,10},{10,11},{12,13},{... | collective-permute-start | bytes 2359304 | tf_op jit(solution)/shard_map/ppermute | solution.py:430
  59.4 21.2 %collective-permute-start.12 = (bf16[384,1024]{1,0:T(8,128)(2,1)S(1)}, bf16[384,1024]{1,0:T(8,128)(2,1)S(1)}, u32[]{:S(2)}, u32[]{:S(2)}) collective-permute-start(bf16[384,1024]{1,0:T(8,128)(2,1)S(1)} %collective-permute-done.5.refs_1_), channel_id=1, source_target_pairs={{1,0},{2,1},{3,2},{5,4},{6,5},{7,6},{9,8},{10,9},{11,10},{13,12},{... | collective-permute-start | bytes 2359304 | tf_op jit(solution)/shard_map/ppermute | solution.py:430
  82.4 3.6 %collective-permute-start.13 = (bf16[384,128]{1,0:T(8,128)(2,1)S(1)}, bf16[384,128]{1,0:T(8,128)(2,1)S(1)}, u32[]{:S(2)}, u32[]{:S(2)}) collective-permute-start(bf16[384,128]{1,0:T(8,128)(2,1)S(1)} %get-tuple-element.108), channel_id=1, source_target_pairs={{0,4},{4,0},{8,12},{12,8},{16,20},{20,16},{24,28},{28,24},{1,5},{5... | collective-permute-start | bytes 294920 | tf_op jit(solution)/shard_map/ppermute | solution.py:427
  82.5 6.0 %collective-permute-start.14 = (bf16[384,128]{1,0:T(8,128)(2,1)S(1)}, bf16[384,128]{1,0:T(8,128)(2,1)S(1)}, u32[]{:S(2)}, u32[]{:S(2)}) collective-permute-start(bf16[384,128]{1,0:T(8,128)(2,1)S(1)} %get-tuple-element.109), channel_id=1, source_target_pairs={{0,8},{4,12},{8,0},{12,4},{16,24},{20,28},{24,16},{28,20},{1,9},{5... | collective-permute-start | bytes 294920 | tf_op jit(solution)/shard_map/ppermute | solution.py:427
  84.0 5.4 %collective-permute-start.15 = (bf16[384,128]{1,0:T(8,128)(2,1)S(1)}, bf16[384,128]{1,0:T(8,128)(2,1)S(1)}, u32[]{:S(2)}, u32[]{:S(2)}) collective-permute-start(bf16[384,128]{1,0:T(8,128)(2,1)S(1)} %get-tuple-element.110), channel_id=1, source_target_pairs={{0,12},{4,8},{8,4},{12,0},{16,28},{20,24},{24,20},{28,16},{1,13},{... | collective-permute-start | bytes 294920 | tf_op jit(solution)/shard_map/ppermute | solution.py:427
  84.4 5.6 %collective-permute-start.16 = (bf16[384,128]{1,0:T(8,128)(2,1)S(1)}, bf16[384,128]{1,0:T(8,128)(2,1)S(1)}, u32[]{:S(2)}, u32[]{:S(2)}) collective-permute-start(bf16[384,128]{1,0:T(8,128)(2,1)S(1)} %get-tuple-element.111), channel_id=1, source_target_pairs={{0,16},{4,20},{8,24},{12,28},{16,0},{20,4},{24,8},{28,12},{1,17},{... | collective-permute-start | bytes 294920 | tf_op jit(solution)/shard_map/ppermute | solution.py:427
  85.9 9.3 %collective-permute-start.17 = (bf16[384,128]{1,0:T(8,128)(2,1)S(1)}, bf16[384,128]{1,0:T(8,128)(2,1)S(1)}, u32[]{:S(2)}, u32[]{:S(2)}) collective-permute-start(bf16[384,128]{1,0:T(8,128)(2,1)S(1)} %get-tuple-element.112), channel_id=1, source_target_pairs={{0,20},{4,16},{8,28},{12,24},{16,4},{20,0},{24,12},{28,8},{1,21},{... | collective-permute-start | bytes 294920 | tf_op jit(solution)/shard_map/ppermute | solution.py:427
  86.1 9.1 %collective-permute-start.18 = (bf16[384,128]{1,0:T(8,128)(2,1)S(1)}, bf16[384,128]{1,0:T(8,128)(2,1)S(1)}, u32[]{:S(2)}, u32[]{:S(2)}) collective-permute-start(bf16[384,128]{1,0:T(8,128)(2,1)S(1)} %get-tuple-element.113), channel_id=1, source_target_pairs={{0,24},{4,28},{8,16},{12,20},{16,8},{20,12},{24,0},{28,4},{1,25},{... | collective-permute-start | bytes 294920 | tf_op jit(solution)/shard_map/ppermute | solution.py:427
  88.5 6.7 %collective-permute-start.19 = (bf16[384,128]{1,0:T(8,128)(2,1)S(1)}, bf16[384,128]{1,0:T(8,128)(2,1)S(1)}, u32[]{:S(2)}, u32[]{:S(2)}) collective-permute-start(bf16[384,128]{1,0:T(8,128)(2,1)S(1)} %get-tuple-element.114), channel_id=1, source_target_pairs={{0,28},{4,24},{8,20},{12,16},{16,12},{20,8},{24,4},{28,0},{1,29},{... | collective-permute-start | bytes 294920 | tf_op jit(solution)/shard_map/ppermute | solution.py:427
  110.3 3.9 %collective-permute-start.20 = (bf16[1152,128]{1,0:T(8,128)(2,1)S(1)}, bf16[1152,128]{1,0:T(8,128)(2,1)S(1)}, u32[]{:S(2)}, u32[]{:S(2)}) collective-permute-start(bf16[1152,128]{1,0:T(8,128)(2,1)S(1)} %get-tuple-element.116), channel_id=1, source_target_pairs={{0,4},{4,0},{8,12},{12,8},{16,20},{20,16},{24,28},{28,24},{1,5},{5... | collective-permute-start | bytes 884744 | tf_op jit(solution)/shard_map/ppermute | solution.py:427
  110.7 9.9 %collective-permute-start.21 = (bf16[1152,128]{1,0:T(8,128)(2,1)S(1)}, bf16[1152,128]{1,0:T(8,128)(2,1)S(1)}, u32[]{:S(2)}, u32[]{:S(2)}) collective-permute-start(bf16[1152,128]{1,0:T(8,128)(2,1)S(1)} %get-tuple-element.117), channel_id=1, source_target_pairs={{0,8},{4,12},{8,0},{12,4},{16,24},{20,28},{24,16},{28,20},{1,9},{5... | collective-permute-start | bytes 884744 | tf_op jit(solution)/shard_map/ppermute | solution.py:427
  112.2 13.7 %collective-permute-start.22 = (bf16[1152,128]{1,0:T(8,128)(2,1)S(1)}, bf16[1152,128]{1,0:T(8,128)(2,1)S(1)}, u32[]{:S(2)}, u32[]{:S(2)}) collective-permute-start(bf16[1152,128]{1,0:T(8,128)(2,1)S(1)} %get-tuple-element.118), channel_id=1, source_target_pairs={{0,12},{4,8},{8,4},{12,0},{16,28},{20,24},{24,20},{28,16},{1,13},{... | collective-permute-start | bytes 884744 | tf_op jit(solution)/shard_map/ppermute | solution.py:427
  112.2 13.7 %collective-permute-start.23 = (bf16[1152,128]{1,0:T(8,128)(2,1)S(1)}, bf16[1152,128]{1,0:T(8,128)(2,1)S(1)}, u32[]{:S(2)}, u32[]{:S(2)}) collective-permute-start(bf16[1152,128]{1,0:T(8,128)(2,1)S(1)} %get-tuple-element.119), channel_id=1, source_target_pairs={{0,16},{4,20},{8,24},{12,28},{16,0},{20,4},{24,8},{28,12},{1,17},{... | collective-permute-start | bytes 884744 | tf_op jit(solution)/shard_map/ppermute | solution.py:427
  113.7 26.7 %collective-permute-start.24 = (bf16[1152,128]{1,0:T(8,128)(2,1)S(1)}, bf16[1152,128]{1,0:T(8,128)(2,1)S(1)}, u32[]{:S(2)}, u32[]{:S(2)}) collective-permute-start(bf16[1152,128]{1,0:T(8,128)(2,1)S(1)} %get-tuple-element.120), channel_id=1, source_target_pairs={{0,20},{4,16},{8,28},{12,24},{16,4},{20,0},{24,12},{28,8},{1,21},{... | collective-permute-start | bytes 884744 | tf_op jit(solution)/shard_map/ppermute | solution.py:427
  114.2 26.3 %collective-permute-start.25 = (bf16[1152,128]{1,0:T(8,128)(2,1)S(1)}, bf16[1152,128]{1,0:T(8,128)(2,1)S(1)}, u32[]{:S(2)}, u32[]{:S(2)}) collective-permute-start(bf16[1152,128]{1,0:T(8,128)(2,1)S(1)} %get-tuple-element.121), channel_id=1, source_target_pairs={{0,24},{4,28},{8,16},{12,20},{16,8},{20,12},{24,0},{28,4},{1,25},{... | collective-permute-start | bytes 884744 | tf_op jit(solution)/shard_map/ppermute | solution.py:427
  120.5 19.9 %collective-permute-start.26 = (bf16[1152,128]{1,0:T(8,128)(2,1)S(1)}, bf16[1152,128]{1,0:T(8,128)(2,1)S(1)}, u32[]{:S(2)}, u32[]{:S(2)}) collective-permute-start(bf16[1152,128]{1,0:T(8,128)(2,1)S(1)} %get-tuple-element.122), channel_id=1, source_target_pairs={{0,28},{4,24},{8,20},{12,16},{16,12},{20,8},{24,4},{28,0},{1,29},{... | collective-permute-start | bytes 884744 | tf_op jit(solution)/shard_map/ppermute | solution.py:427

commit v10 on v8

--- a/solution.py
+++ b/solution.py
@@ -12,6 +12,7 @@
 DOC_VALUES = 8
 DOC_ROWS = 16
 ONES_ROWS = 16
+STRIP = 64
 NEG_LARGE = -1e30
 VMEM_SPARE = 6 * 1024 * 1024
 LIST_BYTES = 16 * 1024 * 1024
@@ -250,27 +251,33 @@
     def early(now, qi, ki, buffer, diagonal):
         s_ref, top_ref = buffer
         keys, queries = aligned(ki, bk), aligned(qi, bq)
-        s = dot32(kx_ref[keys, :], qx_ref[queries, :], NT) * factor
-        if diagonal:
-            s = jnp.where(at_or_before(qi * bq, ki * bk, (bk, bq)), s, NEG_LARGE)
-        s_ref[...] = s
-        top_ref[...] = jnp.max(s, axis=0, keepdims=True)
+        top = jnp.full((8, bq), NEG_LARGE, jnp.float32)
+        for strip in range(0, bk, STRIP):
+            s = dot32(kx_ref[aligned(ki * (bk // STRIP) + strip // STRIP, STRIP), :], qx_ref[queries, :], NT)
+            s = s * factor
+            if diagonal:
+                s = jnp.where(at_or_before(qi * bq, ki * bk + strip, (STRIP, bq)), s, NEG_LARGE)
+            s_ref[strip:strip + STRIP, :] = s
+            top = jnp.maximum(top, jnp.max(s.reshape(STRIP // 8, 8, bq), axis=0))
+        top_ref[...] = jnp.max(top, axis=0, keepdims=True)
 
     def late(now, qi, ki, buffer):
         s_ref, top_ref = buffer
         keys, queries = aligned(ki, bk), aligned(qi, bq)
         top = log_ref[:, queries]
         new_top = jnp.maximum(top, top_ref[...])
-        p = jnp.exp2(s_ref[...] - new_top)
         fix = jnp.exp2(top - new_top)
-        high = p.astype(jnp.bfloat16)
         vt = vt_ref[:, keys]
-        sums = dot32(vt, high)
         if kept:
-            p_list[now] = high
+            for strip in range(0, bk, STRIP):
+                part = slice(strip, strip + STRIP)
+                p_list[now, part, :] = jnp.exp2(s_ref[part, :] - new_top).astype(jnp.bfloat16)
             top_list[now] = new_top
+            sums = dot32(vt, p_list[now])
         else:
-            sums = sums + dot32(vt, (p - high.astype(jnp.float32)).astype(jnp.bfloat16))
+            p = jnp.exp2(s_ref[...] - new_top)
+            high = p.astype(jnp.bfloat16)
+            sums = dot32(vt, high) + dot32(vt, (p - high.astype(jnp.float32)).astype(jnp.bfloat16))
         out_ref[:, queries] = out_ref[:, queries] * fix + sums[:HD, :]
         sum_ref[:, queries] = sum_ref[:, queries] * fix + sums[HD:HD + 1, :]
         log_ref[:, queries] = new_top
@@ -310,17 +317,22 @@
 
     def early(now, qi, ki, buffer, diagonal):
         p_ref, ds_ref = buffer
-        keys, queries = aligned(ki, bk), aligned(qi, bq)
-        log_row = log_ref[:, queries]
+        queries = aligned(qi, bq)
+        log_row, dot_row = log_ref[:, queries], dot_ref[:, queries]
         if kept:
-            p = p_list[now].astype(jnp.float32) * jnp.exp2(top_list[now] - log_row)
-        else:
-            p = jnp.exp2(dot32(kx_ref[keys, :], qx_ref[queries, :], NT) * factor - log_row)
-            if diagonal:
-                p = jnp.where(at_or_before(qi * bq, ki * bk, (bk, bq)), p, 0.0)
-        p_ref[...] = p.astype(jnp.bfloat16)
-        dp = dot32(v_ref[keys, :], g_ref[queries, :], NT)
-        ds_ref[...] = (p * (dp - dot_ref[:, queries])).astype(jnp.bfloat16)
+            share = jnp.exp2(top_list[now] - log_row)
+        for strip in range(0, bk, STRIP):
+            part = slice(strip, strip + STRIP)
+            keys = aligned(ki * (bk // STRIP) + strip // STRIP, STRIP)
+            if kept:
+                p = p_list[now, part, :].astype(jnp.float32) * share
+            else:
+                p = jnp.exp2(dot32(kx_ref[keys, :], qx_ref[queries, :], NT) * factor - log_row)
+                if diagonal:
+                    p = jnp.where(at_or_before(qi * bq, ki * bk + strip, (STRIP, bq)), p, 0.0)
+            p_ref[part, :] = p.astype(jnp.bfloat16)
+            dp = dot32(v_ref[keys, :], g_ref[queries, :], NT)
+            ds_ref[part, :] = (p * (dp - dot_row)).astype(jnp.bfloat16)
 
     def late(now, qi, ki, buffer):
         p_ref, ds_ref = buffer

time: 128 us -> 129 us (level); the launches traced: 127 us -> 127 us
  waiting for transfers between devices: 51.8 us -> 49.3 us
  Pallas kernels: 38.4 us -> 40.3 us
    ppermute x3, waiting for transfers between devices: 4.59 us -> 2.12 us  [pass_on(): lax.ppermute(x, 'head', [(i, (i + 1) % groups) for i in range(groups)])]
    pallas_call x1, Pallas kernels: 16 us -> 18.5 us  [attention_forward(): pl.pallas_call(functools.partial(forward_kernel, peers, heads, rows, bq,...]
  transfers between devices with their start and end apart: 24 -> 24, of which waited for: 12 -> 12; matrix products, arithmetic and copies ran while one was open for 4% -> 4% of each run, Pallas kernels for 16% -> 18%
where the time goes in v10:
time: 129 us; the launch traced here: 127 us
  waiting for transfers between devices  49.3 us (38%)
  Pallas kernels  40.3 us (31%)
  starting transfers between devices  24.7 us (19%)
  local copies, waits for them, and re-layouts  11.8 us (9%)
    ppermute x21, waiting for transfers between devices, exchange(): lax.ppermute(x, 'seq', [(i, i ^ d) for i in range(peers)])  47.2 us
    ppermute x21, starting transfers between devices, exchange(): lax.ppermute(x, 'seq', [(i, i ^ d) for i in range(peers)])  20.3 us
    pallas_call x1, Pallas kernels, attention_forward(): pl.pallas_call(functools.partial(forward_kernel, peers, heads, rows, bq,...  18.5 us
    pallas_call x1, Pallas kernels, attention_backward(): pl.pallas_call(functools.partial(backward_kernel, peers, heads, rows, bq,...  13.9 us
    unnamed x26, local copies, waits for them, and re-layouts  6.98 us
    dynamic_slice x1, local copies, waits for them, and re-layouts, per_device(): lax.dynamic_slice_in_dim(out_weight, block * width, width, 1)  4.79 us
    ppermute x3, starting transfers between devices, pass_on(): lax.ppermute(x, 'head', [(i, (i + 1) % groups) for i in range(groups)])  4.43 us
    pallas_call x3, Pallas kernels, project(): pl.pallas_call(functools.partial(project_kernel, acc is None), in_specs=[...  3.06 us
  transfers between devices with their start and end apart: 24, of which 12 were waited for; matrix products, arithmetic and copies ran while one was open for 4% of the time, Pallas kernels for 18%

profile of v10, /device:TPU:0, one launch (start us, length us, event | category | flops | bytes accessed | tf_op | source)
XLA Modules:
  0.0 126.9 jit_solution(15777594774826273596)
XLA Ops:
  0.6 3.1 %collective-permute-start = (bf16[384,1024]{1,0:T(8,128)(2,1)}, bf16[384,1024]{1,0:T(8,128)(2,1)S(1)}, u32[]{:S(2)}, u32[]{:S(2)}) collective-permute-start(bf16[384,1024]{1,0:T(8,128)(2,1)} %o_ref.1), channel_id=1, source_target_pairs={{0,1},{1,2},{2,3},{3,0},{4,5},{5,6},{6,7},{7,4},{8,9},{9,10},{10,1... | collective-permute-start | bytes 2359304 | tf_op jit(solution)/shard_map/ppermute | solution.py:437
  3.7 1.1 copy-done
  4.8 1.1 copy-done.1
  6.0 1.1 copy-done.2
  7.1 0.7 copy-done.4
  7.8 1.7 %shard_map.85 = (bf16[1168,128]{1,0:T(8,128)(2,1)S(1)}, bf16[1168,128]{1,0:T(8,128)(2,1)S(1)}, bf16[1168,128]{1,0:T(8,128)(2,1)}, bf16[1168,128]{1,0:T(8,128)(2,...) custom-call(s32[1]{0:T(128)} %bitcast.me_s, ...), custom_call_target="tpu_custom_call" | custom-call | tf_op jit(solution)/shard_map/pallas_call | solution.py:69
  9.5 0.7 copy-done.5
  10.2 0.7 copy-done.7
  10.9 0.7 copy-done.9
  11.7 0.7 copy-done.11
  12.4 1.5 %collective-permute-start.1 = (bf16[1168,128]{1,0:T(8,128)(2,1)}, bf16[1168,128]{1,0:T(8,128)(2,1)S(1)}, u32[]{:S(2)}, u32[]{:S(2)}) collective-permute-start(bf16[1168,128]{1,0:T(8,128)(2,1)} %get-tuple-element.58), channel_id=1, source_target_pairs={{0,8},{4,12},{8,0},{12,4},{16,24},{20,28},{24,16},{28,20},{1,9},{5... | collective-permute-start | bytes 897032 | tf_op jit(solution)/shard_map/ppermute | solution.py:434
  13.9 1.5 %collective-permute-start.2 = (bf16[1168,128]{1,0:T(8,128)(2,1)}, bf16[1168,128]{1,0:T(8,128)(2,1)S(1)}, u32[]{:S(2)}, u32[]{:S(2)}) collective-permute-start(bf16[1168,128]{1,0:T(8,128)(2,1)} %get-tuple-element.59), channel_id=1, source_target_pairs={{0,16},{4,20},{8,24},{12,28},{16,0},{20,4},{24,8},{28,12},{1,17},{... | collective-permute-start | bytes 897032 | tf_op jit(solution)/shard_map/ppermute | solution.py:434
  15.4 4.8 %constant_dynamic-slice_fusion = (bf16[1024,1024]{1,0:T(8,128)(2,1)S(1)}, bf16[1024,1024]{1,0:T(8,128)(2,1)S(1)}, bf16[1024,1024]{1,0:T(8,128)(2,1)S(1)}, bf16[1024,1024]{1,0:T(8,128)(2,1)S(1)}) fusion(bf16[1024,4096]{1,0:T(8,128)(2,1)} %param.10, s32[]{:T(128)S(6)} %select_n.15, s32[]{:T(128)S(6)} %select_n.13, s32[]{:T(128)S(6)} %select_n.12, s32[]{:T(128)S(6)} %select_n.14), kind=kLoop, calls=%fused_computation | loop fusion | bytes 16777232 | tf_op jit(solution)/shard_map/dynamic_slice | solution.py:456
  20.3 1.0 shard_map.86.refs_0_
  21.3 1.1 collective-permute-done.2.refs_4_
  22.4 1.1 collective-permute-done.o_ref
  23.5 0.5 collective-permute-start.3
  24.0 2.0 %collective-permute-start.4 = (bf16[1168,128]{1,0:T(8,128)(2,1)S(1)}, bf16[1168,128]{1,0:T(8,128)(2,1)S(1)}, u32[]{:S(2)}, u32[]{:S(2)}) collective-permute-start(bf16[1168,128]{1,0:T(8,128)(2,1)S(1)} %copy-done.12), channel_id=1, source_target_pairs={{0,24},{4,28},{8,16},{12,20},{16,8},{20,12},{24,0},{28,4},{1,25},{... | collective-permute-start | bytes 897032 | tf_op jit(solution)/shard_map/ppermute | solution.py:434
  26.0 2.2 %collective-permute-start.6 = (bf16[1168,128]{1,0:T(8,128)(2,1)S(1)}, bf16[1168,128]{1,0:T(8,128)(2,1)S(1)}, u32[]{:S(2)}, u32[]{:S(2)}) collective-permute-start(bf16[1168,128]{1,0:T(8,128)(2,1)S(1)} %copy-done.8), channel_id=1, source_target_pairs={{0,20},{4,16},{8,28},{12,24},{16,4},{20,0},{24,12},{28,8},{1,21},{... | collective-permute-start | bytes 897032 | tf_op jit(solution)/shard_map/ppermute | solution.py:434
  28.1 6.9 %collective-permute-done.4.refs_6_ = bf16[1168,128]{1,0:T(8,128)(2,1)S(1)} collective-permute-done((bf16[1168,128]{1,0:T(8,128)(2,1)S(1)}, bf16[1168,128]{1,0:T(8,128)(2,1)S(1)}, u32[]{:S(2)}, u32[]{:S(2)}) %collective-permute-start.4) | collective-permute-done | bytes 299040 | tf_op jit(solution)/shard_map/ppermute | solution.py:434
  35.0 1.0 shard_map.87.refs_0_
  36.0 3.9 %collective-permute-done.5.refs_7_ = bf16[1168,128]{1,0:T(8,128)(2,1)S(1)} collective-permute-done((bf16[1168,128]{1,0:T(8,128)(2,1)S(1)}, bf16[1168,128]{1,0:T(8,128)(2,1)S(1)}, u32[]{:S(2)}, u32[]{:S(2)}) %collective-permute-start.5) | collective-permute-done | bytes 299040 | tf_op jit(solution)/shard_map/ppermute | solution.py:434
  39.9 5.5 %collective-permute-done.6.refs_5_ = bf16[1168,128]{1,0:T(8,128)(2,1)S(1)} collective-permute-done((bf16[1168,128]{1,0:T(8,128)(2,1)S(1)}, bf16[1168,128]{1,0:T(8,128)(2,1)S(1)}, u32[]{:S(2)}, u32[]{:S(2)}) %collective-permute-start.6) | collective-permute-done | bytes 299040 | tf_op jit(solution)/shard_map/ppermute | solution.py:434
  45.4 0.9 collective-permute-start.9
  46.3 18.5 %shard_map.88 = (bf16[3072,128]{1,0:T(8,128)(2,1)S(1)}, bf16[3072,256]{1,0:T(8,128)(2,1)S(1)}, bf16[3072,256]{1,0:T(8,128)(2,1)S(1)}, bf16[128,3072]{1,0:T(8,128...) custom-call(s32[1]{0:T(128)} %bitcast.me_s, ...), custom_call_target="tpu_custom_call" | custom-call | flops 1811939328 | bytes 6291456 | tf_op jit(solution)/shard_map/pallas_call | solution.py:390
  64.8 1.0 shard_map.89.acc_ref
  65.8 1.0 collective-permute-done.9.o_ref
  66.9 1.0 shard_map.90
  68.0 1.3 %collective-permute-start.11 = (bf16[384,128]{1,0:T(8,128)(2,1)S(1)}, bf16[384,128]{1,0:T(8,128)(2,1)S(1)}, u32[]{:S(2)}, u32[]{:S(2)}) collective-permute-start(bf16[384,128]{1,0:T(8,128)(2,1)S(1)} %get-tuple-element.97), channel_id=1, source_target_pairs={{0,8},{4,12},{8,0},{12,4},{16,24},{20,28},{24,16},{28,20},{1,9},{5... | collective-permute-start | bytes 294920 | tf_op jit(solution)/shard_map/ppermute | solution.py:434
  69.3 0.6 collective-permute-start.12
  69.8 1.2 collective-permute-start.13
  71.1 0.4 collective-permute-start.14
  71.5 2.2 %collective-permute-start.15 = (bf16[384,128]{1,0:T(8,128)(2,1)S(1)}, bf16[384,128]{1,0:T(8,128)(2,1)S(1)}, u32[]{:S(2)}, u32[]{:S(2)}) collective-permute-start(bf16[384,128]{1,0:T(8,128)(2,1)S(1)} %get-tuple-element.101), channel_id=1, source_target_pairs={{0,24},{4,28},{8,16},{12,20},{16,8},{20,12},{24,0},{28,4},{1,25},{... | collective-permute-start | bytes 294920 | tf_op jit(solution)/shard_map/ppermute | solution.py:434
  73.7 0.9 collective-permute-start.16
  74.6 0.2 collective-permute-done.12.refs_5_
  74.8 0.6 collective-permute-done.13.refs_6_
  75.4 5.2 %collective-permute-done.14.refs_7_ = bf16[384,128]{1,0:T(8,128)(2,1)S(1)} collective-permute-done((bf16[384,128]{1,0:T(8,128)(2,1)S(1)}, bf16[384,128]{1,0:T(8,128)(2,1)S(1)}, u32[]{:S(2)}, u32[]{:S(2)}) %collective-permute-start.14) | collective-permute-done | bytes 98336 | tf_op jit(solution)/shard_map/ppermute | solution.py:434
  80.6 13.9 %shard_map.91 = (bf16[1152,128]{1,0:T(8,128)(2,1)S(1)}, bf16[1152,128]{1,0:T(8,128)(2,1)S(1)}, bf16[1152,128]{1,0:T(8,128)(2,1)S(1)}, bf16[1152,128]{1,0:T(8,128...) custom-call(s32[1]{0:T(128)} %bitcast.me_s, ...), custom_call_target="tpu_custom_call" | custom-call | flops 3019898880 | bytes 6291456 | tf_op jit(solution)/shard_map/pallas_call | solution.py:416
  94.6 0.5 collective-permute-start.17
  95.0 1.2 collective-permute-start.18
  96.3 0.2 collective-permute-start.19
  96.5 1.3 %collective-permute-start.20 = (bf16[1152,128]{1,0:T(8,128)(2,1)S(1)}, bf16[1152,128]{1,0:T(8,128)(2,1)S(1)}, u32[]{:S(2)}, u32[]{:S(2)}) collective-permute-start(bf16[1152,128]{1,0:T(8,128)(2,1)S(1)} %get-tuple-element.107), channel_id=1, source_target_pairs={{0,16},{4,20},{8,24},{12,28},{16,0},{20,4},{24,8},{28,12},{1,17},{... | collective-permute-start | bytes 884744 | tf_op jit(solution)/shard_map/ppermute | solution.py:434
  97.8 0.8 collective-permute-start.21
  98.6 2.2 %collective-permute-start.22 = (bf16[1152,128]{1,0:T(8,128)(2,1)S(1)}, bf16[1152,128]{1,0:T(8,128)(2,1)S(1)}, u32[]{:S(2)}, u32[]{:S(2)}) collective-permute-start(bf16[1152,128]{1,0:T(8,128)(2,1)S(1)} %get-tuple-element.109), channel_id=1, source_target_pairs={{0,24},{4,28},{8,16},{12,20},{16,8},{20,12},{24,0},{28,4},{1,25},{... | collective-permute-start | bytes 884744 | tf_op jit(solution)/shard_map/ppermute | solution.py:434
  100.7 4.2 %collective-permute-done.18.refs_2_ = bf16[1152,128]{1,0:T(8,128)(2,1)S(1)} collective-permute-done((bf16[1152,128]{1,0:T(8,128)(2,1)S(1)}, bf16[1152,128]{1,0:T(8,128)(2,1)S(1)}, u32[]{:S(2)}, u32[]{:S(2)}) %collective-permute-start.18) | collective-permute-done | bytes 294944 | tf_op jit(solution)/shard_map/ppermute | solution.py:434
  105.1 4.9 %collective-permute-done.19.refs_3_ = bf16[1152,128]{1,0:T(8,128)(2,1)S(1)} collective-permute-done((bf16[1152,128]{1,0:T(8,128)(2,1)S(1)}, bf16[1152,128]{1,0:T(8,128)(2,1)S(1)}, u32[]{:S(2)}, u32[]{:S(2)}) %collective-permute-start.19) | collective-permute-done | bytes 294944 | tf_op jit(solution)/shard_map/ppermute | solution.py:434
  110.0 14.8 %collective-permute-done.21.refs_5_ = bf16[1152,128]{1,0:T(8,128)(2,1)S(1)} collective-permute-done((bf16[1152,128]{1,0:T(8,128)(2,1)S(1)}, bf16[1152,128]{1,0:T(8,128)(2,1)S(1)}, u32[]{:S(2)}, u32[]{:S(2)}) %collective-permute-start.21) | collective-permute-done | bytes 294944 | tf_op jit(solution)/shard_map/ppermute | solution.py:434
  124.8 2.1 %shard_map.92 = (bf16[384,1024]{1,0:T(8,128)(2,1)}, bf16[384,1024]{1,0:T(8,128)(2,1)}, bf16[384,1024]{1,0:T(8,128)(2,1)}) custom-call(s32[1]{0:T(128)} %bitcast.me_s, bf16[1152,128]{1,0:T(8,128)(2,1)S(1)} %get-tuple-element.103.refs_0_, bf16[1152,128]{1,0:T(8,128)(2,1)S(1)} %collective-permute-done.17.refs_1_, ...), custom_call_target="tpu_custom_call" | custom-call | tf_op jit(solution)/shard_map/pallas_call | solution.py:89
  (35 shorter events, 0.3 us)
Async XLA Ops:
  0.6 22.9 %collective-permute-start = (bf16[384,1024]{1,0:T(8,128)(2,1)}, bf16[384,1024]{1,0:T(8,128)(2,1)S(1)}, u32[]{:S(2)}, u32[]{:S(2)}) collective-permute-start(bf16[384,1024]{1,0:T(8,128)(2,1)} %o_ref.1), channel_id=1, source_target_pairs={{0,1},{1,2},{2,3},{3,0},{4,5},{5,6},{6,7},{7,4},{8,9},{9,10},{10,1... | collective-permute-start | bytes 2359304 | tf_op jit(solution)/shard_map/ppermute | solution.py:437
  3.7 1.1 copy-start
  4.8 1.1 copy-start.1
  6.0 1.1 copy-start.2
  7.1 0.7 copy-start.4
  9.5 0.7 copy-start.5
  10.2 0.7 copy-start.7
  10.9 0.7 copy-start.9
  11.7 0.7 copy-start.11
  12.4 8.9 %collective-permute-start.1 = (bf16[1168,128]{1,0:T(8,128)(2,1)}, bf16[1168,128]{1,0:T(8,128)(2,1)S(1)}, u32[]{:S(2)}, u32[]{:S(2)}) collective-permute-start(bf16[1168,128]{1,0:T(8,128)(2,1)} %get-tuple-element.58), channel_id=1, source_target_pairs={{0,8},{4,12},{8,0},{12,4},{16,24},{20,28},{24,16},{28,20},{1,9},{5... | collective-permute-start | bytes 897032 | tf_op jit(solution)/shard_map/ppermute | solution.py:434
  13.9 8.5 %collective-permute-start.2 = (bf16[1168,128]{1,0:T(8,128)(2,1)}, bf16[1168,128]{1,0:T(8,128)(2,1)S(1)}, u32[]{:S(2)}, u32[]{:S(2)}) collective-permute-start(bf16[1168,128]{1,0:T(8,128)(2,1)} %get-tuple-element.59), channel_id=1, source_target_pairs={{0,16},{4,20},{8,24},{12,28},{16,0},{20,4},{24,8},{28,12},{1,17},{... | collective-permute-start | bytes 897032 | tf_op jit(solution)/shard_map/ppermute | solution.py:434
  15.4 4.8 %copy-start.3 = (bf16[384,1024]{1,0:T(8,128)(2,1)S(1)}, bf16[384,1024]{1,0:T(8,128)(2,1)}, u32[]{:S(2)}) copy-start(bf16[384,1024]{1,0:T(8,128)(2,1)} %o_ref.1) | copy-start | bytes 2359300
  20.2 3.7 %copy-start.12 = (bf16[1168,128]{1,0:T(8,128)(2,1)S(1)}, bf16[1168,128]{1,0:T(8,128)(2,1)}, u32[]{:S(2)}) copy-start(bf16[1168,128]{1,0:T(8,128)(2,1)} %copy-done.11) | copy-start | bytes 897028
  20.2 5.7 %copy-start.10 = (bf16[1168,128]{1,0:T(8,128)(2,1)S(1)}, bf16[1168,128]{1,0:T(8,128)(2,1)}, u32[]{:S(2)}) copy-start(bf16[1168,128]{1,0:T(8,128)(2,1)} %copy-done.9) | copy-start | bytes 897028
  20.2 5.7 %copy-start.8 = (bf16[1168,128]{1,0:T(8,128)(2,1)S(1)}, bf16[1168,128]{1,0:T(8,128)(2,1)}, u32[]{:S(2)}) copy-start(bf16[1168,128]{1,0:T(8,128)(2,1)} %copy-done.7) | copy-start | bytes 897028
  20.3 7.9 %copy-start.6 = (bf16[1168,128]{1,0:T(8,128)(2,1)S(1)}, bf16[1168,128]{1,0:T(8,128)(2,1)}, u32[]{:S(2)}) copy-start(bf16[1168,128]{1,0:T(8,128)(2,1)} %copy-done.5) | copy-start | bytes 897028
  23.5 21.9 %collective-permute-start.3 = (bf16[384,1024]{1,0:T(8,128)(2,1)S(1)}, bf16[384,1024]{1,0:T(8,128)(2,1)S(1)}, u32[]{:S(2)}, u32[]{:S(2)}) collective-permute-start(bf16[384,1024]{1,0:T(8,128)(2,1)S(1)} %collective-permute-done.o_ref), channel_id=1, source_target_pairs={{0,1},{1,2},{2,3},{3,0},{4,5},{5,6},{6,7},{7,4},{8,9},{9,10},{10,1... | collective-permute-start | bytes 2359304 | tf_op jit(solution)/shard_map/ppermute | solution.py:437
  24.0 11.0 %collective-permute-start.4 = (bf16[1168,128]{1,0:T(8,128)(2,1)S(1)}, bf16[1168,128]{1,0:T(8,128)(2,1)S(1)}, u32[]{:S(2)}, u32[]{:S(2)}) collective-permute-start(bf16[1168,128]{1,0:T(8,128)(2,1)S(1)} %copy-done.12), channel_id=1, source_target_pairs={{0,24},{4,28},{8,16},{12,20},{16,8},{20,12},{24,0},{28,4},{1,25},{... | collective-permute-start | bytes 897032 | tf_op jit(solution)/shard_map/ppermute | solution.py:434
  25.9 14.0 %collective-permute-start.5 = (bf16[1168,128]{1,0:T(8,128)(2,1)S(1)}, bf16[1168,128]{1,0:T(8,128)(2,1)S(1)}, u32[]{:S(2)}, u32[]{:S(2)}) collective-permute-start(bf16[1168,128]{1,0:T(8,128)(2,1)S(1)} %copy-done.10), channel_id=1, source_target_pairs={{0,28},{4,24},{8,20},{12,16},{16,12},{20,8},{24,4},{28,0},{1,29},{... | collective-permute-start | bytes 897032 | tf_op jit(solution)/shard_map/ppermute | solution.py:434
  26.0 19.5 %collective-permute-start.6 = (bf16[1168,128]{1,0:T(8,128)(2,1)S(1)}, bf16[1168,128]{1,0:T(8,128)(2,1)S(1)}, u32[]{:S(2)}, u32[]{:S(2)}) collective-permute-start(bf16[1168,128]{1,0:T(8,128)(2,1)S(1)} %copy-done.8), channel_id=1, source_target_pairs={{0,20},{4,16},{8,28},{12,24},{16,4},{20,0},{24,12},{28,8},{1,21},{... | collective-permute-start | bytes 897032 | tf_op jit(solution)/shard_map/ppermute | solution.py:434
  28.1 17.3 %collective-permute-start.7 = (bf16[1168,128]{1,0:T(8,128)(2,1)S(1)}, bf16[1168,128]{1,0:T(8,128)(2,1)S(1)}, u32[]{:S(2)}, u32[]{:S(2)}) collective-permute-start(bf16[1168,128]{1,0:T(8,128)(2,1)S(1)} %copy-done.6), channel_id=1, source_target_pairs={{0,12},{4,8},{8,4},{12,0},{16,28},{20,24},{24,20},{28,16},{1,13},{... | collective-permute-start | bytes 897032 | tf_op jit(solution)/shard_map/ppermute | solution.py:434
  35.0 10.4 %collective-permute-start.8 = (bf16[1168,128]{1,0:T(8,128)(2,1)S(1)}, bf16[1168,128]{1,0:T(8,128)(2,1)S(1)}, u32[]{:S(2)}, u32[]{:S(2)}) collective-permute-start(bf16[1168,128]{1,0:T(8,128)(2,1)S(1)} %get-tuple-element.66), channel_id=1, source_target_pairs={{0,4},{4,0},{8,12},{12,8},{16,20},{20,16},{24,28},{28,24},{1,5},{5... | collective-permute-start | bytes 897032 | tf_op jit(solution)/shard_map/ppermute | solution.py:434
  45.4 21.4 %collective-permute-start.9 = (bf16[384,1024]{1,0:T(8,128)(2,1)S(1)}, bf16[384,1024]{1,0:T(8,128)(2,1)S(1)}, u32[]{:S(2)}, u32[]{:S(2)}) collective-permute-start(bf16[384,1024]{1,0:T(8,128)(2,1)S(1)} %collective-permute-done.3.o_ref), channel_id=1, source_target_pairs={{0,1},{1,2},{2,3},{3,0},{4,5},{5,6},{6,7},{7,4},{8,9},{9,10},{10,1... | collective-permute-start | bytes 2359304 | tf_op jit(solution)/shard_map/ppermute | solution.py:437
  67.9 3.6 %collective-permute-start.10 = (bf16[384,128]{1,0:T(8,128)(2,1)S(1)}, bf16[384,128]{1,0:T(8,128)(2,1)S(1)}, u32[]{:S(2)}, u32[]{:S(2)}) collective-permute-start(bf16[384,128]{1,0:T(8,128)(2,1)S(1)} %get-tuple-element.96), channel_id=1, source_target_pairs={{0,4},{4,0},{8,12},{12,8},{16,20},{20,16},{24,28},{28,24},{1,5},{5... | collective-permute-start | bytes 294920 | tf_op jit(solution)/shard_map/ppermute | solution.py:434
  68.0 5.7 %collective-permute-start.11 = (bf16[384,128]{1,0:T(8,128)(2,1)S(1)}, bf16[384,128]{1,0:T(8,128)(2,1)S(1)}, u32[]{:S(2)}, u32[]{:S(2)}) collective-permute-start(bf16[384,128]{1,0:T(8,128)(2,1)S(1)} %get-tuple-element.97), channel_id=1, source_target_pairs={{0,8},{4,12},{8,0},{12,4},{16,24},{20,28},{24,16},{28,20},{1,9},{5... | collective-permute-start | bytes 294920 | tf_op jit(solution)/shard_map/ppermute | solution.py:434
  69.3 5.6 %collective-permute-start.12 = (bf16[384,128]{1,0:T(8,128)(2,1)S(1)}, bf16[384,128]{1,0:T(8,128)(2,1)S(1)}, u32[]{:S(2)}, u32[]{:S(2)}) collective-permute-start(bf16[384,128]{1,0:T(8,128)(2,1)S(1)} %get-tuple-element.98), channel_id=1, source_target_pairs={{0,12},{4,8},{8,4},{12,0},{16,28},{20,24},{24,20},{28,16},{1,13},{... | collective-permute-start | bytes 294920 | tf_op jit(solution)/shard_map/ppermute | solution.py:434
  69.8 5.6 %collective-permute-start.13 = (bf16[384,128]{1,0:T(8,128)(2,1)S(1)}, bf16[384,128]{1,0:T(8,128)(2,1)S(1)}, u32[]{:S(2)}, u32[]{:S(2)}) collective-permute-start(bf16[384,128]{1,0:T(8,128)(2,1)S(1)} %get-tuple-element.99), channel_id=1, source_target_pairs={{0,16},{4,20},{8,24},{12,28},{16,0},{20,4},{24,8},{28,12},{1,17},{... | collective-permute-start | bytes 294920 | tf_op jit(solution)/shard_map/ppermute | solution.py:434
  71.1 9.5 %collective-permute-start.14 = (bf16[384,128]{1,0:T(8,128)(2,1)S(1)}, bf16[384,128]{1,0:T(8,128)(2,1)S(1)}, u32[]{:S(2)}, u32[]{:S(2)}) collective-permute-start(bf16[384,128]{1,0:T(8,128)(2,1)S(1)} %get-tuple-element.100), channel_id=1, source_target_pairs={{0,20},{4,16},{8,28},{12,24},{16,4},{20,0},{24,12},{28,8},{1,21},{... | collective-permute-start | bytes 294920 | tf_op jit(solution)/shard_map/ppermute | solution.py:434
  71.5 9.1 %collective-permute-start.15 = (bf16[384,128]{1,0:T(8,128)(2,1)S(1)}, bf16[384,128]{1,0:T(8,128)(2,1)S(1)}, u32[]{:S(2)}, u32[]{:S(2)}) collective-permute-start(bf16[384,128]{1,0:T(8,128)(2,1)S(1)} %get-tuple-element.101), channel_id=1, source_target_pairs={{0,24},{4,28},{8,16},{12,20},{16,8},{20,12},{24,0},{28,4},{1,25},{... | collective-permute-start | bytes 294920 | tf_op jit(solution)/shard_map/ppermute | solution.py:434
  73.7 6.9 %collective-permute-start.16 = (bf16[384,128]{1,0:T(8,128)(2,1)S(1)}, bf16[384,128]{1,0:T(8,128)(2,1)S(1)}, u32[]{:S(2)}, u32[]{:S(2)}) collective-permute-start(bf16[384,128]{1,0:T(8,128)(2,1)S(1)} %get-tuple-element.102), channel_id=1, source_target_pairs={{0,28},{4,24},{8,20},{12,16},{16,12},{20,8},{24,4},{28,0},{1,29},{... | collective-permute-start | bytes 294920 | tf_op jit(solution)/shard_map/ppermute | solution.py:434
  94.6 4.0 %collective-permute-start.17 = (bf16[1152,128]{1,0:T(8,128)(2,1)S(1)}, bf16[1152,128]{1,0:T(8,128)(2,1)S(1)}, u32[]{:S(2)}, u32[]{:S(2)}) collective-permute-start(bf16[1152,128]{1,0:T(8,128)(2,1)S(1)} %get-tuple-element.104), channel_id=1, source_target_pairs={{0,4},{4,0},{8,12},{12,8},{16,20},{20,16},{24,28},{28,24},{1,5},{5... | collective-permute-start | bytes 884744 | tf_op jit(solution)/shard_map/ppermute | solution.py:434
  95.0 9.9 %collective-permute-start.18 = (bf16[1152,128]{1,0:T(8,128)(2,1)S(1)}, bf16[1152,128]{1,0:T(8,128)(2,1)S(1)}, u32[]{:S(2)}, u32[]{:S(2)}) collective-permute-start(bf16[1152,128]{1,0:T(8,128)(2,1)S(1)} %get-tuple-element.105), channel_id=1, source_target_pairs={{0,8},{4,12},{8,0},{12,4},{16,24},{20,28},{24,16},{28,20},{1,9},{5... | collective-permute-start | bytes 884744 | tf_op jit(solution)/shard_map/ppermute | solution.py:434
  96.3 13.7 %collective-permute-start.19 = (bf16[1152,128]{1,0:T(8,128)(2,1)S(1)}, bf16[1152,128]{1,0:T(8,128)(2,1)S(1)}, u32[]{:S(2)}, u32[]{:S(2)}) collective-permute-start(bf16[1152,128]{1,0:T(8,128)(2,1)S(1)} %get-tuple-element.106), channel_id=1, source_target_pairs={{0,12},{4,8},{8,4},{12,0},{16,28},{20,24},{24,20},{28,16},{1,13},{... | collective-permute-start | bytes 884744 | tf_op jit(solution)/shard_map/ppermute | solution.py:434
  96.5 13.5 %collective-permute-start.20 = (bf16[1152,128]{1,0:T(8,128)(2,1)S(1)}, bf16[1152,128]{1,0:T(8,128)(2,1)S(1)}, u32[]{:S(2)}, u32[]{:S(2)}) collective-permute-start(bf16[1152,128]{1,0:T(8,128)(2,1)S(1)} %get-tuple-element.107), channel_id=1, source_target_pairs={{0,16},{4,20},{8,24},{12,28},{16,0},{20,4},{24,8},{28,12},{1,17},{... | collective-permute-start | bytes 884744 | tf_op jit(solution)/shard_map/ppermute | solution.py:434
  97.8 27.0 %collective-permute-start.21 = (bf16[1152,128]{1,0:T(8,128)(2,1)S(1)}, bf16[1152,128]{1,0:T(8,128)(2,1)S(1)}, u32[]{:S(2)}, u32[]{:S(2)}) collective-permute-start(bf16[1152,128]{1,0:T(8,128)(2,1)S(1)} %get-tuple-element.108), channel_id=1, source_target_pairs={{0,20},{4,16},{8,28},{12,24},{16,4},{20,0},{24,12},{28,8},{1,21},{... | collective-permute-start | bytes 884744 | tf_op jit(solution)/shard_map/ppermute | solution.py:434
  98.6 26.2 %collective-permute-start.22 = (bf16[1152,128]{1,0:T(8,128)(2,1)S(1)}, bf16[1152,128]{1,0:T(8,128)(2,1)S(1)}, u32[]{:S(2)}, u32[]{:S(2)}) collective-permute-start(bf16[1152,128]{1,0:T(8,128)(2,1)S(1)} %get-tuple-element.109), channel_id=1, source_target_pairs={{0,24},{4,28},{8,16},{12,20},{16,8},{20,12},{24,0},{28,4},{1,25},{... | collective-permute-start | bytes 884744 | tf_op jit(solution)/shard_map/ppermute | solution.py:434
  104.9 19.9 %collective-permute-start.23 = (bf16[1152,128]{1,0:T(8,128)(2,1)S(1)}, bf16[1152,128]{1,0:T(8,128)(2,1)S(1)}, u32[]{:S(2)}, u32[]{:S(2)}) collective-permute-start(bf16[1152,128]{1,0:T(8,128)(2,1)S(1)} %get-tuple-element.110), channel_id=1, source_target_pairs={{0,28},{4,24},{8,20},{12,16},{16,12},{20,8},{24,4},{28,0},{1,29},{... | collective-permute-start | bytes 884744 | tf_op jit(solution)/shard_map/ppermute | solution.py:434

commit v11 on v10

--- a/solution.py
+++ b/solution.py
@@ -76,18 +76,19 @@
     )(me, q, k, v, doc_ids.reshape(rows // HD, HD))
 
 
-def unpack_kernel(heads, rows, me_s, *refs):
+def unpack_kernel(listed, rows, me_s, *refs):
+    heads = len(listed)
     own = lax.rem(me_s[0], heads)
-    for d in range(heads):
+    for d, block in zip(listed, refs):
         columns = aligned(own ^ d, HD)
         for part in range(3):
-            refs[heads + part][:, columns] = refs[d][part * rows:(part + 1) * rows, :]
-
-
-def unpack_heads(me, blocks, rows):
+            refs[heads + part][:, columns] = block[part * rows:(part + 1) * rows, :]
+
+
+def unpack_heads(me, listed, blocks, rows):
     heads = len(blocks)
     return pl.pallas_call(
-        functools.partial(unpack_kernel, heads, rows),
+        functools.partial(unpack_kernel, listed, rows),
         in_specs=[SMEM_SPEC] + [VMEM_SPEC] * heads,
         out_specs=[VMEM_SPEC] * 3,
         out_shape=[jax.ShapeDtypeStruct((rows, heads * HD), blocks[0].dtype)] * 3,
@@ -230,13 +231,16 @@
         before = jnp.sum((docs < value).astype(jnp.float32))
         first = jnp.where(docs >= value, before, first)
     first = first.astype(jnp.int32)
-    lows = [jnp.min(first[:, qi * bq:(qi + 1) * bq]) for qi in range(total // bq)]
-    fill_plan(lows, total, bq, bk, None, own_q, own_k, own_count)
+    back_q, back_k = block_sizes(total)[1]
+    lows = [jnp.min(first[:, qi * back_q:(qi + 1) * back_q]) for qi in range(total // back_q)]
     group = (me // heads) * heads * rows
     own = None if heads == peers else (group, group + heads * rows)
-    back_q, back_k = block_sizes(total)[1]
-    lows = [jnp.min(first[:, qi * back_q:(qi + 1) * back_q]) for qi in range(total // back_q)]
     fill_plan(lows, total, back_q, back_k, own, plan_q, plan_k, count_ref)
+    if kept:
+        own_q, own_k, own_count = plan_q, plan_k, count_ref
+    else:
+        lows = [jnp.min(first[:, qi * bq:(qi + 1) * bq]) for qi in range(total // bq)]
+        fill_plan(lows, total, bq, bk, None, own_q, own_k, own_count)
     same = lax.broadcasted_iota(jnp.int32, (HD, total), 0).astype(jnp.float32) == docs
     ones = jnp.where(same, 1.0, 0.0).astype(jnp.bfloat16).T
     kx_ref[:, HD:] = ones
@@ -251,15 +255,11 @@
     def early(now, qi, ki, buffer, diagonal):
         s_ref, top_ref = buffer
         keys, queries = aligned(ki, bk), aligned(qi, bq)
-        top = jnp.full((8, bq), NEG_LARGE, jnp.float32)
-        for strip in range(0, bk, STRIP):
-            s = dot32(kx_ref[aligned(ki * (bk // STRIP) + strip // STRIP, STRIP), :], qx_ref[queries, :], NT)
-            s = s * factor
-            if diagonal:
-                s = jnp.where(at_or_before(qi * bq, ki * bk + strip, (STRIP, bq)), s, NEG_LARGE)
-            s_ref[strip:strip + STRIP, :] = s
-            top = jnp.maximum(top, jnp.max(s.reshape(STRIP // 8, 8, bq), axis=0))
-        top_ref[...] = jnp.max(top, axis=0, keepdims=True)
+        s = dot32(kx_ref[keys, :], qx_ref[queries, :], NT) * factor
+        if diagonal:
+            s = jnp.where(at_or_before(qi * bq, ki * bk, (bk, bq)), s, NEG_LARGE)
+        s_ref[...] = s
+        top_ref[...] = jnp.max(s, axis=0, keepdims=True)
 
     def late(now, qi, ki, buffer):
         s_ref, top_ref = buffer
@@ -268,16 +268,14 @@
         new_top = jnp.maximum(top, top_ref[...])
         fix = jnp.exp2(top - new_top)
         vt = vt_ref[:, keys]
+        p = jnp.exp2(s_ref[...] - new_top)
+        high = p.astype(jnp.bfloat16)
+        sums = dot32(vt, high)
         if kept:
-            for strip in range(0, bk, STRIP):
-                part = slice(strip, strip + STRIP)
-                p_list[now, part, :] = jnp.exp2(s_ref[part, :] - new_top).astype(jnp.bfloat16)
+            p_list[now] = high
             top_list[now] = new_top
-            sums = dot32(vt, p_list[now])
         else:
-            p = jnp.exp2(s_ref[...] - new_top)
-            high = p.astype(jnp.bfloat16)
-            sums = dot32(vt, high) + dot32(vt, (p - high.astype(jnp.float32)).astype(jnp.bfloat16))
+            sums = sums + dot32(vt, (p - high.astype(jnp.float32)).astype(jnp.bfloat16))
         out_ref[:, queries] = out_ref[:, queries] * fix + sums[:HD, :]
         sum_ref[:, queries] = sum_ref[:, queries] * fix + sums[HD:HD + 1, :]
         log_ref[:, queries] = new_top
@@ -288,18 +286,19 @@
     log_ref[...] = log_ref[...] + jnp.log2(total_p)
 
 
-def backward_kernel(peers, heads, rows, bq, bk, kept, me_s, plan_q, plan_k, count_ref, v_ref,
+def backward_kernel(listed, heads, rows, bq, bk, kept, me_s, plan_q, plan_k, count_ref, v_ref,
                     qx_ref, kx_ref, kt_ref, rows_ref, log_ref, *refs):
     if kept:
         p_list, top_list = refs[:2]
         refs = refs[2:]
+    peers = len(listed)
     blocks = refs[:peers]
     results = refs[peers:peers + heads]
     g_ref, dot_ref, dk_acc, dv_acc, dq_acc, p0, ds0, p1, ds1 = refs[peers + heads:]
     scale = HD ** (-0.5)
     factor = scale * math.log2(math.e)
     me = me_s[0]
-    for d, block in enumerate(blocks):
+    for d, block in zip(listed, blocks):
         g_ref[aligned(me ^ d, rows), :] = block[...]
     ones = jnp.ones((ONES_ROWS, HD), jnp.bfloat16)
     for start in range(0, g_ref.shape[0], bq):
@@ -398,7 +397,7 @@
     )(me, *blocks)
 
 
-def attention_backward(me, heads, state, blocks):
+def attention_backward(me, heads, state, listed, blocks):
     peers, rows = len(blocks), blocks[0].shape[0]
     total = peers * rows
     bq, bk = block_sizes(total)[1]
@@ -414,7 +413,7 @@
         *[pltpu.VMEM((bk, bq), jnp.bfloat16)] * 4,
     ]
     return pl.pallas_call(
-        functools.partial(backward_kernel, peers, heads, rows, bq, bk, kept),
+        functools.partial(backward_kernel, listed, heads, rows, bq, bk, kept),
         in_specs=[SMEM_SPEC] * 4 + [VMEM_SPEC] * (len(vectors) + peers),
         out_specs=[VMEM_SPEC] * heads,
         out_shape=out_shape,
@@ -438,12 +437,14 @@
 
     order = [*range(2, peers, 2), *range(peers - 1, 0, -2)]
 
-    def exchange_all(blocks, wanted):
-        moved = {d: exchange(blocks[d % heads], d) for d in order if d < wanted}
-        return [blocks[0]] + [moved[d] for d in range(1, wanted)]
+    far_first = sorted(range(peers), key=lambda d: (-bin(d >> 1).count("1"), d & 1, d))
+    returning = [d for d in far_first if d < heads]
+
+    def exchange_all(blocks, listed):
+        return [exchange(blocks[d % heads], d) for d in listed]
 
     packed = list(pack_heads(me_vector, queries, keys_in, values, doc_ids))
-    received = exchange_all(packed, peers)
+    received = exchange_all(packed, range(peers))
 
     def share(step):
         return len(order) * step * (step + 1) // ((groups - 2) * (groups - 1))
@@ -471,11 +472,11 @@
                 features, acc, here, weights[2:] = after((features, acc, here, weights[2:]))
                 for d, block in zip(batch, here):
                     received[d] = block
-    grads = exchange_all(acc, peers)
-
-    results = attention_backward(me_vector, heads, state, grads)
-    returned = exchange_all(results, heads)
-    return tuple(unpack_heads(me_vector, returned, rows))
+    grads = exchange_all(acc, far_first)
+
+    results = attention_backward(me_vector, heads, state, far_first, grads)
+    returned = exchange_all(results, returning)
+    return tuple(unpack_heads(me_vector, returning, returned, rows))
 
 
 def solution(mesh):

time: 129 us -> 125 us (0.969); the launches traced: 127 us -> 125 us
  Pallas kernels: 40.3 us -> 38.5 us
    pallas_call x1, Pallas kernels: 18.5 us -> 16.2 us  [attention_forward(): pl.pallas_call(functools.partial(forward_kernel, peers, heads, rows, bq,...]
    ppermute x3, waiting for transfers between devices: 2.12 us -> 4.43 us  [pass_on(): lax.ppermute(x, 'head', [(i, (i + 1) % groups) for i in range(groups)])]
    ppermute x21, waiting for transfers between devices: 47.2 us -> 45.8 us  [exchange(): lax.ppermute(x, 'seq', [(i, i ^ d) for i in range(peers)])]
  transfers between devices with their start and end apart: 24 -> 24, of which waited for: 12 -> 16; matrix products, arithmetic and copies ran while one was open for 4% -> 4% of each run, Pallas kernels for 18% -> 17%
where the time goes in v11:
time: 125 us
  waiting for transfers between devices  50.2 us (40%)
  Pallas kernels  38.5 us (31%)
  starting transfers between devices  24 us (19%)
  local copies, waits for them, and re-layouts  11.8 us (9%)
    ppermute x21, waiting for transfers between devices, exchange(): lax.ppermute(x, 'seq', [(i, i ^ d) for i in range(peers)])  45.8 us
    ppermute x21, starting transfers between devices, exchange(): lax.ppermute(x, 'seq', [(i, i ^ d) for i in range(peers)])  19.5 us
    pallas_call x1, Pallas kernels, attention_forward(): pl.pallas_call(functools.partial(forward_kernel, peers, heads, rows, bq,...  16.2 us
    pallas_call x1, Pallas kernels, attention_backward(): pl.pallas_call(functools.partial(backward_kernel, listed, heads, rows, bq...  14.5 us
    unnamed x26, local copies, waits for them, and re-layouts  6.98 us
    dynamic_slice x1, local copies, waits for them, and re-layouts, per_device(): lax.dynamic_slice_in_dim(out_weight, block * width, width, 1)  4.79 us
    ppermute x3, waiting for transfers between devices, pass_on(): lax.ppermute(x, 'head', [(i, (i + 1) % groups) for i in range(groups)])  4.43 us
    ppermute x3, starting transfers between devices, pass_on(): lax.ppermute(x, 'head', [(i, (i + 1) % groups) for i in range(groups)])  4.43 us
  transfers between devices with their start and end apart: 24, of which 16 were waited for; matrix products, arithmetic and copies ran while one was open for 4% of the time, Pallas kernels for 17%

profile of v11, /device:TPU:0, one launch (start us, length us, event | category | flops | bytes accessed | tf_op | source)
XLA Modules:
  0.0 125.2 jit_solution(15613756527379757647)
XLA Ops:
  0.6 3.1 %collective-permute-start = (bf16[384,1024]{1,0:T(8,128)(2,1)}, bf16[384,1024]{1,0:T(8,128)(2,1)S(1)}, u32[]{:S(2)}, u32[]{:S(2)}) collective-permute-start(bf16[384,1024]{1,0:T(8,128)(2,1)} %o_ref.1), channel_id=1, source_target_pairs={{0,1},{1,2},{2,3},{3,0},{4,5},{5,6},{6,7},{7,4},{8,9},{9,10},{10,1... | collective-permute-start | bytes 2359304 | tf_op jit(solution)/shard_map/ppermute | solution.py:436
  3.7 1.1 copy-done
  4.8 1.1 copy-done.1
  6.0 1.1 copy-done.2
  7.1 0.7 copy-done.4
  7.8 1.7 %shard_map.85 = (bf16[1168,128]{1,0:T(8,128)(2,1)S(1)}, bf16[1168,128]{1,0:T(8,128)(2,1)S(1)}, bf16[1168,128]{1,0:T(8,128)(2,1)}, bf16[1168,128]{1,0:T(8,128)(2,...) custom-call(s32[1]{0:T(128)} %bitcast.me_s, ...), custom_call_target="tpu_custom_call" | custom-call | tf_op jit(solution)/shard_map/pallas_call | solution.py:69
  9.5 0.7 copy-done.5
  10.2 0.7 copy-done.7
  10.9 0.7 copy-done.9
  11.7 0.7 copy-done.11
  12.4 1.5 %collective-permute-start.1 = (bf16[1168,128]{1,0:T(8,128)(2,1)}, bf16[1168,128]{1,0:T(8,128)(2,1)S(1)}, u32[]{:S(2)}, u32[]{:S(2)}) collective-permute-start(bf16[1168,128]{1,0:T(8,128)(2,1)} %get-tuple-element.58), channel_id=1, source_target_pairs={{0,8},{4,12},{8,0},{12,4},{16,24},{20,28},{24,16},{28,20},{1,9},{5... | collective-permute-start | bytes 897032 | tf_op jit(solution)/shard_map/ppermute | solution.py:433
  13.9 1.5 %collective-permute-start.2 = (bf16[1168,128]{1,0:T(8,128)(2,1)}, bf16[1168,128]{1,0:T(8,128)(2,1)S(1)}, u32[]{:S(2)}, u32[]{:S(2)}) collective-permute-start(bf16[1168,128]{1,0:T(8,128)(2,1)} %get-tuple-element.59), channel_id=1, source_target_pairs={{0,16},{4,20},{8,24},{12,28},{16,0},{20,4},{24,8},{28,12},{1,17},{... | collective-permute-start | bytes 897032 | tf_op jit(solution)/shard_map/ppermute | solution.py:433
  15.4 4.8 %constant_dynamic-slice_fusion = (bf16[1024,1024]{1,0:T(8,128)(2,1)S(1)}, bf16[1024,1024]{1,0:T(8,128)(2,1)S(1)}, bf16[1024,1024]{1,0:T(8,128)(2,1)S(1)}, bf16[1024,1024]{1,0:T(8,128)(2,1)S(1)}) fusion(bf16[1024,4096]{1,0:T(8,128)(2,1)} %param.10, s32[]{:T(128)S(6)} %select_n.15, s32[]{:T(128)S(6)} %select_n.13, s32[]{:T(128)S(6)} %select_n.12, s32[]{:T(128)S(6)} %select_n.14), kind=kLoop, calls=%fused_computation | loop fusion | bytes 16777232 | tf_op jit(solution)/shard_map/dynamic_slice | solution.py:457
  20.3 1.0 shard_map.86.refs_0_
  21.3 1.1 collective-permute-done.2.refs_4_
  22.4 1.1 collective-permute-done.o_ref
  23.5 0.5 collective-permute-start.3
  24.0 2.0 %collective-permute-start.4 = (bf16[1168,128]{1,0:T(8,128)(2,1)S(1)}, bf16[1168,128]{1,0:T(8,128)(2,1)S(1)}, u32[]{:S(2)}, u32[]{:S(2)}) collective-permute-start(bf16[1168,128]{1,0:T(8,128)(2,1)S(1)} %copy-done.12), channel_id=1, source_target_pairs={{0,24},{4,28},{8,16},{12,20},{16,8},{20,12},{24,0},{28,4},{1,25},{... | collective-permute-start | bytes 897032 | tf_op jit(solution)/shard_map/ppermute | solution.py:433
  26.0 2.2 %collective-permute-start.6 = (bf16[1168,128]{1,0:T(8,128)(2,1)S(1)}, bf16[1168,128]{1,0:T(8,128)(2,1)S(1)}, u32[]{:S(2)}, u32[]{:S(2)}) collective-permute-start(bf16[1168,128]{1,0:T(8,128)(2,1)S(1)} %copy-done.8), channel_id=1, source_target_pairs={{0,20},{4,16},{8,28},{12,24},{16,4},{20,0},{24,12},{28,8},{1,21},{... | collective-permute-start | bytes 897032 | tf_op jit(solution)/shard_map/ppermute | solution.py:433
  28.1 6.9 %collective-permute-done.4.refs_6_ = bf16[1168,128]{1,0:T(8,128)(2,1)S(1)} collective-permute-done((bf16[1168,128]{1,0:T(8,128)(2,1)S(1)}, bf16[1168,128]{1,0:T(8,128)(2,1)S(1)}, u32[]{:S(2)}, u32[]{:S(2)}) %collective-permute-start.4) | collective-permute-done | bytes 299040 | tf_op jit(solution)/shard_map/ppermute | solution.py:433
  35.0 1.0 shard_map.87.refs_0_
  36.0 3.9 %collective-permute-done.5.refs_7_ = bf16[1168,128]{1,0:T(8,128)(2,1)S(1)} collective-permute-done((bf16[1168,128]{1,0:T(8,128)(2,1)S(1)}, bf16[1168,128]{1,0:T(8,128)(2,1)S(1)}, u32[]{:S(2)}, u32[]{:S(2)}) %collective-permute-start.5) | collective-permute-done | bytes 299040 | tf_op jit(solution)/shard_map/ppermute | solution.py:433
  39.9 5.5 %collective-permute-done.6.refs_5_ = bf16[1168,128]{1,0:T(8,128)(2,1)S(1)} collective-permute-done((bf16[1168,128]{1,0:T(8,128)(2,1)S(1)}, bf16[1168,128]{1,0:T(8,128)(2,1)S(1)}, u32[]{:S(2)}, u32[]{:S(2)}) %collective-permute-start.6) | collective-permute-done | bytes 299040 | tf_op jit(solution)/shard_map/ppermute | solution.py:433
  45.4 0.9 collective-permute-start.9
  46.3 16.2 %shard_map.88 = (bf16[3072,128]{1,0:T(8,128)(2,1)S(1)}, bf16[3072,256]{1,0:T(8,128)(2,1)S(1)}, bf16[3072,256]{1,0:T(8,128)(2,1)S(1)}, bf16[128,3072]{1,0:T(8,128...) custom-call(s32[1]{0:T(128)} %bitcast.me_s, ...), custom_call_target="tpu_custom_call" | custom-call | flops 1811939328 | bytes 6291456 | tf_op jit(solution)/shard_map/pallas_call | solution.py:389
  62.5 1.0 shard_map.89.acc_ref
  63.5 3.3 %collective-permute-done.9.o_ref = bf16[384,1024]{1,0:T(8,128)(2,1)S(1)} collective-permute-done((bf16[384,1024]{1,0:T(8,128)(2,1)S(1)}, bf16[384,1024]{1,0:T(8,128)(2,1)S(1)}, u32[]{:S(2)}, u32[]{:S(2)}) %collective-permute-start.9) | collective-permute-done | bytes 786464 | tf_op jit(solution)/shard_map/ppermute | solution.py:436
  66.9 1.0 shard_map.90
  67.9 2.2 %collective-permute-start.10 = (bf16[384,128]{1,0:T(8,128)(2,1)S(1)}, bf16[384,128]{1,0:T(8,128)(2,1)S(1)}, u32[]{:S(2)}, u32[]{:S(2)}) collective-permute-start(bf16[384,128]{1,0:T(8,128)(2,1)S(1)} %get-tuple-element.95), channel_id=1, source_target_pairs={{0,24},{4,28},{8,16},{12,20},{16,8},{20,12},{24,0},{28,4},{1,25},{... | collective-permute-start | bytes 294920 | tf_op jit(solution)/shard_map/ppermute | solution.py:433
  70.1 0.6 collective-permute-start.12
  70.7 1.5 %collective-permute-start.13 = (bf16[384,128]{1,0:T(8,128)(2,1)S(1)}, bf16[384,128]{1,0:T(8,128)(2,1)S(1)}, u32[]{:S(2)}, u32[]{:S(2)}) collective-permute-start(bf16[384,128]{1,0:T(8,128)(2,1)S(1)} %get-tuple-element.98), channel_id=1, source_target_pairs={{0,16},{4,20},{8,24},{12,28},{16,0},{20,4},{24,8},{28,12},{1,17},{... | collective-permute-start | bytes 294920 | tf_op jit(solution)/shard_map/ppermute | solution.py:433
  72.2 1.1 collective-permute-start.14
  73.5 0.4 collective-permute-start.15
  73.9 2.3 %collective-permute-done.11.refs_3_ = bf16[384,128]{1,0:T(8,128)(2,1)S(1)} collective-permute-done((bf16[384,128]{1,0:T(8,128)(2,1)S(1)}, bf16[384,128]{1,0:T(8,128)(2,1)S(1)}, u32[]{:S(2)}, u32[]{:S(2)}) %collective-permute-start.11) | collective-permute-done | bytes 98336 | tf_op jit(solution)/shard_map/ppermute | solution.py:433
  76.2 1.5 %collective-permute-done.12.refs_4_ = bf16[384,128]{1,0:T(8,128)(2,1)S(1)} collective-permute-done((bf16[384,128]{1,0:T(8,128)(2,1)S(1)}, bf16[384,128]{1,0:T(8,128)(2,1)S(1)}, u32[]{:S(2)}, u32[]{:S(2)}) %collective-permute-start.12) | collective-permute-done | bytes 98336 | tf_op jit(solution)/shard_map/ppermute | solution.py:433
  77.7 1.7 %collective-permute-done.14.refs_6_ = bf16[384,128]{1,0:T(8,128)(2,1)S(1)} collective-permute-done((bf16[384,128]{1,0:T(8,128)(2,1)S(1)}, bf16[384,128]{1,0:T(8,128)(2,1)S(1)}, u32[]{:S(2)}, u32[]{:S(2)}) %collective-permute-start.14) | collective-permute-done | bytes 98336 | tf_op jit(solution)/shard_map/ppermute | solution.py:433
  79.4 0.4 collective-permute-done.15.refs_7_
  79.8 14.5 %shard_map.91 = (bf16[1152,128]{1,0:T(8,128)(2,1)S(1)}, bf16[1152,128]{1,0:T(8,128)(2,1)S(1)}, bf16[1152,128]{1,0:T(8,128)(2,1)S(1)}, bf16[1152,128]{1,0:T(8,128...) custom-call(s32[1]{0:T(128)} %bitcast.me_s, ...), custom_call_target="tpu_custom_call" | custom-call | flops 3019898880 | bytes 6291456 | tf_op jit(solution)/shard_map/pallas_call | solution.py:415
  94.3 2.2 %collective-permute-start.17 = (bf16[1152,128]{1,0:T(8,128)(2,1)S(1)}, bf16[1152,128]{1,0:T(8,128)(2,1)S(1)}, u32[]{:S(2)}, u32[]{:S(2)}) collective-permute-start(bf16[1152,128]{1,0:T(8,128)(2,1)S(1)} %get-tuple-element.103), channel_id=1, source_target_pairs={{0,24},{4,28},{8,16},{12,20},{16,8},{20,12},{24,0},{28,4},{1,25},{... | collective-permute-start | bytes 884744 | tf_op jit(solution)/shard_map/ppermute | solution.py:433
  96.7 1.2 collective-permute-start.19
  97.9 1.5 %collective-permute-start.20 = (bf16[1152,128]{1,0:T(8,128)(2,1)S(1)}, bf16[1152,128]{1,0:T(8,128)(2,1)S(1)}, u32[]{:S(2)}, u32[]{:S(2)}) collective-permute-start(bf16[1152,128]{1,0:T(8,128)(2,1)S(1)} %get-tuple-element.106), channel_id=1, source_target_pairs={{0,16},{4,20},{8,24},{12,28},{16,0},{20,4},{24,8},{28,12},{1,17},{... | collective-permute-start | bytes 884744 | tf_op jit(solution)/shard_map/ppermute | solution.py:433
  99.7 5.5 %collective-permute-done.17.refs_0_ = bf16[1152,128]{1,0:T(8,128)(2,1)S(1)} collective-permute-done((bf16[1152,128]{1,0:T(8,128)(2,1)S(1)}, bf16[1152,128]{1,0:T(8,128)(2,1)S(1)}, u32[]{:S(2)}, u32[]{:S(2)}) %collective-permute-start.17) | collective-permute-done | bytes 294944 | tf_op jit(solution)/shard_map/ppermute | solution.py:433
  105.2 5.1 %collective-permute-done.18.refs_1_ = bf16[1152,128]{1,0:T(8,128)(2,1)S(1)} collective-permute-done((bf16[1152,128]{1,0:T(8,128)(2,1)S(1)}, bf16[1152,128]{1,0:T(8,128)(2,1)S(1)}, u32[]{:S(2)}, u32[]{:S(2)}) %collective-permute-start.18) | collective-permute-done | bytes 294944 | tf_op jit(solution)/shard_map/ppermute | solution.py:433
  110.2 1.0 collective-permute-start.23
  111.3 6.3 %collective-permute-done.19.refs_2_ = bf16[1152,128]{1,0:T(8,128)(2,1)S(1)} collective-permute-done((bf16[1152,128]{1,0:T(8,128)(2,1)S(1)}, bf16[1152,128]{1,0:T(8,128)(2,1)S(1)}, u32[]{:S(2)}, u32[]{:S(2)}) %collective-permute-start.19) | collective-permute-done | bytes 294944 | tf_op jit(solution)/shard_map/ppermute | solution.py:433
  117.6 4.6 %collective-permute-done.21.refs_4_ = bf16[1152,128]{1,0:T(8,128)(2,1)S(1)} collective-permute-done((bf16[1152,128]{1,0:T(8,128)(2,1)S(1)}, bf16[1152,128]{1,0:T(8,128)(2,1)S(1)}, u32[]{:S(2)}, u32[]{:S(2)}) %collective-permute-start.21) | collective-permute-done | bytes 294944 | tf_op jit(solution)/shard_map/ppermute | solution.py:433
  122.2 1.0 collective-permute-done.22.refs_5_
  123.1 2.1 %shard_map.92 = (bf16[384,1024]{1,0:T(8,128)(2,1)}, bf16[384,1024]{1,0:T(8,128)(2,1)}, bf16[384,1024]{1,0:T(8,128)(2,1)}) custom-call(s32[1]{0:T(128)} %bitcast.me_s, bf16[1152,128]{1,0:T(8,128)(2,1)S(1)} %collective-permute-done.17.refs_0_, bf16[1152,128]{1,0:T(8,128)(2,1)S(1)} %collective-permute-done.18.refs_1_, ...), custom_call_target="tpu_custom_call" | custom-call | tf_op jit(solution)/shard_map/pallas_call | solution.py:90
  (35 shorter events, 0.7 us)
Async XLA Ops:
  0.6 22.9 %collective-permute-start = (bf16[384,1024]{1,0:T(8,128)(2,1)}, bf16[384,1024]{1,0:T(8,128)(2,1)S(1)}, u32[]{:S(2)}, u32[]{:S(2)}) collective-permute-start(bf16[384,1024]{1,0:T(8,128)(2,1)} %o_ref.1), channel_id=1, source_target_pairs={{0,1},{1,2},{2,3},{3,0},{4,5},{5,6},{6,7},{7,4},{8,9},{9,10},{10,1... | collective-permute-start | bytes 2359304 | tf_op jit(solution)/shard_map/ppermute | solution.py:436
  3.7 1.1 copy-start
  4.8 1.1 copy-start.1
  6.0 1.1 copy-start.2
  7.1 0.7 copy-start.4
  9.5 0.7 copy-start.5
  10.2 0.7 copy-start.7
  10.9 0.7 copy-start.9
  11.7 0.7 copy-start.11
  12.4 8.9 %collective-permute-start.1 = (bf16[1168,128]{1,0:T(8,128)(2,1)}, bf16[1168,128]{1,0:T(8,128)(2,1)S(1)}, u32[]{:S(2)}, u32[]{:S(2)}) collective-permute-start(bf16[1168,128]{1,0:T(8,128)(2,1)} %get-tuple-element.58), channel_id=1, source_target_pairs={{0,8},{4,12},{8,0},{12,4},{16,24},{20,28},{24,16},{28,20},{1,9},{5... | collective-permute-start | bytes 897032 | tf_op jit(solution)/shard_map/ppermute | solution.py:433
  13.9 8.5 %collective-permute-start.2 = (bf16[1168,128]{1,0:T(8,128)(2,1)}, bf16[1168,128]{1,0:T(8,128)(2,1)S(1)}, u32[]{:S(2)}, u32[]{:S(2)}) collective-permute-start(bf16[1168,128]{1,0:T(8,128)(2,1)} %get-tuple-element.59), channel_id=1, source_target_pairs={{0,16},{4,20},{8,24},{12,28},{16,0},{20,4},{24,8},{28,12},{1,17},{... | collective-permute-start | bytes 897032 | tf_op jit(solution)/shard_map/ppermute | solution.py:433
  15.4 4.8 %copy-start.3 = (bf16[384,1024]{1,0:T(8,128)(2,1)S(1)}, bf16[384,1024]{1,0:T(8,128)(2,1)}, u32[]{:S(2)}) copy-start(bf16[384,1024]{1,0:T(8,128)(2,1)} %o_ref.1) | copy-start | bytes 2359300
  20.2 3.7 %copy-start.12 = (bf16[1168,128]{1,0:T(8,128)(2,1)S(1)}, bf16[1168,128]{1,0:T(8,128)(2,1)}, u32[]{:S(2)}) copy-start(bf16[1168,128]{1,0:T(8,128)(2,1)} %copy-done.11) | copy-start | bytes 897028
  20.2 5.7 %copy-start.10 = (bf16[1168,128]{1,0:T(8,128)(2,1)S(1)}, bf16[1168,128]{1,0:T(8,128)(2,1)}, u32[]{:S(2)}) copy-start(bf16[1168,128]{1,0:T(8,128)(2,1)} %copy-done.9) | copy-start | bytes 897028
  20.2 5.7 %copy-start.8 = (bf16[1168,128]{1,0:T(8,128)(2,1)S(1)}, bf16[1168,128]{1,0:T(8,128)(2,1)}, u32[]{:S(2)}) copy-start(bf16[1168,128]{1,0:T(8,128)(2,1)} %copy-done.7) | copy-start | bytes 897028
  20.3 7.9 %copy-start.6 = (bf16[1168,128]{1,0:T(8,128)(2,1)S(1)}, bf16[1168,128]{1,0:T(8,128)(2,1)}, u32[]{:S(2)}) copy-start(bf16[1168,128]{1,0:T(8,128)(2,1)} %copy-done.5) | copy-start | bytes 897028
  23.5 21.9 %collective-permute-start.3 = (bf16[384,1024]{1,0:T(8,128)(2,1)S(1)}, bf16[384,1024]{1,0:T(8,128)(2,1)S(1)}, u32[]{:S(2)}, u32[]{:S(2)}) collective-permute-start(bf16[384,1024]{1,0:T(8,128)(2,1)S(1)} %collective-permute-done.o_ref), channel_id=1, source_target_pairs={{0,1},{1,2},{2,3},{3,0},{4,5},{5,6},{6,7},{7,4},{8,9},{9,10},{10,1... | collective-permute-start | bytes 2359304 | tf_op jit(solution)/shard_map/ppermute | solution.py:436
  24.0 11.0 %collective-permute-start.4 = (bf16[1168,128]{1,0:T(8,128)(2,1)S(1)}, bf16[1168,128]{1,0:T(8,128)(2,1)S(1)}, u32[]{:S(2)}, u32[]{:S(2)}) collective-permute-start(bf16[1168,128]{1,0:T(8,128)(2,1)S(1)} %copy-done.12), channel_id=1, source_target_pairs={{0,24},{4,28},{8,16},{12,20},{16,8},{20,12},{24,0},{28,4},{1,25},{... | collective-permute-start | bytes 897032 | tf_op jit(solution)/shard_map/ppermute | solution.py:433
  25.9 14.0 %collective-permute-start.5 = (bf16[1168,128]{1,0:T(8,128)(2,1)S(1)}, bf16[1168,128]{1,0:T(8,128)(2,1)S(1)}, u32[]{:S(2)}, u32[]{:S(2)}) collective-permute-start(bf16[1168,128]{1,0:T(8,128)(2,1)S(1)} %copy-done.10), channel_id=1, source_target_pairs={{0,28},{4,24},{8,20},{12,16},{16,12},{20,8},{24,4},{28,0},{1,29},{... | collective-permute-start | bytes 897032 | tf_op jit(solution)/shard_map/ppermute | solution.py:433
  26.0 19.5 %collective-permute-start.6 = (bf16[1168,128]{1,0:T(8,128)(2,1)S(1)}, bf16[1168,128]{1,0:T(8,128)(2,1)S(1)}, u32[]{:S(2)}, u32[]{:S(2)}) collective-permute-start(bf16[1168,128]{1,0:T(8,128)(2,1)S(1)} %copy-done.8), channel_id=1, source_target_pairs={{0,20},{4,16},{8,28},{12,24},{16,4},{20,0},{24,12},{28,8},{1,21},{... | collective-permute-start | bytes 897032 | tf_op jit(solution)/shard_map/ppermute | solution.py:433
  28.1 17.3 %collective-permute-start.7 = (bf16[1168,128]{1,0:T(8,128)(2,1)S(1)}, bf16[1168,128]{1,0:T(8,128)(2,1)S(1)}, u32[]{:S(2)}, u32[]{:S(2)}) collective-permute-start(bf16[1168,128]{1,0:T(8,128)(2,1)S(1)} %copy-done.6), channel_id=1, source_target_pairs={{0,12},{4,8},{8,4},{12,0},{16,28},{20,24},{24,20},{28,16},{1,13},{... | collective-permute-start | bytes 897032 | tf_op jit(solution)/shard_map/ppermute | solution.py:433
  35.0 10.4 %collective-permute-start.8 = (bf16[1168,128]{1,0:T(8,128)(2,1)S(1)}, bf16[1168,128]{1,0:T(8,128)(2,1)S(1)}, u32[]{:S(2)}, u32[]{:S(2)}) collective-permute-start(bf16[1168,128]{1,0:T(8,128)(2,1)S(1)} %get-tuple-element.66), channel_id=1, source_target_pairs={{0,4},{4,0},{8,12},{12,8},{16,20},{20,16},{24,28},{28,24},{1,5},{5... | collective-permute-start | bytes 897032 | tf_op jit(solution)/shard_map/ppermute | solution.py:433
  45.4 21.4 %collective-permute-start.9 = (bf16[384,1024]{1,0:T(8,128)(2,1)S(1)}, bf16[384,1024]{1,0:T(8,128)(2,1)S(1)}, u32[]{:S(2)}, u32[]{:S(2)}) collective-permute-start(bf16[384,1024]{1,0:T(8,128)(2,1)S(1)} %collective-permute-done.3.o_ref), channel_id=1, source_target_pairs={{0,1},{1,2},{2,3},{3,0},{4,5},{5,6},{6,7},{7,4},{8,9},{9,10},{10,1... | collective-permute-start | bytes 2359304 | tf_op jit(solution)/shard_map/ppermute | solution.py:436
  67.9 5.6 %collective-permute-start.10 = (bf16[384,128]{1,0:T(8,128)(2,1)S(1)}, bf16[384,128]{1,0:T(8,128)(2,1)S(1)}, u32[]{:S(2)}, u32[]{:S(2)}) collective-permute-start(bf16[384,128]{1,0:T(8,128)(2,1)S(1)} %get-tuple-element.95), channel_id=1, source_target_pairs={{0,24},{4,28},{8,16},{12,20},{16,8},{20,12},{24,0},{28,4},{1,25},{... | collective-permute-start | bytes 294920 | tf_op jit(solution)/shard_map/ppermute | solution.py:433
  70.1 6.1 %collective-permute-start.11 = (bf16[384,128]{1,0:T(8,128)(2,1)S(1)}, bf16[384,128]{1,0:T(8,128)(2,1)S(1)}, u32[]{:S(2)}, u32[]{:S(2)}) collective-permute-start(bf16[384,128]{1,0:T(8,128)(2,1)S(1)} %get-tuple-element.96), channel_id=1, source_target_pairs={{0,28},{4,24},{8,20},{12,16},{16,12},{20,8},{24,4},{28,0},{1,29},{... | collective-permute-start | bytes 294920 | tf_op jit(solution)/shard_map/ppermute | solution.py:433
  70.1 7.5 %collective-permute-start.12 = (bf16[384,128]{1,0:T(8,128)(2,1)S(1)}, bf16[384,128]{1,0:T(8,128)(2,1)S(1)}, u32[]{:S(2)}, u32[]{:S(2)}) collective-permute-start(bf16[384,128]{1,0:T(8,128)(2,1)S(1)} %get-tuple-element.97), channel_id=1, source_target_pairs={{0,8},{4,12},{8,0},{12,4},{16,24},{20,28},{24,16},{28,20},{1,9},{5... | collective-permute-start | bytes 294920 | tf_op jit(solution)/shard_map/ppermute | solution.py:433
  70.7 6.9 %collective-permute-start.13 = (bf16[384,128]{1,0:T(8,128)(2,1)S(1)}, bf16[384,128]{1,0:T(8,128)(2,1)S(1)}, u32[]{:S(2)}, u32[]{:S(2)}) collective-permute-start(bf16[384,128]{1,0:T(8,128)(2,1)S(1)} %get-tuple-element.98), channel_id=1, source_target_pairs={{0,16},{4,20},{8,24},{12,28},{16,0},{20,4},{24,8},{28,12},{1,17},{... | collective-permute-start | bytes 294920 | tf_op jit(solution)/shard_map/ppermute | solution.py:433
  72.2 7.2 %collective-permute-start.14 = (bf16[384,128]{1,0:T(8,128)(2,1)S(1)}, bf16[384,128]{1,0:T(8,128)(2,1)S(1)}, u32[]{:S(2)}, u32[]{:S(2)}) collective-permute-start(bf16[384,128]{1,0:T(8,128)(2,1)S(1)} %get-tuple-element.99), channel_id=1, source_target_pairs={{0,12},{4,8},{8,4},{12,0},{16,28},{20,24},{24,20},{28,16},{1,13},{... | collective-permute-start | bytes 294920 | tf_op jit(solution)/shard_map/ppermute | solution.py:433
  73.5 6.3 %collective-permute-start.15 = (bf16[384,128]{1,0:T(8,128)(2,1)S(1)}, bf16[384,128]{1,0:T(8,128)(2,1)S(1)}, u32[]{:S(2)}, u32[]{:S(2)}) collective-permute-start(bf16[384,128]{1,0:T(8,128)(2,1)S(1)} %get-tuple-element.100), channel_id=1, source_target_pairs={{0,20},{4,16},{8,28},{12,24},{16,4},{20,0},{24,12},{28,8},{1,21},{... | collective-permute-start | bytes 294920 | tf_op jit(solution)/shard_map/ppermute | solution.py:433
  76.2 3.6 %collective-permute-start.16 = (bf16[384,128]{1,0:T(8,128)(2,1)S(1)}, bf16[384,128]{1,0:T(8,128)(2,1)S(1)}, u32[]{:S(2)}, u32[]{:S(2)}) collective-permute-start(bf16[384,128]{1,0:T(8,128)(2,1)S(1)} %get-tuple-element.102), channel_id=1, source_target_pairs={{0,4},{4,0},{8,12},{12,8},{16,20},{20,16},{24,28},{28,24},{1,5},{5... | collective-permute-start | bytes 294920 | tf_op jit(solution)/shard_map/ppermute | solution.py:433
  94.3 10.9 %collective-permute-start.17 = (bf16[1152,128]{1,0:T(8,128)(2,1)S(1)}, bf16[1152,128]{1,0:T(8,128)(2,1)S(1)}, u32[]{:S(2)}, u32[]{:S(2)}) collective-permute-start(bf16[1152,128]{1,0:T(8,128)(2,1)S(1)} %get-tuple-element.103), channel_id=1, source_target_pairs={{0,24},{4,28},{8,16},{12,20},{16,8},{20,12},{24,0},{28,4},{1,25},{... | collective-permute-start | bytes 884744 | tf_op jit(solution)/shard_map/ppermute | solution.py:433
  96.5 13.7 %collective-permute-start.18 = (bf16[1152,128]{1,0:T(8,128)(2,1)S(1)}, bf16[1152,128]{1,0:T(8,128)(2,1)S(1)}, u32[]{:S(2)}, u32[]{:S(2)}) collective-permute-start(bf16[1152,128]{1,0:T(8,128)(2,1)S(1)} %get-tuple-element.104), channel_id=1, source_target_pairs={{0,28},{4,24},{8,20},{12,16},{16,12},{20,8},{24,4},{28,0},{1,29},{... | collective-permute-start | bytes 884744 | tf_op jit(solution)/shard_map/ppermute | solution.py:433
  96.7 20.9 %collective-permute-start.19 = (bf16[1152,128]{1,0:T(8,128)(2,1)S(1)}, bf16[1152,128]{1,0:T(8,128)(2,1)S(1)}, u32[]{:S(2)}, u32[]{:S(2)}) collective-permute-start(bf16[1152,128]{1,0:T(8,128)(2,1)S(1)} %get-tuple-element.105), channel_id=1, source_target_pairs={{0,8},{4,12},{8,0},{12,4},{16,24},{20,28},{24,16},{28,20},{1,9},{5... | collective-permute-start | bytes 884744 | tf_op jit(solution)/shard_map/ppermute | solution.py:433
  97.9 19.6 %collective-permute-start.20 = (bf16[1152,128]{1,0:T(8,128)(2,1)S(1)}, bf16[1152,128]{1,0:T(8,128)(2,1)S(1)}, u32[]{:S(2)}, u32[]{:S(2)}) collective-permute-start(bf16[1152,128]{1,0:T(8,128)(2,1)S(1)} %get-tuple-element.106), channel_id=1, source_target_pairs={{0,16},{4,20},{8,24},{12,28},{16,0},{20,4},{24,8},{28,12},{1,17},{... | collective-permute-start | bytes 884744 | tf_op jit(solution)/shard_map/ppermute | solution.py:433
  99.4 22.8 %collective-permute-start.21 = (bf16[1152,128]{1,0:T(8,128)(2,1)S(1)}, bf16[1152,128]{1,0:T(8,128)(2,1)S(1)}, u32[]{:S(2)}, u32[]{:S(2)}) collective-permute-start(bf16[1152,128]{1,0:T(8,128)(2,1)S(1)} %get-tuple-element.107), channel_id=1, source_target_pairs={{0,12},{4,8},{8,4},{12,0},{16,28},{20,24},{24,20},{28,16},{1,13},{... | collective-permute-start | bytes 884744 | tf_op jit(solution)/shard_map/ppermute | solution.py:433
  105.2 18.0 %collective-permute-start.22 = (bf16[1152,128]{1,0:T(8,128)(2,1)S(1)}, bf16[1152,128]{1,0:T(8,128)(2,1)S(1)}, u32[]{:S(2)}, u32[]{:S(2)}) collective-permute-start(bf16[1152,128]{1,0:T(8,128)(2,1)S(1)} %get-tuple-element.108), channel_id=1, source_target_pairs={{0,20},{4,16},{8,28},{12,24},{16,4},{20,0},{24,12},{28,8},{1,21},{... | collective-permute-start | bytes 884744 | tf_op jit(solution)/shard_map/ppermute | solution.py:433
  110.2 12.9 %collective-permute-start.23 = (bf16[1152,128]{1,0:T(8,128)(2,1)S(1)}, bf16[1152,128]{1,0:T(8,128)(2,1)S(1)}, u32[]{:S(2)}, u32[]{:S(2)}) collective-permute-start(bf16[1152,128]{1,0:T(8,128)(2,1)S(1)} %get-tuple-element.110), channel_id=1, source_target_pairs={{0,4},{4,0},{8,12},{12,8},{16,20},{20,16},{24,28},{28,24},{1,5},{5... | collective-permute-start | bytes 884744 | tf_op jit(solution)/shard_map/ppermute | solution.py:433

commit v12 on v11

--- a/solution.py
+++ b/solution.py
@@ -210,8 +210,8 @@
 def forward_kernel(peers, heads, rows, bq, bk, kept, me_s, *refs):
     blocks = refs[:peers]
     if kept:
-        p_list, top_list = refs[peers + 6:peers + 8]
-        refs = refs[:peers + 6] + refs[peers + 8:]
+        p_list, top_list = refs[peers + 6], refs[-1]
+        refs = refs[:peers + 6] + refs[peers + 7:-1]
     v_ref, qx_ref, kx_ref, kt_ref, rows_ref, log_ref = refs[peers:peers + 6]
     plan_q, plan_k, count_ref, own_q, own_k, own_count = refs[peers + 6:peers + 12]
     vt_ref, out_ref, doc_ref, sum_ref, s0, top0, s1, top1 = refs[peers + 12:]
@@ -284,13 +284,20 @@
     total_p = sum_ref[...]
     rows_ref[...] = (out_ref[...] / total_p).T
     log_ref[...] = log_ref[...] + jnp.log2(total_p)
+    if kept:
+
+        @pl.loop(0, 2 * count_ref[1])
+        def _(now):
+            share = jnp.exp2(top_list[now] - log_ref[:, aligned(plan_q[now], bq)])
+            for strip in range(0, bk, STRIP):
+                part = slice(strip, strip + STRIP)
+                p_list[now, part, :] = (p_list[now, part, :].astype(jnp.float32) * share).astype(jnp.bfloat16)
 
 
 def backward_kernel(listed, heads, rows, bq, bk, kept, me_s, plan_q, plan_k, count_ref, v_ref,
                     qx_ref, kx_ref, kt_ref, rows_ref, log_ref, *refs):
     if kept:
-        p_list, top_list = refs[:2]
-        refs = refs[2:]
+        p_list, refs = refs[0], refs[1:]
     peers = len(listed)
     blocks = refs[:peers]
     results = refs[peers:peers + heads]
@@ -318,25 +325,23 @@
         p_ref, ds_ref = buffer
         queries = aligned(qi, bq)
         log_row, dot_row = log_ref[:, queries], dot_ref[:, queries]
-        if kept:
-            share = jnp.exp2(top_list[now] - log_row)
         for strip in range(0, bk, STRIP):
             part = slice(strip, strip + STRIP)
             keys = aligned(ki * (bk // STRIP) + strip // STRIP, STRIP)
             if kept:
-                p = p_list[now, part, :].astype(jnp.float32) * share
+                p = p_list[now, part, :].astype(jnp.float32)
             else:
                 p = jnp.exp2(dot32(kx_ref[keys, :], qx_ref[queries, :], NT) * factor - log_row)
                 if diagonal:
                     p = jnp.where(at_or_before(qi * bq, ki * bk + strip, (STRIP, bq)), p, 0.0)
-            p_ref[part, :] = p.astype(jnp.bfloat16)
+                p_ref[part, :] = p.astype(jnp.bfloat16)
             dp = dot32(v_ref[keys, :], g_ref[queries, :], NT)
             ds_ref[part, :] = (p * (dp - dot_row)).astype(jnp.bfloat16)
 
     def late(now, qi, ki, buffer):
         p_ref, ds_ref = buffer
         keys, queries = aligned(ki, bk), aligned(qi, bq)
-        dv_acc[keys, :] += dot32(p_ref[...], g_ref[queries, :])
+        dv_acc[keys, :] += dot32(p_list[now] if kept else p_ref[...], g_ref[queries, :])
         dk_acc[keys, :] += dot32(ds_ref[...], qx_ref[queries, :HD])
         dq_acc[:, queries] += dot32(kt_ref[:, keys], ds_ref[...])
 
@@ -375,10 +380,6 @@
         jax.ShapeDtypeStruct((total, HD), jnp.float32),
         jax.ShapeDtypeStruct((1, total), jnp.float32),
     ]
-    kept = keeps_list(total, peers, heads)
-    if kept:
-        vectors.append(jax.ShapeDtypeStruct((*own_plan[0], bk, bq), jnp.bfloat16))
-        vectors.append(jax.ShapeDtypeStruct((*own_plan[0], 1, bq), jnp.float32))
     scratch = [
         pltpu.VMEM((HD + ONES_ROWS, total), jnp.bfloat16),
         pltpu.VMEM((HD, total), jnp.float32),
@@ -386,6 +387,10 @@
         pltpu.VMEM((1, total), jnp.float32),
         *[pltpu.VMEM((bk, bq), jnp.float32), pltpu.VMEM((1, bq), jnp.float32)] * 2,
     ]
+    kept = keeps_list(total, peers, heads)
+    if kept:
+        vectors.append(jax.ShapeDtypeStruct((*own_plan[0], bk, bq), jnp.bfloat16))
+        scratch.append(pltpu.VMEM((*own_plan[0], 1, bq), jnp.float32))
     return pl.pallas_call(
         functools.partial(forward_kernel, peers, heads, rows, bq, bk, kept),
         in_specs=[SMEM_SPEC] + [VMEM_SPEC] * peers,

time: 125 us -> 127 us (1.016); the launches traced: 125 us -> 125 us
  Pallas kernels: 38.5 us -> 40.6 us
  waiting for transfers between devices: 50.2 us -> 48.2 us
    pallas_call x1, Pallas kernels: 16.2 us -> 18.1 us  [attention_forward(): pl.pallas_call(functools.partial(forward_kernel, peers, heads, rows, bq,...]
    ppermute x3, waiting for transfers between devices: 4.43 us -> 2.5 us  [pass_on(): lax.ppermute(x, 'head', [(i, (i + 1) % groups) for i in range(groups)])]
  transfers between devices with their start and end apart: 24 -> 24, of which waited for: 16 -> 16; matrix products, arithmetic and copies ran while one was open for 4% -> 4% of each run, Pallas kernels for 17% -> 18%
where the time goes in v12:
time: 127 us; the launch traced here: 125 us
  waiting for transfers between devices  48.2 us (38%)
  Pallas kernels  40.6 us (32%)
  starting transfers between devices  24 us (19%)
  local copies, waits for them, and re-layouts  11.8 us (9%)
    ppermute x21, waiting for transfers between devices, exchange(): lax.ppermute(x, 'seq', [(i, i ^ d) for i in range(peers)])  45.7 us
    ppermute x21, starting transfers between devices, exchange(): lax.ppermute(x, 'seq', [(i, i ^ d) for i in range(peers)])  19.5 us
    pallas_call x1, Pallas kernels, attention_forward(): pl.pallas_call(functools.partial(forward_kernel, peers, heads, rows, bq,...  18.1 us
    pallas_call x1, Pallas kernels, attention_backward(): pl.pallas_call(functools.partial(backward_kernel, listed, heads, rows, bq...  14.6 us
    unnamed x26, local copies, waits for them, and re-layouts  6.98 us
    dynamic_slice x1, local copies, waits for them, and re-layouts, per_device(): lax.dynamic_slice_in_dim(out_weight, block * width, width, 1)  4.79 us
    ppermute x3, starting transfers between devices, pass_on(): lax.ppermute(x, 'head', [(i, (i + 1) % groups) for i in range(groups)])  4.43 us
    pallas_call x3, Pallas kernels, project(): pl.pallas_call(functools.partial(project_kernel, acc is None), in_specs=[...  3.06 us
  transfers between devices with their start and end apart: 24, of which 16 were waited for; matrix products, arithmetic and copies ran while one was open for 4% of the time, Pallas kernels for 18%

profile of v12, /device:TPU:0, one launch (start us, length us, event | category | flops | bytes accessed | tf_op | source)
XLA Modules:
  0.0 125.4 jit_solution(9252595123009745045)
XLA Ops:
  0.6 3.1 %collective-permute-start = (bf16[384,1024]{1,0:T(8,128)(2,1)}, bf16[384,1024]{1,0:T(8,128)(2,1)S(1)}, u32[]{:S(2)}, u32[]{:S(2)}) collective-permute-start(bf16[384,1024]{1,0:T(8,128)(2,1)} %o_ref.1), channel_id=1, source_target_pairs={{0,1},{1,2},{2,3},{3,0},{4,5},{5,6},{6,7},{7,4},{8,9},{9,10},{10,1... | collective-permute-start | bytes 2359304 | tf_op jit(solution)/shard_map/ppermute | solution.py:441
  3.7 1.1 copy-done
  4.8 1.1 copy-done.1
  6.0 1.1 copy-done.2
  7.1 0.7 copy-done.4
  7.8 1.7 %shard_map.85 = (bf16[1168,128]{1,0:T(8,128)(2,1)S(1)}, bf16[1168,128]{1,0:T(8,128)(2,1)S(1)}, bf16[1168,128]{1,0:T(8,128)(2,1)}, bf16[1168,128]{1,0:T(8,128)(2,...) custom-call(s32[1]{0:T(128)} %bitcast.me_s, ...), custom_call_target="tpu_custom_call" | custom-call | tf_op jit(solution)/shard_map/pallas_call | solution.py:69
  9.5 0.7 copy-done.5
  10.2 0.7 copy-done.7
  10.9 0.7 copy-done.9
  11.7 0.7 copy-done.11
  12.4 1.5 %collective-permute-start.1 = (bf16[1168,128]{1,0:T(8,128)(2,1)}, bf16[1168,128]{1,0:T(8,128)(2,1)S(1)}, u32[]{:S(2)}, u32[]{:S(2)}) collective-permute-start(bf16[1168,128]{1,0:T(8,128)(2,1)} %get-tuple-element.57), channel_id=1, source_target_pairs={{0,8},{4,12},{8,0},{12,4},{16,24},{20,28},{24,16},{28,20},{1,9},{5... | collective-permute-start | bytes 897032 | tf_op jit(solution)/shard_map/ppermute | solution.py:438
  13.9 1.5 %collective-permute-start.2 = (bf16[1168,128]{1,0:T(8,128)(2,1)}, bf16[1168,128]{1,0:T(8,128)(2,1)S(1)}, u32[]{:S(2)}, u32[]{:S(2)}) collective-permute-start(bf16[1168,128]{1,0:T(8,128)(2,1)} %get-tuple-element.58), channel_id=1, source_target_pairs={{0,16},{4,20},{8,24},{12,28},{16,0},{20,4},{24,8},{28,12},{1,17},{... | collective-permute-start | bytes 897032 | tf_op jit(solution)/shard_map/ppermute | solution.py:438
  15.4 4.8 %constant_dynamic-slice_fusion = (bf16[1024,1024]{1,0:T(8,128)(2,1)S(1)}, bf16[1024,1024]{1,0:T(8,128)(2,1)S(1)}, bf16[1024,1024]{1,0:T(8,128)(2,1)S(1)}, bf16[1024,1024]{1,0:T(8,128)(2,1)S(1)}) fusion(bf16[1024,4096]{1,0:T(8,128)(2,1)} %param.10, s32[]{:T(128)S(6)} %select_n.15, s32[]{:T(128)S(6)} %select_n.13, s32[]{:T(128)S(6)} %select_n.12, s32[]{:T(128)S(6)} %select_n.14), kind=kLoop, calls=%fused_computation | loop fusion | bytes 16777232 | tf_op jit(solution)/shard_map/dynamic_slice | solution.py:462
  20.3 1.0 shard_map.86.refs_0_
  21.3 1.1 collective-permute-done.2.refs_4_
  22.4 1.1 collective-permute-done.o_ref
  23.5 0.5 collective-permute-start.3
  24.0 2.0 %collective-permute-start.4 = (bf16[1168,128]{1,0:T(8,128)(2,1)S(1)}, bf16[1168,128]{1,0:T(8,128)(2,1)S(1)}, u32[]{:S(2)}, u32[]{:S(2)}) collective-permute-start(bf16[1168,128]{1,0:T(8,128)(2,1)S(1)} %copy-done.12), channel_id=1, source_target_pairs={{0,24},{4,28},{8,16},{12,20},{16,8},{20,12},{24,0},{28,4},{1,25},{... | collective-permute-start | bytes 897032 | tf_op jit(solution)/shard_map/ppermute | solution.py:438
  26.0 2.2 %collective-permute-start.6 = (bf16[1168,128]{1,0:T(8,128)(2,1)S(1)}, bf16[1168,128]{1,0:T(8,128)(2,1)S(1)}, u32[]{:S(2)}, u32[]{:S(2)}) collective-permute-start(bf16[1168,128]{1,0:T(8,128)(2,1)S(1)} %copy-done.8), channel_id=1, source_target_pairs={{0,20},{4,16},{8,28},{12,24},{16,4},{20,0},{24,12},{28,8},{1,21},{... | collective-permute-start | bytes 897032 | tf_op jit(solution)/shard_map/ppermute | solution.py:438
  28.1 6.9 %collective-permute-done.4.refs_6_ = bf16[1168,128]{1,0:T(8,128)(2,1)S(1)} collective-permute-done((bf16[1168,128]{1,0:T(8,128)(2,1)S(1)}, bf16[1168,128]{1,0:T(8,128)(2,1)S(1)}, u32[]{:S(2)}, u32[]{:S(2)}) %collective-permute-start.4) | collective-permute-done | bytes 299040 | tf_op jit(solution)/shard_map/ppermute | solution.py:438
  35.0 1.0 shard_map.87.refs_0_
  36.0 3.9 %collective-permute-done.5.refs_7_ = bf16[1168,128]{1,0:T(8,128)(2,1)S(1)} collective-permute-done((bf16[1168,128]{1,0:T(8,128)(2,1)S(1)}, bf16[1168,128]{1,0:T(8,128)(2,1)S(1)}, u32[]{:S(2)}, u32[]{:S(2)}) %collective-permute-start.5) | collective-permute-done | bytes 299040 | tf_op jit(solution)/shard_map/ppermute | solution.py:438
  39.9 5.5 %collective-permute-done.6.refs_5_ = bf16[1168,128]{1,0:T(8,128)(2,1)S(1)} collective-permute-done((bf16[1168,128]{1,0:T(8,128)(2,1)S(1)}, bf16[1168,128]{1,0:T(8,128)(2,1)S(1)}, u32[]{:S(2)}, u32[]{:S(2)}) %collective-permute-start.6) | collective-permute-done | bytes 299040 | tf_op jit(solution)/shard_map/ppermute | solution.py:438
  45.4 0.9 collective-permute-start.9
  46.3 18.1 %shard_map.88 = (bf16[3072,128]{1,0:T(8,128)(2,1)S(1)}, bf16[3072,256]{1,0:T(8,128)(2,1)S(1)}, bf16[3072,256]{1,0:T(8,128)(2,1)S(1)}, bf16[128,3072]{1,0:T(8,128...) custom-call(s32[1]{0:T(128)} %bitcast.me_s, ...), custom_call_target="tpu_custom_call" | custom-call | flops 1811939328 | bytes 6291456 | tf_op jit(solution)/shard_map/pallas_call | solution.py:394
  64.4 1.0 shard_map.89.acc_ref
  65.5 1.4 %collective-permute-done.9.o_ref = bf16[384,1024]{1,0:T(8,128)(2,1)S(1)} collective-permute-done((bf16[384,1024]{1,0:T(8,128)(2,1)S(1)}, bf16[384,1024]{1,0:T(8,128)(2,1)S(1)}, u32[]{:S(2)}, u32[]{:S(2)}) %collective-permute-start.9) | collective-permute-done | bytes 786464 | tf_op jit(solution)/shard_map/ppermute | solution.py:441
  66.9 1.0 shard_map.90
  67.9 2.2 %collective-permute-start.10 = (bf16[384,128]{1,0:T(8,128)(2,1)S(1)}, bf16[384,128]{1,0:T(8,128)(2,1)S(1)}, u32[]{:S(2)}, u32[]{:S(2)}) collective-permute-start(bf16[384,128]{1,0:T(8,128)(2,1)S(1)} %get-tuple-element.93), channel_id=1, source_target_pairs={{0,24},{4,28},{8,16},{12,20},{16,8},{20,12},{24,0},{28,4},{1,25},{... | collective-permute-start | bytes 294920 | tf_op jit(solution)/shard_map/ppermute | solution.py:438
  70.1 0.6 collective-permute-start.12
  70.7 1.5 %collective-permute-start.13 = (bf16[384,128]{1,0:T(8,128)(2,1)S(1)}, bf16[384,128]{1,0:T(8,128)(2,1)S(1)}, u32[]{:S(2)}, u32[]{:S(2)}) collective-permute-start(bf16[384,128]{1,0:T(8,128)(2,1)S(1)} %get-tuple-element.96), channel_id=1, source_target_pairs={{0,16},{4,20},{8,24},{12,28},{16,0},{20,4},{24,8},{28,12},{1,17},{... | collective-permute-start | bytes 294920 | tf_op jit(solution)/shard_map/ppermute | solution.py:438
  72.2 1.1 collective-permute-start.14
  73.5 0.4 collective-permute-start.15
  73.9 2.3 %collective-permute-done.11.refs_2_ = bf16[384,128]{1,0:T(8,128)(2,1)S(1)} collective-permute-done((bf16[384,128]{1,0:T(8,128)(2,1)S(1)}, bf16[384,128]{1,0:T(8,128)(2,1)S(1)}, u32[]{:S(2)}, u32[]{:S(2)}) %collective-permute-start.11) | collective-permute-done | bytes 98336 | tf_op jit(solution)/shard_map/ppermute | solution.py:438
  76.2 1.5 %collective-permute-done.12.refs_3_ = bf16[384,128]{1,0:T(8,128)(2,1)S(1)} collective-permute-done((bf16[384,128]{1,0:T(8,128)(2,1)S(1)}, bf16[384,128]{1,0:T(8,128)(2,1)S(1)}, u32[]{:S(2)}, u32[]{:S(2)}) %collective-permute-start.12) | collective-permute-done | bytes 98336 | tf_op jit(solution)/shard_map/ppermute | solution.py:438
  77.7 1.7 %collective-permute-done.14.refs_5_ = bf16[384,128]{1,0:T(8,128)(2,1)S(1)} collective-permute-done((bf16[384,128]{1,0:T(8,128)(2,1)S(1)}, bf16[384,128]{1,0:T(8,128)(2,1)S(1)}, u32[]{:S(2)}, u32[]{:S(2)}) %collective-permute-start.14) | collective-permute-done | bytes 98336 | tf_op jit(solution)/shard_map/ppermute | solution.py:438
  79.4 0.4 collective-permute-done.15.refs_6_
  79.8 14.6 %shard_map.91 = (bf16[1152,128]{1,0:T(8,128)(2,1)S(1)}, bf16[1152,128]{1,0:T(8,128)(2,1)S(1)}, bf16[1152,128]{1,0:T(8,128)(2,1)S(1)}, bf16[1152,128]{1,0:T(8,128...) custom-call(s32[1]{0:T(128)} %bitcast.me_s, ...), custom_call_target="tpu_custom_call" | custom-call | flops 3019898880 | bytes 6291456 | tf_op jit(solution)/shard_map/pallas_call | solution.py:420
  94.4 2.2 %collective-permute-start.17 = (bf16[1152,128]{1,0:T(8,128)(2,1)S(1)}, bf16[1152,128]{1,0:T(8,128)(2,1)S(1)}, u32[]{:S(2)}, u32[]{:S(2)}) collective-permute-start(bf16[1152,128]{1,0:T(8,128)(2,1)S(1)} %get-tuple-element.101), channel_id=1, source_target_pairs={{0,24},{4,28},{8,16},{12,20},{16,8},{20,12},{24,0},{28,4},{1,25},{... | collective-permute-start | bytes 884744 | tf_op jit(solution)/shard_map/ppermute | solution.py:438
  96.8 1.2 collective-permute-start.19
  98.1 1.5 %collective-permute-start.20 = (bf16[1152,128]{1,0:T(8,128)(2,1)S(1)}, bf16[1152,128]{1,0:T(8,128)(2,1)S(1)}, u32[]{:S(2)}, u32[]{:S(2)}) collective-permute-start(bf16[1152,128]{1,0:T(8,128)(2,1)S(1)} %get-tuple-element.104), channel_id=1, source_target_pairs={{0,16},{4,20},{8,24},{12,28},{16,0},{20,4},{24,8},{28,12},{1,17},{... | collective-permute-start | bytes 884744 | tf_op jit(solution)/shard_map/ppermute | solution.py:438
  99.8 5.5 %collective-permute-done.17.refs_0_ = bf16[1152,128]{1,0:T(8,128)(2,1)S(1)} collective-permute-done((bf16[1152,128]{1,0:T(8,128)(2,1)S(1)}, bf16[1152,128]{1,0:T(8,128)(2,1)S(1)}, u32[]{:S(2)}, u32[]{:S(2)}) %collective-permute-start.17) | collective-permute-done | bytes 294944 | tf_op jit(solution)/shard_map/ppermute | solution.py:438
  105.3 5.0 %collective-permute-done.18.refs_1_ = bf16[1152,128]{1,0:T(8,128)(2,1)S(1)} collective-permute-done((bf16[1152,128]{1,0:T(8,128)(2,1)S(1)}, bf16[1152,128]{1,0:T(8,128)(2,1)S(1)}, u32[]{:S(2)}, u32[]{:S(2)}) %collective-permute-start.18) | collective-permute-done | bytes 294944 | tf_op jit(solution)/shard_map/ppermute | solution.py:438
  110.4 1.0 collective-permute-start.23
  111.4 6.3 %collective-permute-done.19.refs_2_ = bf16[1152,128]{1,0:T(8,128)(2,1)S(1)} collective-permute-done((bf16[1152,128]{1,0:T(8,128)(2,1)S(1)}, bf16[1152,128]{1,0:T(8,128)(2,1)S(1)}, u32[]{:S(2)}, u32[]{:S(2)}) %collective-permute-start.19) | collective-permute-done | bytes 294944 | tf_op jit(solution)/shard_map/ppermute | solution.py:438
  117.7 4.6 %collective-permute-done.21.refs_4_ = bf16[1152,128]{1,0:T(8,128)(2,1)S(1)} collective-permute-done((bf16[1152,128]{1,0:T(8,128)(2,1)S(1)}, bf16[1152,128]{1,0:T(8,128)(2,1)S(1)}, u32[]{:S(2)}, u32[]{:S(2)}) %collective-permute-start.21) | collective-permute-done | bytes 294944 | tf_op jit(solution)/shard_map/ppermute | solution.py:438
  122.3 1.0 collective-permute-done.22.refs_5_
  123.3 2.1 %shard_map.92 = (bf16[384,1024]{1,0:T(8,128)(2,1)}, bf16[384,1024]{1,0:T(8,128)(2,1)}, bf16[384,1024]{1,0:T(8,128)(2,1)}) custom-call(s32[1]{0:T(128)} %bitcast.me_s, bf16[1152,128]{1,0:T(8,128)(2,1)S(1)} %collective-permute-done.17.refs_0_, bf16[1152,128]{1,0:T(8,128)(2,1)S(1)} %collective-permute-done.18.refs_1_, ...), custom_call_target="tpu_custom_call" | custom-call | tf_op jit(solution)/shard_map/pallas_call | solution.py:90
  (35 shorter events, 0.7 us)
Async XLA Ops:
  0.6 22.9 %collective-permute-start = (bf16[384,1024]{1,0:T(8,128)(2,1)}, bf16[384,1024]{1,0:T(8,128)(2,1)S(1)}, u32[]{:S(2)}, u32[]{:S(2)}) collective-permute-start(bf16[384,1024]{1,0:T(8,128)(2,1)} %o_ref.1), channel_id=1, source_target_pairs={{0,1},{1,2},{2,3},{3,0},{4,5},{5,6},{6,7},{7,4},{8,9},{9,10},{10,1... | collective-permute-start | bytes 2359304 | tf_op jit(solution)/shard_map/ppermute | solution.py:441
  3.7 1.1 copy-start
  4.8 1.1 copy-start.1
  6.0 1.1 copy-start.2
  7.1 0.7 copy-start.4
  9.5 0.7 copy-start.5
  10.2 0.7 copy-start.7
  10.9 0.7 copy-start.9
  11.7 0.7 copy-start.11
  12.4 8.9 %collective-permute-start.1 = (bf16[1168,128]{1,0:T(8,128)(2,1)}, bf16[1168,128]{1,0:T(8,128)(2,1)S(1)}, u32[]{:S(2)}, u32[]{:S(2)}) collective-permute-start(bf16[1168,128]{1,0:T(8,128)(2,1)} %get-tuple-element.57), channel_id=1, source_target_pairs={{0,8},{4,12},{8,0},{12,4},{16,24},{20,28},{24,16},{28,20},{1,9},{5... | collective-permute-start | bytes 897032 | tf_op jit(solution)/shard_map/ppermute | solution.py:438
  13.9 8.5 %collective-permute-start.2 = (bf16[1168,128]{1,0:T(8,128)(2,1)}, bf16[1168,128]{1,0:T(8,128)(2,1)S(1)}, u32[]{:S(2)}, u32[]{:S(2)}) collective-permute-start(bf16[1168,128]{1,0:T(8,128)(2,1)} %get-tuple-element.58), channel_id=1, source_target_pairs={{0,16},{4,20},{8,24},{12,28},{16,0},{20,4},{24,8},{28,12},{1,17},{... | collective-permute-start | bytes 897032 | tf_op jit(solution)/shard_map/ppermute | solution.py:438
  15.4 4.8 %copy-start.3 = (bf16[384,1024]{1,0:T(8,128)(2,1)S(1)}, bf16[384,1024]{1,0:T(8,128)(2,1)}, u32[]{:S(2)}) copy-start(bf16[384,1024]{1,0:T(8,128)(2,1)} %o_ref.1) | copy-start | bytes 2359300
  20.2 3.7 %copy-start.12 = (bf16[1168,128]{1,0:T(8,128)(2,1)S(1)}, bf16[1168,128]{1,0:T(8,128)(2,1)}, u32[]{:S(2)}) copy-start(bf16[1168,128]{1,0:T(8,128)(2,1)} %copy-done.11) | copy-start | bytes 897028
  20.2 5.7 %copy-start.10 = (bf16[1168,128]{1,0:T(8,128)(2,1)S(1)}, bf16[1168,128]{1,0:T(8,128)(2,1)}, u32[]{:S(2)}) copy-start(bf16[1168,128]{1,0:T(8,128)(2,1)} %copy-done.9) | copy-start | bytes 897028
  20.2 5.7 %copy-start.8 = (bf16[1168,128]{1,0:T(8,128)(2,1)S(1)}, bf16[1168,128]{1,0:T(8,128)(2,1)}, u32[]{:S(2)}) copy-start(bf16[1168,128]{1,0:T(8,128)(2,1)} %copy-done.7) | copy-start | bytes 897028
  20.3 7.9 %copy-start.6 = (bf16[1168,128]{1,0:T(8,128)(2,1)S(1)}, bf16[1168,128]{1,0:T(8,128)(2,1)}, u32[]{:S(2)}) copy-start(bf16[1168,128]{1,0:T(8,128)(2,1)} %copy-done.5) | copy-start | bytes 897028
  23.5 21.9 %collective-permute-start.3 = (bf16[384,1024]{1,0:T(8,128)(2,1)S(1)}, bf16[384,1024]{1,0:T(8,128)(2,1)S(1)}, u32[]{:S(2)}, u32[]{:S(2)}) collective-permute-start(bf16[384,1024]{1,0:T(8,128)(2,1)S(1)} %collective-permute-done.o_ref), channel_id=1, source_target_pairs={{0,1},{1,2},{2,3},{3,0},{4,5},{5,6},{6,7},{7,4},{8,9},{9,10},{10,1... | collective-permute-start | bytes 2359304 | tf_op jit(solution)/shard_map/ppermute | solution.py:441
  24.0 11.0 %collective-permute-start.4 = (bf16[1168,128]{1,0:T(8,128)(2,1)S(1)}, bf16[1168,128]{1,0:T(8,128)(2,1)S(1)}, u32[]{:S(2)}, u32[]{:S(2)}) collective-permute-start(bf16[1168,128]{1,0:T(8,128)(2,1)S(1)} %copy-done.12), channel_id=1, source_target_pairs={{0,24},{4,28},{8,16},{12,20},{16,8},{20,12},{24,0},{28,4},{1,25},{... | collective-permute-start | bytes 897032 | tf_op jit(solution)/shard_map/ppermute | solution.py:438
  25.9 14.0 %collective-permute-start.5 = (bf16[1168,128]{1,0:T(8,128)(2,1)S(1)}, bf16[1168,128]{1,0:T(8,128)(2,1)S(1)}, u32[]{:S(2)}, u32[]{:S(2)}) collective-permute-start(bf16[1168,128]{1,0:T(8,128)(2,1)S(1)} %copy-done.10), channel_id=1, source_target_pairs={{0,28},{4,24},{8,20},{12,16},{16,12},{20,8},{24,4},{28,0},{1,29},{... | collective-permute-start | bytes 897032 | tf_op jit(solution)/shard_map/ppermute | solution.py:438
  26.0 19.5 %collective-permute-start.6 = (bf16[1168,128]{1,0:T(8,128)(2,1)S(1)}, bf16[1168,128]{1,0:T(8,128)(2,1)S(1)}, u32[]{:S(2)}, u32[]{:S(2)}) collective-permute-start(bf16[1168,128]{1,0:T(8,128)(2,1)S(1)} %copy-done.8), channel_id=1, source_target_pairs={{0,20},{4,16},{8,28},{12,24},{16,4},{20,0},{24,12},{28,8},{1,21},{... | collective-permute-start | bytes 897032 | tf_op jit(solution)/shard_map/ppermute | solution.py:438
  28.1 17.3 %collective-permute-start.7 = (bf16[1168,128]{1,0:T(8,128)(2,1)S(1)}, bf16[1168,128]{1,0:T(8,128)(2,1)S(1)}, u32[]{:S(2)}, u32[]{:S(2)}) collective-permute-start(bf16[1168,128]{1,0:T(8,128)(2,1)S(1)} %copy-done.6), channel_id=1, source_target_pairs={{0,12},{4,8},{8,4},{12,0},{16,28},{20,24},{24,20},{28,16},{1,13},{... | collective-permute-start | bytes 897032 | tf_op jit(solution)/shard_map/ppermute | solution.py:438
  35.0 10.4 %collective-permute-start.8 = (bf16[1168,128]{1,0:T(8,128)(2,1)S(1)}, bf16[1168,128]{1,0:T(8,128)(2,1)S(1)}, u32[]{:S(2)}, u32[]{:S(2)}) collective-permute-start(bf16[1168,128]{1,0:T(8,128)(2,1)S(1)} %get-tuple-element.65), channel_id=1, source_target_pairs={{0,4},{4,0},{8,12},{12,8},{16,20},{20,16},{24,28},{28,24},{1,5},{5... | collective-permute-start | bytes 897032 | tf_op jit(solution)/shard_map/ppermute | solution.py:438
  45.4 21.4 %collective-permute-start.9 = (bf16[384,1024]{1,0:T(8,128)(2,1)S(1)}, bf16[384,1024]{1,0:T(8,128)(2,1)S(1)}, u32[]{:S(2)}, u32[]{:S(2)}) collective-permute-start(bf16[384,1024]{1,0:T(8,128)(2,1)S(1)} %collective-permute-done.3.o_ref), channel_id=1, source_target_pairs={{0,1},{1,2},{2,3},{3,0},{4,5},{5,6},{6,7},{7,4},{8,9},{9,10},{10,1... | collective-permute-start | bytes 2359304 | tf_op jit(solution)/shard_map/ppermute | solution.py:441
  67.9 5.6 %collective-permute-start.10 = (bf16[384,128]{1,0:T(8,128)(2,1)S(1)}, bf16[384,128]{1,0:T(8,128)(2,1)S(1)}, u32[]{:S(2)}, u32[]{:S(2)}) collective-permute-start(bf16[384,128]{1,0:T(8,128)(2,1)S(1)} %get-tuple-element.93), channel_id=1, source_target_pairs={{0,24},{4,28},{8,16},{12,20},{16,8},{20,12},{24,0},{28,4},{1,25},{... | collective-permute-start | bytes 294920 | tf_op jit(solution)/shard_map/ppermute | solution.py:438
  70.1 6.1 %collective-permute-start.11 = (bf16[384,128]{1,0:T(8,128)(2,1)S(1)}, bf16[384,128]{1,0:T(8,128)(2,1)S(1)}, u32[]{:S(2)}, u32[]{:S(2)}) collective-permute-start(bf16[384,128]{1,0:T(8,128)(2,1)S(1)} %get-tuple-element.94), channel_id=1, source_target_pairs={{0,28},{4,24},{8,20},{12,16},{16,12},{20,8},{24,4},{28,0},{1,29},{... | collective-permute-start | bytes 294920 | tf_op jit(solution)/shard_map/ppermute | solution.py:438
  70.1 7.5 %collective-permute-start.12 = (bf16[384,128]{1,0:T(8,128)(2,1)S(1)}, bf16[384,128]{1,0:T(8,128)(2,1)S(1)}, u32[]{:S(2)}, u32[]{:S(2)}) collective-permute-start(bf16[384,128]{1,0:T(8,128)(2,1)S(1)} %get-tuple-element.95), channel_id=1, source_target_pairs={{0,8},{4,12},{8,0},{12,4},{16,24},{20,28},{24,16},{28,20},{1,9},{5... | collective-permute-start | bytes 294920 | tf_op jit(solution)/shard_map/ppermute | solution.py:438
  70.7 6.9 %collective-permute-start.13 = (bf16[384,128]{1,0:T(8,128)(2,1)S(1)}, bf16[384,128]{1,0:T(8,128)(2,1)S(1)}, u32[]{:S(2)}, u32[]{:S(2)}) collective-permute-start(bf16[384,128]{1,0:T(8,128)(2,1)S(1)} %get-tuple-element.96), channel_id=1, source_target_pairs={{0,16},{4,20},{8,24},{12,28},{16,0},{20,4},{24,8},{28,12},{1,17},{... | collective-permute-start | bytes 294920 | tf_op jit(solution)/shard_map/ppermute | solution.py:438
  72.2 7.2 %collective-permute-start.14 = (bf16[384,128]{1,0:T(8,128)(2,1)S(1)}, bf16[384,128]{1,0:T(8,128)(2,1)S(1)}, u32[]{:S(2)}, u32[]{:S(2)}) collective-permute-start(bf16[384,128]{1,0:T(8,128)(2,1)S(1)} %get-tuple-element.97), channel_id=1, source_target_pairs={{0,12},{4,8},{8,4},{12,0},{16,28},{20,24},{24,20},{28,16},{1,13},{... | collective-permute-start | bytes 294920 | tf_op jit(solution)/shard_map/ppermute | solution.py:438
  73.5 6.3 %collective-permute-start.15 = (bf16[384,128]{1,0:T(8,128)(2,1)S(1)}, bf16[384,128]{1,0:T(8,128)(2,1)S(1)}, u32[]{:S(2)}, u32[]{:S(2)}) collective-permute-start(bf16[384,128]{1,0:T(8,128)(2,1)S(1)} %get-tuple-element.98), channel_id=1, source_target_pairs={{0,20},{4,16},{8,28},{12,24},{16,4},{20,0},{24,12},{28,8},{1,21},{... | collective-permute-start | bytes 294920 | tf_op jit(solution)/shard_map/ppermute | solution.py:438
  76.2 3.6 %collective-permute-start.16 = (bf16[384,128]{1,0:T(8,128)(2,1)S(1)}, bf16[384,128]{1,0:T(8,128)(2,1)S(1)}, u32[]{:S(2)}, u32[]{:S(2)}) collective-permute-start(bf16[384,128]{1,0:T(8,128)(2,1)S(1)} %get-tuple-element.100), channel_id=1, source_target_pairs={{0,4},{4,0},{8,12},{12,8},{16,20},{20,16},{24,28},{28,24},{1,5},{5... | collective-permute-start | bytes 294920 | tf_op jit(solution)/shard_map/ppermute | solution.py:438
  94.4 10.9 %collective-permute-start.17 = (bf16[1152,128]{1,0:T(8,128)(2,1)S(1)}, bf16[1152,128]{1,0:T(8,128)(2,1)S(1)}, u32[]{:S(2)}, u32[]{:S(2)}) collective-permute-start(bf16[1152,128]{1,0:T(8,128)(2,1)S(1)} %get-tuple-element.101), channel_id=1, source_target_pairs={{0,24},{4,28},{8,16},{12,20},{16,8},{20,12},{24,0},{28,4},{1,25},{... | collective-permute-start | bytes 884744 | tf_op jit(solution)/shard_map/ppermute | solution.py:438
  96.6 13.7 %collective-permute-start.18 = (bf16[1152,128]{1,0:T(8,128)(2,1)S(1)}, bf16[1152,128]{1,0:T(8,128)(2,1)S(1)}, u32[]{:S(2)}, u32[]{:S(2)}) collective-permute-start(bf16[1152,128]{1,0:T(8,128)(2,1)S(1)} %get-tuple-element.102), channel_id=1, source_target_pairs={{0,28},{4,24},{8,20},{12,16},{16,12},{20,8},{24,4},{28,0},{1,29},{... | collective-permute-start | bytes 884744 | tf_op jit(solution)/shard_map/ppermute | solution.py:438
  96.8 20.9 %collective-permute-start.19 = (bf16[1152,128]{1,0:T(8,128)(2,1)S(1)}, bf16[1152,128]{1,0:T(8,128)(2,1)S(1)}, u32[]{:S(2)}, u32[]{:S(2)}) collective-permute-start(bf16[1152,128]{1,0:T(8,128)(2,1)S(1)} %get-tuple-element.103), channel_id=1, source_target_pairs={{0,8},{4,12},{8,0},{12,4},{16,24},{20,28},{24,16},{28,20},{1,9},{5... | collective-permute-start | bytes 884744 | tf_op jit(solution)/shard_map/ppermute | solution.py:438
  98.1 19.7 %collective-permute-start.20 = (bf16[1152,128]{1,0:T(8,128)(2,1)S(1)}, bf16[1152,128]{1,0:T(8,128)(2,1)S(1)}, u32[]{:S(2)}, u32[]{:S(2)}) collective-permute-start(bf16[1152,128]{1,0:T(8,128)(2,1)S(1)} %get-tuple-element.104), channel_id=1, source_target_pairs={{0,16},{4,20},{8,24},{12,28},{16,0},{20,4},{24,8},{28,12},{1,17},{... | collective-permute-start | bytes 884744 | tf_op jit(solution)/shard_map/ppermute | solution.py:438
  99.5 22.7 %collective-permute-start.21 = (bf16[1152,128]{1,0:T(8,128)(2,1)S(1)}, bf16[1152,128]{1,0:T(8,128)(2,1)S(1)}, u32[]{:S(2)}, u32[]{:S(2)}) collective-permute-start(bf16[1152,128]{1,0:T(8,128)(2,1)S(1)} %get-tuple-element.105), channel_id=1, source_target_pairs={{0,12},{4,8},{8,4},{12,0},{16,28},{20,24},{24,20},{28,16},{1,13},{... | collective-permute-start | bytes 884744 | tf_op jit(solution)/shard_map/ppermute | solution.py:438
  105.3 17.9 %collective-permute-start.22 = (bf16[1152,128]{1,0:T(8,128)(2,1)S(1)}, bf16[1152,128]{1,0:T(8,128)(2,1)S(1)}, u32[]{:S(2)}, u32[]{:S(2)}) collective-permute-start(bf16[1152,128]{1,0:T(8,128)(2,1)S(1)} %get-tuple-element.106), channel_id=1, source_target_pairs={{0,20},{4,16},{8,28},{12,24},{16,4},{20,0},{24,12},{28,8},{1,21},{... | collective-permute-start | bytes 884744 | tf_op jit(solution)/shard_map/ppermute | solution.py:438
  110.4 12.9 %collective-permute-start.23 = (bf16[1152,128]{1,0:T(8,128)(2,1)S(1)}, bf16[1152,128]{1,0:T(8,128)(2,1)S(1)}, u32[]{:S(2)}, u32[]{:S(2)}) collective-permute-start(bf16[1152,128]{1,0:T(8,128)(2,1)S(1)} %get-tuple-element.108), channel_id=1, source_target_pairs={{0,4},{4,0},{8,12},{12,8},{16,20},{20,16},{24,28},{28,24},{1,5},{5... | collective-permute-start | bytes 884744 | tf_op jit(solution)/shard_map/ppermute | solution.py:438

commit v13 on v11

--- a/solution.py
+++ b/solution.py
@@ -15,12 +15,14 @@
 STRIP = 64
 NEG_LARGE = -1e30
 VMEM_SPARE = 6 * 1024 * 1024
+VMEM_MOST = 56 * 1024 * 1024
 LIST_BYTES = 16 * 1024 * 1024
 
 NN = (((1,), (0,)), ((), ()))
 NT = (((1,), (1,)), ((), ()))
 SMEM_SPEC = pl.BlockSpec(memory_space=pltpu.SMEM)
 VMEM_SPEC = pl.BlockSpec(memory_space=pltpu.VMEM)
+ANY_SPEC = pl.BlockSpec(memory_space=pl.ANY)
 
 
 def dot32(a, b, dims=NN):
@@ -44,7 +46,7 @@
 
 
 def pack_kernel(heads, rows, me_s, q_ref, k_ref, v_ref, doc_ref, *refs):
-    outs, done = refs[:heads], refs[heads]
+    outs, doc_block, done, doc_done = refs[:heads], refs[heads], refs[heads + 1], refs[heads + 2]
     own = lax.rem(me_s[0], heads)
     copies = []
     for d, out in enumerate(outs):
@@ -55,9 +57,10 @@
             copies[-1].start()
     docs = doc_ref[...].astype(jnp.float32)
     docs = jnp.concatenate([docs, jnp.zeros((DOC_ROWS - docs.shape[0], HD), jnp.float32)], axis=0)
-    docs = docs.astype(jnp.bfloat16)
-    for out in outs:
-        out[3 * rows:, :] = docs
+    doc_block[...] = docs.astype(jnp.bfloat16)
+    for d, out in enumerate(outs):
+        copies.append(pltpu.make_async_copy(doc_block, out.at[pl.ds(3 * rows, DOC_ROWS), :], doc_done.at[d]))
+        copies[-1].start()
     for copy in copies:
         copy.wait()
 
@@ -65,35 +68,45 @@
 def pack_heads(me, q, k, v, doc_ids):
     rows, width = q.shape
     heads = width // HD
-    out_shape = [jax.ShapeDtypeStruct((3 * rows + DOC_ROWS, HD), q.dtype)] * heads
     return pl.pallas_call(
         functools.partial(pack_kernel, heads, rows),
-        in_specs=[SMEM_SPEC] + [pl.BlockSpec(memory_space=pltpu.HBM)] * 3 + [VMEM_SPEC],
-        out_specs=[VMEM_SPEC] * heads,
-        out_shape=out_shape,
-        scratch_shapes=[pltpu.SemaphoreType.DMA((heads, 3))],
-        compiler_params=params(out_shape),
+        in_specs=[SMEM_SPEC] + [ANY_SPEC] * 3 + [VMEM_SPEC],
+        out_specs=[ANY_SPEC] * heads,
+        out_shape=[jax.ShapeDtypeStruct((3 * rows + DOC_ROWS, HD), q.dtype)] * heads,
+        scratch_shapes=[
+            pltpu.VMEM((DOC_ROWS, HD), jnp.bfloat16),
+            pltpu.SemaphoreType.DMA((heads, 3)),
+            pltpu.SemaphoreType.DMA((heads,)),
+        ],
+        compiler_params=pltpu.CompilerParams(vmem_limit_bytes=VMEM_MOST),
     )(me, q, k, v, doc_ids.reshape(rows // HD, HD))
 
 
-def unpack_kernel(listed, rows, me_s, *refs):
-    heads = len(listed)
+def unpack_kernel(listed, heads, rows, me_s, *refs):
+    outs, done = refs[-4:-1], refs[-1]
     own = lax.rem(me_s[0], heads)
-    for d, block in zip(listed, refs):
+    copies = []
+    for place, (d, block) in enumerate(zip(listed, refs)):
         columns = aligned(own ^ d, HD)
-        for part in range(3):
-            refs[heads + part][:, columns] = block[part * rows:(part + 1) * rows, :]
-
-
-def unpack_heads(me, listed, blocks, rows):
-    heads = len(blocks)
+        for part, out in enumerate(outs):
+            source = block.at[pl.ds(part * rows, rows), :]
+            copies.append(pltpu.make_async_copy(source, out.at[:, columns], done.at[place, part]))
+            copies[-1].start()
+    for copy in copies:
+        copy.wait()
+
+
+def unpack_heads(me, listed, blocks, rows, heads, partial=()):
+    count = len(blocks)
     return pl.pallas_call(
-        functools.partial(unpack_kernel, listed, rows),
-        in_specs=[SMEM_SPEC] + [VMEM_SPEC] * heads,
-        out_specs=[VMEM_SPEC] * 3,
+        functools.partial(unpack_kernel, listed, heads, rows),
+        in_specs=[SMEM_SPEC] + [VMEM_SPEC] * count + [ANY_SPEC] * len(partial),
+        out_specs=[ANY_SPEC] * 3,
         out_shape=[jax.ShapeDtypeStruct((rows, heads * HD), blocks[0].dtype)] * 3,
-        compiler_params=params([*blocks, *blocks]),
-    )(me, *blocks)
+        scratch_shapes=[pltpu.SemaphoreType.DMA((count, 3))],
+        input_output_aliases={1 + count + i: i for i in range(len(partial))},
+        compiler_params=params([*blocks]),
+    )(me, *blocks, *partial)
 
 
 def project_kernel(first, o_ref, w_ref, *refs):
@@ -476,7 +489,11 @@
 
     results = attention_backward(me_vector, heads, state, far_first, grads)
     returned = exchange_all(results, returning)
-    return tuple(unpack_heads(me_vector, returning, returned, rows))
+    early = [d for d in returning if d == 0 or bin(d >> 1).count("1") > 1]
+    late = [d for d in returning if d not in early]
+    block_of = dict(zip(returning, returned))
+    partial = unpack_heads(me_vector, early, [block_of[d] for d in early], rows, heads)
+    return tuple(unpack_heads(me_vector, late, [block_of[d] for d in late], rows, heads, partial))
 
 
 def solution(mesh):

time: 125 us -> 190 us (1.52)
  Pallas kernels: 38.5 us -> 110 us
  local copies, waits for them, and re-layouts: 11.8 us -> 4.57 us
  waiting for transfers between devices: 50.2 us -> 45.7 us
  starting transfers between devices: 24 us -> 27 us
    pallas_call x1, Pallas kernels: 1.71 us -> 73.5 us  [pack_heads(): pl.pallas_call(functools.partial(pack_kernel, heads, rows), in_specs=[SME...]
    unnamed x26 -> x14, local copies, waits for them, and re-layouts: 6.98 us -> 0.03 us
    ppermute x21, waiting for transfers between devices: 45.8 us -> 43.1 us  [exchange(): lax.ppermute(x, 'seq', [(i, i ^ d) for i in range(peers)])]
  transfers between devices with their start and end apart: 24 -> 24, of which waited for: 16 -> 14; matrix products, arithmetic and copies ran while one was open for 4% -> 2% of each run, Pallas kernels for 17% -> 50%
where the time goes in v13:
time: 190 us; the launch traced here: 189 us
  Pallas kernels  110 us (58%)
  waiting for transfers between devices  45.7 us (24%)
  starting transfers between devices  27 us (14%)
  local copies, waits for them, and re-layouts  4.57 us (2%)
    pallas_call x1, Pallas kernels, pack_heads(): pl.pallas_call(functools.partial(pack_kernel, heads, rows), in_specs=[SME...  73.5 us
    ppermute x21, waiting for transfers between devices, exchange(): lax.ppermute(x, 'seq', [(i, i ^ d) for i in range(peers)])  43.1 us
    ppermute x21, starting transfers between devices, exchange(): lax.ppermute(x, 'seq', [(i, i ^ d) for i in range(peers)])  20.7 us
    pallas_call x1, Pallas kernels, attention_forward(): pl.pallas_call(functools.partial(forward_kernel, peers, heads, rows, bq,...  16.2 us
    pallas_call x1, Pallas kernels, attention_backward(): pl.pallas_call(functools.partial(backward_kernel, listed, heads, rows, bq...  14.5 us
    ppermute x3, starting transfers between devices, pass_on(): lax.ppermute(x, 'head', [(i, (i + 1) % groups) for i in range(groups)])  6.28 us
    dynamic_slice x1, local copies, waits for them, and re-layouts, per_device(): lax.dynamic_slice_in_dim(out_weight, block * width, width, 1)  4.54 us
  transfers between devices with their start and end apart: 24, of which 14 were waited for; matrix products, arithmetic and copies ran while one was open for 2% of the time, Pallas kernels for 50%

profile of v13, /device:TPU:0, one launch (start us, length us, event | category | flops | bytes accessed | tf_op | source)
XLA Modules:
  0.0 188.5 jit_solution(3069976365031343954)
XLA Ops:
  0.6 3.1 %collective-permute-start = (bf16[384,1024]{1,0:T(8,128)(2,1)}, bf16[384,1024]{1,0:T(8,128)(2,1)S(1)}, u32[]{:S(2)}, u32[]{:S(2)}) collective-permute-start(bf16[384,1024]{1,0:T(8,128)(2,1)} %o_ref.1), channel_id=1, source_target_pairs={{0,1},{1,2},{2,3},{3,0},{4,5},{5,6},{6,7},{7,4},{8,9},{9,10},{10,1... | collective-permute-start | bytes 2359304 | tf_op jit(solution)/shard_map/ppermute | solution.py:449
  3.7 73.5 %shard_map.85 = (bf16[1168,128]{1,0:T(8,128)(2,1)}, bf16[1168,128]{1,0:T(8,128)(2,1)}, bf16[1168,128]{1,0:T(8,128)(2,1)}, bf16[1168,128]{1,0:T(8,128)(2,1)}, bf1...) custom-call(s32[1]{0:T(128)} %bitcast.me_s, ...), custom_call_target="tpu_custom_call" | custom-call | tf_op jit(solution)/shard_map/pallas_call | solution.py:71
  77.3 1.6 collective-permute-start.1
  78.8 1.5 collective-permute-start.2
  80.3 4.5 %constant_dynamic-slice_fusion = (bf16[1024,1024]{1,0:T(8,128)(2,1)S(1)}, bf16[1024,1024]{1,0:T(8,128)(2,1)S(1)}, bf16[1024,1024]{1,0:T(8,128)(2,1)S(1)}, bf16[1024,1024]{1,0:T(8,128)(2,1)S(1)}) fusion(bf16[1024,4096]{1,0:T(8,128)(2,1)} %param.10, s32[]{:T(128)S(6)} %select_n.15, s32[]{:T(128)S(6)} %select_n.13, s32[]{:T(128)S(6)} %select_n.12, s32[]{:T(128)S(6)} %select_n.14), kind=kLoop, calls=%fused_computation | loop fusion | bytes 16777232 | tf_op jit(solution)/shard_map/dynamic_slice | solution.py:470
  84.9 0.0 copy-start.2
  84.9 1.0 shard_map.86.refs_0_
  86.0 0.1 collective-permute-done.1.refs_2_
  86.1 1.2 collective-permute-done.2.refs_4_
  87.3 0.0 collective-permute-done.o_ref
  87.3 1.6 collective-permute-start.3
  88.9 1.5 collective-permute-start.4
  90.4 0.0 collective-permute-start.5
  90.4 2.7 %collective-permute-start.6 = (bf16[1168,128]{1,0:T(8,128)(2,1)S(1)}, bf16[1168,128]{1,0:T(8,128)(2,1)S(1)}, u32[]{:S(2)}, u32[]{:S(2)}) collective-permute-start(bf16[1168,128]{1,0:T(8,128)(2,1)S(1)} %copy-done.4), channel_id=1, source_target_pairs={{0,20},{4,16},{8,28},{12,24},{16,4},{20,0},{24,12},{28,8},{1,21},{... | collective-permute-start | bytes 897032 | tf_op jit(solution)/shard_map/ppermute | solution.py:446
  93.1 0.0 collective-permute-start.7
  93.1 6.5 %collective-permute-done.4.refs_6_ = bf16[1168,128]{1,0:T(8,128)(2,1)S(1)} collective-permute-done((bf16[1168,128]{1,0:T(8,128)(2,1)S(1)}, bf16[1168,128]{1,0:T(8,128)(2,1)S(1)}, u32[]{:S(2)}, u32[]{:S(2)}) %collective-permute-start.4) | collective-permute-done | bytes 299040 | tf_op jit(solution)/shard_map/ppermute | solution.py:446
  99.6 1.0 shard_map.87.refs_0_
  100.6 3.6 %collective-permute-done.5.refs_7_ = bf16[1168,128]{1,0:T(8,128)(2,1)S(1)} collective-permute-done((bf16[1168,128]{1,0:T(8,128)(2,1)S(1)}, bf16[1168,128]{1,0:T(8,128)(2,1)S(1)}, u32[]{:S(2)}, u32[]{:S(2)}) %collective-permute-start.5) | collective-permute-done | bytes 299040 | tf_op jit(solution)/shard_map/ppermute | solution.py:446
  104.2 5.4 %collective-permute-done.6.refs_5_ = bf16[1168,128]{1,0:T(8,128)(2,1)S(1)} collective-permute-done((bf16[1168,128]{1,0:T(8,128)(2,1)S(1)}, bf16[1168,128]{1,0:T(8,128)(2,1)S(1)}, u32[]{:S(2)}, u32[]{:S(2)}) %collective-permute-start.6) | collective-permute-done | bytes 299040 | tf_op jit(solution)/shard_map/ppermute | solution.py:446
  109.6 1.6 collective-permute-start.9
  111.2 16.2 %shard_map.88 = (bf16[3072,128]{1,0:T(8,128)(2,1)S(1)}, bf16[3072,256]{1,0:T(8,128)(2,1)S(1)}, bf16[3072,256]{1,0:T(8,128)(2,1)S(1)}, bf16[128,3072]{1,0:T(8,128...) custom-call(s32[1]{0:T(128)} %bitcast.me_s, ...), custom_call_target="tpu_custom_call" | custom-call | flops 1811939328 | bytes 6291456 | tf_op jit(solution)/shard_map/pallas_call | solution.py:402
  127.4 1.0 shard_map.89.acc_ref
  128.5 2.6 %collective-permute-done.9.o_ref = bf16[384,1024]{1,0:T(8,128)(2,1)S(1)} collective-permute-done((bf16[384,1024]{1,0:T(8,128)(2,1)S(1)}, bf16[384,1024]{1,0:T(8,128)(2,1)S(1)}, u32[]{:S(2)}, u32[]{:S(2)}) %collective-permute-start.9) | collective-permute-done | bytes 786464 | tf_op jit(solution)/shard_map/ppermute | solution.py:449
  131.0 1.0 shard_map.90
  132.1 1.6 collective-permute-start.10
  133.6 0.0 collective-permute-start.11
  133.7 1.4 collective-permute-start.12
  135.1 0.7 collective-permute-start.13
  135.7 2.0 %collective-permute-start.14 = (bf16[384,128]{1,0:T(8,128)(2,1)S(1)}, bf16[384,128]{1,0:T(8,128)(2,1)S(1)}, u32[]{:S(2)}, u32[]{:S(2)}) collective-permute-start(bf16[384,128]{1,0:T(8,128)(2,1)S(1)} %get-tuple-element.102), channel_id=1, source_target_pairs={{0,12},{4,8},{8,4},{12,0},{16,28},{20,24},{24,20},{28,16},{1,13},{... | collective-permute-start | bytes 294920 | tf_op jit(solution)/shard_map/ppermute | solution.py:446
  137.7 0.0 collective-permute-done.10.refs_2_
  137.8 1.9 %collective-permute-done.11.refs_3_ = bf16[384,128]{1,0:T(8,128)(2,1)S(1)} collective-permute-done((bf16[384,128]{1,0:T(8,128)(2,1)S(1)}, bf16[384,128]{1,0:T(8,128)(2,1)S(1)}, u32[]{:S(2)}, u32[]{:S(2)}) %collective-permute-start.11) | collective-permute-done | bytes 98336 | tf_op jit(solution)/shard_map/ppermute | solution.py:446
  139.7 0.7 collective-permute-start.16
  140.4 2.5 %collective-permute-done.12.refs_4_ = bf16[384,128]{1,0:T(8,128)(2,1)S(1)} collective-permute-done((bf16[384,128]{1,0:T(8,128)(2,1)S(1)}, bf16[384,128]{1,0:T(8,128)(2,1)S(1)}, u32[]{:S(2)}, u32[]{:S(2)}) %collective-permute-start.12) | collective-permute-done | bytes 98336 | tf_op jit(solution)/shard_map/ppermute | solution.py:446
  142.9 1.0 collective-permute-done.15.refs_7_
  143.9 14.5 %shard_map.91 = (bf16[1152,128]{1,0:T(8,128)(2,1)S(1)}, bf16[1152,128]{1,0:T(8,128)(2,1)S(1)}, bf16[1152,128]{1,0:T(8,128)(2,1)S(1)}, bf16[1152,128]{1,0:T(8,128...) custom-call(s32[1]{0:T(128)} %bitcast.me_s, ...), custom_call_target="tpu_custom_call" | custom-call | flops 3019898880 | bytes 6291456 | tf_op jit(solution)/shard_map/pallas_call | solution.py:428
  158.4 1.6 collective-permute-start.22
  160.0 0.8 collective-permute-start.23
  160.8 0.7 collective-permute-start.17
  161.5 1.4 collective-permute-start.18
  162.9 1.2 collective-permute-start.19
  164.1 5.2 %collective-permute-done.22.refs_0_ = bf16[1152,128]{1,0:T(8,128)(2,1)S(1)} collective-permute-done((bf16[1152,128]{1,0:T(8,128)(2,1)S(1)}, bf16[1152,128]{1,0:T(8,128)(2,1)S(1)}, u32[]{:S(2)}, u32[]{:S(2)}) %collective-permute-start.22) | collective-permute-done | bytes 294944 | tf_op jit(solution)/shard_map/ppermute | solution.py:446
  169.3 4.7 %collective-permute-done.23.refs_1_ = bf16[1152,128]{1,0:T(8,128)(2,1)S(1)} collective-permute-done((bf16[1152,128]{1,0:T(8,128)(2,1)S(1)}, bf16[1152,128]{1,0:T(8,128)(2,1)S(1)}, u32[]{:S(2)}, u32[]{:S(2)}) %collective-permute-start.23) | collective-permute-done | bytes 294944 | tf_op jit(solution)/shard_map/ppermute | solution.py:446
  174.0 1.4 collective-permute-start.21
  175.4 1.0 shard_map.92
  176.4 5.6 %collective-permute-done.17.refs_0_ = bf16[1152,128]{1,0:T(8,128)(2,1)S(1)} collective-permute-done((bf16[1152,128]{1,0:T(8,128)(2,1)S(1)}, bf16[1152,128]{1,0:T(8,128)(2,1)S(1)}, u32[]{:S(2)}, u32[]{:S(2)}) %collective-permute-start.17) | collective-permute-done | bytes 294944 | tf_op jit(solution)/shard_map/ppermute | solution.py:446
  182.0 4.6 %collective-permute-done.19.refs_2_ = bf16[1152,128]{1,0:T(8,128)(2,1)S(1)} collective-permute-done((bf16[1152,128]{1,0:T(8,128)(2,1)S(1)}, bf16[1152,128]{1,0:T(8,128)(2,1)S(1)}, u32[]{:S(2)}, u32[]{:S(2)}) %collective-permute-start.19) | collective-permute-done | bytes 294944 | tf_op jit(solution)/shard_map/ppermute | solution.py:446
  186.6 0.7 collective-permute-done.20.refs_3_
  187.3 1.2 shard_map.93
  (24 shorter events, 0.1 us)
Async XLA Ops:
  0.6 86.7 %collective-permute-start = (bf16[384,1024]{1,0:T(8,128)(2,1)}, bf16[384,1024]{1,0:T(8,128)(2,1)S(1)}, u32[]{:S(2)}, u32[]{:S(2)}) collective-permute-start(bf16[384,1024]{1,0:T(8,128)(2,1)} %o_ref.1), channel_id=1, source_target_pairs={{0,1},{1,2},{2,3},{3,0},{4,5},{5,6},{6,7},{7,4},{8,9},{9,10},{10,1... | collective-permute-start | bytes 2359304 | tf_op jit(solution)/shard_map/ppermute | solution.py:449
  77.3 8.8 %collective-permute-start.1 = (bf16[1168,128]{1,0:T(8,128)(2,1)}, bf16[1168,128]{1,0:T(8,128)(2,1)S(1)}, u32[]{:S(2)}, u32[]{:S(2)}) collective-permute-start(bf16[1168,128]{1,0:T(8,128)(2,1)} %get-tuple-element.61), channel_id=1, source_target_pairs={{0,8},{4,12},{8,0},{12,4},{16,24},{20,28},{24,16},{28,20},{1,9},{5... | collective-permute-start | bytes 897032 | tf_op jit(solution)/shard_map/ppermute | solution.py:446
  78.8 8.5 %collective-permute-start.2 = (bf16[1168,128]{1,0:T(8,128)(2,1)}, bf16[1168,128]{1,0:T(8,128)(2,1)S(1)}, u32[]{:S(2)}, u32[]{:S(2)}) collective-permute-start(bf16[1168,128]{1,0:T(8,128)(2,1)} %get-tuple-element.62), channel_id=1, source_target_pairs={{0,16},{4,20},{8,24},{12,28},{16,0},{20,4},{24,8},{28,12},{1,17},{... | collective-permute-start | bytes 897032 | tf_op jit(solution)/shard_map/ppermute | solution.py:446
  80.3 4.5 %copy-start = (bf16[384,1024]{1,0:T(8,128)(2,1)S(1)}, bf16[384,1024]{1,0:T(8,128)(2,1)}, u32[]{:S(2)}) copy-start(bf16[384,1024]{1,0:T(8,128)(2,1)} %o_ref.1) | copy-start | bytes 2359300
  84.9 4.0 %copy-start.6 = (bf16[1168,128]{1,0:T(8,128)(2,1)S(1)}, bf16[1168,128]{1,0:T(8,128)(2,1)}, u32[]{:S(2)}) copy-start(bf16[1168,128]{1,0:T(8,128)(2,1)} %get-tuple-element.65) | copy-start | bytes 897028
  84.9 5.5 %copy-start.5 = (bf16[1168,128]{1,0:T(8,128)(2,1)S(1)}, bf16[1168,128]{1,0:T(8,128)(2,1)}, u32[]{:S(2)}) copy-start(bf16[1168,128]{1,0:T(8,128)(2,1)} %get-tuple-element.66) | copy-start | bytes 897028
  84.9 5.5 %copy-start.4 = (bf16[1168,128]{1,0:T(8,128)(2,1)S(1)}, bf16[1168,128]{1,0:T(8,128)(2,1)}, u32[]{:S(2)}) copy-start(bf16[1168,128]{1,0:T(8,128)(2,1)} %get-tuple-element.67) | copy-start | bytes 897028
  84.9 8.1 %copy-start.3 = (bf16[1168,128]{1,0:T(8,128)(2,1)S(1)}, bf16[1168,128]{1,0:T(8,128)(2,1)}, u32[]{:S(2)}) copy-start(bf16[1168,128]{1,0:T(8,128)(2,1)} %get-tuple-element.68) | copy-start | bytes 897028
  84.9 14.6 %copy-start.2 = (bf16[1168,128]{1,0:T(8,128)(2,1)S(1)}, bf16[1168,128]{1,0:T(8,128)(2,1)}, u32[]{:S(2)}) copy-start(bf16[1168,128]{1,0:T(8,128)(2,1)} %get-tuple-element.69) | copy-start | bytes 897028
  87.3 22.3 %collective-permute-start.3 = (bf16[384,1024]{1,0:T(8,128)(2,1)S(1)}, bf16[384,1024]{1,0:T(8,128)(2,1)S(1)}, u32[]{:S(2)}, u32[]{:S(2)}) collective-permute-start(bf16[384,1024]{1,0:T(8,128)(2,1)S(1)} %collective-permute-done.o_ref), channel_id=1, source_target_pairs={{0,1},{1,2},{2,3},{3,0},{4,5},{5,6},{6,7},{7,4},{8,9},{9,10},{10,1... | collective-permute-start | bytes 2359304 | tf_op jit(solution)/shard_map/ppermute | solution.py:449
  88.9 10.7 %collective-permute-start.4 = (bf16[1168,128]{1,0:T(8,128)(2,1)S(1)}, bf16[1168,128]{1,0:T(8,128)(2,1)S(1)}, u32[]{:S(2)}, u32[]{:S(2)}) collective-permute-start(bf16[1168,128]{1,0:T(8,128)(2,1)S(1)} %copy-done.6), channel_id=1, source_target_pairs={{0,24},{4,28},{8,16},{12,20},{16,8},{20,12},{24,0},{28,4},{1,25},{... | collective-permute-start | bytes 897032 | tf_op jit(solution)/shard_map/ppermute | solution.py:446
  90.4 13.8 %collective-permute-start.5 = (bf16[1168,128]{1,0:T(8,128)(2,1)S(1)}, bf16[1168,128]{1,0:T(8,128)(2,1)S(1)}, u32[]{:S(2)}, u32[]{:S(2)}) collective-permute-start(bf16[1168,128]{1,0:T(8,128)(2,1)S(1)} %copy-done.5), channel_id=1, source_target_pairs={{0,28},{4,24},{8,20},{12,16},{16,12},{20,8},{24,4},{28,0},{1,29},{... | collective-permute-start | bytes 897032 | tf_op jit(solution)/shard_map/ppermute | solution.py:446
  90.4 19.2 %collective-permute-start.6 = (bf16[1168,128]{1,0:T(8,128)(2,1)S(1)}, bf16[1168,128]{1,0:T(8,128)(2,1)S(1)}, u32[]{:S(2)}, u32[]{:S(2)}) collective-permute-start(bf16[1168,128]{1,0:T(8,128)(2,1)S(1)} %copy-done.4), channel_id=1, source_target_pairs={{0,20},{4,16},{8,28},{12,24},{16,4},{20,0},{24,12},{28,8},{1,21},{... | collective-permute-start | bytes 897032 | tf_op jit(solution)/shard_map/ppermute | solution.py:446
  93.1 16.5 %collective-permute-start.7 = (bf16[1168,128]{1,0:T(8,128)(2,1)S(1)}, bf16[1168,128]{1,0:T(8,128)(2,1)S(1)}, u32[]{:S(2)}, u32[]{:S(2)}) collective-permute-start(bf16[1168,128]{1,0:T(8,128)(2,1)S(1)} %copy-done.3), channel_id=1, source_target_pairs={{0,12},{4,8},{8,4},{12,0},{16,28},{20,24},{24,20},{28,16},{1,13},{... | collective-permute-start | bytes 897032 | tf_op jit(solution)/shard_map/ppermute | solution.py:446
  99.6 10.0 %collective-permute-start.8 = (bf16[1168,128]{1,0:T(8,128)(2,1)S(1)}, bf16[1168,128]{1,0:T(8,128)(2,1)S(1)}, u32[]{:S(2)}, u32[]{:S(2)}) collective-permute-start(bf16[1168,128]{1,0:T(8,128)(2,1)S(1)} %copy-done.2), channel_id=1, source_target_pairs={{0,4},{4,0},{8,12},{12,8},{16,20},{20,16},{24,28},{28,24},{1,5},{5... | collective-permute-start | bytes 897032 | tf_op jit(solution)/shard_map/ppermute | solution.py:446
  99.6 11.7 %copy-start.1 = (bf16[1168,128]{1,0:T(8,128)(2,1)S(1)}, bf16[1168,128]{1,0:T(8,128)(2,1)}, u32[]{:S(2)}) copy-start(bf16[1168,128]{1,0:T(8,128)(2,1)} %get-tuple-element.73.refs_0_) | copy-start | bytes 897028
  109.6 21.4 %collective-permute-start.9 = (bf16[384,1024]{1,0:T(8,128)(2,1)S(1)}, bf16[384,1024]{1,0:T(8,128)(2,1)S(1)}, u32[]{:S(2)}, u32[]{:S(2)}) collective-permute-start(bf16[384,1024]{1,0:T(8,128)(2,1)S(1)} %collective-permute-done.3.o_ref), channel_id=1, source_target_pairs={{0,1},{1,2},{2,3},{3,0},{4,5},{5,6},{6,7},{7,4},{8,9},{9,10},{10,1... | collective-permute-start | bytes 2359304 | tf_op jit(solution)/shard_map/ppermute | solution.py:449
  132.1 5.7 %collective-permute-start.10 = (bf16[384,128]{1,0:T(8,128)(2,1)S(1)}, bf16[384,128]{1,0:T(8,128)(2,1)S(1)}, u32[]{:S(2)}, u32[]{:S(2)}) collective-permute-start(bf16[384,128]{1,0:T(8,128)(2,1)S(1)} %get-tuple-element.98), channel_id=1, source_target_pairs={{0,24},{4,28},{8,16},{12,20},{16,8},{20,12},{24,0},{28,4},{1,25},{... | collective-permute-start | bytes 294920 | tf_op jit(solution)/shard_map/ppermute | solution.py:446
  133.6 6.1 %collective-permute-start.11 = (bf16[384,128]{1,0:T(8,128)(2,1)S(1)}, bf16[384,128]{1,0:T(8,128)(2,1)S(1)}, u32[]{:S(2)}, u32[]{:S(2)}) collective-permute-start(bf16[384,128]{1,0:T(8,128)(2,1)S(1)} %get-tuple-element.99), channel_id=1, source_target_pairs={{0,28},{4,24},{8,20},{12,16},{16,12},{20,8},{24,4},{28,0},{1,29},{... | collective-permute-start | bytes 294920 | tf_op jit(solution)/shard_map/ppermute | solution.py:446
  133.7 9.3 %collective-permute-start.12 = (bf16[384,128]{1,0:T(8,128)(2,1)S(1)}, bf16[384,128]{1,0:T(8,128)(2,1)S(1)}, u32[]{:S(2)}, u32[]{:S(2)}) collective-permute-start(bf16[384,128]{1,0:T(8,128)(2,1)S(1)} %get-tuple-element.100), channel_id=1, source_target_pairs={{0,8},{4,12},{8,0},{12,4},{16,24},{20,28},{24,16},{28,20},{1,9},{5... | collective-permute-start | bytes 294920 | tf_op jit(solution)/shard_map/ppermute | solution.py:446
  135.1 7.8 %collective-permute-start.13 = (bf16[384,128]{1,0:T(8,128)(2,1)S(1)}, bf16[384,128]{1,0:T(8,128)(2,1)S(1)}, u32[]{:S(2)}, u32[]{:S(2)}) collective-permute-start(bf16[384,128]{1,0:T(8,128)(2,1)S(1)} %get-tuple-element.101), channel_id=1, source_target_pairs={{0,16},{4,20},{8,24},{12,28},{16,0},{20,4},{24,8},{28,12},{1,17},{... | collective-permute-start | bytes 294920 | tf_op jit(solution)/shard_map/ppermute | solution.py:446
  135.7 7.2 %collective-permute-start.14 = (bf16[384,128]{1,0:T(8,128)(2,1)S(1)}, bf16[384,128]{1,0:T(8,128)(2,1)S(1)}, u32[]{:S(2)}, u32[]{:S(2)}) collective-permute-start(bf16[384,128]{1,0:T(8,128)(2,1)S(1)} %get-tuple-element.102), channel_id=1, source_target_pairs={{0,12},{4,8},{8,4},{12,0},{16,28},{20,24},{24,20},{28,16},{1,13},{... | collective-permute-start | bytes 294920 | tf_op jit(solution)/shard_map/ppermute | solution.py:446
  137.8 6.1 %collective-permute-start.15 = (bf16[384,128]{1,0:T(8,128)(2,1)S(1)}, bf16[384,128]{1,0:T(8,128)(2,1)S(1)}, u32[]{:S(2)}, u32[]{:S(2)}) collective-permute-start(bf16[384,128]{1,0:T(8,128)(2,1)S(1)} %get-tuple-element.103), channel_id=1, source_target_pairs={{0,20},{4,16},{8,28},{12,24},{16,4},{20,0},{24,12},{28,8},{1,21},{... | collective-permute-start | bytes 294920 | tf_op jit(solution)/shard_map/ppermute | solution.py:446
  139.7 4.2 %collective-permute-start.16 = (bf16[384,128]{1,0:T(8,128)(2,1)S(1)}, bf16[384,128]{1,0:T(8,128)(2,1)S(1)}, u32[]{:S(2)}, u32[]{:S(2)}) collective-permute-start(bf16[384,128]{1,0:T(8,128)(2,1)S(1)} %get-tuple-element.105), channel_id=1, source_target_pairs={{0,4},{4,0},{8,12},{12,8},{16,20},{20,16},{24,28},{28,24},{1,5},{5... | collective-permute-start | bytes 294920 | tf_op jit(solution)/shard_map/ppermute | solution.py:446
  158.4 10.9 %collective-permute-start.22 = (bf16[1152,128]{1,0:T(8,128)(2,1)S(1)}, bf16[1152,128]{1,0:T(8,128)(2,1)S(1)}, u32[]{:S(2)}, u32[]{:S(2)}) collective-permute-start(bf16[1152,128]{1,0:T(8,128)(2,1)S(1)} %get-tuple-element.111), channel_id=1, source_target_pairs={{0,24},{4,28},{8,16},{12,20},{16,8},{20,12},{24,0},{28,4},{1,25},{... | collective-permute-start | bytes 884744 | tf_op jit(solution)/shard_map/ppermute | solution.py:446
  160.0 14.0 %collective-permute-start.23 = (bf16[1152,128]{1,0:T(8,128)(2,1)S(1)}, bf16[1152,128]{1,0:T(8,128)(2,1)S(1)}, u32[]{:S(2)}, u32[]{:S(2)}) collective-permute-start(bf16[1152,128]{1,0:T(8,128)(2,1)S(1)} %get-tuple-element.112), channel_id=1, source_target_pairs={{0,28},{4,24},{8,20},{12,16},{16,12},{20,8},{24,4},{28,0},{1,29},{... | collective-permute-start | bytes 884744 | tf_op jit(solution)/shard_map/ppermute | solution.py:446
  160.8 21.1 %collective-permute-start.17 = (bf16[1152,128]{1,0:T(8,128)(2,1)S(1)}, bf16[1152,128]{1,0:T(8,128)(2,1)S(1)}, u32[]{:S(2)}, u32[]{:S(2)}) collective-permute-start(bf16[1152,128]{1,0:T(8,128)(2,1)S(1)} %get-tuple-element.106), channel_id=1, source_target_pairs={{0,8},{4,12},{8,0},{12,4},{16,24},{20,28},{24,16},{28,20},{1,9},{5... | collective-permute-start | bytes 884744 | tf_op jit(solution)/shard_map/ppermute | solution.py:446
  161.5 20.5 %collective-permute-start.18 = (bf16[1152,128]{1,0:T(8,128)(2,1)S(1)}, bf16[1152,128]{1,0:T(8,128)(2,1)S(1)}, u32[]{:S(2)}, u32[]{:S(2)}) collective-permute-start(bf16[1152,128]{1,0:T(8,128)(2,1)S(1)} %get-tuple-element.107), channel_id=1, source_target_pairs={{0,16},{4,20},{8,24},{12,28},{16,0},{20,4},{24,8},{28,12},{1,17},{... | collective-permute-start | bytes 884744 | tf_op jit(solution)/shard_map/ppermute | solution.py:446
  162.9 23.7 %collective-permute-start.19 = (bf16[1152,128]{1,0:T(8,128)(2,1)S(1)}, bf16[1152,128]{1,0:T(8,128)(2,1)S(1)}, u32[]{:S(2)}, u32[]{:S(2)}) collective-permute-start(bf16[1152,128]{1,0:T(8,128)(2,1)S(1)} %get-tuple-element.108), channel_id=1, source_target_pairs={{0,12},{4,8},{8,4},{12,0},{16,28},{20,24},{24,20},{28,16},{1,13},{... | collective-permute-start | bytes 884744 | tf_op jit(solution)/shard_map/ppermute | solution.py:446
  169.3 18.0 %collective-permute-start.20 = (bf16[1152,128]{1,0:T(8,128)(2,1)S(1)}, bf16[1152,128]{1,0:T(8,128)(2,1)S(1)}, u32[]{:S(2)}, u32[]{:S(2)}) collective-permute-start(bf16[1152,128]{1,0:T(8,128)(2,1)S(1)} %get-tuple-element.109), channel_id=1, source_target_pairs={{0,20},{4,16},{8,28},{12,24},{16,4},{20,0},{24,12},{28,8},{1,21},{... | collective-permute-start | bytes 884744 | tf_op jit(solution)/shard_map/ppermute | solution.py:446
  174.0 13.3 %collective-permute-start.21 = (bf16[1152,128]{1,0:T(8,128)(2,1)S(1)}, bf16[1152,128]{1,0:T(8,128)(2,1)S(1)}, u32[]{:S(2)}, u32[]{:S(2)}) collective-permute-start(bf16[1152,128]{1,0:T(8,128)(2,1)S(1)} %get-tuple-element.110), channel_id=1, source_target_pairs={{0,4},{4,0},{8,12},{12,8},{16,20},{20,16},{24,28},{28,24},{1,5},{5... | collective-permute-start | bytes 884744 | tf_op jit(solution)/shard_map/ppermute | solution.py:446

commit v14 on v13

--- a/solution.py
+++ b/solution.py
@@ -45,24 +45,16 @@
     return pltpu.CompilerParams(vmem_limit_bytes=total + VMEM_SPARE)
 
 
-def pack_kernel(heads, rows, me_s, q_ref, k_ref, v_ref, doc_ref, *refs):
-    outs, doc_block, done, doc_done = refs[:heads], refs[heads], refs[heads + 1], refs[heads + 2]
+def pack_kernel(heads, rows, me_s, q_ref, k_ref, v_ref, doc_ref, *outs):
     own = lax.rem(me_s[0], heads)
-    copies = []
+    docs = doc_ref[...].astype(jnp.float32)
+    docs = jnp.concatenate([docs, jnp.zeros((DOC_ROWS - docs.shape[0], HD), jnp.float32)], axis=0)
+    docs = docs.astype(jnp.bfloat16)
     for d, out in enumerate(outs):
         columns = aligned(own ^ d, HD)
         for part, ref in enumerate((q_ref, k_ref, v_ref)):
-            place = out.at[pl.ds(part * rows, rows), :]
-            copies.append(pltpu.make_async_copy(ref.at[:, columns], place, done.at[d, part]))
-            copies[-1].start()
-    docs = doc_ref[...].astype(jnp.float32)
-    docs = jnp.concatenate([docs, jnp.zeros((DOC_ROWS - docs.shape[0], HD), jnp.float32)], axis=0)
-    doc_block[...] = docs.astype(jnp.bfloat16)
-    for d, out in enumerate(outs):
-        copies.append(pltpu.make_async_copy(doc_block, out.at[pl.ds(3 * rows, DOC_ROWS), :], doc_done.at[d]))
-        copies[-1].start()
-    for copy in copies:
-        copy.wait()
+            out[part * rows:(part + 1) * rows, :] = ref[:, columns]
+        out[3 * rows:, :] = docs
 
 
 def pack_heads(me, q, k, v, doc_ids):
@@ -70,14 +62,9 @@
     heads = width // HD
     return pl.pallas_call(
         functools.partial(pack_kernel, heads, rows),
-        in_specs=[SMEM_SPEC] + [ANY_SPEC] * 3 + [VMEM_SPEC],
-        out_specs=[ANY_SPEC] * heads,
+        in_specs=[SMEM_SPEC] + [VMEM_SPEC] * 4,
+        out_specs=[VMEM_SPEC] * heads,
         out_shape=[jax.ShapeDtypeStruct((3 * rows + DOC_ROWS, HD), q.dtype)] * heads,
-        scratch_shapes=[
-            pltpu.VMEM((DOC_ROWS, HD), jnp.bfloat16),
-            pltpu.SemaphoreType.DMA((heads, 3)),
-            pltpu.SemaphoreType.DMA((heads,)),
-        ],
         compiler_params=pltpu.CompilerParams(vmem_limit_bytes=VMEM_MOST),
     )(me, q, k, v, doc_ids.reshape(rows // HD, HD))
 

time: 190 us -> 125 us (0.66); the launches traced: 189 us -> 125 us
  Pallas kernels: 110 us -> 42.8 us
  waiting for transfers between devices: 45.7 us -> 53.9 us
  starting transfers between devices: 27 us -> 23.4 us
    pallas_call x1, Pallas kernels: 73.5 us -> 3.62 us  [pack_heads(): pl.pallas_call(functools.partial(pack_kernel, heads, rows), in_specs=[SME...]
    ppermute x3, waiting for transfers between devices: 2.56 us -> 8.44 us  [pass_on(): lax.ppermute(x, 'head', [(i, (i + 1) % groups) for i in range(groups)])]
    ppermute x3, starting transfers between devices: 6.28 us -> 3.82 us  [pass_on(): lax.ppermute(x, 'head', [(i, (i + 1) % groups) for i in range(groups)])]
    ppermute x21, waiting for transfers between devices: 43.1 us -> 45.5 us  [exchange(): lax.ppermute(x, 'seq', [(i, i ^ d) for i in range(peers)])]
  transfers between devices with their start and end apart: 24 -> 24, of which waited for: 14 -> 17; matrix products, arithmetic and copies ran while one was open for 2% -> 4% of each run, Pallas kernels for 50% -> 20%
where the time goes in v14:
time: 125 us
  waiting for transfers between devices  53.9 us (43%)
  Pallas kernels  42.8 us (34%)
  starting transfers between devices  23.4 us (19%)
  local copies, waits for them, and re-layouts  4.57 us (4%)
    ppermute x21, waiting for transfers between devices, exchange(): lax.ppermute(x, 'seq', [(i, i ^ d) for i in range(peers)])  45.5 us
    ppermute x21, starting transfers between devices, exchange(): lax.ppermute(x, 'seq', [(i, i ^ d) for i in range(peers)])  19.6 us
    pallas_call x1, Pallas kernels, attention_forward(): pl.pallas_call(functools.partial(forward_kernel, peers, heads, rows, bq,...  17.4 us
    pallas_call x1, Pallas kernels, attention_backward(): pl.pallas_call(functools.partial(backward_kernel, listed, heads, rows, bq...  15.6 us
    ppermute x3, waiting for transfers between devices, pass_on(): lax.ppermute(x, 'head', [(i, (i + 1) % groups) for i in range(groups)])  8.44 us
    dynamic_slice x1, local copies, waits for them, and re-layouts, per_device(): lax.dynamic_slice_in_dim(out_weight, block * width, width, 1)  4.54 us
    ppermute x3, starting transfers between devices, pass_on(): lax.ppermute(x, 'head', [(i, (i + 1) % groups) for i in range(groups)])  3.82 us
    pallas_call x1, Pallas kernels, pack_heads(): pl.pallas_call(functools.partial(pack_kernel, heads, rows), in_specs=[SME...  3.62 us
  transfers between devices with their start and end apart: 24, of which 17 were waited for; matrix products, arithmetic and copies ran while one was open for 4% of the time, Pallas kernels for 20%

profile of v14, /device:TPU:0, one launch (start us, length us, event | category | flops | bytes accessed | tf_op | source)
XLA Modules:
  0.0 125.5 jit_solution(6918816358165493265)
XLA Ops:
  0.6 3.1 %collective-permute-start = (bf16[384,1024]{1,0:T(8,128)(2,1)}, bf16[384,1024]{1,0:T(8,128)(2,1)S(1)}, u32[]{:S(2)}, u32[]{:S(2)}) collective-permute-start(bf16[384,1024]{1,0:T(8,128)(2,1)} %o_ref.1), channel_id=1, source_target_pairs={{0,1},{1,2},{2,3},{3,0},{4,5},{5,6},{6,7},{7,4},{8,9},{9,10},{10,1... | collective-permute-start | bytes 2359304 | tf_op jit(solution)/shard_map/ppermute | solution.py:436
  3.7 3.6 %shard_map.85 = (bf16[1168,128]{1,0:T(8,128)(2,1)}, bf16[1168,128]{1,0:T(8,128)(2,1)}, bf16[1168,128]{1,0:T(8,128)(2,1)}, bf16[1168,128]{1,0:T(8,128)(2,1)}, bf1...) custom-call(s32[1]{0:T(128)} %bitcast.me_s, ...), custom_call_target="tpu_custom_call" | custom-call | tf_op jit(solution)/shard_map/pallas_call | solution.py:63
  7.3 1.5 %collective-permute-start.1 = (bf16[1168,128]{1,0:T(8,128)(2,1)}, bf16[1168,128]{1,0:T(8,128)(2,1)S(1)}, u32[]{:S(2)}, u32[]{:S(2)}) collective-permute-start(bf16[1168,128]{1,0:T(8,128)(2,1)} %get-tuple-element.61), channel_id=1, source_target_pairs={{0,8},{4,12},{8,0},{12,4},{16,24},{20,28},{24,16},{28,20},{1,9},{5... | collective-permute-start | bytes 897032 | tf_op jit(solution)/shard_map/ppermute | solution.py:433
  8.8 1.5 %collective-permute-start.2 = (bf16[1168,128]{1,0:T(8,128)(2,1)}, bf16[1168,128]{1,0:T(8,128)(2,1)S(1)}, u32[]{:S(2)}, u32[]{:S(2)}) collective-permute-start(bf16[1168,128]{1,0:T(8,128)(2,1)} %get-tuple-element.62), channel_id=1, source_target_pairs={{0,16},{4,20},{8,24},{12,28},{16,0},{20,4},{24,8},{28,12},{1,17},{... | collective-permute-start | bytes 897032 | tf_op jit(solution)/shard_map/ppermute | solution.py:433
  10.3 4.5 %constant_dynamic-slice_fusion = (bf16[1024,1024]{1,0:T(8,128)(2,1)S(1)}, bf16[1024,1024]{1,0:T(8,128)(2,1)S(1)}, bf16[1024,1024]{1,0:T(8,128)(2,1)S(1)}, bf16[1024,1024]{1,0:T(8,128)(2,1)S(1)}) fusion(bf16[1024,4096]{1,0:T(8,128)(2,1)} %param.10, s32[]{:T(128)S(6)} %select_n.15, s32[]{:T(128)S(6)} %select_n.13, s32[]{:T(128)S(6)} %select_n.12, s32[]{:T(128)S(6)} %select_n.14), kind=kLoop, calls=%fused_computation | loop fusion | bytes 16777232 | tf_op jit(solution)/shard_map/dynamic_slice | solution.py:457
  14.9 0.0 copy-start.2
  14.9 1.0 shard_map.86.refs_0_
  16.0 0.1 collective-permute-done.1.refs_2_
  16.1 1.2 collective-permute-done.2.refs_4_
  17.3 6.2 %collective-permute-done.o_ref = bf16[384,1024]{1,0:T(8,128)(2,1)S(1)} collective-permute-done((bf16[384,1024]{1,0:T(8,128)(2,1)}, bf16[384,1024]{1,0:T(8,128)(2,1)S(1)}, u32[]{:S(2)}, u32[]{:S(2)}) %collective-permute-start) | collective-permute-done | bytes 786464 | tf_op jit(solution)/shard_map/ppermute | solution.py:436
  23.5 0.0 collective-permute-start.3
  23.5 2.4 %collective-permute-start.4 = (bf16[1168,128]{1,0:T(8,128)(2,1)S(1)}, bf16[1168,128]{1,0:T(8,128)(2,1)S(1)}, u32[]{:S(2)}, u32[]{:S(2)}) collective-permute-start(bf16[1168,128]{1,0:T(8,128)(2,1)S(1)} %copy-done.6), channel_id=1, source_target_pairs={{0,24},{4,28},{8,16},{12,20},{16,8},{20,12},{24,0},{28,4},{1,25},{... | collective-permute-start | bytes 897032 | tf_op jit(solution)/shard_map/ppermute | solution.py:433
  26.0 1.7 %collective-permute-start.6 = (bf16[1168,128]{1,0:T(8,128)(2,1)S(1)}, bf16[1168,128]{1,0:T(8,128)(2,1)S(1)}, u32[]{:S(2)}, u32[]{:S(2)}) collective-permute-start(bf16[1168,128]{1,0:T(8,128)(2,1)S(1)} %copy-done.4), channel_id=1, source_target_pairs={{0,20},{4,16},{8,28},{12,24},{16,4},{20,0},{24,12},{28,8},{1,21},{... | collective-permute-start | bytes 897032 | tf_op jit(solution)/shard_map/ppermute | solution.py:433
  27.7 0.0 collective-permute-start.7
  27.7 6.8 %collective-permute-done.4.refs_6_ = bf16[1168,128]{1,0:T(8,128)(2,1)S(1)} collective-permute-done((bf16[1168,128]{1,0:T(8,128)(2,1)S(1)}, bf16[1168,128]{1,0:T(8,128)(2,1)S(1)}, u32[]{:S(2)}, u32[]{:S(2)}) %collective-permute-start.4) | collective-permute-done | bytes 299040 | tf_op jit(solution)/shard_map/ppermute | solution.py:433
  34.5 1.0 shard_map.87.refs_0_
  35.6 4.4 %collective-permute-done.5.refs_7_ = bf16[1168,128]{1,0:T(8,128)(2,1)S(1)} collective-permute-done((bf16[1168,128]{1,0:T(8,128)(2,1)S(1)}, bf16[1168,128]{1,0:T(8,128)(2,1)S(1)}, u32[]{:S(2)}, u32[]{:S(2)}) %collective-permute-start.5) | collective-permute-done | bytes 299040 | tf_op jit(solution)/shard_map/ppermute | solution.py:433
  39.9 5.5 %collective-permute-done.6.refs_5_ = bf16[1168,128]{1,0:T(8,128)(2,1)S(1)} collective-permute-done((bf16[1168,128]{1,0:T(8,128)(2,1)S(1)}, bf16[1168,128]{1,0:T(8,128)(2,1)S(1)}, u32[]{:S(2)}, u32[]{:S(2)}) %collective-permute-start.6) | collective-permute-done | bytes 299040 | tf_op jit(solution)/shard_map/ppermute | solution.py:433
  45.4 0.7 collective-permute-start.9
  46.2 17.4 %shard_map.88 = (bf16[3072,128]{1,0:T(8,128)(2,1)S(1)}, bf16[3072,256]{1,0:T(8,128)(2,1)S(1)}, bf16[3072,256]{1,0:T(8,128)(2,1)S(1)}, bf16[128,3072]{1,0:T(8,128...) custom-call(s32[1]{0:T(128)} %bitcast.me_s, ...), custom_call_target="tpu_custom_call" | custom-call | flops 1811939328 | bytes 6291456 | tf_op jit(solution)/shard_map/pallas_call | solution.py:389
  63.6 1.0 shard_map.89.acc_ref
  64.6 2.3 %collective-permute-done.9.o_ref = bf16[384,1024]{1,0:T(8,128)(2,1)S(1)} collective-permute-done((bf16[384,1024]{1,0:T(8,128)(2,1)S(1)}, bf16[384,1024]{1,0:T(8,128)(2,1)S(1)}, u32[]{:S(2)}, u32[]{:S(2)}) %collective-permute-start.9) | collective-permute-done | bytes 786464 | tf_op jit(solution)/shard_map/ppermute | solution.py:436
  66.9 1.0 shard_map.90
  67.9 2.2 %collective-permute-start.10 = (bf16[384,128]{1,0:T(8,128)(2,1)S(1)}, bf16[384,128]{1,0:T(8,128)(2,1)S(1)}, u32[]{:S(2)}, u32[]{:S(2)}) collective-permute-start(bf16[384,128]{1,0:T(8,128)(2,1)S(1)} %get-tuple-element.98), channel_id=1, source_target_pairs={{0,24},{4,28},{8,16},{12,20},{16,8},{20,12},{24,0},{28,4},{1,25},{... | collective-permute-start | bytes 294920 | tf_op jit(solution)/shard_map/ppermute | solution.py:433
  70.1 0.6 collective-permute-start.12
  70.7 1.5 %collective-permute-start.13 = (bf16[384,128]{1,0:T(8,128)(2,1)S(1)}, bf16[384,128]{1,0:T(8,128)(2,1)S(1)}, u32[]{:S(2)}, u32[]{:S(2)}) collective-permute-start(bf16[384,128]{1,0:T(8,128)(2,1)S(1)} %get-tuple-element.101), channel_id=1, source_target_pairs={{0,16},{4,20},{8,24},{12,28},{16,0},{20,4},{24,8},{28,12},{1,17},{... | collective-permute-start | bytes 294920 | tf_op jit(solution)/shard_map/ppermute | solution.py:433
  72.2 1.1 collective-permute-start.14
  73.3 0.2 collective-permute-done.10.refs_2_
  73.5 0.4 collective-permute-start.15
  73.9 2.3 %collective-permute-done.11.refs_3_ = bf16[384,128]{1,0:T(8,128)(2,1)S(1)} collective-permute-done((bf16[384,128]{1,0:T(8,128)(2,1)S(1)}, bf16[384,128]{1,0:T(8,128)(2,1)S(1)}, u32[]{:S(2)}, u32[]{:S(2)}) %collective-permute-start.11) | collective-permute-done | bytes 98336 | tf_op jit(solution)/shard_map/ppermute | solution.py:433
  76.2 1.5 %collective-permute-done.12.refs_4_ = bf16[384,128]{1,0:T(8,128)(2,1)S(1)} collective-permute-done((bf16[384,128]{1,0:T(8,128)(2,1)S(1)}, bf16[384,128]{1,0:T(8,128)(2,1)S(1)}, u32[]{:S(2)}, u32[]{:S(2)}) %collective-permute-start.12) | collective-permute-done | bytes 98336 | tf_op jit(solution)/shard_map/ppermute | solution.py:433
  77.6 0.0 collective-permute-done.13.refs_5_
  77.7 1.7 %collective-permute-done.14.refs_6_ = bf16[384,128]{1,0:T(8,128)(2,1)S(1)} collective-permute-done((bf16[384,128]{1,0:T(8,128)(2,1)S(1)}, bf16[384,128]{1,0:T(8,128)(2,1)S(1)}, u32[]{:S(2)}, u32[]{:S(2)}) %collective-permute-start.14) | collective-permute-done | bytes 98336 | tf_op jit(solution)/shard_map/ppermute | solution.py:433
  79.4 0.4 collective-permute-done.15.refs_7_
  79.8 15.6 %shard_map.91 = (bf16[1152,128]{1,0:T(8,128)(2,1)S(1)}, bf16[1152,128]{1,0:T(8,128)(2,1)S(1)}, bf16[1152,128]{1,0:T(8,128)(2,1)S(1)}, bf16[1152,128]{1,0:T(8,128...) custom-call(s32[1]{0:T(128)} %bitcast.me_s, ...), custom_call_target="tpu_custom_call" | custom-call | flops 3019898880 | bytes 6291456 | tf_op jit(solution)/shard_map/pallas_call | solution.py:415
  95.3 2.2 %collective-permute-start.22 = (bf16[1152,128]{1,0:T(8,128)(2,1)S(1)}, bf16[1152,128]{1,0:T(8,128)(2,1)S(1)}, u32[]{:S(2)}, u32[]{:S(2)}) collective-permute-start(bf16[1152,128]{1,0:T(8,128)(2,1)S(1)} %get-tuple-element.111), channel_id=1, source_target_pairs={{0,24},{4,28},{8,16},{12,20},{16,8},{20,12},{24,0},{28,4},{1,25},{... | collective-permute-start | bytes 884744 | tf_op jit(solution)/shard_map/ppermute | solution.py:433
  97.6 0.2 collective-permute-start.23
  97.8 1.2 collective-permute-start.17
  99.0 1.5 %collective-permute-start.18 = (bf16[1152,128]{1,0:T(8,128)(2,1)S(1)}, bf16[1152,128]{1,0:T(8,128)(2,1)S(1)}, u32[]{:S(2)}, u32[]{:S(2)}) collective-permute-start(bf16[1152,128]{1,0:T(8,128)(2,1)S(1)} %get-tuple-element.107), channel_id=1, source_target_pairs={{0,16},{4,20},{8,24},{12,28},{16,0},{20,4},{24,8},{28,12},{1,17},{... | collective-permute-start | bytes 884744 | tf_op jit(solution)/shard_map/ppermute | solution.py:433
  100.5 0.3 collective-permute-start.19
  100.8 5.5 %collective-permute-done.22.refs_0_ = bf16[1152,128]{1,0:T(8,128)(2,1)S(1)} collective-permute-done((bf16[1152,128]{1,0:T(8,128)(2,1)S(1)}, bf16[1152,128]{1,0:T(8,128)(2,1)S(1)}, u32[]{:S(2)}, u32[]{:S(2)}) %collective-permute-start.22) | collective-permute-done | bytes 294944 | tf_op jit(solution)/shard_map/ppermute | solution.py:433
  106.3 5.1 %collective-permute-done.23.refs_1_ = bf16[1152,128]{1,0:T(8,128)(2,1)S(1)} collective-permute-done((bf16[1152,128]{1,0:T(8,128)(2,1)S(1)}, bf16[1152,128]{1,0:T(8,128)(2,1)S(1)}, u32[]{:S(2)}, u32[]{:S(2)}) %collective-permute-start.23) | collective-permute-done | bytes 294944 | tf_op jit(solution)/shard_map/ppermute | solution.py:433
  111.3 1.0 collective-permute-start.21
  112.4 1.0 shard_map.92
  113.3 5.3 %collective-permute-done.17.refs_0_ = bf16[1152,128]{1,0:T(8,128)(2,1)S(1)} collective-permute-done((bf16[1152,128]{1,0:T(8,128)(2,1)S(1)}, bf16[1152,128]{1,0:T(8,128)(2,1)S(1)}, u32[]{:S(2)}, u32[]{:S(2)}) %collective-permute-start.17) | collective-permute-done | bytes 294944 | tf_op jit(solution)/shard_map/ppermute | solution.py:433
  118.6 4.6 %collective-permute-done.19.refs_2_ = bf16[1152,128]{1,0:T(8,128)(2,1)S(1)} collective-permute-done((bf16[1152,128]{1,0:T(8,128)(2,1)S(1)}, bf16[1152,128]{1,0:T(8,128)(2,1)S(1)}, u32[]{:S(2)}, u32[]{:S(2)}) %collective-permute-start.19) | collective-permute-done | bytes 294944 | tf_op jit(solution)/shard_map/ppermute | solution.py:433
  123.3 1.0 collective-permute-done.20.refs_3_
  124.2 1.2 shard_map.93
  (24 shorter events, 0.1 us)
Async XLA Ops:
  0.6 22.9 %collective-permute-start = (bf16[384,1024]{1,0:T(8,128)(2,1)}, bf16[384,1024]{1,0:T(8,128)(2,1)S(1)}, u32[]{:S(2)}, u32[]{:S(2)}) collective-permute-start(bf16[384,1024]{1,0:T(8,128)(2,1)} %o_ref.1), channel_id=1, source_target_pairs={{0,1},{1,2},{2,3},{3,0},{4,5},{5,6},{6,7},{7,4},{8,9},{9,10},{10,1... | collective-permute-start | bytes 2359304 | tf_op jit(solution)/shard_map/ppermute | solution.py:436
  7.3 8.8 %collective-permute-start.1 = (bf16[1168,128]{1,0:T(8,128)(2,1)}, bf16[1168,128]{1,0:T(8,128)(2,1)S(1)}, u32[]{:S(2)}, u32[]{:S(2)}) collective-permute-start(bf16[1168,128]{1,0:T(8,128)(2,1)} %get-tuple-element.61), channel_id=1, source_target_pairs={{0,8},{4,12},{8,0},{12,4},{16,24},{20,28},{24,16},{28,20},{1,9},{5... | collective-permute-start | bytes 897032 | tf_op jit(solution)/shard_map/ppermute | solution.py:433
  8.8 8.5 %collective-permute-start.2 = (bf16[1168,128]{1,0:T(8,128)(2,1)}, bf16[1168,128]{1,0:T(8,128)(2,1)S(1)}, u32[]{:S(2)}, u32[]{:S(2)}) collective-permute-start(bf16[1168,128]{1,0:T(8,128)(2,1)} %get-tuple-element.62), channel_id=1, source_target_pairs={{0,16},{4,20},{8,24},{12,28},{16,0},{20,4},{24,8},{28,12},{1,17},{... | collective-permute-start | bytes 897032 | tf_op jit(solution)/shard_map/ppermute | solution.py:433
  10.3 4.5 %copy-start = (bf16[384,1024]{1,0:T(8,128)(2,1)S(1)}, bf16[384,1024]{1,0:T(8,128)(2,1)}, u32[]{:S(2)}) copy-start(bf16[384,1024]{1,0:T(8,128)(2,1)} %o_ref.1) | copy-start | bytes 2359300
  14.9 8.6 %copy-start.6 = (bf16[1168,128]{1,0:T(8,128)(2,1)S(1)}, bf16[1168,128]{1,0:T(8,128)(2,1)}, u32[]{:S(2)}) copy-start(bf16[1168,128]{1,0:T(8,128)(2,1)} %get-tuple-element.65) | copy-start | bytes 897028
  14.9 11.0 %copy-start.5 = (bf16[1168,128]{1,0:T(8,128)(2,1)S(1)}, bf16[1168,128]{1,0:T(8,128)(2,1)}, u32[]{:S(2)}) copy-start(bf16[1168,128]{1,0:T(8,128)(2,1)} %get-tuple-element.66) | copy-start | bytes 897028
  14.9 11.0 %copy-start.4 = (bf16[1168,128]{1,0:T(8,128)(2,1)S(1)}, bf16[1168,128]{1,0:T(8,128)(2,1)}, u32[]{:S(2)}) copy-start(bf16[1168,128]{1,0:T(8,128)(2,1)} %get-tuple-element.67) | copy-start | bytes 897028
  14.9 12.8 %copy-start.3 = (bf16[1168,128]{1,0:T(8,128)(2,1)S(1)}, bf16[1168,128]{1,0:T(8,128)(2,1)}, u32[]{:S(2)}) copy-start(bf16[1168,128]{1,0:T(8,128)(2,1)} %get-tuple-element.68) | copy-start | bytes 897028
  14.9 19.6 %copy-start.2 = (bf16[1168,128]{1,0:T(8,128)(2,1)S(1)}, bf16[1168,128]{1,0:T(8,128)(2,1)}, u32[]{:S(2)}) copy-start(bf16[1168,128]{1,0:T(8,128)(2,1)} %get-tuple-element.69) | copy-start | bytes 897028
  23.5 21.9 %collective-permute-start.3 = (bf16[384,1024]{1,0:T(8,128)(2,1)S(1)}, bf16[384,1024]{1,0:T(8,128)(2,1)S(1)}, u32[]{:S(2)}, u32[]{:S(2)}) collective-permute-start(bf16[384,1024]{1,0:T(8,128)(2,1)S(1)} %collective-permute-done.o_ref), channel_id=1, source_target_pairs={{0,1},{1,2},{2,3},{3,0},{4,5},{5,6},{6,7},{7,4},{8,9},{9,10},{10,1... | collective-permute-start | bytes 2359304 | tf_op jit(solution)/shard_map/ppermute | solution.py:436
  23.5 11.0 %collective-permute-start.4 = (bf16[1168,128]{1,0:T(8,128)(2,1)S(1)}, bf16[1168,128]{1,0:T(8,128)(2,1)S(1)}, u32[]{:S(2)}, u32[]{:S(2)}) collective-permute-start(bf16[1168,128]{1,0:T(8,128)(2,1)S(1)} %copy-done.6), channel_id=1, source_target_pairs={{0,24},{4,28},{8,16},{12,20},{16,8},{20,12},{24,0},{28,4},{1,25},{... | collective-permute-start | bytes 897032 | tf_op jit(solution)/shard_map/ppermute | solution.py:433
  25.9 14.0 %collective-permute-start.5 = (bf16[1168,128]{1,0:T(8,128)(2,1)S(1)}, bf16[1168,128]{1,0:T(8,128)(2,1)S(1)}, u32[]{:S(2)}, u32[]{:S(2)}) collective-permute-start(bf16[1168,128]{1,0:T(8,128)(2,1)S(1)} %copy-done.5), channel_id=1, source_target_pairs={{0,28},{4,24},{8,20},{12,16},{16,12},{20,8},{24,4},{28,0},{1,29},{... | collective-permute-start | bytes 897032 | tf_op jit(solution)/shard_map/ppermute | solution.py:433
  26.0 19.5 %collective-permute-start.6 = (bf16[1168,128]{1,0:T(8,128)(2,1)S(1)}, bf16[1168,128]{1,0:T(8,128)(2,1)S(1)}, u32[]{:S(2)}, u32[]{:S(2)}) collective-permute-start(bf16[1168,128]{1,0:T(8,128)(2,1)S(1)} %copy-done.4), channel_id=1, source_target_pairs={{0,20},{4,16},{8,28},{12,24},{16,4},{20,0},{24,12},{28,8},{1,21},{... | collective-permute-start | bytes 897032 | tf_op jit(solution)/shard_map/ppermute | solution.py:433
  27.7 17.8 %collective-permute-start.7 = (bf16[1168,128]{1,0:T(8,128)(2,1)S(1)}, bf16[1168,128]{1,0:T(8,128)(2,1)S(1)}, u32[]{:S(2)}, u32[]{:S(2)}) collective-permute-start(bf16[1168,128]{1,0:T(8,128)(2,1)S(1)} %copy-done.3), channel_id=1, source_target_pairs={{0,12},{4,8},{8,4},{12,0},{16,28},{20,24},{24,20},{28,16},{1,13},{... | collective-permute-start | bytes 897032 | tf_op jit(solution)/shard_map/ppermute | solution.py:433
  34.5 10.9 %collective-permute-start.8 = (bf16[1168,128]{1,0:T(8,128)(2,1)S(1)}, bf16[1168,128]{1,0:T(8,128)(2,1)S(1)}, u32[]{:S(2)}, u32[]{:S(2)}) collective-permute-start(bf16[1168,128]{1,0:T(8,128)(2,1)S(1)} %copy-done.2), channel_id=1, source_target_pairs={{0,4},{4,0},{8,12},{12,8},{16,20},{20,16},{24,28},{28,24},{1,5},{5... | collective-permute-start | bytes 897032 | tf_op jit(solution)/shard_map/ppermute | solution.py:433
  34.5 11.6 %copy-start.1 = (bf16[1168,128]{1,0:T(8,128)(2,1)S(1)}, bf16[1168,128]{1,0:T(8,128)(2,1)}, u32[]{:S(2)}) copy-start(bf16[1168,128]{1,0:T(8,128)(2,1)} %get-tuple-element.73.refs_0_) | copy-start | bytes 897028
  45.4 21.4 %collective-permute-start.9 = (bf16[384,1024]{1,0:T(8,128)(2,1)S(1)}, bf16[384,1024]{1,0:T(8,128)(2,1)S(1)}, u32[]{:S(2)}, u32[]{:S(2)}) collective-permute-start(bf16[384,1024]{1,0:T(8,128)(2,1)S(1)} %collective-permute-done.3.o_ref), channel_id=1, source_target_pairs={{0,1},{1,2},{2,3},{3,0},{4,5},{5,6},{6,7},{7,4},{8,9},{9,10},{10,1... | collective-permute-start | bytes 2359304 | tf_op jit(solution)/shard_map/ppermute | solution.py:436
  67.9 5.6 %collective-permute-start.10 = (bf16[384,128]{1,0:T(8,128)(2,1)S(1)}, bf16[384,128]{1,0:T(8,128)(2,1)S(1)}, u32[]{:S(2)}, u32[]{:S(2)}) collective-permute-start(bf16[384,128]{1,0:T(8,128)(2,1)S(1)} %get-tuple-element.98), channel_id=1, source_target_pairs={{0,24},{4,28},{8,16},{12,20},{16,8},{20,12},{24,0},{28,4},{1,25},{... | collective-permute-start | bytes 294920 | tf_op jit(solution)/shard_map/ppermute | solution.py:433
  70.1 6.1 %collective-permute-start.11 = (bf16[384,128]{1,0:T(8,128)(2,1)S(1)}, bf16[384,128]{1,0:T(8,128)(2,1)S(1)}, u32[]{:S(2)}, u32[]{:S(2)}) collective-permute-start(bf16[384,128]{1,0:T(8,128)(2,1)S(1)} %get-tuple-element.99), channel_id=1, source_target_pairs={{0,28},{4,24},{8,20},{12,16},{16,12},{20,8},{24,4},{28,0},{1,29},{... | collective-permute-start | bytes 294920 | tf_op jit(solution)/shard_map/ppermute | solution.py:433
  70.1 7.5 %collective-permute-start.12 = (bf16[384,128]{1,0:T(8,128)(2,1)S(1)}, bf16[384,128]{1,0:T(8,128)(2,1)S(1)}, u32[]{:S(2)}, u32[]{:S(2)}) collective-permute-start(bf16[384,128]{1,0:T(8,128)(2,1)S(1)} %get-tuple-element.100), channel_id=1, source_target_pairs={{0,8},{4,12},{8,0},{12,4},{16,24},{20,28},{24,16},{28,20},{1,9},{5... | collective-permute-start | bytes 294920 | tf_op jit(solution)/shard_map/ppermute | solution.py:433
  70.7 6.9 %collective-permute-start.13 = (bf16[384,128]{1,0:T(8,128)(2,1)S(1)}, bf16[384,128]{1,0:T(8,128)(2,1)S(1)}, u32[]{:S(2)}, u32[]{:S(2)}) collective-permute-start(bf16[384,128]{1,0:T(8,128)(2,1)S(1)} %get-tuple-element.101), channel_id=1, source_target_pairs={{0,16},{4,20},{8,24},{12,28},{16,0},{20,4},{24,8},{28,12},{1,17},{... | collective-permute-start | bytes 294920 | tf_op jit(solution)/shard_map/ppermute | solution.py:433
  72.2 7.2 %collective-permute-start.14 = (bf16[384,128]{1,0:T(8,128)(2,1)S(1)}, bf16[384,128]{1,0:T(8,128)(2,1)S(1)}, u32[]{:S(2)}, u32[]{:S(2)}) collective-permute-start(bf16[384,128]{1,0:T(8,128)(2,1)S(1)} %get-tuple-element.102), channel_id=1, source_target_pairs={{0,12},{4,8},{8,4},{12,0},{16,28},{20,24},{24,20},{28,16},{1,13},{... | collective-permute-start | bytes 294920 | tf_op jit(solution)/shard_map/ppermute | solution.py:433
  73.5 6.3 %collective-permute-start.15 = (bf16[384,128]{1,0:T(8,128)(2,1)S(1)}, bf16[384,128]{1,0:T(8,128)(2,1)S(1)}, u32[]{:S(2)}, u32[]{:S(2)}) collective-permute-start(bf16[384,128]{1,0:T(8,128)(2,1)S(1)} %get-tuple-element.103), channel_id=1, source_target_pairs={{0,20},{4,16},{8,28},{12,24},{16,4},{20,0},{24,12},{28,8},{1,21},{... | collective-permute-start | bytes 294920 | tf_op jit(solution)/shard_map/ppermute | solution.py:433
  76.2 3.6 %collective-permute-start.16 = (bf16[384,128]{1,0:T(8,128)(2,1)S(1)}, bf16[384,128]{1,0:T(8,128)(2,1)S(1)}, u32[]{:S(2)}, u32[]{:S(2)}) collective-permute-start(bf16[384,128]{1,0:T(8,128)(2,1)S(1)} %get-tuple-element.105), channel_id=1, source_target_pairs={{0,4},{4,0},{8,12},{12,8},{16,20},{20,16},{24,28},{28,24},{1,5},{5... | collective-permute-start | bytes 294920 | tf_op jit(solution)/shard_map/ppermute | solution.py:433
  95.3 10.9 %collective-permute-start.22 = (bf16[1152,128]{1,0:T(8,128)(2,1)S(1)}, bf16[1152,128]{1,0:T(8,128)(2,1)S(1)}, u32[]{:S(2)}, u32[]{:S(2)}) collective-permute-start(bf16[1152,128]{1,0:T(8,128)(2,1)S(1)} %get-tuple-element.111), channel_id=1, source_target_pairs={{0,24},{4,28},{8,16},{12,20},{16,8},{20,12},{24,0},{28,4},{1,25},{... | collective-permute-start | bytes 884744 | tf_op jit(solution)/shard_map/ppermute | solution.py:433
  97.6 13.7 %collective-permute-start.23 = (bf16[1152,128]{1,0:T(8,128)(2,1)S(1)}, bf16[1152,128]{1,0:T(8,128)(2,1)S(1)}, u32[]{:S(2)}, u32[]{:S(2)}) collective-permute-start(bf16[1152,128]{1,0:T(8,128)(2,1)S(1)} %get-tuple-element.112), channel_id=1, source_target_pairs={{0,28},{4,24},{8,20},{12,16},{16,12},{20,8},{24,4},{28,0},{1,29},{... | collective-permute-start | bytes 884744 | tf_op jit(solution)/shard_map/ppermute | solution.py:433
  97.8 20.9 %collective-permute-start.17 = (bf16[1152,128]{1,0:T(8,128)(2,1)S(1)}, bf16[1152,128]{1,0:T(8,128)(2,1)S(1)}, u32[]{:S(2)}, u32[]{:S(2)}) collective-permute-start(bf16[1152,128]{1,0:T(8,128)(2,1)S(1)} %get-tuple-element.106), channel_id=1, source_target_pairs={{0,8},{4,12},{8,0},{12,4},{16,24},{20,28},{24,16},{28,20},{1,9},{5... | collective-permute-start | bytes 884744 | tf_op jit(solution)/shard_map/ppermute | solution.py:433
  99.0 19.6 %collective-permute-start.18 = (bf16[1152,128]{1,0:T(8,128)(2,1)S(1)}, bf16[1152,128]{1,0:T(8,128)(2,1)S(1)}, u32[]{:S(2)}, u32[]{:S(2)}) collective-permute-start(bf16[1152,128]{1,0:T(8,128)(2,1)S(1)} %get-tuple-element.107), channel_id=1, source_target_pairs={{0,16},{4,20},{8,24},{12,28},{16,0},{20,4},{24,8},{28,12},{1,17},{... | collective-permute-start | bytes 884744 | tf_op jit(solution)/shard_map/ppermute | solution.py:433
  100.5 22.8 %collective-permute-start.19 = (bf16[1152,128]{1,0:T(8,128)(2,1)S(1)}, bf16[1152,128]{1,0:T(8,128)(2,1)S(1)}, u32[]{:S(2)}, u32[]{:S(2)}) collective-permute-start(bf16[1152,128]{1,0:T(8,128)(2,1)S(1)} %get-tuple-element.108), channel_id=1, source_target_pairs={{0,12},{4,8},{8,4},{12,0},{16,28},{20,24},{24,20},{28,16},{1,13},{... | collective-permute-start | bytes 884744 | tf_op jit(solution)/shard_map/ppermute | solution.py:433
  106.3 18.0 %collective-permute-start.20 = (bf16[1152,128]{1,0:T(8,128)(2,1)S(1)}, bf16[1152,128]{1,0:T(8,128)(2,1)S(1)}, u32[]{:S(2)}, u32[]{:S(2)}) collective-permute-start(bf16[1152,128]{1,0:T(8,128)(2,1)S(1)} %get-tuple-element.109), channel_id=1, source_target_pairs={{0,20},{4,16},{8,28},{12,24},{16,4},{20,0},{24,12},{28,8},{1,21},{... | collective-permute-start | bytes 884744 | tf_op jit(solution)/shard_map/ppermute | solution.py:433
  111.3 12.9 %collective-permute-start.21 = (bf16[1152,128]{1,0:T(8,128)(2,1)S(1)}, bf16[1152,128]{1,0:T(8,128)(2,1)S(1)}, u32[]{:S(2)}, u32[]{:S(2)}) collective-permute-start(bf16[1152,128]{1,0:T(8,128)(2,1)S(1)} %get-tuple-element.110), channel_id=1, source_target_pairs={{0,4},{4,0},{8,12},{12,8},{16,20},{20,16},{24,28},{28,24},{1,5},{5... | collective-permute-start | bytes 884744 | tf_op jit(solution)/shard_map/ppermute | solution.py:433

commit v15 on v14

--- a/solution.py
+++ b/solution.py
@@ -12,7 +12,7 @@
 DOC_VALUES = 8
 DOC_ROWS = 16
 ONES_ROWS = 16
-STRIP = 64
+STRIP = 128
 NEG_LARGE = -1e30
 VMEM_SPARE = 6 * 1024 * 1024
 VMEM_MOST = 56 * 1024 * 1024
@@ -447,7 +447,7 @@
     received = exchange_all(packed, range(peers))
 
     def share(step):
-        return len(order) * step * (step + 1) // ((groups - 2) * (groups - 1))
+        return len(order) * step // (groups - 2)
 
     after = lax.optimization_barrier
     features, acc = out_grad, None

time: 125 us -> 122 us (0.976)
  waiting for transfers between devices: 53.9 us -> 49.8 us
    ppermute x3, waiting for transfers between devices: 8.44 us -> 3.32 us  [pass_on(): lax.ppermute(x, 'head', [(i, (i + 1) % groups) for i in range(groups)])]
  transfers between devices with their start and end apart: 24 -> 24, of which waited for: 17 -> 17; matrix products, arithmetic and copies ran while one was open for 4% -> 4% of each run, Pallas kernels for 20% -> 21%
where the time goes in v15:
time: 122 us
  waiting for transfers between devices  49.8 us (41%)
  Pallas kernels  43 us (35%)
  starting transfers between devices  23.4 us (19%)
  local copies, waits for them, and re-layouts  4.56 us (4%)
    ppermute x21, waiting for transfers between devices, exchange(): lax.ppermute(x, 'seq', [(i, i ^ d) for i in range(peers)])  46.5 us
    ppermute x21, starting transfers between devices, exchange(): lax.ppermute(x, 'seq', [(i, i ^ d) for i in range(peers)])  18.7 us
    pallas_call x1, Pallas kernels, attention_forward(): pl.pallas_call(functools.partial(forward_kernel, peers, heads, rows, bq,...  17.9 us
    pallas_call x1, Pallas kernels, attention_backward(): pl.pallas_call(functools.partial(backward_kernel, listed, heads, rows, bq...  15.2 us
    ppermute x3, starting transfers between devices, pass_on(): lax.ppermute(x, 'head', [(i, (i + 1) % groups) for i in range(groups)])  4.66 us
    dynamic_slice x1, local copies, waits for them, and re-layouts, per_device(): lax.dynamic_slice_in_dim(out_weight, block * width, width, 1)  4.54 us
    pallas_call x1, Pallas kernels, pack_heads(): pl.pallas_call(functools.partial(pack_kernel, heads, rows), in_specs=[SME...  3.62 us
    ppermute x3, waiting for transfers between devices, pass_on(): lax.ppermute(x, 'head', [(i, (i + 1) % groups) for i in range(groups)])  3.32 us
  transfers between devices with their start and end apart: 24, of which 17 were waited for; matrix products, arithmetic and copies ran while one was open for 4% of the time, Pallas kernels for 21%

profile of v15, /device:TPU:0, one launch (start us, length us, event | category | flops | bytes accessed | tf_op | source)
XLA Modules:
  0.0 121.6 jit_solution(4827880156416007970)
XLA Ops:
  0.6 3.1 %collective-permute-start = (bf16[384,1024]{1,0:T(8,128)(2,1)}, bf16[384,1024]{1,0:T(8,128)(2,1)S(1)}, u32[]{:S(2)}, u32[]{:S(2)}) collective-permute-start(bf16[384,1024]{1,0:T(8,128)(2,1)} %o_ref.1), channel_id=1, source_target_pairs={{0,1},{1,2},{2,3},{3,0},{4,5},{5,6},{6,7},{7,4},{8,9},{9,10},{10,1... | collective-permute-start | bytes 2359304 | tf_op jit(solution)/shard_map/ppermute | solution.py:436
  3.7 3.6 %shard_map.85 = (bf16[1168,128]{1,0:T(8,128)(2,1)}, bf16[1168,128]{1,0:T(8,128)(2,1)}, bf16[1168,128]{1,0:T(8,128)(2,1)}, bf16[1168,128]{1,0:T(8,128)(2,1)}, bf1...) custom-call(s32[1]{0:T(128)} %bitcast.me_s, ...), custom_call_target="tpu_custom_call" | custom-call | tf_op jit(solution)/shard_map/pallas_call | solution.py:63
  7.3 1.5 %collective-permute-start.1 = (bf16[1168,128]{1,0:T(8,128)(2,1)}, bf16[1168,128]{1,0:T(8,128)(2,1)S(1)}, u32[]{:S(2)}, u32[]{:S(2)}) collective-permute-start(bf16[1168,128]{1,0:T(8,128)(2,1)} %get-tuple-element.61), channel_id=1, source_target_pairs={{0,8},{4,12},{8,0},{12,4},{16,24},{20,28},{24,16},{28,20},{1,9},{5... | collective-permute-start | bytes 897032 | tf_op jit(solution)/shard_map/ppermute | solution.py:433
  8.8 1.5 %collective-permute-start.2 = (bf16[1168,128]{1,0:T(8,128)(2,1)}, bf16[1168,128]{1,0:T(8,128)(2,1)S(1)}, u32[]{:S(2)}, u32[]{:S(2)}) collective-permute-start(bf16[1168,128]{1,0:T(8,128)(2,1)} %get-tuple-element.62), channel_id=1, source_target_pairs={{0,16},{4,20},{8,24},{12,28},{16,0},{20,4},{24,8},{28,12},{1,17},{... | collective-permute-start | bytes 897032 | tf_op jit(solution)/shard_map/ppermute | solution.py:433
  10.3 0.5 collective-permute-start.3
  10.8 4.5 %constant_dynamic-slice_fusion = (bf16[1024,1024]{1,0:T(8,128)(2,1)S(1)}, bf16[1024,1024]{1,0:T(8,128)(2,1)S(1)}, bf16[1024,1024]{1,0:T(8,128)(2,1)S(1)}, bf16[1024,1024]{1,0:T(8,128)(2,1)S(1)}) fusion(bf16[1024,4096]{1,0:T(8,128)(2,1)} %param.10, s32[]{:T(128)S(6)} %select_n.15, s32[]{:T(128)S(6)} %select_n.13, s32[]{:T(128)S(6)} %select_n.12, s32[]{:T(128)S(6)} %select_n.14), kind=kLoop, calls=%fused_computation | loop fusion | bytes 16777232 | tf_op jit(solution)/shard_map/dynamic_slice | solution.py:457
  15.4 0.0 copy-start.2
  15.4 1.0 shard_map.86.refs_0_
  16.4 1.1 collective-permute-done.1.refs_2_
  17.6 6.2 %collective-permute-done.2.refs_4_ = bf16[1168,128]{1,0:T(8,128)(2,1)S(1)} collective-permute-done((bf16[1168,128]{1,0:T(8,128)(2,1)}, bf16[1168,128]{1,0:T(8,128)(2,1)S(1)}, u32[]{:S(2)}, u32[]{:S(2)}) %collective-permute-start.2) | collective-permute-done | bytes 299040 | tf_op jit(solution)/shard_map/ppermute | solution.py:433
  23.7 0.0 collective-permute-done.3.refs_6_
  23.7 1.6 %collective-permute-start.4 = (bf16[384,1024]{1,0:T(8,128)(2,1)S(1)}, bf16[384,1024]{1,0:T(8,128)(2,1)S(1)}, u32[]{:S(2)}, u32[]{:S(2)}) collective-permute-start(bf16[384,1024]{1,0:T(8,128)(2,1)S(1)} %collective-permute-done.o_ref), channel_id=1, source_target_pairs={{0,1},{1,2},{2,3},{3,0},{4,5},{5,6},{6,7},{7,4},{8,9},{9,10},{10,1... | collective-permute-start | bytes 2359304 | tf_op jit(solution)/shard_map/ppermute | solution.py:436
  25.3 2.4 %collective-permute-start.6 = (bf16[1168,128]{1,0:T(8,128)(2,1)S(1)}, bf16[1168,128]{1,0:T(8,128)(2,1)S(1)}, u32[]{:S(2)}, u32[]{:S(2)}) collective-permute-start(bf16[1168,128]{1,0:T(8,128)(2,1)S(1)} %copy-done.4), channel_id=1, source_target_pairs={{0,20},{4,16},{8,28},{12,24},{16,4},{20,0},{24,12},{28,8},{1,21},{... | collective-permute-start | bytes 897032 | tf_op jit(solution)/shard_map/ppermute | solution.py:433
  27.7 0.4 collective-permute-start.7
  28.1 0.6 collective-permute-start.8
  28.6 1.0 shard_map.87.refs_0_
  29.7 6.0 %collective-permute-done.5.refs_7_ = bf16[1168,128]{1,0:T(8,128)(2,1)S(1)} collective-permute-done((bf16[1168,128]{1,0:T(8,128)(2,1)S(1)}, bf16[1168,128]{1,0:T(8,128)(2,1)S(1)}, u32[]{:S(2)}, u32[]{:S(2)}) %collective-permute-start.5) | collective-permute-done | bytes 299040 | tf_op jit(solution)/shard_map/ppermute | solution.py:433
  35.6 5.4 %collective-permute-done.6.refs_5_ = bf16[1168,128]{1,0:T(8,128)(2,1)S(1)} collective-permute-done((bf16[1168,128]{1,0:T(8,128)(2,1)S(1)}, bf16[1168,128]{1,0:T(8,128)(2,1)S(1)}, u32[]{:S(2)}, u32[]{:S(2)}) %collective-permute-start.6) | collective-permute-done | bytes 299040 | tf_op jit(solution)/shard_map/ppermute | solution.py:433
  41.1 3.0 %collective-permute-done.4.o_ref = bf16[384,1024]{1,0:T(8,128)(2,1)S(1)} collective-permute-done((bf16[384,1024]{1,0:T(8,128)(2,1)S(1)}, bf16[384,1024]{1,0:T(8,128)(2,1)S(1)}, u32[]{:S(2)}, u32[]{:S(2)}) %collective-permute-start.4) | collective-permute-done | bytes 786464 | tf_op jit(solution)/shard_map/ppermute | solution.py:436
  44.0 17.9 %shard_map.88 = (bf16[3072,128]{1,0:T(8,128)(2,1)S(1)}, bf16[3072,256]{1,0:T(8,128)(2,1)S(1)}, bf16[3072,256]{1,0:T(8,128)(2,1)S(1)}, bf16[128,3072]{1,0:T(8,128...) custom-call(s32[1]{0:T(128)} %bitcast.me_s, ...), custom_call_target="tpu_custom_call" | custom-call | flops 1811939328 | bytes 6291456 | tf_op jit(solution)/shard_map/pallas_call | solution.py:389
  62.0 1.0 shard_map.89.acc_ref
  63.0 0.4 collective-permute-done.9.o_ref
  63.4 1.0 shard_map.90
  64.4 2.3 %collective-permute-start.10 = (bf16[384,128]{1,0:T(8,128)(2,1)S(1)}, bf16[384,128]{1,0:T(8,128)(2,1)S(1)}, u32[]{:S(2)}, u32[]{:S(2)}) collective-permute-start(bf16[384,128]{1,0:T(8,128)(2,1)S(1)} %get-tuple-element.98), channel_id=1, source_target_pairs={{0,24},{4,28},{8,16},{12,20},{16,8},{20,12},{24,0},{28,4},{1,25},{... | collective-permute-start | bytes 294920 | tf_op jit(solution)/shard_map/ppermute | solution.py:433
  66.7 0.0 collective-permute-start.11
  66.7 0.3 collective-permute-start.12
  67.0 1.0 collective-permute-start.13
  68.0 1.7 %collective-permute-start.14 = (bf16[384,128]{1,0:T(8,128)(2,1)S(1)}, bf16[384,128]{1,0:T(8,128)(2,1)S(1)}, u32[]{:S(2)}, u32[]{:S(2)}) collective-permute-start(bf16[384,128]{1,0:T(8,128)(2,1)S(1)} %get-tuple-element.102), channel_id=1, source_target_pairs={{0,12},{4,8},{8,4},{12,0},{16,28},{20,24},{24,20},{28,16},{1,13},{... | collective-permute-start | bytes 294920 | tf_op jit(solution)/shard_map/ppermute | solution.py:433
  69.6 0.4 collective-permute-done.10.refs_2_
  70.0 0.5 collective-permute-start.15
  70.5 2.3 %collective-permute-done.11.refs_3_ = bf16[384,128]{1,0:T(8,128)(2,1)S(1)} collective-permute-done((bf16[384,128]{1,0:T(8,128)(2,1)S(1)}, bf16[384,128]{1,0:T(8,128)(2,1)S(1)}, u32[]{:S(2)}, u32[]{:S(2)}) %collective-permute-start.11) | collective-permute-done | bytes 98336 | tf_op jit(solution)/shard_map/ppermute | solution.py:433
  72.7 1.2 collective-permute-done.12.refs_4_
  73.9 0.2 collective-permute-done.13.refs_5_
  74.2 1.7 %collective-permute-done.14.refs_6_ = bf16[384,128]{1,0:T(8,128)(2,1)S(1)} collective-permute-done((bf16[384,128]{1,0:T(8,128)(2,1)S(1)}, bf16[384,128]{1,0:T(8,128)(2,1)S(1)}, u32[]{:S(2)}, u32[]{:S(2)}) %collective-permute-start.14) | collective-permute-done | bytes 98336 | tf_op jit(solution)/shard_map/ppermute | solution.py:433
  75.9 0.4 collective-permute-done.15.refs_7_
  76.3 15.2 %shard_map.91 = (bf16[1152,128]{1,0:T(8,128)(2,1)S(1)}, bf16[1152,128]{1,0:T(8,128)(2,1)S(1)}, bf16[1152,128]{1,0:T(8,128)(2,1)S(1)}, bf16[1152,128]{1,0:T(8,128...) custom-call(s32[1]{0:T(128)} %bitcast.me_s, ...), custom_call_target="tpu_custom_call" | custom-call | flops 3019898880 | bytes 6291456 | tf_op jit(solution)/shard_map/pallas_call | solution.py:415
  91.5 2.3 %collective-permute-start.22 = (bf16[1152,128]{1,0:T(8,128)(2,1)S(1)}, bf16[1152,128]{1,0:T(8,128)(2,1)S(1)}, u32[]{:S(2)}, u32[]{:S(2)}) collective-permute-start(bf16[1152,128]{1,0:T(8,128)(2,1)S(1)} %get-tuple-element.111), channel_id=1, source_target_pairs={{0,24},{4,28},{8,16},{12,20},{16,8},{20,12},{24,0},{28,4},{1,25},{... | collective-permute-start | bytes 884744 | tf_op jit(solution)/shard_map/ppermute | solution.py:433
  93.8 0.1 collective-permute-start.23
  93.9 1.3 %collective-permute-start.17 = (bf16[1152,128]{1,0:T(8,128)(2,1)S(1)}, bf16[1152,128]{1,0:T(8,128)(2,1)S(1)}, u32[]{:S(2)}, u32[]{:S(2)}) collective-permute-start(bf16[1152,128]{1,0:T(8,128)(2,1)S(1)} %get-tuple-element.106), channel_id=1, source_target_pairs={{0,8},{4,12},{8,0},{12,4},{16,24},{20,28},{24,16},{28,20},{1,9},{5... | collective-permute-start | bytes 884744 | tf_op jit(solution)/shard_map/ppermute | solution.py:433
  95.2 1.6 %collective-permute-start.18 = (bf16[1152,128]{1,0:T(8,128)(2,1)S(1)}, bf16[1152,128]{1,0:T(8,128)(2,1)S(1)}, u32[]{:S(2)}, u32[]{:S(2)}) collective-permute-start(bf16[1152,128]{1,0:T(8,128)(2,1)S(1)} %get-tuple-element.107), channel_id=1, source_target_pairs={{0,16},{4,20},{8,24},{12,28},{16,0},{20,4},{24,8},{28,12},{1,17},{... | collective-permute-start | bytes 884744 | tf_op jit(solution)/shard_map/ppermute | solution.py:433
  96.7 5.7 %collective-permute-done.22.refs_0_ = bf16[1152,128]{1,0:T(8,128)(2,1)S(1)} collective-permute-done((bf16[1152,128]{1,0:T(8,128)(2,1)S(1)}, bf16[1152,128]{1,0:T(8,128)(2,1)S(1)}, u32[]{:S(2)}, u32[]{:S(2)}) %collective-permute-start.22) | collective-permute-done | bytes 294944 | tf_op jit(solution)/shard_map/ppermute | solution.py:433
  102.4 5.1 %collective-permute-done.23.refs_1_ = bf16[1152,128]{1,0:T(8,128)(2,1)S(1)} collective-permute-done((bf16[1152,128]{1,0:T(8,128)(2,1)S(1)}, bf16[1152,128]{1,0:T(8,128)(2,1)S(1)}, u32[]{:S(2)}, u32[]{:S(2)}) %collective-permute-start.23) | collective-permute-done | bytes 294944 | tf_op jit(solution)/shard_map/ppermute | solution.py:433
  107.5 1.0 collective-permute-start.21
  108.5 1.0 shard_map.92
  109.5 5.1 %collective-permute-done.17.refs_0_ = bf16[1152,128]{1,0:T(8,128)(2,1)S(1)} collective-permute-done((bf16[1152,128]{1,0:T(8,128)(2,1)S(1)}, bf16[1152,128]{1,0:T(8,128)(2,1)S(1)}, u32[]{:S(2)}, u32[]{:S(2)}) %collective-permute-start.17) | collective-permute-done | bytes 294944 | tf_op jit(solution)/shard_map/ppermute | solution.py:433
  114.6 4.7 %collective-permute-done.19.refs_2_ = bf16[1152,128]{1,0:T(8,128)(2,1)S(1)} collective-permute-done((bf16[1152,128]{1,0:T(8,128)(2,1)S(1)}, bf16[1152,128]{1,0:T(8,128)(2,1)S(1)}, u32[]{:S(2)}, u32[]{:S(2)}) %collective-permute-start.19) | collective-permute-done | bytes 294944 | tf_op jit(solution)/shard_map/ppermute | solution.py:433
  119.3 1.0 collective-permute-done.20.refs_3_
  120.4 1.2 %shard_map.93 = (bf16[384,1024]{1,0:T(8,128)(2,1)}, bf16[384,1024]{1,0:T(8,128)(2,1)}, bf16[384,1024]{1,0:T(8,128)(2,1)}) custom-call(s32[1]{0:T(128)} %bitcast.me_s, bf16[1152,128]{1,0:T(8,128)(2,1)S(1)} %collective-permute-done.17.refs_0_, ...), custom_call_target="tpu_custom_call", output_to_operand_aliasing={{0}: (6, {}), {1}: (7, {}), {2}: (8, {})} | custom-call | tf_op jit(solution)/shard_map/pallas_call | solution.py:88
  (22 shorter events, 0.1 us)
Async XLA Ops:
  0.6 23.1 %collective-permute-start = (bf16[384,1024]{1,0:T(8,128)(2,1)}, bf16[384,1024]{1,0:T(8,128)(2,1)S(1)}, u32[]{:S(2)}, u32[]{:S(2)}) collective-permute-start(bf16[384,1024]{1,0:T(8,128)(2,1)} %o_ref.1), channel_id=1, source_target_pairs={{0,1},{1,2},{2,3},{3,0},{4,5},{5,6},{6,7},{7,4},{8,9},{9,10},{10,1... | collective-permute-start | bytes 2359304 | tf_op jit(solution)/shard_map/ppermute | solution.py:436
  7.3 10.2 %collective-permute-start.1 = (bf16[1168,128]{1,0:T(8,128)(2,1)}, bf16[1168,128]{1,0:T(8,128)(2,1)S(1)}, u32[]{:S(2)}, u32[]{:S(2)}) collective-permute-start(bf16[1168,128]{1,0:T(8,128)(2,1)} %get-tuple-element.61), channel_id=1, source_target_pairs={{0,8},{4,12},{8,0},{12,4},{16,24},{20,28},{24,16},{28,20},{1,9},{5... | collective-permute-start | bytes 897032 | tf_op jit(solution)/shard_map/ppermute | solution.py:433
  8.8 14.9 %collective-permute-start.2 = (bf16[1168,128]{1,0:T(8,128)(2,1)}, bf16[1168,128]{1,0:T(8,128)(2,1)S(1)}, u32[]{:S(2)}, u32[]{:S(2)}) collective-permute-start(bf16[1168,128]{1,0:T(8,128)(2,1)} %get-tuple-element.62), channel_id=1, source_target_pairs={{0,16},{4,20},{8,24},{12,28},{16,0},{20,4},{24,8},{28,12},{1,17},{... | collective-permute-start | bytes 897032 | tf_op jit(solution)/shard_map/ppermute | solution.py:433
  10.3 13.4 %collective-permute-start.3 = (bf16[1168,128]{1,0:T(8,128)(2,1)}, bf16[1168,128]{1,0:T(8,128)(2,1)S(1)}, u32[]{:S(2)}, u32[]{:S(2)}) collective-permute-start(bf16[1168,128]{1,0:T(8,128)(2,1)} %get-tuple-element.63), channel_id=1, source_target_pairs={{0,24},{4,28},{8,16},{12,20},{16,8},{20,12},{24,0},{28,4},{1,25},{... | collective-permute-start | bytes 897032 | tf_op jit(solution)/shard_map/ppermute | solution.py:433
  10.8 4.5 %copy-start = (bf16[384,1024]{1,0:T(8,128)(2,1)S(1)}, bf16[384,1024]{1,0:T(8,128)(2,1)}, u32[]{:S(2)}) copy-start(bf16[384,1024]{1,0:T(8,128)(2,1)} %o_ref.1) | copy-start | bytes 2359300
  15.4 9.9 %copy-start.5 = (bf16[1168,128]{1,0:T(8,128)(2,1)S(1)}, bf16[1168,128]{1,0:T(8,128)(2,1)}, u32[]{:S(2)}) copy-start(bf16[1168,128]{1,0:T(8,128)(2,1)} %get-tuple-element.66) | copy-start | bytes 897028
  15.4 9.9 %copy-start.4 = (bf16[1168,128]{1,0:T(8,128)(2,1)S(1)}, bf16[1168,128]{1,0:T(8,128)(2,1)}, u32[]{:S(2)}) copy-start(bf16[1168,128]{1,0:T(8,128)(2,1)} %get-tuple-element.67) | copy-start | bytes 897028
  15.4 12.3 %copy-start.3 = (bf16[1168,128]{1,0:T(8,128)(2,1)S(1)}, bf16[1168,128]{1,0:T(8,128)(2,1)}, u32[]{:S(2)}) copy-start(bf16[1168,128]{1,0:T(8,128)(2,1)} %get-tuple-element.68) | copy-start | bytes 897028
  15.4 12.7 %copy-start.2 = (bf16[1168,128]{1,0:T(8,128)(2,1)S(1)}, bf16[1168,128]{1,0:T(8,128)(2,1)}, u32[]{:S(2)}) copy-start(bf16[1168,128]{1,0:T(8,128)(2,1)} %get-tuple-element.69) | copy-start | bytes 897028
  23.7 20.3 %collective-permute-start.4 = (bf16[384,1024]{1,0:T(8,128)(2,1)S(1)}, bf16[384,1024]{1,0:T(8,128)(2,1)S(1)}, u32[]{:S(2)}, u32[]{:S(2)}) collective-permute-start(bf16[384,1024]{1,0:T(8,128)(2,1)S(1)} %collective-permute-done.o_ref), channel_id=1, source_target_pairs={{0,1},{1,2},{2,3},{3,0},{4,5},{5,6},{6,7},{7,4},{8,9},{9,10},{10,1... | collective-permute-start | bytes 2359304 | tf_op jit(solution)/shard_map/ppermute | solution.py:436
  25.3 10.3 %collective-permute-start.5 = (bf16[1168,128]{1,0:T(8,128)(2,1)S(1)}, bf16[1168,128]{1,0:T(8,128)(2,1)S(1)}, u32[]{:S(2)}, u32[]{:S(2)}) collective-permute-start(bf16[1168,128]{1,0:T(8,128)(2,1)S(1)} %copy-done.5), channel_id=1, source_target_pairs={{0,28},{4,24},{8,20},{12,16},{16,12},{20,8},{24,4},{28,0},{1,29},{... | collective-permute-start | bytes 897032 | tf_op jit(solution)/shard_map/ppermute | solution.py:433
  25.3 15.7 %collective-permute-start.6 = (bf16[1168,128]{1,0:T(8,128)(2,1)S(1)}, bf16[1168,128]{1,0:T(8,128)(2,1)S(1)}, u32[]{:S(2)}, u32[]{:S(2)}) collective-permute-start(bf16[1168,128]{1,0:T(8,128)(2,1)S(1)} %copy-done.4), channel_id=1, source_target_pairs={{0,20},{4,16},{8,28},{12,24},{16,4},{20,0},{24,12},{28,8},{1,21},{... | collective-permute-start | bytes 897032 | tf_op jit(solution)/shard_map/ppermute | solution.py:433
  27.7 13.3 %collective-permute-start.7 = (bf16[1168,128]{1,0:T(8,128)(2,1)S(1)}, bf16[1168,128]{1,0:T(8,128)(2,1)S(1)}, u32[]{:S(2)}, u32[]{:S(2)}) collective-permute-start(bf16[1168,128]{1,0:T(8,128)(2,1)S(1)} %copy-done.3), channel_id=1, source_target_pairs={{0,12},{4,8},{8,4},{12,0},{16,28},{20,24},{24,20},{28,16},{1,13},{... | collective-permute-start | bytes 897032 | tf_op jit(solution)/shard_map/ppermute | solution.py:433
  28.1 13.0 %collective-permute-start.8 = (bf16[1168,128]{1,0:T(8,128)(2,1)S(1)}, bf16[1168,128]{1,0:T(8,128)(2,1)S(1)}, u32[]{:S(2)}, u32[]{:S(2)}) collective-permute-start(bf16[1168,128]{1,0:T(8,128)(2,1)S(1)} %copy-done.2), channel_id=1, source_target_pairs={{0,4},{4,0},{8,12},{12,8},{16,20},{20,16},{24,28},{28,24},{1,5},{5... | collective-permute-start | bytes 897032 | tf_op jit(solution)/shard_map/ppermute | solution.py:433
  28.6 15.4 %copy-start.1 = (bf16[1168,128]{1,0:T(8,128)(2,1)S(1)}, bf16[1168,128]{1,0:T(8,128)(2,1)}, u32[]{:S(2)}) copy-start(bf16[1168,128]{1,0:T(8,128)(2,1)} %get-tuple-element.73.refs_0_) | copy-start | bytes 897028
  44.0 19.4 %collective-permute-start.9 = (bf16[384,1024]{1,0:T(8,128)(2,1)S(1)}, bf16[384,1024]{1,0:T(8,128)(2,1)S(1)}, u32[]{:S(2)}, u32[]{:S(2)}) collective-permute-start(bf16[384,1024]{1,0:T(8,128)(2,1)S(1)} %collective-permute-done.4.o_ref), channel_id=1, source_target_pairs={{0,1},{1,2},{2,3},{3,0},{4,5},{5,6},{6,7},{7,4},{8,9},{9,10},{10,1... | collective-permute-start | bytes 2359304 | tf_op jit(solution)/shard_map/ppermute | solution.py:436
  64.4 5.6 %collective-permute-start.10 = (bf16[384,128]{1,0:T(8,128)(2,1)S(1)}, bf16[384,128]{1,0:T(8,128)(2,1)S(1)}, u32[]{:S(2)}, u32[]{:S(2)}) collective-permute-start(bf16[384,128]{1,0:T(8,128)(2,1)S(1)} %get-tuple-element.98), channel_id=1, source_target_pairs={{0,24},{4,28},{8,16},{12,20},{16,8},{20,12},{24,0},{28,4},{1,25},{... | collective-permute-start | bytes 294920 | tf_op jit(solution)/shard_map/ppermute | solution.py:433
  66.7 6.1 %collective-permute-start.11 = (bf16[384,128]{1,0:T(8,128)(2,1)S(1)}, bf16[384,128]{1,0:T(8,128)(2,1)S(1)}, u32[]{:S(2)}, u32[]{:S(2)}) collective-permute-start(bf16[384,128]{1,0:T(8,128)(2,1)S(1)} %get-tuple-element.99), channel_id=1, source_target_pairs={{0,28},{4,24},{8,20},{12,16},{16,12},{20,8},{24,4},{28,0},{1,29},{... | collective-permute-start | bytes 294920 | tf_op jit(solution)/shard_map/ppermute | solution.py:433
  66.7 7.3 %collective-permute-start.12 = (bf16[384,128]{1,0:T(8,128)(2,1)S(1)}, bf16[384,128]{1,0:T(8,128)(2,1)S(1)}, u32[]{:S(2)}, u32[]{:S(2)}) collective-permute-start(bf16[384,128]{1,0:T(8,128)(2,1)S(1)} %get-tuple-element.100), channel_id=1, source_target_pairs={{0,8},{4,12},{8,0},{12,4},{16,24},{20,28},{24,16},{28,20},{1,9},{5... | collective-permute-start | bytes 294920 | tf_op jit(solution)/shard_map/ppermute | solution.py:433
  67.0 7.2 %collective-permute-start.13 = (bf16[384,128]{1,0:T(8,128)(2,1)S(1)}, bf16[384,128]{1,0:T(8,128)(2,1)S(1)}, u32[]{:S(2)}, u32[]{:S(2)}) collective-permute-start(bf16[384,128]{1,0:T(8,128)(2,1)S(1)} %get-tuple-element.101), channel_id=1, source_target_pairs={{0,16},{4,20},{8,24},{12,28},{16,0},{20,4},{24,8},{28,12},{1,17},{... | collective-permute-start | bytes 294920 | tf_op jit(solution)/shard_map/ppermute | solution.py:433
  68.0 7.9 %collective-permute-start.14 = (bf16[384,128]{1,0:T(8,128)(2,1)S(1)}, bf16[384,128]{1,0:T(8,128)(2,1)S(1)}, u32[]{:S(2)}, u32[]{:S(2)}) collective-permute-start(bf16[384,128]{1,0:T(8,128)(2,1)S(1)} %get-tuple-element.102), channel_id=1, source_target_pairs={{0,12},{4,8},{8,4},{12,0},{16,28},{20,24},{24,20},{28,16},{1,13},{... | collective-permute-start | bytes 294920 | tf_op jit(solution)/shard_map/ppermute | solution.py:433
  70.0 6.3 %collective-permute-start.15 = (bf16[384,128]{1,0:T(8,128)(2,1)S(1)}, bf16[384,128]{1,0:T(8,128)(2,1)S(1)}, u32[]{:S(2)}, u32[]{:S(2)}) collective-permute-start(bf16[384,128]{1,0:T(8,128)(2,1)S(1)} %get-tuple-element.103), channel_id=1, source_target_pairs={{0,20},{4,16},{8,28},{12,24},{16,4},{20,0},{24,12},{28,8},{1,21},{... | collective-permute-start | bytes 294920 | tf_op jit(solution)/shard_map/ppermute | solution.py:433
  72.7 3.6 %collective-permute-start.16 = (bf16[384,128]{1,0:T(8,128)(2,1)S(1)}, bf16[384,128]{1,0:T(8,128)(2,1)S(1)}, u32[]{:S(2)}, u32[]{:S(2)}) collective-permute-start(bf16[384,128]{1,0:T(8,128)(2,1)S(1)} %get-tuple-element.105), channel_id=1, source_target_pairs={{0,4},{4,0},{8,12},{12,8},{16,20},{20,16},{24,28},{28,24},{1,5},{5... | collective-permute-start | bytes 294920 | tf_op jit(solution)/shard_map/ppermute | solution.py:433
  91.5 10.9 %collective-permute-start.22 = (bf16[1152,128]{1,0:T(8,128)(2,1)S(1)}, bf16[1152,128]{1,0:T(8,128)(2,1)S(1)}, u32[]{:S(2)}, u32[]{:S(2)}) collective-permute-start(bf16[1152,128]{1,0:T(8,128)(2,1)S(1)} %get-tuple-element.111), channel_id=1, source_target_pairs={{0,24},{4,28},{8,16},{12,20},{16,8},{20,12},{24,0},{28,4},{1,25},{... | collective-permute-start | bytes 884744 | tf_op jit(solution)/shard_map/ppermute | solution.py:433
  93.8 13.7 %collective-permute-start.23 = (bf16[1152,128]{1,0:T(8,128)(2,1)S(1)}, bf16[1152,128]{1,0:T(8,128)(2,1)S(1)}, u32[]{:S(2)}, u32[]{:S(2)}) collective-permute-start(bf16[1152,128]{1,0:T(8,128)(2,1)S(1)} %get-tuple-element.112), channel_id=1, source_target_pairs={{0,28},{4,24},{8,20},{12,16},{16,12},{20,8},{24,4},{28,0},{1,29},{... | collective-permute-start | bytes 884744 | tf_op jit(solution)/shard_map/ppermute | solution.py:433
  93.9 20.7 %collective-permute-start.17 = (bf16[1152,128]{1,0:T(8,128)(2,1)S(1)}, bf16[1152,128]{1,0:T(8,128)(2,1)S(1)}, u32[]{:S(2)}, u32[]{:S(2)}) collective-permute-start(bf16[1152,128]{1,0:T(8,128)(2,1)S(1)} %get-tuple-element.106), channel_id=1, source_target_pairs={{0,8},{4,12},{8,0},{12,4},{16,24},{20,28},{24,16},{28,20},{1,9},{5... | collective-permute-start | bytes 884744 | tf_op jit(solution)/shard_map/ppermute | solution.py:433
  95.2 19.4 %collective-permute-start.18 = (bf16[1152,128]{1,0:T(8,128)(2,1)S(1)}, bf16[1152,128]{1,0:T(8,128)(2,1)S(1)}, u32[]{:S(2)}, u32[]{:S(2)}) collective-permute-start(bf16[1152,128]{1,0:T(8,128)(2,1)S(1)} %get-tuple-element.107), channel_id=1, source_target_pairs={{0,16},{4,20},{8,24},{12,28},{16,0},{20,4},{24,8},{28,12},{1,17},{... | collective-permute-start | bytes 884744 | tf_op jit(solution)/shard_map/ppermute | solution.py:433
  96.7 22.6 %collective-permute-start.19 = (bf16[1152,128]{1,0:T(8,128)(2,1)S(1)}, bf16[1152,128]{1,0:T(8,128)(2,1)S(1)}, u32[]{:S(2)}, u32[]{:S(2)}) collective-permute-start(bf16[1152,128]{1,0:T(8,128)(2,1)S(1)} %get-tuple-element.108), channel_id=1, source_target_pairs={{0,12},{4,8},{8,4},{12,0},{16,28},{20,24},{24,20},{28,16},{1,13},{... | collective-permute-start | bytes 884744 | tf_op jit(solution)/shard_map/ppermute | solution.py:433
  102.4 17.9 %collective-permute-start.20 = (bf16[1152,128]{1,0:T(8,128)(2,1)S(1)}, bf16[1152,128]{1,0:T(8,128)(2,1)S(1)}, u32[]{:S(2)}, u32[]{:S(2)}) collective-permute-start(bf16[1152,128]{1,0:T(8,128)(2,1)S(1)} %get-tuple-element.109), channel_id=1, source_target_pairs={{0,20},{4,16},{8,28},{12,24},{16,4},{20,0},{24,12},{28,8},{1,21},{... | collective-permute-start | bytes 884744 | tf_op jit(solution)/shard_map/ppermute | solution.py:433
  107.5 12.8 %collective-permute-start.21 = (bf16[1152,128]{1,0:T(8,128)(2,1)S(1)}, bf16[1152,128]{1,0:T(8,128)(2,1)S(1)}, u32[]{:S(2)}, u32[]{:S(2)}) collective-permute-start(bf16[1152,128]{1,0:T(8,128)(2,1)S(1)} %get-tuple-element.110), channel_id=1, source_target_pairs={{0,4},{4,0},{8,12},{12,8},{16,20},{20,16},{24,28},{28,24},{1,5},{5... | collective-permute-start | bytes 884744 | tf_op jit(solution)/shard_map/ppermute | solution.py:433

commit v16 on v15

--- a/solution.py
+++ b/solution.py
@@ -293,8 +293,7 @@
         refs = refs[2:]
     peers = len(listed)
     blocks = refs[:peers]
-    results = refs[peers:peers + heads]
-    g_ref, dot_ref, dk_acc, dv_acc, dq_acc, p0, ds0, p1, ds1 = refs[peers + heads:]
+    dq_acc, dk_acc, dv_acc, g_ref, dot_ref, p0, ds0, p1, ds1 = refs[peers:]
     scale = HD ** (-0.5)
     factor = scale * math.log2(math.e)
     me = me_s[0]
@@ -341,11 +340,27 @@
         dq_acc[:, queries] += dot32(kt_ref[:, keys], ds_ref[...])
 
     pipelined(plan_q, plan_k, count_ref, early, late, ((p0, ds0), (p1, ds1)))
-    for d, result in enumerate(results):
-        own = aligned(me ^ d, rows)
-        result[:rows, :] = (scale * dq_acc[:, own]).astype(result.dtype).T
-        result[rows:2 * rows, :] = (scale * dk_acc[own, :]).astype(result.dtype)
-        result[2 * rows:, :] = dv_acc[own, :].astype(result.dtype)
+
+
+def finish_kernel(listed, rows, me_s, dq_ref, dk_ref, dv_ref, *results):
+    scale = HD ** (-0.5)
+    for d, result in zip(listed, results):
+        own = aligned(me_s[0] ^ d, rows)
+        result[:rows, :] = (scale * dq_ref[:, own]).astype(result.dtype).T
+        result[rows:2 * rows, :] = (scale * dk_ref[own, :]).astype(result.dtype)
+        result[2 * rows:, :] = dv_ref[own, :].astype(result.dtype)
+
+
+def finish(me, listed, totals, rows):
+    out_shape = [jax.ShapeDtypeStruct((3 * rows, HD), jnp.bfloat16)] * len(listed)
+    results = pl.pallas_call(
+        functools.partial(finish_kernel, listed, rows),
+        in_specs=[SMEM_SPEC] + [VMEM_SPEC] * 3,
+        out_specs=[VMEM_SPEC] * len(listed),
+        out_shape=out_shape,
+        compiler_params=params([*totals, *out_shape]),
+    )(me, *totals)
+    return dict(zip(listed, results))
 
 
 def keeps_list(total, peers, heads):
@@ -403,19 +418,17 @@
     bq, bk = block_sizes(total)[1]
     vectors, plan = state[:-3], state[-3:]
     kept = keeps_list(total, peers, heads)
-    out_shape = [jax.ShapeDtypeStruct((3 * rows, HD), jnp.bfloat16)] * heads
+    shapes = [(HD, total), (total, HD), (total, HD)]
+    out_shape = [jax.ShapeDtypeStruct(shape, jnp.float32) for shape in shapes]
     scratch = [
         pltpu.VMEM((total, HD), jnp.bfloat16),
         pltpu.VMEM((1, total), jnp.float32),
-        pltpu.VMEM((total, HD), jnp.float32),
-        pltpu.VMEM((total, HD), jnp.float32),
-        pltpu.VMEM((HD, total), jnp.float32),
         *[pltpu.VMEM((bk, bq), jnp.bfloat16)] * 4,
     ]
     return pl.pallas_call(
         functools.partial(backward_kernel, listed, heads, rows, bq, bk, kept),
         in_specs=[SMEM_SPEC] * 4 + [VMEM_SPEC] * (len(vectors) + peers),
-        out_specs=[VMEM_SPEC] * heads,
+        out_specs=[VMEM_SPEC] * 3,
         out_shape=out_shape,
         scratch_shapes=scratch,
         compiler_params=params([*vectors, *blocks, *out_shape], scratch),
@@ -474,13 +487,15 @@
                     received[d] = block
     grads = exchange_all(acc, far_first)
 
-    results = attention_backward(me_vector, heads, state, far_first, grads)
-    returned = exchange_all(results, returning)
-    early = [d for d in returning if d == 0 or bin(d >> 1).count("1") > 1]
-    late = [d for d in returning if d not in early]
-    block_of = dict(zip(returning, returned))
-    partial = unpack_heads(me_vector, early, [block_of[d] for d in early], rows, heads)
-    return tuple(unpack_heads(me_vector, late, [block_of[d] for d in late], rows, heads, partial))
+    totals = attention_backward(me_vector, heads, state, far_first, grads)
+
+    far = [d for d in returning if bin(d >> 1).count("1") > 1]
+    near = [d for d in returning if d not in far]
+    results = {**(finish(me_vector, far, totals, rows) if far else {}), **finish(me_vector, near, totals, rows)}
+    returned = {d: exchange(results[d], d) for d in returning}
+    early, late = [*far, 0], [d for d in near if d > 0]
+    partial = unpack_heads(me_vector, early, [returned[d] for d in early], rows, heads)
+    return tuple(unpack_heads(me_vector, late, [returned[d] for d in late], rows, heads, partial))
 
 
 def solution(mesh):

time: 122 us -> 120 us (0.984)
  Pallas kernels: 43 us -> 38.7 us
  waiting for transfers between devices: 49.8 us -> 51.8 us
    pallas_call x1, Pallas kernels: 15.2 us -> 12.7 us  [attention_backward(): pl.pallas_call(functools.partial(backward_kernel, listed, heads, rows, bq...]
    ppermute x3, waiting for transfers between devices: 3.32 us -> 5.69 us  [pass_on(): lax.ppermute(x, 'head', [(i, (i + 1) % groups) for i in range(groups)])]
    pallas_call x1, Pallas kernels: 17.9 us -> 15.6 us  [attention_forward(): pl.pallas_call(functools.partial(forward_kernel, peers, heads, rows, bq,...]
  transfers between devices with their start and end apart: 24 -> 24, of which waited for: 17 -> 17; matrix products, arithmetic and copies ran while one was open for 4% -> 4% of each run, Pallas kernels for 21% -> 20%
where the time goes in v16:
time: 120 us; the launch traced here: 119 us
  waiting for transfers between devices  51.8 us (43%)
  Pallas kernels  38.7 us (32%)
  starting transfers between devices  23.5 us (20%)
  local copies, waits for them, and re-layouts  4.56 us (4%)
    ppermute x21, waiting for transfers between devices, exchange(): lax.ppermute(x, 'seq', [(i, i ^ d) for i in range(peers)])  46.1 us
    ppermute x21, starting transfers between devices, exchange(): lax.ppermute(x, 'seq', [(i, i ^ d) for i in range(peers)])  18.8 us
    pallas_call x1, Pallas kernels, attention_forward(): pl.pallas_call(functools.partial(forward_kernel, peers, heads, rows, bq,...  15.6 us
    pallas_call x1, Pallas kernels, attention_backward(): pl.pallas_call(functools.partial(backward_kernel, listed, heads, rows, bq...  12.7 us
    ppermute x3, waiting for transfers between devices, pass_on(): lax.ppermute(x, 'head', [(i, (i + 1) % groups) for i in range(groups)])  5.69 us
    ppermute x3, starting transfers between devices, pass_on(): lax.ppermute(x, 'head', [(i, (i + 1) % groups) for i in range(groups)])  4.66 us
    dynamic_slice x1, local copies, waits for them, and re-layouts, per_device(): lax.dynamic_slice_in_dim(out_weight, block * width, width, 1)  4.54 us
    pallas_call x1, Pallas kernels, pack_heads(): pl.pallas_call(functools.partial(pack_kernel, heads, rows), in_specs=[SME...  3.62 us
  transfers between devices with their start and end apart: 24, of which 17 were waited for; matrix products, arithmetic and copies ran while one was open for 4% of the time, Pallas kernels for 20%

profile of v16, /device:TPU:0, one launch (start us, length us, event | category | flops | bytes accessed | tf_op | source)
XLA Modules:
  0.0 119.3 jit_solution(17154219043570479080)
XLA Ops:
  0.6 3.1 %collective-permute-start = (bf16[384,1024]{1,0:T(8,128)(2,1)}, bf16[384,1024]{1,0:T(8,128)(2,1)S(1)}, u32[]{:S(2)}, u32[]{:S(2)}) collective-permute-start(bf16[384,1024]{1,0:T(8,128)(2,1)} %o_ref.1), channel_id=1, source_target_pairs={{0,1},{1,2},{2,3},{3,0},{4,5},{5,6},{6,7},{7,4},{8,9},{9,10},{10,1... | collective-permute-start | bytes 2359304 | tf_op jit(solution)/shard_map/ppermute | solution.py:449
  3.7 3.6 %shard_map.85 = (bf16[1168,128]{1,0:T(8,128)(2,1)}, bf16[1168,128]{1,0:T(8,128)(2,1)}, bf16[1168,128]{1,0:T(8,128)(2,1)}, bf16[1168,128]{1,0:T(8,128)(2,1)}, bf1...) custom-call(s32[1]{0:T(128)} %bitcast.me_s, ...), custom_call_target="tpu_custom_call" | custom-call | tf_op jit(solution)/shard_map/pallas_call | solution.py:63
  7.3 1.5 %collective-permute-start.1 = (bf16[1168,128]{1,0:T(8,128)(2,1)}, bf16[1168,128]{1,0:T(8,128)(2,1)S(1)}, u32[]{:S(2)}, u32[]{:S(2)}) collective-permute-start(bf16[1168,128]{1,0:T(8,128)(2,1)} %get-tuple-element.64), channel_id=1, source_target_pairs={{0,8},{4,12},{8,0},{12,4},{16,24},{20,28},{24,16},{28,20},{1,9},{5... | collective-permute-start | bytes 897032 | tf_op jit(solution)/shard_map/ppermute | solution.py:446
  8.8 1.5 %collective-permute-start.2 = (bf16[1168,128]{1,0:T(8,128)(2,1)}, bf16[1168,128]{1,0:T(8,128)(2,1)S(1)}, u32[]{:S(2)}, u32[]{:S(2)}) collective-permute-start(bf16[1168,128]{1,0:T(8,128)(2,1)} %get-tuple-element.65), channel_id=1, source_target_pairs={{0,16},{4,20},{8,24},{12,28},{16,0},{20,4},{24,8},{28,12},{1,17},{... | collective-permute-start | bytes 897032 | tf_op jit(solution)/shard_map/ppermute | solution.py:446
  10.3 0.5 collective-permute-start.3
  10.8 4.5 %constant_dynamic-slice_fusion = (bf16[1024,1024]{1,0:T(8,128)(2,1)S(1)}, bf16[1024,1024]{1,0:T(8,128)(2,1)S(1)}, bf16[1024,1024]{1,0:T(8,128)(2,1)S(1)}, bf16[1024,1024]{1,0:T(8,128)(2,1)S(1)}) fusion(bf16[1024,4096]{1,0:T(8,128)(2,1)} %param.10, s32[]{:T(128)S(6)} %select_n.15, s32[]{:T(128)S(6)} %select_n.13, s32[]{:T(128)S(6)} %select_n.12, s32[]{:T(128)S(6)} %select_n.14), kind=kLoop, calls=%fused_computation | loop fusion | bytes 16777232 | tf_op jit(solution)/shard_map/dynamic_slice | solution.py:470
  15.4 1.0 shard_map.86.refs_0_
  16.4 1.1 collective-permute-done.1.refs_2_
  17.6 6.2 %collective-permute-done.2.refs_4_ = bf16[1168,128]{1,0:T(8,128)(2,1)S(1)} collective-permute-done((bf16[1168,128]{1,0:T(8,128)(2,1)}, bf16[1168,128]{1,0:T(8,128)(2,1)S(1)}, u32[]{:S(2)}, u32[]{:S(2)}) %collective-permute-start.2) | collective-permute-done | bytes 299040 | tf_op jit(solution)/shard_map/ppermute | solution.py:446
  23.7 1.6 %collective-permute-start.4 = (bf16[384,1024]{1,0:T(8,128)(2,1)S(1)}, bf16[384,1024]{1,0:T(8,128)(2,1)S(1)}, u32[]{:S(2)}, u32[]{:S(2)}) collective-permute-start(bf16[384,1024]{1,0:T(8,128)(2,1)S(1)} %collective-permute-done.o_ref), channel_id=1, source_target_pairs={{0,1},{1,2},{2,3},{3,0},{4,5},{5,6},{6,7},{7,4},{8,9},{9,10},{10,1... | collective-permute-start | bytes 2359304 | tf_op jit(solution)/shard_map/ppermute | solution.py:449
  25.3 2.4 %collective-permute-start.6 = (bf16[1168,128]{1,0:T(8,128)(2,1)S(1)}, bf16[1168,128]{1,0:T(8,128)(2,1)S(1)}, u32[]{:S(2)}, u32[]{:S(2)}) collective-permute-start(bf16[1168,128]{1,0:T(8,128)(2,1)S(1)} %copy-done.4), channel_id=1, source_target_pairs={{0,20},{4,16},{8,28},{12,24},{16,4},{20,0},{24,12},{28,8},{1,21},{... | collective-permute-start | bytes 897032 | tf_op jit(solution)/shard_map/ppermute | solution.py:446
  27.7 0.4 collective-permute-start.7
  28.1 0.6 collective-permute-start.8
  28.6 1.0 shard_map.87.refs_0_
  29.7 6.0 %collective-permute-done.5.refs_7_ = bf16[1168,128]{1,0:T(8,128)(2,1)S(1)} collective-permute-done((bf16[1168,128]{1,0:T(8,128)(2,1)S(1)}, bf16[1168,128]{1,0:T(8,128)(2,1)S(1)}, u32[]{:S(2)}, u32[]{:S(2)}) %collective-permute-start.5) | collective-permute-done | bytes 299040 | tf_op jit(solution)/shard_map/ppermute | solution.py:446
  35.6 5.4 %collective-permute-done.6.refs_5_ = bf16[1168,128]{1,0:T(8,128)(2,1)S(1)} collective-permute-done((bf16[1168,128]{1,0:T(8,128)(2,1)S(1)}, bf16[1168,128]{1,0:T(8,128)(2,1)S(1)}, u32[]{:S(2)}, u32[]{:S(2)}) %collective-permute-start.6) | collective-permute-done | bytes 299040 | tf_op jit(solution)/shard_map/ppermute | solution.py:446
  41.1 3.0 %collective-permute-done.4.o_ref = bf16[384,1024]{1,0:T(8,128)(2,1)S(1)} collective-permute-done((bf16[384,1024]{1,0:T(8,128)(2,1)S(1)}, bf16[384,1024]{1,0:T(8,128)(2,1)S(1)}, u32[]{:S(2)}, u32[]{:S(2)}) %collective-permute-start.4) | collective-permute-done | bytes 786464 | tf_op jit(solution)/shard_map/ppermute | solution.py:449
  44.0 15.6 %shard_map.88 = (bf16[3072,128]{1,0:T(8,128)(2,1)S(1)}, bf16[3072,256]{1,0:T(8,128)(2,1)S(1)}, bf16[3072,256]{1,0:T(8,128)(2,1)S(1)}, bf16[128,3072]{1,0:T(8,128...) custom-call(s32[1]{0:T(128)} %bitcast.me_s, ...), custom_call_target="tpu_custom_call" | custom-call | flops 1811939328 | bytes 6291456 | tf_op jit(solution)/shard_map/pallas_call | solution.py:404
  59.6 1.0 shard_map.89.acc_ref
  60.6 2.7 %collective-permute-done.9.o_ref = bf16[384,1024]{1,0:T(8,128)(2,1)S(1)} collective-permute-done((bf16[384,1024]{1,0:T(8,128)(2,1)S(1)}, bf16[384,1024]{1,0:T(8,128)(2,1)S(1)}, u32[]{:S(2)}, u32[]{:S(2)}) %collective-permute-start.9) | collective-permute-done | bytes 786464 | tf_op jit(solution)/shard_map/ppermute | solution.py:449
  63.4 1.0 shard_map.90
  64.4 2.3 %collective-permute-start.10 = (bf16[384,128]{1,0:T(8,128)(2,1)S(1)}, bf16[384,128]{1,0:T(8,128)(2,1)S(1)}, u32[]{:S(2)}, u32[]{:S(2)}) collective-permute-start(bf16[384,128]{1,0:T(8,128)(2,1)S(1)} %get-tuple-element.101), channel_id=1, source_target_pairs={{0,24},{4,28},{8,16},{12,20},{16,8},{20,12},{24,0},{28,4},{1,25},{... | collective-permute-start | bytes 294920 | tf_op jit(solution)/shard_map/ppermute | solution.py:446
  66.7 0.3 collective-permute-start.12
  67.0 1.0 collective-permute-start.13
  68.0 1.7 %collective-permute-start.14 = (bf16[384,128]{1,0:T(8,128)(2,1)S(1)}, bf16[384,128]{1,0:T(8,128)(2,1)S(1)}, u32[]{:S(2)}, u32[]{:S(2)}) collective-permute-start(bf16[384,128]{1,0:T(8,128)(2,1)S(1)} %get-tuple-element.105), channel_id=1, source_target_pairs={{0,12},{4,8},{8,4},{12,0},{16,28},{20,24},{24,20},{28,16},{1,13},{... | collective-permute-start | bytes 294920 | tf_op jit(solution)/shard_map/ppermute | solution.py:446
  69.6 0.4 collective-permute-done.10.refs_2_
  70.0 0.5 collective-permute-start.15
  70.5 2.3 %collective-permute-done.11.refs_3_ = bf16[384,128]{1,0:T(8,128)(2,1)S(1)} collective-permute-done((bf16[384,128]{1,0:T(8,128)(2,1)S(1)}, bf16[384,128]{1,0:T(8,128)(2,1)S(1)}, u32[]{:S(2)}, u32[]{:S(2)}) %collective-permute-start.11) | collective-permute-done | bytes 98336 | tf_op jit(solution)/shard_map/ppermute | solution.py:446
  72.7 1.2 collective-permute-done.12.refs_4_
  73.9 0.2 collective-permute-done.13.refs_5_
  74.2 1.7 %collective-permute-done.14.refs_6_ = bf16[384,128]{1,0:T(8,128)(2,1)S(1)} collective-permute-done((bf16[384,128]{1,0:T(8,128)(2,1)S(1)}, bf16[384,128]{1,0:T(8,128)(2,1)S(1)}, u32[]{:S(2)}, u32[]{:S(2)}) %collective-permute-start.14) | collective-permute-done | bytes 98336 | tf_op jit(solution)/shard_map/ppermute | solution.py:446
  75.9 0.4 collective-permute-done.15.refs_7_
  76.3 12.7 %shard_map.91 = (f32[128,3072]{1,0:T(8,128)S(1)}, f32[3072,128]{1,0:T(8,128)S(1)}, f32[3072,128]{1,0:T(8,128)S(1)}) custom-call(s32[1]{0:T(128)} %bitcast.me_s, s32[80]{0:T(128)S(1)} %get-tuple-element.84.plan_q, s32[80]{0:T(128)S(1)} %get-tuple-element.85.plan_k, s32[2]{0:T(128)S(1)} %get-tuple-element.86.count_ref, ...), custom_call_target="tpu_custom_call" | custom-call | flops 3019898880 | bytes 6291456 | tf_op jit(solution)/shard_map/pallas_call | solution.py:428
  89.0 0.2 shard_map.93
  89.2 2.3 %collective-permute-start.22 = (bf16[1152,128]{1,0:T(8,128)(2,1)S(1)}, bf16[1152,128]{1,0:T(8,128)(2,1)S(1)}, u32[]{:S(2)}, u32[]{:S(2)}) collective-permute-start(bf16[1152,128]{1,0:T(8,128)(2,1)S(1)} %get-tuple-element.117), channel_id=1, source_target_pairs={{0,24},{4,28},{8,16},{12,20},{16,8},{20,12},{24,0},{28,4},{1,25},{... | collective-permute-start | bytes 884744 | tf_op jit(solution)/shard_map/ppermute | solution.py:446
  91.5 0.1 collective-permute-start.23
  91.6 0.3 shard_map.92
  91.9 1.3 %collective-permute-start.17 = (bf16[1152,128]{1,0:T(8,128)(2,1)S(1)}, bf16[1152,128]{1,0:T(8,128)(2,1)S(1)}, u32[]{:S(2)}, u32[]{:S(2)}) collective-permute-start(bf16[1152,128]{1,0:T(8,128)(2,1)S(1)} %get-tuple-element.112), channel_id=1, source_target_pairs={{0,8},{4,12},{8,0},{12,4},{16,24},{20,28},{24,16},{28,20},{1,9},{5... | collective-permute-start | bytes 884744 | tf_op jit(solution)/shard_map/ppermute | solution.py:446
  93.3 1.6 %collective-permute-start.18 = (bf16[1152,128]{1,0:T(8,128)(2,1)S(1)}, bf16[1152,128]{1,0:T(8,128)(2,1)S(1)}, u32[]{:S(2)}, u32[]{:S(2)}) collective-permute-start(bf16[1152,128]{1,0:T(8,128)(2,1)S(1)} %get-tuple-element.113), channel_id=1, source_target_pairs={{0,16},{4,20},{8,24},{12,28},{16,0},{20,4},{24,8},{28,12},{1,17},{... | collective-permute-start | bytes 884744 | tf_op jit(solution)/shard_map/ppermute | solution.py:446
  94.8 0.0 collective-permute-start.19
  94.9 5.3 %collective-permute-done.22.refs_0_ = bf16[1152,128]{1,0:T(8,128)(2,1)S(1)} collective-permute-done((bf16[1152,128]{1,0:T(8,128)(2,1)S(1)}, bf16[1152,128]{1,0:T(8,128)(2,1)S(1)}, u32[]{:S(2)}, u32[]{:S(2)}) %collective-permute-start.22) | collective-permute-done | bytes 294944 | tf_op jit(solution)/shard_map/ppermute | solution.py:446
  100.1 5.1 %collective-permute-done.23.refs_1_ = bf16[1152,128]{1,0:T(8,128)(2,1)S(1)} collective-permute-done((bf16[1152,128]{1,0:T(8,128)(2,1)S(1)}, bf16[1152,128]{1,0:T(8,128)(2,1)S(1)}, u32[]{:S(2)}, u32[]{:S(2)}) %collective-permute-start.23) | collective-permute-done | bytes 294944 | tf_op jit(solution)/shard_map/ppermute | solution.py:446
  105.2 1.0 collective-permute-start.21
  106.2 1.0 shard_map.94
  107.2 5.1 %collective-permute-done.17.refs_0_ = bf16[1152,128]{1,0:T(8,128)(2,1)S(1)} collective-permute-done((bf16[1152,128]{1,0:T(8,128)(2,1)S(1)}, bf16[1152,128]{1,0:T(8,128)(2,1)S(1)}, u32[]{:S(2)}, u32[]{:S(2)}) %collective-permute-start.17) | collective-permute-done | bytes 294944 | tf_op jit(solution)/shard_map/ppermute | solution.py:446
  112.3 4.7 %collective-permute-done.19.refs_2_ = bf16[1152,128]{1,0:T(8,128)(2,1)S(1)} collective-permute-done((bf16[1152,128]{1,0:T(8,128)(2,1)S(1)}, bf16[1152,128]{1,0:T(8,128)(2,1)S(1)}, u32[]{:S(2)}, u32[]{:S(2)}) %collective-permute-start.19) | collective-permute-done | bytes 294944 | tf_op jit(solution)/shard_map/ppermute | solution.py:446
  117.0 1.0 collective-permute-done.20.refs_3_
  118.0 1.2 %shard_map.95 = (bf16[384,1024]{1,0:T(8,128)(2,1)}, bf16[384,1024]{1,0:T(8,128)(2,1)}, bf16[384,1024]{1,0:T(8,128)(2,1)}) custom-call(s32[1]{0:T(128)} %bitcast.me_s, bf16[1152,128]{1,0:T(8,128)(2,1)S(1)} %collective-permute-done.17.refs_0_, ...), custom_call_target="tpu_custom_call", output_to_operand_aliasing={{0}: (6, {}), {1}: (7, {}), {2}: (8, {})} | custom-call | tf_op jit(solution)/shard_map/pallas_call | solution.py:88
  (24 shorter events, 0.1 us)
Async XLA Ops:
  0.6 23.1 %collective-permute-start = (bf16[384,1024]{1,0:T(8,128)(2,1)}, bf16[384,1024]{1,0:T(8,128)(2,1)S(1)}, u32[]{:S(2)}, u32[]{:S(2)}) collective-permute-start(bf16[384,1024]{1,0:T(8,128)(2,1)} %o_ref.1), channel_id=1, source_target_pairs={{0,1},{1,2},{2,3},{3,0},{4,5},{5,6},{6,7},{7,4},{8,9},{9,10},{10,1... | collective-permute-start | bytes 2359304 | tf_op jit(solution)/shard_map/ppermute | solution.py:449
  7.3 10.2 %collective-permute-start.1 = (bf16[1168,128]{1,0:T(8,128)(2,1)}, bf16[1168,128]{1,0:T(8,128)(2,1)S(1)}, u32[]{:S(2)}, u32[]{:S(2)}) collective-permute-start(bf16[1168,128]{1,0:T(8,128)(2,1)} %get-tuple-element.64), channel_id=1, source_target_pairs={{0,8},{4,12},{8,0},{12,4},{16,24},{20,28},{24,16},{28,20},{1,9},{5... | collective-permute-start | bytes 897032 | tf_op jit(solution)/shard_map/ppermute | solution.py:446
  8.8 14.9 %collective-permute-start.2 = (bf16[1168,128]{1,0:T(8,128)(2,1)}, bf16[1168,128]{1,0:T(8,128)(2,1)S(1)}, u32[]{:S(2)}, u32[]{:S(2)}) collective-permute-start(bf16[1168,128]{1,0:T(8,128)(2,1)} %get-tuple-element.65), channel_id=1, source_target_pairs={{0,16},{4,20},{8,24},{12,28},{16,0},{20,4},{24,8},{28,12},{1,17},{... | collective-permute-start | bytes 897032 | tf_op jit(solution)/shard_map/ppermute | solution.py:446
  10.3 13.4 %collective-permute-start.3 = (bf16[1168,128]{1,0:T(8,128)(2,1)}, bf16[1168,128]{1,0:T(8,128)(2,1)S(1)}, u32[]{:S(2)}, u32[]{:S(2)}) collective-permute-start(bf16[1168,128]{1,0:T(8,128)(2,1)} %get-tuple-element.66), channel_id=1, source_target_pairs={{0,24},{4,28},{8,16},{12,20},{16,8},{20,12},{24,0},{28,4},{1,25},{... | collective-permute-start | bytes 897032 | tf_op jit(solution)/shard_map/ppermute | solution.py:446
  10.8 4.5 %copy-start = (bf16[384,1024]{1,0:T(8,128)(2,1)S(1)}, bf16[384,1024]{1,0:T(8,128)(2,1)}, u32[]{:S(2)}) copy-start(bf16[384,1024]{1,0:T(8,128)(2,1)} %o_ref.1) | copy-start | bytes 2359300
  15.4 9.9 %copy-start.5 = (bf16[1168,128]{1,0:T(8,128)(2,1)S(1)}, bf16[1168,128]{1,0:T(8,128)(2,1)}, u32[]{:S(2)}) copy-start(bf16[1168,128]{1,0:T(8,128)(2,1)} %get-tuple-element.69) | copy-start | bytes 897028
  15.4 9.9 %copy-start.4 = (bf16[1168,128]{1,0:T(8,128)(2,1)S(1)}, bf16[1168,128]{1,0:T(8,128)(2,1)}, u32[]{:S(2)}) copy-start(bf16[1168,128]{1,0:T(8,128)(2,1)} %get-tuple-element.70) | copy-start | bytes 897028
  15.4 12.3 %copy-start.3 = (bf16[1168,128]{1,0:T(8,128)(2,1)S(1)}, bf16[1168,128]{1,0:T(8,128)(2,1)}, u32[]{:S(2)}) copy-start(bf16[1168,128]{1,0:T(8,128)(2,1)} %get-tuple-element.71) | copy-start | bytes 897028
  15.4 12.7 %copy-start.2 = (bf16[1168,128]{1,0:T(8,128)(2,1)S(1)}, bf16[1168,128]{1,0:T(8,128)(2,1)}, u32[]{:S(2)}) copy-start(bf16[1168,128]{1,0:T(8,128)(2,1)} %get-tuple-element.72) | copy-start | bytes 897028
  23.7 20.3 %collective-permute-start.4 = (bf16[384,1024]{1,0:T(8,128)(2,1)S(1)}, bf16[384,1024]{1,0:T(8,128)(2,1)S(1)}, u32[]{:S(2)}, u32[]{:S(2)}) collective-permute-start(bf16[384,1024]{1,0:T(8,128)(2,1)S(1)} %collective-permute-done.o_ref), channel_id=1, source_target_pairs={{0,1},{1,2},{2,3},{3,0},{4,5},{5,6},{6,7},{7,4},{8,9},{9,10},{10,1... | collective-permute-start | bytes 2359304 | tf_op jit(solution)/shard_map/ppermute | solution.py:449
  25.3 10.3 %collective-permute-start.5 = (bf16[1168,128]{1,0:T(8,128)(2,1)S(1)}, bf16[1168,128]{1,0:T(8,128)(2,1)S(1)}, u32[]{:S(2)}, u32[]{:S(2)}) collective-permute-start(bf16[1168,128]{1,0:T(8,128)(2,1)S(1)} %copy-done.5), channel_id=1, source_target_pairs={{0,28},{4,24},{8,20},{12,16},{16,12},{20,8},{24,4},{28,0},{1,29},{... | collective-permute-start | bytes 897032 | tf_op jit(solution)/shard_map/ppermute | solution.py:446
  25.3 15.7 %collective-permute-start.6 = (bf16[1168,128]{1,0:T(8,128)(2,1)S(1)}, bf16[1168,128]{1,0:T(8,128)(2,1)S(1)}, u32[]{:S(2)}, u32[]{:S(2)}) collective-permute-start(bf16[1168,128]{1,0:T(8,128)(2,1)S(1)} %copy-done.4), channel_id=1, source_target_pairs={{0,20},{4,16},{8,28},{12,24},{16,4},{20,0},{24,12},{28,8},{1,21},{... | collective-permute-start | bytes 897032 | tf_op jit(solution)/shard_map/ppermute | solution.py:446
  27.7 13.3 %collective-permute-start.7 = (bf16[1168,128]{1,0:T(8,128)(2,1)S(1)}, bf16[1168,128]{1,0:T(8,128)(2,1)S(1)}, u32[]{:S(2)}, u32[]{:S(2)}) collective-permute-start(bf16[1168,128]{1,0:T(8,128)(2,1)S(1)} %copy-done.3), channel_id=1, source_target_pairs={{0,12},{4,8},{8,4},{12,0},{16,28},{20,24},{24,20},{28,16},{1,13},{... | collective-permute-start | bytes 897032 | tf_op jit(solution)/shard_map/ppermute | solution.py:446
  28.1 13.0 %collective-permute-start.8 = (bf16[1168,128]{1,0:T(8,128)(2,1)S(1)}, bf16[1168,128]{1,0:T(8,128)(2,1)S(1)}, u32[]{:S(2)}, u32[]{:S(2)}) collective-permute-start(bf16[1168,128]{1,0:T(8,128)(2,1)S(1)} %copy-done.2), channel_id=1, source_target_pairs={{0,4},{4,0},{8,12},{12,8},{16,20},{20,16},{24,28},{28,24},{1,5},{5... | collective-permute-start | bytes 897032 | tf_op jit(solution)/shard_map/ppermute | solution.py:446
  28.6 15.4 %copy-start.1 = (bf16[1168,128]{1,0:T(8,128)(2,1)S(1)}, bf16[1168,128]{1,0:T(8,128)(2,1)}, u32[]{:S(2)}) copy-start(bf16[1168,128]{1,0:T(8,128)(2,1)} %get-tuple-element.76.refs_0_) | copy-start | bytes 897028
  44.0 19.4 %collective-permute-start.9 = (bf16[384,1024]{1,0:T(8,128)(2,1)S(1)}, bf16[384,1024]{1,0:T(8,128)(2,1)S(1)}, u32[]{:S(2)}, u32[]{:S(2)}) collective-permute-start(bf16[384,1024]{1,0:T(8,128)(2,1)S(1)} %collective-permute-done.4.o_ref), channel_id=1, source_target_pairs={{0,1},{1,2},{2,3},{3,0},{4,5},{5,6},{6,7},{7,4},{8,9},{9,10},{10,1... | collective-permute-start | bytes 2359304 | tf_op jit(solution)/shard_map/ppermute | solution.py:449
  64.4 5.6 %collective-permute-start.10 = (bf16[384,128]{1,0:T(8,128)(2,1)S(1)}, bf16[384,128]{1,0:T(8,128)(2,1)S(1)}, u32[]{:S(2)}, u32[]{:S(2)}) collective-permute-start(bf16[384,128]{1,0:T(8,128)(2,1)S(1)} %get-tuple-element.101), channel_id=1, source_target_pairs={{0,24},{4,28},{8,16},{12,20},{16,8},{20,12},{24,0},{28,4},{1,25},{... | collective-permute-start | bytes 294920 | tf_op jit(solution)/shard_map/ppermute | solution.py:446
  66.7 6.1 %collective-permute-start.11 = (bf16[384,128]{1,0:T(8,128)(2,1)S(1)}, bf16[384,128]{1,0:T(8,128)(2,1)S(1)}, u32[]{:S(2)}, u32[]{:S(2)}) collective-permute-start(bf16[384,128]{1,0:T(8,128)(2,1)S(1)} %get-tuple-element.102), channel_id=1, source_target_pairs={{0,28},{4,24},{8,20},{12,16},{16,12},{20,8},{24,4},{28,0},{1,29},{... | collective-permute-start | bytes 294920 | tf_op jit(solution)/shard_map/ppermute | solution.py:446
  66.7 7.3 %collective-permute-start.12 = (bf16[384,128]{1,0:T(8,128)(2,1)S(1)}, bf16[384,128]{1,0:T(8,128)(2,1)S(1)}, u32[]{:S(2)}, u32[]{:S(2)}) collective-permute-start(bf16[384,128]{1,0:T(8,128)(2,1)S(1)} %get-tuple-element.103), channel_id=1, source_target_pairs={{0,8},{4,12},{8,0},{12,4},{16,24},{20,28},{24,16},{28,20},{1,9},{5... | collective-permute-start | bytes 294920 | tf_op jit(solution)/shard_map/ppermute | solution.py:446
  67.0 7.2 %collective-permute-start.13 = (bf16[384,128]{1,0:T(8,128)(2,1)S(1)}, bf16[384,128]{1,0:T(8,128)(2,1)S(1)}, u32[]{:S(2)}, u32[]{:S(2)}) collective-permute-start(bf16[384,128]{1,0:T(8,128)(2,1)S(1)} %get-tuple-element.104), channel_id=1, source_target_pairs={{0,16},{4,20},{8,24},{12,28},{16,0},{20,4},{24,8},{28,12},{1,17},{... | collective-permute-start | bytes 294920 | tf_op jit(solution)/shard_map/ppermute | solution.py:446
  68.0 7.9 %collective-permute-start.14 = (bf16[384,128]{1,0:T(8,128)(2,1)S(1)}, bf16[384,128]{1,0:T(8,128)(2,1)S(1)}, u32[]{:S(2)}, u32[]{:S(2)}) collective-permute-start(bf16[384,128]{1,0:T(8,128)(2,1)S(1)} %get-tuple-element.105), channel_id=1, source_target_pairs={{0,12},{4,8},{8,4},{12,0},{16,28},{20,24},{24,20},{28,16},{1,13},{... | collective-permute-start | bytes 294920 | tf_op jit(solution)/shard_map/ppermute | solution.py:446
  70.0 6.3 %collective-permute-start.15 = (bf16[384,128]{1,0:T(8,128)(2,1)S(1)}, bf16[384,128]{1,0:T(8,128)(2,1)S(1)}, u32[]{:S(2)}, u32[]{:S(2)}) collective-permute-start(bf16[384,128]{1,0:T(8,128)(2,1)S(1)} %get-tuple-element.106), channel_id=1, source_target_pairs={{0,20},{4,16},{8,28},{12,24},{16,4},{20,0},{24,12},{28,8},{1,21},{... | collective-permute-start | bytes 294920 | tf_op jit(solution)/shard_map/ppermute | solution.py:446
  72.7 3.6 %collective-permute-start.16 = (bf16[384,128]{1,0:T(8,128)(2,1)S(1)}, bf16[384,128]{1,0:T(8,128)(2,1)S(1)}, u32[]{:S(2)}, u32[]{:S(2)}) collective-permute-start(bf16[384,128]{1,0:T(8,128)(2,1)S(1)} %get-tuple-element.108), channel_id=1, source_target_pairs={{0,4},{4,0},{8,12},{12,8},{16,20},{20,16},{24,28},{28,24},{1,5},{5... | collective-permute-start | bytes 294920 | tf_op jit(solution)/shard_map/ppermute | solution.py:446
  89.2 10.9 %collective-permute-start.22 = (bf16[1152,128]{1,0:T(8,128)(2,1)S(1)}, bf16[1152,128]{1,0:T(8,128)(2,1)S(1)}, u32[]{:S(2)}, u32[]{:S(2)}) collective-permute-start(bf16[1152,128]{1,0:T(8,128)(2,1)S(1)} %get-tuple-element.117), channel_id=1, source_target_pairs={{0,24},{4,28},{8,16},{12,20},{16,8},{20,12},{24,0},{28,4},{1,25},{... | collective-permute-start | bytes 884744 | tf_op jit(solution)/shard_map/ppermute | solution.py:446
  91.5 13.7 %collective-permute-start.23 = (bf16[1152,128]{1,0:T(8,128)(2,1)S(1)}, bf16[1152,128]{1,0:T(8,128)(2,1)S(1)}, u32[]{:S(2)}, u32[]{:S(2)}) collective-permute-start(bf16[1152,128]{1,0:T(8,128)(2,1)S(1)} %get-tuple-element.118), channel_id=1, source_target_pairs={{0,28},{4,24},{8,20},{12,16},{16,12},{20,8},{24,4},{28,0},{1,29},{... | collective-permute-start | bytes 884744 | tf_op jit(solution)/shard_map/ppermute | solution.py:446
  91.9 20.4 %collective-permute-start.17 = (bf16[1152,128]{1,0:T(8,128)(2,1)S(1)}, bf16[1152,128]{1,0:T(8,128)(2,1)S(1)}, u32[]{:S(2)}, u32[]{:S(2)}) collective-permute-start(bf16[1152,128]{1,0:T(8,128)(2,1)S(1)} %get-tuple-element.112), channel_id=1, source_target_pairs={{0,8},{4,12},{8,0},{12,4},{16,24},{20,28},{24,16},{28,20},{1,9},{5... | collective-permute-start | bytes 884744 | tf_op jit(solution)/shard_map/ppermute | solution.py:446
  93.3 19.0 %collective-permute-start.18 = (bf16[1152,128]{1,0:T(8,128)(2,1)S(1)}, bf16[1152,128]{1,0:T(8,128)(2,1)S(1)}, u32[]{:S(2)}, u32[]{:S(2)}) collective-permute-start(bf16[1152,128]{1,0:T(8,128)(2,1)S(1)} %get-tuple-element.113), channel_id=1, source_target_pairs={{0,16},{4,20},{8,24},{12,28},{16,0},{20,4},{24,8},{28,12},{1,17},{... | collective-permute-start | bytes 884744 | tf_op jit(solution)/shard_map/ppermute | solution.py:446
  94.8 22.2 %collective-permute-start.19 = (bf16[1152,128]{1,0:T(8,128)(2,1)S(1)}, bf16[1152,128]{1,0:T(8,128)(2,1)S(1)}, u32[]{:S(2)}, u32[]{:S(2)}) collective-permute-start(bf16[1152,128]{1,0:T(8,128)(2,1)S(1)} %get-tuple-element.114), channel_id=1, source_target_pairs={{0,12},{4,8},{8,4},{12,0},{16,28},{20,24},{24,20},{28,16},{1,13},{... | collective-permute-start | bytes 884744 | tf_op jit(solution)/shard_map/ppermute | solution.py:446
  100.1 17.9 %collective-permute-start.20 = (bf16[1152,128]{1,0:T(8,128)(2,1)S(1)}, bf16[1152,128]{1,0:T(8,128)(2,1)S(1)}, u32[]{:S(2)}, u32[]{:S(2)}) collective-permute-start(bf16[1152,128]{1,0:T(8,128)(2,1)S(1)} %get-tuple-element.115), channel_id=1, source_target_pairs={{0,20},{4,16},{8,28},{12,24},{16,4},{20,0},{24,12},{28,8},{1,21},{... | collective-permute-start | bytes 884744 | tf_op jit(solution)/shard_map/ppermute | solution.py:446
  105.2 12.8 %collective-permute-start.21 = (bf16[1152,128]{1,0:T(8,128)(2,1)S(1)}, bf16[1152,128]{1,0:T(8,128)(2,1)S(1)}, u32[]{:S(2)}, u32[]{:S(2)}) collective-permute-start(bf16[1152,128]{1,0:T(8,128)(2,1)S(1)} %get-tuple-element.116), channel_id=1, source_target_pairs={{0,4},{4,0},{8,12},{12,8},{16,20},{20,16},{24,28},{28,24},{1,5},{5... | collective-permute-start | bytes 884744 | tf_op jit(solution)/shard_map/ppermute | solution.py:446

commit v17 on v16

--- a/solution.py
+++ b/solution.py
@@ -289,9 +289,10 @@
 def backward_kernel(listed, heads, rows, bq, bk, kept, me_s, plan_q, plan_k, count_ref, v_ref,
                     qx_ref, kx_ref, kt_ref, rows_ref, log_ref, *refs):
     if kept:
-        p_list, top_list = refs[:2]
-        refs = refs[2:]
+        p_list, refs = refs[0], refs[1:]
     peers = len(listed)
+    if kept:
+        refs = refs[3:]
     blocks = refs[:peers]
     dq_acc, dk_acc, dv_acc, g_ref, dot_ref, p0, ds0, p1, ds1 = refs[peers:]
     scale = HD ** (-0.5)
@@ -309,37 +310,47 @@
             left = left - term.astype(jnp.float32)
             dots = dots + dot32(ones, term, NT)
         dot_ref[:, part] = dots[:1, :]
-    dk_acc[...] = jnp.zeros_like(dk_acc)
-    dv_acc[...] = jnp.zeros_like(dv_acc)
-    dq_acc[...] = jnp.zeros_like(dq_acc)
+    if not kept:
+        for ref in (dq_acc, dk_acc, dv_acc):
+            ref[...] = jnp.zeros_like(ref)
 
     def early(now, qi, ki, buffer, diagonal):
         p_ref, ds_ref = buffer
         queries = aligned(qi, bq)
         log_row, dot_row = log_ref[:, queries], dot_ref[:, queries]
-        if kept:
-            share = jnp.exp2(top_list[now] - log_row)
         for strip in range(0, bk, STRIP):
             part = slice(strip, strip + STRIP)
             keys = aligned(ki * (bk // STRIP) + strip // STRIP, STRIP)
             if kept:
-                p = p_list[now, part, :].astype(jnp.float32) * share
+                p = p_list[now, part, :].astype(jnp.float32)
             else:
                 p = jnp.exp2(dot32(kx_ref[keys, :], qx_ref[queries, :], NT) * factor - log_row)
                 if diagonal:
                     p = jnp.where(at_or_before(qi * bq, ki * bk + strip, (STRIP, bq)), p, 0.0)
-            p_ref[part, :] = p.astype(jnp.bfloat16)
+                p_ref[part, :] = p.astype(jnp.bfloat16)
             dp = dot32(v_ref[keys, :], g_ref[queries, :], NT)
             ds_ref[part, :] = (p * (dp - dot_row)).astype(jnp.bfloat16)
 
     def late(now, qi, ki, buffer):
         p_ref, ds_ref = buffer
         keys, queries = aligned(ki, bk), aligned(qi, bq)
-        dv_acc[keys, :] += dot32(p_ref[...], g_ref[queries, :])
+        dv_acc[keys, :] += dot32(p_list[now] if kept else p_ref[...], g_ref[queries, :])
         dk_acc[keys, :] += dot32(ds_ref[...], qx_ref[queries, :HD])
         dq_acc[:, queries] += dot32(kt_ref[:, keys], ds_ref[...])
 
     pipelined(plan_q, plan_k, count_ref, early, late, ((p0, ds0), (p1, ds1)))
+
+
+def prepare_kernel(bq, bk, plan_q, count_ref, log_ref, top_list, p_list, p_out, *totals):
+    for total in totals:
+        total[...] = jnp.zeros_like(total)
+
+    @pl.loop(0, 2 * count_ref[1])
+    def _(now):
+        share = jnp.exp2(top_list[now] - log_ref[:, aligned(plan_q[now], bq)])
+        for strip in range(0, bk, STRIP):
+            part = slice(strip, strip + STRIP)
+            p_out[now, part, :] = (p_list[now, part, :].astype(jnp.float32) * share).astype(jnp.bfloat16)
 
 
 def finish_kernel(listed, rows, me_s, dq_ref, dk_ref, dv_ref, *results):
@@ -412,14 +423,31 @@
     )(me, *blocks)
 
 
-def attention_backward(me, heads, state, listed, blocks):
+def total_shapes(total):
+    shapes = [(HD, total), (total, HD), (total, HD)]
+    return [jax.ShapeDtypeStruct(shape, jnp.float32) for shape in shapes]
+
+
+def prepare(log_total, p_list, top_list, plan_q, count):
+    bk, bq = p_list.shape[1:]
+    out_shape = [jax.ShapeDtypeStruct(p_list.shape, p_list.dtype)] + total_shapes(log_total.shape[1])
+    return pl.pallas_call(
+        functools.partial(prepare_kernel, bq, bk),
+        in_specs=[SMEM_SPEC] * 2 + [VMEM_SPEC] * 3,
+        out_specs=[VMEM_SPEC] * len(out_shape),
+        out_shape=out_shape,
+        input_output_aliases={4: 0},
+        compiler_params=params([log_total, top_list, *out_shape[1:]]),
+    )(plan_q, count, log_total, top_list, p_list)
+
+
+def attention_backward(me, heads, state, listed, blocks, ready=()):
     peers, rows = len(blocks), blocks[0].shape[0]
     total = peers * rows
     bq, bk = block_sizes(total)[1]
-    vectors, plan = state[:-3], state[-3:]
-    kept = keeps_list(total, peers, heads)
-    shapes = [(HD, total), (total, HD), (total, HD)]
-    out_shape = [jax.ShapeDtypeStruct(shape, jnp.float32) for shape in shapes]
+    kept = bool(ready)
+    vectors, plan = [*state[:6], *ready], state[-3:]
+    out_shape = total_shapes(total)
     scratch = [
         pltpu.VMEM((total, HD), jnp.bfloat16),
         pltpu.VMEM((1, total), jnp.float32),
@@ -431,7 +459,8 @@
         out_specs=[VMEM_SPEC] * 3,
         out_shape=out_shape,
         scratch_shapes=scratch,
-        compiler_params=params([*vectors, *blocks, *out_shape], scratch),
+        input_output_aliases={4 + 7 + i: i for i in range(3)} if kept else {},
+        compiler_params=params([*vectors[:6], *blocks] if kept else [*vectors, *blocks, *out_shape], scratch),
         cost_estimate=attention_cost(total, 5),
     )(me, *plan, *vectors, *blocks)
 
@@ -487,7 +516,11 @@
                     received[d] = block
     grads = exchange_all(acc, far_first)
 
-    totals = attention_backward(me_vector, heads, state, far_first, grads)
+    ready = ()
+    if len(state) > 9:
+        p_list, grads[0] = after((state[6], grads[0]))
+        ready = prepare(state[5], p_list, state[7], state[-3], state[-1])
+    totals = attention_backward(me_vector, heads, state, far_first, grads, ready)
 
     far = [d for d in returning if bin(d >> 1).count("1") > 1]
     near = [d for d in returning if d not in far]

time: 120 us -> 119 us (level)
  Pallas kernels: 38.7 us -> 42 us
  waiting for transfers between devices: 51.8 us -> 48.6 us
    ppermute x21, waiting for transfers between devices: 46.1 us -> 43.5 us  [exchange(): lax.ppermute(x, 'seq', [(i, i ^ d) for i in range(peers)])]
    pallas_call x0 -> x1, Pallas kernels: none -> 2.54 us  [prepare(): pl.pallas_call(functools.partial(prepare_kernel, bq, bk), in_specs=[SMEM_...]
  transfers between devices with their start and end apart: 24 -> 24, of which waited for: 17 -> 15; matrix products, arithmetic and copies ran while one was open for 4% -> 4% of each run, Pallas kernels for 20% -> 22%
where the time goes in v17:
time: 119 us
  waiting for transfers between devices  48.6 us (41%)
  Pallas kernels  42 us (35%)
  starting transfers between devices  23.5 us (20%)
  local copies, waits for them, and re-layouts  4.56 us (4%)
    ppermute x21, waiting for transfers between devices, exchange(): lax.ppermute(x, 'seq', [(i, i ^ d) for i in range(peers)])  43.5 us
    ppermute x21, starting transfers between devices, exchange(): lax.ppermute(x, 'seq', [(i, i ^ d) for i in range(peers)])  18.8 us
    pallas_call x1, Pallas kernels, attention_forward(): pl.pallas_call(functools.partial(forward_kernel, peers, heads, rows, bq,...  16.2 us
    pallas_call x1, Pallas kernels, attention_backward(): pl.pallas_call(functools.partial(backward_kernel, listed, heads, rows, bq...  12.9 us
    ppermute x3, waiting for transfers between devices, pass_on(): lax.ppermute(x, 'head', [(i, (i + 1) % groups) for i in range(groups)])  5.13 us
    ppermute x3, starting transfers between devices, pass_on(): lax.ppermute(x, 'head', [(i, (i + 1) % groups) for i in range(groups)])  4.66 us
    dynamic_slice x1, local copies, waits for them, and re-layouts, per_device(): lax.dynamic_slice_in_dim(out_weight, block * width, width, 1)  4.54 us
    pallas_call x1, Pallas kernels, pack_heads(): pl.pallas_call(functools.partial(pack_kernel, heads, rows), in_specs=[SME...  3.62 us
  transfers between devices with their start and end apart: 24, of which 15 were waited for; matrix products, arithmetic and copies ran while one was open for 4% of the time, Pallas kernels for 22%

profile of v17, /device:TPU:0, one launch (start us, length us, event | category | flops | bytes accessed | tf_op | source)
XLA Modules:
  0.0 119.4 jit_solution(9043193787684860229)
XLA Ops:
  0.6 3.1 %collective-permute-start = (bf16[384,1024]{1,0:T(8,128)(2,1)}, bf16[384,1024]{1,0:T(8,128)(2,1)S(1)}, u32[]{:S(2)}, u32[]{:S(2)}) collective-permute-start(bf16[384,1024]{1,0:T(8,128)(2,1)} %o_ref.1), channel_id=1, source_target_pairs={{0,1},{1,2},{2,3},{3,0},{4,5},{5,6},{6,7},{7,4},{8,9},{9,10},{10,1... | collective-permute-start | bytes 2359304 | tf_op jit(solution)/shard_map/ppermute | solution.py:478
  3.7 3.6 %shard_map.85 = (bf16[1168,128]{1,0:T(8,128)(2,1)}, bf16[1168,128]{1,0:T(8,128)(2,1)}, bf16[1168,128]{1,0:T(8,128)(2,1)}, bf16[1168,128]{1,0:T(8,128)(2,1)}, bf1...) custom-call(s32[1]{0:T(128)} %bitcast.me_s, ...), custom_call_target="tpu_custom_call" | custom-call | tf_op jit(solution)/shard_map/pallas_call | solution.py:63
  7.3 1.5 %collective-permute-start.1 = (bf16[1168,128]{1,0:T(8,128)(2,1)}, bf16[1168,128]{1,0:T(8,128)(2,1)S(1)}, u32[]{:S(2)}, u32[]{:S(2)}) collective-permute-start(bf16[1168,128]{1,0:T(8,128)(2,1)} %get-tuple-element.70), channel_id=1, source_target_pairs={{0,8},{4,12},{8,0},{12,4},{16,24},{20,28},{24,16},{28,20},{1,9},{5... | collective-permute-start | bytes 897032 | tf_op jit(solution)/shard_map/ppermute | solution.py:475
  8.8 1.5 %collective-permute-start.2 = (bf16[1168,128]{1,0:T(8,128)(2,1)}, bf16[1168,128]{1,0:T(8,128)(2,1)S(1)}, u32[]{:S(2)}, u32[]{:S(2)}) collective-permute-start(bf16[1168,128]{1,0:T(8,128)(2,1)} %get-tuple-element.71), channel_id=1, source_target_pairs={{0,16},{4,20},{8,24},{12,28},{16,0},{20,4},{24,8},{28,12},{1,17},{... | collective-permute-start | bytes 897032 | tf_op jit(solution)/shard_map/ppermute | solution.py:475
  10.3 0.5 collective-permute-start.3
  10.8 4.5 %constant_dynamic-slice_fusion = (bf16[1024,1024]{1,0:T(8,128)(2,1)S(1)}, bf16[1024,1024]{1,0:T(8,128)(2,1)S(1)}, bf16[1024,1024]{1,0:T(8,128)(2,1)S(1)}, bf16[1024,1024]{1,0:T(8,128)(2,1)S(1)}) fusion(bf16[1024,4096]{1,0:T(8,128)(2,1)} %param.10, s32[]{:T(128)S(6)} %select_n.15, s32[]{:T(128)S(6)} %select_n.13, s32[]{:T(128)S(6)} %select_n.12, s32[]{:T(128)S(6)} %select_n.14), kind=kLoop, calls=%fused_computation | loop fusion | bytes 16777232 | tf_op jit(solution)/shard_map/dynamic_slice | solution.py:499
  15.4 0.0 copy-start.2
  15.4 1.0 shard_map.86.refs_0_
  16.4 1.1 collective-permute-done.1.refs_2_
  17.6 6.2 %collective-permute-done.2.refs_4_ = bf16[1168,128]{1,0:T(8,128)(2,1)S(1)} collective-permute-done((bf16[1168,128]{1,0:T(8,128)(2,1)}, bf16[1168,128]{1,0:T(8,128)(2,1)S(1)}, u32[]{:S(2)}, u32[]{:S(2)}) %collective-permute-start.2) | collective-permute-done | bytes 299040 | tf_op jit(solution)/shard_map/ppermute | solution.py:475
  23.7 1.6 %collective-permute-start.4 = (bf16[384,1024]{1,0:T(8,128)(2,1)S(1)}, bf16[384,1024]{1,0:T(8,128)(2,1)S(1)}, u32[]{:S(2)}, u32[]{:S(2)}) collective-permute-start(bf16[384,1024]{1,0:T(8,128)(2,1)S(1)} %collective-permute-done.o_ref), channel_id=1, source_target_pairs={{0,1},{1,2},{2,3},{3,0},{4,5},{5,6},{6,7},{7,4},{8,9},{9,10},{10,1... | collective-permute-start | bytes 2359304 | tf_op jit(solution)/shard_map/ppermute | solution.py:478
  25.3 2.4 %collective-permute-start.6 = (bf16[1168,128]{1,0:T(8,128)(2,1)S(1)}, bf16[1168,128]{1,0:T(8,128)(2,1)S(1)}, u32[]{:S(2)}, u32[]{:S(2)}) collective-permute-start(bf16[1168,128]{1,0:T(8,128)(2,1)S(1)} %copy-done.4), channel_id=1, source_target_pairs={{0,20},{4,16},{8,28},{12,24},{16,4},{20,0},{24,12},{28,8},{1,21},{... | collective-permute-start | bytes 897032 | tf_op jit(solution)/shard_map/ppermute | solution.py:475
  27.7 0.4 collective-permute-start.7
  28.1 0.6 collective-permute-start.8
  28.6 1.0 shard_map.87.refs_0_
  29.7 6.0 %collective-permute-done.5.refs_7_ = bf16[1168,128]{1,0:T(8,128)(2,1)S(1)} collective-permute-done((bf16[1168,128]{1,0:T(8,128)(2,1)S(1)}, bf16[1168,128]{1,0:T(8,128)(2,1)S(1)}, u32[]{:S(2)}, u32[]{:S(2)}) %collective-permute-start.5) | collective-permute-done | bytes 299040 | tf_op jit(solution)/shard_map/ppermute | solution.py:475
  35.6 5.4 %collective-permute-done.6.refs_5_ = bf16[1168,128]{1,0:T(8,128)(2,1)S(1)} collective-permute-done((bf16[1168,128]{1,0:T(8,128)(2,1)S(1)}, bf16[1168,128]{1,0:T(8,128)(2,1)S(1)}, u32[]{:S(2)}, u32[]{:S(2)}) %collective-permute-start.6) | collective-permute-done | bytes 299040 | tf_op jit(solution)/shard_map/ppermute | solution.py:475
  41.1 3.0 %collective-permute-done.4.o_ref = bf16[384,1024]{1,0:T(8,128)(2,1)S(1)} collective-permute-done((bf16[384,1024]{1,0:T(8,128)(2,1)S(1)}, bf16[384,1024]{1,0:T(8,128)(2,1)S(1)}, u32[]{:S(2)}, u32[]{:S(2)}) %collective-permute-start.4) | collective-permute-done | bytes 786464 | tf_op jit(solution)/shard_map/ppermute | solution.py:478
  44.0 16.2 %shard_map.88 = (bf16[3072,128]{1,0:T(8,128)(2,1)S(1)}, bf16[3072,256]{1,0:T(8,128)(2,1)S(1)}, bf16[3072,256]{1,0:T(8,128)(2,1)S(1)}, bf16[128,3072]{1,0:T(8,128...) custom-call(s32[1]{0:T(128)} %bitcast.me_s, ...), custom_call_target="tpu_custom_call" | custom-call | flops 1811939328 | bytes 6291456 | tf_op jit(solution)/shard_map/pallas_call | solution.py:415
  60.2 1.0 shard_map.89.acc_ref
  61.2 2.2 %collective-permute-done.9.o_ref = bf16[384,1024]{1,0:T(8,128)(2,1)S(1)} collective-permute-done((bf16[384,1024]{1,0:T(8,128)(2,1)S(1)}, bf16[384,1024]{1,0:T(8,128)(2,1)S(1)}, u32[]{:S(2)}, u32[]{:S(2)}) %collective-permute-start.9) | collective-permute-done | bytes 786464 | tf_op jit(solution)/shard_map/ppermute | solution.py:478
  63.4 1.0 shard_map.90
  64.4 2.3 %collective-permute-start.10 = (bf16[384,128]{1,0:T(8,128)(2,1)S(1)}, bf16[384,128]{1,0:T(8,128)(2,1)S(1)}, u32[]{:S(2)}, u32[]{:S(2)}) collective-permute-start(bf16[384,128]{1,0:T(8,128)(2,1)S(1)} %get-tuple-element.107), channel_id=1, source_target_pairs={{0,24},{4,28},{8,16},{12,20},{16,8},{20,12},{24,0},{28,4},{1,25},{... | collective-permute-start | bytes 294920 | tf_op jit(solution)/shard_map/ppermute | solution.py:475
  66.7 0.3 collective-permute-start.12
  67.0 1.0 collective-permute-start.13
  68.0 1.7 %collective-permute-start.14 = (bf16[384,128]{1,0:T(8,128)(2,1)S(1)}, bf16[384,128]{1,0:T(8,128)(2,1)S(1)}, u32[]{:S(2)}, u32[]{:S(2)}) collective-permute-start(bf16[384,128]{1,0:T(8,128)(2,1)S(1)} %get-tuple-element.117), channel_id=1, source_target_pairs={{0,12},{4,8},{8,4},{12,0},{16,28},{20,24},{24,20},{28,16},{1,13},{... | collective-permute-start | bytes 294920 | tf_op jit(solution)/shard_map/ppermute | solution.py:475
  69.6 0.4 collective-permute-done.10.refs_4_
  70.0 0.5 collective-permute-start.15
  70.5 2.3 %collective-permute-done.11.refs_5_ = bf16[384,128]{1,0:T(8,128)(2,1)S(1)} collective-permute-done((bf16[384,128]{1,0:T(8,128)(2,1)S(1)}, bf16[384,128]{1,0:T(8,128)(2,1)S(1)}, u32[]{:S(2)}, u32[]{:S(2)}) %collective-permute-start.11) | collective-permute-done | bytes 98336 | tf_op jit(solution)/shard_map/ppermute | solution.py:475
  72.7 2.5 %shard_map.91 = (bf16[80,256,256]{2,1,0:T(8,128)(2,1)S(1)}, f32[128,3072]{1,0:T(8,128)S(1)}, f32[3072,128]{1,0:T(8,128)S(1)}, f32[3072,128]{1,0:T(8,128)S(1)}) custom-call(s32[80]{0:T(128)S(1)} %get-tuple-element.90.plan_q, s32[2]{0:T(128)S(1)} %get-tuple-element.92.count_ref, ...), custom_call_target="tpu_custom_call", output_to_operand_aliasing={{0}: (4, {})} | custom-call | tf_op jit(solution)/shard_map/pallas_call | solution.py:434
  75.3 0.6 collective-permute-done.14.refs_8_
  75.9 0.4 collective-permute-done.15.refs_9_
  76.3 12.9 %shard_map.92 = (f32[128,3072]{1,0:T(8,128)S(1)}, f32[3072,128]{1,0:T(8,128)S(1)}, f32[3072,128]{1,0:T(8,128)S(1)}) custom-call(s32[1]{0:T(128)} %bitcast.me_s, s32[80]{0:T(128)S(1)} %get-tuple-element.90.plan_q, s32[80]{0:T(128)S(1)} %get-tuple-element.91.plan_k, ...), custom_call_target="tpu_custom_call", output_to_operand_aliasing={{0}: (11, {}), {1}: (12, {}), {2}: (13, {})} | custom-call | flops 3019898880 | bytes 6291456 | tf_op jit(solution)/shard_map/pallas_call | solution.py:456
  89.2 0.2 shard_map.94
  89.4 2.3 %collective-permute-start.22 = (bf16[1152,128]{1,0:T(8,128)(2,1)S(1)}, bf16[1152,128]{1,0:T(8,128)(2,1)S(1)}, u32[]{:S(2)}, u32[]{:S(2)}) collective-permute-start(bf16[1152,128]{1,0:T(8,128)(2,1)S(1)} %get-tuple-element.129), channel_id=1, source_target_pairs={{0,24},{4,28},{8,16},{12,20},{16,8},{20,12},{24,0},{28,4},{1,25},{... | collective-permute-start | bytes 884744 | tf_op jit(solution)/shard_map/ppermute | solution.py:475
  91.6 0.1 collective-permute-start.23
  91.7 0.3 shard_map.93
  92.1 1.3 %collective-permute-start.17 = (bf16[1152,128]{1,0:T(8,128)(2,1)S(1)}, bf16[1152,128]{1,0:T(8,128)(2,1)S(1)}, u32[]{:S(2)}, u32[]{:S(2)}) collective-permute-start(bf16[1152,128]{1,0:T(8,128)(2,1)S(1)} %get-tuple-element.124), channel_id=1, source_target_pairs={{0,8},{4,12},{8,0},{12,4},{16,24},{20,28},{24,16},{28,20},{1,9},{5... | collective-permute-start | bytes 884744 | tf_op jit(solution)/shard_map/ppermute | solution.py:475
  93.4 1.5 %collective-permute-start.18 = (bf16[1152,128]{1,0:T(8,128)(2,1)S(1)}, bf16[1152,128]{1,0:T(8,128)(2,1)S(1)}, u32[]{:S(2)}, u32[]{:S(2)}) collective-permute-start(bf16[1152,128]{1,0:T(8,128)(2,1)S(1)} %get-tuple-element.125), channel_id=1, source_target_pairs={{0,16},{4,20},{8,24},{12,28},{16,0},{20,4},{24,8},{28,12},{1,17},{... | collective-permute-start | bytes 884744 | tf_op jit(solution)/shard_map/ppermute | solution.py:475
  95.0 0.1 collective-permute-start.19
  95.0 5.2 %collective-permute-done.22.refs_0_ = bf16[1152,128]{1,0:T(8,128)(2,1)S(1)} collective-permute-done((bf16[1152,128]{1,0:T(8,128)(2,1)S(1)}, bf16[1152,128]{1,0:T(8,128)(2,1)S(1)}, u32[]{:S(2)}, u32[]{:S(2)}) %collective-permute-start.22) | collective-permute-done | bytes 294944 | tf_op jit(solution)/shard_map/ppermute | solution.py:475
  100.3 5.1 %collective-permute-done.23.refs_1_ = bf16[1152,128]{1,0:T(8,128)(2,1)S(1)} collective-permute-done((bf16[1152,128]{1,0:T(8,128)(2,1)S(1)}, bf16[1152,128]{1,0:T(8,128)(2,1)S(1)}, u32[]{:S(2)}, u32[]{:S(2)}) %collective-permute-start.23) | collective-permute-done | bytes 294944 | tf_op jit(solution)/shard_map/ppermute | solution.py:475
  105.4 1.0 collective-permute-start.21
  106.4 1.0 shard_map.95
  107.4 5.1 %collective-permute-done.17.refs_0_ = bf16[1152,128]{1,0:T(8,128)(2,1)S(1)} collective-permute-done((bf16[1152,128]{1,0:T(8,128)(2,1)S(1)}, bf16[1152,128]{1,0:T(8,128)(2,1)S(1)}, u32[]{:S(2)}, u32[]{:S(2)}) %collective-permute-start.17) | collective-permute-done | bytes 294944 | tf_op jit(solution)/shard_map/ppermute | solution.py:475
  112.5 4.7 %collective-permute-done.19.refs_2_ = bf16[1152,128]{1,0:T(8,128)(2,1)S(1)} collective-permute-done((bf16[1152,128]{1,0:T(8,128)(2,1)S(1)}, bf16[1152,128]{1,0:T(8,128)(2,1)S(1)}, u32[]{:S(2)}, u32[]{:S(2)}) %collective-permute-start.19) | collective-permute-done | bytes 294944 | tf_op jit(solution)/shard_map/ppermute | solution.py:475
  117.2 1.0 collective-permute-done.20.refs_3_
  118.2 1.2 %shard_map.96 = (bf16[384,1024]{1,0:T(8,128)(2,1)}, bf16[384,1024]{1,0:T(8,128)(2,1)}, bf16[384,1024]{1,0:T(8,128)(2,1)}) custom-call(s32[1]{0:T(128)} %bitcast.me_s, bf16[1152,128]{1,0:T(8,128)(2,1)S(1)} %collective-permute-done.17.refs_0_, ...), custom_call_target="tpu_custom_call", output_to_operand_aliasing={{0}: (6, {}), {1}: (7, {}), {2}: (8, {})} | custom-call | tf_op jit(solution)/shard_map/pallas_call | solution.py:88
  (25 shorter events, 0.1 us)
Async XLA Ops:
  0.6 23.1 %collective-permute-start = (bf16[384,1024]{1,0:T(8,128)(2,1)}, bf16[384,1024]{1,0:T(8,128)(2,1)S(1)}, u32[]{:S(2)}, u32[]{:S(2)}) collective-permute-start(bf16[384,1024]{1,0:T(8,128)(2,1)} %o_ref.1), channel_id=1, source_target_pairs={{0,1},{1,2},{2,3},{3,0},{4,5},{5,6},{6,7},{7,4},{8,9},{9,10},{10,1... | collective-permute-start | bytes 2359304 | tf_op jit(solution)/shard_map/ppermute | solution.py:478
  7.3 10.2 %collective-permute-start.1 = (bf16[1168,128]{1,0:T(8,128)(2,1)}, bf16[1168,128]{1,0:T(8,128)(2,1)S(1)}, u32[]{:S(2)}, u32[]{:S(2)}) collective-permute-start(bf16[1168,128]{1,0:T(8,128)(2,1)} %get-tuple-element.70), channel_id=1, source_target_pairs={{0,8},{4,12},{8,0},{12,4},{16,24},{20,28},{24,16},{28,20},{1,9},{5... | collective-permute-start | bytes 897032 | tf_op jit(solution)/shard_map/ppermute | solution.py:475
  8.8 14.9 %collective-permute-start.2 = (bf16[1168,128]{1,0:T(8,128)(2,1)}, bf16[1168,128]{1,0:T(8,128)(2,1)S(1)}, u32[]{:S(2)}, u32[]{:S(2)}) collective-permute-start(bf16[1168,128]{1,0:T(8,128)(2,1)} %get-tuple-element.71), channel_id=1, source_target_pairs={{0,16},{4,20},{8,24},{12,28},{16,0},{20,4},{24,8},{28,12},{1,17},{... | collective-permute-start | bytes 897032 | tf_op jit(solution)/shard_map/ppermute | solution.py:475
  10.3 13.4 %collective-permute-start.3 = (bf16[1168,128]{1,0:T(8,128)(2,1)}, bf16[1168,128]{1,0:T(8,128)(2,1)S(1)}, u32[]{:S(2)}, u32[]{:S(2)}) collective-permute-start(bf16[1168,128]{1,0:T(8,128)(2,1)} %get-tuple-element.72), channel_id=1, source_target_pairs={{0,24},{4,28},{8,16},{12,20},{16,8},{20,12},{24,0},{28,4},{1,25},{... | collective-permute-start | bytes 897032 | tf_op jit(solution)/shard_map/ppermute | solution.py:475
  10.8 4.5 %copy-start = (bf16[384,1024]{1,0:T(8,128)(2,1)S(1)}, bf16[384,1024]{1,0:T(8,128)(2,1)}, u32[]{:S(2)}) copy-start(bf16[384,1024]{1,0:T(8,128)(2,1)} %o_ref.1) | copy-start | bytes 2359300
  15.4 9.9 %copy-start.5 = (bf16[1168,128]{1,0:T(8,128)(2,1)S(1)}, bf16[1168,128]{1,0:T(8,128)(2,1)}, u32[]{:S(2)}) copy-start(bf16[1168,128]{1,0:T(8,128)(2,1)} %get-tuple-element.75) | copy-start | bytes 897028
  15.4 9.9 %copy-start.4 = (bf16[1168,128]{1,0:T(8,128)(2,1)S(1)}, bf16[1168,128]{1,0:T(8,128)(2,1)}, u32[]{:S(2)}) copy-start(bf16[1168,128]{1,0:T(8,128)(2,1)} %get-tuple-element.76) | copy-start | bytes 897028
  15.4 12.3 %copy-start.3 = (bf16[1168,128]{1,0:T(8,128)(2,1)S(1)}, bf16[1168,128]{1,0:T(8,128)(2,1)}, u32[]{:S(2)}) copy-start(bf16[1168,128]{1,0:T(8,128)(2,1)} %get-tuple-element.77) | copy-start | bytes 897028
  15.4 12.7 %copy-start.2 = (bf16[1168,128]{1,0:T(8,128)(2,1)S(1)}, bf16[1168,128]{1,0:T(8,128)(2,1)}, u32[]{:S(2)}) copy-start(bf16[1168,128]{1,0:T(8,128)(2,1)} %get-tuple-element.78) | copy-start | bytes 897028
  23.7 20.3 %collective-permute-start.4 = (bf16[384,1024]{1,0:T(8,128)(2,1)S(1)}, bf16[384,1024]{1,0:T(8,128)(2,1)S(1)}, u32[]{:S(2)}, u32[]{:S(2)}) collective-permute-start(bf16[384,1024]{1,0:T(8,128)(2,1)S(1)} %collective-permute-done.o_ref), channel_id=1, source_target_pairs={{0,1},{1,2},{2,3},{3,0},{4,5},{5,6},{6,7},{7,4},{8,9},{9,10},{10,1... | collective-permute-start | bytes 2359304 | tf_op jit(solution)/shard_map/ppermute | solution.py:478
  25.3 10.3 %collective-permute-start.5 = (bf16[1168,128]{1,0:T(8,128)(2,1)S(1)}, bf16[1168,128]{1,0:T(8,128)(2,1)S(1)}, u32[]{:S(2)}, u32[]{:S(2)}) collective-permute-start(bf16[1168,128]{1,0:T(8,128)(2,1)S(1)} %copy-done.5), channel_id=1, source_target_pairs={{0,28},{4,24},{8,20},{12,16},{16,12},{20,8},{24,4},{28,0},{1,29},{... | collective-permute-start | bytes 897032 | tf_op jit(solution)/shard_map/ppermute | solution.py:475
  25.3 15.7 %collective-permute-start.6 = (bf16[1168,128]{1,0:T(8,128)(2,1)S(1)}, bf16[1168,128]{1,0:T(8,128)(2,1)S(1)}, u32[]{:S(2)}, u32[]{:S(2)}) collective-permute-start(bf16[1168,128]{1,0:T(8,128)(2,1)S(1)} %copy-done.4), channel_id=1, source_target_pairs={{0,20},{4,16},{8,28},{12,24},{16,4},{20,0},{24,12},{28,8},{1,21},{... | collective-permute-start | bytes 897032 | tf_op jit(solution)/shard_map/ppermute | solution.py:475
  27.7 13.3 %collective-permute-start.7 = (bf16[1168,128]{1,0:T(8,128)(2,1)S(1)}, bf16[1168,128]{1,0:T(8,128)(2,1)S(1)}, u32[]{:S(2)}, u32[]{:S(2)}) collective-permute-start(bf16[1168,128]{1,0:T(8,128)(2,1)S(1)} %copy-done.3), channel_id=1, source_target_pairs={{0,12},{4,8},{8,4},{12,0},{16,28},{20,24},{24,20},{28,16},{1,13},{... | collective-permute-start | bytes 897032 | tf_op jit(solution)/shard_map/ppermute | solution.py:475
  28.1 13.0 %collective-permute-start.8 = (bf16[1168,128]{1,0:T(8,128)(2,1)S(1)}, bf16[1168,128]{1,0:T(8,128)(2,1)S(1)}, u32[]{:S(2)}, u32[]{:S(2)}) collective-permute-start(bf16[1168,128]{1,0:T(8,128)(2,1)S(1)} %copy-done.2), channel_id=1, source_target_pairs={{0,4},{4,0},{8,12},{12,8},{16,20},{20,16},{24,28},{28,24},{1,5},{5... | collective-permute-start | bytes 897032 | tf_op jit(solution)/shard_map/ppermute | solution.py:475
  28.6 15.4 %copy-start.1 = (bf16[1168,128]{1,0:T(8,128)(2,1)S(1)}, bf16[1168,128]{1,0:T(8,128)(2,1)}, u32[]{:S(2)}) copy-start(bf16[1168,128]{1,0:T(8,128)(2,1)} %get-tuple-element.82.refs_0_) | copy-start | bytes 897028
  44.0 19.4 %collective-permute-start.9 = (bf16[384,1024]{1,0:T(8,128)(2,1)S(1)}, bf16[384,1024]{1,0:T(8,128)(2,1)S(1)}, u32[]{:S(2)}, u32[]{:S(2)}) collective-permute-start(bf16[384,1024]{1,0:T(8,128)(2,1)S(1)} %collective-permute-done.4.o_ref), channel_id=1, source_target_pairs={{0,1},{1,2},{2,3},{3,0},{4,5},{5,6},{6,7},{7,4},{8,9},{9,10},{10,1... | collective-permute-start | bytes 2359304 | tf_op jit(solution)/shard_map/ppermute | solution.py:478
  64.4 5.6 %collective-permute-start.10 = (bf16[384,128]{1,0:T(8,128)(2,1)S(1)}, bf16[384,128]{1,0:T(8,128)(2,1)S(1)}, u32[]{:S(2)}, u32[]{:S(2)}) collective-permute-start(bf16[384,128]{1,0:T(8,128)(2,1)S(1)} %get-tuple-element.107), channel_id=1, source_target_pairs={{0,24},{4,28},{8,16},{12,20},{16,8},{20,12},{24,0},{28,4},{1,25},{... | collective-permute-start | bytes 294920 | tf_op jit(solution)/shard_map/ppermute | solution.py:475
  66.7 6.1 %collective-permute-start.11 = (bf16[384,128]{1,0:T(8,128)(2,1)S(1)}, bf16[384,128]{1,0:T(8,128)(2,1)S(1)}, u32[]{:S(2)}, u32[]{:S(2)}) collective-permute-start(bf16[384,128]{1,0:T(8,128)(2,1)S(1)} %get-tuple-element.114), channel_id=1, source_target_pairs={{0,28},{4,24},{8,20},{12,16},{16,12},{20,8},{24,4},{28,0},{1,29},{... | collective-permute-start | bytes 294920 | tf_op jit(solution)/shard_map/ppermute | solution.py:475
  66.7 8.6 %collective-permute-start.12 = (bf16[384,128]{1,0:T(8,128)(2,1)S(1)}, bf16[384,128]{1,0:T(8,128)(2,1)S(1)}, u32[]{:S(2)}, u32[]{:S(2)}) collective-permute-start(bf16[384,128]{1,0:T(8,128)(2,1)S(1)} %get-tuple-element.115), channel_id=1, source_target_pairs={{0,8},{4,12},{8,0},{12,4},{16,24},{20,28},{24,16},{28,20},{1,9},{5... | collective-permute-start | bytes 294920 | tf_op jit(solution)/shard_map/ppermute | solution.py:475
  67.0 8.3 %collective-permute-start.13 = (bf16[384,128]{1,0:T(8,128)(2,1)S(1)}, bf16[384,128]{1,0:T(8,128)(2,1)S(1)}, u32[]{:S(2)}, u32[]{:S(2)}) collective-permute-start(bf16[384,128]{1,0:T(8,128)(2,1)S(1)} %get-tuple-element.116), channel_id=1, source_target_pairs={{0,16},{4,20},{8,24},{12,28},{16,0},{20,4},{24,8},{28,12},{1,17},{... | collective-permute-start | bytes 294920 | tf_op jit(solution)/shard_map/ppermute | solution.py:475
  68.0 7.9 %collective-permute-start.14 = (bf16[384,128]{1,0:T(8,128)(2,1)S(1)}, bf16[384,128]{1,0:T(8,128)(2,1)S(1)}, u32[]{:S(2)}, u32[]{:S(2)}) collective-permute-start(bf16[384,128]{1,0:T(8,128)(2,1)S(1)} %get-tuple-element.117), channel_id=1, source_target_pairs={{0,12},{4,8},{8,4},{12,0},{16,28},{20,24},{24,20},{28,16},{1,13},{... | collective-permute-start | bytes 294920 | tf_op jit(solution)/shard_map/ppermute | solution.py:475
  70.0 6.3 %collective-permute-start.15 = (bf16[384,128]{1,0:T(8,128)(2,1)S(1)}, bf16[384,128]{1,0:T(8,128)(2,1)S(1)}, u32[]{:S(2)}, u32[]{:S(2)}) collective-permute-start(bf16[384,128]{1,0:T(8,128)(2,1)S(1)} %get-tuple-element.118), channel_id=1, source_target_pairs={{0,20},{4,16},{8,28},{12,24},{16,4},{20,0},{24,12},{28,8},{1,21},{... | collective-permute-start | bytes 294920 | tf_op jit(solution)/shard_map/ppermute | solution.py:475
  72.7 3.6 %collective-permute-start.16 = (bf16[384,128]{1,0:T(8,128)(2,1)S(1)}, bf16[384,128]{1,0:T(8,128)(2,1)S(1)}, u32[]{:S(2)}, u32[]{:S(2)}) collective-permute-start(bf16[384,128]{1,0:T(8,128)(2,1)S(1)} %get-tuple-element.120), channel_id=1, source_target_pairs={{0,4},{4,0},{8,12},{12,8},{16,20},{20,16},{24,28},{28,24},{1,5},{5... | collective-permute-start | bytes 294920 | tf_op jit(solution)/shard_map/ppermute | solution.py:475
  89.4 10.9 %collective-permute-start.22 = (bf16[1152,128]{1,0:T(8,128)(2,1)S(1)}, bf16[1152,128]{1,0:T(8,128)(2,1)S(1)}, u32[]{:S(2)}, u32[]{:S(2)}) collective-permute-start(bf16[1152,128]{1,0:T(8,128)(2,1)S(1)} %get-tuple-element.129), channel_id=1, source_target_pairs={{0,24},{4,28},{8,16},{12,20},{16,8},{20,12},{24,0},{28,4},{1,25},{... | collective-permute-start | bytes 884744 | tf_op jit(solution)/shard_map/ppermute | solution.py:475
  91.6 13.7 %collective-permute-start.23 = (bf16[1152,128]{1,0:T(8,128)(2,1)S(1)}, bf16[1152,128]{1,0:T(8,128)(2,1)S(1)}, u32[]{:S(2)}, u32[]{:S(2)}) collective-permute-start(bf16[1152,128]{1,0:T(8,128)(2,1)S(1)} %get-tuple-element.130), channel_id=1, source_target_pairs={{0,28},{4,24},{8,20},{12,16},{16,12},{20,8},{24,4},{28,0},{1,29},{... | collective-permute-start | bytes 884744 | tf_op jit(solution)/shard_map/ppermute | solution.py:475
  92.1 20.4 %collective-permute-start.17 = (bf16[1152,128]{1,0:T(8,128)(2,1)S(1)}, bf16[1152,128]{1,0:T(8,128)(2,1)S(1)}, u32[]{:S(2)}, u32[]{:S(2)}) collective-permute-start(bf16[1152,128]{1,0:T(8,128)(2,1)S(1)} %get-tuple-element.124), channel_id=1, source_target_pairs={{0,8},{4,12},{8,0},{12,4},{16,24},{20,28},{24,16},{28,20},{1,9},{5... | collective-permute-start | bytes 884744 | tf_op jit(solution)/shard_map/ppermute | solution.py:475
  93.4 19.0 %collective-permute-start.18 = (bf16[1152,128]{1,0:T(8,128)(2,1)S(1)}, bf16[1152,128]{1,0:T(8,128)(2,1)S(1)}, u32[]{:S(2)}, u32[]{:S(2)}) collective-permute-start(bf16[1152,128]{1,0:T(8,128)(2,1)S(1)} %get-tuple-element.125), channel_id=1, source_target_pairs={{0,16},{4,20},{8,24},{12,28},{16,0},{20,4},{24,8},{28,12},{1,17},{... | collective-permute-start | bytes 884744 | tf_op jit(solution)/shard_map/ppermute | solution.py:475
  95.0 22.2 %collective-permute-start.19 = (bf16[1152,128]{1,0:T(8,128)(2,1)S(1)}, bf16[1152,128]{1,0:T(8,128)(2,1)S(1)}, u32[]{:S(2)}, u32[]{:S(2)}) collective-permute-start(bf16[1152,128]{1,0:T(8,128)(2,1)S(1)} %get-tuple-element.126), channel_id=1, source_target_pairs={{0,12},{4,8},{8,4},{12,0},{16,28},{20,24},{24,20},{28,16},{1,13},{... | collective-permute-start | bytes 884744 | tf_op jit(solution)/shard_map/ppermute | solution.py:475
  100.3 17.9 %collective-permute-start.20 = (bf16[1152,128]{1,0:T(8,128)(2,1)S(1)}, bf16[1152,128]{1,0:T(8,128)(2,1)S(1)}, u32[]{:S(2)}, u32[]{:S(2)}) collective-permute-start(bf16[1152,128]{1,0:T(8,128)(2,1)S(1)} %get-tuple-element.127), channel_id=1, source_target_pairs={{0,20},{4,16},{8,28},{12,24},{16,4},{20,0},{24,12},{28,8},{1,21},{... | collective-permute-start | bytes 884744 | tf_op jit(solution)/shard_map/ppermute | solution.py:475
  105.4 12.8 %collective-permute-start.21 = (bf16[1152,128]{1,0:T(8,128)(2,1)S(1)}, bf16[1152,128]{1,0:T(8,128)(2,1)S(1)}, u32[]{:S(2)}, u32[]{:S(2)}) collective-permute-start(bf16[1152,128]{1,0:T(8,128)(2,1)S(1)} %get-tuple-element.128), channel_id=1, source_target_pairs={{0,4},{4,0},{8,12},{12,8},{16,20},{20,16},{24,28},{28,24},{1,5},{5... | collective-permute-start | bytes 884744 | tf_op jit(solution)/shard_map/ppermute | solution.py:475

commit v18 on v17

--- a/solution.py
+++ b/solution.py
@@ -193,18 +193,25 @@
 def pipelined(plan_q, plan_k, count_ref, early, late, buffers):
     early(0, plan_q[0], plan_k[0], buffers[0], True)
 
-    def turns(diagonal):
-        def body(i, carry):
-            for turn in range(2):
-                now = 2 * i + turn
-                late(now, plan_q[now], plan_k[now], buffers[turn])
-                early(now + 1, plan_q[now + 1], plan_k[now + 1], buffers[1 - turn], diagonal)
-            return carry
-
-        return body
-
-    lax.fori_loop(0, count_ref[0], turns(False), 0)
-    lax.fori_loop(count_ref[0], count_ref[1], turns(True), 0)
+    def turns(base, count, diagonal):
+        for turn in range(2 * count):
+            now = 2 * base + turn
+            late(now, plan_q[now], plan_k[now], buffers[turn % 2])
+            early(now + 1, plan_q[now + 1], plan_k[now + 1], buffers[1 - turn % 2], diagonal)
+
+    def run(start, stop, diagonal):
+        doubles = (stop - start) // 2
+
+        @pl.loop(0, doubles)
+        def _(i):
+            turns(start + 2 * i, 2, diagonal)
+
+        @pl.loop(start + 2 * doubles, stop)
+        def _(i):
+            turns(i, 1, diagonal)
+
+    run(0, count_ref[0], False)
+    run(count_ref[0], count_ref[1], True)
 
 
 def forward_kernel(peers, heads, rows, bq, bk, kept, me_s, *refs):

time: 119 us -> 119 us (level)
  no operation moved by 1% of the time
where the time goes in v18:
time: 119 us; the launch traced here: 120 us
  waiting for transfers between devices  49.2 us (41%)
  Pallas kernels  41.6 us (35%)
  starting transfers between devices  23.5 us (20%)
  local copies, waits for them, and re-layouts  4.56 us (4%)
    ppermute x21, waiting for transfers between devices, exchange(): lax.ppermute(x, 'seq', [(i, i ^ d) for i in range(peers)])  43.1 us
    ppermute x21, starting transfers between devices, exchange(): lax.ppermute(x, 'seq', [(i, i ^ d) for i in range(peers)])  18.8 us
    pallas_call x1, Pallas kernels, attention_forward(): pl.pallas_call(functools.partial(forward_kernel, peers, heads, rows, bq,...  15.2 us
    pallas_call x1, Pallas kernels, attention_backward(): pl.pallas_call(functools.partial(backward_kernel, listed, heads, rows, bq...  13.1 us
    ppermute x3, waiting for transfers between devices, pass_on(): lax.ppermute(x, 'head', [(i, (i + 1) % groups) for i in range(groups)])  6.11 us
    ppermute x3, starting transfers between devices, pass_on(): lax.ppermute(x, 'head', [(i, (i + 1) % groups) for i in range(groups)])  4.66 us
    dynamic_slice x1, local copies, waits for them, and re-layouts, per_device(): lax.dynamic_slice_in_dim(out_weight, block * width, width, 1)  4.54 us
    pallas_call x1, Pallas kernels, pack_heads(): pl.pallas_call(functools.partial(pack_kernel, heads, rows), in_specs=[SME...  3.62 us
  transfers between devices with their start and end apart: 24, of which 15 were waited for; matrix products, arithmetic and copies ran while one was open for 4% of the time, Pallas kernels for 22%

profile of v18, /device:TPU:0, one launch (start us, length us, event | category | flops | bytes accessed | tf_op | source)
XLA Modules:
  0.0 119.8 jit_solution(8718658995448346033)
XLA Ops:
  0.6 3.1 %collective-permute-start = (bf16[384,1024]{1,0:T(8,128)(2,1)}, bf16[384,1024]{1,0:T(8,128)(2,1)S(1)}, u32[]{:S(2)}, u32[]{:S(2)}) collective-permute-start(bf16[384,1024]{1,0:T(8,128)(2,1)} %o_ref.1), channel_id=1, source_target_pairs={{0,1},{1,2},{2,3},{3,0},{4,5},{5,6},{6,7},{7,4},{8,9},{9,10},{10,1... | collective-permute-start | bytes 2359304 | tf_op jit(solution)/shard_map/ppermute | solution.py:485
  3.7 3.6 %shard_map.85 = (bf16[1168,128]{1,0:T(8,128)(2,1)}, bf16[1168,128]{1,0:T(8,128)(2,1)}, bf16[1168,128]{1,0:T(8,128)(2,1)}, bf16[1168,128]{1,0:T(8,128)(2,1)}, bf1...) custom-call(s32[1]{0:T(128)} %bitcast.me_s, ...), custom_call_target="tpu_custom_call" | custom-call | tf_op jit(solution)/shard_map/pallas_call | solution.py:63
  7.3 1.5 %collective-permute-start.1 = (bf16[1168,128]{1,0:T(8,128)(2,1)}, bf16[1168,128]{1,0:T(8,128)(2,1)S(1)}, u32[]{:S(2)}, u32[]{:S(2)}) collective-permute-start(bf16[1168,128]{1,0:T(8,128)(2,1)} %get-tuple-element.70), channel_id=1, source_target_pairs={{0,8},{4,12},{8,0},{12,4},{16,24},{20,28},{24,16},{28,20},{1,9},{5... | collective-permute-start | bytes 897032 | tf_op jit(solution)/shard_map/ppermute | solution.py:482
  8.8 1.5 %collective-permute-start.2 = (bf16[1168,128]{1,0:T(8,128)(2,1)}, bf16[1168,128]{1,0:T(8,128)(2,1)S(1)}, u32[]{:S(2)}, u32[]{:S(2)}) collective-permute-start(bf16[1168,128]{1,0:T(8,128)(2,1)} %get-tuple-element.71), channel_id=1, source_target_pairs={{0,16},{4,20},{8,24},{12,28},{16,0},{20,4},{24,8},{28,12},{1,17},{... | collective-permute-start | bytes 897032 | tf_op jit(solution)/shard_map/ppermute | solution.py:482
  10.3 0.5 collective-permute-start.3
  10.8 4.5 %constant_dynamic-slice_fusion = (bf16[1024,1024]{1,0:T(8,128)(2,1)S(1)}, bf16[1024,1024]{1,0:T(8,128)(2,1)S(1)}, bf16[1024,1024]{1,0:T(8,128)(2,1)S(1)}, bf16[1024,1024]{1,0:T(8,128)(2,1)S(1)}) fusion(bf16[1024,4096]{1,0:T(8,128)(2,1)} %param.10, s32[]{:T(128)S(6)} %select_n.15, s32[]{:T(128)S(6)} %select_n.13, s32[]{:T(128)S(6)} %select_n.12, s32[]{:T(128)S(6)} %select_n.14), kind=kLoop, calls=%fused_computation | loop fusion | bytes 16777232 | tf_op jit(solution)/shard_map/dynamic_slice | solution.py:506
  15.4 0.0 copy-start.2
  15.4 1.0 shard_map.86.refs_0_
  16.4 1.1 collective-permute-done.1.refs_2_
  17.6 6.2 %collective-permute-done.2.refs_4_ = bf16[1168,128]{1,0:T(8,128)(2,1)S(1)} collective-permute-done((bf16[1168,128]{1,0:T(8,128)(2,1)}, bf16[1168,128]{1,0:T(8,128)(2,1)S(1)}, u32[]{:S(2)}, u32[]{:S(2)}) %collective-permute-start.2) | collective-permute-done | bytes 299040 | tf_op jit(solution)/shard_map/ppermute | solution.py:482
  23.7 1.6 %collective-permute-start.4 = (bf16[384,1024]{1,0:T(8,128)(2,1)S(1)}, bf16[384,1024]{1,0:T(8,128)(2,1)S(1)}, u32[]{:S(2)}, u32[]{:S(2)}) collective-permute-start(bf16[384,1024]{1,0:T(8,128)(2,1)S(1)} %collective-permute-done.o_ref), channel_id=1, source_target_pairs={{0,1},{1,2},{2,3},{3,0},{4,5},{5,6},{6,7},{7,4},{8,9},{9,10},{10,1... | collective-permute-start | bytes 2359304 | tf_op jit(solution)/shard_map/ppermute | solution.py:485
  25.3 2.4 %collective-permute-start.6 = (bf16[1168,128]{1,0:T(8,128)(2,1)S(1)}, bf16[1168,128]{1,0:T(8,128)(2,1)S(1)}, u32[]{:S(2)}, u32[]{:S(2)}) collective-permute-start(bf16[1168,128]{1,0:T(8,128)(2,1)S(1)} %copy-done.4), channel_id=1, source_target_pairs={{0,20},{4,16},{8,28},{12,24},{16,4},{20,0},{24,12},{28,8},{1,21},{... | collective-permute-start | bytes 897032 | tf_op jit(solution)/shard_map/ppermute | solution.py:482
  27.7 0.4 collective-permute-start.7
  28.1 0.6 collective-permute-start.8
  28.6 1.0 shard_map.87.refs_0_
  29.7 6.0 %collective-permute-done.5.refs_7_ = bf16[1168,128]{1,0:T(8,128)(2,1)S(1)} collective-permute-done((bf16[1168,128]{1,0:T(8,128)(2,1)S(1)}, bf16[1168,128]{1,0:T(8,128)(2,1)S(1)}, u32[]{:S(2)}, u32[]{:S(2)}) %collective-permute-start.5) | collective-permute-done | bytes 299040 | tf_op jit(solution)/shard_map/ppermute | solution.py:482
  35.6 5.4 %collective-permute-done.6.refs_5_ = bf16[1168,128]{1,0:T(8,128)(2,1)S(1)} collective-permute-done((bf16[1168,128]{1,0:T(8,128)(2,1)S(1)}, bf16[1168,128]{1,0:T(8,128)(2,1)S(1)}, u32[]{:S(2)}, u32[]{:S(2)}) %collective-permute-start.6) | collective-permute-done | bytes 299040 | tf_op jit(solution)/shard_map/ppermute | solution.py:482
  41.1 3.0 %collective-permute-done.4.o_ref = bf16[384,1024]{1,0:T(8,128)(2,1)S(1)} collective-permute-done((bf16[384,1024]{1,0:T(8,128)(2,1)S(1)}, bf16[384,1024]{1,0:T(8,128)(2,1)S(1)}, u32[]{:S(2)}, u32[]{:S(2)}) %collective-permute-start.4) | collective-permute-done | bytes 786464 | tf_op jit(solution)/shard_map/ppermute | solution.py:485
  44.0 15.2 %shard_map.88 = (bf16[3072,128]{1,0:T(8,128)(2,1)S(1)}, bf16[3072,256]{1,0:T(8,128)(2,1)S(1)}, bf16[3072,256]{1,0:T(8,128)(2,1)S(1)}, bf16[128,3072]{1,0:T(8,128...) custom-call(s32[1]{0:T(128)} %bitcast.me_s, ...), custom_call_target="tpu_custom_call" | custom-call | flops 1811939328 | bytes 6291456 | tf_op jit(solution)/shard_map/pallas_call | solution.py:422
  59.2 1.0 shard_map.89.acc_ref
  60.2 3.1 %collective-permute-done.9.o_ref = bf16[384,1024]{1,0:T(8,128)(2,1)S(1)} collective-permute-done((bf16[384,1024]{1,0:T(8,128)(2,1)S(1)}, bf16[384,1024]{1,0:T(8,128)(2,1)S(1)}, u32[]{:S(2)}, u32[]{:S(2)}) %collective-permute-start.9) | collective-permute-done | bytes 786464 | tf_op jit(solution)/shard_map/ppermute | solution.py:485
  63.4 1.0 shard_map.90
  64.4 2.3 %collective-permute-start.10 = (bf16[384,128]{1,0:T(8,128)(2,1)S(1)}, bf16[384,128]{1,0:T(8,128)(2,1)S(1)}, u32[]{:S(2)}, u32[]{:S(2)}) collective-permute-start(bf16[384,128]{1,0:T(8,128)(2,1)S(1)} %get-tuple-element.107), channel_id=1, source_target_pairs={{0,24},{4,28},{8,16},{12,20},{16,8},{20,12},{24,0},{28,4},{1,25},{... | collective-permute-start | bytes 294920 | tf_op jit(solution)/shard_map/ppermute | solution.py:482
  66.7 0.3 collective-permute-start.12
  67.0 1.0 collective-permute-start.13
  68.0 1.7 %collective-permute-start.14 = (bf16[384,128]{1,0:T(8,128)(2,1)S(1)}, bf16[384,128]{1,0:T(8,128)(2,1)S(1)}, u32[]{:S(2)}, u32[]{:S(2)}) collective-permute-start(bf16[384,128]{1,0:T(8,128)(2,1)S(1)} %get-tuple-element.117), channel_id=1, source_target_pairs={{0,12},{4,8},{8,4},{12,0},{16,28},{20,24},{24,20},{28,16},{1,13},{... | collective-permute-start | bytes 294920 | tf_op jit(solution)/shard_map/ppermute | solution.py:482
  69.6 0.4 collective-permute-done.10.refs_4_
  70.0 0.5 collective-permute-start.15
  70.5 2.3 %collective-permute-done.11.refs_5_ = bf16[384,128]{1,0:T(8,128)(2,1)S(1)} collective-permute-done((bf16[384,128]{1,0:T(8,128)(2,1)S(1)}, bf16[384,128]{1,0:T(8,128)(2,1)S(1)}, u32[]{:S(2)}, u32[]{:S(2)}) %collective-permute-start.11) | collective-permute-done | bytes 98336 | tf_op jit(solution)/shard_map/ppermute | solution.py:482
  72.7 2.9 %shard_map.91 = (bf16[80,256,256]{2,1,0:T(8,128)(2,1)S(1)}, f32[128,3072]{1,0:T(8,128)S(1)}, f32[3072,128]{1,0:T(8,128)S(1)}, f32[3072,128]{1,0:T(8,128)S(1)}) custom-call(s32[80]{0:T(128)S(1)} %get-tuple-element.90.plan_q, s32[2]{0:T(128)S(1)} %get-tuple-element.92.count_ref, ...), custom_call_target="tpu_custom_call", output_to_operand_aliasing={{0}: (4, {})} | custom-call | tf_op jit(solution)/shard_map/pallas_call | solution.py:441
  75.7 0.2 collective-permute-done.14.refs_8_
  75.9 0.4 collective-permute-done.15.refs_9_
  76.3 13.1 %shard_map.92 = (f32[128,3072]{1,0:T(8,128)S(1)}, f32[3072,128]{1,0:T(8,128)S(1)}, f32[3072,128]{1,0:T(8,128)S(1)}) custom-call(s32[1]{0:T(128)} %bitcast.me_s, s32[80]{0:T(128)S(1)} %get-tuple-element.90.plan_q, s32[80]{0:T(128)S(1)} %get-tuple-element.91.plan_k, ...), custom_call_target="tpu_custom_call", output_to_operand_aliasing={{0}: (11, {}), {1}: (12, {}), {2}: (13, {})} | custom-call | flops 3019898880 | bytes 6291456 | tf_op jit(solution)/shard_map/pallas_call | solution.py:463
  89.4 0.2 shard_map.94
  89.5 2.3 %collective-permute-start.22 = (bf16[1152,128]{1,0:T(8,128)(2,1)S(1)}, bf16[1152,128]{1,0:T(8,128)(2,1)S(1)}, u32[]{:S(2)}, u32[]{:S(2)}) collective-permute-start(bf16[1152,128]{1,0:T(8,128)(2,1)S(1)} %get-tuple-element.129), channel_id=1, source_target_pairs={{0,24},{4,28},{8,16},{12,20},{16,8},{20,12},{24,0},{28,4},{1,25},{... | collective-permute-start | bytes 884744 | tf_op jit(solution)/shard_map/ppermute | solution.py:482
  91.8 0.1 collective-permute-start.23
  91.9 0.3 shard_map.93
  92.3 1.3 %collective-permute-start.17 = (bf16[1152,128]{1,0:T(8,128)(2,1)S(1)}, bf16[1152,128]{1,0:T(8,128)(2,1)S(1)}, u32[]{:S(2)}, u32[]{:S(2)}) collective-permute-start(bf16[1152,128]{1,0:T(8,128)(2,1)S(1)} %get-tuple-element.124), channel_id=1, source_target_pairs={{0,8},{4,12},{8,0},{12,4},{16,24},{20,28},{24,16},{28,20},{1,9},{5... | collective-permute-start | bytes 884744 | tf_op jit(solution)/shard_map/ppermute | solution.py:482
  93.6 1.5 %collective-permute-start.18 = (bf16[1152,128]{1,0:T(8,128)(2,1)S(1)}, bf16[1152,128]{1,0:T(8,128)(2,1)S(1)}, u32[]{:S(2)}, u32[]{:S(2)}) collective-permute-start(bf16[1152,128]{1,0:T(8,128)(2,1)S(1)} %get-tuple-element.125), channel_id=1, source_target_pairs={{0,16},{4,20},{8,24},{12,28},{16,0},{20,4},{24,8},{28,12},{1,17},{... | collective-permute-start | bytes 884744 | tf_op jit(solution)/shard_map/ppermute | solution.py:482
  95.1 0.1 collective-permute-start.19
  95.2 5.2 %collective-permute-done.22.refs_0_ = bf16[1152,128]{1,0:T(8,128)(2,1)S(1)} collective-permute-done((bf16[1152,128]{1,0:T(8,128)(2,1)S(1)}, bf16[1152,128]{1,0:T(8,128)(2,1)S(1)}, u32[]{:S(2)}, u32[]{:S(2)}) %collective-permute-start.22) | collective-permute-done | bytes 294944 | tf_op jit(solution)/shard_map/ppermute | solution.py:482
  100.5 5.1 %collective-permute-done.23.refs_1_ = bf16[1152,128]{1,0:T(8,128)(2,1)S(1)} collective-permute-done((bf16[1152,128]{1,0:T(8,128)(2,1)S(1)}, bf16[1152,128]{1,0:T(8,128)(2,1)S(1)}, u32[]{:S(2)}, u32[]{:S(2)}) %collective-permute-start.23) | collective-permute-done | bytes 294944 | tf_op jit(solution)/shard_map/ppermute | solution.py:482
  105.5 1.0 collective-permute-start.21
  106.6 1.0 shard_map.95
  107.5 5.1 %collective-permute-done.17.refs_0_ = bf16[1152,128]{1,0:T(8,128)(2,1)S(1)} collective-permute-done((bf16[1152,128]{1,0:T(8,128)(2,1)S(1)}, bf16[1152,128]{1,0:T(8,128)(2,1)S(1)}, u32[]{:S(2)}, u32[]{:S(2)}) %collective-permute-start.17) | collective-permute-done | bytes 294944 | tf_op jit(solution)/shard_map/ppermute | solution.py:482
  112.6 4.7 %collective-permute-done.19.refs_2_ = bf16[1152,128]{1,0:T(8,128)(2,1)S(1)} collective-permute-done((bf16[1152,128]{1,0:T(8,128)(2,1)S(1)}, bf16[1152,128]{1,0:T(8,128)(2,1)S(1)}, u32[]{:S(2)}, u32[]{:S(2)}) %collective-permute-start.19) | collective-permute-done | bytes 294944 | tf_op jit(solution)/shard_map/ppermute | solution.py:482
  117.3 1.0 collective-permute-done.20.refs_3_
  118.4 1.2 %shard_map.96 = (bf16[384,1024]{1,0:T(8,128)(2,1)}, bf16[384,1024]{1,0:T(8,128)(2,1)}, bf16[384,1024]{1,0:T(8,128)(2,1)}) custom-call(s32[1]{0:T(128)} %bitcast.me_s, bf16[1152,128]{1,0:T(8,128)(2,1)S(1)} %collective-permute-done.17.refs_0_, ...), custom_call_target="tpu_custom_call", output_to_operand_aliasing={{0}: (6, {}), {1}: (7, {}), {2}: (8, {})} | custom-call | tf_op jit(solution)/shard_map/pallas_call | solution.py:88
  (25 shorter events, 0.1 us)
Async XLA Ops:
  0.6 23.1 %collective-permute-start = (bf16[384,1024]{1,0:T(8,128)(2,1)}, bf16[384,1024]{1,0:T(8,128)(2,1)S(1)}, u32[]{:S(2)}, u32[]{:S(2)}) collective-permute-start(bf16[384,1024]{1,0:T(8,128)(2,1)} %o_ref.1), channel_id=1, source_target_pairs={{0,1},{1,2},{2,3},{3,0},{4,5},{5,6},{6,7},{7,4},{8,9},{9,10},{10,1... | collective-permute-start | bytes 2359304 | tf_op jit(solution)/shard_map/ppermute | solution.py:485
  7.3 10.2 %collective-permute-start.1 = (bf16[1168,128]{1,0:T(8,128)(2,1)}, bf16[1168,128]{1,0:T(8,128)(2,1)S(1)}, u32[]{:S(2)}, u32[]{:S(2)}) collective-permute-start(bf16[1168,128]{1,0:T(8,128)(2,1)} %get-tuple-element.70), channel_id=1, source_target_pairs={{0,8},{4,12},{8,0},{12,4},{16,24},{20,28},{24,16},{28,20},{1,9},{5... | collective-permute-start | bytes 897032 | tf_op jit(solution)/shard_map/ppermute | solution.py:482
  8.8 14.9 %collective-permute-start.2 = (bf16[1168,128]{1,0:T(8,128)(2,1)}, bf16[1168,128]{1,0:T(8,128)(2,1)S(1)}, u32[]{:S(2)}, u32[]{:S(2)}) collective-permute-start(bf16[1168,128]{1,0:T(8,128)(2,1)} %get-tuple-element.71), channel_id=1, source_target_pairs={{0,16},{4,20},{8,24},{12,28},{16,0},{20,4},{24,8},{28,12},{1,17},{... | collective-permute-start | bytes 897032 | tf_op jit(solution)/shard_map/ppermute | solution.py:482
  10.3 13.4 %collective-permute-start.3 = (bf16[1168,128]{1,0:T(8,128)(2,1)}, bf16[1168,128]{1,0:T(8,128)(2,1)S(1)}, u32[]{:S(2)}, u32[]{:S(2)}) collective-permute-start(bf16[1168,128]{1,0:T(8,128)(2,1)} %get-tuple-element.72), channel_id=1, source_target_pairs={{0,24},{4,28},{8,16},{12,20},{16,8},{20,12},{24,0},{28,4},{1,25},{... | collective-permute-start | bytes 897032 | tf_op jit(solution)/shard_map/ppermute | solution.py:482
  10.8 4.5 %copy-start = (bf16[384,1024]{1,0:T(8,128)(2,1)S(1)}, bf16[384,1024]{1,0:T(8,128)(2,1)}, u32[]{:S(2)}) copy-start(bf16[384,1024]{1,0:T(8,128)(2,1)} %o_ref.1) | copy-start | bytes 2359300
  15.4 9.9 %copy-start.5 = (bf16[1168,128]{1,0:T(8,128)(2,1)S(1)}, bf16[1168,128]{1,0:T(8,128)(2,1)}, u32[]{:S(2)}) copy-start(bf16[1168,128]{1,0:T(8,128)(2,1)} %get-tuple-element.75) | copy-start | bytes 897028
  15.4 9.9 %copy-start.4 = (bf16[1168,128]{1,0:T(8,128)(2,1)S(1)}, bf16[1168,128]{1,0:T(8,128)(2,1)}, u32[]{:S(2)}) copy-start(bf16[1168,128]{1,0:T(8,128)(2,1)} %get-tuple-element.76) | copy-start | bytes 897028
  15.4 12.3 %copy-start.3 = (bf16[1168,128]{1,0:T(8,128)(2,1)S(1)}, bf16[1168,128]{1,0:T(8,128)(2,1)}, u32[]{:S(2)}) copy-start(bf16[1168,128]{1,0:T(8,128)(2,1)} %get-tuple-element.77) | copy-start | bytes 897028
  15.4 12.7 %copy-start.2 = (bf16[1168,128]{1,0:T(8,128)(2,1)S(1)}, bf16[1168,128]{1,0:T(8,128)(2,1)}, u32[]{:S(2)}) copy-start(bf16[1168,128]{1,0:T(8,128)(2,1)} %get-tuple-element.78) | copy-start | bytes 897028
  23.7 20.3 %collective-permute-start.4 = (bf16[384,1024]{1,0:T(8,128)(2,1)S(1)}, bf16[384,1024]{1,0:T(8,128)(2,1)S(1)}, u32[]{:S(2)}, u32[]{:S(2)}) collective-permute-start(bf16[384,1024]{1,0:T(8,128)(2,1)S(1)} %collective-permute-done.o_ref), channel_id=1, source_target_pairs={{0,1},{1,2},{2,3},{3,0},{4,5},{5,6},{6,7},{7,4},{8,9},{9,10},{10,1... | collective-permute-start | bytes 2359304 | tf_op jit(solution)/shard_map/ppermute | solution.py:485
  25.3 10.3 %collective-permute-start.5 = (bf16[1168,128]{1,0:T(8,128)(2,1)S(1)}, bf16[1168,128]{1,0:T(8,128)(2,1)S(1)}, u32[]{:S(2)}, u32[]{:S(2)}) collective-permute-start(bf16[1168,128]{1,0:T(8,128)(2,1)S(1)} %copy-done.5), channel_id=1, source_target_pairs={{0,28},{4,24},{8,20},{12,16},{16,12},{20,8},{24,4},{28,0},{1,29},{... | collective-permute-start | bytes 897032 | tf_op jit(solution)/shard_map/ppermute | solution.py:482
  25.3 15.7 %collective-permute-start.6 = (bf16[1168,128]{1,0:T(8,128)(2,1)S(1)}, bf16[1168,128]{1,0:T(8,128)(2,1)S(1)}, u32[]{:S(2)}, u32[]{:S(2)}) collective-permute-start(bf16[1168,128]{1,0:T(8,128)(2,1)S(1)} %copy-done.4), channel_id=1, source_target_pairs={{0,20},{4,16},{8,28},{12,24},{16,4},{20,0},{24,12},{28,8},{1,21},{... | collective-permute-start | bytes 897032 | tf_op jit(solution)/shard_map/ppermute | solution.py:482
  27.7 13.3 %collective-permute-start.7 = (bf16[1168,128]{1,0:T(8,128)(2,1)S(1)}, bf16[1168,128]{1,0:T(8,128)(2,1)S(1)}, u32[]{:S(2)}, u32[]{:S(2)}) collective-permute-start(bf16[1168,128]{1,0:T(8,128)(2,1)S(1)} %copy-done.3), channel_id=1, source_target_pairs={{0,12},{4,8},{8,4},{12,0},{16,28},{20,24},{24,20},{28,16},{1,13},{... | collective-permute-start | bytes 897032 | tf_op jit(solution)/shard_map/ppermute | solution.py:482
  28.1 13.0 %collective-permute-start.8 = (bf16[1168,128]{1,0:T(8,128)(2,1)S(1)}, bf16[1168,128]{1,0:T(8,128)(2,1)S(1)}, u32[]{:S(2)}, u32[]{:S(2)}) collective-permute-start(bf16[1168,128]{1,0:T(8,128)(2,1)S(1)} %copy-done.2), channel_id=1, source_target_pairs={{0,4},{4,0},{8,12},{12,8},{16,20},{20,16},{24,28},{28,24},{1,5},{5... | collective-permute-start | bytes 897032 | tf_op jit(solution)/shard_map/ppermute | solution.py:482
  28.6 15.4 %copy-start.1 = (bf16[1168,128]{1,0:T(8,128)(2,1)S(1)}, bf16[1168,128]{1,0:T(8,128)(2,1)}, u32[]{:S(2)}) copy-start(bf16[1168,128]{1,0:T(8,128)(2,1)} %get-tuple-element.82.refs_0_) | copy-start | bytes 897028
  44.0 19.4 %collective-permute-start.9 = (bf16[384,1024]{1,0:T(8,128)(2,1)S(1)}, bf16[384,1024]{1,0:T(8,128)(2,1)S(1)}, u32[]{:S(2)}, u32[]{:S(2)}) collective-permute-start(bf16[384,1024]{1,0:T(8,128)(2,1)S(1)} %collective-permute-done.4.o_ref), channel_id=1, source_target_pairs={{0,1},{1,2},{2,3},{3,0},{4,5},{5,6},{6,7},{7,4},{8,9},{9,10},{10,1... | collective-permute-start | bytes 2359304 | tf_op jit(solution)/shard_map/ppermute | solution.py:485
  64.4 5.6 %collective-permute-start.10 = (bf16[384,128]{1,0:T(8,128)(2,1)S(1)}, bf16[384,128]{1,0:T(8,128)(2,1)S(1)}, u32[]{:S(2)}, u32[]{:S(2)}) collective-permute-start(bf16[384,128]{1,0:T(8,128)(2,1)S(1)} %get-tuple-element.107), channel_id=1, source_target_pairs={{0,24},{4,28},{8,16},{12,20},{16,8},{20,12},{24,0},{28,4},{1,25},{... | collective-permute-start | bytes 294920 | tf_op jit(solution)/shard_map/ppermute | solution.py:482
  66.7 6.1 %collective-permute-start.11 = (bf16[384,128]{1,0:T(8,128)(2,1)S(1)}, bf16[384,128]{1,0:T(8,128)(2,1)S(1)}, u32[]{:S(2)}, u32[]{:S(2)}) collective-permute-start(bf16[384,128]{1,0:T(8,128)(2,1)S(1)} %get-tuple-element.114), channel_id=1, source_target_pairs={{0,28},{4,24},{8,20},{12,16},{16,12},{20,8},{24,4},{28,0},{1,29},{... | collective-permute-start | bytes 294920 | tf_op jit(solution)/shard_map/ppermute | solution.py:482
  66.7 9.0 %collective-permute-start.12 = (bf16[384,128]{1,0:T(8,128)(2,1)S(1)}, bf16[384,128]{1,0:T(8,128)(2,1)S(1)}, u32[]{:S(2)}, u32[]{:S(2)}) collective-permute-start(bf16[384,128]{1,0:T(8,128)(2,1)S(1)} %get-tuple-element.115), channel_id=1, source_target_pairs={{0,8},{4,12},{8,0},{12,4},{16,24},{20,28},{24,16},{28,20},{1,9},{5... | collective-permute-start | bytes 294920 | tf_op jit(solution)/shard_map/ppermute | solution.py:482
  67.0 8.7 %collective-permute-start.13 = (bf16[384,128]{1,0:T(8,128)(2,1)S(1)}, bf16[384,128]{1,0:T(8,128)(2,1)S(1)}, u32[]{:S(2)}, u32[]{:S(2)}) collective-permute-start(bf16[384,128]{1,0:T(8,128)(2,1)S(1)} %get-tuple-element.116), channel_id=1, source_target_pairs={{0,16},{4,20},{8,24},{12,28},{16,0},{20,4},{24,8},{28,12},{1,17},{... | collective-permute-start | bytes 294920 | tf_op jit(solution)/shard_map/ppermute | solution.py:482
  68.0 7.9 %collective-permute-start.14 = (bf16[384,128]{1,0:T(8,128)(2,1)S(1)}, bf16[384,128]{1,0:T(8,128)(2,1)S(1)}, u32[]{:S(2)}, u32[]{:S(2)}) collective-permute-start(bf16[384,128]{1,0:T(8,128)(2,1)S(1)} %get-tuple-element.117), channel_id=1, source_target_pairs={{0,12},{4,8},{8,4},{12,0},{16,28},{20,24},{24,20},{28,16},{1,13},{... | collective-permute-start | bytes 294920 | tf_op jit(solution)/shard_map/ppermute | solution.py:482
  70.0 6.3 %collective-permute-start.15 = (bf16[384,128]{1,0:T(8,128)(2,1)S(1)}, bf16[384,128]{1,0:T(8,128)(2,1)S(1)}, u32[]{:S(2)}, u32[]{:S(2)}) collective-permute-start(bf16[384,128]{1,0:T(8,128)(2,1)S(1)} %get-tuple-element.118), channel_id=1, source_target_pairs={{0,20},{4,16},{8,28},{12,24},{16,4},{20,0},{24,12},{28,8},{1,21},{... | collective-permute-start | bytes 294920 | tf_op jit(solution)/shard_map/ppermute | solution.py:482
  72.7 3.6 %collective-permute-start.16 = (bf16[384,128]{1,0:T(8,128)(2,1)S(1)}, bf16[384,128]{1,0:T(8,128)(2,1)S(1)}, u32[]{:S(2)}, u32[]{:S(2)}) collective-permute-start(bf16[384,128]{1,0:T(8,128)(2,1)S(1)} %get-tuple-element.120), channel_id=1, source_target_pairs={{0,4},{4,0},{8,12},{12,8},{16,20},{20,16},{24,28},{28,24},{1,5},{5... | collective-permute-start | bytes 294920 | tf_op jit(solution)/shard_map/ppermute | solution.py:482
  89.5 10.9 %collective-permute-start.22 = (bf16[1152,128]{1,0:T(8,128)(2,1)S(1)}, bf16[1152,128]{1,0:T(8,128)(2,1)S(1)}, u32[]{:S(2)}, u32[]{:S(2)}) collective-permute-start(bf16[1152,128]{1,0:T(8,128)(2,1)S(1)} %get-tuple-element.129), channel_id=1, source_target_pairs={{0,24},{4,28},{8,16},{12,20},{16,8},{20,12},{24,0},{28,4},{1,25},{... | collective-permute-start | bytes 884744 | tf_op jit(solution)/shard_map/ppermute | solution.py:482
  91.8 13.7 %collective-permute-start.23 = (bf16[1152,128]{1,0:T(8,128)(2,1)S(1)}, bf16[1152,128]{1,0:T(8,128)(2,1)S(1)}, u32[]{:S(2)}, u32[]{:S(2)}) collective-permute-start(bf16[1152,128]{1,0:T(8,128)(2,1)S(1)} %get-tuple-element.130), channel_id=1, source_target_pairs={{0,28},{4,24},{8,20},{12,16},{16,12},{20,8},{24,4},{28,0},{1,29},{... | collective-permute-start | bytes 884744 | tf_op jit(solution)/shard_map/ppermute | solution.py:482
  92.3 20.4 %collective-permute-start.17 = (bf16[1152,128]{1,0:T(8,128)(2,1)S(1)}, bf16[1152,128]{1,0:T(8,128)(2,1)S(1)}, u32[]{:S(2)}, u32[]{:S(2)}) collective-permute-start(bf16[1152,128]{1,0:T(8,128)(2,1)S(1)} %get-tuple-element.124), channel_id=1, source_target_pairs={{0,8},{4,12},{8,0},{12,4},{16,24},{20,28},{24,16},{28,20},{1,9},{5... | collective-permute-start | bytes 884744 | tf_op jit(solution)/shard_map/ppermute | solution.py:482
  93.6 19.0 %collective-permute-start.18 = (bf16[1152,128]{1,0:T(8,128)(2,1)S(1)}, bf16[1152,128]{1,0:T(8,128)(2,1)S(1)}, u32[]{:S(2)}, u32[]{:S(2)}) collective-permute-start(bf16[1152,128]{1,0:T(8,128)(2,1)S(1)} %get-tuple-element.125), channel_id=1, source_target_pairs={{0,16},{4,20},{8,24},{12,28},{16,0},{20,4},{24,8},{28,12},{1,17},{... | collective-permute-start | bytes 884744 | tf_op jit(solution)/shard_map/ppermute | solution.py:482
  95.1 22.2 %collective-permute-start.19 = (bf16[1152,128]{1,0:T(8,128)(2,1)S(1)}, bf16[1152,128]{1,0:T(8,128)(2,1)S(1)}, u32[]{:S(2)}, u32[]{:S(2)}) collective-permute-start(bf16[1152,128]{1,0:T(8,128)(2,1)S(1)} %get-tuple-element.126), channel_id=1, source_target_pairs={{0,12},{4,8},{8,4},{12,0},{16,28},{20,24},{24,20},{28,16},{1,13},{... | collective-permute-start | bytes 884744 | tf_op jit(solution)/shard_map/ppermute | solution.py:482
  100.5 17.9 %collective-permute-start.20 = (bf16[1152,128]{1,0:T(8,128)(2,1)S(1)}, bf16[1152,128]{1,0:T(8,128)(2,1)S(1)}, u32[]{:S(2)}, u32[]{:S(2)}) collective-permute-start(bf16[1152,128]{1,0:T(8,128)(2,1)S(1)} %get-tuple-element.127), channel_id=1, source_target_pairs={{0,20},{4,16},{8,28},{12,24},{16,4},{20,0},{24,12},{28,8},{1,21},{... | collective-permute-start | bytes 884744 | tf_op jit(solution)/shard_map/ppermute | solution.py:482
  105.5 12.8 %collective-permute-start.21 = (bf16[1152,128]{1,0:T(8,128)(2,1)S(1)}, bf16[1152,128]{1,0:T(8,128)(2,1)S(1)}, u32[]{:S(2)}, u32[]{:S(2)}) collective-permute-start(bf16[1152,128]{1,0:T(8,128)(2,1)S(1)} %get-tuple-element.128), channel_id=1, source_target_pairs={{0,4},{4,0},{8,12},{12,8},{16,20},{20,16},{24,28},{28,24},{1,5},{5... | collective-permute-start | bytes 884744 | tf_op jit(solution)/shard_map/ppermute | solution.py:482

commit v19 on v18

--- a/solution.py
+++ b/solution.py
@@ -13,6 +13,7 @@
 DOC_ROWS = 16
 ONES_ROWS = 16
 STRIP = 128
+LOOP_TURNS = 4
 NEG_LARGE = -1e30
 VMEM_SPARE = 6 * 1024 * 1024
 VMEM_MOST = 56 * 1024 * 1024
@@ -200,13 +201,13 @@
             early(now + 1, plan_q[now + 1], plan_k[now + 1], buffers[1 - turn % 2], diagonal)
 
     def run(start, stop, diagonal):
-        doubles = (stop - start) // 2
-
-        @pl.loop(0, doubles)
+        many = (stop - start) // LOOP_TURNS
+
+        @pl.loop(0, many)
         def _(i):
-            turns(start + 2 * i, 2, diagonal)
-
-        @pl.loop(start + 2 * doubles, stop)
+            turns(start + LOOP_TURNS * i, LOOP_TURNS, diagonal)
+
+        @pl.loop(start + LOOP_TURNS * many, stop)
         def _(i):
             turns(i, 1, diagonal)
 

time: 119 us -> 118 us (level)
  Pallas kernels: 41.6 us -> 37.4 us
  waiting for transfers between devices: 49.2 us -> 51.5 us
    pallas_call x1, Pallas kernels: 13.1 us -> 11.1 us  [attention_backward(): pl.pallas_call(functools.partial(backward_kernel, listed, heads, rows, bq...]
    ppermute x3, waiting for transfers between devices: 6.11 us -> 7.9 us  [pass_on(): lax.ppermute(x, 'head', [(i, (i + 1) % groups) for i in range(groups)])]
    pallas_call x1, Pallas kernels: 15.2 us -> 13.4 us  [attention_forward(): pl.pallas_call(functools.partial(forward_kernel, peers, heads, rows, bq,...]
  transfers between devices with their start and end apart: 24 -> 24, of which waited for: 15 -> 15; matrix products, arithmetic and copies ran while one was open for 4% -> 4% of each run, Pallas kernels for 22% -> 20%
where the time goes in v19:
time: 118 us
  waiting for transfers between devices  51.5 us (44%)
  Pallas kernels  37.4 us (32%)
  starting transfers between devices  23.5 us (20%)
  local copies, waits for them, and re-layouts  4.56 us (4%)
    ppermute x21, waiting for transfers between devices, exchange(): lax.ppermute(x, 'seq', [(i, i ^ d) for i in range(peers)])  43.6 us
    ppermute x21, starting transfers between devices, exchange(): lax.ppermute(x, 'seq', [(i, i ^ d) for i in range(peers)])  18.8 us
    pallas_call x1, Pallas kernels, attention_forward(): pl.pallas_call(functools.partial(forward_kernel, peers, heads, rows, bq,...  13.4 us
    pallas_call x1, Pallas kernels, attention_backward(): pl.pallas_call(functools.partial(backward_kernel, listed, heads, rows, bq...  11.1 us
    ppermute x3, waiting for transfers between devices, pass_on(): lax.ppermute(x, 'head', [(i, (i + 1) % groups) for i in range(groups)])  7.9 us
    ppermute x3, starting transfers between devices, pass_on(): lax.ppermute(x, 'head', [(i, (i + 1) % groups) for i in range(groups)])  4.66 us
    dynamic_slice x1, local copies, waits for them, and re-layouts, per_device(): lax.dynamic_slice_in_dim(out_weight, block * width, width, 1)  4.54 us
    pallas_call x1, Pallas kernels, pack_heads(): pl.pallas_call(functools.partial(pack_kernel, heads, rows), in_specs=[SME...  3.62 us
  transfers between devices with their start and end apart: 24, of which 15 were waited for; matrix products, arithmetic and copies ran while one was open for 4% of the time, Pallas kernels for 20%

profile of v19, /device:TPU:0, one launch (start us, length us, event | category | flops | bytes accessed | tf_op | source)
XLA Modules:
  0.0 117.8 jit_solution(2141060130137475655)
XLA Ops:
  0.6 3.1 %collective-permute-start = (bf16[384,1024]{1,0:T(8,128)(2,1)}, bf16[384,1024]{1,0:T(8,128)(2,1)S(1)}, u32[]{:S(2)}, u32[]{:S(2)}) collective-permute-start(bf16[384,1024]{1,0:T(8,128)(2,1)} %o_ref.1), channel_id=1, source_target_pairs={{0,1},{1,2},{2,3},{3,0},{4,5},{5,6},{6,7},{7,4},{8,9},{9,10},{10,1... | collective-permute-start | bytes 2359304 | tf_op jit(solution)/shard_map/ppermute | solution.py:486
  3.7 3.6 %shard_map.85 = (bf16[1168,128]{1,0:T(8,128)(2,1)}, bf16[1168,128]{1,0:T(8,128)(2,1)}, bf16[1168,128]{1,0:T(8,128)(2,1)}, bf16[1168,128]{1,0:T(8,128)(2,1)}, bf1...) custom-call(s32[1]{0:T(128)} %bitcast.me_s, ...), custom_call_target="tpu_custom_call" | custom-call | tf_op jit(solution)/shard_map/pallas_call | solution.py:64
  7.3 1.5 %collective-permute-start.1 = (bf16[1168,128]{1,0:T(8,128)(2,1)}, bf16[1168,128]{1,0:T(8,128)(2,1)S(1)}, u32[]{:S(2)}, u32[]{:S(2)}) collective-permute-start(bf16[1168,128]{1,0:T(8,128)(2,1)} %get-tuple-element.70), channel_id=1, source_target_pairs={{0,8},{4,12},{8,0},{12,4},{16,24},{20,28},{24,16},{28,20},{1,9},{5... | collective-permute-start | bytes 897032 | tf_op jit(solution)/shard_map/ppermute | solution.py:483
  8.8 1.5 %collective-permute-start.2 = (bf16[1168,128]{1,0:T(8,128)(2,1)}, bf16[1168,128]{1,0:T(8,128)(2,1)S(1)}, u32[]{:S(2)}, u32[]{:S(2)}) collective-permute-start(bf16[1168,128]{1,0:T(8,128)(2,1)} %get-tuple-element.71), channel_id=1, source_target_pairs={{0,16},{4,20},{8,24},{12,28},{16,0},{20,4},{24,8},{28,12},{1,17},{... | collective-permute-start | bytes 897032 | tf_op jit(solution)/shard_map/ppermute | solution.py:483
  10.3 0.5 collective-permute-start.3
  10.8 4.5 %constant_dynamic-slice_fusion = (bf16[1024,1024]{1,0:T(8,128)(2,1)S(1)}, bf16[1024,1024]{1,0:T(8,128)(2,1)S(1)}, bf16[1024,1024]{1,0:T(8,128)(2,1)S(1)}, bf16[1024,1024]{1,0:T(8,128)(2,1)S(1)}) fusion(bf16[1024,4096]{1,0:T(8,128)(2,1)} %param.10, s32[]{:T(128)S(6)} %select_n.15, s32[]{:T(128)S(6)} %select_n.13, s32[]{:T(128)S(6)} %select_n.12, s32[]{:T(128)S(6)} %select_n.14), kind=kLoop, calls=%fused_computation | loop fusion | bytes 16777232 | tf_op jit(solution)/shard_map/dynamic_slice | solution.py:507
  15.4 0.0 copy-start.2
  15.4 1.0 shard_map.86.refs_0_
  16.4 1.1 collective-permute-done.1.refs_2_
  17.6 6.2 %collective-permute-done.2.refs_4_ = bf16[1168,128]{1,0:T(8,128)(2,1)S(1)} collective-permute-done((bf16[1168,128]{1,0:T(8,128)(2,1)}, bf16[1168,128]{1,0:T(8,128)(2,1)S(1)}, u32[]{:S(2)}, u32[]{:S(2)}) %collective-permute-start.2) | collective-permute-done | bytes 299040 | tf_op jit(solution)/shard_map/ppermute | solution.py:483
  23.7 1.6 %collective-permute-start.4 = (bf16[384,1024]{1,0:T(8,128)(2,1)S(1)}, bf16[384,1024]{1,0:T(8,128)(2,1)S(1)}, u32[]{:S(2)}, u32[]{:S(2)}) collective-permute-start(bf16[384,1024]{1,0:T(8,128)(2,1)S(1)} %collective-permute-done.o_ref), channel_id=1, source_target_pairs={{0,1},{1,2},{2,3},{3,0},{4,5},{5,6},{6,7},{7,4},{8,9},{9,10},{10,1... | collective-permute-start | bytes 2359304 | tf_op jit(solution)/shard_map/ppermute | solution.py:486
  25.3 2.4 %collective-permute-start.6 = (bf16[1168,128]{1,0:T(8,128)(2,1)S(1)}, bf16[1168,128]{1,0:T(8,128)(2,1)S(1)}, u32[]{:S(2)}, u32[]{:S(2)}) collective-permute-start(bf16[1168,128]{1,0:T(8,128)(2,1)S(1)} %copy-done.4), channel_id=1, source_target_pairs={{0,20},{4,16},{8,28},{12,24},{16,4},{20,0},{24,12},{28,8},{1,21},{... | collective-permute-start | bytes 897032 | tf_op jit(solution)/shard_map/ppermute | solution.py:483
  27.7 0.4 collective-permute-start.7
  28.1 0.6 collective-permute-start.8
  28.6 1.0 shard_map.87.refs_0_
  29.7 6.0 %collective-permute-done.5.refs_7_ = bf16[1168,128]{1,0:T(8,128)(2,1)S(1)} collective-permute-done((bf16[1168,128]{1,0:T(8,128)(2,1)S(1)}, bf16[1168,128]{1,0:T(8,128)(2,1)S(1)}, u32[]{:S(2)}, u32[]{:S(2)}) %collective-permute-start.5) | collective-permute-done | bytes 299040 | tf_op jit(solution)/shard_map/ppermute | solution.py:483
  35.6 5.4 %collective-permute-done.6.refs_5_ = bf16[1168,128]{1,0:T(8,128)(2,1)S(1)} collective-permute-done((bf16[1168,128]{1,0:T(8,128)(2,1)S(1)}, bf16[1168,128]{1,0:T(8,128)(2,1)S(1)}, u32[]{:S(2)}, u32[]{:S(2)}) %collective-permute-start.6) | collective-permute-done | bytes 299040 | tf_op jit(solution)/shard_map/ppermute | solution.py:483
  41.1 3.0 %collective-permute-done.4.o_ref = bf16[384,1024]{1,0:T(8,128)(2,1)S(1)} collective-permute-done((bf16[384,1024]{1,0:T(8,128)(2,1)S(1)}, bf16[384,1024]{1,0:T(8,128)(2,1)S(1)}, u32[]{:S(2)}, u32[]{:S(2)}) %collective-permute-start.4) | collective-permute-done | bytes 786464 | tf_op jit(solution)/shard_map/ppermute | solution.py:486
  44.0 13.4 %shard_map.88 = (bf16[3072,128]{1,0:T(8,128)(2,1)S(1)}, bf16[3072,256]{1,0:T(8,128)(2,1)S(1)}, bf16[3072,256]{1,0:T(8,128)(2,1)S(1)}, bf16[128,3072]{1,0:T(8,128...) custom-call(s32[1]{0:T(128)} %bitcast.me_s, ...), custom_call_target="tpu_custom_call" | custom-call | flops 1811939328 | bytes 6291456 | tf_op jit(solution)/shard_map/pallas_call | solution.py:423
  57.4 1.0 shard_map.89.acc_ref
  58.4 4.9 %collective-permute-done.9.o_ref = bf16[384,1024]{1,0:T(8,128)(2,1)S(1)} collective-permute-done((bf16[384,1024]{1,0:T(8,128)(2,1)S(1)}, bf16[384,1024]{1,0:T(8,128)(2,1)S(1)}, u32[]{:S(2)}, u32[]{:S(2)}) %collective-permute-start.9) | collective-permute-done | bytes 786464 | tf_op jit(solution)/shard_map/ppermute | solution.py:486
  63.4 1.0 shard_map.90
  64.4 2.3 %collective-permute-start.10 = (bf16[384,128]{1,0:T(8,128)(2,1)S(1)}, bf16[384,128]{1,0:T(8,128)(2,1)S(1)}, u32[]{:S(2)}, u32[]{:S(2)}) collective-permute-start(bf16[384,128]{1,0:T(8,128)(2,1)S(1)} %get-tuple-element.107), channel_id=1, source_target_pairs={{0,24},{4,28},{8,16},{12,20},{16,8},{20,12},{24,0},{28,4},{1,25},{... | collective-permute-start | bytes 294920 | tf_op jit(solution)/shard_map/ppermute | solution.py:483
  66.7 0.3 collective-permute-start.12
  67.0 1.0 collective-permute-start.13
  68.0 1.7 %collective-permute-start.14 = (bf16[384,128]{1,0:T(8,128)(2,1)S(1)}, bf16[384,128]{1,0:T(8,128)(2,1)S(1)}, u32[]{:S(2)}, u32[]{:S(2)}) collective-permute-start(bf16[384,128]{1,0:T(8,128)(2,1)S(1)} %get-tuple-element.117), channel_id=1, source_target_pairs={{0,12},{4,8},{8,4},{12,0},{16,28},{20,24},{24,20},{28,16},{1,13},{... | collective-permute-start | bytes 294920 | tf_op jit(solution)/shard_map/ppermute | solution.py:483
  69.6 0.4 collective-permute-done.10.refs_4_
  70.0 0.5 collective-permute-start.15
  70.5 2.3 %collective-permute-done.11.refs_5_ = bf16[384,128]{1,0:T(8,128)(2,1)S(1)} collective-permute-done((bf16[384,128]{1,0:T(8,128)(2,1)S(1)}, bf16[384,128]{1,0:T(8,128)(2,1)S(1)}, u32[]{:S(2)}, u32[]{:S(2)}) %collective-permute-start.11) | collective-permute-done | bytes 98336 | tf_op jit(solution)/shard_map/ppermute | solution.py:483
  72.7 2.5 %shard_map.91 = (bf16[80,256,256]{2,1,0:T(8,128)(2,1)S(1)}, f32[128,3072]{1,0:T(8,128)S(1)}, f32[3072,128]{1,0:T(8,128)S(1)}, f32[3072,128]{1,0:T(8,128)S(1)}) custom-call(s32[80]{0:T(128)S(1)} %get-tuple-element.90.plan_q, s32[2]{0:T(128)S(1)} %get-tuple-element.92.count_ref, ...), custom_call_target="tpu_custom_call", output_to_operand_aliasing={{0}: (4, {})} | custom-call | tf_op jit(solution)/shard_map/pallas_call | solution.py:442
  75.2 0.7 collective-permute-done.14.refs_8_
  75.9 0.4 collective-permute-done.15.refs_9_
  76.3 11.1 %shard_map.92 = (f32[128,3072]{1,0:T(8,128)S(1)}, f32[3072,128]{1,0:T(8,128)S(1)}, f32[3072,128]{1,0:T(8,128)S(1)}) custom-call(s32[1]{0:T(128)} %bitcast.me_s, s32[80]{0:T(128)S(1)} %get-tuple-element.90.plan_q, s32[80]{0:T(128)S(1)} %get-tuple-element.91.plan_k, ...), custom_call_target="tpu_custom_call", output_to_operand_aliasing={{0}: (11, {}), {1}: (12, {}), {2}: (13, {})} | custom-call | flops 3019898880 | bytes 6291456 | tf_op jit(solution)/shard_map/pallas_call | solution.py:464
  87.5 0.2 shard_map.94
  87.6 2.3 %collective-permute-start.22 = (bf16[1152,128]{1,0:T(8,128)(2,1)S(1)}, bf16[1152,128]{1,0:T(8,128)(2,1)S(1)}, u32[]{:S(2)}, u32[]{:S(2)}) collective-permute-start(bf16[1152,128]{1,0:T(8,128)(2,1)S(1)} %get-tuple-element.129), channel_id=1, source_target_pairs={{0,24},{4,28},{8,16},{12,20},{16,8},{20,12},{24,0},{28,4},{1,25},{... | collective-permute-start | bytes 884744 | tf_op jit(solution)/shard_map/ppermute | solution.py:483
  89.9 0.1 collective-permute-start.23
  90.0 0.3 shard_map.93
  90.3 1.3 %collective-permute-start.17 = (bf16[1152,128]{1,0:T(8,128)(2,1)S(1)}, bf16[1152,128]{1,0:T(8,128)(2,1)S(1)}, u32[]{:S(2)}, u32[]{:S(2)}) collective-permute-start(bf16[1152,128]{1,0:T(8,128)(2,1)S(1)} %get-tuple-element.124), channel_id=1, source_target_pairs={{0,8},{4,12},{8,0},{12,4},{16,24},{20,28},{24,16},{28,20},{1,9},{5... | collective-permute-start | bytes 884744 | tf_op jit(solution)/shard_map/ppermute | solution.py:483
  91.7 1.5 %collective-permute-start.18 = (bf16[1152,128]{1,0:T(8,128)(2,1)S(1)}, bf16[1152,128]{1,0:T(8,128)(2,1)S(1)}, u32[]{:S(2)}, u32[]{:S(2)}) collective-permute-start(bf16[1152,128]{1,0:T(8,128)(2,1)S(1)} %get-tuple-element.125), channel_id=1, source_target_pairs={{0,16},{4,20},{8,24},{12,28},{16,0},{20,4},{24,8},{28,12},{1,17},{... | collective-permute-start | bytes 884744 | tf_op jit(solution)/shard_map/ppermute | solution.py:483
  93.2 0.1 collective-permute-start.19
  93.3 5.2 %collective-permute-done.22.refs_0_ = bf16[1152,128]{1,0:T(8,128)(2,1)S(1)} collective-permute-done((bf16[1152,128]{1,0:T(8,128)(2,1)S(1)}, bf16[1152,128]{1,0:T(8,128)(2,1)S(1)}, u32[]{:S(2)}, u32[]{:S(2)}) %collective-permute-start.22) | collective-permute-done | bytes 294944 | tf_op jit(solution)/shard_map/ppermute | solution.py:483
  98.5 5.1 %collective-permute-done.23.refs_1_ = bf16[1152,128]{1,0:T(8,128)(2,1)S(1)} collective-permute-done((bf16[1152,128]{1,0:T(8,128)(2,1)S(1)}, bf16[1152,128]{1,0:T(8,128)(2,1)S(1)}, u32[]{:S(2)}, u32[]{:S(2)}) %collective-permute-start.23) | collective-permute-done | bytes 294944 | tf_op jit(solution)/shard_map/ppermute | solution.py:483
  103.6 1.0 collective-permute-start.21
  104.6 1.0 shard_map.95
  105.6 5.1 %collective-permute-done.17.refs_0_ = bf16[1152,128]{1,0:T(8,128)(2,1)S(1)} collective-permute-done((bf16[1152,128]{1,0:T(8,128)(2,1)S(1)}, bf16[1152,128]{1,0:T(8,128)(2,1)S(1)}, u32[]{:S(2)}, u32[]{:S(2)}) %collective-permute-start.17) | collective-permute-done | bytes 294944 | tf_op jit(solution)/shard_map/ppermute | solution.py:483
  110.7 4.7 %collective-permute-done.19.refs_2_ = bf16[1152,128]{1,0:T(8,128)(2,1)S(1)} collective-permute-done((bf16[1152,128]{1,0:T(8,128)(2,1)S(1)}, bf16[1152,128]{1,0:T(8,128)(2,1)S(1)}, u32[]{:S(2)}, u32[]{:S(2)}) %collective-permute-start.19) | collective-permute-done | bytes 294944 | tf_op jit(solution)/shard_map/ppermute | solution.py:483
  115.4 1.0 collective-permute-done.20.refs_3_
  116.5 1.2 %shard_map.96 = (bf16[384,1024]{1,0:T(8,128)(2,1)}, bf16[384,1024]{1,0:T(8,128)(2,1)}, bf16[384,1024]{1,0:T(8,128)(2,1)}) custom-call(s32[1]{0:T(128)} %bitcast.me_s, bf16[1152,128]{1,0:T(8,128)(2,1)S(1)} %collective-permute-done.17.refs_0_, ...), custom_call_target="tpu_custom_call", output_to_operand_aliasing={{0}: (6, {}), {1}: (7, {}), {2}: (8, {})} | custom-call | tf_op jit(solution)/shard_map/pallas_call | solution.py:89
  (25 shorter events, 0.1 us)
Async XLA Ops:
  0.6 23.1 %collective-permute-start = (bf16[384,1024]{1,0:T(8,128)(2,1)}, bf16[384,1024]{1,0:T(8,128)(2,1)S(1)}, u32[]{:S(2)}, u32[]{:S(2)}) collective-permute-start(bf16[384,1024]{1,0:T(8,128)(2,1)} %o_ref.1), channel_id=1, source_target_pairs={{0,1},{1,2},{2,3},{3,0},{4,5},{5,6},{6,7},{7,4},{8,9},{9,10},{10,1... | collective-permute-start | bytes 2359304 | tf_op jit(solution)/shard_map/ppermute | solution.py:486
  7.3 10.2 %collective-permute-start.1 = (bf16[1168,128]{1,0:T(8,128)(2,1)}, bf16[1168,128]{1,0:T(8,128)(2,1)S(1)}, u32[]{:S(2)}, u32[]{:S(2)}) collective-permute-start(bf16[1168,128]{1,0:T(8,128)(2,1)} %get-tuple-element.70), channel_id=1, source_target_pairs={{0,8},{4,12},{8,0},{12,4},{16,24},{20,28},{24,16},{28,20},{1,9},{5... | collective-permute-start | bytes 897032 | tf_op jit(solution)/shard_map/ppermute | solution.py:483
  8.8 14.9 %collective-permute-start.2 = (bf16[1168,128]{1,0:T(8,128)(2,1)}, bf16[1168,128]{1,0:T(8,128)(2,1)S(1)}, u32[]{:S(2)}, u32[]{:S(2)}) collective-permute-start(bf16[1168,128]{1,0:T(8,128)(2,1)} %get-tuple-element.71), channel_id=1, source_target_pairs={{0,16},{4,20},{8,24},{12,28},{16,0},{20,4},{24,8},{28,12},{1,17},{... | collective-permute-start | bytes 897032 | tf_op jit(solution)/shard_map/ppermute | solution.py:483
  10.3 13.4 %collective-permute-start.3 = (bf16[1168,128]{1,0:T(8,128)(2,1)}, bf16[1168,128]{1,0:T(8,128)(2,1)S(1)}, u32[]{:S(2)}, u32[]{:S(2)}) collective-permute-start(bf16[1168,128]{1,0:T(8,128)(2,1)} %get-tuple-element.72), channel_id=1, source_target_pairs={{0,24},{4,28},{8,16},{12,20},{16,8},{20,12},{24,0},{28,4},{1,25},{... | collective-permute-start | bytes 897032 | tf_op jit(solution)/shard_map/ppermute | solution.py:483
  10.8 4.5 %copy-start = (bf16[384,1024]{1,0:T(8,128)(2,1)S(1)}, bf16[384,1024]{1,0:T(8,128)(2,1)}, u32[]{:S(2)}) copy-start(bf16[384,1024]{1,0:T(8,128)(2,1)} %o_ref.1) | copy-start | bytes 2359300
  15.4 9.9 %copy-start.5 = (bf16[1168,128]{1,0:T(8,128)(2,1)S(1)}, bf16[1168,128]{1,0:T(8,128)(2,1)}, u32[]{:S(2)}) copy-start(bf16[1168,128]{1,0:T(8,128)(2,1)} %get-tuple-element.75) | copy-start | bytes 897028
  15.4 9.9 %copy-start.4 = (bf16[1168,128]{1,0:T(8,128)(2,1)S(1)}, bf16[1168,128]{1,0:T(8,128)(2,1)}, u32[]{:S(2)}) copy-start(bf16[1168,128]{1,0:T(8,128)(2,1)} %get-tuple-element.76) | copy-start | bytes 897028
  15.4 12.3 %copy-start.3 = (bf16[1168,128]{1,0:T(8,128)(2,1)S(1)}, bf16[1168,128]{1,0:T(8,128)(2,1)}, u32[]{:S(2)}) copy-start(bf16[1168,128]{1,0:T(8,128)(2,1)} %get-tuple-element.77) | copy-start | bytes 897028
  15.4 12.7 %copy-start.2 = (bf16[1168,128]{1,0:T(8,128)(2,1)S(1)}, bf16[1168,128]{1,0:T(8,128)(2,1)}, u32[]{:S(2)}) copy-start(bf16[1168,128]{1,0:T(8,128)(2,1)} %get-tuple-element.78) | copy-start | bytes 897028
  23.7 20.3 %collective-permute-start.4 = (bf16[384,1024]{1,0:T(8,128)(2,1)S(1)}, bf16[384,1024]{1,0:T(8,128)(2,1)S(1)}, u32[]{:S(2)}, u32[]{:S(2)}) collective-permute-start(bf16[384,1024]{1,0:T(8,128)(2,1)S(1)} %collective-permute-done.o_ref), channel_id=1, source_target_pairs={{0,1},{1,2},{2,3},{3,0},{4,5},{5,6},{6,7},{7,4},{8,9},{9,10},{10,1... | collective-permute-start | bytes 2359304 | tf_op jit(solution)/shard_map/ppermute | solution.py:486
  25.3 10.3 %collective-permute-start.5 = (bf16[1168,128]{1,0:T(8,128)(2,1)S(1)}, bf16[1168,128]{1,0:T(8,128)(2,1)S(1)}, u32[]{:S(2)}, u32[]{:S(2)}) collective-permute-start(bf16[1168,128]{1,0:T(8,128)(2,1)S(1)} %copy-done.5), channel_id=1, source_target_pairs={{0,28},{4,24},{8,20},{12,16},{16,12},{20,8},{24,4},{28,0},{1,29},{... | collective-permute-start | bytes 897032 | tf_op jit(solution)/shard_map/ppermute | solution.py:483
  25.3 15.7 %collective-permute-start.6 = (bf16[1168,128]{1,0:T(8,128)(2,1)S(1)}, bf16[1168,128]{1,0:T(8,128)(2,1)S(1)}, u32[]{:S(2)}, u32[]{:S(2)}) collective-permute-start(bf16[1168,128]{1,0:T(8,128)(2,1)S(1)} %copy-done.4), channel_id=1, source_target_pairs={{0,20},{4,16},{8,28},{12,24},{16,4},{20,0},{24,12},{28,8},{1,21},{... | collective-permute-start | bytes 897032 | tf_op jit(solution)/shard_map/ppermute | solution.py:483
  27.7 13.3 %collective-permute-start.7 = (bf16[1168,128]{1,0:T(8,128)(2,1)S(1)}, bf16[1168,128]{1,0:T(8,128)(2,1)S(1)}, u32[]{:S(2)}, u32[]{:S(2)}) collective-permute-start(bf16[1168,128]{1,0:T(8,128)(2,1)S(1)} %copy-done.3), channel_id=1, source_target_pairs={{0,12},{4,8},{8,4},{12,0},{16,28},{20,24},{24,20},{28,16},{1,13},{... | collective-permute-start | bytes 897032 | tf_op jit(solution)/shard_map/ppermute | solution.py:483
  28.1 13.0 %collective-permute-start.8 = (bf16[1168,128]{1,0:T(8,128)(2,1)S(1)}, bf16[1168,128]{1,0:T(8,128)(2,1)S(1)}, u32[]{:S(2)}, u32[]{:S(2)}) collective-permute-start(bf16[1168,128]{1,0:T(8,128)(2,1)S(1)} %copy-done.2), channel_id=1, source_target_pairs={{0,4},{4,0},{8,12},{12,8},{16,20},{20,16},{24,28},{28,24},{1,5},{5... | collective-permute-start | bytes 897032 | tf_op jit(solution)/shard_map/ppermute | solution.py:483
  28.6 15.4 %copy-start.1 = (bf16[1168,128]{1,0:T(8,128)(2,1)S(1)}, bf16[1168,128]{1,0:T(8,128)(2,1)}, u32[]{:S(2)}) copy-start(bf16[1168,128]{1,0:T(8,128)(2,1)} %get-tuple-element.82.refs_0_) | copy-start | bytes 897028
  44.0 19.4 %collective-permute-start.9 = (bf16[384,1024]{1,0:T(8,128)(2,1)S(1)}, bf16[384,1024]{1,0:T(8,128)(2,1)S(1)}, u32[]{:S(2)}, u32[]{:S(2)}) collective-permute-start(bf16[384,1024]{1,0:T(8,128)(2,1)S(1)} %collective-permute-done.4.o_ref), channel_id=1, source_target_pairs={{0,1},{1,2},{2,3},{3,0},{4,5},{5,6},{6,7},{7,4},{8,9},{9,10},{10,1... | collective-permute-start | bytes 2359304 | tf_op jit(solution)/shard_map/ppermute | solution.py:486
  64.4 5.6 %collective-permute-start.10 = (bf16[384,128]{1,0:T(8,128)(2,1)S(1)}, bf16[384,128]{1,0:T(8,128)(2,1)S(1)}, u32[]{:S(2)}, u32[]{:S(2)}) collective-permute-start(bf16[384,128]{1,0:T(8,128)(2,1)S(1)} %get-tuple-element.107), channel_id=1, source_target_pairs={{0,24},{4,28},{8,16},{12,20},{16,8},{20,12},{24,0},{28,4},{1,25},{... | collective-permute-start | bytes 294920 | tf_op jit(solution)/shard_map/ppermute | solution.py:483
  66.7 6.1 %collective-permute-start.11 = (bf16[384,128]{1,0:T(8,128)(2,1)S(1)}, bf16[384,128]{1,0:T(8,128)(2,1)S(1)}, u32[]{:S(2)}, u32[]{:S(2)}) collective-permute-start(bf16[384,128]{1,0:T(8,128)(2,1)S(1)} %get-tuple-element.114), channel_id=1, source_target_pairs={{0,28},{4,24},{8,20},{12,16},{16,12},{20,8},{24,4},{28,0},{1,29},{... | collective-permute-start | bytes 294920 | tf_op jit(solution)/shard_map/ppermute | solution.py:483
  66.7 8.5 %collective-permute-start.12 = (bf16[384,128]{1,0:T(8,128)(2,1)S(1)}, bf16[384,128]{1,0:T(8,128)(2,1)S(1)}, u32[]{:S(2)}, u32[]{:S(2)}) collective-permute-start(bf16[384,128]{1,0:T(8,128)(2,1)S(1)} %get-tuple-element.115), channel_id=1, source_target_pairs={{0,8},{4,12},{8,0},{12,4},{16,24},{20,28},{24,16},{28,20},{1,9},{5... | collective-permute-start | bytes 294920 | tf_op jit(solution)/shard_map/ppermute | solution.py:483
  67.0 8.3 %collective-permute-start.13 = (bf16[384,128]{1,0:T(8,128)(2,1)S(1)}, bf16[384,128]{1,0:T(8,128)(2,1)S(1)}, u32[]{:S(2)}, u32[]{:S(2)}) collective-permute-start(bf16[384,128]{1,0:T(8,128)(2,1)S(1)} %get-tuple-element.116), channel_id=1, source_target_pairs={{0,16},{4,20},{8,24},{12,28},{16,0},{20,4},{24,8},{28,12},{1,17},{... | collective-permute-start | bytes 294920 | tf_op jit(solution)/shard_map/ppermute | solution.py:483
  68.0 7.9 %collective-permute-start.14 = (bf16[384,128]{1,0:T(8,128)(2,1)S(1)}, bf16[384,128]{1,0:T(8,128)(2,1)S(1)}, u32[]{:S(2)}, u32[]{:S(2)}) collective-permute-start(bf16[384,128]{1,0:T(8,128)(2,1)S(1)} %get-tuple-element.117), channel_id=1, source_target_pairs={{0,12},{4,8},{8,4},{12,0},{16,28},{20,24},{24,20},{28,16},{1,13},{... | collective-permute-start | bytes 294920 | tf_op jit(solution)/shard_map/ppermute | solution.py:483
  70.0 6.3 %collective-permute-start.15 = (bf16[384,128]{1,0:T(8,128)(2,1)S(1)}, bf16[384,128]{1,0:T(8,128)(2,1)S(1)}, u32[]{:S(2)}, u32[]{:S(2)}) collective-permute-start(bf16[384,128]{1,0:T(8,128)(2,1)S(1)} %get-tuple-element.118), channel_id=1, source_target_pairs={{0,20},{4,16},{8,28},{12,24},{16,4},{20,0},{24,12},{28,8},{1,21},{... | collective-permute-start | bytes 294920 | tf_op jit(solution)/shard_map/ppermute | solution.py:483
  72.7 3.6 %collective-permute-start.16 = (bf16[384,128]{1,0:T(8,128)(2,1)S(1)}, bf16[384,128]{1,0:T(8,128)(2,1)S(1)}, u32[]{:S(2)}, u32[]{:S(2)}) collective-permute-start(bf16[384,128]{1,0:T(8,128)(2,1)S(1)} %get-tuple-element.120), channel_id=1, source_target_pairs={{0,4},{4,0},{8,12},{12,8},{16,20},{20,16},{24,28},{28,24},{1,5},{5... | collective-permute-start | bytes 294920 | tf_op jit(solution)/shard_map/ppermute | solution.py:483
  87.6 10.9 %collective-permute-start.22 = (bf16[1152,128]{1,0:T(8,128)(2,1)S(1)}, bf16[1152,128]{1,0:T(8,128)(2,1)S(1)}, u32[]{:S(2)}, u32[]{:S(2)}) collective-permute-start(bf16[1152,128]{1,0:T(8,128)(2,1)S(1)} %get-tuple-element.129), channel_id=1, source_target_pairs={{0,24},{4,28},{8,16},{12,20},{16,8},{20,12},{24,0},{28,4},{1,25},{... | collective-permute-start | bytes 884744 | tf_op jit(solution)/shard_map/ppermute | solution.py:483
  89.9 13.7 %collective-permute-start.23 = (bf16[1152,128]{1,0:T(8,128)(2,1)S(1)}, bf16[1152,128]{1,0:T(8,128)(2,1)S(1)}, u32[]{:S(2)}, u32[]{:S(2)}) collective-permute-start(bf16[1152,128]{1,0:T(8,128)(2,1)S(1)} %get-tuple-element.130), channel_id=1, source_target_pairs={{0,28},{4,24},{8,20},{12,16},{16,12},{20,8},{24,4},{28,0},{1,29},{... | collective-permute-start | bytes 884744 | tf_op jit(solution)/shard_map/ppermute | solution.py:483
  90.3 20.4 %collective-permute-start.17 = (bf16[1152,128]{1,0:T(8,128)(2,1)S(1)}, bf16[1152,128]{1,0:T(8,128)(2,1)S(1)}, u32[]{:S(2)}, u32[]{:S(2)}) collective-permute-start(bf16[1152,128]{1,0:T(8,128)(2,1)S(1)} %get-tuple-element.124), channel_id=1, source_target_pairs={{0,8},{4,12},{8,0},{12,4},{16,24},{20,28},{24,16},{28,20},{1,9},{5... | collective-permute-start | bytes 884744 | tf_op jit(solution)/shard_map/ppermute | solution.py:483
  91.7 19.0 %collective-permute-start.18 = (bf16[1152,128]{1,0:T(8,128)(2,1)S(1)}, bf16[1152,128]{1,0:T(8,128)(2,1)S(1)}, u32[]{:S(2)}, u32[]{:S(2)}) collective-permute-start(bf16[1152,128]{1,0:T(8,128)(2,1)S(1)} %get-tuple-element.125), channel_id=1, source_target_pairs={{0,16},{4,20},{8,24},{12,28},{16,0},{20,4},{24,8},{28,12},{1,17},{... | collective-permute-start | bytes 884744 | tf_op jit(solution)/shard_map/ppermute | solution.py:483
  93.2 22.2 %collective-permute-start.19 = (bf16[1152,128]{1,0:T(8,128)(2,1)S(1)}, bf16[1152,128]{1,0:T(8,128)(2,1)S(1)}, u32[]{:S(2)}, u32[]{:S(2)}) collective-permute-start(bf16[1152,128]{1,0:T(8,128)(2,1)S(1)} %get-tuple-element.126), channel_id=1, source_target_pairs={{0,12},{4,8},{8,4},{12,0},{16,28},{20,24},{24,20},{28,16},{1,13},{... | collective-permute-start | bytes 884744 | tf_op jit(solution)/shard_map/ppermute | solution.py:483
  98.5 17.9 %collective-permute-start.20 = (bf16[1152,128]{1,0:T(8,128)(2,1)S(1)}, bf16[1152,128]{1,0:T(8,128)(2,1)S(1)}, u32[]{:S(2)}, u32[]{:S(2)}) collective-permute-start(bf16[1152,128]{1,0:T(8,128)(2,1)S(1)} %get-tuple-element.127), channel_id=1, source_target_pairs={{0,20},{4,16},{8,28},{12,24},{16,4},{20,0},{24,12},{28,8},{1,21},{... | collective-permute-start | bytes 884744 | tf_op jit(solution)/shard_map/ppermute | solution.py:483
  103.6 12.8 %collective-permute-start.21 = (bf16[1152,128]{1,0:T(8,128)(2,1)S(1)}, bf16[1152,128]{1,0:T(8,128)(2,1)S(1)}, u32[]{:S(2)}, u32[]{:S(2)}) collective-permute-start(bf16[1152,128]{1,0:T(8,128)(2,1)S(1)} %get-tuple-element.128), channel_id=1, source_target_pairs={{0,4},{4,0},{8,12},{12,8},{16,20},{20,16},{24,28},{28,24},{1,5},{5... | collective-permute-start | bytes 884744 | tf_op jit(solution)/shard_map/ppermute | solution.py:483

commit v20 on v19

--- a/solution.py
+++ b/solution.py
@@ -191,7 +191,7 @@
         plan_k[count + spare] = total // bk - 1
 
 
-def pipelined(plan_q, plan_k, count_ref, early, late, buffers):
+def pipelined(plan_q, plan_k, count_ref, early, late, buffers, diagonals=True):
     early(0, plan_q[0], plan_k[0], buffers[0], True)
 
     def turns(base, count, diagonal):
@@ -211,8 +211,11 @@
         def _(i):
             turns(i, 1, diagonal)
 
-    run(0, count_ref[0], False)
-    run(count_ref[0], count_ref[1], True)
+    if diagonals:
+        run(0, count_ref[0], False)
+        run(count_ref[0], count_ref[1], True)
+    else:
+        run(0, count_ref[1], False)
 
 
 def forward_kernel(peers, heads, rows, bq, bk, kept, me_s, *refs):
@@ -346,7 +349,7 @@
         dk_acc[keys, :] += dot32(ds_ref[...], qx_ref[queries, :HD])
         dq_acc[:, queries] += dot32(kt_ref[:, keys], ds_ref[...])
 
-    pipelined(plan_q, plan_k, count_ref, early, late, ((p0, ds0), (p1, ds1)))
+    pipelined(plan_q, plan_k, count_ref, early, late, ((p0, ds0), (p1, ds1)), diagonals=not kept)
 
 
 def prepare_kernel(bq, bk, plan_q, count_ref, log_ref, top_list, p_list, p_out, *totals):

time: 118 us -> 118 us (level)
  no operation moved by 1% of the time
where the time goes in v20:
time: 118 us
  waiting for transfers between devices  51.5 us (44%)
  Pallas kernels  37 us (31%)
  starting transfers between devices  23.5 us (20%)
  local copies, waits for them, and re-layouts  4.56 us (4%)
    ppermute x21, waiting for transfers between devices, exchange(): lax.ppermute(x, 'seq', [(i, i ^ d) for i in range(peers)])  43.6 us
    ppermute x21, starting transfers between devices, exchange(): lax.ppermute(x, 'seq', [(i, i ^ d) for i in range(peers)])  18.8 us
    pallas_call x1, Pallas kernels, attention_forward(): pl.pallas_call(functools.partial(forward_kernel, peers, heads, rows, bq,...  13.4 us
    pallas_call x1, Pallas kernels, attention_backward(): pl.pallas_call(functools.partial(backward_kernel, listed, heads, rows, bq...  10.8 us
    ppermute x3, waiting for transfers between devices, pass_on(): lax.ppermute(x, 'head', [(i, (i + 1) % groups) for i in range(groups)])  7.9 us
    ppermute x3, starting transfers between devices, pass_on(): lax.ppermute(x, 'head', [(i, (i + 1) % groups) for i in range(groups)])  4.66 us
    dynamic_slice x1, local copies, waits for them, and re-layouts, per_device(): lax.dynamic_slice_in_dim(out_weight, block * width, width, 1)  4.54 us
    pallas_call x1, Pallas kernels, pack_heads(): pl.pallas_call(functools.partial(pack_kernel, heads, rows), in_specs=[SME...  3.62 us
  transfers between devices with their start and end apart: 24, of which 15 were waited for; matrix products, arithmetic and copies ran while one was open for 4% of the time, Pallas kernels for 20%

profile of v20, /device:TPU:0, one launch (start us, length us, event | category | flops | bytes accessed | tf_op | source)
XLA Modules:
  0.0 117.5 jit_solution(15733287049429050177)
XLA Ops:
  0.6 3.1 %collective-permute-start = (bf16[384,1024]{1,0:T(8,128)(2,1)}, bf16[384,1024]{1,0:T(8,128)(2,1)S(1)}, u32[]{:S(2)}, u32[]{:S(2)}) collective-permute-start(bf16[384,1024]{1,0:T(8,128)(2,1)} %o_ref.1), channel_id=1, source_target_pairs={{0,1},{1,2},{2,3},{3,0},{4,5},{5,6},{6,7},{7,4},{8,9},{9,10},{10,1... | collective-permute-start | bytes 2359304 | tf_op jit(solution)/shard_map/ppermute | solution.py:489
  3.7 3.6 %shard_map.85 = (bf16[1168,128]{1,0:T(8,128)(2,1)}, bf16[1168,128]{1,0:T(8,128)(2,1)}, bf16[1168,128]{1,0:T(8,128)(2,1)}, bf16[1168,128]{1,0:T(8,128)(2,1)}, bf1...) custom-call(s32[1]{0:T(128)} %bitcast.me_s, ...), custom_call_target="tpu_custom_call" | custom-call | tf_op jit(solution)/shard_map/pallas_call | solution.py:64
  7.3 1.5 %collective-permute-start.1 = (bf16[1168,128]{1,0:T(8,128)(2,1)}, bf16[1168,128]{1,0:T(8,128)(2,1)S(1)}, u32[]{:S(2)}, u32[]{:S(2)}) collective-permute-start(bf16[1168,128]{1,0:T(8,128)(2,1)} %get-tuple-element.70), channel_id=1, source_target_pairs={{0,8},{4,12},{8,0},{12,4},{16,24},{20,28},{24,16},{28,20},{1,9},{5... | collective-permute-start | bytes 897032 | tf_op jit(solution)/shard_map/ppermute | solution.py:486
  8.8 1.5 %collective-permute-start.2 = (bf16[1168,128]{1,0:T(8,128)(2,1)}, bf16[1168,128]{1,0:T(8,128)(2,1)S(1)}, u32[]{:S(2)}, u32[]{:S(2)}) collective-permute-start(bf16[1168,128]{1,0:T(8,128)(2,1)} %get-tuple-element.71), channel_id=1, source_target_pairs={{0,16},{4,20},{8,24},{12,28},{16,0},{20,4},{24,8},{28,12},{1,17},{... | collective-permute-start | bytes 897032 | tf_op jit(solution)/shard_map/ppermute | solution.py:486
  10.3 0.5 collective-permute-start.3
  10.8 4.5 %constant_dynamic-slice_fusion = (bf16[1024,1024]{1,0:T(8,128)(2,1)S(1)}, bf16[1024,1024]{1,0:T(8,128)(2,1)S(1)}, bf16[1024,1024]{1,0:T(8,128)(2,1)S(1)}, bf16[1024,1024]{1,0:T(8,128)(2,1)S(1)}) fusion(bf16[1024,4096]{1,0:T(8,128)(2,1)} %param.10, s32[]{:T(128)S(6)} %select_n.15, s32[]{:T(128)S(6)} %select_n.13, s32[]{:T(128)S(6)} %select_n.12, s32[]{:T(128)S(6)} %select_n.14), kind=kLoop, calls=%fused_computation | loop fusion | bytes 16777232 | tf_op jit(solution)/shard_map/dynamic_slice | solution.py:510
  15.4 0.0 copy-start.2
  15.4 1.0 shard_map.86.refs_0_
  16.4 1.1 collective-permute-done.1.refs_2_
  17.6 6.2 %collective-permute-done.2.refs_4_ = bf16[1168,128]{1,0:T(8,128)(2,1)S(1)} collective-permute-done((bf16[1168,128]{1,0:T(8,128)(2,1)}, bf16[1168,128]{1,0:T(8,128)(2,1)S(1)}, u32[]{:S(2)}, u32[]{:S(2)}) %collective-permute-start.2) | collective-permute-done | bytes 299040 | tf_op jit(solution)/shard_map/ppermute | solution.py:486
  23.7 1.6 %collective-permute-start.4 = (bf16[384,1024]{1,0:T(8,128)(2,1)S(1)}, bf16[384,1024]{1,0:T(8,128)(2,1)S(1)}, u32[]{:S(2)}, u32[]{:S(2)}) collective-permute-start(bf16[384,1024]{1,0:T(8,128)(2,1)S(1)} %collective-permute-done.o_ref), channel_id=1, source_target_pairs={{0,1},{1,2},{2,3},{3,0},{4,5},{5,6},{6,7},{7,4},{8,9},{9,10},{10,1... | collective-permute-start | bytes 2359304 | tf_op jit(solution)/shard_map/ppermute | solution.py:489
  25.3 2.4 %collective-permute-start.6 = (bf16[1168,128]{1,0:T(8,128)(2,1)S(1)}, bf16[1168,128]{1,0:T(8,128)(2,1)S(1)}, u32[]{:S(2)}, u32[]{:S(2)}) collective-permute-start(bf16[1168,128]{1,0:T(8,128)(2,1)S(1)} %copy-done.4), channel_id=1, source_target_pairs={{0,20},{4,16},{8,28},{12,24},{16,4},{20,0},{24,12},{28,8},{1,21},{... | collective-permute-start | bytes 897032 | tf_op jit(solution)/shard_map/ppermute | solution.py:486
  27.7 0.4 collective-permute-start.7
  28.1 0.6 collective-permute-start.8
  28.6 1.0 shard_map.87.refs_0_
  29.7 6.0 %collective-permute-done.5.refs_7_ = bf16[1168,128]{1,0:T(8,128)(2,1)S(1)} collective-permute-done((bf16[1168,128]{1,0:T(8,128)(2,1)S(1)}, bf16[1168,128]{1,0:T(8,128)(2,1)S(1)}, u32[]{:S(2)}, u32[]{:S(2)}) %collective-permute-start.5) | collective-permute-done | bytes 299040 | tf_op jit(solution)/shard_map/ppermute | solution.py:486
  35.6 5.4 %collective-permute-done.6.refs_5_ = bf16[1168,128]{1,0:T(8,128)(2,1)S(1)} collective-permute-done((bf16[1168,128]{1,0:T(8,128)(2,1)S(1)}, bf16[1168,128]{1,0:T(8,128)(2,1)S(1)}, u32[]{:S(2)}, u32[]{:S(2)}) %collective-permute-start.6) | collective-permute-done | bytes 299040 | tf_op jit(solution)/shard_map/ppermute | solution.py:486
  41.1 3.0 %collective-permute-done.4.o_ref = bf16[384,1024]{1,0:T(8,128)(2,1)S(1)} collective-permute-done((bf16[384,1024]{1,0:T(8,128)(2,1)S(1)}, bf16[384,1024]{1,0:T(8,128)(2,1)S(1)}, u32[]{:S(2)}, u32[]{:S(2)}) %collective-permute-start.4) | collective-permute-done | bytes 786464 | tf_op jit(solution)/shard_map/ppermute | solution.py:489
  44.0 13.4 %shard_map.88 = (bf16[3072,128]{1,0:T(8,128)(2,1)S(1)}, bf16[3072,256]{1,0:T(8,128)(2,1)S(1)}, bf16[3072,256]{1,0:T(8,128)(2,1)S(1)}, bf16[128,3072]{1,0:T(8,128...) custom-call(s32[1]{0:T(128)} %bitcast.me_s, ...), custom_call_target="tpu_custom_call" | custom-call | flops 1811939328 | bytes 6291456 | tf_op jit(solution)/shard_map/pallas_call | solution.py:426
  57.4 1.0 shard_map.89.acc_ref
  58.4 4.9 %collective-permute-done.9.o_ref = bf16[384,1024]{1,0:T(8,128)(2,1)S(1)} collective-permute-done((bf16[384,1024]{1,0:T(8,128)(2,1)S(1)}, bf16[384,1024]{1,0:T(8,128)(2,1)S(1)}, u32[]{:S(2)}, u32[]{:S(2)}) %collective-permute-start.9) | collective-permute-done | bytes 786464 | tf_op jit(solution)/shard_map/ppermute | solution.py:489
  63.4 1.0 shard_map.90
  64.4 2.3 %collective-permute-start.10 = (bf16[384,128]{1,0:T(8,128)(2,1)S(1)}, bf16[384,128]{1,0:T(8,128)(2,1)S(1)}, u32[]{:S(2)}, u32[]{:S(2)}) collective-permute-start(bf16[384,128]{1,0:T(8,128)(2,1)S(1)} %get-tuple-element.107), channel_id=1, source_target_pairs={{0,24},{4,28},{8,16},{12,20},{16,8},{20,12},{24,0},{28,4},{1,25},{... | collective-permute-start | bytes 294920 | tf_op jit(solution)/shard_map/ppermute | solution.py:486
  66.7 0.3 collective-permute-start.12
  67.0 1.0 collective-permute-start.13
  68.0 1.7 %collective-permute-start.14 = (bf16[384,128]{1,0:T(8,128)(2,1)S(1)}, bf16[384,128]{1,0:T(8,128)(2,1)S(1)}, u32[]{:S(2)}, u32[]{:S(2)}) collective-permute-start(bf16[384,128]{1,0:T(8,128)(2,1)S(1)} %get-tuple-element.117), channel_id=1, source_target_pairs={{0,12},{4,8},{8,4},{12,0},{16,28},{20,24},{24,20},{28,16},{1,13},{... | collective-permute-start | bytes 294920 | tf_op jit(solution)/shard_map/ppermute | solution.py:486
  69.6 0.4 collective-permute-done.10.refs_4_
  70.0 0.5 collective-permute-start.15
  70.5 2.3 %collective-permute-done.11.refs_5_ = bf16[384,128]{1,0:T(8,128)(2,1)S(1)} collective-permute-done((bf16[384,128]{1,0:T(8,128)(2,1)S(1)}, bf16[384,128]{1,0:T(8,128)(2,1)S(1)}, u32[]{:S(2)}, u32[]{:S(2)}) %collective-permute-start.11) | collective-permute-done | bytes 98336 | tf_op jit(solution)/shard_map/ppermute | solution.py:486
  72.7 2.5 %shard_map.91 = (bf16[80,256,256]{2,1,0:T(8,128)(2,1)S(1)}, f32[128,3072]{1,0:T(8,128)S(1)}, f32[3072,128]{1,0:T(8,128)S(1)}, f32[3072,128]{1,0:T(8,128)S(1)}) custom-call(s32[80]{0:T(128)S(1)} %get-tuple-element.90.plan_q, s32[2]{0:T(128)S(1)} %get-tuple-element.92.count_ref, ...), custom_call_target="tpu_custom_call", output_to_operand_aliasing={{0}: (4, {})} | custom-call | tf_op jit(solution)/shard_map/pallas_call | solution.py:445
  75.2 0.7 collective-permute-done.14.refs_8_
  75.9 0.4 collective-permute-done.15.refs_9_
  76.3 10.8 %shard_map.92 = (f32[128,3072]{1,0:T(8,128)S(1)}, f32[3072,128]{1,0:T(8,128)S(1)}, f32[3072,128]{1,0:T(8,128)S(1)}) custom-call(s32[1]{0:T(128)} %bitcast.me_s, s32[80]{0:T(128)S(1)} %get-tuple-element.90.plan_q, s32[80]{0:T(128)S(1)} %get-tuple-element.91.plan_k, ...), custom_call_target="tpu_custom_call", output_to_operand_aliasing={{0}: (11, {}), {1}: (12, {}), {2}: (13, {})} | custom-call | flops 3019898880 | bytes 6291456 | tf_op jit(solution)/shard_map/pallas_call | solution.py:467
  87.1 0.2 shard_map.94
  87.3 2.3 %collective-permute-start.22 = (bf16[1152,128]{1,0:T(8,128)(2,1)S(1)}, bf16[1152,128]{1,0:T(8,128)(2,1)S(1)}, u32[]{:S(2)}, u32[]{:S(2)}) collective-permute-start(bf16[1152,128]{1,0:T(8,128)(2,1)S(1)} %get-tuple-element.129), channel_id=1, source_target_pairs={{0,24},{4,28},{8,16},{12,20},{16,8},{20,12},{24,0},{28,4},{1,25},{... | collective-permute-start | bytes 884744 | tf_op jit(solution)/shard_map/ppermute | solution.py:486
  89.5 0.1 collective-permute-start.23
  89.7 0.3 shard_map.93
  90.0 1.3 %collective-permute-start.17 = (bf16[1152,128]{1,0:T(8,128)(2,1)S(1)}, bf16[1152,128]{1,0:T(8,128)(2,1)S(1)}, u32[]{:S(2)}, u32[]{:S(2)}) collective-permute-start(bf16[1152,128]{1,0:T(8,128)(2,1)S(1)} %get-tuple-element.124), channel_id=1, source_target_pairs={{0,8},{4,12},{8,0},{12,4},{16,24},{20,28},{24,16},{28,20},{1,9},{5... | collective-permute-start | bytes 884744 | tf_op jit(solution)/shard_map/ppermute | solution.py:486
  91.3 1.5 %collective-permute-start.18 = (bf16[1152,128]{1,0:T(8,128)(2,1)S(1)}, bf16[1152,128]{1,0:T(8,128)(2,1)S(1)}, u32[]{:S(2)}, u32[]{:S(2)}) collective-permute-start(bf16[1152,128]{1,0:T(8,128)(2,1)S(1)} %get-tuple-element.125), channel_id=1, source_target_pairs={{0,16},{4,20},{8,24},{12,28},{16,0},{20,4},{24,8},{28,12},{1,17},{... | collective-permute-start | bytes 884744 | tf_op jit(solution)/shard_map/ppermute | solution.py:486
  92.9 0.1 collective-permute-start.19
  93.0 5.2 %collective-permute-done.22.refs_0_ = bf16[1152,128]{1,0:T(8,128)(2,1)S(1)} collective-permute-done((bf16[1152,128]{1,0:T(8,128)(2,1)S(1)}, bf16[1152,128]{1,0:T(8,128)(2,1)S(1)}, u32[]{:S(2)}, u32[]{:S(2)}) %collective-permute-start.22) | collective-permute-done | bytes 294944 | tf_op jit(solution)/shard_map/ppermute | solution.py:486
  98.2 5.1 %collective-permute-done.23.refs_1_ = bf16[1152,128]{1,0:T(8,128)(2,1)S(1)} collective-permute-done((bf16[1152,128]{1,0:T(8,128)(2,1)S(1)}, bf16[1152,128]{1,0:T(8,128)(2,1)S(1)}, u32[]{:S(2)}, u32[]{:S(2)}) %collective-permute-start.23) | collective-permute-done | bytes 294944 | tf_op jit(solution)/shard_map/ppermute | solution.py:486
  103.3 1.0 collective-permute-start.21
  104.3 1.0 shard_map.95
  105.3 5.1 %collective-permute-done.17.refs_0_ = bf16[1152,128]{1,0:T(8,128)(2,1)S(1)} collective-permute-done((bf16[1152,128]{1,0:T(8,128)(2,1)S(1)}, bf16[1152,128]{1,0:T(8,128)(2,1)S(1)}, u32[]{:S(2)}, u32[]{:S(2)}) %collective-permute-start.17) | collective-permute-done | bytes 294944 | tf_op jit(solution)/shard_map/ppermute | solution.py:486
  110.4 4.7 %collective-permute-done.19.refs_2_ = bf16[1152,128]{1,0:T(8,128)(2,1)S(1)} collective-permute-done((bf16[1152,128]{1,0:T(8,128)(2,1)S(1)}, bf16[1152,128]{1,0:T(8,128)(2,1)S(1)}, u32[]{:S(2)}, u32[]{:S(2)}) %collective-permute-start.19) | collective-permute-done | bytes 294944 | tf_op jit(solution)/shard_map/ppermute | solution.py:486
  115.1 1.0 collective-permute-done.20.refs_3_
  116.1 1.2 %shard_map.96 = (bf16[384,1024]{1,0:T(8,128)(2,1)}, bf16[384,1024]{1,0:T(8,128)(2,1)}, bf16[384,1024]{1,0:T(8,128)(2,1)}) custom-call(s32[1]{0:T(128)} %bitcast.me_s, bf16[1152,128]{1,0:T(8,128)(2,1)S(1)} %collective-permute-done.17.refs_0_, ...), custom_call_target="tpu_custom_call", output_to_operand_aliasing={{0}: (6, {}), {1}: (7, {}), {2}: (8, {})} | custom-call | tf_op jit(solution)/shard_map/pallas_call | solution.py:89
  (25 shorter events, 0.1 us)
Async XLA Ops:
  0.6 23.1 %collective-permute-start = (bf16[384,1024]{1,0:T(8,128)(2,1)}, bf16[384,1024]{1,0:T(8,128)(2,1)S(1)}, u32[]{:S(2)}, u32[]{:S(2)}) collective-permute-start(bf16[384,1024]{1,0:T(8,128)(2,1)} %o_ref.1), channel_id=1, source_target_pairs={{0,1},{1,2},{2,3},{3,0},{4,5},{5,6},{6,7},{7,4},{8,9},{9,10},{10,1... | collective-permute-start | bytes 2359304 | tf_op jit(solution)/shard_map/ppermute | solution.py:489
  7.3 10.2 %collective-permute-start.1 = (bf16[1168,128]{1,0:T(8,128)(2,1)}, bf16[1168,128]{1,0:T(8,128)(2,1)S(1)}, u32[]{:S(2)}, u32[]{:S(2)}) collective-permute-start(bf16[1168,128]{1,0:T(8,128)(2,1)} %get-tuple-element.70), channel_id=1, source_target_pairs={{0,8},{4,12},{8,0},{12,4},{16,24},{20,28},{24,16},{28,20},{1,9},{5... | collective-permute-start | bytes 897032 | tf_op jit(solution)/shard_map/ppermute | solution.py:486
  8.8 14.9 %collective-permute-start.2 = (bf16[1168,128]{1,0:T(8,128)(2,1)}, bf16[1168,128]{1,0:T(8,128)(2,1)S(1)}, u32[]{:S(2)}, u32[]{:S(2)}) collective-permute-start(bf16[1168,128]{1,0:T(8,128)(2,1)} %get-tuple-element.71), channel_id=1, source_target_pairs={{0,16},{4,20},{8,24},{12,28},{16,0},{20,4},{24,8},{28,12},{1,17},{... | collective-permute-start | bytes 897032 | tf_op jit(solution)/shard_map/ppermute | solution.py:486
  10.3 13.4 %collective-permute-start.3 = (bf16[1168,128]{1,0:T(8,128)(2,1)}, bf16[1168,128]{1,0:T(8,128)(2,1)S(1)}, u32[]{:S(2)}, u32[]{:S(2)}) collective-permute-start(bf16[1168,128]{1,0:T(8,128)(2,1)} %get-tuple-element.72), channel_id=1, source_target_pairs={{0,24},{4,28},{8,16},{12,20},{16,8},{20,12},{24,0},{28,4},{1,25},{... | collective-permute-start | bytes 897032 | tf_op jit(solution)/shard_map/ppermute | solution.py:486
  10.8 4.5 %copy-start = (bf16[384,1024]{1,0:T(8,128)(2,1)S(1)}, bf16[384,1024]{1,0:T(8,128)(2,1)}, u32[]{:S(2)}) copy-start(bf16[384,1024]{1,0:T(8,128)(2,1)} %o_ref.1) | copy-start | bytes 2359300
  15.4 9.9 %copy-start.5 = (bf16[1168,128]{1,0:T(8,128)(2,1)S(1)}, bf16[1168,128]{1,0:T(8,128)(2,1)}, u32[]{:S(2)}) copy-start(bf16[1168,128]{1,0:T(8,128)(2,1)} %get-tuple-element.75) | copy-start | bytes 897028
  15.4 9.9 %copy-start.4 = (bf16[1168,128]{1,0:T(8,128)(2,1)S(1)}, bf16[1168,128]{1,0:T(8,128)(2,1)}, u32[]{:S(2)}) copy-start(bf16[1168,128]{1,0:T(8,128)(2,1)} %get-tuple-element.76) | copy-start | bytes 897028
  15.4 12.3 %copy-start.3 = (bf16[1168,128]{1,0:T(8,128)(2,1)S(1)}, bf16[1168,128]{1,0:T(8,128)(2,1)}, u32[]{:S(2)}) copy-start(bf16[1168,128]{1,0:T(8,128)(2,1)} %get-tuple-element.77) | copy-start | bytes 897028
  15.4 12.7 %copy-start.2 = (bf16[1168,128]{1,0:T(8,128)(2,1)S(1)}, bf16[1168,128]{1,0:T(8,128)(2,1)}, u32[]{:S(2)}) copy-start(bf16[1168,128]{1,0:T(8,128)(2,1)} %get-tuple-element.78) | copy-start | bytes 897028
  23.7 20.3 %collective-permute-start.4 = (bf16[384,1024]{1,0:T(8,128)(2,1)S(1)}, bf16[384,1024]{1,0:T(8,128)(2,1)S(1)}, u32[]{:S(2)}, u32[]{:S(2)}) collective-permute-start(bf16[384,1024]{1,0:T(8,128)(2,1)S(1)} %collective-permute-done.o_ref), channel_id=1, source_target_pairs={{0,1},{1,2},{2,3},{3,0},{4,5},{5,6},{6,7},{7,4},{8,9},{9,10},{10,1... | collective-permute-start | bytes 2359304 | tf_op jit(solution)/shard_map/ppermute | solution.py:489
  25.3 10.3 %collective-permute-start.5 = (bf16[1168,128]{1,0:T(8,128)(2,1)S(1)}, bf16[1168,128]{1,0:T(8,128)(2,1)S(1)}, u32[]{:S(2)}, u32[]{:S(2)}) collective-permute-start(bf16[1168,128]{1,0:T(8,128)(2,1)S(1)} %copy-done.5), channel_id=1, source_target_pairs={{0,28},{4,24},{8,20},{12,16},{16,12},{20,8},{24,4},{28,0},{1,29},{... | collective-permute-start | bytes 897032 | tf_op jit(solution)/shard_map/ppermute | solution.py:486
  25.3 15.7 %collective-permute-start.6 = (bf16[1168,128]{1,0:T(8,128)(2,1)S(1)}, bf16[1168,128]{1,0:T(8,128)(2,1)S(1)}, u32[]{:S(2)}, u32[]{:S(2)}) collective-permute-start(bf16[1168,128]{1,0:T(8,128)(2,1)S(1)} %copy-done.4), channel_id=1, source_target_pairs={{0,20},{4,16},{8,28},{12,24},{16,4},{20,0},{24,12},{28,8},{1,21},{... | collective-permute-start | bytes 897032 | tf_op jit(solution)/shard_map/ppermute | solution.py:486
  27.7 13.3 %collective-permute-start.7 = (bf16[1168,128]{1,0:T(8,128)(2,1)S(1)}, bf16[1168,128]{1,0:T(8,128)(2,1)S(1)}, u32[]{:S(2)}, u32[]{:S(2)}) collective-permute-start(bf16[1168,128]{1,0:T(8,128)(2,1)S(1)} %copy-done.3), channel_id=1, source_target_pairs={{0,12},{4,8},{8,4},{12,0},{16,28},{20,24},{24,20},{28,16},{1,13},{... | collective-permute-start | bytes 897032 | tf_op jit(solution)/shard_map/ppermute | solution.py:486
  28.1 13.0 %collective-permute-start.8 = (bf16[1168,128]{1,0:T(8,128)(2,1)S(1)}, bf16[1168,128]{1,0:T(8,128)(2,1)S(1)}, u32[]{:S(2)}, u32[]{:S(2)}) collective-permute-start(bf16[1168,128]{1,0:T(8,128)(2,1)S(1)} %copy-done.2), channel_id=1, source_target_pairs={{0,4},{4,0},{8,12},{12,8},{16,20},{20,16},{24,28},{28,24},{1,5},{5... | collective-permute-start | bytes 897032 | tf_op jit(solution)/shard_map/ppermute | solution.py:486
  28.6 15.4 %copy-start.1 = (bf16[1168,128]{1,0:T(8,128)(2,1)S(1)}, bf16[1168,128]{1,0:T(8,128)(2,1)}, u32[]{:S(2)}) copy-start(bf16[1168,128]{1,0:T(8,128)(2,1)} %get-tuple-element.82.refs_0_) | copy-start | bytes 897028
  44.0 19.4 %collective-permute-start.9 = (bf16[384,1024]{1,0:T(8,128)(2,1)S(1)}, bf16[384,1024]{1,0:T(8,128)(2,1)S(1)}, u32[]{:S(2)}, u32[]{:S(2)}) collective-permute-start(bf16[384,1024]{1,0:T(8,128)(2,1)S(1)} %collective-permute-done.4.o_ref), channel_id=1, source_target_pairs={{0,1},{1,2},{2,3},{3,0},{4,5},{5,6},{6,7},{7,4},{8,9},{9,10},{10,1... | collective-permute-start | bytes 2359304 | tf_op jit(solution)/shard_map/ppermute | solution.py:489
  64.4 5.6 %collective-permute-start.10 = (bf16[384,128]{1,0:T(8,128)(2,1)S(1)}, bf16[384,128]{1,0:T(8,128)(2,1)S(1)}, u32[]{:S(2)}, u32[]{:S(2)}) collective-permute-start(bf16[384,128]{1,0:T(8,128)(2,1)S(1)} %get-tuple-element.107), channel_id=1, source_target_pairs={{0,24},{4,28},{8,16},{12,20},{16,8},{20,12},{24,0},{28,4},{1,25},{... | collective-permute-start | bytes 294920 | tf_op jit(solution)/shard_map/ppermute | solution.py:486
  66.7 6.1 %collective-permute-start.11 = (bf16[384,128]{1,0:T(8,128)(2,1)S(1)}, bf16[384,128]{1,0:T(8,128)(2,1)S(1)}, u32[]{:S(2)}, u32[]{:S(2)}) collective-permute-start(bf16[384,128]{1,0:T(8,128)(2,1)S(1)} %get-tuple-element.114), channel_id=1, source_target_pairs={{0,28},{4,24},{8,20},{12,16},{16,12},{20,8},{24,4},{28,0},{1,29},{... | collective-permute-start | bytes 294920 | tf_op jit(solution)/shard_map/ppermute | solution.py:486
  66.7 8.5 %collective-permute-start.12 = (bf16[384,128]{1,0:T(8,128)(2,1)S(1)}, bf16[384,128]{1,0:T(8,128)(2,1)S(1)}, u32[]{:S(2)}, u32[]{:S(2)}) collective-permute-start(bf16[384,128]{1,0:T(8,128)(2,1)S(1)} %get-tuple-element.115), channel_id=1, source_target_pairs={{0,8},{4,12},{8,0},{12,4},{16,24},{20,28},{24,16},{28,20},{1,9},{5... | collective-permute-start | bytes 294920 | tf_op jit(solution)/shard_map/ppermute | solution.py:486
  67.0 8.3 %collective-permute-start.13 = (bf16[384,128]{1,0:T(8,128)(2,1)S(1)}, bf16[384,128]{1,0:T(8,128)(2,1)S(1)}, u32[]{:S(2)}, u32[]{:S(2)}) collective-permute-start(bf16[384,128]{1,0:T(8,128)(2,1)S(1)} %get-tuple-element.116), channel_id=1, source_target_pairs={{0,16},{4,20},{8,24},{12,28},{16,0},{20,4},{24,8},{28,12},{1,17},{... | collective-permute-start | bytes 294920 | tf_op jit(solution)/shard_map/ppermute | solution.py:486
  68.0 7.9 %collective-permute-start.14 = (bf16[384,128]{1,0:T(8,128)(2,1)S(1)}, bf16[384,128]{1,0:T(8,128)(2,1)S(1)}, u32[]{:S(2)}, u32[]{:S(2)}) collective-permute-start(bf16[384,128]{1,0:T(8,128)(2,1)S(1)} %get-tuple-element.117), channel_id=1, source_target_pairs={{0,12},{4,8},{8,4},{12,0},{16,28},{20,24},{24,20},{28,16},{1,13},{... | collective-permute-start | bytes 294920 | tf_op jit(solution)/shard_map/ppermute | solution.py:486
  70.0 6.3 %collective-permute-start.15 = (bf16[384,128]{1,0:T(8,128)(2,1)S(1)}, bf16[384,128]{1,0:T(8,128)(2,1)S(1)}, u32[]{:S(2)}, u32[]{:S(2)}) collective-permute-start(bf16[384,128]{1,0:T(8,128)(2,1)S(1)} %get-tuple-element.118), channel_id=1, source_target_pairs={{0,20},{4,16},{8,28},{12,24},{16,4},{20,0},{24,12},{28,8},{1,21},{... | collective-permute-start | bytes 294920 | tf_op jit(solution)/shard_map/ppermute | solution.py:486
  72.7 3.6 %collective-permute-start.16 = (bf16[384,128]{1,0:T(8,128)(2,1)S(1)}, bf16[384,128]{1,0:T(8,128)(2,1)S(1)}, u32[]{:S(2)}, u32[]{:S(2)}) collective-permute-start(bf16[384,128]{1,0:T(8,128)(2,1)S(1)} %get-tuple-element.120), channel_id=1, source_target_pairs={{0,4},{4,0},{8,12},{12,8},{16,20},{20,16},{24,28},{28,24},{1,5},{5... | collective-permute-start | bytes 294920 | tf_op jit(solution)/shard_map/ppermute | solution.py:486
  87.3 10.9 %collective-permute-start.22 = (bf16[1152,128]{1,0:T(8,128)(2,1)S(1)}, bf16[1152,128]{1,0:T(8,128)(2,1)S(1)}, u32[]{:S(2)}, u32[]{:S(2)}) collective-permute-start(bf16[1152,128]{1,0:T(8,128)(2,1)S(1)} %get-tuple-element.129), channel_id=1, source_target_pairs={{0,24},{4,28},{8,16},{12,20},{16,8},{20,12},{24,0},{28,4},{1,25},{... | collective-permute-start | bytes 884744 | tf_op jit(solution)/shard_map/ppermute | solution.py:486
  89.5 13.7 %collective-permute-start.23 = (bf16[1152,128]{1,0:T(8,128)(2,1)S(1)}, bf16[1152,128]{1,0:T(8,128)(2,1)S(1)}, u32[]{:S(2)}, u32[]{:S(2)}) collective-permute-start(bf16[1152,128]{1,0:T(8,128)(2,1)S(1)} %get-tuple-element.130), channel_id=1, source_target_pairs={{0,28},{4,24},{8,20},{12,16},{16,12},{20,8},{24,4},{28,0},{1,29},{... | collective-permute-start | bytes 884744 | tf_op jit(solution)/shard_map/ppermute | solution.py:486
  90.0 20.4 %collective-permute-start.17 = (bf16[1152,128]{1,0:T(8,128)(2,1)S(1)}, bf16[1152,128]{1,0:T(8,128)(2,1)S(1)}, u32[]{:S(2)}, u32[]{:S(2)}) collective-permute-start(bf16[1152,128]{1,0:T(8,128)(2,1)S(1)} %get-tuple-element.124), channel_id=1, source_target_pairs={{0,8},{4,12},{8,0},{12,4},{16,24},{20,28},{24,16},{28,20},{1,9},{5... | collective-permute-start | bytes 884744 | tf_op jit(solution)/shard_map/ppermute | solution.py:486
  91.3 19.0 %collective-permute-start.18 = (bf16[1152,128]{1,0:T(8,128)(2,1)S(1)}, bf16[1152,128]{1,0:T(8,128)(2,1)S(1)}, u32[]{:S(2)}, u32[]{:S(2)}) collective-permute-start(bf16[1152,128]{1,0:T(8,128)(2,1)S(1)} %get-tuple-element.125), channel_id=1, source_target_pairs={{0,16},{4,20},{8,24},{12,28},{16,0},{20,4},{24,8},{28,12},{1,17},{... | collective-permute-start | bytes 884744 | tf_op jit(solution)/shard_map/ppermute | solution.py:486
  92.9 22.2 %collective-permute-start.19 = (bf16[1152,128]{1,0:T(8,128)(2,1)S(1)}, bf16[1152,128]{1,0:T(8,128)(2,1)S(1)}, u32[]{:S(2)}, u32[]{:S(2)}) collective-permute-start(bf16[1152,128]{1,0:T(8,128)(2,1)S(1)} %get-tuple-element.126), channel_id=1, source_target_pairs={{0,12},{4,8},{8,4},{12,0},{16,28},{20,24},{24,20},{28,16},{1,13},{... | collective-permute-start | bytes 884744 | tf_op jit(solution)/shard_map/ppermute | solution.py:486
  98.2 17.9 %collective-permute-start.20 = (bf16[1152,128]{1,0:T(8,128)(2,1)S(1)}, bf16[1152,128]{1,0:T(8,128)(2,1)S(1)}, u32[]{:S(2)}, u32[]{:S(2)}) collective-permute-start(bf16[1152,128]{1,0:T(8,128)(2,1)S(1)} %get-tuple-element.127), channel_id=1, source_target_pairs={{0,20},{4,16},{8,28},{12,24},{16,4},{20,0},{24,12},{28,8},{1,21},{... | collective-permute-start | bytes 884744 | tf_op jit(solution)/shard_map/ppermute | solution.py:486
  103.3 12.8 %collective-permute-start.21 = (bf16[1152,128]{1,0:T(8,128)(2,1)S(1)}, bf16[1152,128]{1,0:T(8,128)(2,1)S(1)}, u32[]{:S(2)}, u32[]{:S(2)}) collective-permute-start(bf16[1152,128]{1,0:T(8,128)(2,1)S(1)} %get-tuple-element.128), channel_id=1, source_target_pairs={{0,4},{4,0},{8,12},{12,8},{16,20},{20,16},{24,28},{28,24},{1,5},{5... | collective-permute-start | bytes 884744 | tf_op jit(solution)/shard_map/ppermute | solution.py:486

commit v21 on v20

--- a/solution.py
+++ b/solution.py
@@ -13,7 +13,7 @@
 DOC_ROWS = 16
 ONES_ROWS = 16
 STRIP = 128
-LOOP_TURNS = 4
+LOOP_TURNS = 6
 NEG_LARGE = -1e30
 VMEM_SPARE = 6 * 1024 * 1024
 VMEM_MOST = 56 * 1024 * 1024

time: 118 us -> 118 us (level)
  no operation moved by 1% of the time
where the time goes in v21:
time: 118 us
  waiting for transfers between devices  52 us (44%)
  Pallas kernels  36.5 us (31%)
  starting transfers between devices  23.5 us (20%)
  local copies, waits for them, and re-layouts  4.56 us (4%)
    ppermute x21, waiting for transfers between devices, exchange(): lax.ppermute(x, 'seq', [(i, i ^ d) for i in range(peers)])  43.6 us
    ppermute x21, starting transfers between devices, exchange(): lax.ppermute(x, 'seq', [(i, i ^ d) for i in range(peers)])  18.8 us
    pallas_call x1, Pallas kernels, attention_forward(): pl.pallas_call(functools.partial(forward_kernel, peers, heads, rows, bq,...  12.9 us
    pallas_call x1, Pallas kernels, attention_backward(): pl.pallas_call(functools.partial(backward_kernel, listed, heads, rows, bq...  10.8 us
    ppermute x3, waiting for transfers between devices, pass_on(): lax.ppermute(x, 'head', [(i, (i + 1) % groups) for i in range(groups)])  8.42 us
    ppermute x3, starting transfers between devices, pass_on(): lax.ppermute(x, 'head', [(i, (i + 1) % groups) for i in range(groups)])  4.66 us
    dynamic_slice x1, local copies, waits for them, and re-layouts, per_device(): lax.dynamic_slice_in_dim(out_weight, block * width, width, 1)  4.54 us
    pallas_call x1, Pallas kernels, pack_heads(): pl.pallas_call(functools.partial(pack_kernel, heads, rows), in_specs=[SME...  3.62 us
  transfers between devices with their start and end apart: 24, of which 15 were waited for; matrix products, arithmetic and copies ran while one was open for 4% of the time, Pallas kernels for 20%

profile of v21, /device:TPU:0, one launch (start us, length us, event | category | flops | bytes accessed | tf_op | source)
XLA Modules:
  0.0 117.5 jit_solution(2976688512933074758)
XLA Ops:
  0.6 3.1 %collective-permute-start = (bf16[384,1024]{1,0:T(8,128)(2,1)}, bf16[384,1024]{1,0:T(8,128)(2,1)S(1)}, u32[]{:S(2)}, u32[]{:S(2)}) collective-permute-start(bf16[384,1024]{1,0:T(8,128)(2,1)} %o_ref.1), channel_id=1, source_target_pairs={{0,1},{1,2},{2,3},{3,0},{4,5},{5,6},{6,7},{7,4},{8,9},{9,10},{10,1... | collective-permute-start | bytes 2359304 | tf_op jit(solution)/shard_map/ppermute | solution.py:489
  3.7 3.6 %shard_map.85 = (bf16[1168,128]{1,0:T(8,128)(2,1)}, bf16[1168,128]{1,0:T(8,128)(2,1)}, bf16[1168,128]{1,0:T(8,128)(2,1)}, bf16[1168,128]{1,0:T(8,128)(2,1)}, bf1...) custom-call(s32[1]{0:T(128)} %bitcast.me_s, ...), custom_call_target="tpu_custom_call" | custom-call | tf_op jit(solution)/shard_map/pallas_call | solution.py:64
  7.3 1.5 %collective-permute-start.1 = (bf16[1168,128]{1,0:T(8,128)(2,1)}, bf16[1168,128]{1,0:T(8,128)(2,1)S(1)}, u32[]{:S(2)}, u32[]{:S(2)}) collective-permute-start(bf16[1168,128]{1,0:T(8,128)(2,1)} %get-tuple-element.70), channel_id=1, source_target_pairs={{0,8},{4,12},{8,0},{12,4},{16,24},{20,28},{24,16},{28,20},{1,9},{5... | collective-permute-start | bytes 897032 | tf_op jit(solution)/shard_map/ppermute | solution.py:486
  8.8 1.5 %collective-permute-start.2 = (bf16[1168,128]{1,0:T(8,128)(2,1)}, bf16[1168,128]{1,0:T(8,128)(2,1)S(1)}, u32[]{:S(2)}, u32[]{:S(2)}) collective-permute-start(bf16[1168,128]{1,0:T(8,128)(2,1)} %get-tuple-element.71), channel_id=1, source_target_pairs={{0,16},{4,20},{8,24},{12,28},{16,0},{20,4},{24,8},{28,12},{1,17},{... | collective-permute-start | bytes 897032 | tf_op jit(solution)/shard_map/ppermute | solution.py:486
  10.3 0.5 collective-permute-start.3
  10.8 4.5 %constant_dynamic-slice_fusion = (bf16[1024,1024]{1,0:T(8,128)(2,1)S(1)}, bf16[1024,1024]{1,0:T(8,128)(2,1)S(1)}, bf16[1024,1024]{1,0:T(8,128)(2,1)S(1)}, bf16[1024,1024]{1,0:T(8,128)(2,1)S(1)}) fusion(bf16[1024,4096]{1,0:T(8,128)(2,1)} %param.10, s32[]{:T(128)S(6)} %select_n.15, s32[]{:T(128)S(6)} %select_n.13, s32[]{:T(128)S(6)} %select_n.12, s32[]{:T(128)S(6)} %select_n.14), kind=kLoop, calls=%fused_computation | loop fusion | bytes 16777232 | tf_op jit(solution)/shard_map/dynamic_slice | solution.py:510
  15.4 0.0 copy-start.2
  15.4 1.0 shard_map.86.refs_0_
  16.4 1.1 collective-permute-done.1.refs_2_
  17.6 6.2 %collective-permute-done.2.refs_4_ = bf16[1168,128]{1,0:T(8,128)(2,1)S(1)} collective-permute-done((bf16[1168,128]{1,0:T(8,128)(2,1)}, bf16[1168,128]{1,0:T(8,128)(2,1)S(1)}, u32[]{:S(2)}, u32[]{:S(2)}) %collective-permute-start.2) | collective-permute-done | bytes 299040 | tf_op jit(solution)/shard_map/ppermute | solution.py:486
  23.7 1.6 %collective-permute-start.4 = (bf16[384,1024]{1,0:T(8,128)(2,1)S(1)}, bf16[384,1024]{1,0:T(8,128)(2,1)S(1)}, u32[]{:S(2)}, u32[]{:S(2)}) collective-permute-start(bf16[384,1024]{1,0:T(8,128)(2,1)S(1)} %collective-permute-done.o_ref), channel_id=1, source_target_pairs={{0,1},{1,2},{2,3},{3,0},{4,5},{5,6},{6,7},{7,4},{8,9},{9,10},{10,1... | collective-permute-start | bytes 2359304 | tf_op jit(solution)/shard_map/ppermute | solution.py:489
  25.3 2.4 %collective-permute-start.6 = (bf16[1168,128]{1,0:T(8,128)(2,1)S(1)}, bf16[1168,128]{1,0:T(8,128)(2,1)S(1)}, u32[]{:S(2)}, u32[]{:S(2)}) collective-permute-start(bf16[1168,128]{1,0:T(8,128)(2,1)S(1)} %copy-done.4), channel_id=1, source_target_pairs={{0,20},{4,16},{8,28},{12,24},{16,4},{20,0},{24,12},{28,8},{1,21},{... | collective-permute-start | bytes 897032 | tf_op jit(solution)/shard_map/ppermute | solution.py:486
  27.7 0.4 collective-permute-start.7
  28.1 0.6 collective-permute-start.8
  28.6 1.0 shard_map.87.refs_0_
  29.7 6.0 %collective-permute-done.5.refs_7_ = bf16[1168,128]{1,0:T(8,128)(2,1)S(1)} collective-permute-done((bf16[1168,128]{1,0:T(8,128)(2,1)S(1)}, bf16[1168,128]{1,0:T(8,128)(2,1)S(1)}, u32[]{:S(2)}, u32[]{:S(2)}) %collective-permute-start.5) | collective-permute-done | bytes 299040 | tf_op jit(solution)/shard_map/ppermute | solution.py:486
  35.6 5.4 %collective-permute-done.6.refs_5_ = bf16[1168,128]{1,0:T(8,128)(2,1)S(1)} collective-permute-done((bf16[1168,128]{1,0:T(8,128)(2,1)S(1)}, bf16[1168,128]{1,0:T(8,128)(2,1)S(1)}, u32[]{:S(2)}, u32[]{:S(2)}) %collective-permute-start.6) | collective-permute-done | bytes 299040 | tf_op jit(solution)/shard_map/ppermute | solution.py:486
  41.1 3.0 %collective-permute-done.4.o_ref = bf16[384,1024]{1,0:T(8,128)(2,1)S(1)} collective-permute-done((bf16[384,1024]{1,0:T(8,128)(2,1)S(1)}, bf16[384,1024]{1,0:T(8,128)(2,1)S(1)}, u32[]{:S(2)}, u32[]{:S(2)}) %collective-permute-start.4) | collective-permute-done | bytes 786464 | tf_op jit(solution)/shard_map/ppermute | solution.py:489
  44.0 12.9 %shard_map.88 = (bf16[3072,128]{1,0:T(8,128)(2,1)S(1)}, bf16[3072,256]{1,0:T(8,128)(2,1)S(1)}, bf16[3072,256]{1,0:T(8,128)(2,1)S(1)}, bf16[128,3072]{1,0:T(8,128...) custom-call(s32[1]{0:T(128)} %bitcast.me_s, ...), custom_call_target="tpu_custom_call" | custom-call | flops 1811939328 | bytes 6291456 | tf_op jit(solution)/shard_map/pallas_call | solution.py:426
  56.9 1.0 shard_map.89.acc_ref
  57.9 5.5 %collective-permute-done.9.o_ref = bf16[384,1024]{1,0:T(8,128)(2,1)S(1)} collective-permute-done((bf16[384,1024]{1,0:T(8,128)(2,1)S(1)}, bf16[384,1024]{1,0:T(8,128)(2,1)S(1)}, u32[]{:S(2)}, u32[]{:S(2)}) %collective-permute-start.9) | collective-permute-done | bytes 786464 | tf_op jit(solution)/shard_map/ppermute | solution.py:489
  63.4 1.0 shard_map.90
  64.4 2.3 %collective-permute-start.10 = (bf16[384,128]{1,0:T(8,128)(2,1)S(1)}, bf16[384,128]{1,0:T(8,128)(2,1)S(1)}, u32[]{:S(2)}, u32[]{:S(2)}) collective-permute-start(bf16[384,128]{1,0:T(8,128)(2,1)S(1)} %get-tuple-element.107), channel_id=1, source_target_pairs={{0,24},{4,28},{8,16},{12,20},{16,8},{20,12},{24,0},{28,4},{1,25},{... | collective-permute-start | bytes 294920 | tf_op jit(solution)/shard_map/ppermute | solution.py:486
  66.7 0.3 collective-permute-start.12
  67.0 1.0 collective-permute-start.13
  68.0 1.7 %collective-permute-start.14 = (bf16[384,128]{1,0:T(8,128)(2,1)S(1)}, bf16[384,128]{1,0:T(8,128)(2,1)S(1)}, u32[]{:S(2)}, u32[]{:S(2)}) collective-permute-start(bf16[384,128]{1,0:T(8,128)(2,1)S(1)} %get-tuple-element.117), channel_id=1, source_target_pairs={{0,12},{4,8},{8,4},{12,0},{16,28},{20,24},{24,20},{28,16},{1,13},{... | collective-permute-start | bytes 294920 | tf_op jit(solution)/shard_map/ppermute | solution.py:486
  69.6 0.4 collective-permute-done.10.refs_4_
  70.0 0.5 collective-permute-start.15
  70.5 2.3 %collective-permute-done.11.refs_5_ = bf16[384,128]{1,0:T(8,128)(2,1)S(1)} collective-permute-done((bf16[384,128]{1,0:T(8,128)(2,1)S(1)}, bf16[384,128]{1,0:T(8,128)(2,1)S(1)}, u32[]{:S(2)}, u32[]{:S(2)}) %collective-permute-start.11) | collective-permute-done | bytes 98336 | tf_op jit(solution)/shard_map/ppermute | solution.py:486
  72.7 2.5 %shard_map.91 = (bf16[80,256,256]{2,1,0:T(8,128)(2,1)S(1)}, f32[128,3072]{1,0:T(8,128)S(1)}, f32[3072,128]{1,0:T(8,128)S(1)}, f32[3072,128]{1,0:T(8,128)S(1)}) custom-call(s32[80]{0:T(128)S(1)} %get-tuple-element.90.plan_q, s32[2]{0:T(128)S(1)} %get-tuple-element.92.count_ref, ...), custom_call_target="tpu_custom_call", output_to_operand_aliasing={{0}: (4, {})} | custom-call | tf_op jit(solution)/shard_map/pallas_call | solution.py:445
  75.2 0.7 collective-permute-done.14.refs_8_
  75.9 0.4 collective-permute-done.15.refs_9_
  76.3 10.8 %shard_map.92 = (f32[128,3072]{1,0:T(8,128)S(1)}, f32[3072,128]{1,0:T(8,128)S(1)}, f32[3072,128]{1,0:T(8,128)S(1)}) custom-call(s32[1]{0:T(128)} %bitcast.me_s, s32[80]{0:T(128)S(1)} %get-tuple-element.90.plan_q, s32[80]{0:T(128)S(1)} %get-tuple-element.91.plan_k, ...), custom_call_target="tpu_custom_call", output_to_operand_aliasing={{0}: (11, {}), {1}: (12, {}), {2}: (13, {})} | custom-call | flops 3019898880 | bytes 6291456 | tf_op jit(solution)/shard_map/pallas_call | solution.py:467
  87.1 0.2 shard_map.94
  87.3 2.3 %collective-permute-start.22 = (bf16[1152,128]{1,0:T(8,128)(2,1)S(1)}, bf16[1152,128]{1,0:T(8,128)(2,1)S(1)}, u32[]{:S(2)}, u32[]{:S(2)}) collective-permute-start(bf16[1152,128]{1,0:T(8,128)(2,1)S(1)} %get-tuple-element.129), channel_id=1, source_target_pairs={{0,24},{4,28},{8,16},{12,20},{16,8},{20,12},{24,0},{28,4},{1,25},{... | collective-permute-start | bytes 884744 | tf_op jit(solution)/shard_map/ppermute | solution.py:486
  89.6 0.1 collective-permute-start.23
  89.7 0.3 shard_map.93
  90.0 1.3 %collective-permute-start.17 = (bf16[1152,128]{1,0:T(8,128)(2,1)S(1)}, bf16[1152,128]{1,0:T(8,128)(2,1)S(1)}, u32[]{:S(2)}, u32[]{:S(2)}) collective-permute-start(bf16[1152,128]{1,0:T(8,128)(2,1)S(1)} %get-tuple-element.124), channel_id=1, source_target_pairs={{0,8},{4,12},{8,0},{12,4},{16,24},{20,28},{24,16},{28,20},{1,9},{5... | collective-permute-start | bytes 884744 | tf_op jit(solution)/shard_map/ppermute | solution.py:486
  91.3 1.5 %collective-permute-start.18 = (bf16[1152,128]{1,0:T(8,128)(2,1)S(1)}, bf16[1152,128]{1,0:T(8,128)(2,1)S(1)}, u32[]{:S(2)}, u32[]{:S(2)}) collective-permute-start(bf16[1152,128]{1,0:T(8,128)(2,1)S(1)} %get-tuple-element.125), channel_id=1, source_target_pairs={{0,16},{4,20},{8,24},{12,28},{16,0},{20,4},{24,8},{28,12},{1,17},{... | collective-permute-start | bytes 884744 | tf_op jit(solution)/shard_map/ppermute | solution.py:486
  92.9 0.1 collective-permute-start.19
  93.0 5.3 %collective-permute-done.22.refs_0_ = bf16[1152,128]{1,0:T(8,128)(2,1)S(1)} collective-permute-done((bf16[1152,128]{1,0:T(8,128)(2,1)S(1)}, bf16[1152,128]{1,0:T(8,128)(2,1)S(1)}, u32[]{:S(2)}, u32[]{:S(2)}) %collective-permute-start.22) | collective-permute-done | bytes 294944 | tf_op jit(solution)/shard_map/ppermute | solution.py:486
  98.2 5.1 %collective-permute-done.23.refs_1_ = bf16[1152,128]{1,0:T(8,128)(2,1)S(1)} collective-permute-done((bf16[1152,128]{1,0:T(8,128)(2,1)S(1)}, bf16[1152,128]{1,0:T(8,128)(2,1)S(1)}, u32[]{:S(2)}, u32[]{:S(2)}) %collective-permute-start.23) | collective-permute-done | bytes 294944 | tf_op jit(solution)/shard_map/ppermute | solution.py:486
  103.3 1.0 collective-permute-start.21
  104.3 1.0 shard_map.95
  105.3 5.1 %collective-permute-done.17.refs_0_ = bf16[1152,128]{1,0:T(8,128)(2,1)S(1)} collective-permute-done((bf16[1152,128]{1,0:T(8,128)(2,1)S(1)}, bf16[1152,128]{1,0:T(8,128)(2,1)S(1)}, u32[]{:S(2)}, u32[]{:S(2)}) %collective-permute-start.17) | collective-permute-done | bytes 294944 | tf_op jit(solution)/shard_map/ppermute | solution.py:486
  110.4 4.7 %collective-permute-done.19.refs_2_ = bf16[1152,128]{1,0:T(8,128)(2,1)S(1)} collective-permute-done((bf16[1152,128]{1,0:T(8,128)(2,1)S(1)}, bf16[1152,128]{1,0:T(8,128)(2,1)S(1)}, u32[]{:S(2)}, u32[]{:S(2)}) %collective-permute-start.19) | collective-permute-done | bytes 294944 | tf_op jit(solution)/shard_map/ppermute | solution.py:486
  115.1 1.0 collective-permute-done.20.refs_3_
  116.1 1.2 %shard_map.96 = (bf16[384,1024]{1,0:T(8,128)(2,1)}, bf16[384,1024]{1,0:T(8,128)(2,1)}, bf16[384,1024]{1,0:T(8,128)(2,1)}) custom-call(s32[1]{0:T(128)} %bitcast.me_s, bf16[1152,128]{1,0:T(8,128)(2,1)S(1)} %collective-permute-done.17.refs_0_, ...), custom_call_target="tpu_custom_call", output_to_operand_aliasing={{0}: (6, {}), {1}: (7, {}), {2}: (8, {})} | custom-call | tf_op jit(solution)/shard_map/pallas_call | solution.py:89
  (25 shorter events, 0.1 us)
Async XLA Ops:
  0.6 23.1 %collective-permute-start = (bf16[384,1024]{1,0:T(8,128)(2,1)}, bf16[384,1024]{1,0:T(8,128)(2,1)S(1)}, u32[]{:S(2)}, u32[]{:S(2)}) collective-permute-start(bf16[384,1024]{1,0:T(8,128)(2,1)} %o_ref.1), channel_id=1, source_target_pairs={{0,1},{1,2},{2,3},{3,0},{4,5},{5,6},{6,7},{7,4},{8,9},{9,10},{10,1... | collective-permute-start | bytes 2359304 | tf_op jit(solution)/shard_map/ppermute | solution.py:489
  7.3 10.2 %collective-permute-start.1 = (bf16[1168,128]{1,0:T(8,128)(2,1)}, bf16[1168,128]{1,0:T(8,128)(2,1)S(1)}, u32[]{:S(2)}, u32[]{:S(2)}) collective-permute-start(bf16[1168,128]{1,0:T(8,128)(2,1)} %get-tuple-element.70), channel_id=1, source_target_pairs={{0,8},{4,12},{8,0},{12,4},{16,24},{20,28},{24,16},{28,20},{1,9},{5... | collective-permute-start | bytes 897032 | tf_op jit(solution)/shard_map/ppermute | solution.py:486
  8.8 14.9 %collective-permute-start.2 = (bf16[1168,128]{1,0:T(8,128)(2,1)}, bf16[1168,128]{1,0:T(8,128)(2,1)S(1)}, u32[]{:S(2)}, u32[]{:S(2)}) collective-permute-start(bf16[1168,128]{1,0:T(8,128)(2,1)} %get-tuple-element.71), channel_id=1, source_target_pairs={{0,16},{4,20},{8,24},{12,28},{16,0},{20,4},{24,8},{28,12},{1,17},{... | collective-permute-start | bytes 897032 | tf_op jit(solution)/shard_map/ppermute | solution.py:486
  10.3 13.4 %collective-permute-start.3 = (bf16[1168,128]{1,0:T(8,128)(2,1)}, bf16[1168,128]{1,0:T(8,128)(2,1)S(1)}, u32[]{:S(2)}, u32[]{:S(2)}) collective-permute-start(bf16[1168,128]{1,0:T(8,128)(2,1)} %get-tuple-element.72), channel_id=1, source_target_pairs={{0,24},{4,28},{8,16},{12,20},{16,8},{20,12},{24,0},{28,4},{1,25},{... | collective-permute-start | bytes 897032 | tf_op jit(solution)/shard_map/ppermute | solution.py:486
  10.8 4.5 %copy-start = (bf16[384,1024]{1,0:T(8,128)(2,1)S(1)}, bf16[384,1024]{1,0:T(8,128)(2,1)}, u32[]{:S(2)}) copy-start(bf16[384,1024]{1,0:T(8,128)(2,1)} %o_ref.1) | copy-start | bytes 2359300
  15.4 9.9 %copy-start.5 = (bf16[1168,128]{1,0:T(8,128)(2,1)S(1)}, bf16[1168,128]{1,0:T(8,128)(2,1)}, u32[]{:S(2)}) copy-start(bf16[1168,128]{1,0:T(8,128)(2,1)} %get-tuple-element.75) | copy-start | bytes 897028
  15.4 9.9 %copy-start.4 = (bf16[1168,128]{1,0:T(8,128)(2,1)S(1)}, bf16[1168,128]{1,0:T(8,128)(2,1)}, u32[]{:S(2)}) copy-start(bf16[1168,128]{1,0:T(8,128)(2,1)} %get-tuple-element.76) | copy-start | bytes 897028
  15.4 12.3 %copy-start.3 = (bf16[1168,128]{1,0:T(8,128)(2,1)S(1)}, bf16[1168,128]{1,0:T(8,128)(2,1)}, u32[]{:S(2)}) copy-start(bf16[1168,128]{1,0:T(8,128)(2,1)} %get-tuple-element.77) | copy-start | bytes 897028
  15.4 12.7 %copy-start.2 = (bf16[1168,128]{1,0:T(8,128)(2,1)S(1)}, bf16[1168,128]{1,0:T(8,128)(2,1)}, u32[]{:S(2)}) copy-start(bf16[1168,128]{1,0:T(8,128)(2,1)} %get-tuple-element.78) | copy-start | bytes 897028
  23.7 20.3 %collective-permute-start.4 = (bf16[384,1024]{1,0:T(8,128)(2,1)S(1)}, bf16[384,1024]{1,0:T(8,128)(2,1)S(1)}, u32[]{:S(2)}, u32[]{:S(2)}) collective-permute-start(bf16[384,1024]{1,0:T(8,128)(2,1)S(1)} %collective-permute-done.o_ref), channel_id=1, source_target_pairs={{0,1},{1,2},{2,3},{3,0},{4,5},{5,6},{6,7},{7,4},{8,9},{9,10},{10,1... | collective-permute-start | bytes 2359304 | tf_op jit(solution)/shard_map/ppermute | solution.py:489
  25.3 10.3 %collective-permute-start.5 = (bf16[1168,128]{1,0:T(8,128)(2,1)S(1)}, bf16[1168,128]{1,0:T(8,128)(2,1)S(1)}, u32[]{:S(2)}, u32[]{:S(2)}) collective-permute-start(bf16[1168,128]{1,0:T(8,128)(2,1)S(1)} %copy-done.5), channel_id=1, source_target_pairs={{0,28},{4,24},{8,20},{12,16},{16,12},{20,8},{24,4},{28,0},{1,29},{... | collective-permute-start | bytes 897032 | tf_op jit(solution)/shard_map/ppermute | solution.py:486
  25.3 15.7 %collective-permute-start.6 = (bf16[1168,128]{1,0:T(8,128)(2,1)S(1)}, bf16[1168,128]{1,0:T(8,128)(2,1)S(1)}, u32[]{:S(2)}, u32[]{:S(2)}) collective-permute-start(bf16[1168,128]{1,0:T(8,128)(2,1)S(1)} %copy-done.4), channel_id=1, source_target_pairs={{0,20},{4,16},{8,28},{12,24},{16,4},{20,0},{24,12},{28,8},{1,21},{... | collective-permute-start | bytes 897032 | tf_op jit(solution)/shard_map/ppermute | solution.py:486
  27.7 13.3 %collective-permute-start.7 = (bf16[1168,128]{1,0:T(8,128)(2,1)S(1)}, bf16[1168,128]{1,0:T(8,128)(2,1)S(1)}, u32[]{:S(2)}, u32[]{:S(2)}) collective-permute-start(bf16[1168,128]{1,0:T(8,128)(2,1)S(1)} %copy-done.3), channel_id=1, source_target_pairs={{0,12},{4,8},{8,4},{12,0},{16,28},{20,24},{24,20},{28,16},{1,13},{... | collective-permute-start | bytes 897032 | tf_op jit(solution)/shard_map/ppermute | solution.py:486
  28.1 13.0 %collective-permute-start.8 = (bf16[1168,128]{1,0:T(8,128)(2,1)S(1)}, bf16[1168,128]{1,0:T(8,128)(2,1)S(1)}, u32[]{:S(2)}, u32[]{:S(2)}) collective-permute-start(bf16[1168,128]{1,0:T(8,128)(2,1)S(1)} %copy-done.2), channel_id=1, source_target_pairs={{0,4},{4,0},{8,12},{12,8},{16,20},{20,16},{24,28},{28,24},{1,5},{5... | collective-permute-start | bytes 897032 | tf_op jit(solution)/shard_map/ppermute | solution.py:486
  28.6 15.4 %copy-start.1 = (bf16[1168,128]{1,0:T(8,128)(2,1)S(1)}, bf16[1168,128]{1,0:T(8,128)(2,1)}, u32[]{:S(2)}) copy-start(bf16[1168,128]{1,0:T(8,128)(2,1)} %get-tuple-element.82.refs_0_) | copy-start | bytes 897028
  44.0 19.4 %collective-permute-start.9 = (bf16[384,1024]{1,0:T(8,128)(2,1)S(1)}, bf16[384,1024]{1,0:T(8,128)(2,1)S(1)}, u32[]{:S(2)}, u32[]{:S(2)}) collective-permute-start(bf16[384,1024]{1,0:T(8,128)(2,1)S(1)} %collective-permute-done.4.o_ref), channel_id=1, source_target_pairs={{0,1},{1,2},{2,3},{3,0},{4,5},{5,6},{6,7},{7,4},{8,9},{9,10},{10,1... | collective-permute-start | bytes 2359304 | tf_op jit(solution)/shard_map/ppermute | solution.py:489
  64.4 5.6 %collective-permute-start.10 = (bf16[384,128]{1,0:T(8,128)(2,1)S(1)}, bf16[384,128]{1,0:T(8,128)(2,1)S(1)}, u32[]{:S(2)}, u32[]{:S(2)}) collective-permute-start(bf16[384,128]{1,0:T(8,128)(2,1)S(1)} %get-tuple-element.107), channel_id=1, source_target_pairs={{0,24},{4,28},{8,16},{12,20},{16,8},{20,12},{24,0},{28,4},{1,25},{... | collective-permute-start | bytes 294920 | tf_op jit(solution)/shard_map/ppermute | solution.py:486
  66.7 6.1 %collective-permute-start.11 = (bf16[384,128]{1,0:T(8,128)(2,1)S(1)}, bf16[384,128]{1,0:T(8,128)(2,1)S(1)}, u32[]{:S(2)}, u32[]{:S(2)}) collective-permute-start(bf16[384,128]{1,0:T(8,128)(2,1)S(1)} %get-tuple-element.114), channel_id=1, source_target_pairs={{0,28},{4,24},{8,20},{12,16},{16,12},{20,8},{24,4},{28,0},{1,29},{... | collective-permute-start | bytes 294920 | tf_op jit(solution)/shard_map/ppermute | solution.py:486
  66.7 8.5 %collective-permute-start.12 = (bf16[384,128]{1,0:T(8,128)(2,1)S(1)}, bf16[384,128]{1,0:T(8,128)(2,1)S(1)}, u32[]{:S(2)}, u32[]{:S(2)}) collective-permute-start(bf16[384,128]{1,0:T(8,128)(2,1)S(1)} %get-tuple-element.115), channel_id=1, source_target_pairs={{0,8},{4,12},{8,0},{12,4},{16,24},{20,28},{24,16},{28,20},{1,9},{5... | collective-permute-start | bytes 294920 | tf_op jit(solution)/shard_map/ppermute | solution.py:486
  67.0 8.3 %collective-permute-start.13 = (bf16[384,128]{1,0:T(8,128)(2,1)S(1)}, bf16[384,128]{1,0:T(8,128)(2,1)S(1)}, u32[]{:S(2)}, u32[]{:S(2)}) collective-permute-start(bf16[384,128]{1,0:T(8,128)(2,1)S(1)} %get-tuple-element.116), channel_id=1, source_target_pairs={{0,16},{4,20},{8,24},{12,28},{16,0},{20,4},{24,8},{28,12},{1,17},{... | collective-permute-start | bytes 294920 | tf_op jit(solution)/shard_map/ppermute | solution.py:486
  68.0 7.9 %collective-permute-start.14 = (bf16[384,128]{1,0:T(8,128)(2,1)S(1)}, bf16[384,128]{1,0:T(8,128)(2,1)S(1)}, u32[]{:S(2)}, u32[]{:S(2)}) collective-permute-start(bf16[384,128]{1,0:T(8,128)(2,1)S(1)} %get-tuple-element.117), channel_id=1, source_target_pairs={{0,12},{4,8},{8,4},{12,0},{16,28},{20,24},{24,20},{28,16},{1,13},{... | collective-permute-start | bytes 294920 | tf_op jit(solution)/shard_map/ppermute | solution.py:486
  70.0 6.3 %collective-permute-start.15 = (bf16[384,128]{1,0:T(8,128)(2,1)S(1)}, bf16[384,128]{1,0:T(8,128)(2,1)S(1)}, u32[]{:S(2)}, u32[]{:S(2)}) collective-permute-start(bf16[384,128]{1,0:T(8,128)(2,1)S(1)} %get-tuple-element.118), channel_id=1, source_target_pairs={{0,20},{4,16},{8,28},{12,24},{16,4},{20,0},{24,12},{28,8},{1,21},{... | collective-permute-start | bytes 294920 | tf_op jit(solution)/shard_map/ppermute | solution.py:486
  72.7 3.6 %collective-permute-start.16 = (bf16[384,128]{1,0:T(8,128)(2,1)S(1)}, bf16[384,128]{1,0:T(8,128)(2,1)S(1)}, u32[]{:S(2)}, u32[]{:S(2)}) collective-permute-start(bf16[384,128]{1,0:T(8,128)(2,1)S(1)} %get-tuple-element.120), channel_id=1, source_target_pairs={{0,4},{4,0},{8,12},{12,8},{16,20},{20,16},{24,28},{28,24},{1,5},{5... | collective-permute-start | bytes 294920 | tf_op jit(solution)/shard_map/ppermute | solution.py:486
  87.3 10.9 %collective-permute-start.22 = (bf16[1152,128]{1,0:T(8,128)(2,1)S(1)}, bf16[1152,128]{1,0:T(8,128)(2,1)S(1)}, u32[]{:S(2)}, u32[]{:S(2)}) collective-permute-start(bf16[1152,128]{1,0:T(8,128)(2,1)S(1)} %get-tuple-element.129), channel_id=1, source_target_pairs={{0,24},{4,28},{8,16},{12,20},{16,8},{20,12},{24,0},{28,4},{1,25},{... | collective-permute-start | bytes 884744 | tf_op jit(solution)/shard_map/ppermute | solution.py:486
  89.6 13.7 %collective-permute-start.23 = (bf16[1152,128]{1,0:T(8,128)(2,1)S(1)}, bf16[1152,128]{1,0:T(8,128)(2,1)S(1)}, u32[]{:S(2)}, u32[]{:S(2)}) collective-permute-start(bf16[1152,128]{1,0:T(8,128)(2,1)S(1)} %get-tuple-element.130), channel_id=1, source_target_pairs={{0,28},{4,24},{8,20},{12,16},{16,12},{20,8},{24,4},{28,0},{1,29},{... | collective-permute-start | bytes 884744 | tf_op jit(solution)/shard_map/ppermute | solution.py:486
  90.0 20.4 %collective-permute-start.17 = (bf16[1152,128]{1,0:T(8,128)(2,1)S(1)}, bf16[1152,128]{1,0:T(8,128)(2,1)S(1)}, u32[]{:S(2)}, u32[]{:S(2)}) collective-permute-start(bf16[1152,128]{1,0:T(8,128)(2,1)S(1)} %get-tuple-element.124), channel_id=1, source_target_pairs={{0,8},{4,12},{8,0},{12,4},{16,24},{20,28},{24,16},{28,20},{1,9},{5... | collective-permute-start | bytes 884744 | tf_op jit(solution)/shard_map/ppermute | solution.py:486
  91.3 19.1 %collective-permute-start.18 = (bf16[1152,128]{1,0:T(8,128)(2,1)S(1)}, bf16[1152,128]{1,0:T(8,128)(2,1)S(1)}, u32[]{:S(2)}, u32[]{:S(2)}) collective-permute-start(bf16[1152,128]{1,0:T(8,128)(2,1)S(1)} %get-tuple-element.125), channel_id=1, source_target_pairs={{0,16},{4,20},{8,24},{12,28},{16,0},{20,4},{24,8},{28,12},{1,17},{... | collective-permute-start | bytes 884744 | tf_op jit(solution)/shard_map/ppermute | solution.py:486
  92.9 22.2 %collective-permute-start.19 = (bf16[1152,128]{1,0:T(8,128)(2,1)S(1)}, bf16[1152,128]{1,0:T(8,128)(2,1)S(1)}, u32[]{:S(2)}, u32[]{:S(2)}) collective-permute-start(bf16[1152,128]{1,0:T(8,128)(2,1)S(1)} %get-tuple-element.126), channel_id=1, source_target_pairs={{0,12},{4,8},{8,4},{12,0},{16,28},{20,24},{24,20},{28,16},{1,13},{... | collective-permute-start | bytes 884744 | tf_op jit(solution)/shard_map/ppermute | solution.py:486
  98.2 17.9 %collective-permute-start.20 = (bf16[1152,128]{1,0:T(8,128)(2,1)S(1)}, bf16[1152,128]{1,0:T(8,128)(2,1)S(1)}, u32[]{:S(2)}, u32[]{:S(2)}) collective-permute-start(bf16[1152,128]{1,0:T(8,128)(2,1)S(1)} %get-tuple-element.127), channel_id=1, source_target_pairs={{0,20},{4,16},{8,28},{12,24},{16,4},{20,0},{24,12},{28,8},{1,21},{... | collective-permute-start | bytes 884744 | tf_op jit(solution)/shard_map/ppermute | solution.py:486
  103.3 12.8 %collective-permute-start.21 = (bf16[1152,128]{1,0:T(8,128)(2,1)S(1)}, bf16[1152,128]{1,0:T(8,128)(2,1)S(1)}, u32[]{:S(2)}, u32[]{:S(2)}) collective-permute-start(bf16[1152,128]{1,0:T(8,128)(2,1)S(1)} %get-tuple-element.128), channel_id=1, source_target_pairs={{0,4},{4,0},{8,12},{12,8},{16,20},{20,16},{24,28},{28,24},{1,5},{5... | collective-permute-start | bytes 884744 | tf_op jit(solution)/shard_map/ppermute | solution.py:486
